TPU v7x, 32 devices: a whole 2x2x4 slice. The times are simulated.
32 devices in a mesh: seq: 8 (over z, y), head: 4 (over x, core).
Axes of the slice: x: 2, y: 2, z: 4, core: 2. Of those that a mesh axis runs over, the one named last changes fastest.
Arguments:
- ids: int32 [16, 256], P('seq'), may hold values from 0 to 32
- pad_mask: int32 [16], P('seq'), may hold values from 0 to 1, as said below
- embed: bfloat16 [33, 768], replicated, may hold values from -16 to 16
- row_qkv: bfloat16 [3, 768, 768], P(None, 'head'), may hold values from -24 to 24
- row_out: bfloat16 [768, 768], P('head'), may hold values from -0.4375 to 0.4375
- col_qkv: bfloat16 [3, 768, 768], P(None, 'head'), may hold values from -24 to 24
- col_out: bfloat16 [768, 768], P('head'), may hold values from -0.21875 to 0.21875
Outputs:
- layer_out: bfloat16 [16, 256, 768], P('seq', None, 'head')
Inputs may be any that keep to these rules, and one draw needn't show every extreme that they name: `pad_mask`: sequence 0 is always real.
All inputs are finite; a program needn't handle non-finite values.
Results may differ from a plain program's by a relative error of at most 0.007.
Values may be sent and summed in bfloat16 or wider, within the bound.
No kernel may reach another device: no remote copies, remote signals or barrier semaphores. Data moves between devices by JAX's collectives and lax.ppermute only.
A program may use at most 64 MiB of HBM per device.

v0:
```python
import jax
import jax.numpy as jnp
from jax import lax
from jax.sharding import PartitionSpec as P

HEAD_DIM = 64


EPS = 1e-05


def layer_norm(values):
    mean = jnp.mean(values, axis=-1, keepdims=True)
    centred = values - mean
    spread = jnp.mean(centred * centred, axis=-1, keepdims=True)
    return centred * lax.rsqrt(spread + EPS)


def softmax_last(scores):
    top = jnp.max(scores, axis=-1, keepdims=True)
    weights = jnp.exp(scores - top)
    return weights / jnp.sum(weights, axis=-1, keepdims=True)


def weight_fold(out_weight, piece):
    return jnp.einsum("rce,fe->rcf", piece, out_weight, preferred_element_type=jnp.float32)


def attend_columns(query, keys, values, key_live):
    rows_all, count_cols, local_width = query.shape
    heads_here = local_width // HEAD_DIM
    shape = (rows_all, count_cols, heads_here, HEAD_DIM)
    scores = jnp.einsum(
        "rchd,schd->chrs",
        query.reshape(shape),
        keys.reshape(shape),
        preferred_element_type=jnp.float32,
    ) * HEAD_DIM ** (-0.5)
    scores = jnp.where(key_live > 0, scores, -jnp.inf)
    probs = softmax_last(scores).astype(jnp.bfloat16)
    context = jnp.einsum(
        "chrs,schd->rchd", probs, values.reshape(shape), preferred_element_type=jnp.float32
    )
    return context.astype(jnp.bfloat16).reshape(rows_all, count_cols, local_width)


def send_back(context):
    return lax.all_to_all(context[:, None], "seq", split_axis=0, concat_axis=1, tiled=True)


def body(ids, pad_mask, embed, row_qkv, row_out, col_qkv, col_out):
    rows_here, cols = ids.shape
    width = embed.shape[1]
    local_width = row_out.shape[0]
    heads_here = local_width // HEAD_DIM
    groups = lax.axis_size("seq")
    per_group = cols // groups
    codes = lax.broadcasted_iota(jnp.int32, (1, 1, embed.shape[0]), 2)
    onehot = (ids[:, :, None] == codes).astype(jnp.bfloat16)
    embedded = jnp.einsum("rcv,vd->rcd", onehot, embed, preferred_element_type=jnp.float32)
    normed = layer_norm(embedded).astype(jnp.bfloat16)
    row_proj = jnp.einsum(
        "rcd,ted->trce", normed, row_qkv, preferred_element_type=jnp.float32
    ).astype(jnp.bfloat16)
    live = pad_mask.astype(jnp.bfloat16)
    head_shape = (rows_here, cols, heads_here, HEAD_DIM)
    query = (row_proj[0] * live[:, None, None]).reshape(head_shape)
    keys = row_proj[1].reshape(head_shape)
    values = row_proj[2].reshape(head_shape)
    partial_scores = jnp.einsum("rihd,rjhd->hij", query, keys, preferred_element_type=jnp.float32)
    count_here = jnp.sum(pad_mask.astype(jnp.float32))
    scale = HEAD_DIM ** (-0.5)
    total, count = lax.psum((partial_scores, count_here), "seq")
    row_probs = softmax_last(total * (scale / jnp.sqrt(count))).astype(jnp.bfloat16)
    row_context = jnp.einsum(
        "hij,rjhd->rihd", row_probs, values, preferred_element_type=jnp.float32
    )
    row_context = row_context.astype(jnp.bfloat16).reshape(rows_here, cols, local_width)
    start_feature = lax.axis_index("head") * local_width
    resident = lax.dynamic_slice_in_dim(embedded, start_feature, local_width, 2)
    row_update = weight_fold(row_out, lax.all_gather(row_context, "head", axis=2, tiled=True))
    mixed = resident + row_update
    sums, squares = lax.psum((jnp.sum(mixed, axis=-1), jnp.sum(mixed * mixed, axis=-1)), "head")
    mean = sums / width
    spread = squares / width - mean * mean
    normed_here = ((mixed - mean[..., None]) * lax.rsqrt(spread[..., None] + EPS)).astype(
        jnp.bfloat16
    )
    live_tile = jnp.broadcast_to(live[:, None, None, None], (rows_here, groups, per_group, 1))
    normed_full = lax.all_gather(normed_here, "head", axis=2, tiled=True)
    col_proj = jnp.einsum("rcd,ted->rcte", normed_full, col_qkv, preferred_element_type=jnp.float32)
    packed = col_proj.astype(jnp.bfloat16).reshape(rows_here, groups, per_group, 3 * local_width)
    received = lax.all_to_all(packed, "seq", split_axis=1, concat_axis=0, tiled=True)
    mask_part = lax.all_to_all(live_tile, "seq", split_axis=1, concat_axis=0, tiled=True)
    column_out = send_back(
        attend_columns(
            received[:, 0, :, :local_width],
            received[:, 0, :, local_width : 2 * local_width],
            received[:, 0, :, 2 * local_width :],
            mask_part[:, 0, 0, 0],
        )
    )
    column_out = column_out.reshape(rows_here, cols, local_width)
    col_update = weight_fold(col_out, lax.all_gather(column_out, "head", axis=2, tiled=True))
    return (mixed + col_update).astype(jnp.bfloat16)


def solution(mesh):
    placed = (
        P("seq", None),
        P("seq"),
        P(),
        P(None, "head", None),
        P("head", None),
        P(None, "head", None),
        P("head", None),
    )
    return jax.shard_map(
        body, mesh=mesh, in_specs=placed, out_specs=P("seq", None, "head"), check_vma=False
    )
```

profile of v0, /device:TPU:0, one launch (start us, length us, event | category | flops | bytes accessed | tf_op | source)
XLA Modules:
  0.0 179.3 jit_solution(11635607736094724836)
XLA Ops:
  6.5 0.0 copy-start
  6.5 0.0 all-reduce.3.cloned.1.call-start
  6.5 1.4 fusion.46
  8.0 0.3 multiply_reduce_fusion
  8.3 0.0 copy-done
  8.3 0.0 copy-start.4
  8.3 0.8 fusion.7
  9.2 1.3 convolution_bitcast_fusion
  10.5 0.0 all-reduce.3.cloned.1.call-update
  10.5 0.6 convert_reduce_fusion
  11.1 0.7 broadcast_in_dim.8
  11.8 7.3 %all-to-all-start.1 = ((bf16[2,8,32,1]{2,0,3,1:T(2,128)(2,1)}), bf16[2,8,32,1]{2,0,3,1:T(2,128)(2,1)S(1)}, u32[]{:S(2)}, u32[]{:S(2)}) async-start(bf16[2,8,32,1]{2,0,3,1:T(2,128)(2,1)} %broadcast_in_dim.8), calls=%async_computation.1 | async-start | bytes 8192 | tf_op jit(solution)/shard_map/all_to_all | solution.py:94
  19.1 22.6 %psum.29 = f32[]{:T(128)} all-reduce(f32[]{:T(128)} %convert_reduce_fusion), channel_id=1, replica_groups=mesh['seq'=8,'head'=4] {'seq'}, use_global_device_ids=true, to_apply=%region_4.0 | all-reduce | flops 1 | bytes 8 | tf_op jit(solution)/shard_map/psum | solution.py:73
  42.4 46.0 %all-reduce.3.cloned.1.call-done = f32[3,256,256]{2,1,0:T(8,128)} async-done(((f32[3,256,256]{2,1,0:T(8,128)}), f32[3,256,256]{2,1,0:T(8,128)}) %all-reduce.3.cloned.1.call-update) | async-done | bytes 786448 | tf_op jit(solution)/shard_map/psum | solution.py:73
  88.3 1.4 fusion.47
  89.8 0.0 copy-start.1
  89.8 2.7 %fusion.10 = bf16[2,256,3,64]{1,3,0,2:T(8,128)(2,1)S(1)} fusion(f32[3,256]{1,0:T(4,128)S(1)} %fusion.47, bf16[2,256,3,64]{1,3,2,0:T(8,128)(2,1)S(1)} %bitcast.81, f32[3,256,256]{2,1,0:T(8,128)} %all-reduce.3.cloned.1.call-done, f32[]{:T(128)S(6)} %div.33), kind=kOutput, calls=%fused_computation.20 | convolution fusion | flops 51217408 | bytes 1182724 | tf_op jit(solution)/shard_map/hij,rjhd->rihd/dot_general | solution.py:75
  92.5 8.6 %all_gather.9 = bf16[2,256,768]{1,2,0:T(8,128)(2,1)S(1)} all-gather(bf16[2,256,192]{1,2,0:T(8,128)(2,1)S(1)} %bitcast.80), channel_id=1, replica_groups=mesh['seq'=8,'head'=4] {'head'}, dimensions={2}, use_global_device_ids=true | all-gather | bytes 983040 | tf_op jit(solution)/shard_map/all_gather | solution.py:81
  101.1 0.0 copy-done.1
  101.1 0.6 fusion.43
  101.7 0.0 copy-start.3
  101.7 6.3 %all-reduce = (f32[2,256]{1,0:T(2,128)S(1)}, f32[2,256]{1,0:T(2,128)S(1)}) all-reduce(f32[2,256]{1,0:T(2,128)S(1)} %get-tuple-element.6, f32[2,256]{1,0:T(2,128)S(1)} %get-tuple-element.5), channel_id=1, replica_groups=mesh['seq'=8,'head'=4] {'head'}, use_global_device_ids=true, to_apply=%region_10.0 | all-reduce | flops 1024 | bytes 8192 | tf_op jit(solution)/shard_map/psum | solution.py:83
  108.0 0.2 multiply_convert_fusion.1
  108.2 0.2 copy.55
  108.4 8.6 %all_gather.10 = bf16[2,256,768]{1,0,2:T(2,128)(2,1)S(1)} all-gather(bf16[2,256,192]{1,0,2:T(2,128)(2,1)S(1)} %copy.55), channel_id=1, replica_groups=mesh['seq'=8,'head'=4] {'head'}, dimensions={2}, use_global_device_ids=true | all-gather | bytes 983040 | tf_op jit(solution)/shard_map/all_gather | solution.py:90
  117.0 1.4 convolution_convert_fusion
  118.4 1.6 copy.57
  120.0 1.5 reshape.40
  121.6 2.0 %copy.58 = bf16[2,8,32,576]{3,2,0,1:T(8,128)(2,1)} copy(bf16[2,8,32,576]{3,2,1,0:T(8,128)(2,1)} %reshape.40) | data formatting | bytes 1179648 | tf_op jit(solution)/shard_map/reshape | solution.py:92
  123.6 0.0 all-to-all-done.1
  123.6 3.7 %all-to-all-start = ((bf16[2,8,32,576]{3,2,0,1:T(8,128)(2,1)}), bf16[2,8,32,576]{3,2,0,1:T(8,128)(2,1)S(1)}, u32[]{:S(2)}, u32[]{:S(2)}) async-start(bf16[2,8,32,576]{3,2,0,1:T(8,128)(2,1)} %copy.58), calls=%async_computation | async-start | bytes 1310720 | tf_op jit(solution)/shard_map/all_to_all | solution.py:93
  127.3 0.1 compare_reduce_fusion
  127.4 17.7 %all-to-all-done = bf16[2,8,32,576]{3,2,0,1:T(8,128)(2,1)S(1)} async-done(((bf16[2,8,32,576]{3,2,0,1:T(8,128)(2,1)}), bf16[2,8,32,576]{3,2,0,1:T(8,128)(2,1)S(1)}, u32[]{:S(2)}, u32[]{:S(2)}) %all-to-all-start) | async-done | bytes 589856 | tf_op jit(solution)/shard_map/all_to_all | solution.py:93
  145.1 0.2 fusion.44
  145.3 0.1 reshape_squeeze.18
  145.5 0.1 reshape_squeeze.19
  145.6 1.6 fusion.6
  147.2 0.9 fusion.48
  148.1 0.1 reshape_squeeze.17
  148.3 2.0 %fusion.9 = bf16[16,32,3,64]{3,0,2,1:T(8,128)(2,1)S(1)} fusion(bf16[16,32,3,64]{3,2,1,0:T(4,128)(2,1)S(1)} %reshape_squeeze.17, f32[32,3,16]{2,1,0:T(4,128)S(1)} %fusion.48, f32[32,3,16,16]{2,3,1,0:T(8,128)} %fusion.6), kind=kOutput, calls=%fused_computation.18 | convolution fusion | flops 3319311 | bytes 497664 | tf_op jit(solution)/shard_map/chrs,schd->rchd/dot_general | solution.py:41
  150.3 0.3 copy.63
  150.5 0.0 copy-start.2
  150.5 0.3 broadcast_in_dim_reshape.3
  150.9 12.5 %all_to_all.51 = bf16[16,1,32,192]{3,2,1,0:T(8,128)(2,1)S(1)} all-to-all(bf16[16,1,32,192]{3,2,1,0:T(8,128)(2,1)S(1)} %bitcast.74), channel_id=1, replica_groups=mesh['seq'=8,'head'=4] {'seq'}, dimensions={0} | all-to-all | bytes 393216 | tf_op jit(solution)/shard_map/all_to_all | solution.py:48
  163.4 0.1 copy.66
  163.6 7.7 %all_gather.11 = bf16[2,256,768]{1,2,0:T(8,128)(2,1)S(1)} all-gather(bf16[2,256,192]{1,2,0:T(8,128)(2,1)S(1)} %copy.66), channel_id=1, replica_groups=mesh['seq'=8,'head'=4] {'head'}, dimensions={2}, use_global_device_ids=true | all-gather | bytes 983040 | tf_op jit(solution)/shard_map/all_gather | solution.py:104
  171.2 0.4 fusion.8
  171.6 0.8 copy.68
  (10 shorter events, 0.1 us)
Async XLA Ops:
  6.5 1.8 copy-start
  6.5 81.8 %all-reduce.3.cloned.1.call-start = ((), (), s32[]{:S(2)}) async-start(), calls=%async_computation.3 | async-start | bytes 1572864 | tf_op jit(solution)/shard_map/psum | solution.py:73
  8.3 0.9 copy-start.4
  11.8 111.8 %all-to-all-start.1 = ((bf16[2,8,32,1]{2,0,3,1:T(2,128)(2,1)}), bf16[2,8,32,1]{2,0,3,1:T(2,128)(2,1)S(1)}, u32[]{:S(2)}, u32[]{:S(2)}) async-start(bf16[2,8,32,1]{2,0,3,1:T(2,128)(2,1)} %broadcast_in_dim.8), calls=%async_computation.1 | async-start | bytes 8192 | tf_op jit(solution)/shard_map/all_to_all | solution.py:94
  89.8 11.3 %copy-start.1 = (bf16[192,768]{1,0:T(8,128)(2,1)S(1)}, bf16[192,768]{1,0:T(8,128)(2,1)}, u32[]{:S(2)}) copy-start(bf16[192,768]{1,0:T(8,128)(2,1)} %param.11) | copy-start | bytes 884740
  101.7 15.3 %copy-start.3 = (bf16[3,192,768]{2,1,0:T(8,128)(2,1)S(1)}, bf16[3,192,768]{2,1,0:T(8,128)(2,1)}, u32[]{:S(2)}) copy-start(bf16[3,192,768]{2,1,0:T(8,128)(2,1)} %param.12) | copy-start | bytes 2654212
  123.6 21.6 %all-to-all-start = ((bf16[2,8,32,576]{3,2,0,1:T(8,128)(2,1)}), bf16[2,8,32,576]{3,2,0,1:T(8,128)(2,1)S(1)}, u32[]{:S(2)}, u32[]{:S(2)}) async-start(bf16[2,8,32,576]{3,2,0,1:T(8,128)(2,1)} %copy.58), calls=%async_computation | async-start | bytes 1310720 | tf_op jit(solution)/shard_map/all_to_all | solution.py:93
  150.5 20.7 %copy-start.2 = (bf16[192,768]{1,0:T(8,128)(2,1)S(1)}, bf16[192,768]{1,0:T(8,128)(2,1)}, u32[]{:S(2)}) copy-start(bf16[192,768]{1,0:T(8,128)(2,1)} %param.13) | copy-start | bytes 884740
Sparse Core Ops, SparseCore 0:
  10.8 77.5 all-reduce.2
where the time goes:
time: 180 us; the launch traced here: 179 us
  blocking collectives  66.3 us (37%)
  waiting for transfers between devices  63.7 us (35%)
  between operations  14.2 us (8%)
  matrix products  13.2 us (7%)
  starting transfers between devices  11 us (6%)
  local copies, waits for them, and re-layouts  8.18 us (5%)
  other arithmetic  2.73 us (2%)
    psum x1, waiting for transfers between devices, body(): total, count = lax.psum((partial_scores, count_here), 'seq')  46 us
    psum x1, blocking collectives, body(): total, count = lax.psum((partial_scores, count_here), 'seq')  22.6 us
    all_to_all x1, waiting for transfers between devices, body(): lax.all_to_all(packed, 'seq', split_axis=1, concat_axis=0, tiled=True)  17.7 us
    all_to_all x1, blocking collectives, send_back(): lax.all_to_all(context[:, None], 'seq', split_axis=0, concat_axis=1, tile...  12.5 us
    all_gather x1, blocking collectives, body(): lax.all_gather(row_context, 'head', axis=2, tiled=True)  8.57 us
    all_gather x1, blocking collectives, body(): normed_full = lax.all_gather(normed_here, 'head', axis=2, tiled=True)  8.57 us
    all_gather x1, blocking collectives, body(): lax.all_gather(column_out, 'head', axis=2, tiled=True)  7.66 us
    all_to_all x1, starting transfers between devices, body(): lax.all_to_all(live_tile, 'seq', split_axis=1, concat_axis=0, tiled=True)  7.29 us
  transfers between devices with their start and end apart: 3, of which 2 were waited for; matrix products, arithmetic and copies ran while one was open for 7% of the time, Pallas kernels for 0%

commit v1 on v0

v1 whole, which is shorter than its diff:
```python
import functools

import jax
import jax.numpy as jnp
from jax import lax
from jax.experimental import pallas as pl
from jax.experimental.pallas import tpu as pltpu
from jax.sharding import PartitionSpec as P

HEAD_DIM = 64
EPS = 1e-05
LANES = 128
CODES = 64
TABLE_ROWS = 48

f32 = jnp.float32
bf16 = jnp.bfloat16


def layer_norm(values):
    mean = jnp.mean(values, axis=-1, keepdims=True)
    centred = values - mean
    spread = jnp.mean(centred * centred, axis=-1, keepdims=True)
    return centred * lax.rsqrt(spread + EPS)


def softmax_last(scores):
    top = jnp.max(scores, axis=-1, keepdims=True)
    weights = jnp.exp(scores - top)
    return weights / jnp.sum(weights, axis=-1, keepdims=True)


def dot_nt(left, right):
    return lax.dot_general(left, right, (((1,), (1,)), ((), ())), preferred_element_type=f32)


def dot_nn(left, right):
    return jnp.dot(left, right, preferred_element_type=f32)


def iota(shape, axis):
    return lax.broadcasted_iota(jnp.int32, shape, axis)


def table_kernel(embed_ref, qkv_ref, out_ref):
    vocab = embed_ref.shape[0]
    normed = layer_norm(embed_ref[...].astype(f32)).astype(bf16)
    for t in range(3):
        table = dot_nt(normed, qkv_ref[t])
        out_ref[t] = jnp.zeros(out_ref.shape[1:], bf16)
        out_ref[t, 0:vocab, :] = table.astype(bf16)


def make_tables(embed, row_qkv):
    local_width = row_qkv.shape[1]
    return pl.pallas_call(
        table_kernel,
        out_shape=jax.ShapeDtypeStruct((3, TABLE_ROWS, local_width), bf16),
        name="tables",
    )(embed, row_qkv)


def halves(pair):
    lane = iota(pair.shape, 1)
    zero = jnp.zeros_like(pair)
    return jnp.where(lane < HEAD_DIM, pair, zero), jnp.where(lane < HEAD_DIM, zero, pair)


def spread_pair(pair):
    first, second = halves(pair)
    zero = jnp.zeros_like(pair)
    return jnp.concatenate(
        [
            jnp.concatenate([first, zero], 1),
            jnp.concatenate([zero, first], 1),
            jnp.concatenate([second, zero], 1),
            jnp.concatenate([zero, second], 1),
        ],
        0,
    )


def main_kernel(
    ids_ref,
    tab_ref,
    embed_ref,
    row_out_ref,
    col_qkv_ref,
    context_ref,
    mixed_out_ref,
    table_ref,
    embed2_ref,
    hot_ref,
    own_ref,
    live_own_ref,
    sum_ref,
    spread_ref,
    row_context_ref,
):
    rows = ids_ref.shape[0]
    pairs = rows // 2
    cols = hot_ref.shape[1]
    own = own_ref.shape[0] // pairs
    vocab, width = embed_ref.shape
    heads = width // HEAD_DIM
    parts = tab_ref.shape[0]
    local = tab_ref.shape[3]
    tokens = rows * own
    group = lax.axis_index("seq")
    part = lax.axis_index("head")

    table_ref[...] = jnp.zeros(table_ref.shape, bf16)
    for t in range(3):
        table_ref[t, 0:TABLE_ROWS, :] = jnp.concatenate([tab_ref[p, t] for p in range(parts)], 1)
    embed2_ref[...] = jnp.zeros(embed2_ref.shape, bf16)
    embed2_ref[0:vocab, 0:width] = embed_ref[...]
    embed2_ref[CODES : CODES + vocab, width : 2 * width] = embed_ref[...]

    ids = ids_ref[:, 0:cols]
    live = ids_ref[:, cols : cols + LANES].astype(f32)
    code = iota((CODES, cols), 0)
    for r in range(rows):
        hot = jnp.broadcast_to(ids[r : r + 1, :], (CODES, cols)) == code
        hot_ref[r * CODES : (r + 1) * CODES, :] = hot.astype(f32).astype(bf16)

    pick = (iota((own, cols), 1) == group * own + iota((own, cols), 0)).astype(f32).astype(bf16)
    mine = dot_nt(pick, ids.astype(f32).astype(bf16))
    lane = iota((own, LANES), 1)
    first_half = lane < CODES
    lane_code = jnp.where(first_half, lane, lane - CODES).astype(f32)
    for k in range(pairs):
        value = jnp.where(first_half, mine[:, 2 * k : 2 * k + 1], mine[:, 2 * k + 1 : 2 * k + 2])
        hot = (value == lane_code).astype(f32)
        alive = jnp.where(first_half, live[2 * k : 2 * k + 1, :], live[2 * k + 1 : 2 * k + 2, :])
        own_ref[k * own : (k + 1) * own, :] = hot.astype(bf16)
        live_own_ref[k * own : (k + 1) * own, :] = (hot * alive).astype(bf16)

    depth = rows * CODES
    for hp in range(heads // 2):
        span = slice(hp * LANES, (hp + 1) * LANES)
        queries = spread_pair(table_ref[0, :, span])
        keys = table_ref[1, :, span]
        zero = jnp.zeros_like(keys)
        keys2 = jnp.concatenate(
            [jnp.concatenate([keys, zero], 1), jnp.concatenate([zero, keys], 1)], 0
        )
        scores = dot_nt(queries, keys2)
        high = scores.astype(bf16)
        low = (scores - high.astype(f32)).astype(bf16)
        looked = dot_nn(
            live_own_ref[...],
            jnp.concatenate([high[:LANES], low[:LANES], high[LANES:], low[LANES:]], 1),
        ).astype(bf16)
        for h2 in range(2):
            base = (hp * 2 + h2) * own
            for piece in range(2):
                at = (h2 * 2 + piece) * LANES
                for k in range(pairs):
                    to = piece * depth + k * LANES
                    sum_ref[base : base + own, to : to + LANES] = looked[
                        k * own : (k + 1) * own, at : at + LANES
                    ]
    tied = dot_nn(sum_ref[:, 0:depth], hot_ref[...]) + dot_nn(
        sum_ref[:, depth : 2 * depth], hot_ref[...]
    )
    count = jnp.sum(live, axis=0, keepdims=True)[:, 0:1]
    probs = softmax_last(tied * (HEAD_DIM ** (-0.5) / jnp.sqrt(count))).astype(bf16)

    spread_ref[...] = dot_nt(probs, hot_ref[...]).astype(bf16)
    for hp in range(heads // 2):
        values = spread_pair(table_ref[2, :, hp * LANES : (hp + 1) * LANES])
        weights = jnp.concatenate(
            [
                jnp.concatenate(
                    [
                        spread_ref[
                            (hp * 2 + h2) * own : (hp * 2 + h2 + 1) * own,
                            k * LANES : (k + 1) * LANES,
                        ]
                        for h2 in range(2)
                    ],
                    1,
                )
                for k in range(pairs)
            ],
            0,
        )
        context = dot_nn(weights, values).astype(bf16)
        for k in range(pairs):
            for r2 in range(2):
                at = (2 * k + r2) * own
                row_context_ref[at : at + own, hp * LANES : (hp + 1) * LANES] = context[
                    k * own : (k + 1) * own, r2 * LANES : (r2 + 1) * LANES
                ]

    embedded2 = dot_nn(own_ref[...], embed2_ref[...])
    embedded = jnp.concatenate(
        [
            embedded2[k * own : (k + 1) * own, r2 * width : (r2 + 1) * width]
            for k in range(pairs)
            for r2 in range(2)
        ],
        0,
    )
    mixed = embedded + dot_nt(row_context_ref[...], row_out_ref[...])
    for p in range(parts):

        @pl.when(part == p)
        def _():
            mixed_out_ref[...] = mixed[:, p * local : (p + 1) * local]

    normed = layer_norm(mixed).astype(bf16)

    few = 8
    groups = own // few
    unit = rows * few

    def regroup(values):
        shape = (rows, groups, few, values.shape[1])
        return jnp.swapaxes(values.reshape(shape), 0, 1).reshape(tokens, values.shape[1])

    proj = [
        regroup(dot_nt(normed, col_qkv_ref[t * local : (t + 1) * local, :])).astype(bf16)
        for t in range(3)
    ]
    sub, lan = iota((unit, unit), 0), iota((unit, unit), 1)
    same_column = (sub % few) == (lan % few)
    seq_of_lane = iota((rows, unit), 1) // few
    live_lane = jnp.sum(
        jnp.where(seq_of_lane == iota((rows, unit), 0), live, 0.0), axis=0, keepdims=True
    )
    visible = jnp.logical_and(same_column, jnp.broadcast_to(live_lane, (unit, unit)) > 0)
    blocks = []
    for g in range(groups):
        at = slice(g * unit, (g + 1) * unit)
        pieces = []
        for first in range(0, local, LANES):
            span = slice(first, min(first + LANES, local))
            query, keys, values = (proj[t][at, span] for t in range(3))
            many = query.shape[1] // HEAD_DIM
            result = None
            for h2 in range(many):
                inside = iota(query.shape, 1) // HEAD_DIM == h2
                this = query if many == 1 else jnp.where(inside, query, jnp.zeros_like(query))
                scores = dot_nt(this, keys) * HEAD_DIM ** (-0.5)
                weights = softmax_last(jnp.where(visible, scores, -jnp.inf)).astype(bf16)
                found = dot_nn(weights, values)
                result = found if result is None else jnp.where(inside, found, result)
            pieces.append(result)
        blocks.append(jnp.concatenate(pieces, 1))
    whole = jnp.concatenate(blocks, 0).reshape(groups, rows, few, local)
    context_ref[...] = jnp.swapaxes(whole, 0, 1).reshape(tokens, local).astype(bf16)


def attend(ids, tables, embed, row_out, col_qkv, own):
    rows = ids.shape[0]
    cols = ids.shape[1] - LANES
    width = embed.shape[1]
    heads = width // HEAD_DIM
    local = tables.shape[3]
    tokens = rows * own
    return pl.pallas_call(
        main_kernel,
        out_shape=(
            jax.ShapeDtypeStruct((tokens, local), bf16),
            jax.ShapeDtypeStruct((tokens, local), f32),
        ),
        scratch_shapes=[
            pltpu.VMEM((3, CODES, width), bf16),
            pltpu.VMEM((2 * CODES, 2 * width), bf16),
            pltpu.VMEM((rows * CODES, cols), bf16),
            pltpu.VMEM((rows // 2 * own, LANES), bf16),
            pltpu.VMEM((rows // 2 * own, LANES), bf16),
            pltpu.VMEM((heads * own, 2 * rows * CODES), bf16),
            pltpu.VMEM((heads * own, rows * CODES), bf16),
            pltpu.VMEM((tokens, width), bf16),
        ],
        compiler_params=pltpu.CompilerParams(vmem_limit_bytes=48 * 1024 * 1024),
        name="attend",
    )(ids, tables, embed, row_out, col_qkv)


def finish_kernel(context_ref, col_out_ref, mixed_ref, out_ref):
    parts, _, local = context_ref.shape
    total = mixed_ref[...]
    for p in range(parts):
        total = total + dot_nt(context_ref[p], col_out_ref[:, p * local : (p + 1) * local])
    out_ref[...] = total.astype(bf16)


def finish(contexts, col_out, mixed):
    return pl.pallas_call(
        finish_kernel,
        out_shape=jax.ShapeDtypeStruct(mixed.shape, bf16),
        compiler_params=pltpu.CompilerParams(vmem_limit_bytes=48 * 1024 * 1024),
        name="finish",
    )(contexts, col_out, mixed)


def fast_body(ids, pad_mask, embed, row_qkv, row_out, col_qkv, col_out):
    rows_here, cols = ids.shape
    local = row_out.shape[0]
    groups = lax.axis_size("seq")
    own = cols // groups
    live = jnp.broadcast_to(pad_mask[:, None], (rows_here, LANES))
    ids_all = lax.all_gather(jnp.concatenate([ids, live], 1), "seq", axis=0, tiled=True)
    tables = lax.all_gather(make_tables(embed, row_qkv), "head", axis=0)
    row_out_all = lax.all_gather(row_out, "head", axis=0, tiled=True)
    context, mixed = attend(
        ids_all, tables, embed, row_out_all, col_qkv.reshape(3 * local, -1), own
    )
    contexts = lax.all_gather(context, "head", axis=0)
    out = finish(contexts, col_out, mixed)
    out = out.reshape(groups, rows_here, own, local)
    back = lax.all_to_all(out, "seq", split_axis=0, concat_axis=2, tiled=True)
    return back.reshape(rows_here, cols, local)


def weight_fold(out_weight, piece):
    return jnp.einsum("rce,fe->rcf", piece, out_weight, preferred_element_type=f32)


def attend_columns(query, keys, values, key_live):
    rows_all, count_cols, local_width = query.shape
    heads_here = local_width // HEAD_DIM
    shape = (rows_all, count_cols, heads_here, HEAD_DIM)
    scores = jnp.einsum(
        "rchd,schd->chrs",
        query.reshape(shape),
        keys.reshape(shape),
        preferred_element_type=f32,
    ) * HEAD_DIM ** (-0.5)
    scores = jnp.where(key_live > 0, scores, -jnp.inf)
    probs = softmax_last(scores).astype(bf16)
    context = jnp.einsum(
        "chrs,schd->rchd", probs, values.reshape(shape), preferred_element_type=f32
    )
    return context.astype(bf16).reshape(rows_all, count_cols, local_width)


def send_back(context):
    return lax.all_to_all(context[:, None], "seq", split_axis=0, concat_axis=1, tiled=True)


def general_body(ids, pad_mask, embed, row_qkv, row_out, col_qkv, col_out):
    rows_here, cols = ids.shape
    width = embed.shape[1]
    local_width = row_out.shape[0]
    heads_here = local_width // HEAD_DIM
    groups = lax.axis_size("seq")
    per_group = cols // groups
    codes = lax.broadcasted_iota(jnp.int32, (1, 1, embed.shape[0]), 2)
    onehot = (ids[:, :, None] == codes).astype(bf16)
    embedded = jnp.einsum("rcv,vd->rcd", onehot, embed, preferred_element_type=f32)
    normed = layer_norm(embedded).astype(bf16)
    row_proj = jnp.einsum("rcd,ted->trce", normed, row_qkv, preferred_element_type=f32)
    row_proj = row_proj.astype(bf16)
    live = pad_mask.astype(bf16)
    head_shape = (rows_here, cols, heads_here, HEAD_DIM)
    query = (row_proj[0] * live[:, None, None]).reshape(head_shape)
    keys = row_proj[1].reshape(head_shape)
    values = row_proj[2].reshape(head_shape)
    partial_scores = jnp.einsum("rihd,rjhd->hij", query, keys, preferred_element_type=f32)
    count_here = jnp.sum(pad_mask.astype(f32))
    scale = HEAD_DIM ** (-0.5)
    total, count = lax.psum((partial_scores, count_here), "seq")
    row_probs = softmax_last(total * (scale / jnp.sqrt(count))).astype(bf16)
    row_context = jnp.einsum("hij,rjhd->rihd", row_probs, values, preferred_element_type=f32)
    row_context = row_context.astype(bf16).reshape(rows_here, cols, local_width)
    start_feature = lax.axis_index("head") * local_width
    resident = lax.dynamic_slice_in_dim(embedded, start_feature, local_width, 2)
    row_update = weight_fold(row_out, lax.all_gather(row_context, "head", axis=2, tiled=True))
    mixed = resident + row_update
    sums, squares = lax.psum((jnp.sum(mixed, axis=-1), jnp.sum(mixed * mixed, axis=-1)), "head")
    mean = sums / width
    spread = squares / width - mean * mean
    normed_here = ((mixed - mean[..., None]) * lax.rsqrt(spread[..., None] + EPS)).astype(bf16)
    live_tile = jnp.broadcast_to(live[:, None, None, None], (rows_here, groups, per_group, 1))
    normed_full = lax.all_gather(normed_here, "head", axis=2, tiled=True)
    col_proj = jnp.einsum("rcd,ted->rcte", normed_full, col_qkv, preferred_element_type=f32)
    packed = col_proj.astype(bf16).reshape(rows_here, groups, per_group, 3 * local_width)
    received = lax.all_to_all(packed, "seq", split_axis=1, concat_axis=0, tiled=True)
    mask_part = lax.all_to_all(live_tile, "seq", split_axis=1, concat_axis=0, tiled=True)
    column_out = send_back(
        attend_columns(
            received[:, 0, :, :local_width],
            received[:, 0, :, local_width : 2 * local_width],
            received[:, 0, :, 2 * local_width :],
            mask_part[:, 0, 0, 0],
        )
    )
    column_out = column_out.reshape(rows_here, cols, local_width)
    col_update = weight_fold(col_out, lax.all_gather(column_out, "head", axis=2, tiled=True))
    return (mixed + col_update).astype(bf16)


def body(ids, pad_mask, embed, row_qkv, row_out, col_qkv, col_out):
    rows_here, cols = ids.shape
    groups = lax.axis_size("seq")
    own, rows = cols // groups, rows_here * groups
    fits = own % 16 == 0 and rows * 8 == LANES and embed.shape[0] <= TABLE_ROWS
    chosen = fast_body if fits else general_body
    return chosen(ids, pad_mask, embed, row_qkv, row_out, col_qkv, col_out)


def solution(mesh):
    placed = (
        P("seq", None),
        P("seq"),
        P(),
        P(None, "head", None),
        P("head", None),
        P(None, "head", None),
        P("head", None),
    )
    return jax.shard_map(
        body, mesh=mesh, in_specs=placed, out_specs=P("seq", None, "head"), check_vma=False
    )
```

time: 180 us -> 93.4 us (0.52)
  waiting for transfers between devices: 63.7 us -> 0.71 us
  matrix products: 13.2 us -> 0 us
  Pallas kernels: 0 us -> 12.2 us
  starting transfers between devices: 11 us -> 0.01 us
  local copies, waits for them, and re-layouts: 8.18 us -> 2.86 us
  blocking collectives: 66.3 us -> 63.3 us
  other arithmetic: 2.73 us -> 0.68 us
    psum x1 -> x0, waiting for transfers between devices: 46 us -> none  [body(): total, count = lax.psum((partial_scores, count_here), 'seq')]
    psum x2 -> x0, blocking collectives: 28.9 us -> none  [the longest x1 22.6 us: body(): total, count = lax.psum((partial_scores, count_here), 'seq')]
    all_gather x3, blocking collectives: 24.8 us -> 48.7 us  [the longest x1 32.1 us: fast_body(): lax.all_gather(jnp.concatenate([ids, live], 1), 'seq', axis=0, tiled=True)]
    all_to_all x2 -> x0, waiting for transfers between devices: 17.7 us -> none  [the longest x1 17.7 us: body(): lax.all_to_all(packed, 'seq', split_axis=1, concat_axis=0, tiled=True)]
    dot_general x9 -> x0, matrix products: 12.2 us -> none  [the longest x1 2.67 us: body(): jnp.einsum('hij,rjhd->rihd', row_probs, values, preferred_element_type=jn...]
    pallas_call x0 -> x3, Pallas kernels: none -> 12.2 us  [the longest x1 9.36 us: attend(): pl.pallas_call(main_kernel, out_shape=(jax.ShapeDtypeStruct((tokens, loca...]
    all_to_all x2 -> x0, starting transfers between devices: 11 us -> none  [the longest x1 7.29 us: body(): lax.all_to_all(live_tile, 'seq', split_axis=1, concat_axis=0, tiled=True)]
    reshape x3 -> x1, local copies, waits for them, and re-layouts: 3.69 us -> 0.82 us  [fast_body(): return back.reshape(rows_here, cols, local)]
  transfers between devices with their start and end apart: 3 -> 1, of which waited for: 2 -> 0; matrix products, arithmetic and copies ran while one was open for 7% -> 2% of each run, Pallas kernels for 0% -> 3%
where the time goes in v1:
time: 93.4 us; the launch traced here: 93.2 us
  blocking collectives  63.3 us (68%)
  between operations  13.4 us (14%)
  Pallas kernels  12.2 us (13%)
  local copies, waits for them, and re-layouts  2.86 us (3%)
    all_gather x1, blocking collectives, fast_body(): lax.all_gather(jnp.concatenate([ids, live], 1), 'seq', axis=0, tiled=True)  32.1 us
    all_to_all x1, blocking collectives, fast_body(): back = lax.all_to_all(out, 'seq', split_axis=0, concat_axis=2, tiled=True)  14.6 us
    all_gather x1, blocking collectives, fast_body(): contexts = lax.all_gather(context, 'head', axis=0)  10.4 us
    pallas_call x1, Pallas kernels, attend(): pl.pallas_call(main_kernel, out_shape=(jax.ShapeDtypeStruct((tokens, loca...  9.36 us
    all_gather x1, blocking collectives, fast_body(): tables = lax.all_gather(make_tables(embed, row_qkv), 'head', axis=0)  6.12 us
    pallas_call x1, Pallas kernels, make_tables(): pl.pallas_call(table_kernel, out_shape=jax.ShapeDtypeStruct((3, TABLE_ROW...  2.38 us
  transfers between devices with their start and end apart: 1, of which 0 were waited for; matrix products, arithmetic and copies ran while one was open for 2% of the time, Pallas kernels for 3%

profile of v1, /device:TPU:0, one launch (start us, length us, event | category | flops | bytes accessed | tf_op | source)
XLA Modules:
  0.0 93.2 jit_solution(17146038524076123414)
XLA Ops:
  6.5 0.0 copy-start.3
  6.5 0.0 copy-start.1
  6.5 0.0 all-gather.5.cloned.1.call-start
  6.5 0.7 all-gather.5.cloned.1.call-update
  7.3 0.7 broadcast_in_dim.2
  8.0 0.7 add_bitcast_fusion
  8.7 32.1 %all-gather.2 = s32[8,2,384]{2,1,0:T(2,128)S(1)} all-gather(s32[1,2,384]{2,1,0:T(2,128)S(1)} %add_bitcast_fusion), channel_id=1, replica_groups=mesh['seq'=8,'head'=4] {'seq'}, dimensions={0}, use_global_device_ids=true | all-gather | bytes 27648 | tf_op jit(solution)/shard_map/all_gather | solution.py:306
  40.8 2.4 %tables.1 = bf16[3,48,192]{2,1,0:T(8,128)(2,1)} custom-call(bf16[33,768]{1,0:T(8,128)(2,1)} %embed_ref.3, bf16[3,192,768]{2,1,0:T(8,128)(2,1)} %qkv_ref.1), custom_call_target="tpu_custom_call" | custom-call | tf_op jit(solution)/shard_map/tables/pallas_call | solution.py:56
  43.2 6.1 %all-gather = bf16[12,48,192]{2,1,0:T(8,128)(2,1)S(1)} all-gather(bf16[3,48,192]{2,1,0:T(8,128)(2,1)} %tables.1), channel_id=2, replica_groups=mesh['seq'=8,'head'=4] {'head'}, dimensions={0}, use_global_device_ids=true | all-gather | bytes 276480 | tf_op jit(solution)/shard_map/all_gather | solution.py:307
  49.3 0.0 all-gather.5.cloned.1.call-done.row_out_ref
  49.3 0.0 copy-done.3
  49.3 0.0 copy-done.1
  49.3 0.0 copy-start
  49.3 1.3 %copy-done = bf16[768,768]{1,0:T(8,128)(2,1)S(1)} copy-done((bf16[768,768]{1,0:T(8,128)(2,1)S(1)}, bf16[768,768]{1,0:T(8,128)(2,1)}, u32[]{:S(2)}) %copy-start) | copy-done | bytes 1179672
  50.6 9.4 %attend.1 = (bf16[512,192]{1,0:T(8,128)(2,1)S(1)}, f32[512,192]{1,0:T(8,128)S(1)}) custom-call(s32[16,384]{1,0:T(8,128)S(1)} %reshape.17.ids_ref, bf16[4,3,48,192]{3,2,1,0:T(8,128)(2,1)S(1)} %bitcast.11, bf16[33,768]{1,0:T(8,128)(2,1)S(1)} %copy-done.3, bf16[768,768]{1,0:T(8,128)(2,1)S(1)} %copy-done, bf16[576,768]{1,0:T(8,128)(2,1)S(1)} %bitcast.13), custom_call_target="tpu_custom_call" | custom-call | tf_op jit(solution)/shard_map/attend/pallas_call | solution.py:262
  59.9 0.0 copy-start.2
  59.9 10.4 %all-gather.1 = bf16[2048,192]{1,0:T(8,128)(2,1)S(1)} all-gather(bf16[512,192]{1,0:T(8,128)(2,1)S(1)} %get-tuple-element.7), channel_id=3, replica_groups=mesh['seq'=8,'head'=4] {'head'}, dimensions={0}, use_global_device_ids=true | all-gather | bytes 983040 | tf_op jit(solution)/shard_map/all_gather | solution.py:312
  70.4 0.0 copy-done.2
  70.4 0.5 finish.1
  70.8 14.6 %all_to_all.15 = bf16[8,2,32,192]{3,2,1,0:T(8,128)(2,1)S(1)} all-to-all(bf16[8,2,32,192]{3,2,1,0:T(8,128)(2,1)S(1)} %bitcast.12), channel_id=1, replica_groups=mesh['seq'=8,'head'=4] {'seq'}, dimensions={0} | all-to-all | bytes 393216 | tf_op jit(solution)/shard_map/all_to_all | solution.py:315
  85.5 0.8 copy.12
  (2 shorter events, 0.0 us)
Async XLA Ops:
  6.5 42.8 %copy-start.3 = (bf16[33,768]{1,0:T(8,128)(2,1)S(1)}, bf16[33,768]{1,0:T(8,128)(2,1)}, u32[]{:S(2)}) copy-start(bf16[33,768]{1,0:T(8,128)(2,1)} %embed_ref.3) | copy-start | bytes 152068
  6.5 42.8 %copy-start.1 = (bf16[3,192,768]{2,1,0:T(8,128)(2,1)S(1)}, bf16[3,192,768]{2,1,0:T(8,128)(2,1)}, u32[]{:S(2)}) copy-start(bf16[3,192,768]{2,1,0:T(8,128)(2,1)} %param.12) | copy-start | bytes 2654212
  6.5 42.8 %all-gather.5.cloned.1.call-start = ((), (), s32[]{:S(2)}) async-start(), calls=%async_computation.1 | async-start | bytes 1474560 | tf_op jit(solution)/shard_map/all_gather | solution.py:308
  49.3 1.3 %copy-start = (bf16[768,768]{1,0:T(8,128)(2,1)S(1)}, bf16[768,768]{1,0:T(8,128)(2,1)}, u32[]{:S(2)}) copy-start(bf16[768,768]{1,0:T(8,128)(2,1)} %all-gather.5.cloned.1.call-done.row_out_ref) | copy-start | bytes 3538948
  59.9 10.4 %copy-start.2 = (bf16[192,768]{1,0:T(8,128)(2,1)S(1)}, bf16[192,768]{1,0:T(8,128)(2,1)}, u32[]{:S(2)}) copy-start(bf16[192,768]{1,0:T(8,128)(2,1)} %col_out_ref.1) | copy-start | bytes 884740
Sparse Core Ops, SparseCore 0:
  8.9 20.1 all-gather.4

commit v2 on v1

--- a/solution.py
+++ b/solution.py
@@ -80,35 +80,49 @@
     )
 
 
-def main_kernel(
-    ids_ref,
-    tab_ref,
-    embed_ref,
-    row_out_ref,
-    col_qkv_ref,
-    context_ref,
-    mixed_out_ref,
-    table_ref,
-    embed2_ref,
-    hot_ref,
-    own_ref,
-    live_own_ref,
-    sum_ref,
-    spread_ref,
-    row_context_ref,
-):
-    rows = ids_ref.shape[0]
+def main_kernel(groups, parts, *refs):
+    ids_refs, refs = refs[:groups], refs[groups:]
+    tab_refs, refs = refs[:parts], refs[parts:]
+    row_out_refs, refs = refs[:parts], refs[parts:]
+    (
+        embed_ref,
+        col_qkv_hbm,
+        context_ref,
+        mixed_out_ref,
+        tab_ref,
+        row_out_ref,
+        col_qkv_ref,
+        table_ref,
+        embed2_ref,
+        hot_ref,
+        own_ref,
+        live_own_ref,
+        sum_ref,
+        spread_ref,
+        row_context_ref,
+        weight_sem,
+    ) = refs
+    rows = ids_refs[0].shape[0] * groups
     pairs = rows // 2
     cols = hot_ref.shape[1]
     own = own_ref.shape[0] // pairs
     vocab, width = embed_ref.shape
     heads = width // HEAD_DIM
-    parts = tab_ref.shape[0]
     local = tab_ref.shape[3]
     tokens = rows * own
     group = lax.axis_index("seq")
     part = lax.axis_index("head")
 
+    loads = [
+        pltpu.make_async_copy(row_out_refs[p], row_out_ref.at[part ^ p], weight_sem.at[p])
+        for p in range(parts)
+    ]
+    loads.append(pltpu.make_async_copy(col_qkv_hbm, col_qkv_ref, weight_sem.at[parts]))
+    for load in loads:
+        load.start()
+
+    for p in range(parts):
+        tab_ref[part ^ p] = tab_refs[p][...]
     table_ref[...] = jnp.zeros(table_ref.shape, bf16)
     for t in range(3):
         table_ref[t, 0:TABLE_ROWS, :] = jnp.concatenate([tab_ref[p, t] for p in range(parts)], 1)
@@ -116,8 +130,9 @@
     embed2_ref[0:vocab, 0:width] = embed_ref[...]
     embed2_ref[CODES : CODES + vocab, width : 2 * width] = embed_ref[...]
 
-    ids = ids_ref[:, 0:cols]
-    live = ids_ref[:, cols : cols + LANES].astype(f32)
+    coded = jnp.concatenate([ref[...] for ref in ids_refs], 0)
+    ids = coded & 0xFFFF
+    live = (coded[:, 0:LANES] >> 16).astype(f32)
     code = iota((CODES, cols), 0)
     for r in range(rows):
         hot = jnp.broadcast_to(ids[r : r + 1, :], (CODES, cols)) == code
@@ -202,7 +217,9 @@
         ],
         0,
     )
-    mixed = embedded + dot_nt(row_context_ref[...], row_out_ref[...])
+    for load in loads[:parts]:
+        load.wait()
+    mixed = embedded + dot_nt(row_context_ref[...], row_out_ref[...].reshape(width, width))
     for p in range(parts):
 
         @pl.when(part == p)
@@ -219,6 +236,7 @@
         shape = (rows, groups, few, values.shape[1])
         return jnp.swapaxes(values.reshape(shape), 0, 1).reshape(tokens, values.shape[1])
 
+    loads[parts].wait()
     proj = [
         regroup(dot_nt(normed, col_qkv_ref[t * local : (t + 1) * local, :])).astype(bf16)
         for t in range(3)
@@ -252,20 +270,28 @@
     context_ref[...] = jnp.swapaxes(whole, 0, 1).reshape(tokens, local).astype(bf16)
 
 
-def attend(ids, tables, embed, row_out, col_qkv, own):
-    rows = ids.shape[0]
-    cols = ids.shape[1] - LANES
+def attend(ids, tables, embed, row_outs, col_qkv):
+    groups, parts = len(ids), len(tables)
+    rows_here, cols = ids[0].shape
+    own = cols // groups
+    rows = rows_here * groups
     width = embed.shape[1]
     heads = width // HEAD_DIM
-    local = tables.shape[3]
+    local = tables[0].shape[2]
     tokens = rows * own
+    vmem = pl.BlockSpec(memory_space=pltpu.VMEM)
+    hbm = pl.BlockSpec(memory_space=pl.ANY)
     return pl.pallas_call(
-        main_kernel,
+        functools.partial(main_kernel, groups, parts),
         out_shape=(
             jax.ShapeDtypeStruct((tokens, local), bf16),
             jax.ShapeDtypeStruct((tokens, local), f32),
         ),
+        in_specs=[vmem] * (groups + parts) + [hbm] * parts + [vmem, hbm],
         scratch_shapes=[
+            pltpu.VMEM((parts, 3, TABLE_ROWS, local), bf16),
+            pltpu.VMEM((parts, local, width), bf16),
+            pltpu.VMEM((3 * local, width), bf16),
             pltpu.VMEM((3, CODES, width), bf16),
             pltpu.VMEM((2 * CODES, 2 * width), bf16),
             pltpu.VMEM((rows * CODES, cols), bf16),
@@ -274,46 +300,77 @@
             pltpu.VMEM((heads * own, 2 * rows * CODES), bf16),
             pltpu.VMEM((heads * own, rows * CODES), bf16),
             pltpu.VMEM((tokens, width), bf16),
+            pltpu.SemaphoreType.DMA((parts + 1,)),
         ],
         compiler_params=pltpu.CompilerParams(vmem_limit_bytes=48 * 1024 * 1024),
         name="attend",
-    )(ids, tables, embed, row_out, col_qkv)
-
-
-def finish_kernel(context_ref, col_out_ref, mixed_ref, out_ref):
-    parts, _, local = context_ref.shape
+    )(*ids, *tables, *row_outs, embed, col_qkv)
+
+
+def finish_kernel(parts, *refs):
+    context_refs = refs[:parts]
+    col_out_ref, mixed_ref, out_ref, weight_ref = refs[parts:]
+    local = mixed_ref.shape[1]
+    part = lax.axis_index("head")
+    for p in range(parts):
+        weight_ref[p] = col_out_ref[:, p * local : (p + 1) * local]
     total = mixed_ref[...]
     for p in range(parts):
-        total = total + dot_nt(context_ref[p], col_out_ref[:, p * local : (p + 1) * local])
+        total = total + dot_nt(context_refs[p][...], weight_ref[part ^ p])
     out_ref[...] = total.astype(bf16)
 
 
 def finish(contexts, col_out, mixed):
+    parts = len(contexts)
+    local = mixed.shape[1]
     return pl.pallas_call(
-        finish_kernel,
+        functools.partial(finish_kernel, parts),
         out_shape=jax.ShapeDtypeStruct(mixed.shape, bf16),
+        scratch_shapes=[pltpu.VMEM((parts, local, local), bf16)],
         compiler_params=pltpu.CompilerParams(vmem_limit_bytes=48 * 1024 * 1024),
         name="finish",
-    )(contexts, col_out, mixed)
+    )(*contexts, col_out, mixed)
+
+
+def order_kernel(groups, *refs):
+    out_ref = refs[groups]
+    group = lax.axis_index("seq")
+    for d in range(groups):
+        out_ref[:, group ^ d] = refs[d][...]
+
+
+def order(blocks):
+    groups = len(blocks)
+    rows_here, own, local = blocks[0].shape
+    return pl.pallas_call(
+        functools.partial(order_kernel, groups),
+        out_shape=jax.ShapeDtypeStruct((rows_here, groups, own, local), bf16),
+        name="order",
+    )(*blocks)
+
+
+def exchange(value, axis, step):
+    if step == 0:
+        return value
+    count = lax.axis_size(axis)
+    return lax.ppermute(value, axis, [(i, i ^ step) for i in range(count)])
 
 
 def fast_body(ids, pad_mask, embed, row_qkv, row_out, col_qkv, col_out):
     rows_here, cols = ids.shape
     local = row_out.shape[0]
-    groups = lax.axis_size("seq")
+    groups, parts = lax.axis_size("seq"), lax.axis_size("head")
     own = cols // groups
-    live = jnp.broadcast_to(pad_mask[:, None], (rows_here, LANES))
-    ids_all = lax.all_gather(jnp.concatenate([ids, live], 1), "seq", axis=0, tiled=True)
-    tables = lax.all_gather(make_tables(embed, row_qkv), "head", axis=0)
-    row_out_all = lax.all_gather(row_out, "head", axis=0, tiled=True)
-    context, mixed = attend(
-        ids_all, tables, embed, row_out_all, col_qkv.reshape(3 * local, -1), own
-    )
-    contexts = lax.all_gather(context, "head", axis=0)
-    out = finish(contexts, col_out, mixed)
-    out = out.reshape(groups, rows_here, own, local)
-    back = lax.all_to_all(out, "seq", split_axis=0, concat_axis=2, tiled=True)
-    return back.reshape(rows_here, cols, local)
+    coded = ids + 65536 * pad_mask[:, None]
+    row_outs = [exchange(row_out, "head", p) for p in range(parts)]
+    codes = [exchange(coded, "seq", d) for d in range(groups)]
+    mine = make_tables(embed, row_qkv)
+    tables = [exchange(mine, "head", p) for p in range(parts)]
+    context, mixed = attend(codes, tables, embed, row_outs, col_qkv.reshape(3 * local, -1))
+    contexts = [exchange(context, "head", p) for p in range(parts)]
+    out = finish(contexts, col_out, mixed).reshape(groups, rows_here, own, local)
+    blocks = [exchange(out[d], "seq", d) for d in range(groups)]
+    return order(blocks).reshape(rows_here, cols, local)
 
 
 def weight_fold(out_weight, piece):
@@ -398,7 +455,8 @@
     rows_here, cols = ids.shape
     groups = lax.axis_size("seq")
     own, rows = cols // groups, rows_here * groups
-    fits = own % 16 == 0 and rows * 8 == LANES and embed.shape[0] <= TABLE_ROWS
+    paired = groups & (groups - 1) == 0 and lax.axis_size("head") in (2, 4)
+    fits = paired and own % 16 == 0 and rows * 8 == LANES and embed.shape[0] <= TABLE_ROWS
     chosen = fast_body if fits else general_body
     return chosen(ids, pad_mask, embed, row_qkv, row_out, col_qkv, col_out)
 

time: 93.4 us -> 89.5 us (0.958)
  blocking collectives: 63.3 us -> 0 us
  waiting for transfers between devices: 0.71 us -> 36.9 us
  starting transfers between devices: 0.01 us -> 32.6 us
  between operations: 13.4 us -> 0.13 us
  Pallas kernels: 12.2 us -> 14.6 us
  local copies, waits for them, and re-layouts: 2.86 us -> 4.85 us
    all_gather x3 -> x0, blocking collectives: 48.7 us -> none  [the longest x1 32.1 us: fast_body(): lax.all_gather(jnp.concatenate([ids, live], 1), 'seq', axis=0, tiled=True)]
    ppermute x0 -> x23, waiting for transfers between devices: none -> 36.9 us  [exchange(): return lax.ppermute(value, axis, [(i, i ^ step) for i in range(count)])]
    ppermute x0 -> x23, starting transfers between devices: none -> 32.6 us  [exchange(): return lax.ppermute(value, axis, [(i, i ^ step) for i in range(count)])]
    all_to_all x1 -> x0, blocking collectives: 14.6 us -> none  [fast_body(): back = lax.all_to_all(out, 'seq', split_axis=0, concat_axis=2, tiled=True)]
    pallas_call x2 -> x3, Pallas kernels: 9.81 us -> 12.2 us  [the longest x1 10.1 us: attend(): pl.pallas_call(functools.partial(main_kernel, groups, parts), out_shape=(...]
    unnamed x9 -> x28, local copies, waits for them, and re-layouts: 1.3 us -> 2.45 us
    reshape x1, local copies, waits for them, and re-layouts: 0.82 us -> 1.76 us  [fast_body(): return order(blocks).reshape(rows_here, cols, local)]
  transfers between devices with their start and end apart: 1 -> 23, of which waited for: 0 -> 13; matrix products, arithmetic and copies ran while one was open for 2% -> 0% of each run, Pallas kernels for 3% -> 3%
where the time goes in v2:
time: 89.5 us; the launch traced here: 89.2 us
  waiting for transfers between devices  36.9 us (41%)
  starting transfers between devices  32.6 us (36%)
  Pallas kernels  14.6 us (16%)
  local copies, waits for them, and re-layouts  4.85 us (5%)
    ppermute x23, waiting for transfers between devices, exchange(): return lax.ppermute(value, axis, [(i, i ^ step) for i in range(count)])  36.9 us
    ppermute x23, starting transfers between devices, exchange(): return lax.ppermute(value, axis, [(i, i ^ step) for i in range(count)])  32.6 us
    pallas_call x1, Pallas kernels, attend(): pl.pallas_call(functools.partial(main_kernel, groups, parts), out_shape=(...  10.1 us
    unnamed x28, local copies, waits for them, and re-layouts  2.45 us
    pallas_call x1, Pallas kernels, make_tables(): pl.pallas_call(table_kernel, out_shape=jax.ShapeDtypeStruct((3, TABLE_ROW...  2.39 us
  transfers between devices with their start and end apart: 23, of which 13 were waited for; matrix products, arithmetic and copies ran while one was open for 0% of the time, Pallas kernels for 3%

profile of v2, /device:TPU:0, one launch (start us, length us, event | category | flops | bytes accessed | tf_op | source)
XLA Modules:
  0.0 89.2 jit_solution(8134152930594689551)
XLA Ops:
  0.0 3.0 %collective-permute-start.11 = (bf16[192,768]{1,0:T(8,128)(2,1)}, bf16[192,768]{1,0:T(8,128)(2,1)S(1)}, u32[]{:S(2)}, u32[]{:S(2)}) collective-permute-start(bf16[192,768]{1,0:T(8,128)(2,1)} %refs_12_.1), channel_id=1, source_target_pairs={{0,2},{1,3},{2,0},{3,1},{4,6},{5,7},{6,4},{7,5},{8,10},{9,11},{10,... | collective-permute-start | bytes 884744 | tf_op jit(solution)/shard_map/ppermute | solution.py:356
  3.0 0.2 collective-permute-start.12
  3.2 2.4 %tables.1.refs_8_ = bf16[3,48,192]{2,1,0:T(8,128)(2,1)} custom-call(bf16[33,768]{1,0:T(8,128)(2,1)} %refs_16_.1, bf16[3,192,768]{2,1,0:T(8,128)(2,1)} %qkv_ref.1), custom_call_target="tpu_custom_call" | custom-call | tf_op jit(solution)/shard_map/tables/pallas_call | solution.py:56
  5.6 1.5 %collective-permute-start.9 = (bf16[3,48,192]{2,1,0:T(8,128)(2,1)}, bf16[3,48,192]{2,1,0:T(8,128)(2,1)S(1)}, u32[]{:S(2)}, u32[]{:S(2)}) collective-permute-start(bf16[3,48,192]{2,1,0:T(8,128)(2,1)} %tables.1.refs_8_), channel_id=1, source_target_pairs={{0,3},{1,2},{2,1},{3,0},{4,7},{5,6},{6,5},{7,4},{8,11},{9,10},{10,... | collective-permute-start | bytes 165896 | tf_op jit(solution)/shard_map/ppermute | solution.py:356
  7.2 0.1 broadcast_add_fusion.refs_0_
  7.2 4.6 %collective-permute-start.6 = (s32[2,256]{1,0:T(2,128)S(1)}, s32[2,256]{1,0:T(2,128)S(1)}, u32[]{:S(2)}, u32[]{:S(2)}) collective-permute-start(s32[2,256]{1,0:T(2,128)S(1)} %broadcast_add_fusion.refs_0_), channel_id=1, source_target_pairs={{0,28},{4,24},{8,20},{12,16},{16,12},{20,8},{24,4},{28,0},{1,29},{... | collective-permute-start | bytes 6152 | tf_op jit(solution)/shard_map/ppermute | solution.py:356
  11.8 1.7 %collective-permute-done.6.refs_7_ = s32[2,256]{1,0:T(2,128)S(1)} collective-permute-done((s32[2,256]{1,0:T(2,128)S(1)}, s32[2,256]{1,0:T(2,128)S(1)}, u32[]{:S(2)}, u32[]{:S(2)}) %collective-permute-start.6) | collective-permute-done | bytes 2080 | tf_op jit(solution)/shard_map/ppermute | solution.py:356
  13.5 3.6 %collective-permute-start.5 = (s32[2,256]{1,0:T(2,128)S(1)}, s32[2,256]{1,0:T(2,128)S(1)}, u32[]{:S(2)}, u32[]{:S(2)}) collective-permute-start(s32[2,256]{1,0:T(2,128)S(1)} %broadcast_add_fusion.refs_0_), channel_id=1, source_target_pairs={{0,24},{4,28},{8,16},{12,20},{16,8},{20,12},{24,0},{28,4},{1,25},{... | collective-permute-start | bytes 6152 | tf_op jit(solution)/shard_map/ppermute | solution.py:356
  17.1 1.8 %collective-permute-done.5.refs_6_ = s32[2,256]{1,0:T(2,128)S(1)} collective-permute-done((s32[2,256]{1,0:T(2,128)S(1)}, s32[2,256]{1,0:T(2,128)S(1)}, u32[]{:S(2)}, u32[]{:S(2)}) %collective-permute-start.5) | collective-permute-done | bytes 2080 | tf_op jit(solution)/shard_map/ppermute | solution.py:356
  18.9 0.0 collective-permute-start.4
  18.9 5.4 %collective-permute-done.4.refs_5_ = s32[2,256]{1,0:T(2,128)S(1)} collective-permute-done((s32[2,256]{1,0:T(2,128)S(1)}, s32[2,256]{1,0:T(2,128)S(1)}, u32[]{:S(2)}, u32[]{:S(2)}) %collective-permute-start.4) | collective-permute-done | bytes 2080 | tf_op jit(solution)/shard_map/ppermute | solution.py:356
  24.3 0.1 collective-permute-start.3
  24.3 4.4 %collective-permute-done.3.refs_4_ = s32[2,256]{1,0:T(2,128)S(1)} collective-permute-done((s32[2,256]{1,0:T(2,128)S(1)}, s32[2,256]{1,0:T(2,128)S(1)}, u32[]{:S(2)}, u32[]{:S(2)}) %collective-permute-start.3) | collective-permute-done | bytes 2080 | tf_op jit(solution)/shard_map/ppermute | solution.py:356
  28.8 2.2 %collective-permute-start.2 = (s32[2,256]{1,0:T(2,128)S(1)}, s32[2,256]{1,0:T(2,128)S(1)}, u32[]{:S(2)}, u32[]{:S(2)}) collective-permute-start(s32[2,256]{1,0:T(2,128)S(1)} %broadcast_add_fusion.refs_0_), channel_id=1, source_target_pairs={{0,12},{4,8},{8,4},{12,0},{16,28},{20,24},{24,20},{28,16},{1,13},{... | collective-permute-start | bytes 6152 | tf_op jit(solution)/shard_map/ppermute | solution.py:356
  31.0 2.3 %collective-permute-done.2.refs_3_ = s32[2,256]{1,0:T(2,128)S(1)} collective-permute-done((s32[2,256]{1,0:T(2,128)S(1)}, s32[2,256]{1,0:T(2,128)S(1)}, u32[]{:S(2)}, u32[]{:S(2)}) %collective-permute-start.2) | collective-permute-done | bytes 2080 | tf_op jit(solution)/shard_map/ppermute | solution.py:356
  33.3 1.3 %collective-permute-start.1 = (s32[2,256]{1,0:T(2,128)S(1)}, s32[2,256]{1,0:T(2,128)S(1)}, u32[]{:S(2)}, u32[]{:S(2)}) collective-permute-start(s32[2,256]{1,0:T(2,128)S(1)} %broadcast_add_fusion.refs_0_), channel_id=1, source_target_pairs={{0,8},{4,12},{8,0},{12,4},{16,24},{20,28},{24,16},{28,20},{1,9},{5... | collective-permute-start | bytes 6152 | tf_op jit(solution)/shard_map/ppermute | solution.py:356
  34.6 2.3 %collective-permute-done.1.refs_2_ = s32[2,256]{1,0:T(2,128)S(1)} collective-permute-done((s32[2,256]{1,0:T(2,128)S(1)}, s32[2,256]{1,0:T(2,128)S(1)}, u32[]{:S(2)}, u32[]{:S(2)}) %collective-permute-start.1) | collective-permute-done | bytes 2080 | tf_op jit(solution)/shard_map/ppermute | solution.py:356
  36.8 1.5 %collective-permute-start = (s32[2,256]{1,0:T(2,128)S(1)}, s32[2,256]{1,0:T(2,128)S(1)}, u32[]{:S(2)}, u32[]{:S(2)}) collective-permute-start(s32[2,256]{1,0:T(2,128)S(1)} %broadcast_add_fusion.refs_0_), channel_id=1, source_target_pairs={{0,4},{4,0},{8,12},{12,8},{16,20},{20,16},{24,28},{28,24},{1,5},{5... | collective-permute-start | bytes 6152 | tf_op jit(solution)/shard_map/ppermute | solution.py:356
  38.4 2.1 %collective-permute-done.refs_1_ = s32[2,256]{1,0:T(2,128)S(1)} collective-permute-done((s32[2,256]{1,0:T(2,128)S(1)}, s32[2,256]{1,0:T(2,128)S(1)}, u32[]{:S(2)}, u32[]{:S(2)}) %collective-permute-start) | collective-permute-done | bytes 2080 | tf_op jit(solution)/shard_map/ppermute | solution.py:356
  40.4 0.4 collective-permute-start.8
  40.8 0.0 collective-permute-done.9.refs_11_
  40.8 0.0 collective-permute-start.7
  40.8 4.1 %collective-permute-done.8.refs_10_ = bf16[3,48,192]{2,1,0:T(8,128)(2,1)S(1)} collective-permute-done((bf16[3,48,192]{2,1,0:T(8,128)(2,1)}, bf16[3,48,192]{2,1,0:T(8,128)(2,1)S(1)}, u32[]{:S(2)}, u32[]{:S(2)}) %collective-permute-start.8) | collective-permute-done | bytes 55328 | tf_op jit(solution)/shard_map/ppermute | solution.py:356
  45.0 0.0 collective-permute-done.11.refs_14_
  45.0 0.0 copy-start.1
  45.0 1.0 %copy-done.1 = bf16[192,768]{1,0:T(8,128)(2,1)S(1)} copy-done((bf16[192,768]{1,0:T(8,128)(2,1)S(1)}, bf16[192,768]{1,0:T(8,128)(2,1)}, u32[]{:S(2)}) %copy-start.1) | copy-done | bytes 294936
  46.0 0.9 copy-done.2
  46.9 10.1 %attend.1 = (bf16[512,192]{1,0:T(8,128)(2,1)S(1)}, f32[512,192]{1,0:T(8,128)S(1)}) custom-call(s32[2,256]{1,0:T(2,128)S(1)} %broadcast_add_fusion.refs_0_, s32[2,256]{1,0:T(2,128)S(1)} %collective-permute-done.refs_1_, s32[2,256]{1,0:T(2,128)S(1)} %collective-permute-done.1.refs_2_, s32[2,256]{1,0:T(2,128)S(1)} %collective-permute-done.2.refs_3_, ...), custom_call_target="tpu_custom_call" | custom-call | tf_op jit(solution)/shard_map/attend/pallas_call | solution.py:284
  57.0 0.1 collective-permute-start.15
  57.1 0.5 collective-permute-start.14
  57.5 1.4 %collective-permute-start.13 = (bf16[512,192]{1,0:T(8,128)(2,1)S(1)}, bf16[512,192]{1,0:T(8,128)(2,1)S(1)}, u32[]{:S(2)}, u32[]{:S(2)}) collective-permute-start(bf16[512,192]{1,0:T(8,128)(2,1)S(1)} %get-tuple-element.7.refs_0_), channel_id=1, source_target_pairs={{0,1},{1,0},{2,3},{3,2},{4,5},{5,4},{6,7},{7,6},{8,9},{9,8},{10,11... | collective-permute-start | bytes 589832 | tf_op jit(solution)/shard_map/ppermute | solution.py:356
  58.9 6.7 %collective-permute-done.15.refs_3_ = bf16[512,192]{1,0:T(8,128)(2,1)S(1)} collective-permute-done((bf16[512,192]{1,0:T(8,128)(2,1)S(1)}, bf16[512,192]{1,0:T(8,128)(2,1)S(1)}, u32[]{:S(2)}, u32[]{:S(2)}) %collective-permute-start.15) | collective-permute-done | bytes 196640 | tf_op jit(solution)/shard_map/ppermute | solution.py:356
  65.6 3.6 %collective-permute-done.14.refs_2_ = bf16[512,192]{1,0:T(8,128)(2,1)S(1)} collective-permute-done((bf16[512,192]{1,0:T(8,128)(2,1)S(1)}, bf16[512,192]{1,0:T(8,128)(2,1)S(1)}, u32[]{:S(2)}, u32[]{:S(2)}) %collective-permute-start.14) | collective-permute-done | bytes 196640 | tf_op jit(solution)/shard_map/ppermute | solution.py:356
  69.2 0.6 finish.1
  69.8 0.6 fusion
  70.4 3.9 %collective-permute-start.21 = (bf16[2,32,192]{2,1,0:T(8,128)(2,1)S(1)}, bf16[2,32,192]{2,1,0:T(8,128)(2,1)S(1)}, u32[]{:S(2)}, u32[]{:S(2)}) collective-permute-start(bf16[2,32,192]{2,1,0:T(8,128)(2,1)S(1)} %bitcast.19), channel_id=1, source_target_pairs={{0,24},{4,28},{8,16},{12,20},{16,8},{20,12},{24,0},{28,4},{1,25},{... | collective-permute-start | bytes 73736 | tf_op jit(solution)/shard_map/ppermute | solution.py:356
  74.3 1.2 %collective-permute-start.22 = (bf16[2,32,192]{2,1,0:T(8,128)(2,1)S(1)}, bf16[2,32,192]{2,1,0:T(8,128)(2,1)S(1)}, u32[]{:S(2)}, u32[]{:S(2)}) collective-permute-start(bf16[2,32,192]{2,1,0:T(8,128)(2,1)S(1)} %bitcast.18), channel_id=1, source_target_pairs={{0,28},{4,24},{8,20},{12,16},{16,12},{20,8},{24,4},{28,0},{1,29},{... | collective-permute-start | bytes 73736 | tf_op jit(solution)/shard_map/ppermute | solution.py:356
  75.5 0.4 collective-permute-start.20
  75.8 2.4 %collective-permute-start.19 = (bf16[2,32,192]{2,1,0:T(8,128)(2,1)S(1)}, bf16[2,32,192]{2,1,0:T(8,128)(2,1)S(1)}, u32[]{:S(2)}, u32[]{:S(2)}) collective-permute-start(bf16[2,32,192]{2,1,0:T(8,128)(2,1)S(1)} %bitcast.16), channel_id=1, source_target_pairs={{0,16},{4,20},{8,24},{12,28},{16,0},{20,4},{24,8},{28,12},{1,17},{... | collective-permute-start | bytes 73736 | tf_op jit(solution)/shard_map/ppermute | solution.py:356
  78.2 2.4 %collective-permute-start.18 = (bf16[2,32,192]{2,1,0:T(8,128)(2,1)S(1)}, bf16[2,32,192]{2,1,0:T(8,128)(2,1)S(1)}, u32[]{:S(2)}, u32[]{:S(2)}) collective-permute-start(bf16[2,32,192]{2,1,0:T(8,128)(2,1)S(1)} %bitcast.15), channel_id=1, source_target_pairs={{0,12},{4,8},{8,4},{12,0},{16,28},{20,24},{24,20},{28,16},{1,13},{... | collective-permute-start | bytes 73736 | tf_op jit(solution)/shard_map/ppermute | solution.py:356
  80.5 0.8 collective-permute-start.17
  81.3 1.4 %collective-permute-start.16 = (bf16[2,32,192]{2,1,0:T(8,128)(2,1)S(1)}, bf16[2,32,192]{2,1,0:T(8,128)(2,1)S(1)}, u32[]{:S(2)}, u32[]{:S(2)}) collective-permute-start(bf16[2,32,192]{2,1,0:T(8,128)(2,1)S(1)} %bitcast.13), channel_id=1, source_target_pairs={{0,4},{4,0},{8,12},{12,8},{16,20},{20,16},{24,28},{28,24},{1,5},{5... | collective-permute-start | bytes 73736 | tf_op jit(solution)/shard_map/ppermute | solution.py:356
  82.7 0.9 %collective-permute-done.18.refs_3_ = bf16[2,32,192]{2,1,0:T(8,128)(2,1)S(1)} collective-permute-done((bf16[2,32,192]{2,1,0:T(8,128)(2,1)S(1)}, bf16[2,32,192]{2,1,0:T(8,128)(2,1)S(1)}, u32[]{:S(2)}, u32[]{:S(2)}) %collective-permute-start.18) | collective-permute-done | bytes 24608 | tf_op jit(solution)/shard_map/ppermute | solution.py:356
  83.6 0.8 collective-permute-done.17.refs_2_
  84.5 0.8 collective-permute-done.16.refs_1_
  85.3 0.6 copy-done.11
  85.8 1.6 %order.1 = bf16[2,8,32,192]{3,2,1,0:T(8,128)(2,1)} custom-call(bf16[2,32,192]{2,1,0:T(8,128)(2,1)} %bitcast.12, bf16[2,32,192]{2,1,0:T(8,128)(2,1)} %copy-done.11, bf16[2,32,192]{2,1,0:T(8,128)(2,1)} %copy-done.10, bf16[2,32,192]{2,1,0:T(8,128)(2,1)} %copy-done.9, bf16[2,32,192]{2,1,0:T(8,128)(2,1)} %copy-done.8, bf16[2,32,192]{2,1,0:T(8,128)(2,1)} %copy-done.7, ...), custom_call_target="tpu_custom_call" | custom-call | tf_op jit(solution)/shard_map/order/pallas_call | solution.py:345
  87.4 1.8 %copy.8 = bf16[2,256,192]{1,2,0:T(8,128)(2,1)} copy(bf16[2,256,192]{2,1,0:T(8,128)(2,1)} %bitcast.11) | data formatting | bytes 393216 | tf_op jit(solution)/shard_map/reshape | solution.py:373
  (34 shorter events, 0.1 us)
Async XLA Ops:
  0.0 45.0 %copy-start.4 = (bf16[33,768]{1,0:T(8,128)(2,1)S(1)}, bf16[33,768]{1,0:T(8,128)(2,1)}, u32[]{:S(2)}) copy-start(bf16[33,768]{1,0:T(8,128)(2,1)} %refs_16_.1) | copy-start | bytes 152068
  0.0 7.2 %copy-start.13 = (s32[2]{0:T(128)S(1)}, s32[2]{0:T(128)}, u32[]{:S(2)}) copy-start(s32[2]{0:T(128)} %param.8) | copy-start | bytes 28
  0.0 45.0 %copy-start = (bf16[3,192,768]{2,1,0:T(8,128)(2,1)S(1)}, bf16[3,192,768]{2,1,0:T(8,128)(2,1)}, u32[]{:S(2)}) copy-start(bf16[3,192,768]{2,1,0:T(8,128)(2,1)} %param.12) | copy-start | bytes 2654212
  0.0 45.0 %collective-permute-start.11 = (bf16[192,768]{1,0:T(8,128)(2,1)}, bf16[192,768]{1,0:T(8,128)(2,1)S(1)}, u32[]{:S(2)}, u32[]{:S(2)}) collective-permute-start(bf16[192,768]{1,0:T(8,128)(2,1)} %refs_12_.1), channel_id=1, source_target_pairs={{0,2},{1,3},{2,0},{3,1},{4,6},{5,7},{6,4},{7,5},{8,10},{9,11},{10,... | collective-permute-start | bytes 884744 | tf_op jit(solution)/shard_map/ppermute | solution.py:356
  3.0 42.0 %collective-permute-start.10 = (bf16[192,768]{1,0:T(8,128)(2,1)}, bf16[192,768]{1,0:T(8,128)(2,1)S(1)}, u32[]{:S(2)}, u32[]{:S(2)}) collective-permute-start(bf16[192,768]{1,0:T(8,128)(2,1)} %refs_12_.1), channel_id=1, source_target_pairs={{0,1},{1,0},{2,3},{3,2},{4,5},{5,4},{6,7},{7,6},{8,9},{9,8},{10,11... | collective-permute-start | bytes 884744 | tf_op jit(solution)/shard_map/ppermute | solution.py:356
  3.0 42.0 %collective-permute-start.12 = (bf16[192,768]{1,0:T(8,128)(2,1)}, bf16[192,768]{1,0:T(8,128)(2,1)S(1)}, u32[]{:S(2)}, u32[]{:S(2)}) collective-permute-start(bf16[192,768]{1,0:T(8,128)(2,1)} %refs_12_.1), channel_id=1, source_target_pairs={{0,3},{1,2},{2,1},{3,0},{4,7},{5,6},{6,5},{7,4},{8,11},{9,10},{10,... | collective-permute-start | bytes 884744 | tf_op jit(solution)/shard_map/ppermute | solution.py:356
  3.2 3.9 %copy-start.12 = (s32[2,256]{1,0:T(2,128)S(1)}, s32[2,256]{1,0:T(2,128)}, u32[]{:S(2)}) copy-start(s32[2,256]{1,0:T(2,128)} %param.7) | copy-start | bytes 6148
  5.6 35.2 %collective-permute-start.9 = (bf16[3,48,192]{2,1,0:T(8,128)(2,1)}, bf16[3,48,192]{2,1,0:T(8,128)(2,1)S(1)}, u32[]{:S(2)}, u32[]{:S(2)}) collective-permute-start(bf16[3,48,192]{2,1,0:T(8,128)(2,1)} %tables.1.refs_8_), channel_id=1, source_target_pairs={{0,3},{1,2},{2,1},{3,0},{4,7},{5,6},{6,5},{7,4},{8,11},{9,10},{10,... | collective-permute-start | bytes 165896 | tf_op jit(solution)/shard_map/ppermute | solution.py:356
  7.2 6.3 %collective-permute-start.6 = (s32[2,256]{1,0:T(2,128)S(1)}, s32[2,256]{1,0:T(2,128)S(1)}, u32[]{:S(2)}, u32[]{:S(2)}) collective-permute-start(s32[2,256]{1,0:T(2,128)S(1)} %broadcast_add_fusion.refs_0_), channel_id=1, source_target_pairs={{0,28},{4,24},{8,20},{12,16},{16,12},{20,8},{24,4},{28,0},{1,29},{... | collective-permute-start | bytes 6152 | tf_op jit(solution)/shard_map/ppermute | solution.py:356
  13.5 5.4 %collective-permute-start.5 = (s32[2,256]{1,0:T(2,128)S(1)}, s32[2,256]{1,0:T(2,128)S(1)}, u32[]{:S(2)}, u32[]{:S(2)}) collective-permute-start(s32[2,256]{1,0:T(2,128)S(1)} %broadcast_add_fusion.refs_0_), channel_id=1, source_target_pairs={{0,24},{4,28},{8,16},{12,20},{16,8},{20,12},{24,0},{28,4},{1,25},{... | collective-permute-start | bytes 6152 | tf_op jit(solution)/shard_map/ppermute | solution.py:356
  18.9 5.4 %collective-permute-start.4 = (s32[2,256]{1,0:T(2,128)S(1)}, s32[2,256]{1,0:T(2,128)S(1)}, u32[]{:S(2)}, u32[]{:S(2)}) collective-permute-start(s32[2,256]{1,0:T(2,128)S(1)} %broadcast_add_fusion.refs_0_), channel_id=1, source_target_pairs={{0,20},{4,16},{8,28},{12,24},{16,4},{20,0},{24,12},{28,8},{1,21},{... | collective-permute-start | bytes 6152 | tf_op jit(solution)/shard_map/ppermute | solution.py:356
  24.3 4.5 %collective-permute-start.3 = (s32[2,256]{1,0:T(2,128)S(1)}, s32[2,256]{1,0:T(2,128)S(1)}, u32[]{:S(2)}, u32[]{:S(2)}) collective-permute-start(s32[2,256]{1,0:T(2,128)S(1)} %broadcast_add_fusion.refs_0_), channel_id=1, source_target_pairs={{0,16},{4,20},{8,24},{12,28},{16,0},{20,4},{24,8},{28,12},{1,17},{... | collective-permute-start | bytes 6152 | tf_op jit(solution)/shard_map/ppermute | solution.py:356
  28.8 4.5 %collective-permute-start.2 = (s32[2,256]{1,0:T(2,128)S(1)}, s32[2,256]{1,0:T(2,128)S(1)}, u32[]{:S(2)}, u32[]{:S(2)}) collective-permute-start(s32[2,256]{1,0:T(2,128)S(1)} %broadcast_add_fusion.refs_0_), channel_id=1, source_target_pairs={{0,12},{4,8},{8,4},{12,0},{16,28},{20,24},{24,20},{28,16},{1,13},{... | collective-permute-start | bytes 6152 | tf_op jit(solution)/shard_map/ppermute | solution.py:356
  33.3 3.6 %collective-permute-start.1 = (s32[2,256]{1,0:T(2,128)S(1)}, s32[2,256]{1,0:T(2,128)S(1)}, u32[]{:S(2)}, u32[]{:S(2)}) collective-permute-start(s32[2,256]{1,0:T(2,128)S(1)} %broadcast_add_fusion.refs_0_), channel_id=1, source_target_pairs={{0,8},{4,12},{8,0},{12,4},{16,24},{20,28},{24,16},{28,20},{1,9},{5... | collective-permute-start | bytes 6152 | tf_op jit(solution)/shard_map/ppermute | solution.py:356
  36.8 3.6 %collective-permute-start = (s32[2,256]{1,0:T(2,128)S(1)}, s32[2,256]{1,0:T(2,128)S(1)}, u32[]{:S(2)}, u32[]{:S(2)}) collective-permute-start(s32[2,256]{1,0:T(2,128)S(1)} %broadcast_add_fusion.refs_0_), channel_id=1, source_target_pairs={{0,4},{4,0},{8,12},{12,8},{16,20},{20,16},{24,28},{28,24},{1,5},{5... | collective-permute-start | bytes 6152 | tf_op jit(solution)/shard_map/ppermute | solution.py:356
  40.4 4.6 %collective-permute-start.8 = (bf16[3,48,192]{2,1,0:T(8,128)(2,1)}, bf16[3,48,192]{2,1,0:T(8,128)(2,1)S(1)}, u32[]{:S(2)}, u32[]{:S(2)}) collective-permute-start(bf16[3,48,192]{2,1,0:T(8,128)(2,1)} %tables.1.refs_8_), channel_id=1, source_target_pairs={{0,2},{1,3},{2,0},{3,1},{4,6},{5,7},{6,4},{7,5},{8,10},{9,11},{10,... | collective-permute-start | bytes 165896 | tf_op jit(solution)/shard_map/ppermute | solution.py:356
  40.8 4.2 %collective-permute-start.7 = (bf16[3,48,192]{2,1,0:T(8,128)(2,1)}, bf16[3,48,192]{2,1,0:T(8,128)(2,1)S(1)}, u32[]{:S(2)}, u32[]{:S(2)}) collective-permute-start(bf16[3,48,192]{2,1,0:T(8,128)(2,1)} %tables.1.refs_8_), channel_id=1, source_target_pairs={{0,1},{1,0},{2,3},{3,2},{4,5},{5,4},{6,7},{7,6},{8,9},{9,8},{10,11... | collective-permute-start | bytes 165896 | tf_op jit(solution)/shard_map/ppermute | solution.py:356
  45.0 1.0 %copy-start.1 = (bf16[192,768]{1,0:T(8,128)(2,1)S(1)}, bf16[192,768]{1,0:T(8,128)(2,1)}, u32[]{:S(2)}) copy-start(bf16[192,768]{1,0:T(8,128)(2,1)} %refs_12_.1) | copy-start | bytes 884740
  46.0 0.9 copy-start.2
  46.9 22.3 %copy-start.3 = (bf16[192,768]{1,0:T(8,128)(2,1)S(1)}, bf16[192,768]{1,0:T(8,128)(2,1)}, u32[]{:S(2)}) copy-start(bf16[192,768]{1,0:T(8,128)(2,1)} %refs_4_.1) | copy-start | bytes 884740
  57.0 8.7 %collective-permute-start.15 = (bf16[512,192]{1,0:T(8,128)(2,1)S(1)}, bf16[512,192]{1,0:T(8,128)(2,1)S(1)}, u32[]{:S(2)}, u32[]{:S(2)}) collective-permute-start(bf16[512,192]{1,0:T(8,128)(2,1)S(1)} %get-tuple-element.7.refs_0_), channel_id=1, source_target_pairs={{0,3},{1,2},{2,1},{3,0},{4,7},{5,6},{6,5},{7,4},{8,11},{9,10},{10,... | collective-permute-start | bytes 589832 | tf_op jit(solution)/shard_map/ppermute | solution.py:356
  57.1 12.2 %collective-permute-start.14 = (bf16[512,192]{1,0:T(8,128)(2,1)S(1)}, bf16[512,192]{1,0:T(8,128)(2,1)S(1)}, u32[]{:S(2)}, u32[]{:S(2)}) collective-permute-start(bf16[512,192]{1,0:T(8,128)(2,1)S(1)} %get-tuple-element.7.refs_0_), channel_id=1, source_target_pairs={{0,2},{1,3},{2,0},{3,1},{4,6},{5,7},{6,4},{7,5},{8,10},{9,11},{10,... | collective-permute-start | bytes 589832 | tf_op jit(solution)/shard_map/ppermute | solution.py:356
  57.5 11.7 %collective-permute-start.13 = (bf16[512,192]{1,0:T(8,128)(2,1)S(1)}, bf16[512,192]{1,0:T(8,128)(2,1)S(1)}, u32[]{:S(2)}, u32[]{:S(2)}) collective-permute-start(bf16[512,192]{1,0:T(8,128)(2,1)S(1)} %get-tuple-element.7.refs_0_), channel_id=1, source_target_pairs={{0,1},{1,0},{2,3},{3,2},{4,5},{5,4},{6,7},{7,6},{8,9},{9,8},{10,11... | collective-permute-start | bytes 589832 | tf_op jit(solution)/shard_map/ppermute | solution.py:356
  70.4 10.1 %collective-permute-start.21 = (bf16[2,32,192]{2,1,0:T(8,128)(2,1)S(1)}, bf16[2,32,192]{2,1,0:T(8,128)(2,1)S(1)}, u32[]{:S(2)}, u32[]{:S(2)}) collective-permute-start(bf16[2,32,192]{2,1,0:T(8,128)(2,1)S(1)} %bitcast.19), channel_id=1, source_target_pairs={{0,24},{4,28},{8,16},{12,20},{16,8},{20,12},{24,0},{28,4},{1,25},{... | collective-permute-start | bytes 73736 | tf_op jit(solution)/shard_map/ppermute | solution.py:356
  74.3 7.0 %collective-permute-start.22 = (bf16[2,32,192]{2,1,0:T(8,128)(2,1)S(1)}, bf16[2,32,192]{2,1,0:T(8,128)(2,1)S(1)}, u32[]{:S(2)}, u32[]{:S(2)}) collective-permute-start(bf16[2,32,192]{2,1,0:T(8,128)(2,1)S(1)} %bitcast.18), channel_id=1, source_target_pairs={{0,28},{4,24},{8,20},{12,16},{16,12},{20,8},{24,4},{28,0},{1,29},{... | collective-permute-start | bytes 73736 | tf_op jit(solution)/shard_map/ppermute | solution.py:356
  75.5 7.2 %collective-permute-start.20 = (bf16[2,32,192]{2,1,0:T(8,128)(2,1)S(1)}, bf16[2,32,192]{2,1,0:T(8,128)(2,1)S(1)}, u32[]{:S(2)}, u32[]{:S(2)}) collective-permute-start(bf16[2,32,192]{2,1,0:T(8,128)(2,1)S(1)} %bitcast.17), channel_id=1, source_target_pairs={{0,20},{4,16},{8,28},{12,24},{16,4},{20,0},{24,12},{28,8},{1,21},{... | collective-permute-start | bytes 73736 | tf_op jit(solution)/shard_map/ppermute | solution.py:356
  75.8 6.9 %collective-permute-start.19 = (bf16[2,32,192]{2,1,0:T(8,128)(2,1)S(1)}, bf16[2,32,192]{2,1,0:T(8,128)(2,1)S(1)}, u32[]{:S(2)}, u32[]{:S(2)}) collective-permute-start(bf16[2,32,192]{2,1,0:T(8,128)(2,1)S(1)} %bitcast.16), channel_id=1, source_target_pairs={{0,16},{4,20},{8,24},{12,28},{16,0},{20,4},{24,8},{28,12},{1,17},{... | collective-permute-start | bytes 73736 | tf_op jit(solution)/shard_map/ppermute | solution.py:356
  78.2 5.4 %collective-permute-start.18 = (bf16[2,32,192]{2,1,0:T(8,128)(2,1)S(1)}, bf16[2,32,192]{2,1,0:T(8,128)(2,1)S(1)}, u32[]{:S(2)}, u32[]{:S(2)}) collective-permute-start(bf16[2,32,192]{2,1,0:T(8,128)(2,1)S(1)} %bitcast.15), channel_id=1, source_target_pairs={{0,12},{4,8},{8,4},{12,0},{16,28},{20,24},{24,20},{28,16},{1,13},{... | collective-permute-start | bytes 73736 | tf_op jit(solution)/shard_map/ppermute | solution.py:356
  80.5 4.7 %copy-start.5 = (bf16[2,32,192]{2,1,0:T(8,128)(2,1)}, bf16[2,32,192]{2,1,0:T(8,128)(2,1)S(1)}, u32[]{:S(2)}) copy-start(bf16[2,32,192]{2,1,0:T(8,128)(2,1)S(1)} %collective-permute-done.21.refs_6_) | copy-start | bytes 73732
  80.5 3.9 %collective-permute-start.17 = (bf16[2,32,192]{2,1,0:T(8,128)(2,1)S(1)}, bf16[2,32,192]{2,1,0:T(8,128)(2,1)S(1)}, u32[]{:S(2)}, u32[]{:S(2)}) collective-permute-start(bf16[2,32,192]{2,1,0:T(8,128)(2,1)S(1)} %bitcast.14), channel_id=1, source_target_pairs={{0,8},{4,12},{8,0},{12,4},{16,24},{20,28},{24,16},{28,20},{1,9},{5... | collective-permute-start | bytes 73736 | tf_op jit(solution)/shard_map/ppermute | solution.py:356
  81.3 3.9 %copy-start.6 = (bf16[2,32,192]{2,1,0:T(8,128)(2,1)}, bf16[2,32,192]{2,1,0:T(8,128)(2,1)S(1)}, u32[]{:S(2)}) copy-start(bf16[2,32,192]{2,1,0:T(8,128)(2,1)S(1)} %collective-permute-done.22.refs_7_) | copy-start | bytes 73732
  81.3 3.9 %collective-permute-start.16 = (bf16[2,32,192]{2,1,0:T(8,128)(2,1)S(1)}, bf16[2,32,192]{2,1,0:T(8,128)(2,1)S(1)}, u32[]{:S(2)}, u32[]{:S(2)}) collective-permute-start(bf16[2,32,192]{2,1,0:T(8,128)(2,1)S(1)} %bitcast.13), channel_id=1, source_target_pairs={{0,4},{4,0},{8,12},{12,8},{16,20},{20,16},{24,28},{28,24},{1,5},{5... | collective-permute-start | bytes 73736 | tf_op jit(solution)/shard_map/ppermute | solution.py:356
  82.7 2.5 %copy-start.7 = (bf16[2,32,192]{2,1,0:T(8,128)(2,1)}, bf16[2,32,192]{2,1,0:T(8,128)(2,1)S(1)}, u32[]{:S(2)}) copy-start(bf16[2,32,192]{2,1,0:T(8,128)(2,1)S(1)} %collective-permute-done.20.refs_5_) | copy-start | bytes 73732
  82.7 2.5 %copy-start.8 = (bf16[2,32,192]{2,1,0:T(8,128)(2,1)}, bf16[2,32,192]{2,1,0:T(8,128)(2,1)S(1)}, u32[]{:S(2)}) copy-start(bf16[2,32,192]{2,1,0:T(8,128)(2,1)S(1)} %collective-permute-done.19.refs_4_) | copy-start | bytes 73732
  83.6 1.6 %copy-start.9 = (bf16[2,32,192]{2,1,0:T(8,128)(2,1)}, bf16[2,32,192]{2,1,0:T(8,128)(2,1)S(1)}, u32[]{:S(2)}) copy-start(bf16[2,32,192]{2,1,0:T(8,128)(2,1)S(1)} %collective-permute-done.18.refs_3_) | copy-start | bytes 73732
  84.5 0.8 copy-start.10
  85.2 0.6 copy-start.11

commit v3 on v1

--- a/solution.py
+++ b/solution.py
@@ -11,6 +11,7 @@
 EPS = 1e-05
 LANES = 128
 CODES = 64
+VOCAB_ROWS = 40
 TABLE_ROWS = 48
 
 f32 = jnp.float32
@@ -42,22 +43,46 @@
     return lax.broadcasted_iota(jnp.int32, shape, axis)
 
 
-def table_kernel(embed_ref, qkv_ref, out_ref):
+def table_kernel(embed_ref, qkv_ref, out_ref, padded_ref):
     vocab = embed_ref.shape[0]
-    normed = layer_norm(embed_ref[...].astype(f32)).astype(bf16)
-    for t in range(3):
-        table = dot_nt(normed, qkv_ref[t])
-        out_ref[t] = jnp.zeros(out_ref.shape[1:], bf16)
-        out_ref[t, 0:vocab, :] = table.astype(bf16)
-
-
-def make_tables(embed, row_qkv):
-    local_width = row_qkv.shape[1]
+    padded_ref[...] = jnp.zeros(padded_ref.shape, f32)
+    padded_ref[0:vocab, :] = embed_ref[...].astype(f32)
+    normed = layer_norm(padded_ref[...]).astype(bf16)
+    out_ref[...] = dot_nt(normed, qkv_ref[...]).astype(bf16)
+
+
+def make_tables(embed, qkv):
     return pl.pallas_call(
         table_kernel,
-        out_shape=jax.ShapeDtypeStruct((3, TABLE_ROWS, local_width), bf16),
+        out_shape=jax.ShapeDtypeStruct((TABLE_ROWS, qkv.shape[0]), bf16),
+        scratch_shapes=[pltpu.VMEM((TABLE_ROWS, embed.shape[1]), f32)],
+        cost_estimate=pl.CostEstimate(
+            flops=2 * TABLE_ROWS * qkv.size, bytes_accessed=2 * qkv.size, transcendentals=0
+        ),
         name="tables",
-    )(embed, row_qkv)
+    )(embed, qkv)
+
+
+def pack_kernel(table_ref, *refs):
+    codes_refs, out_ref = refs[:-1], refs[-1]
+    coded = jnp.concatenate([ref[...] for ref in codes_refs], 0)
+    ids = (coded & 0xFFFF).astype(f32)
+    live = (coded >> 16).astype(f32)
+    some, cols = coded.shape
+    out_ref[...] = table_ref[...]
+    spare = jnp.concatenate(
+        [ids, live[:, 0:LANES], jnp.zeros((some, out_ref.shape[1] - cols - LANES), f32)], 1
+    )
+    if some < 8:
+        spare = jnp.concatenate([spare, jnp.zeros((8 - some, spare.shape[1]), f32)], 0)
+    kept = table_ref[VOCAB_ROWS - 8 : VOCAB_ROWS, :].astype(f32)
+    out_ref[VOCAB_ROWS - 8 : TABLE_ROWS, :] = jnp.concatenate([kept, spare], 0).astype(bf16)
+
+
+def pack(table, codes):
+    return pl.pallas_call(
+        pack_kernel, out_shape=jax.ShapeDtypeStruct(table.shape, bf16), name="pack"
+    )(table, *codes)
 
 
 def halves(pair):
@@ -80,51 +105,53 @@
     )
 
 
-def main_kernel(
-    ids_ref,
-    tab_ref,
-    embed_ref,
-    row_out_ref,
-    col_qkv_ref,
-    context_ref,
-    mixed_out_ref,
+def read_sequences(payload_ref, rows, first, last):
+    parts = payload_ref.shape[0]
+    each = rows // parts
+    return jnp.concatenate(
+        [
+            payload_ref[p, VOCAB_ROWS:TABLE_ROWS, first:last].astype(f32)[0:each]
+            for p in range(parts)
+        ],
+        0,
+    )
+
+
+def row_kernel(
+    payload_ref,
+    row_context_ref,
+    own_ref,
     table_ref,
-    embed2_ref,
     hot_ref,
-    own_ref,
     live_own_ref,
     sum_ref,
     spread_ref,
-    row_context_ref,
 ):
-    rows = ids_ref.shape[0]
+    parts = payload_ref.shape[0]
+    depth, cols = hot_ref.shape
+    rows = depth // CODES
     pairs = rows // 2
-    cols = hot_ref.shape[1]
     own = own_ref.shape[0] // pairs
-    vocab, width = embed_ref.shape
+    width = row_context_ref.shape[1]
     heads = width // HEAD_DIM
-    parts = tab_ref.shape[0]
-    local = tab_ref.shape[3]
-    tokens = rows * own
+    local = width // parts
     group = lax.axis_index("seq")
-    part = lax.axis_index("head")
-
-    table_ref[...] = jnp.zeros(table_ref.shape, bf16)
+
     for t in range(3):
-        table_ref[t, 0:TABLE_ROWS, :] = jnp.concatenate([tab_ref[p, t] for p in range(parts)], 1)
-    embed2_ref[...] = jnp.zeros(embed2_ref.shape, bf16)
-    embed2_ref[0:vocab, 0:width] = embed_ref[...]
-    embed2_ref[CODES : CODES + vocab, width : 2 * width] = embed_ref[...]
-
-    ids = ids_ref[:, 0:cols]
-    live = ids_ref[:, cols : cols + LANES].astype(f32)
-    code = iota((CODES, cols), 0)
+        table_ref[t, 0:VOCAB_ROWS, :] = jnp.concatenate(
+            [payload_ref[p, 0:VOCAB_ROWS, t * local : (t + 1) * local] for p in range(parts)], 1
+        )
+        table_ref[t, VOCAB_ROWS:CODES, :] = jnp.zeros((CODES - VOCAB_ROWS, width), bf16)
+
+    ids = read_sequences(payload_ref, rows, 0, cols)
+    live = read_sequences(payload_ref, rows, cols, cols + LANES)
+    code = iota((CODES, cols), 0).astype(f32)
     for r in range(rows):
         hot = jnp.broadcast_to(ids[r : r + 1, :], (CODES, cols)) == code
         hot_ref[r * CODES : (r + 1) * CODES, :] = hot.astype(f32).astype(bf16)
 
     pick = (iota((own, cols), 1) == group * own + iota((own, cols), 0)).astype(f32).astype(bf16)
-    mine = dot_nt(pick, ids.astype(f32).astype(bf16))
+    mine = dot_nt(pick, ids.astype(bf16))
     lane = iota((own, LANES), 1)
     first_half = lane < CODES
     lane_code = jnp.where(first_half, lane, lane - CODES).astype(f32)
@@ -135,7 +162,6 @@
         own_ref[k * own : (k + 1) * own, :] = hot.astype(bf16)
         live_own_ref[k * own : (k + 1) * own, :] = (hot * alive).astype(bf16)
 
-    depth = rows * CODES
     for hp in range(heads // 2):
         span = slice(hp * LANES, (hp + 1) * LANES)
         queries = spread_pair(table_ref[0, :, span])
@@ -193,6 +219,56 @@
                     k * own : (k + 1) * own, r2 * LANES : (r2 + 1) * LANES
                 ]
 
+
+def attend_rows(payload, rows, cols, own, width):
+    heads = width // HEAD_DIM
+    tokens = rows * own
+    return pl.pallas_call(
+        row_kernel,
+        out_shape=(
+            jax.ShapeDtypeStruct((tokens, width), bf16),
+            jax.ShapeDtypeStruct((rows // 2 * own, LANES), bf16),
+        ),
+        scratch_shapes=[
+            pltpu.VMEM((3, CODES, width), bf16),
+            pltpu.VMEM((rows * CODES, cols), bf16),
+            pltpu.VMEM((rows // 2 * own, LANES), bf16),
+            pltpu.VMEM((heads * own, 2 * rows * CODES), bf16),
+            pltpu.VMEM((heads * own, rows * CODES), bf16),
+        ],
+        cost_estimate=pl.CostEstimate(flops=5 * 10**9, bytes_accessed=10**6, transcendentals=0),
+        compiler_params=pltpu.CompilerParams(vmem_limit_bytes=32 * 1024 * 1024),
+        name="row_attention",
+    )(payload)
+
+
+def column_kernel(parts, cols, *refs):
+    row_out_refs, refs = refs[:parts], refs[parts:]
+    (
+        payload_ref,
+        row_context_ref,
+        own_ref,
+        embed_ref,
+        col_qkv_ref,
+        context_ref,
+        mixed_out_ref,
+        row_out_ref,
+        embed2_ref,
+    ) = refs
+    tokens, width = row_context_ref.shape
+    rows = LANES // 8
+    pairs = rows // 2
+    own = own_ref.shape[0] // pairs
+    vocab = embed_ref.shape[0]
+    local = width // parts
+    part = lax.axis_index("head")
+
+    for p in range(parts):
+        row_out_ref[part ^ p] = row_out_refs[p][...]
+    embed2_ref[...] = jnp.zeros(embed2_ref.shape, bf16)
+    embed2_ref[0:vocab, 0:width] = embed_ref[...]
+    embed2_ref[CODES : CODES + vocab, width : 2 * width] = embed_ref[...]
+
     embedded2 = dot_nn(own_ref[...], embed2_ref[...])
     embedded = jnp.concatenate(
         [
@@ -202,7 +278,7 @@
         ],
         0,
     )
-    mixed = embedded + dot_nt(row_context_ref[...], row_out_ref[...])
+    mixed = embedded + dot_nt(row_context_ref[...], row_out_ref[...].reshape(width, width))
     for p in range(parts):
 
         @pl.when(part == p)
@@ -223,6 +299,7 @@
         regroup(dot_nt(normed, col_qkv_ref[t * local : (t + 1) * local, :])).astype(bf16)
         for t in range(3)
     ]
+    live = read_sequences(payload_ref, rows, cols, cols + LANES)
     sub, lan = iota((unit, unit), 0), iota((unit, unit), 1)
     same_column = (sub % few) == (lan % few)
     seq_of_lane = iota((rows, unit), 1) // few
@@ -249,71 +326,130 @@
             pieces.append(result)
         blocks.append(jnp.concatenate(pieces, 1))
     whole = jnp.concatenate(blocks, 0).reshape(groups, rows, few, local)
-    context_ref[...] = jnp.swapaxes(whole, 0, 1).reshape(tokens, local).astype(bf16)
-
-
-def attend(ids, tables, embed, row_out, col_qkv, own):
-    rows = ids.shape[0]
-    cols = ids.shape[1] - LANES
-    width = embed.shape[1]
-    heads = width // HEAD_DIM
-    local = tables.shape[3]
-    tokens = rows * own
+    context = jnp.swapaxes(whole, 0, 1).reshape(tokens, local)
+    context_ref[0:tokens, :] = context[:, 0:LANES].astype(bf16)
+    half = tokens // 2
+    context_ref[tokens : tokens + half, :] = jnp.concatenate(
+        [context[0:half, LANES:local], context[half:tokens, LANES:local]], 1
+    ).astype(bf16)
+
+
+def attend_columns_here(row_outs, payload, row_context, own_codes, embed, col_qkv, cols):
+    parts = len(row_outs)
+    tokens, width = row_context.shape
+    local = width // parts
     return pl.pallas_call(
-        main_kernel,
+        functools.partial(column_kernel, parts, cols),
         out_shape=(
-            jax.ShapeDtypeStruct((tokens, local), bf16),
+            jax.ShapeDtypeStruct((tokens * local // LANES, LANES), bf16),
             jax.ShapeDtypeStruct((tokens, local), f32),
         ),
         scratch_shapes=[
-            pltpu.VMEM((3, CODES, width), bf16),
+            pltpu.VMEM((parts, local, width), bf16),
             pltpu.VMEM((2 * CODES, 2 * width), bf16),
-            pltpu.VMEM((rows * CODES, cols), bf16),
-            pltpu.VMEM((rows // 2 * own, LANES), bf16),
-            pltpu.VMEM((rows // 2 * own, LANES), bf16),
-            pltpu.VMEM((heads * own, 2 * rows * CODES), bf16),
-            pltpu.VMEM((heads * own, rows * CODES), bf16),
-            pltpu.VMEM((tokens, width), bf16),
         ],
-        compiler_params=pltpu.CompilerParams(vmem_limit_bytes=48 * 1024 * 1024),
-        name="attend",
-    )(ids, tables, embed, row_out, col_qkv)
-
-
-def finish_kernel(context_ref, col_out_ref, mixed_ref, out_ref):
-    parts, _, local = context_ref.shape
+        compiler_params=pltpu.CompilerParams(vmem_limit_bytes=32 * 1024 * 1024),
+        name="column_attention",
+    )(*row_outs, payload, row_context, own_codes, embed, col_qkv)
+
+
+def finish_kernel(groups, context_ref, col_out_ref, mixed_ref, out_ref):
+    parts = context_ref.shape[0]
+    tokens, local = mixed_ref.shape
+    half = tokens // 2
+    group = lax.axis_index("seq")
     total = mixed_ref[...]
     for p in range(parts):
-        total = total + dot_nt(context_ref[p], col_out_ref[:, p * local : (p + 1) * local])
-    out_ref[...] = total.astype(bf16)
-
-
-def finish(contexts, col_out, mixed):
+        weight = col_out_ref[:, p * local : (p + 1) * local]
+        total = total + dot_nt(context_ref[p, 0:tokens, :], weight[:, 0:LANES])
+        rest = weight[:, LANES:local]
+        zero = jnp.zeros_like(rest)
+        last = context_ref[p, tokens : tokens + half, :]
+        total = total + jnp.concatenate(
+            [
+                dot_nt(last, jnp.concatenate([rest, zero], 1)),
+                dot_nt(last, jnp.concatenate([zero, rest], 1)),
+            ],
+            0,
+        )
+    each = tokens // groups
+    for d in range(groups):
+        block = total[d * each : (d + 1) * each, :]
+        packed = jnp.concatenate(
+            [
+                block[:, 0:LANES],
+                jnp.concatenate(
+                    [block[0 : each // 2, LANES:local], block[each // 2 :, LANES:local]], 1
+                ),
+            ],
+            0,
+        )
+        out_ref[group ^ d] = packed.astype(bf16)
+
+
+def finish(contexts, col_out, mixed, groups):
+    tokens, local = mixed.shape
     return pl.pallas_call(
-        finish_kernel,
-        out_shape=jax.ShapeDtypeStruct(mixed.shape, bf16),
-        compiler_params=pltpu.CompilerParams(vmem_limit_bytes=48 * 1024 * 1024),
+        functools.partial(finish_kernel, groups),
+        out_shape=jax.ShapeDtypeStruct((groups, tokens // groups * local // LANES, LANES), bf16),
+        compiler_params=pltpu.CompilerParams(vmem_limit_bytes=32 * 1024 * 1024),
         name="finish",
     )(contexts, col_out, mixed)
 
 
+def order_kernel(blocks_ref, out_ref):
+    groups = blocks_ref.shape[0]
+    local, cols = out_ref.shape[1:]
+    own = cols // groups
+    rest = local - LANES
+    for part in range(3):
+        piece = jnp.concatenate(
+            [blocks_ref[g, part * own : (part + 1) * own, :] for g in range(groups)], 0
+        )
+        turned = piece.astype(f32).T.astype(bf16)
+        if part < 2:
+            out_ref[part, 0:LANES, :] = turned
+        else:
+            for r in range(2):
+                out_ref[r, LANES:local, :] = turned[r * rest : (r + 1) * rest, :]
+
+
+def order(blocks, cols, local):
+    return pl.pallas_call(
+        order_kernel,
+        out_shape=jax.ShapeDtypeStruct((2, local, cols), bf16),
+        name="order",
+    )(blocks)
+
+
 def fast_body(ids, pad_mask, embed, row_qkv, row_out, col_qkv, col_out):
     rows_here, cols = ids.shape
+    width = embed.shape[1]
     local = row_out.shape[0]
-    groups = lax.axis_size("seq")
-    own = cols // groups
-    live = jnp.broadcast_to(pad_mask[:, None], (rows_here, LANES))
-    ids_all = lax.all_gather(jnp.concatenate([ids, live], 1), "seq", axis=0, tiled=True)
-    tables = lax.all_gather(make_tables(embed, row_qkv), "head", axis=0)
-    row_out_all = lax.all_gather(row_out, "head", axis=0, tiled=True)
-    context, mixed = attend(
-        ids_all, tables, embed, row_out_all, col_qkv.reshape(3 * local, -1), own
+    groups, parts = lax.axis_size("seq"), lax.axis_size("head")
+    own, rows = cols // groups, rows_here * groups
+    each = groups // parts
+
+    def pairwise(value, partner):
+        order = [(g, p) for g in range(groups) for p in range(parts)]
+        link = [(g * parts + p, partner(g, p)) for g, p in order]
+        return lax.ppermute(value, ("seq", "head"), [(i, g * parts + p) for i, (g, p) in link])
+
+    coded = ids + 65536 * pad_mask[:, None]
+    codes = [pairwise(coded, lambda g, p, b=b: (g ^ (p * each + b), p)) for b in range(each)]
+    row_outs = [row_out] + [
+        pairwise(row_out, lambda g, p, step=step: (g, p ^ step)) for step in range(1, parts)
+    ]
+    table = make_tables(embed, row_qkv.reshape(3 * local, width))
+    payload = lax.all_gather(pack(table, codes), "head", axis=0)
+    row_context, own_codes = attend_rows(payload, rows, cols, own, width)
+    context, mixed = attend_columns_here(
+        row_outs, payload, row_context, own_codes, embed, col_qkv.reshape(3 * local, width), cols
     )
     contexts = lax.all_gather(context, "head", axis=0)
-    out = finish(contexts, col_out, mixed)
-    out = out.reshape(groups, rows_here, own, local)
-    back = lax.all_to_all(out, "seq", split_axis=0, concat_axis=2, tiled=True)
-    return back.reshape(rows_here, cols, local)
+    blocks = finish(contexts, col_out, mixed, groups)
+    blocks = lax.all_to_all(blocks, "seq", split_axis=0, concat_axis=0, tiled=True)
+    return jnp.swapaxes(order(blocks, cols, local), 1, 2)
 
 
 def weight_fold(out_weight, piece):
@@ -398,7 +534,20 @@
     rows_here, cols = ids.shape
     groups = lax.axis_size("seq")
     own, rows = cols // groups, rows_here * groups
-    fits = own % 16 == 0 and rows * 8 == LANES and embed.shape[0] <= TABLE_ROWS
+    parts = lax.axis_size("head")
+    local = row_out.shape[0]
+    fits = (
+        groups & (groups - 1) == 0
+        and parts in (2, 4)
+        and groups % parts == 0
+        and rows * 8 == LANES
+        and rows_here == 2
+        and rows <= 8 * parts
+        and own % 16 == 0
+        and cols + LANES <= 3 * local
+        and local == LANES + HEAD_DIM
+        and embed.shape[0] <= VOCAB_ROWS
+    )
     chosen = fast_body if fits else general_body
     return chosen(ids, pad_mask, embed, row_qkv, row_out, col_qkv, col_out)
 

time: 93.4 us -> 61 us (0.65)
  blocking collectives: 63.3 us -> 33.1 us
  between operations: 13.4 us -> 0.09 us
  starting transfers between devices: 0.01 us -> 8.98 us
  Pallas kernels: 12.2 us -> 15.9 us
  local copies, waits for them, and re-layouts: 2.86 us -> 1.18 us
    all_gather x2 -> x1, blocking collectives: 38.2 us -> 10.9 us  [fast_body(): payload = lax.all_gather(pack(table, codes), 'head', axis=0)]
    ppermute x0 -> x5, starting transfers between devices: none -> 8.98 us  [pairwise(): lax.ppermute(value, ('seq', 'head'), [(i, g * parts + p) for i, (g, p) in...]
    pallas_call x3 -> x6, Pallas kernels: 12.2 us -> 15.9 us  [the longest x1 6.17 us: attend_columns_here(): pl.pallas_call(functools.partial(column_kernel, parts, cols), out_shape=(...]
    all_to_all x1, blocking collectives: 14.6 us -> 13.2 us  [fast_body(): lax.all_to_all(blocks, 'seq', split_axis=0, concat_axis=0, tiled=True)]
    all_gather x1, blocking collectives: 10.4 us -> 9.03 us  [fast_body(): contexts = lax.all_gather(context, 'head', axis=0)]
  transfers between devices with their start and end apart: 1 -> 5, of which waited for: 0 -> 0; matrix products, arithmetic and copies ran while one was open for 2% -> 0% of each run, Pallas kernels for 3% -> 12%
where the time goes in v3:
time: 61 us; the launch traced here: 60.7 us
  blocking collectives  33.1 us (54%)
  Pallas kernels  15.9 us (26%)
  starting transfers between devices  8.98 us (15%)
  other arithmetic  1.41 us (2%)
  local copies, waits for them, and re-layouts  1.18 us (2%)
    all_to_all x1, blocking collectives, fast_body(): lax.all_to_all(blocks, 'seq', split_axis=0, concat_axis=0, tiled=True)  13.2 us
    all_gather x1, blocking collectives, fast_body(): payload = lax.all_gather(pack(table, codes), 'head', axis=0)  10.9 us
    all_gather x1, blocking collectives, fast_body(): contexts = lax.all_gather(context, 'head', axis=0)  9.03 us
    ppermute x5, starting transfers between devices, pairwise(): lax.ppermute(value, ('seq', 'head'), [(i, g * parts + p) for i, (g, p) in...  8.98 us
    pallas_call x1, Pallas kernels, attend_columns_here(): pl.pallas_call(functools.partial(column_kernel, parts, cols), out_shape=(...  6.17 us
    pallas_call x1, Pallas kernels, attend_rows(): pl.pallas_call(row_kernel, out_shape=(jax.ShapeDtypeStruct((tokens, width...  3.38 us
    pallas_call x1, Pallas kernels, make_tables(): pl.pallas_call(table_kernel, out_shape=jax.ShapeDtypeStruct((TABLE_ROWS,...  2.34 us
    pallas_call x1, Pallas kernels, order(): pl.pallas_call(order_kernel, out_shape=jax.ShapeDtypeStruct((2, local, co...  1.74 us
  transfers between devices with their start and end apart: 5, of which 0 were waited for; matrix products, arithmetic and copies ran while one was open for 0% of the time, Pallas kernels for 12%

profile of v3, /device:TPU:0, one launch (start us, length us, event | category | flops | bytes accessed | tf_op | source)
XLA Modules:
  0.0 60.7 jit_solution(8917096858977167053)
XLA Ops:
  0.0 0.7 %broadcast_multiply_fusion = s32[2]{0:T(128)S(1)} fusion(s32[2]{0:T(128)} %param.8), kind=kLoop, calls=%fused_computation.1 | loop fusion | flops 2 | bytes 16 | tf_op jit(solution)/shard_map/mul | solution.py:438
  0.7 0.8 %broadcast_add_fusion = s32[2,256]{1,0:T(2,128)S(1)} fusion(s32[2,256]{1,0:T(2,128)} %param.7, s32[2]{0:T(128)S(1)} %broadcast_multiply_fusion), kind=kLoop, calls=%fused_computation | loop fusion | flops 512 | bytes 4104 | tf_op jit(solution)/shard_map/add | solution.py:438
  1.4 3.0 %collective-permute-start.4 = (s32[2,256]{1,0:T(2,128)S(1)}, s32[2,256]{1,0:T(2,128)S(1)}, u32[]{:S(2)}, u32[]{:S(2)}) collective-permute-start(s32[2,256]{1,0:T(2,128)S(1)} %broadcast_add_fusion), channel_id=1, source_target_pairs={{0,4},{1,13},{2,22},{3,31},{4,0},{5,9},{6,18},{7,27},{8,12},{9,5},... | collective-permute-start | bytes 6152 | tf_op jit(solution)/shard_map/ppermute | solution.py:436
  4.4 0.6 %collective-permute-start.3 = (s32[2,256]{1,0:T(2,128)S(1)}, s32[2,256]{1,0:T(2,128)S(1)}, u32[]{:S(2)}, u32[]{:S(2)}) collective-permute-start(s32[2,256]{1,0:T(2,128)S(1)} %broadcast_add_fusion), channel_id=1, source_target_pairs={{0,0},{1,9},{2,18},{3,27},{4,4},{5,13},{6,22},{7,31},{8,8},{9,1},{... | collective-permute-start | bytes 6152 | tf_op jit(solution)/shard_map/ppermute | solution.py:436
  5.0 5.2 %collective-permute-start.1 = (bf16[192,768]{1,0:T(8,128)(2,1)}, bf16[192,768]{1,0:T(8,128)(2,1)S(1)}, u32[]{:S(2)}, u32[]{:S(2)}) collective-permute-start(bf16[192,768]{1,0:T(8,128)(2,1)} %refs_0_.1), channel_id=1, source_target_pairs={{0,2},{1,3},{2,0},{3,1},{4,6},{5,7},{6,4},{7,5},{8,10},{9,11},{10,... | collective-permute-start | bytes 884744 | tf_op jit(solution)/shard_map/ppermute | solution.py:436
  10.2 0.0 collective-permute-start
  10.2 0.2 collective-permute-start.2
  10.4 2.3 %tables.1.table_ref = bf16[48,576]{1,0:T(8,128)(2,1)} custom-call(bf16[33,768]{1,0:T(8,128)(2,1)} %refs_7_.1, bf16[576,768]{1,0:T(8,128)(2,1)} %bitcast.9), custom_call_target="tpu_custom_call" | custom-call | flops 42467328 | bytes 884736 | tf_op jit(solution)/shard_map/tables/pallas_call | solution.py:55
  12.7 0.0 collective-permute-done.4.refs_1_
  12.7 0.0 copy-start.4
  12.7 0.0 collective-permute-done.3.refs_0_
  12.8 0.6 copy-done.4
  13.3 0.0 copy-start.5
  13.3 0.6 copy-done.5
  13.9 1.5 %pack.1 = bf16[48,576]{1,0:T(8,128)(2,1)} custom-call(bf16[48,576]{1,0:T(8,128)(2,1)} %tables.1.table_ref, s32[2,256]{1,0:T(2,128)} %copy-done.5, s32[2,256]{1,0:T(2,128)} %copy-done.4), custom_call_target="tpu_custom_call" | custom-call | tf_op jit(solution)/shard_map/pack/pallas_call | solution.py:83
  15.4 10.9 %all-gather = bf16[192,576]{1,0:T(8,128)(2,1)S(1)} all-gather(bf16[48,576]{1,0:T(8,128)(2,1)} %pack.1), channel_id=2, replica_groups=mesh['seq'=8,'head'=4] {'head'}, dimensions={0}, use_global_device_ids=true | all-gather | bytes 276480 | tf_op jit(solution)/shard_map/all_gather | solution.py:444
  26.3 0.0 copy-start
  26.3 0.0 copy-start.1
  26.3 0.0 copy-start.3
  26.3 3.4 %row_attention.1 = (bf16[512,768]{1,0:T(8,128)(2,1)S(1)}, bf16[256,128]{1,0:T(8,128)(2,1)S(1)}) custom-call(bf16[4,48,576]{2,1,0:T(8,128)(2,1)S(1)} %bitcast.6), custom_call_target="tpu_custom_call" | custom-call | flops 5000000000 | bytes 1000000 | tf_op jit(solution)/shard_map/row_attention/pallas_call | solution.py:226
  29.7 0.0 collective-permute-done.1.refs_2_
  29.7 0.0 collective-permute-done.refs_1_
  29.7 0.0 collective-permute-done.2.refs_3_
  29.7 0.0 copy-done
  29.7 0.0 copy-done.1
  29.8 0.0 copy-done.3
  29.8 6.2 %column_attention.1 = (bf16[768,128]{1,0:T(8,128)(2,1)S(1)}, f32[512,192]{1,0:T(8,128)S(1)}) custom-call(bf16[192,768]{1,0:T(8,128)(2,1)S(1)} %copy-done.1, bf16[192,768]{1,0:T(8,128)(2,1)S(1)} %collective-permute-done.refs_1_, bf16[192,768]{1,0:T(8,128)(2,1)S(1)} %collective-permute-done.1.refs_2_, bf16[192,768]{1,0:T(8,128)(2,1)S(1)} %collective-permute-done.2.refs_3_, ...), custom_call_target="tpu_custom_call" | custom-call | tf_op jit(solution)/shard_map/column_attention/pallas_call | solution.py:341
  35.9 0.0 copy-start.2
  36.0 9.0 %all-gather.1 = bf16[3072,128]{1,0:T(8,128)(2,1)S(1)} all-gather(bf16[768,128]{1,0:T(8,128)(2,1)S(1)} %get-tuple-element.11), channel_id=3, replica_groups=mesh['seq'=8,'head'=4] {'head'}, dimensions={0}, use_global_device_ids=true | all-gather | bytes 983040 | tf_op jit(solution)/shard_map/all_gather | solution.py:449
  45.0 0.0 copy-done.2
  45.0 0.8 %finish.1 = bf16[8,96,128]{2,1,0:T(8,128)(2,1)S(1)} custom-call(bf16[4,768,128]{2,1,0:T(8,128)(2,1)S(1)} %bitcast.5, bf16[192,768]{1,0:T(8,128)(2,1)S(1)} %copy-done.2, f32[512,192]{1,0:T(8,128)S(1)} %get-tuple-element.12.mixed_ref), custom_call_target="tpu_custom_call" | custom-call | tf_op jit(solution)/shard_map/finish/pallas_call | solution.py:392
  45.8 13.2 %all_to_all.5.blocks_ref = bf16[8,96,128]{2,1,0:T(8,128)(2,1)} all-to-all(bf16[8,96,128]{2,1,0:T(8,128)(2,1)S(1)} %finish.1), channel_id=1, replica_groups=mesh['seq'=8,'head'=4] {'seq'}, dimensions={0} | all-to-all | bytes 393216 | tf_op jit(solution)/shard_map/all_to_all | solution.py:451
  59.0 1.7 %order.1 = bf16[2,192,256]{2,1,0:T(8,128)(2,1)} custom-call(bf16[8,96,128]{2,1,0:T(8,128)(2,1)} %all_to_all.5.blocks_ref), custom_call_target="tpu_custom_call" | custom-call | tf_op jit(solution)/shard_map/order/pallas_call | solution.py:418
Async XLA Ops:
  1.4 11.3 %collective-permute-start.4 = (s32[2,256]{1,0:T(2,128)S(1)}, s32[2,256]{1,0:T(2,128)S(1)}, u32[]{:S(2)}, u32[]{:S(2)}) collective-permute-start(s32[2,256]{1,0:T(2,128)S(1)} %broadcast_add_fusion), channel_id=1, source_target_pairs={{0,4},{1,13},{2,22},{3,31},{4,0},{5,9},{6,18},{7,27},{8,12},{9,5},... | collective-permute-start | bytes 6152 | tf_op jit(solution)/shard_map/ppermute | solution.py:436
  4.4 8.4 %collective-permute-start.3 = (s32[2,256]{1,0:T(2,128)S(1)}, s32[2,256]{1,0:T(2,128)S(1)}, u32[]{:S(2)}, u32[]{:S(2)}) collective-permute-start(s32[2,256]{1,0:T(2,128)S(1)} %broadcast_add_fusion), channel_id=1, source_target_pairs={{0,0},{1,9},{2,18},{3,27},{4,4},{5,13},{6,22},{7,31},{8,8},{9,1},{... | collective-permute-start | bytes 6152 | tf_op jit(solution)/shard_map/ppermute | solution.py:436
  5.0 24.7 %collective-permute-start.1 = (bf16[192,768]{1,0:T(8,128)(2,1)}, bf16[192,768]{1,0:T(8,128)(2,1)S(1)}, u32[]{:S(2)}, u32[]{:S(2)}) collective-permute-start(bf16[192,768]{1,0:T(8,128)(2,1)} %refs_0_.1), channel_id=1, source_target_pairs={{0,2},{1,3},{2,0},{3,1},{4,6},{5,7},{6,4},{7,5},{8,10},{9,11},{10,... | collective-permute-start | bytes 884744 | tf_op jit(solution)/shard_map/ppermute | solution.py:436
  10.2 19.5 %collective-permute-start = (bf16[192,768]{1,0:T(8,128)(2,1)}, bf16[192,768]{1,0:T(8,128)(2,1)S(1)}, u32[]{:S(2)}, u32[]{:S(2)}) collective-permute-start(bf16[192,768]{1,0:T(8,128)(2,1)} %refs_0_.1), channel_id=1, source_target_pairs={{0,1},{1,0},{2,3},{3,2},{4,5},{5,4},{6,7},{7,6},{8,9},{9,8},{10,11... | collective-permute-start | bytes 884744 | tf_op jit(solution)/shard_map/ppermute | solution.py:436
  10.2 19.5 %collective-permute-start.2 = (bf16[192,768]{1,0:T(8,128)(2,1)}, bf16[192,768]{1,0:T(8,128)(2,1)S(1)}, u32[]{:S(2)}, u32[]{:S(2)}) collective-permute-start(bf16[192,768]{1,0:T(8,128)(2,1)} %refs_0_.1), channel_id=1, source_target_pairs={{0,3},{1,2},{2,1},{3,0},{4,7},{5,6},{6,5},{7,4},{8,11},{9,10},{10,... | collective-permute-start | bytes 884744 | tf_op jit(solution)/shard_map/ppermute | solution.py:436
  12.7 0.6 copy-start.4
  13.3 0.6 copy-start.5
  26.3 3.4 %copy-start = (bf16[3,192,768]{2,1,0:T(8,128)(2,1)S(1)}, bf16[3,192,768]{2,1,0:T(8,128)(2,1)}, u32[]{:S(2)}) copy-start(bf16[3,192,768]{2,1,0:T(8,128)(2,1)} %param.12) | copy-start | bytes 2654212
  26.3 3.4 %copy-start.1 = (bf16[192,768]{1,0:T(8,128)(2,1)S(1)}, bf16[192,768]{1,0:T(8,128)(2,1)}, u32[]{:S(2)}) copy-start(bf16[192,768]{1,0:T(8,128)(2,1)} %refs_0_.1) | copy-start | bytes 884740
  26.3 3.4 %copy-start.3 = (bf16[33,768]{1,0:T(8,128)(2,1)S(1)}, bf16[33,768]{1,0:T(8,128)(2,1)}, u32[]{:S(2)}) copy-start(bf16[33,768]{1,0:T(8,128)(2,1)} %refs_7_.1) | copy-start | bytes 152068
  35.9 9.0 %copy-start.2 = (bf16[192,768]{1,0:T(8,128)(2,1)S(1)}, bf16[192,768]{1,0:T(8,128)(2,1)}, u32[]{:S(2)}) copy-start(bf16[192,768]{1,0:T(8,128)(2,1)} %col_out_ref.1) | copy-start | bytes 884740

commit v4 on v3

--- a/solution.py
+++ b/solution.py
@@ -43,15 +43,47 @@
     return lax.broadcasted_iota(jnp.int32, shape, axis)
 
 
-def table_kernel(embed_ref, qkv_ref, out_ref, padded_ref):
+def code_kernel(ids_ref, live_ref, out_ref):
+    row = iota(ids_ref.shape, 0)
+    live = jnp.zeros(ids_ref.shape, jnp.int32)
+    for r in range(ids_ref.shape[0]):
+        live = jnp.where(row == r, live_ref[r], live)
+    out_ref[...] = ids_ref[...] + 65536 * live
+
+
+def make_codes(ids, pad_mask):
+    return pl.pallas_call(
+        code_kernel,
+        out_shape=jax.ShapeDtypeStruct(ids.shape, jnp.int32),
+        in_specs=[
+            pl.BlockSpec(memory_space=pltpu.VMEM),
+            pl.BlockSpec(memory_space=pltpu.SMEM),
+        ],
+        name="codes",
+    )(ids, pad_mask)
+
+
+def table_kernel(embed_ref, qkv_ref, *refs):
+    codes_refs, (out_ref, padded_ref) = refs[:-2], refs[-2:]
     vocab = embed_ref.shape[0]
     padded_ref[...] = jnp.zeros(padded_ref.shape, f32)
     padded_ref[0:vocab, :] = embed_ref[...].astype(f32)
     normed = layer_norm(padded_ref[...]).astype(bf16)
-    out_ref[...] = dot_nt(normed, qkv_ref[...]).astype(bf16)
-
-
-def make_tables(embed, qkv):
+    table = dot_nt(normed, qkv_ref[...])
+    coded = jnp.concatenate([ref[...] for ref in codes_refs], 0)
+    some, cols = coded.shape
+    ids = (coded & 0xFFFF).astype(f32)
+    live = (coded >> 16).astype(f32)
+    spare = jnp.concatenate(
+        [ids, live[:, 0:LANES], jnp.zeros((some, out_ref.shape[1] - cols - LANES), f32)], 1
+    )
+    if some < TABLE_ROWS - VOCAB_ROWS:
+        empty = jnp.zeros((TABLE_ROWS - VOCAB_ROWS - some, spare.shape[1]), f32)
+        spare = jnp.concatenate([spare, empty], 0)
+    out_ref[...] = jnp.concatenate([table[0:VOCAB_ROWS], spare], 0).astype(bf16)
+
+
+def make_payload(embed, qkv, codes):
     return pl.pallas_call(
         table_kernel,
         out_shape=jax.ShapeDtypeStruct((TABLE_ROWS, qkv.shape[0]), bf16),
@@ -60,29 +92,7 @@
             flops=2 * TABLE_ROWS * qkv.size, bytes_accessed=2 * qkv.size, transcendentals=0
         ),
         name="tables",
-    )(embed, qkv)
-
-
-def pack_kernel(table_ref, *refs):
-    codes_refs, out_ref = refs[:-1], refs[-1]
-    coded = jnp.concatenate([ref[...] for ref in codes_refs], 0)
-    ids = (coded & 0xFFFF).astype(f32)
-    live = (coded >> 16).astype(f32)
-    some, cols = coded.shape
-    out_ref[...] = table_ref[...]
-    spare = jnp.concatenate(
-        [ids, live[:, 0:LANES], jnp.zeros((some, out_ref.shape[1] - cols - LANES), f32)], 1
-    )
-    if some < 8:
-        spare = jnp.concatenate([spare, jnp.zeros((8 - some, spare.shape[1]), f32)], 0)
-    kept = table_ref[VOCAB_ROWS - 8 : VOCAB_ROWS, :].astype(f32)
-    out_ref[VOCAB_ROWS - 8 : TABLE_ROWS, :] = jnp.concatenate([kept, spare], 0).astype(bf16)
-
-
-def pack(table, codes):
-    return pl.pallas_call(
-        pack_kernel, out_shape=jax.ShapeDtypeStruct(table.shape, bf16), name="pack"
-    )(table, *codes)
+    )(embed, qkv, *codes)
 
 
 def halves(pair):
@@ -354,17 +364,18 @@
 
 
 def finish_kernel(groups, context_ref, col_out_ref, mixed_ref, out_ref):
-    parts = context_ref.shape[0]
+    cores, chips = context_ref.shape[0:2]
     tokens, local = mixed_ref.shape
     half = tokens // 2
     group = lax.axis_index("seq")
     total = mixed_ref[...]
-    for p in range(parts):
+    for p in range(cores * chips):
+        core, chip = p % cores, p // cores
         weight = col_out_ref[:, p * local : (p + 1) * local]
-        total = total + dot_nt(context_ref[p, 0:tokens, :], weight[:, 0:LANES])
+        total = total + dot_nt(context_ref[core, chip, 0:tokens, :], weight[:, 0:LANES])
         rest = weight[:, LANES:local]
         zero = jnp.zeros_like(rest)
-        last = context_ref[p, tokens : tokens + half, :]
+        last = context_ref[core, chip, tokens : tokens + half, :]
         total = total + jnp.concatenate(
             [
                 dot_nt(last, jnp.concatenate([rest, zero], 1)),
@@ -435,18 +446,20 @@
         link = [(g * parts + p, partner(g, p)) for g, p in order]
         return lax.ppermute(value, ("seq", "head"), [(i, g * parts + p) for i, (g, p) in link])
 
-    coded = ids + 65536 * pad_mask[:, None]
+    coded = make_codes(ids, pad_mask)
     codes = [pairwise(coded, lambda g, p, b=b: (g ^ (p * each + b), p)) for b in range(each)]
-    row_outs = [row_out] + [
-        pairwise(row_out, lambda g, p, step=step: (g, p ^ step)) for step in range(1, parts)
-    ]
-    table = make_tables(embed, row_qkv.reshape(3 * local, width))
-    payload = lax.all_gather(pack(table, codes), "head", axis=0)
+    sibling = lambda g, p: (g, p ^ 1)
+    across = lambda g, p: (g, p ^ 2)
+    far = pairwise(row_out, across)
+    row_outs = [row_out, pairwise(row_out, sibling), far, pairwise(far, sibling)]
+    payload = make_payload(embed, row_qkv.reshape(3 * local, width), codes)
+    payload = lax.all_gather(payload, "head", axis=0)
     row_context, own_codes = attend_rows(payload, rows, cols, own, width)
     context, mixed = attend_columns_here(
         row_outs, payload, row_context, own_codes, embed, col_qkv.reshape(3 * local, width), cols
     )
-    contexts = lax.all_gather(context, "head", axis=0)
+    contexts = lax.all_gather(context, "head", axis=0, axis_index_groups=[[0, 2], [1, 3]])
+    contexts = lax.all_gather(contexts, "head", axis=0, axis_index_groups=[[0, 1], [2, 3]])
     blocks = finish(contexts, col_out, mixed, groups)
     blocks = lax.all_to_all(blocks, "seq", split_axis=0, concat_axis=0, tiled=True)
     return jnp.swapaxes(order(blocks, cols, local), 1, 2)
@@ -538,7 +551,7 @@
     local = row_out.shape[0]
     fits = (
         groups & (groups - 1) == 0
-        and parts in (2, 4)
+        and parts == 4
         and groups % parts == 0
         and rows * 8 == LANES
         and rows_here == 2

time: 61 us -> 56.9 us (0.933)
  starting transfers between devices: 8.98 us -> 7.23 us
  other arithmetic: 1.41 us -> 0 us
  local copies, waits for them, and re-layouts: 1.18 us -> 0.57 us
    ppermute x5, starting transfers between devices: 8.98 us -> 7.23 us  [pairwise(): lax.ppermute(value, ('seq', 'head'), [(i, g * parts + p) for i, (g, p) in...]
    all_to_all x1, blocking collectives: 13.2 us -> 11.6 us  [fast_body(): lax.all_to_all(blocks, 'seq', split_axis=0, concat_axis=0, tiled=True)]
    all_gather x2 -> x3, blocking collectives: 19.9 us -> 21.4 us  [the longest x1 11.1 us: fast_body(): payload = lax.all_gather(payload, 'head', axis=0)]
    add x1 -> x0, other arithmetic: 0.75 us -> none  [fast_body(): coded = ids + 65536 * pad_mask[:, None]]
    mul x1 -> x0, other arithmetic: 0.66 us -> none  [fast_body(): coded = ids + 65536 * pad_mask[:, None]]
    unnamed x12, local copies, waits for them, and re-layouts: 1.18 us -> 0.57 us
where the time goes in v4:
time: 56.9 us; the launch traced here: 56.6 us
  blocking collectives  33 us (58%)
  Pallas kernels  15.8 us (28%)
  starting transfers between devices  7.23 us (13%)
  local copies, waits for them, and re-layouts  0.57 us (1%)
    all_to_all x1, blocking collectives, fast_body(): lax.all_to_all(blocks, 'seq', split_axis=0, concat_axis=0, tiled=True)  11.6 us
    all_gather x1, blocking collectives, fast_body(): payload = lax.all_gather(payload, 'head', axis=0)  11.1 us
    all_gather x1, blocking collectives, fast_body(): lax.all_gather(context, 'head', axis=0, axis_index_groups=[[0, 2], [1, 3]])  7.83 us
    ppermute x5, starting transfers between devices, pairwise(): lax.ppermute(value, ('seq', 'head'), [(i, g * parts + p) for i, (g, p) in...  7.23 us
    pallas_call x1, Pallas kernels, attend_columns_here(): pl.pallas_call(functools.partial(column_kernel, parts, cols), out_shape=(...  6.18 us
    pallas_call x1, Pallas kernels, attend_rows(): pl.pallas_call(row_kernel, out_shape=(jax.ShapeDtypeStruct((tokens, width...  3.37 us
    all_gather x1, blocking collectives, fast_body(): lax.all_gather(contexts, 'head', axis=0, axis_index_groups=[[0, 1], [2, 3]])  2.49 us
    pallas_call x1, Pallas kernels, make_payload(): pl.pallas_call(table_kernel, out_shape=jax.ShapeDtypeStruct((TABLE_ROWS,...  2.32 us
  transfers between devices with their start and end apart: 5, of which 0 were waited for; matrix products, arithmetic and copies ran while one was open for 0% of the time, Pallas kernels for 12%

profile of v4, /device:TPU:0, one launch (start us, length us, event | category | flops | bytes accessed | tf_op | source)
XLA Modules:
  0.0 56.6 jit_solution(16988871127877665728)
XLA Ops:
  0.0 2.9 %collective-permute-start.1 = (bf16[192,768]{1,0:T(8,128)(2,1)}, bf16[192,768]{1,0:T(8,128)(2,1)S(1)}, u32[]{:S(2)}, u32[]{:S(2)}) collective-permute-start(bf16[192,768]{1,0:T(8,128)(2,1)} %refs_0_.1), channel_id=1, source_target_pairs={{0,2},{1,3},{2,0},{3,1},{4,6},{5,7},{6,4},{7,5},{8,10},{9,11},{10,... | collective-permute-start | bytes 884744 | tf_op jit(solution)/shard_map/ppermute | solution.py:447
  2.9 1.4 %codes.1 = s32[2,256]{1,0:T(2,128)} custom-call(s32[2,256]{1,0:T(2,128)} %ids_ref.1, s32[2]{0:T(128)} %live_ref.1), custom_call_target="tpu_custom_call" | custom-call | tf_op jit(solution)/shard_map/codes/pallas_call | solution.py:55
  4.3 1.5 %collective-permute-start.4 = (s32[2,256]{1,0:T(2,128)}, s32[2,256]{1,0:T(2,128)S(1)}, u32[]{:S(2)}, u32[]{:S(2)}) collective-permute-start(s32[2,256]{1,0:T(2,128)} %codes.1), channel_id=1, source_target_pairs={{0,4},{1,13},{2,22},{3,31},{4,0},{5,9},{6,18},{7,27},{8,12},{9,5},... | collective-permute-start | bytes 6152 | tf_op jit(solution)/shard_map/ppermute | solution.py:447
  5.8 1.3 %collective-permute-start.3 = (s32[2,256]{1,0:T(2,128)}, s32[2,256]{1,0:T(2,128)S(1)}, u32[]{:S(2)}, u32[]{:S(2)}) collective-permute-start(s32[2,256]{1,0:T(2,128)} %codes.1), channel_id=1, source_target_pairs={{0,0},{1,9},{2,18},{3,27},{4,4},{5,13},{6,22},{7,31},{8,8},{9,1},{... | collective-permute-start | bytes 6152 | tf_op jit(solution)/shard_map/ppermute | solution.py:447
  7.2 1.1 %collective-permute-start = (bf16[192,768]{1,0:T(8,128)(2,1)}, bf16[192,768]{1,0:T(8,128)(2,1)S(1)}, u32[]{:S(2)}, u32[]{:S(2)}) collective-permute-start(bf16[192,768]{1,0:T(8,128)(2,1)} %refs_0_.1), channel_id=1, source_target_pairs={{0,1},{1,0},{2,3},{3,2},{4,5},{5,4},{6,7},{7,6},{8,9},{9,8},{10,11... | collective-permute-start | bytes 884744 | tf_op jit(solution)/shard_map/ppermute | solution.py:447
  8.3 0.0 collective-permute-done.4.refs_1_
  8.3 0.0 copy-start.4
  8.3 0.0 collective-permute-done.3.refs_0_
  8.3 0.0 copy-start.5
  8.3 0.5 copy-done.4
  8.8 0.0 copy-done.5
  8.8 2.3 %tables.1 = bf16[48,576]{1,0:T(8,128)(2,1)} custom-call(bf16[33,768]{1,0:T(8,128)(2,1)} %refs_7_.1, bf16[576,768]{1,0:T(8,128)(2,1)} %bitcast.11, s32[2,256]{1,0:T(2,128)} %copy-done.5, s32[2,256]{1,0:T(2,128)} %copy-done.4), custom_call_target="tpu_custom_call" | custom-call | flops 42467328 | bytes 884736 | tf_op jit(solution)/shard_map/tables/pallas_call | solution.py:87
  11.2 11.1 %all-gather = bf16[192,576]{1,0:T(8,128)(2,1)S(1)} all-gather(bf16[48,576]{1,0:T(8,128)(2,1)} %tables.1), channel_id=2, replica_groups=mesh['seq'=8,'head'=4] {'head'}, dimensions={0}, use_global_device_ids=true | all-gather | bytes 276480 | tf_op jit(solution)/shard_map/all_gather | solution.py:456
  22.2 0.0 collective-permute-done.1.refs_2_
  22.2 0.3 collective-permute-start.2
  22.6 0.0 copy-start
  22.6 0.0 copy-start.1
  22.6 0.0 copy-start.3
  22.6 3.4 %row_attention.1 = (bf16[512,768]{1,0:T(8,128)(2,1)S(1)}, bf16[256,128]{1,0:T(8,128)(2,1)S(1)}) custom-call(bf16[4,48,576]{2,1,0:T(8,128)(2,1)S(1)} %bitcast.7), custom_call_target="tpu_custom_call" | custom-call | flops 5000000000 | bytes 1000000 | tf_op jit(solution)/shard_map/row_attention/pallas_call | solution.py:236
  26.0 0.0 collective-permute-done.refs_1_
  26.0 0.0 collective-permute-done.2.refs_3_
  26.0 0.0 copy-done
  26.0 0.0 copy-done.1
  26.0 0.0 copy-done.3
  26.0 6.2 %column_attention.1 = (bf16[768,128]{1,0:T(8,128)(2,1)S(1)}, f32[512,192]{1,0:T(8,128)S(1)}) custom-call(bf16[192,768]{1,0:T(8,128)(2,1)S(1)} %copy-done.1, bf16[192,768]{1,0:T(8,128)(2,1)S(1)} %collective-permute-done.refs_1_, bf16[192,768]{1,0:T(8,128)(2,1)S(1)} %collective-permute-done.1.refs_2_, bf16[192,768]{1,0:T(8,128)(2,1)S(1)} %collective-permute-done.2.refs_3_, ...), custom_call_target="tpu_custom_call" | custom-call | tf_op jit(solution)/shard_map/column_attention/pallas_call | solution.py:351
  32.2 7.8 %all-gather.1 = bf16[1536,128]{1,0:T(8,128)(2,1)S(1)} all-gather(bf16[768,128]{1,0:T(8,128)(2,1)S(1)} %get-tuple-element.11), channel_id=3, replica_groups={{0,2},{1,3},{4,6},{5,7},{8,10},{9,11},{12,14},{13,15},{16,18},{17,19},{..., dimensions={0}, use_global_device_ids=true | all-gather | bytes 589824 | tf_op jit(solution)/shard_map/all_gather | solution.py:461
  40.0 0.0 copy-start.2
  40.0 2.5 %all-gather.2 = bf16[4,768,128]{2,1,0:T(8,128)(2,1)S(1)} all-gather(bf16[2,768,128]{2,1,0:T(8,128)(2,1)S(1)} %bitcast.10), channel_id=4, replica_groups={{0,1},{2,3},{4,5},{6,7},{8,9},{10,11},{12,13},{14,15},{16,17},{18,19},{..., dimensions={0}, use_global_device_ids=true | all-gather | bytes 1179648 | tf_op jit(solution)/shard_map/all_gather | solution.py:462
  42.5 0.0 copy-done.2
  42.5 0.8 %finish.1 = bf16[8,96,128]{2,1,0:T(8,128)(2,1)S(1)} custom-call(bf16[2,2,768,128]{3,2,1,0:T(8,128)(2,1)S(1)} %bitcast.6, bf16[192,768]{1,0:T(8,128)(2,1)S(1)} %copy-done.2, f32[512,192]{1,0:T(8,128)S(1)} %get-tuple-element.12.mixed_ref), custom_call_target="tpu_custom_call" | custom-call | tf_op jit(solution)/shard_map/finish/pallas_call | solution.py:403
  43.3 11.6 %all_to_all.5.blocks_ref = bf16[8,96,128]{2,1,0:T(8,128)(2,1)} all-to-all(bf16[8,96,128]{2,1,0:T(8,128)(2,1)S(1)} %finish.1), channel_id=1, replica_groups=mesh['seq'=8,'head'=4] {'seq'}, dimensions={0} | all-to-all | bytes 393216 | tf_op jit(solution)/shard_map/all_to_all | solution.py:464
  54.9 1.7 %order.1 = bf16[2,192,256]{2,1,0:T(8,128)(2,1)} custom-call(bf16[8,96,128]{2,1,0:T(8,128)(2,1)} %all_to_all.5.blocks_ref), custom_call_target="tpu_custom_call" | custom-call | tf_op jit(solution)/shard_map/order/pallas_call | solution.py:429
Async XLA Ops:
  0.0 22.2 %collective-permute-start.1 = (bf16[192,768]{1,0:T(8,128)(2,1)}, bf16[192,768]{1,0:T(8,128)(2,1)S(1)}, u32[]{:S(2)}, u32[]{:S(2)}) collective-permute-start(bf16[192,768]{1,0:T(8,128)(2,1)} %refs_0_.1), channel_id=1, source_target_pairs={{0,2},{1,3},{2,0},{3,1},{4,6},{5,7},{6,4},{7,5},{8,10},{9,11},{10,... | collective-permute-start | bytes 884744 | tf_op jit(solution)/shard_map/ppermute | solution.py:447
  4.3 3.9 %collective-permute-start.4 = (s32[2,256]{1,0:T(2,128)}, s32[2,256]{1,0:T(2,128)S(1)}, u32[]{:S(2)}, u32[]{:S(2)}) collective-permute-start(s32[2,256]{1,0:T(2,128)} %codes.1), channel_id=1, source_target_pairs={{0,4},{1,13},{2,22},{3,31},{4,0},{5,9},{6,18},{7,27},{8,12},{9,5},... | collective-permute-start | bytes 6152 | tf_op jit(solution)/shard_map/ppermute | solution.py:447
  5.8 2.4 %collective-permute-start.3 = (s32[2,256]{1,0:T(2,128)}, s32[2,256]{1,0:T(2,128)S(1)}, u32[]{:S(2)}, u32[]{:S(2)}) collective-permute-start(s32[2,256]{1,0:T(2,128)} %codes.1), channel_id=1, source_target_pairs={{0,0},{1,9},{2,18},{3,27},{4,4},{5,13},{6,22},{7,31},{8,8},{9,1},{... | collective-permute-start | bytes 6152 | tf_op jit(solution)/shard_map/ppermute | solution.py:447
  7.2 18.8 %collective-permute-start = (bf16[192,768]{1,0:T(8,128)(2,1)}, bf16[192,768]{1,0:T(8,128)(2,1)S(1)}, u32[]{:S(2)}, u32[]{:S(2)}) collective-permute-start(bf16[192,768]{1,0:T(8,128)(2,1)} %refs_0_.1), channel_id=1, source_target_pairs={{0,1},{1,0},{2,3},{3,2},{4,5},{5,4},{6,7},{7,6},{8,9},{9,8},{10,11... | collective-permute-start | bytes 884744 | tf_op jit(solution)/shard_map/ppermute | solution.py:447
  8.3 0.6 copy-start.4
  8.3 0.6 copy-start.5
  22.2 3.7 %collective-permute-start.2 = (bf16[192,768]{1,0:T(8,128)(2,1)S(1)}, bf16[192,768]{1,0:T(8,128)(2,1)S(1)}, u32[]{:S(2)}, u32[]{:S(2)}) collective-permute-start(bf16[192,768]{1,0:T(8,128)(2,1)S(1)} %collective-permute-done.1.refs_2_), channel_id=1, source_target_pairs={{0,1},{1,0},{2,3},{3,2},{4,5},{5,4},{6,7},{7,6},{8,9},{9,8},{10,11... | collective-permute-start | bytes 884744 | tf_op jit(solution)/shard_map/ppermute | solution.py:447
  22.6 3.4 %copy-start = (bf16[3,192,768]{2,1,0:T(8,128)(2,1)S(1)}, bf16[3,192,768]{2,1,0:T(8,128)(2,1)}, u32[]{:S(2)}) copy-start(bf16[3,192,768]{2,1,0:T(8,128)(2,1)} %param.12) | copy-start | bytes 2654212
  22.6 3.4 %copy-start.1 = (bf16[192,768]{1,0:T(8,128)(2,1)S(1)}, bf16[192,768]{1,0:T(8,128)(2,1)}, u32[]{:S(2)}) copy-start(bf16[192,768]{1,0:T(8,128)(2,1)} %refs_0_.1) | copy-start | bytes 884740
  22.6 3.4 %copy-start.3 = (bf16[33,768]{1,0:T(8,128)(2,1)S(1)}, bf16[33,768]{1,0:T(8,128)(2,1)}, u32[]{:S(2)}) copy-start(bf16[33,768]{1,0:T(8,128)(2,1)} %refs_7_.1) | copy-start | bytes 152068
  40.0 2.5 %copy-start.2 = (bf16[192,768]{1,0:T(8,128)(2,1)S(1)}, bf16[192,768]{1,0:T(8,128)(2,1)}, u32[]{:S(2)}) copy-start(bf16[192,768]{1,0:T(8,128)(2,1)} %col_out_ref.1) | copy-start | bytes 884740

commit v5 on v4

--- a/solution.py
+++ b/solution.py
@@ -14,6 +14,9 @@
 VOCAB_ROWS = 40
 TABLE_ROWS = 48
 
+SMALL_VMEM = 8 * 1024 * 1024
+LARGE_VMEM = 32 * 1024 * 1024
+
 f32 = jnp.float32
 bf16 = jnp.bfloat16
 
@@ -28,7 +31,7 @@
 def softmax_last(scores):
     top = jnp.max(scores, axis=-1, keepdims=True)
     weights = jnp.exp(scores - top)
-    return weights / jnp.sum(weights, axis=-1, keepdims=True)
+    return weights * (1.0 / jnp.sum(weights, axis=-1, keepdims=True))
 
 
 def dot_nt(left, right):
@@ -59,6 +62,7 @@
             pl.BlockSpec(memory_space=pltpu.VMEM),
             pl.BlockSpec(memory_space=pltpu.SMEM),
         ],
+        compiler_params=pltpu.CompilerParams(vmem_limit_bytes=SMALL_VMEM),
         name="codes",
     )(ids, pad_mask)
 
@@ -91,6 +95,7 @@
         cost_estimate=pl.CostEstimate(
             flops=2 * TABLE_ROWS * qkv.size, bytes_accessed=2 * qkv.size, transcendentals=0
         ),
+        compiler_params=pltpu.CompilerParams(vmem_limit_bytes=SMALL_VMEM),
         name="tables",
     )(embed, qkv, *codes)
 
@@ -112,6 +117,13 @@
             jnp.concatenate([zero, second], 1),
         ],
         0,
+    )
+
+
+def double(block):
+    zero = jnp.zeros_like(block)
+    return jnp.concatenate(
+        [jnp.concatenate([block, zero], 1), jnp.concatenate([zero, block], 1)], 0
     )
 
 
@@ -172,29 +184,24 @@
         own_ref[k * own : (k + 1) * own, :] = hot.astype(bf16)
         live_own_ref[k * own : (k + 1) * own, :] = (hot * alive).astype(bf16)
 
+    spans = [slice(hp * LANES, (hp + 1) * LANES) for hp in range(heads // 2)]
+    queries = [spread_pair(table_ref[0, :, span]) for span in spans]
+    keys = [double(table_ref[1, :, span]) for span in spans]
+    scores = [dot_nt(query, key) for query, key in zip(queries, keys)]
+    high = [score.astype(bf16) for score in scores]
+    low = [(score - part.astype(f32)).astype(bf16) for score, part in zip(scores, high)]
     for hp in range(heads // 2):
-        span = slice(hp * LANES, (hp + 1) * LANES)
-        queries = spread_pair(table_ref[0, :, span])
-        keys = table_ref[1, :, span]
-        zero = jnp.zeros_like(keys)
-        keys2 = jnp.concatenate(
-            [jnp.concatenate([keys, zero], 1), jnp.concatenate([zero, keys], 1)], 0
-        )
-        scores = dot_nt(queries, keys2)
-        high = scores.astype(bf16)
-        low = (scores - high.astype(f32)).astype(bf16)
-        looked = dot_nn(
-            live_own_ref[...],
-            jnp.concatenate([high[:LANES], low[:LANES], high[LANES:], low[LANES:]], 1),
-        ).astype(bf16)
         for h2 in range(2):
+            half = slice(h2 * LANES, (h2 + 1) * LANES)
+            looked = dot_nn(
+                live_own_ref[...], jnp.concatenate([high[hp][half], low[hp][half]], 1)
+            ).astype(bf16)
             base = (hp * 2 + h2) * own
             for piece in range(2):
-                at = (h2 * 2 + piece) * LANES
                 for k in range(pairs):
                     to = piece * depth + k * LANES
                     sum_ref[base : base + own, to : to + LANES] = looked[
-                        k * own : (k + 1) * own, at : at + LANES
+                        k * own : (k + 1) * own, piece * LANES : (piece + 1) * LANES
                     ]
     tied = dot_nn(sum_ref[:, 0:depth], hot_ref[...]) + dot_nn(
         sum_ref[:, depth : 2 * depth], hot_ref[...]
@@ -203,17 +210,16 @@
     probs = softmax_last(tied * (HEAD_DIM ** (-0.5) / jnp.sqrt(count))).astype(bf16)
 
     spread_ref[...] = dot_nt(probs, hot_ref[...]).astype(bf16)
+    values = [spread_pair(table_ref[2, :, span]) for span in spans]
+    contexts = []
     for hp in range(heads // 2):
-        values = spread_pair(table_ref[2, :, hp * LANES : (hp + 1) * LANES])
+        first = (hp * 2) * own
         weights = jnp.concatenate(
             [
                 jnp.concatenate(
                     [
-                        spread_ref[
-                            (hp * 2 + h2) * own : (hp * 2 + h2 + 1) * own,
-                            k * LANES : (k + 1) * LANES,
-                        ]
-                        for h2 in range(2)
+                        spread_ref[first : first + own, k * LANES : (k + 1) * LANES],
+                        spread_ref[first + own : first + 2 * own, k * LANES : (k + 1) * LANES],
                     ],
                     1,
                 )
@@ -221,11 +227,12 @@
             ],
             0,
         )
-        context = dot_nn(weights, values).astype(bf16)
+        contexts.append(dot_nn(weights, values[hp]).astype(bf16))
+    for hp in range(heads // 2):
         for k in range(pairs):
             for r2 in range(2):
                 at = (2 * k + r2) * own
-                row_context_ref[at : at + own, hp * LANES : (hp + 1) * LANES] = context[
+                row_context_ref[at : at + own, spans[hp]] = contexts[hp][
                     k * own : (k + 1) * own, r2 * LANES : (r2 + 1) * LANES
                 ]
 
@@ -247,7 +254,7 @@
             pltpu.VMEM((heads * own, rows * CODES), bf16),
         ],
         cost_estimate=pl.CostEstimate(flops=5 * 10**9, bytes_accessed=10**6, transcendentals=0),
-        compiler_params=pltpu.CompilerParams(vmem_limit_bytes=32 * 1024 * 1024),
+        compiler_params=pltpu.CompilerParams(vmem_limit_bytes=LARGE_VMEM),
         name="row_attention",
     )(payload)
 
@@ -306,9 +313,10 @@
         return jnp.swapaxes(values.reshape(shape), 0, 1).reshape(tokens, values.shape[1])
 
     proj = [
-        regroup(dot_nt(normed, col_qkv_ref[t * local : (t + 1) * local, :])).astype(bf16)
-        for t in range(3)
+        dot_nt(normed, col_qkv_ref[t * local : (t + 1) * local, :]) for t in range(3)
     ]
+    proj[0] = proj[0] * HEAD_DIM ** (-0.5)
+    proj = [regroup(values).astype(bf16) for values in proj]
     live = read_sequences(payload_ref, rows, cols, cols + LANES)
     sub, lan = iota((unit, unit), 0), iota((unit, unit), 1)
     same_column = (sub % few) == (lan % few)
@@ -317,24 +325,31 @@
         jnp.where(seq_of_lane == iota((rows, unit), 0), live, 0.0), axis=0, keepdims=True
     )
     visible = jnp.logical_and(same_column, jnp.broadcast_to(live_lane, (unit, unit)) > 0)
-    blocks = []
+    chosen = []
     for g in range(groups):
         at = slice(g * unit, (g + 1) * unit)
-        pieces = []
-        for first in range(0, local, LANES):
+        for h in range(local // HEAD_DIM):
+            first = h * HEAD_DIM // LANES * LANES
             span = slice(first, min(first + LANES, local))
             query, keys, values = (proj[t][at, span] for t in range(3))
-            many = query.shape[1] // HEAD_DIM
-            result = None
-            for h2 in range(many):
-                inside = iota(query.shape, 1) // HEAD_DIM == h2
-                this = query if many == 1 else jnp.where(inside, query, jnp.zeros_like(query))
-                scores = dot_nt(this, keys) * HEAD_DIM ** (-0.5)
-                weights = softmax_last(jnp.where(visible, scores, -jnp.inf)).astype(bf16)
-                found = dot_nn(weights, values)
-                result = found if result is None else jnp.where(inside, found, result)
-            pieces.append(result)
-        blocks.append(jnp.concatenate(pieces, 1))
+            if query.shape[1] > HEAD_DIM:
+                inside = iota(query.shape, 1) // HEAD_DIM == h % 2
+                query = jnp.where(inside, query, jnp.zeros_like(query))
+            chosen.append((query, keys, values))
+    scores = [jnp.where(visible, dot_nt(query, keys), -jnp.inf) for query, keys, _ in chosen]
+    tops = [jnp.max(score, axis=-1, keepdims=True) for score in scores]
+    weights = [jnp.exp(score - top) for score, top in zip(scores, tops)]
+    shares = [1.0 / jnp.sum(weight, axis=-1, keepdims=True) for weight in weights]
+    probs = [(weight * share).astype(bf16) for weight, share in zip(weights, shares)]
+    found = [dot_nn(prob, values) for prob, (_, _, values) in zip(probs, chosen)]
+    many = local // HEAD_DIM
+    first_head = iota((unit, LANES), 1) < HEAD_DIM
+    blocks = [
+        jnp.concatenate(
+            [jnp.where(first_head, found[g * many], found[g * many + 1]), found[g * many + 2]], 1
+        )
+        for g in range(groups)
+    ]
     whole = jnp.concatenate(blocks, 0).reshape(groups, rows, few, local)
     context = jnp.swapaxes(whole, 0, 1).reshape(tokens, local)
     context_ref[0:tokens, :] = context[:, 0:LANES].astype(bf16)
@@ -358,24 +373,23 @@
             pltpu.VMEM((parts, local, width), bf16),
             pltpu.VMEM((2 * CODES, 2 * width), bf16),
         ],
-        compiler_params=pltpu.CompilerParams(vmem_limit_bytes=32 * 1024 * 1024),
+        compiler_params=pltpu.CompilerParams(vmem_limit_bytes=LARGE_VMEM),
         name="column_attention",
     )(*row_outs, payload, row_context, own_codes, embed, col_qkv)
 
 
 def finish_kernel(groups, context_ref, col_out_ref, mixed_ref, out_ref):
-    cores, chips = context_ref.shape[0:2]
+    parts = context_ref.shape[0]
     tokens, local = mixed_ref.shape
     half = tokens // 2
     group = lax.axis_index("seq")
     total = mixed_ref[...]
-    for p in range(cores * chips):
-        core, chip = p % cores, p // cores
+    for p in range(parts):
         weight = col_out_ref[:, p * local : (p + 1) * local]
-        total = total + dot_nt(context_ref[core, chip, 0:tokens, :], weight[:, 0:LANES])
+        total = total + dot_nt(context_ref[p, 0:tokens, :], weight[:, 0:LANES])
         rest = weight[:, LANES:local]
         zero = jnp.zeros_like(rest)
-        last = context_ref[core, chip, tokens : tokens + half, :]
+        last = context_ref[p, tokens : tokens + half, :]
         total = total + jnp.concatenate(
             [
                 dot_nt(last, jnp.concatenate([rest, zero], 1)),
@@ -403,7 +417,7 @@
     return pl.pallas_call(
         functools.partial(finish_kernel, groups),
         out_shape=jax.ShapeDtypeStruct((groups, tokens // groups * local // LANES, LANES), bf16),
-        compiler_params=pltpu.CompilerParams(vmem_limit_bytes=32 * 1024 * 1024),
+        compiler_params=pltpu.CompilerParams(vmem_limit_bytes=LARGE_VMEM),
         name="finish",
     )(contexts, col_out, mixed)
 
@@ -429,6 +443,7 @@
     return pl.pallas_call(
         order_kernel,
         out_shape=jax.ShapeDtypeStruct((2, local, cols), bf16),
+        compiler_params=pltpu.CompilerParams(vmem_limit_bytes=SMALL_VMEM),
         name="order",
     )(blocks)
 
@@ -451,15 +466,15 @@
     sibling = lambda g, p: (g, p ^ 1)
     across = lambda g, p: (g, p ^ 2)
     far = pairwise(row_out, across)
-    row_outs = [row_out, pairwise(row_out, sibling), far, pairwise(far, sibling)]
     payload = make_payload(embed, row_qkv.reshape(3 * local, width), codes)
     payload = lax.all_gather(payload, "head", axis=0)
+    payload, near, far = lax.optimization_barrier((payload, row_out, far))
+    row_outs = [row_out, pairwise(near, sibling), far, pairwise(far, sibling)]
     row_context, own_codes = attend_rows(payload, rows, cols, own, width)
     context, mixed = attend_columns_here(
         row_outs, payload, row_context, own_codes, embed, col_qkv.reshape(3 * local, width), cols
     )
-    contexts = lax.all_gather(context, "head", axis=0, axis_index_groups=[[0, 2], [1, 3]])
-    contexts = lax.all_gather(contexts, "head", axis=0, axis_index_groups=[[0, 1], [2, 3]])
+    contexts = lax.all_gather(context, "head", axis=0)
     blocks = finish(contexts, col_out, mixed, groups)
     blocks = lax.all_to_all(blocks, "seq", split_axis=0, concat_axis=0, tiled=True)
     return jnp.swapaxes(order(blocks, cols, local), 1, 2)

time: 56.9 us -> 51.1 us (0.90)
  Pallas kernels: 15.8 us -> 8.8 us
  local copies, waits for them, and re-layouts: 0.57 us -> 3.35 us
  blocking collectives: 33 us -> 31.3 us
  starting transfers between devices: 7.23 us -> 5.75 us
  waiting for transfers between devices: 0.01 us -> 1.42 us
    pallas_call x1, Pallas kernels: 6.18 us -> 3.34 us  [attend_columns_here(): pl.pallas_call(functools.partial(column_kernel, parts, cols), out_shape=(...]
    unnamed x12 -> x16, local copies, waits for them, and re-layouts: 0.57 us -> 3.35 us
    pallas_call x1, Pallas kernels: 2.32 us -> 0.5 us  [make_payload(): pl.pallas_call(table_kernel, out_shape=jax.ShapeDtypeStruct((TABLE_ROWS,...]
    ppermute x5, starting transfers between devices: 7.23 us -> 5.75 us  [pairwise(): lax.ppermute(value, ('seq', 'head'), [(i, g * parts + p) for i, (g, p) in...]
    ppermute x5, waiting for transfers between devices: 0.01 us -> 1.42 us  [pairwise(): lax.ppermute(value, ('seq', 'head'), [(i, g * parts + p) for i, (g, p) in...]
    all_gather x2 -> x1, blocking collectives: 10.3 us -> 9.02 us  [fast_body(): contexts = lax.all_gather(context, 'head', axis=0)]
    pallas_call x1, Pallas kernels: 1.74 us -> 0.81 us  [order(): pl.pallas_call(order_kernel, out_shape=jax.ShapeDtypeStruct((2, local, co...]
    pallas_call x1, Pallas kernels: 1.38 us -> 0.55 us  [make_codes(): pl.pallas_call(code_kernel, out_shape=jax.ShapeDtypeStruct(ids.shape, jnp...]
  transfers between devices with their start and end apart: 5 -> 5, of which waited for: 0 -> 1; matrix products, arithmetic and copies ran while one was open for 0% -> 0% of each run, Pallas kernels for 12% -> 8%
where the time goes in v5:
time: 51.1 us; the launch traced here: 50.7 us
  blocking collectives  31.3 us (61%)
  Pallas kernels  8.8 us (17%)
  starting transfers between devices  5.75 us (11%)
  local copies, waits for them, and re-layouts  3.35 us (7%)
  waiting for transfers between devices  1.42 us (3%)
    all_gather x1, blocking collectives, fast_body(): payload = lax.all_gather(payload, 'head', axis=0)  11.2 us
    all_to_all x1, blocking collectives, fast_body(): lax.all_to_all(blocks, 'seq', split_axis=0, concat_axis=0, tiled=True)  11.1 us
    all_gather x1, blocking collectives, fast_body(): contexts = lax.all_gather(context, 'head', axis=0)  9.02 us
    ppermute x5, starting transfers between devices, pairwise(): lax.ppermute(value, ('seq', 'head'), [(i, g * parts + p) for i, (g, p) in...  5.75 us
    unnamed x16, local copies, waits for them, and re-layouts  3.35 us
    pallas_call x1, Pallas kernels, attend_columns_here(): pl.pallas_call(functools.partial(column_kernel, parts, cols), out_shape=(...  3.34 us
    pallas_call x1, Pallas kernels, attend_rows(): pl.pallas_call(row_kernel, out_shape=(jax.ShapeDtypeStruct((tokens, width...  2.8 us
    ppermute x5, waiting for transfers between devices, pairwise(): lax.ppermute(value, ('seq', 'head'), [(i, g * parts + p) for i, (g, p) in...  1.42 us
  transfers between devices with their start and end apart: 5, of which 1 were waited for; matrix products, arithmetic and copies ran while one was open for 0% of the time, Pallas kernels for 8%

profile of v5, /device:TPU:0, one launch (start us, length us, event | category | flops | bytes accessed | tf_op | source)
XLA Modules:
  0.0 50.7 jit_solution(4555200779624635622)
XLA Ops:
  0.0 2.9 %collective-permute-start.2 = (bf16[192,768]{1,0:T(8,128)(2,1)}, bf16[192,768]{1,0:T(8,128)(2,1)S(1)}, u32[]{:S(2)}, u32[]{:S(2)}) collective-permute-start(bf16[192,768]{1,0:T(8,128)(2,1)} %refs_0_.1), channel_id=1, source_target_pairs={{0,2},{1,3},{2,0},{3,1},{4,6},{5,7},{6,4},{7,5},{8,10},{9,11},{10,... | collective-permute-start | bytes 884744 | tf_op jit(solution)/shard_map/ppermute | solution.py:462
  2.9 0.0 copy-start.6
  2.9 0.7 %copy-done.6 = s32[2,256]{1,0:T(2,128)S(1)} copy-done((s32[2,256]{1,0:T(2,128)S(1)}, s32[2,256]{1,0:T(2,128)}, u32[]{:S(2)}) %copy-start.6) | copy-done | bytes 2072
  3.6 0.0 copy-start.7
  3.6 0.7 %copy-done.7 = s32[2]{0:T(128)S(1)} copy-done((s32[2]{0:T(128)S(1)}, s32[2]{0:T(128)}, u32[]{:S(2)}) %copy-start.7) | copy-done | bytes 32
  4.3 0.5 %codes.1 = s32[2,256]{1,0:T(2,128)S(1)} custom-call(s32[2,256]{1,0:T(2,128)S(1)} %copy-done.6, s32[2]{0:T(128)S(1)} %copy-done.7), custom_call_target="tpu_custom_call" | custom-call | tf_op jit(solution)/shard_map/codes/pallas_call | solution.py:58
  4.8 1.6 %collective-permute-start.1 = (s32[2,256]{1,0:T(2,128)S(1)}, s32[2,256]{1,0:T(2,128)S(1)}, u32[]{:S(2)}, u32[]{:S(2)}) collective-permute-start(s32[2,256]{1,0:T(2,128)S(1)} %codes.1), channel_id=1, source_target_pairs={{0,4},{1,13},{2,22},{3,31},{4,0},{5,9},{6,18},{7,27},{8,12},{9,5},... | collective-permute-start | bytes 6152 | tf_op jit(solution)/shard_map/ppermute | solution.py:462
  6.4 0.6 %collective-permute-start = (s32[2,256]{1,0:T(2,128)S(1)}, s32[2,256]{1,0:T(2,128)S(1)}, u32[]{:S(2)}, u32[]{:S(2)}) collective-permute-start(s32[2,256]{1,0:T(2,128)S(1)} %codes.1), channel_id=1, source_target_pairs={{0,0},{1,9},{2,18},{3,27},{4,4},{5,13},{6,22},{7,31},{8,8},{9,1},{... | collective-permute-start | bytes 6152 | tf_op jit(solution)/shard_map/ppermute | solution.py:462
  7.1 1.4 %collective-permute-done.1.refs_1_ = s32[2,256]{1,0:T(2,128)S(1)} collective-permute-done((s32[2,256]{1,0:T(2,128)S(1)}, s32[2,256]{1,0:T(2,128)S(1)}, u32[]{:S(2)}, u32[]{:S(2)}) %collective-permute-start.1) | collective-permute-done | bytes 2080 | tf_op jit(solution)/shard_map/ppermute | solution.py:462
  8.5 0.0 collective-permute-done.refs_0_
  8.5 0.0 copy-start.1
  8.5 1.2 %copy-done.1 = bf16[3,192,768]{2,1,0:T(8,128)(2,1)S(1)} copy-done((bf16[3,192,768]{2,1,0:T(8,128)(2,1)S(1)}, bf16[3,192,768]{2,1,0:T(8,128)(2,1)}, u32[]{:S(2)}) %copy-start.1) | copy-done | bytes 884760
  9.7 0.0 copy-start.4
  9.7 0.8 %copy-done.4 = bf16[33,768]{1,0:T(8,128)(2,1)S(1)} copy-done((bf16[33,768]{1,0:T(8,128)(2,1)S(1)}, bf16[33,768]{1,0:T(8,128)(2,1)}, u32[]{:S(2)}) %copy-start.4) | copy-done | bytes 50712
  10.5 0.5 tables.1
  11.0 0.0 copy-start.2
  11.0 11.2 %all-gather = bf16[192,576]{1,0:T(8,128)(2,1)S(1)} all-gather(bf16[48,576]{1,0:T(8,128)(2,1)S(1)} %tables.1), channel_id=2, replica_groups=mesh['seq'=8,'head'=4] {'head'}, dimensions={0}, use_global_device_ids=true | all-gather | bytes 276480 | tf_op jit(solution)/shard_map/all_gather | solution.py:470
  22.2 0.0 collective-permute-done.2.refs_2_
  22.2 0.0 copy-done.2
  22.2 0.0 copy-start
  22.2 0.0 copy-start.5
  22.2 0.4 collective-permute-start.3
  22.6 0.2 collective-permute-start.4
  22.8 2.8 %row_attention.1 = (bf16[512,768]{1,0:T(8,128)(2,1)S(1)}, bf16[256,128]{1,0:T(8,128)(2,1)S(1)}) custom-call(bf16[4,48,576]{2,1,0:T(8,128)(2,1)S(1)} %bitcast.6), custom_call_target="tpu_custom_call" | custom-call | flops 5000000000 | bytes 1000000 | tf_op jit(solution)/shard_map/row_attention/pallas_call | solution.py:243
  25.6 0.0 collective-permute-done.3.refs_1_
  25.6 0.0 collective-permute-done.4.refs_3_
  25.6 0.0 copy-done
  25.6 0.0 copy-done.5
  25.6 3.3 %column_attention.1 = (bf16[768,128]{1,0:T(8,128)(2,1)S(1)}, f32[512,192]{1,0:T(8,128)S(1)}) custom-call(bf16[192,768]{1,0:T(8,128)(2,1)S(1)} %copy-done.2, bf16[192,768]{1,0:T(8,128)(2,1)S(1)} %collective-permute-done.3.refs_1_, bf16[192,768]{1,0:T(8,128)(2,1)S(1)} %collective-permute-done.2.refs_2_, bf16[192,768]{1,0:T(8,128)(2,1)S(1)} %collective-permute-done.4.refs_3_, ...), custom_call_target="tpu_custom_call" | custom-call | tf_op jit(solution)/shard_map/column_attention/pallas_call | solution.py:366
  28.9 0.0 copy-start.3
  29.0 9.0 %all-gather.1 = bf16[3072,128]{1,0:T(8,128)(2,1)S(1)} all-gather(bf16[768,128]{1,0:T(8,128)(2,1)S(1)} %get-tuple-element.17), channel_id=3, replica_groups=mesh['seq'=8,'head'=4] {'head'}, dimensions={0}, use_global_device_ids=true | all-gather | bytes 983040 | tf_op jit(solution)/shard_map/all_gather | solution.py:477
  38.0 0.0 copy-done.3
  38.0 0.8 %finish.1 = bf16[8,96,128]{2,1,0:T(8,128)(2,1)S(1)} custom-call(bf16[4,768,128]{2,1,0:T(8,128)(2,1)S(1)} %bitcast.5, bf16[192,768]{1,0:T(8,128)(2,1)S(1)} %copy-done.3, f32[512,192]{1,0:T(8,128)S(1)} %get-tuple-element.18.mixed_ref), custom_call_target="tpu_custom_call" | custom-call | tf_op jit(solution)/shard_map/finish/pallas_call | solution.py:417
  38.8 11.1 %all_to_all.5.blocks_ref = bf16[8,96,128]{2,1,0:T(8,128)(2,1)S(1)} all-to-all(bf16[8,96,128]{2,1,0:T(8,128)(2,1)S(1)} %finish.1), channel_id=1, replica_groups=mesh['seq'=8,'head'=4] {'seq'}, dimensions={0} | all-to-all | bytes 393216 | tf_op jit(solution)/shard_map/all_to_all | solution.py:479
  49.9 0.8 %order.1 = bf16[2,192,256]{2,1,0:T(8,128)(2,1)} custom-call(bf16[8,96,128]{2,1,0:T(8,128)(2,1)S(1)} %all_to_all.5.blocks_ref), custom_call_target="tpu_custom_call" | custom-call | tf_op jit(solution)/shard_map/order/pallas_call | solution.py:443
Async XLA Ops:
  0.0 22.2 %collective-permute-start.2 = (bf16[192,768]{1,0:T(8,128)(2,1)}, bf16[192,768]{1,0:T(8,128)(2,1)S(1)}, u32[]{:S(2)}, u32[]{:S(2)}) collective-permute-start(bf16[192,768]{1,0:T(8,128)(2,1)} %refs_0_.1), channel_id=1, source_target_pairs={{0,2},{1,3},{2,0},{3,1},{4,6},{5,7},{6,4},{7,5},{8,10},{9,11},{10,... | collective-permute-start | bytes 884744 | tf_op jit(solution)/shard_map/ppermute | solution.py:462
  2.9 0.7 %copy-start.6 = (s32[2,256]{1,0:T(2,128)S(1)}, s32[2,256]{1,0:T(2,128)}, u32[]{:S(2)}) copy-start(s32[2,256]{1,0:T(2,128)} %ids_ref.1) | copy-start | bytes 6148
  3.6 0.7 %copy-start.7 = (s32[2]{0:T(128)S(1)}, s32[2]{0:T(128)}, u32[]{:S(2)}) copy-start(s32[2]{0:T(128)} %live_ref.1) | copy-start | bytes 28
  4.8 3.7 %collective-permute-start.1 = (s32[2,256]{1,0:T(2,128)S(1)}, s32[2,256]{1,0:T(2,128)S(1)}, u32[]{:S(2)}, u32[]{:S(2)}) collective-permute-start(s32[2,256]{1,0:T(2,128)S(1)} %codes.1), channel_id=1, source_target_pairs={{0,4},{1,13},{2,22},{3,31},{4,0},{5,9},{6,18},{7,27},{8,12},{9,5},... | collective-permute-start | bytes 6152 | tf_op jit(solution)/shard_map/ppermute | solution.py:462
  6.4 2.1 %collective-permute-start = (s32[2,256]{1,0:T(2,128)S(1)}, s32[2,256]{1,0:T(2,128)S(1)}, u32[]{:S(2)}, u32[]{:S(2)}) collective-permute-start(s32[2,256]{1,0:T(2,128)S(1)} %codes.1), channel_id=1, source_target_pairs={{0,0},{1,9},{2,18},{3,27},{4,4},{5,13},{6,22},{7,31},{8,8},{9,1},{... | collective-permute-start | bytes 6152 | tf_op jit(solution)/shard_map/ppermute | solution.py:462
  8.5 1.2 %copy-start.1 = (bf16[3,192,768]{2,1,0:T(8,128)(2,1)S(1)}, bf16[3,192,768]{2,1,0:T(8,128)(2,1)}, u32[]{:S(2)}) copy-start(bf16[3,192,768]{2,1,0:T(8,128)(2,1)} %param.10) | copy-start | bytes 2654212
  9.7 0.8 %copy-start.4 = (bf16[33,768]{1,0:T(8,128)(2,1)S(1)}, bf16[33,768]{1,0:T(8,128)(2,1)}, u32[]{:S(2)}) copy-start(bf16[33,768]{1,0:T(8,128)(2,1)} %refs_7_.1) | copy-start | bytes 152068
  11.0 11.2 %copy-start.2 = (bf16[192,768]{1,0:T(8,128)(2,1)S(1)}, bf16[192,768]{1,0:T(8,128)(2,1)}, u32[]{:S(2)}) copy-start(bf16[192,768]{1,0:T(8,128)(2,1)} %refs_0_.1) | copy-start | bytes 884740
  22.2 3.4 %copy-start = (bf16[3,192,768]{2,1,0:T(8,128)(2,1)S(1)}, bf16[3,192,768]{2,1,0:T(8,128)(2,1)}, u32[]{:S(2)}) copy-start(bf16[3,192,768]{2,1,0:T(8,128)(2,1)} %param.12) | copy-start | bytes 2654212
  22.2 3.4 %copy-start.5 = (bf16[33,768]{1,0:T(8,128)(2,1)S(1)}, bf16[33,768]{1,0:T(8,128)(2,1)}, u32[]{:S(2)}) copy-start(bf16[33,768]{1,0:T(8,128)(2,1)} %refs_7_.1) | copy-start | bytes 152068
  22.2 3.4 %collective-permute-start.3 = (bf16[192,768]{1,0:T(8,128)(2,1)S(1)}, bf16[192,768]{1,0:T(8,128)(2,1)S(1)}, u32[]{:S(2)}, u32[]{:S(2)}) collective-permute-start(bf16[192,768]{1,0:T(8,128)(2,1)S(1)} %copy-done.2), channel_id=1, source_target_pairs={{0,1},{1,0},{2,3},{3,2},{4,5},{5,4},{6,7},{7,6},{8,9},{9,8},{10,11... | collective-permute-start | bytes 884744 | tf_op jit(solution)/shard_map/ppermute | solution.py:462
  22.6 3.0 %collective-permute-start.4 = (bf16[192,768]{1,0:T(8,128)(2,1)S(1)}, bf16[192,768]{1,0:T(8,128)(2,1)S(1)}, u32[]{:S(2)}, u32[]{:S(2)}) collective-permute-start(bf16[192,768]{1,0:T(8,128)(2,1)S(1)} %collective-permute-done.2.refs_2_), channel_id=1, source_target_pairs={{0,1},{1,0},{2,3},{3,2},{4,5},{5,4},{6,7},{7,6},{8,9},{9,8},{10,11... | collective-permute-start | bytes 884744 | tf_op jit(solution)/shard_map/ppermute | solution.py:462
  28.9 9.0 %copy-start.3 = (bf16[192,768]{1,0:T(8,128)(2,1)S(1)}, bf16[192,768]{1,0:T(8,128)(2,1)}, u32[]{:S(2)}) copy-start(bf16[192,768]{1,0:T(8,128)(2,1)} %col_out_ref.1) | copy-start | bytes 884740

commit v6 on v5

--- a/solution.py
+++ b/solution.py
@@ -42,11 +42,23 @@
     return jnp.dot(left, right, preferred_element_type=f32)
 
 
+def in_hbm(value):
+    return pltpu.with_memory_space_constraint(value, pltpu.HBM)
+
+
 def iota(shape, axis):
     return lax.broadcasted_iota(jnp.int32, shape, axis)
 
 
-def code_kernel(ids_ref, live_ref, out_ref):
+def code_kernel(ids_hbm, live_hbm, out_ref, ids_ref, live_ref, sems):
+    loads = [
+        pltpu.make_async_copy(ids_hbm, ids_ref, sems.at[0]),
+        pltpu.make_async_copy(live_hbm, live_ref, sems.at[1]),
+    ]
+    for load in loads:
+        load.start()
+    for load in loads:
+        load.wait()
     row = iota(ids_ref.shape, 0)
     live = jnp.zeros(ids_ref.shape, jnp.int32)
     for r in range(ids_ref.shape[0]):
@@ -58,22 +70,60 @@
     return pl.pallas_call(
         code_kernel,
         out_shape=jax.ShapeDtypeStruct(ids.shape, jnp.int32),
-        in_specs=[
-            pl.BlockSpec(memory_space=pltpu.VMEM),
-            pl.BlockSpec(memory_space=pltpu.SMEM),
+        in_specs=[pl.BlockSpec(memory_space=pltpu.HBM)] * 2,
+        scratch_shapes=[
+            pltpu.VMEM(ids.shape, jnp.int32),
+            pltpu.SMEM(pad_mask.shape, jnp.int32),
+            pltpu.SemaphoreType.DMA((2,)),
         ],
         compiler_params=pltpu.CompilerParams(vmem_limit_bytes=SMALL_VMEM),
         name="codes",
-    )(ids, pad_mask)
-
-
-def table_kernel(embed_ref, qkv_ref, *refs):
-    codes_refs, (out_ref, padded_ref) = refs[:-2], refs[-2:]
-    vocab = embed_ref.shape[0]
+    )(in_hbm(ids), in_hbm(pad_mask))
+
+
+def table_kernel(embed_hbm, qkv_hbm, out_ref, embed_ref, qkv_ref, padded_ref, sems):
+    kinds, local = qkv_ref.shape[0:2]
+    loads = [pltpu.make_async_copy(embed_hbm, embed_ref, sems.at[kinds])]
+    loads += [
+        pltpu.make_async_copy(qkv_hbm.at[t], qkv_ref.at[t], sems.at[t]) for t in range(kinds)
+    ]
+    for load in loads:
+        load.start()
     padded_ref[...] = jnp.zeros(padded_ref.shape, f32)
-    padded_ref[0:vocab, :] = embed_ref[...].astype(f32)
+    loads[0].wait()
+    padded_ref[0 : embed_ref.shape[0], :] = embed_ref[...].astype(f32)
     normed = layer_norm(padded_ref[...]).astype(bf16)
-    table = dot_nt(normed, qkv_ref[...])
+    tables = []
+    for t in range(kinds):
+        loads[1 + t].wait()
+        tables.append(dot_nt(normed, qkv_ref[t]))
+    out_ref[...] = jnp.concatenate(tables, 1).astype(bf16)
+
+
+def make_tables(embed, row_qkv):
+    kinds, local, width = row_qkv.shape
+    return pl.pallas_call(
+        table_kernel,
+        out_shape=jax.ShapeDtypeStruct((TABLE_ROWS, kinds * local), bf16),
+        in_specs=[pl.BlockSpec(memory_space=pltpu.HBM)] * 2,
+        scratch_shapes=[
+            pltpu.VMEM(embed.shape, bf16),
+            pltpu.VMEM(row_qkv.shape, bf16),
+            pltpu.VMEM((TABLE_ROWS, width), f32),
+            pltpu.SemaphoreType.DMA((kinds + 1,)),
+        ],
+        cost_estimate=pl.CostEstimate(
+            flops=2 * TABLE_ROWS * row_qkv.size,
+            bytes_accessed=2 * row_qkv.size,
+            transcendentals=0,
+        ),
+        compiler_params=pltpu.CompilerParams(vmem_limit_bytes=SMALL_VMEM),
+        name="tables",
+    )(in_hbm(embed), in_hbm(row_qkv))
+
+
+def pack_kernel(table_ref, *refs):
+    codes_refs, out_ref = refs[:-1], refs[-1]
     coded = jnp.concatenate([ref[...] for ref in codes_refs], 0)
     some, cols = coded.shape
     ids = (coded & 0xFFFF).astype(f32)
@@ -84,20 +134,17 @@
     if some < TABLE_ROWS - VOCAB_ROWS:
         empty = jnp.zeros((TABLE_ROWS - VOCAB_ROWS - some, spare.shape[1]), f32)
         spare = jnp.concatenate([spare, empty], 0)
-    out_ref[...] = jnp.concatenate([table[0:VOCAB_ROWS], spare], 0).astype(bf16)
-
-
-def make_payload(embed, qkv, codes):
+    table = table_ref[...].astype(f32)[0:VOCAB_ROWS]
+    out_ref[...] = jnp.concatenate([table, spare], 0).astype(bf16)
+
+
+def pack(table, codes):
     return pl.pallas_call(
-        table_kernel,
-        out_shape=jax.ShapeDtypeStruct((TABLE_ROWS, qkv.shape[0]), bf16),
-        scratch_shapes=[pltpu.VMEM((TABLE_ROWS, embed.shape[1]), f32)],
-        cost_estimate=pl.CostEstimate(
-            flops=2 * TABLE_ROWS * qkv.size, bytes_accessed=2 * qkv.size, transcendentals=0
-        ),
+        pack_kernel,
+        out_shape=jax.ShapeDtypeStruct(table.shape, bf16),
         compiler_params=pltpu.CompilerParams(vmem_limit_bytes=SMALL_VMEM),
-        name="tables",
-    )(embed, qkv, *codes)
+        name="pack",
+    )(table, *codes)
 
 
 def halves(pair):
@@ -139,25 +186,31 @@
     )
 
 
-def row_kernel(
-    payload_ref,
-    row_context_ref,
-    own_ref,
-    table_ref,
-    hot_ref,
-    live_own_ref,
-    sum_ref,
-    spread_ref,
-):
-    parts = payload_ref.shape[0]
+def row_kernel(parts, *refs):
+    payload_refs, refs = refs[:parts], refs[parts:]
+    (
+        row_context_ref,
+        own_ref,
+        live_ref,
+        payload_ref,
+        table_ref,
+        hot_ref,
+        live_own_ref,
+        sum_ref,
+        spread_ref,
+    ) = refs
     depth, cols = hot_ref.shape
     rows = depth // CODES
     pairs = rows // 2
-    own = own_ref.shape[0] // pairs
-    width = row_context_ref.shape[1]
+    own = live_own_ref.shape[0] // pairs
+    half = own // 2
+    width = row_context_ref.shape[2]
     heads = width // HEAD_DIM
     local = width // parts
     group = lax.axis_index("seq")
+    part = lax.axis_index("head")
+    for p in range(parts):
+        payload_ref[part ^ p] = payload_refs[p][...]
 
     for t in range(3):
         table_ref[t, 0:VOCAB_ROWS, :] = jnp.concatenate(
@@ -167,6 +220,7 @@
 
     ids = read_sequences(payload_ref, rows, 0, cols)
     live = read_sequences(payload_ref, rows, cols, cols + LANES)
+    live_ref[...] = live
     code = iota((CODES, cols), 0).astype(f32)
     for r in range(rows):
         hot = jnp.broadcast_to(ids[r : r + 1, :], (CODES, cols)) == code
@@ -181,7 +235,8 @@
         value = jnp.where(first_half, mine[:, 2 * k : 2 * k + 1], mine[:, 2 * k + 1 : 2 * k + 2])
         hot = (value == lane_code).astype(f32)
         alive = jnp.where(first_half, live[2 * k : 2 * k + 1, :], live[2 * k + 1 : 2 * k + 2, :])
-        own_ref[k * own : (k + 1) * own, :] = hot.astype(bf16)
+        for c in range(2):
+            own_ref[c, k * half : (k + 1) * half, :] = hot[c * half : (c + 1) * half].astype(bf16)
         live_own_ref[k * own : (k + 1) * own, :] = (hot * alive).astype(bf16)
 
     spans = [slice(hp * LANES, (hp + 1) * LANES) for hp in range(heads // 2)]
@@ -192,9 +247,9 @@
     low = [(score - part.astype(f32)).astype(bf16) for score, part in zip(scores, high)]
     for hp in range(heads // 2):
         for h2 in range(2):
-            half = slice(h2 * LANES, (h2 + 1) * LANES)
+            these = slice(h2 * LANES, (h2 + 1) * LANES)
             looked = dot_nn(
-                live_own_ref[...], jnp.concatenate([high[hp][half], low[hp][half]], 1)
+                live_own_ref[...], jnp.concatenate([high[hp][these], low[hp][these]], 1)
             ).astype(bf16)
             base = (hp * 2 + h2) * own
             for piece in range(2):
@@ -231,38 +286,42 @@
     for hp in range(heads // 2):
         for k in range(pairs):
             for r2 in range(2):
-                at = (2 * k + r2) * own
-                row_context_ref[at : at + own, spans[hp]] = contexts[hp][
-                    k * own : (k + 1) * own, r2 * LANES : (r2 + 1) * LANES
-                ]
-
-
-def attend_rows(payload, rows, cols, own, width):
+                at = (2 * k + r2) * half
+                for c in range(2):
+                    row_context_ref[c, at : at + half, spans[hp]] = contexts[hp][
+                        k * own + c * half : k * own + (c + 1) * half,
+                        r2 * LANES : (r2 + 1) * LANES,
+                    ]
+
+
+def attend_rows(payloads, rows, cols, own, width):
     heads = width // HEAD_DIM
-    tokens = rows * own
+    parts = len(payloads)
     return pl.pallas_call(
-        row_kernel,
+        functools.partial(row_kernel, parts),
         out_shape=(
-            jax.ShapeDtypeStruct((tokens, width), bf16),
-            jax.ShapeDtypeStruct((rows // 2 * own, LANES), bf16),
+            jax.ShapeDtypeStruct((2, rows * own // 2, width), bf16),
+            jax.ShapeDtypeStruct((2, rows * own // 4, LANES), bf16),
+            jax.ShapeDtypeStruct((rows, LANES), f32),
         ),
         scratch_shapes=[
+            pltpu.VMEM((parts,) + payloads[0].shape, bf16),
             pltpu.VMEM((3, CODES, width), bf16),
             pltpu.VMEM((rows * CODES, cols), bf16),
             pltpu.VMEM((rows // 2 * own, LANES), bf16),
             pltpu.VMEM((heads * own, 2 * rows * CODES), bf16),
             pltpu.VMEM((heads * own, rows * CODES), bf16),
         ],
-        cost_estimate=pl.CostEstimate(flops=5 * 10**9, bytes_accessed=10**6, transcendentals=0),
+        cost_estimate=pl.CostEstimate(flops=3 * 10**9, bytes_accessed=10**6, transcendentals=0),
         compiler_params=pltpu.CompilerParams(vmem_limit_bytes=LARGE_VMEM),
         name="row_attention",
-    )(payload)
-
-
-def column_kernel(parts, cols, *refs):
+    )(*payloads)
+
+
+def column_kernel(parts, c, *refs):
     row_out_refs, refs = refs[:parts], refs[parts:]
     (
-        payload_ref,
+        live_ref,
         row_context_ref,
         own_ref,
         embed_ref,
@@ -272,10 +331,10 @@
         row_out_ref,
         embed2_ref,
     ) = refs
-    tokens, width = row_context_ref.shape
-    rows = LANES // 8
+    rows = live_ref.shape[0]
+    tokens, width = row_context_ref.shape[1:]
     pairs = rows // 2
-    own = own_ref.shape[0] // pairs
+    own = tokens // rows
     vocab = embed_ref.shape[0]
     local = width // parts
     part = lax.axis_index("head")
@@ -286,7 +345,7 @@
     embed2_ref[0:vocab, 0:width] = embed_ref[...]
     embed2_ref[CODES : CODES + vocab, width : 2 * width] = embed_ref[...]
 
-    embedded2 = dot_nn(own_ref[...], embed2_ref[...])
+    embedded2 = dot_nn(own_ref[c], embed2_ref[...])
     embedded = jnp.concatenate(
         [
             embedded2[k * own : (k + 1) * own, r2 * width : (r2 + 1) * width]
@@ -295,7 +354,7 @@
         ],
         0,
     )
-    mixed = embedded + dot_nt(row_context_ref[...], row_out_ref[...].reshape(width, width))
+    mixed = embedded + dot_nt(row_context_ref[c], row_out_ref[...].reshape(width, width))
     for p in range(parts):
 
         @pl.when(part == p)
@@ -317,12 +376,11 @@
     ]
     proj[0] = proj[0] * HEAD_DIM ** (-0.5)
     proj = [regroup(values).astype(bf16) for values in proj]
-    live = read_sequences(payload_ref, rows, cols, cols + LANES)
     sub, lan = iota((unit, unit), 0), iota((unit, unit), 1)
     same_column = (sub % few) == (lan % few)
     seq_of_lane = iota((rows, unit), 1) // few
     live_lane = jnp.sum(
-        jnp.where(seq_of_lane == iota((rows, unit), 0), live, 0.0), axis=0, keepdims=True
+        jnp.where(seq_of_lane == iota((rows, unit), 0), live_ref[...], 0.0), axis=0, keepdims=True
     )
     visible = jnp.logical_and(same_column, jnp.broadcast_to(live_lane, (unit, unit)) > 0)
     chosen = []
@@ -353,18 +411,18 @@
     whole = jnp.concatenate(blocks, 0).reshape(groups, rows, few, local)
     context = jnp.swapaxes(whole, 0, 1).reshape(tokens, local)
     context_ref[0:tokens, :] = context[:, 0:LANES].astype(bf16)
-    half = tokens // 2
-    context_ref[tokens : tokens + half, :] = jnp.concatenate(
-        [context[0:half, LANES:local], context[half:tokens, LANES:local]], 1
+    some = tokens // 2
+    context_ref[tokens : tokens + some, :] = jnp.concatenate(
+        [context[0:some, LANES:local], context[some:tokens, LANES:local]], 1
     ).astype(bf16)
 
 
-def attend_columns_here(row_outs, payload, row_context, own_codes, embed, col_qkv, cols):
+def attend_columns_here(c, row_outs, live, row_context, own_codes, embed, col_qkv):
     parts = len(row_outs)
-    tokens, width = row_context.shape
+    tokens, width = row_context.shape[1:]
     local = width // parts
     return pl.pallas_call(
-        functools.partial(column_kernel, parts, cols),
+        functools.partial(column_kernel, parts, c),
         out_shape=(
             jax.ShapeDtypeStruct((tokens * local // LANES, LANES), bf16),
             jax.ShapeDtypeStruct((tokens, local), f32),
@@ -373,53 +431,63 @@
             pltpu.VMEM((parts, local, width), bf16),
             pltpu.VMEM((2 * CODES, 2 * width), bf16),
         ],
+        cost_estimate=pl.CostEstimate(flops=2 * 10**9, bytes_accessed=10**6, transcendentals=0),
         compiler_params=pltpu.CompilerParams(vmem_limit_bytes=LARGE_VMEM),
         name="column_attention",
-    )(*row_outs, payload, row_context, own_codes, embed, col_qkv)
-
-
-def finish_kernel(groups, context_ref, col_out_ref, mixed_ref, out_ref):
-    parts = context_ref.shape[0]
-    tokens, local = mixed_ref.shape
-    half = tokens // 2
+    )(*row_outs, live, row_context, own_codes, embed, col_qkv)
+
+
+def finish_kernel(parts, groups, *refs):
+    context_refs = [refs[:parts], refs[parts : 2 * parts]]
+    mixed_refs = refs[2 * parts : 2 * parts + 2]
+    col_out_ref, out_ref, weight_ref = refs[2 * parts + 2 :]
+    tokens, local = mixed_refs[0].shape
+    some = tokens // 2
     group = lax.axis_index("seq")
-    total = mixed_ref[...]
+    part = lax.axis_index("head")
     for p in range(parts):
-        weight = col_out_ref[:, p * local : (p + 1) * local]
-        total = total + dot_nt(context_ref[p, 0:tokens, :], weight[:, 0:LANES])
+        weight_ref[p] = col_out_ref[:, p * local : (p + 1) * local]
+    totals = [ref[...] for ref in mixed_refs]
+    for p in range(parts):
+        weight = weight_ref[part ^ p]
         rest = weight[:, LANES:local]
         zero = jnp.zeros_like(rest)
-        last = context_ref[p, tokens : tokens + half, :]
-        total = total + jnp.concatenate(
-            [
-                dot_nt(last, jnp.concatenate([rest, zero], 1)),
-                dot_nt(last, jnp.concatenate([zero, rest], 1)),
-            ],
-            0,
+        left = jnp.concatenate([rest, zero], 1)
+        right = jnp.concatenate([zero, rest], 1)
+        for c in range(2):
+            context = context_refs[c][p]
+            last = context[tokens : tokens + some, :]
+            totals[c] = (
+                totals[c]
+                + dot_nt(context[0:tokens, :], weight[:, 0:LANES])
+                + jnp.concatenate([dot_nt(last, left), dot_nt(last, right)], 0)
+            )
+    own = tokens // groups // 2
+    for d in range(groups):
+        first, second = (
+            jnp.concatenate(
+                [total[(2 * d + r) * own : (2 * d + r + 1) * own, :] for total in totals], 0
+            )
+            for r in range(2)
         )
-    each = tokens // groups
-    for d in range(groups):
-        block = total[d * each : (d + 1) * each, :]
-        packed = jnp.concatenate(
-            [
-                block[:, 0:LANES],
-                jnp.concatenate(
-                    [block[0 : each // 2, LANES:local], block[each // 2 :, LANES:local]], 1
-                ),
-            ],
-            0,
-        )
-        out_ref[group ^ d] = packed.astype(bf16)
-
-
-def finish(contexts, col_out, mixed, groups):
-    tokens, local = mixed.shape
+        rest = jnp.concatenate([first[:, LANES:local], second[:, LANES:local]], 1)
+        out_ref[group ^ d] = jnp.concatenate(
+            [first[:, 0:LANES], second[:, 0:LANES], rest], 0
+        ).astype(bf16)
+
+
+def finish(contexts, mixed, col_out, groups):
+    parts = len(contexts[0])
+    tokens, local = mixed[0].shape
     return pl.pallas_call(
-        functools.partial(finish_kernel, groups),
-        out_shape=jax.ShapeDtypeStruct((groups, tokens // groups * local // LANES, LANES), bf16),
+        functools.partial(finish_kernel, parts, groups),
+        out_shape=jax.ShapeDtypeStruct(
+            (groups, 2 * tokens // groups * local // LANES, LANES), bf16
+        ),
+        scratch_shapes=[pltpu.VMEM((parts, local, local), bf16)],
         compiler_params=pltpu.CompilerParams(vmem_limit_bytes=LARGE_VMEM),
         name="finish",
-    )(contexts, col_out, mixed)
+    )(*contexts[0], *contexts[1], *mixed, col_out)
 
 
 def order_kernel(blocks_ref, out_ref):
@@ -461,21 +529,33 @@
         link = [(g * parts + p, partner(g, p)) for g, p in order]
         return lax.ppermute(value, ("seq", "head"), [(i, g * parts + p) for i, (g, p) in link])
 
+    def sibling(g, p):
+        return g, p ^ 1
+
+    def across(g, p):
+        return g, p ^ 2
+
+    def opposite(g, p):
+        return g, p ^ 3
+
+    far = pairwise(row_out, across)
     coded = make_codes(ids, pad_mask)
     codes = [pairwise(coded, lambda g, p, b=b: (g ^ (p * each + b), p)) for b in range(each)]
-    sibling = lambda g, p: (g, p ^ 1)
-    across = lambda g, p: (g, p ^ 2)
-    far = pairwise(row_out, across)
-    payload = make_payload(embed, row_qkv.reshape(3 * local, width), codes)
-    payload = lax.all_gather(payload, "head", axis=0)
-    payload, near, far = lax.optimization_barrier((payload, row_out, far))
+    payload = pack(make_tables(embed, row_qkv), codes)
+    payloads = [payload] + [pairwise(payload, to) for to in (sibling, across, opposite)]
+    *payloads, near, far = lax.optimization_barrier((*payloads, row_out, far))
     row_outs = [row_out, pairwise(near, sibling), far, pairwise(far, sibling)]
-    row_context, own_codes = attend_rows(payload, rows, cols, own, width)
-    context, mixed = attend_columns_here(
-        row_outs, payload, row_context, own_codes, embed, col_qkv.reshape(3 * local, width), cols
-    )
-    contexts = lax.all_gather(context, "head", axis=0)
-    blocks = finish(contexts, col_out, mixed, groups)
+    row_context, own_codes, live = attend_rows(payloads, rows, cols, own, width)
+    contexts, mixed = [], []
+    for c in range(2):
+        context, residual = attend_columns_here(
+            c, row_outs, live, row_context, own_codes, embed, col_qkv.reshape(3 * local, width)
+        )
+        beyond = pairwise(context, across)
+        near = pairwise(context, sibling)
+        contexts.append((context, near, beyond, pairwise(beyond, sibling)))
+        mixed.append(residual)
+    blocks = finish(contexts, mixed, col_out, groups)
     blocks = lax.all_to_all(blocks, "seq", split_axis=0, concat_axis=0, tiled=True)
     return jnp.swapaxes(order(blocks, cols, local), 1, 2)
 
@@ -571,7 +651,7 @@
         and rows * 8 == LANES
         and rows_here == 2
         and rows <= 8 * parts
-        and own % 16 == 0
+        and own % 32 == 0
         and cols + LANES <= 3 * local
         and local == LANES + HEAD_DIM
         and embed.shape[0] <= VOCAB_ROWS

time: 51.1 us -> 47 us (0.920)
  blocking collectives: 31.3 us -> 11 us
  starting transfers between devices: 5.75 us -> 15 us
  waiting for transfers between devices: 1.42 us -> 8.99 us
  local copies, waits for them, and re-layouts: 3.35 us -> 0.03 us
  Pallas kernels: 8.8 us -> 11.7 us
    all_gather x2 -> x0, blocking collectives: 20.2 us -> none  [the longest x1 11.2 us: fast_body(): payload = lax.all_gather(payload, 'head', axis=0)]
    ppermute x5 -> x14, starting transfers between devices: 5.75 us -> 15 us  [pairwise(): lax.ppermute(value, ('seq', 'head'), [(i, g * parts + p) for i, (g, p) in...]
    ppermute x5 -> x14, waiting for transfers between devices: 1.42 us -> 8.99 us  [pairwise(): lax.ppermute(value, ('seq', 'head'), [(i, g * parts + p) for i, (g, p) in...]
    unnamed x16 -> x8, local copies, waits for them, and re-layouts: 3.35 us -> 0.03 us
    pallas_call x4 -> x6, Pallas kernels: 7.44 us -> 10.1 us  [the longest x2 4.26 us: attend_columns_here(): pl.pallas_call(functools.partial(column_kernel, parts, c), out_shape=(jax...]
  transfers between devices with their start and end apart: 5 -> 14, of which waited for: 1 -> 5; matrix products, arithmetic and copies ran while one was open for 0% -> 0% of each run, Pallas kernels for 8% -> 16%
where the time goes in v6:
time: 47 us; the launch traced here: 46.8 us
  starting transfers between devices  15 us (32%)
  Pallas kernels  11.7 us (25%)
  blocking collectives  11 us (23%)
  waiting for transfers between devices  8.99 us (19%)
    ppermute x14, starting transfers between devices, pairwise(): lax.ppermute(value, ('seq', 'head'), [(i, g * parts + p) for i, (g, p) in...  15 us
    all_to_all x1, blocking collectives, fast_body(): lax.all_to_all(blocks, 'seq', split_axis=0, concat_axis=0, tiled=True)  11 us
    ppermute x14, waiting for transfers between devices, pairwise(): lax.ppermute(value, ('seq', 'head'), [(i, g * parts + p) for i, (g, p) in...  8.99 us
    pallas_call x2, Pallas kernels, attend_columns_here(): pl.pallas_call(functools.partial(column_kernel, parts, c), out_shape=(jax...  4.26 us
    pallas_call x1, Pallas kernels, attend_rows(): pl.pallas_call(functools.partial(row_kernel, parts), out_shape=(jax.Shape...  2.84 us
    pallas_call x1, Pallas kernels, make_tables(): pl.pallas_call(table_kernel, out_shape=jax.ShapeDtypeStruct((TABLE_ROWS,...  1.85 us
    pallas_call x1, Pallas kernels, finish(): pl.pallas_call(functools.partial(finish_kernel, parts, groups), out_shape...  1.09 us
  transfers between devices with their start and end apart: 14, of which 5 were waited for; matrix products, arithmetic and copies ran while one was open for 0% of the time, Pallas kernels for 16%

profile of v6, /device:TPU:0, one launch (start us, length us, event | category | flops | bytes accessed | tf_op | source)
XLA Modules:
  0.0 46.8 jit_solution(17152892595815404279)
XLA Ops:
  0.0 2.9 %collective-permute-start.5 = (bf16[192,768]{1,0:T(8,128)(2,1)}, bf16[192,768]{1,0:T(8,128)(2,1)S(1)}, u32[]{:S(2)}, u32[]{:S(2)}) collective-permute-start(bf16[192,768]{1,0:T(8,128)(2,1)} %refs_0_.3), channel_id=1, source_target_pairs={{0,2},{1,3},{2,0},{3,1},{4,6},{5,7},{6,4},{7,5},{8,10},{9,11},{10,... | collective-permute-start | bytes 884744 | tf_op jit(solution)/shard_map/ppermute | solution.py:530
  2.9 0.8 %codes.1 = s32[2,256]{1,0:T(2,128)S(1)} custom-call(s32[2,256]{1,0:T(2,128)} %ids_hbm.1, s32[2]{0:T(128)} %live_hbm.1), custom_call_target="tpu_custom_call" | custom-call | tf_op jit(solution)/shard_map/codes/pallas_call | solution.py:70
  3.8 0.0 copy-start.3
  3.8 1.6 %collective-permute-start.1 = (s32[2,256]{1,0:T(2,128)S(1)}, s32[2,256]{1,0:T(2,128)S(1)}, u32[]{:S(2)}, u32[]{:S(2)}) collective-permute-start(s32[2,256]{1,0:T(2,128)S(1)} %codes.1), channel_id=1, source_target_pairs={{0,4},{1,13},{2,22},{3,31},{4,0},{5,9},{6,18},{7,27},{8,12},{9,5},... | collective-permute-start | bytes 6152 | tf_op jit(solution)/shard_map/ppermute | solution.py:530
  5.4 0.6 %collective-permute-start = (s32[2,256]{1,0:T(2,128)S(1)}, s32[2,256]{1,0:T(2,128)S(1)}, u32[]{:S(2)}, u32[]{:S(2)}) collective-permute-start(s32[2,256]{1,0:T(2,128)S(1)} %codes.1), channel_id=1, source_target_pairs={{0,0},{1,9},{2,18},{3,27},{4,4},{5,13},{6,22},{7,31},{8,8},{9,1},{... | collective-permute-start | bytes 6152 | tf_op jit(solution)/shard_map/ppermute | solution.py:530
  6.0 1.8 %tables.1.table_ref = bf16[48,576]{1,0:T(8,128)(2,1)S(1)} custom-call(bf16[33,768]{1,0:T(8,128)(2,1)} %refs_7_.3, bf16[3,192,768]{2,1,0:T(8,128)(2,1)} %qkv_hbm.1), custom_call_target="tpu_custom_call" | custom-call | flops 42467328 | bytes 884736 | tf_op jit(solution)/shard_map/tables/pallas_call | solution.py:105
  7.9 0.0 collective-permute-done.1.refs_1_
  7.9 0.0 collective-permute-done.refs_0_
  7.9 0.0 copy-start.1
  7.9 0.0 copy-start.2
  7.9 6.1 %collective-permute-start.4 = (bf16[48,576]{1,0:T(8,128)(2,1)S(1)}, bf16[48,576]{1,0:T(8,128)(2,1)S(1)}, u32[]{:S(2)}, u32[]{:S(2)}) collective-permute-start(bf16[48,576]{1,0:T(8,128)(2,1)S(1)} %pack.1.refs_0_), channel_id=1, source_target_pairs={{0,3},{1,2},{2,1},{3,0},{4,7},{5,6},{6,5},{7,4},{8,11},{9,10},{10,... | collective-permute-start | bytes 165896 | tf_op jit(solution)/shard_map/ppermute | solution.py:530
  14.0 0.4 collective-permute-start.3
  14.5 0.0 collective-permute-start.2
  14.5 1.9 %collective-permute-done.4.refs_3_ = bf16[48,576]{1,0:T(8,128)(2,1)S(1)} collective-permute-done((bf16[48,576]{1,0:T(8,128)(2,1)S(1)}, bf16[48,576]{1,0:T(8,128)(2,1)S(1)}, u32[]{:S(2)}, u32[]{:S(2)}) %collective-permute-start.4) | collective-permute-done | bytes 55328 | tf_op jit(solution)/shard_map/ppermute | solution.py:530
  16.4 2.0 %collective-permute-done.3.refs_2_ = bf16[48,576]{1,0:T(8,128)(2,1)S(1)} collective-permute-done((bf16[48,576]{1,0:T(8,128)(2,1)S(1)}, bf16[48,576]{1,0:T(8,128)(2,1)S(1)}, u32[]{:S(2)}, u32[]{:S(2)}) %collective-permute-start.3) | collective-permute-done | bytes 55328 | tf_op jit(solution)/shard_map/ppermute | solution.py:530
  18.4 0.0 collective-permute-done.2.refs_1_
  18.4 0.0 collective-permute-done.5.refs_2_
  18.4 0.0 copy-done.3
  18.4 0.1 collective-permute-start.6
  18.5 0.5 %collective-permute-start.7 = (bf16[192,768]{1,0:T(8,128)(2,1)S(1)}, bf16[192,768]{1,0:T(8,128)(2,1)S(1)}, u32[]{:S(2)}, u32[]{:S(2)}) collective-permute-start(bf16[192,768]{1,0:T(8,128)(2,1)S(1)} %collective-permute-done.5.refs_2_), channel_id=1, source_target_pairs={{0,1},{1,0},{2,3},{3,2},{4,5},{5,4},{6,7},{7,6},{8,9},{9,8},{10,11... | collective-permute-start | bytes 884744 | tf_op jit(solution)/shard_map/ppermute | solution.py:530
  19.0 2.8 %row_attention.1 = (bf16[2,256,768]{2,1,0:T(8,128)(2,1)S(1)}, bf16[2,128,128]{2,1,0:T(8,128)(2,1)S(1)}, f32[16,128]{1,0:T(8,128)S(1)}) custom-call(bf16[48,576]{1,0:T(8,128)(2,1)S(1)} %pack.1.refs_0_, bf16[48,576]{1,0:T(8,128)(2,1)S(1)} %collective-permute-done.2.refs_1_, bf16[48,576]{1,0:T(8,128)(2,1)S(1)} %collective-permute-done.3.refs_2_, ...), custom_call_target="tpu_custom_call" | custom-call | flops 3000000000 | bytes 1000000 | tf_op jit(solution)/shard_map/row_attention/pallas_call | solution.py:300
  21.9 0.0 collective-permute-done.6.refs_1_
  21.9 0.0 collective-permute-done.7.refs_3_
  21.9 0.0 copy-done.1
  21.9 0.0 copy-done.2
  21.9 2.1 %column_attention.3 = (bf16[384,128]{1,0:T(8,128)(2,1)S(1)}, f32[256,192]{1,0:T(8,128)S(1)}) custom-call(bf16[192,768]{1,0:T(8,128)(2,1)S(1)} %copy-done.3, bf16[192,768]{1,0:T(8,128)(2,1)S(1)} %collective-permute-done.6.refs_1_, bf16[192,768]{1,0:T(8,128)(2,1)S(1)} %collective-permute-done.5.refs_2_, bf16[192,768]{1,0:T(8,128)(2,1)S(1)} %collective-permute-done.7.refs_3_, ...), custom_call_target="tpu_custom_call" | custom-call | flops 2000000000 | bytes 1000000 | tf_op jit(solution)/shard_map/column_attention/pallas_call | solution.py:424
  24.0 0.0 copy-start
  24.1 1.7 %collective-permute-start.12 = (bf16[384,128]{1,0:T(8,128)(2,1)S(1)}, bf16[384,128]{1,0:T(8,128)(2,1)S(1)}, u32[]{:S(2)}, u32[]{:S(2)}) collective-permute-start(bf16[384,128]{1,0:T(8,128)(2,1)S(1)} %get-tuple-element.28.refs_4_), channel_id=1, source_target_pairs={{0,2},{1,3},{2,0},{3,1},{4,6},{5,7},{6,4},{7,5},{8,10},{9,11},{10,... | collective-permute-start | bytes 294920 | tf_op jit(solution)/shard_map/ppermute | solution.py:530
  25.7 2.1 %column_attention.2 = (bf16[384,128]{1,0:T(8,128)(2,1)S(1)}, f32[256,192]{1,0:T(8,128)S(1)}) custom-call(bf16[192,768]{1,0:T(8,128)(2,1)S(1)} %copy-done.3, bf16[192,768]{1,0:T(8,128)(2,1)S(1)} %collective-permute-done.6.refs_1_, bf16[192,768]{1,0:T(8,128)(2,1)S(1)} %collective-permute-done.5.refs_2_, bf16[192,768]{1,0:T(8,128)(2,1)S(1)} %collective-permute-done.7.refs_3_, ...), custom_call_target="tpu_custom_call" | custom-call | flops 2000000000 | bytes 1000000 | tf_op jit(solution)/shard_map/column_attention/pallas_call | solution.py:424
  27.9 0.5 %collective-permute-start.9 = (bf16[384,128]{1,0:T(8,128)(2,1)S(1)}, bf16[384,128]{1,0:T(8,128)(2,1)S(1)}, u32[]{:S(2)}, u32[]{:S(2)}) collective-permute-start(bf16[384,128]{1,0:T(8,128)(2,1)S(1)} %get-tuple-element.27.refs_0_), channel_id=1, source_target_pairs={{0,2},{1,3},{2,0},{3,1},{4,6},{5,7},{6,4},{7,5},{8,10},{9,11},{10,... | collective-permute-start | bytes 294920 | tf_op jit(solution)/shard_map/ppermute | solution.py:530
  28.4 0.0 collective-permute-start.11
  28.4 0.5 %collective-permute-start.8 = (bf16[384,128]{1,0:T(8,128)(2,1)S(1)}, bf16[384,128]{1,0:T(8,128)(2,1)S(1)}, u32[]{:S(2)}, u32[]{:S(2)}) collective-permute-start(bf16[384,128]{1,0:T(8,128)(2,1)S(1)} %get-tuple-element.27.refs_0_), channel_id=1, source_target_pairs={{0,1},{1,0},{2,3},{3,2},{4,5},{5,4},{6,7},{7,6},{8,9},{9,8},{10,11... | collective-permute-start | bytes 294920 | tf_op jit(solution)/shard_map/ppermute | solution.py:530
  28.9 0.1 collective-permute-done.12.refs_6_
  29.0 0.0 collective-permute-start.13
  29.0 3.6 %collective-permute-done.9.refs_2_ = bf16[384,128]{1,0:T(8,128)(2,1)S(1)} collective-permute-done((bf16[384,128]{1,0:T(8,128)(2,1)S(1)}, bf16[384,128]{1,0:T(8,128)(2,1)S(1)}, u32[]{:S(2)}, u32[]{:S(2)}) %collective-permute-start.9) | collective-permute-done | bytes 98336 | tf_op jit(solution)/shard_map/ppermute | solution.py:530
  32.7 0.0 collective-permute-start.10
  32.7 0.0 collective-permute-done.11.refs_5_
  32.7 0.0 collective-permute-done.8.refs_1_
  32.7 0.0 collective-permute-done.13.refs_7_
  32.7 1.3 %collective-permute-done.10.refs_3_ = bf16[384,128]{1,0:T(8,128)(2,1)S(1)} collective-permute-done((bf16[384,128]{1,0:T(8,128)(2,1)S(1)}, bf16[384,128]{1,0:T(8,128)(2,1)S(1)}, u32[]{:S(2)}, u32[]{:S(2)}) %collective-permute-start.10) | collective-permute-done | bytes 98336 | tf_op jit(solution)/shard_map/ppermute | solution.py:530
  34.0 0.0 copy-done
  34.0 1.1 %finish.1 = bf16[8,96,128]{2,1,0:T(8,128)(2,1)S(1)} custom-call(bf16[384,128]{1,0:T(8,128)(2,1)S(1)} %get-tuple-element.27.refs_0_, bf16[384,128]{1,0:T(8,128)(2,1)S(1)} %collective-permute-done.8.refs_1_, bf16[384,128]{1,0:T(8,128)(2,1)S(1)} %collective-permute-done.9.refs_2_, bf16[384,128]{1,0:T(8,128)(2,1)S(1)} %collective-permute-done.10.refs_3_, ...), custom_call_target="tpu_custom_call" | custom-call | tf_op jit(solution)/shard_map/finish/pallas_call | solution.py:482
  35.1 11.0 %all_to_all.5.blocks_ref = bf16[8,96,128]{2,1,0:T(8,128)(2,1)S(1)} all-to-all(bf16[8,96,128]{2,1,0:T(8,128)(2,1)S(1)} %finish.1), channel_id=1, replica_groups=mesh['seq'=8,'head'=4] {'seq'}, dimensions={0} | all-to-all | bytes 393216 | tf_op jit(solution)/shard_map/all_to_all | solution.py:559
  46.0 0.8 %order.1 = bf16[2,192,256]{2,1,0:T(8,128)(2,1)} custom-call(bf16[8,96,128]{2,1,0:T(8,128)(2,1)S(1)} %all_to_all.5.blocks_ref), custom_call_target="tpu_custom_call" | custom-call | tf_op jit(solution)/shard_map/order/pallas_call | solution.py:511
  (1 shorter events, 0.0 us)
Async XLA Ops:
  0.0 18.4 %collective-permute-start.5 = (bf16[192,768]{1,0:T(8,128)(2,1)}, bf16[192,768]{1,0:T(8,128)(2,1)S(1)}, u32[]{:S(2)}, u32[]{:S(2)}) collective-permute-start(bf16[192,768]{1,0:T(8,128)(2,1)} %refs_0_.3), channel_id=1, source_target_pairs={{0,2},{1,3},{2,0},{3,1},{4,6},{5,7},{6,4},{7,5},{8,10},{9,11},{10,... | collective-permute-start | bytes 884744 | tf_op jit(solution)/shard_map/ppermute | solution.py:530
  3.8 14.7 %copy-start.3 = (bf16[192,768]{1,0:T(8,128)(2,1)S(1)}, bf16[192,768]{1,0:T(8,128)(2,1)}, u32[]{:S(2)}) copy-start(bf16[192,768]{1,0:T(8,128)(2,1)} %refs_0_.3) | copy-start | bytes 884740
  3.8 4.1 %collective-permute-start.1 = (s32[2,256]{1,0:T(2,128)S(1)}, s32[2,256]{1,0:T(2,128)S(1)}, u32[]{:S(2)}, u32[]{:S(2)}) collective-permute-start(s32[2,256]{1,0:T(2,128)S(1)} %codes.1), channel_id=1, source_target_pairs={{0,4},{1,13},{2,22},{3,31},{4,0},{5,9},{6,18},{7,27},{8,12},{9,5},... | collective-permute-start | bytes 6152 | tf_op jit(solution)/shard_map/ppermute | solution.py:530
  5.4 2.5 %collective-permute-start = (s32[2,256]{1,0:T(2,128)S(1)}, s32[2,256]{1,0:T(2,128)S(1)}, u32[]{:S(2)}, u32[]{:S(2)}) collective-permute-start(s32[2,256]{1,0:T(2,128)S(1)} %codes.1), channel_id=1, source_target_pairs={{0,0},{1,9},{2,18},{3,27},{4,4},{5,13},{6,22},{7,31},{8,8},{9,1},{... | collective-permute-start | bytes 6152 | tf_op jit(solution)/shard_map/ppermute | solution.py:530
  7.9 14.0 %copy-start.1 = (bf16[33,768]{1,0:T(8,128)(2,1)S(1)}, bf16[33,768]{1,0:T(8,128)(2,1)}, u32[]{:S(2)}) copy-start(bf16[33,768]{1,0:T(8,128)(2,1)} %refs_7_.3) | copy-start | bytes 152068
  7.9 14.0 %copy-start.2 = (bf16[3,192,768]{2,1,0:T(8,128)(2,1)S(1)}, bf16[3,192,768]{2,1,0:T(8,128)(2,1)}, u32[]{:S(2)}) copy-start(bf16[3,192,768]{2,1,0:T(8,128)(2,1)} %param.12) | copy-start | bytes 2654212
  7.9 8.5 %collective-permute-start.4 = (bf16[48,576]{1,0:T(8,128)(2,1)S(1)}, bf16[48,576]{1,0:T(8,128)(2,1)S(1)}, u32[]{:S(2)}, u32[]{:S(2)}) collective-permute-start(bf16[48,576]{1,0:T(8,128)(2,1)S(1)} %pack.1.refs_0_), channel_id=1, source_target_pairs={{0,3},{1,2},{2,1},{3,0},{4,7},{5,6},{6,5},{7,4},{8,11},{9,10},{10,... | collective-permute-start | bytes 165896 | tf_op jit(solution)/shard_map/ppermute | solution.py:530
  14.0 4.4 %collective-permute-start.3 = (bf16[48,576]{1,0:T(8,128)(2,1)S(1)}, bf16[48,576]{1,0:T(8,128)(2,1)S(1)}, u32[]{:S(2)}, u32[]{:S(2)}) collective-permute-start(bf16[48,576]{1,0:T(8,128)(2,1)S(1)} %pack.1.refs_0_), channel_id=1, source_target_pairs={{0,2},{1,3},{2,0},{3,1},{4,6},{5,7},{6,4},{7,5},{8,10},{9,11},{10,... | collective-permute-start | bytes 165896 | tf_op jit(solution)/shard_map/ppermute | solution.py:530
  14.5 3.9 %collective-permute-start.2 = (bf16[48,576]{1,0:T(8,128)(2,1)S(1)}, bf16[48,576]{1,0:T(8,128)(2,1)S(1)}, u32[]{:S(2)}, u32[]{:S(2)}) collective-permute-start(bf16[48,576]{1,0:T(8,128)(2,1)S(1)} %pack.1.refs_0_), channel_id=1, source_target_pairs={{0,1},{1,0},{2,3},{3,2},{4,5},{5,4},{6,7},{7,6},{8,9},{9,8},{10,11... | collective-permute-start | bytes 165896 | tf_op jit(solution)/shard_map/ppermute | solution.py:530
  18.4 3.4 %collective-permute-start.6 = (bf16[192,768]{1,0:T(8,128)(2,1)S(1)}, bf16[192,768]{1,0:T(8,128)(2,1)S(1)}, u32[]{:S(2)}, u32[]{:S(2)}) collective-permute-start(bf16[192,768]{1,0:T(8,128)(2,1)S(1)} %copy-done.3), channel_id=1, source_target_pairs={{0,1},{1,0},{2,3},{3,2},{4,5},{5,4},{6,7},{7,6},{8,9},{9,8},{10,11... | collective-permute-start | bytes 884744 | tf_op jit(solution)/shard_map/ppermute | solution.py:530
  18.5 3.4 %collective-permute-start.7 = (bf16[192,768]{1,0:T(8,128)(2,1)S(1)}, bf16[192,768]{1,0:T(8,128)(2,1)S(1)}, u32[]{:S(2)}, u32[]{:S(2)}) collective-permute-start(bf16[192,768]{1,0:T(8,128)(2,1)S(1)} %collective-permute-done.5.refs_2_), channel_id=1, source_target_pairs={{0,1},{1,0},{2,3},{3,2},{4,5},{5,4},{6,7},{7,6},{8,9},{9,8},{10,11... | collective-permute-start | bytes 884744 | tf_op jit(solution)/shard_map/ppermute | solution.py:530
  24.0 9.9 %copy-start = (bf16[192,768]{1,0:T(8,128)(2,1)S(1)}, bf16[192,768]{1,0:T(8,128)(2,1)}, u32[]{:S(2)}) copy-start(bf16[192,768]{1,0:T(8,128)(2,1)} %refs_10_.1) | copy-start | bytes 884740
  24.1 5.0 %collective-permute-start.12 = (bf16[384,128]{1,0:T(8,128)(2,1)S(1)}, bf16[384,128]{1,0:T(8,128)(2,1)S(1)}, u32[]{:S(2)}, u32[]{:S(2)}) collective-permute-start(bf16[384,128]{1,0:T(8,128)(2,1)S(1)} %get-tuple-element.28.refs_4_), channel_id=1, source_target_pairs={{0,2},{1,3},{2,0},{3,1},{4,6},{5,7},{6,4},{7,5},{8,10},{9,11},{10,... | collective-permute-start | bytes 294920 | tf_op jit(solution)/shard_map/ppermute | solution.py:530
  27.9 4.8 %collective-permute-start.9 = (bf16[384,128]{1,0:T(8,128)(2,1)S(1)}, bf16[384,128]{1,0:T(8,128)(2,1)S(1)}, u32[]{:S(2)}, u32[]{:S(2)}) collective-permute-start(bf16[384,128]{1,0:T(8,128)(2,1)S(1)} %get-tuple-element.27.refs_0_), channel_id=1, source_target_pairs={{0,2},{1,3},{2,0},{3,1},{4,6},{5,7},{6,4},{7,5},{8,10},{9,11},{10,... | collective-permute-start | bytes 294920 | tf_op jit(solution)/shard_map/ppermute | solution.py:530
  28.4 4.3 %collective-permute-start.11 = (bf16[384,128]{1,0:T(8,128)(2,1)S(1)}, bf16[384,128]{1,0:T(8,128)(2,1)S(1)}, u32[]{:S(2)}, u32[]{:S(2)}) collective-permute-start(bf16[384,128]{1,0:T(8,128)(2,1)S(1)} %get-tuple-element.28.refs_4_), channel_id=1, source_target_pairs={{0,1},{1,0},{2,3},{3,2},{4,5},{5,4},{6,7},{7,6},{8,9},{9,8},{10,11... | collective-permute-start | bytes 294920 | tf_op jit(solution)/shard_map/ppermute | solution.py:530
  28.4 4.3 %collective-permute-start.8 = (bf16[384,128]{1,0:T(8,128)(2,1)S(1)}, bf16[384,128]{1,0:T(8,128)(2,1)S(1)}, u32[]{:S(2)}, u32[]{:S(2)}) collective-permute-start(bf16[384,128]{1,0:T(8,128)(2,1)S(1)} %get-tuple-element.27.refs_0_), channel_id=1, source_target_pairs={{0,1},{1,0},{2,3},{3,2},{4,5},{5,4},{6,7},{7,6},{8,9},{9,8},{10,11... | collective-permute-start | bytes 294920 | tf_op jit(solution)/shard_map/ppermute | solution.py:530
  29.0 3.7 %collective-permute-start.13 = (bf16[384,128]{1,0:T(8,128)(2,1)S(1)}, bf16[384,128]{1,0:T(8,128)(2,1)S(1)}, u32[]{:S(2)}, u32[]{:S(2)}) collective-permute-start(bf16[384,128]{1,0:T(8,128)(2,1)S(1)} %collective-permute-done.12.refs_6_), channel_id=1, source_target_pairs={{0,1},{1,0},{2,3},{3,2},{4,5},{5,4},{6,7},{7,6},{8,9},{9,8},{10,11... | collective-permute-start | bytes 294920 | tf_op jit(solution)/shard_map/ppermute | solution.py:530
  32.7 1.3 %collective-permute-start.10 = (bf16[384,128]{1,0:T(8,128)(2,1)S(1)}, bf16[384,128]{1,0:T(8,128)(2,1)S(1)}, u32[]{:S(2)}, u32[]{:S(2)}) collective-permute-start(bf16[384,128]{1,0:T(8,128)(2,1)S(1)} %collective-permute-done.9.refs_2_), channel_id=1, source_target_pairs={{0,1},{1,0},{2,3},{3,2},{4,5},{5,4},{6,7},{7,6},{8,9},{9,8},{10,11... | collective-permute-start | bytes 294920 | tf_op jit(solution)/shard_map/ppermute | solution.py:530

commit v7 on v6

--- a/solution.py
+++ b/solution.py
@@ -50,35 +50,47 @@
     return lax.broadcasted_iota(jnp.int32, shape, axis)
 
 
-def code_kernel(ids_hbm, live_hbm, out_ref, ids_ref, live_ref, sems):
+def code_kernel(
+    ids_hbm, live_hbm, row_out_hbm, out_ref, early_ref, late_ref, ids_ref, live_ref, sems
+):
+    cut = early_ref.shape[0]
     loads = [
         pltpu.make_async_copy(ids_hbm, ids_ref, sems.at[0]),
         pltpu.make_async_copy(live_hbm, live_ref, sems.at[1]),
+        pltpu.make_async_copy(row_out_hbm.at[0:cut], early_ref, sems.at[2]),
+        pltpu.make_async_copy(row_out_hbm.at[cut : cut + late_ref.shape[0]], late_ref, sems.at[3]),
     ]
     for load in loads:
         load.start()
-    for load in loads:
+    for load in loads[0:2]:
         load.wait()
     row = iota(ids_ref.shape, 0)
     live = jnp.zeros(ids_ref.shape, jnp.int32)
     for r in range(ids_ref.shape[0]):
         live = jnp.where(row == r, live_ref[r], live)
     out_ref[...] = ids_ref[...] + 65536 * live
-
-
-def make_codes(ids, pad_mask):
+    for load in loads[2:]:
+        load.wait()
+
+
+def make_codes(ids, pad_mask, row_out):
+    local, width = row_out.shape
     return pl.pallas_call(
         code_kernel,
-        out_shape=jax.ShapeDtypeStruct(ids.shape, jnp.int32),
-        in_specs=[pl.BlockSpec(memory_space=pltpu.HBM)] * 2,
+        out_shape=(
+            jax.ShapeDtypeStruct(ids.shape, jnp.int32),
+            jax.ShapeDtypeStruct((local - HEAD_DIM, width), bf16),
+            jax.ShapeDtypeStruct((HEAD_DIM, width), bf16),
+        ),
+        in_specs=[pl.BlockSpec(memory_space=pltpu.HBM)] * 3,
         scratch_shapes=[
             pltpu.VMEM(ids.shape, jnp.int32),
             pltpu.SMEM(pad_mask.shape, jnp.int32),
-            pltpu.SemaphoreType.DMA((2,)),
+            pltpu.SemaphoreType.DMA((4,)),
         ],
         compiler_params=pltpu.CompilerParams(vmem_limit_bytes=SMALL_VMEM),
         name="codes",
-    )(in_hbm(ids), in_hbm(pad_mask))
+    )(in_hbm(ids), in_hbm(pad_mask), in_hbm(row_out))
 
 
 def table_kernel(embed_hbm, qkv_hbm, out_ref, embed_ref, qkv_ref, padded_ref, sems):
@@ -319,7 +331,7 @@
 
 
 def column_kernel(parts, c, *refs):
-    row_out_refs, refs = refs[:parts], refs[parts:]
+    row_out_refs, refs = refs[: 2 * parts], refs[2 * parts :]
     (
         live_ref,
         row_context_ref,
@@ -340,7 +352,9 @@
     part = lax.axis_index("head")
 
     for p in range(parts):
-        row_out_ref[part ^ p] = row_out_refs[p][...]
+        early, late = row_out_refs[2 * p : 2 * p + 2]
+        row_out_ref[part ^ p, 0 : early.shape[0]] = early[...]
+        row_out_ref[part ^ p, early.shape[0] : local] = late[...]
     embed2_ref[...] = jnp.zeros(embed2_ref.shape, bf16)
     embed2_ref[0:vocab, 0:width] = embed_ref[...]
     embed2_ref[CODES : CODES + vocab, width : 2 * width] = embed_ref[...]
@@ -418,7 +432,7 @@
 
 
 def attend_columns_here(c, row_outs, live, row_context, own_codes, embed, col_qkv):
-    parts = len(row_outs)
+    parts = len(row_outs) // 2
     tokens, width = row_context.shape[1:]
     local = width // parts
     return pl.pallas_call(
@@ -438,38 +452,31 @@
 
 
 def finish_kernel(parts, groups, *refs):
-    context_refs = [refs[:parts], refs[parts : 2 * parts]]
-    mixed_refs = refs[2 * parts : 2 * parts + 2]
-    col_out_ref, out_ref, weight_ref = refs[2 * parts + 2 :]
-    tokens, local = mixed_refs[0].shape
+    context_refs = refs[:parts]
+    mixed_ref, col_out_ref, out_ref, weight_ref = refs[parts:]
+    tokens, local = mixed_ref.shape
     some = tokens // 2
     group = lax.axis_index("seq")
     part = lax.axis_index("head")
     for p in range(parts):
         weight_ref[p] = col_out_ref[:, p * local : (p + 1) * local]
-    totals = [ref[...] for ref in mixed_refs]
+    total = mixed_ref[...]
     for p in range(parts):
+        context = context_refs[p]
         weight = weight_ref[part ^ p]
         rest = weight[:, LANES:local]
         zero = jnp.zeros_like(rest)
         left = jnp.concatenate([rest, zero], 1)
         right = jnp.concatenate([zero, rest], 1)
-        for c in range(2):
-            context = context_refs[c][p]
-            last = context[tokens : tokens + some, :]
-            totals[c] = (
-                totals[c]
-                + dot_nt(context[0:tokens, :], weight[:, 0:LANES])
-                + jnp.concatenate([dot_nt(last, left), dot_nt(last, right)], 0)
-            )
+        last = context[tokens : tokens + some, :]
+        total = (
+            total
+            + dot_nt(context[0:tokens, :], weight[:, 0:LANES])
+            + jnp.concatenate([dot_nt(last, left), dot_nt(last, right)], 0)
+        )
     own = tokens // groups // 2
     for d in range(groups):
-        first, second = (
-            jnp.concatenate(
-                [total[(2 * d + r) * own : (2 * d + r + 1) * own, :] for total in totals], 0
-            )
-            for r in range(2)
-        )
+        first, second = (total[(2 * d + r) * own : (2 * d + r + 1) * own, :] for r in range(2))
         rest = jnp.concatenate([first[:, LANES:local], second[:, LANES:local]], 1)
         out_ref[group ^ d] = jnp.concatenate(
             [first[:, 0:LANES], second[:, 0:LANES], rest], 0
@@ -477,27 +484,32 @@
 
 
 def finish(contexts, mixed, col_out, groups):
-    parts = len(contexts[0])
-    tokens, local = mixed[0].shape
+    parts = len(contexts)
+    tokens, local = mixed.shape
     return pl.pallas_call(
         functools.partial(finish_kernel, parts, groups),
-        out_shape=jax.ShapeDtypeStruct(
-            (groups, 2 * tokens // groups * local // LANES, LANES), bf16
-        ),
+        out_shape=jax.ShapeDtypeStruct((groups, tokens // groups * local // LANES, LANES), bf16),
         scratch_shapes=[pltpu.VMEM((parts, local, local), bf16)],
+        cost_estimate=pl.CostEstimate(flops=10**9, bytes_accessed=10**6, transcendentals=0),
         compiler_params=pltpu.CompilerParams(vmem_limit_bytes=LARGE_VMEM),
         name="finish",
-    )(*contexts[0], *contexts[1], *mixed, col_out)
-
-
-def order_kernel(blocks_ref, out_ref):
-    groups = blocks_ref.shape[0]
+    )(*contexts, mixed, col_out)
+
+
+def order_kernel(*refs):
+    blocks_refs, out_ref = refs[:-1], refs[-1]
+    groups = blocks_refs[0].shape[0]
     local, cols = out_ref.shape[1:]
-    own = cols // groups
+    own = cols // groups // len(blocks_refs)
     rest = local - LANES
     for part in range(3):
         piece = jnp.concatenate(
-            [blocks_ref[g, part * own : (part + 1) * own, :] for g in range(groups)], 0
+            [
+                ref[g, part * own : (part + 1) * own, :]
+                for g in range(groups)
+                for ref in blocks_refs
+            ],
+            0,
         )
         turned = piece.astype(f32).T.astype(bf16)
         if part < 2:
@@ -513,7 +525,7 @@
         out_shape=jax.ShapeDtypeStruct((2, local, cols), bf16),
         compiler_params=pltpu.CompilerParams(vmem_limit_bytes=SMALL_VMEM),
         name="order",
-    )(blocks)
+    )(*blocks)
 
 
 def fast_body(ids, pad_mask, embed, row_qkv, row_out, col_qkv, col_out):
@@ -538,25 +550,28 @@
     def opposite(g, p):
         return g, p ^ 3
 
-    far = pairwise(row_out, across)
-    coded = make_codes(ids, pad_mask)
+    coded, early, late = make_codes(ids, pad_mask, row_out)
+    early_far = pairwise(early, across)
     codes = [pairwise(coded, lambda g, p, b=b: (g ^ (p * each + b), p)) for b in range(each)]
     payload = pack(make_tables(embed, row_qkv), codes)
     payloads = [payload] + [pairwise(payload, to) for to in (sibling, across, opposite)]
-    *payloads, near, far = lax.optimization_barrier((*payloads, row_out, far))
-    row_outs = [row_out, pairwise(near, sibling), far, pairwise(far, sibling)]
+    *payloads, near, late, early_far = lax.optimization_barrier(
+        (*payloads, early, late, early_far)
+    )
+    row_outs = [early, late, pairwise(near, sibling), pairwise(late, sibling)]
+    row_outs += [early_far, pairwise(late, across)]
+    row_outs += [pairwise(early_far, sibling), pairwise(late, opposite)]
     row_context, own_codes, live = attend_rows(payloads, rows, cols, own, width)
-    contexts, mixed = [], []
+    blocks = []
     for c in range(2):
-        context, residual = attend_columns_here(
+        context, mixed = attend_columns_here(
             c, row_outs, live, row_context, own_codes, embed, col_qkv.reshape(3 * local, width)
         )
         beyond = pairwise(context, across)
         near = pairwise(context, sibling)
-        contexts.append((context, near, beyond, pairwise(beyond, sibling)))
-        mixed.append(residual)
-    blocks = finish(contexts, mixed, col_out, groups)
-    blocks = lax.all_to_all(blocks, "seq", split_axis=0, concat_axis=0, tiled=True)
+        contexts = (context, near, beyond, pairwise(beyond, sibling))
+        block = finish(contexts, mixed, col_out, groups)
+        blocks.append(lax.all_to_all(block, "seq", split_axis=0, concat_axis=0, tiled=True))
     return jnp.swapaxes(order(blocks, cols, local), 1, 2)
 
 

time: 47 us -> 59.5 us (1.27)
  waiting for transfers between devices: 8.99 us -> 16.3 us
  starting transfers between devices: 15 us -> 20.2 us
  blocking collectives: 11 us -> 9.5 us
  Pallas kernels: 11.7 us -> 13 us
    all_to_all x0 -> x1, waiting for transfers between devices: none -> 6.58 us  [fast_body(): lax.all_to_all(block, 'seq', split_axis=0, concat_axis=0, tiled=True)]
    all_to_all x0 -> x1, starting transfers between devices: none -> 3.36 us  [fast_body(): lax.all_to_all(block, 'seq', split_axis=0, concat_axis=0, tiled=True)]
    ppermute x14 -> x17, starting transfers between devices: 15 us -> 16.9 us  [pairwise(): lax.ppermute(value, ('seq', 'head'), [(i, g * parts + p) for i, (g, p) in...]
    all_to_all x1, blocking collectives: 11 us -> 9.5 us  [fast_body(): lax.all_to_all(block, 'seq', split_axis=0, concat_axis=0, tiled=True)]
    pallas_call x1 -> x2, Pallas kernels: 1.09 us -> 2.2 us  [finish(): pl.pallas_call(functools.partial(finish_kernel, parts, groups), out_shape...]
    ppermute x14 -> x17, waiting for transfers between devices: 8.99 us -> 9.68 us  [pairwise(): lax.ppermute(value, ('seq', 'head'), [(i, g * parts + p) for i, (g, p) in...]
  transfers between devices with their start and end apart: 14 -> 18, of which waited for: 5 -> 6; matrix products, arithmetic and copies ran while one was open for 0% -> 0% of each run, Pallas kernels for 16% -> 15%
where the time goes in v7:
time: 59.5 us; the launch traced here: 59.2 us
  starting transfers between devices  20.2 us (34%)
  waiting for transfers between devices  16.3 us (27%)
  Pallas kernels  13 us (22%)
  blocking collectives  9.5 us (16%)
    ppermute x17, starting transfers between devices, pairwise(): lax.ppermute(value, ('seq', 'head'), [(i, g * parts + p) for i, (g, p) in...  16.9 us
    ppermute x17, waiting for transfers between devices, pairwise(): lax.ppermute(value, ('seq', 'head'), [(i, g * parts + p) for i, (g, p) in...  9.68 us
    all_to_all x1, blocking collectives, fast_body(): lax.all_to_all(block, 'seq', split_axis=0, concat_axis=0, tiled=True)  9.5 us
    all_to_all x1, waiting for transfers between devices, fast_body(): lax.all_to_all(block, 'seq', split_axis=0, concat_axis=0, tiled=True)  6.58 us
    pallas_call x2, Pallas kernels, attend_columns_here(): pl.pallas_call(functools.partial(column_kernel, parts, c), out_shape=(jax...  4.26 us
    all_to_all x1, starting transfers between devices, fast_body(): lax.all_to_all(block, 'seq', split_axis=0, concat_axis=0, tiled=True)  3.36 us
    pallas_call x1, Pallas kernels, attend_rows(): pl.pallas_call(functools.partial(row_kernel, parts), out_shape=(jax.Shape...  2.84 us
    pallas_call x2, Pallas kernels, finish(): pl.pallas_call(functools.partial(finish_kernel, parts, groups), out_shape...  2.2 us
  transfers between devices with their start and end apart: 18, of which 6 were waited for; matrix products, arithmetic and copies ran while one was open for 0% of the time, Pallas kernels for 15%

profile of v7, /device:TPU:0, one launch (start us, length us, event | category | flops | bytes accessed | tf_op | source)
XLA Modules:
  0.0 59.2 jit_solution(1019959923723298850)
XLA Ops:
  0.0 1.0 %codes.1 = (s32[2,256]{1,0:T(2,128)S(1)}, bf16[128,768]{1,0:T(8,128)(2,1)S(1)}, bf16[64,768]{1,0:T(8,128)(2,1)S(1)}) custom-call(s32[2,256]{1,0:T(2,128)} %ids_hbm.1, s32[2]{0:T(128)} %live_hbm.1, bf16[192,768]{1,0:T(8,128)(2,1)} %row_out_hbm.1), custom_call_target="tpu_custom_call" | custom-call | tf_op jit(solution)/shard_map/codes/pallas_call | solution.py:78
  1.0 3.0 %collective-permute-start.5 = (bf16[128,768]{1,0:T(8,128)(2,1)S(1)}, bf16[128,768]{1,0:T(8,128)(2,1)S(1)}, u32[]{:S(2)}, u32[]{:S(2)}) collective-permute-start(bf16[128,768]{1,0:T(8,128)(2,1)S(1)} %get-tuple-element.26.refs_0_), channel_id=1, source_target_pairs={{0,2},{1,3},{2,0},{3,1},{4,6},{5,7},{6,4},{7,5},{8,10},{9,11},{10,... | collective-permute-start | bytes 589832 | tf_op jit(solution)/shard_map/ppermute | solution.py:542
  4.0 1.5 %collective-permute-start.1 = (s32[2,256]{1,0:T(2,128)S(1)}, s32[2,256]{1,0:T(2,128)S(1)}, u32[]{:S(2)}, u32[]{:S(2)}) collective-permute-start(s32[2,256]{1,0:T(2,128)S(1)} %get-tuple-element.23), channel_id=1, source_target_pairs={{0,4},{1,13},{2,22},{3,31},{4,0},{5,9},{6,18},{7,27},{8,12},{9,5},... | collective-permute-start | bytes 6152 | tf_op jit(solution)/shard_map/ppermute | solution.py:542
  5.6 0.6 %collective-permute-start = (s32[2,256]{1,0:T(2,128)S(1)}, s32[2,256]{1,0:T(2,128)S(1)}, u32[]{:S(2)}, u32[]{:S(2)}) collective-permute-start(s32[2,256]{1,0:T(2,128)S(1)} %get-tuple-element.23), channel_id=1, source_target_pairs={{0,0},{1,9},{2,18},{3,27},{4,4},{5,13},{6,22},{7,31},{8,8},{9,1},{... | collective-permute-start | bytes 6152 | tf_op jit(solution)/shard_map/ppermute | solution.py:542
  6.2 1.8 %tables.1.table_ref = bf16[48,576]{1,0:T(8,128)(2,1)S(1)} custom-call(bf16[33,768]{1,0:T(8,128)(2,1)} %refs_11_.3, bf16[3,192,768]{2,1,0:T(8,128)(2,1)} %qkv_hbm.1), custom_call_target="tpu_custom_call" | custom-call | flops 42467328 | bytes 884736 | tf_op jit(solution)/shard_map/tables/pallas_call | solution.py:117
  8.1 0.0 collective-permute-done.1.refs_1_
  8.1 0.0 collective-permute-done.refs_0_
  8.1 6.1 %collective-permute-start.4 = (bf16[48,576]{1,0:T(8,128)(2,1)S(1)}, bf16[48,576]{1,0:T(8,128)(2,1)S(1)}, u32[]{:S(2)}, u32[]{:S(2)}) collective-permute-start(bf16[48,576]{1,0:T(8,128)(2,1)S(1)} %pack.1.refs_0_), channel_id=1, source_target_pairs={{0,3},{1,2},{2,1},{3,0},{4,7},{5,6},{6,5},{7,4},{8,11},{9,10},{10,... | collective-permute-start | bytes 165896 | tf_op jit(solution)/shard_map/ppermute | solution.py:542
  14.2 0.4 collective-permute-start.3
  14.7 0.0 collective-permute-start.2
  14.7 1.9 %collective-permute-done.4.refs_3_ = bf16[48,576]{1,0:T(8,128)(2,1)S(1)} collective-permute-done((bf16[48,576]{1,0:T(8,128)(2,1)S(1)}, bf16[48,576]{1,0:T(8,128)(2,1)S(1)}, u32[]{:S(2)}, u32[]{:S(2)}) %collective-permute-start.4) | collective-permute-done | bytes 55328 | tf_op jit(solution)/shard_map/ppermute | solution.py:542
  16.6 2.0 %collective-permute-done.3.refs_2_ = bf16[48,576]{1,0:T(8,128)(2,1)S(1)} collective-permute-done((bf16[48,576]{1,0:T(8,128)(2,1)S(1)}, bf16[48,576]{1,0:T(8,128)(2,1)S(1)}, u32[]{:S(2)}, u32[]{:S(2)}) %collective-permute-start.3) | collective-permute-done | bytes 55328 | tf_op jit(solution)/shard_map/ppermute | solution.py:542
  18.6 0.0 collective-permute-done.2.refs_1_
  18.6 0.0 collective-permute-done.5.refs_4_
  18.6 0.0 copy-start.1
  18.6 1.2 %collective-permute-start.10 = (bf16[64,768]{1,0:T(8,128)(2,1)S(1)}, bf16[64,768]{1,0:T(8,128)(2,1)S(1)}, u32[]{:S(2)}, u32[]{:S(2)}) collective-permute-start(bf16[64,768]{1,0:T(8,128)(2,1)S(1)} %get-tuple-element.25.refs_1_), channel_id=1, source_target_pairs={{0,3},{1,2},{2,1},{3,0},{4,7},{5,6},{6,5},{7,4},{8,11},{9,10},{10,... | collective-permute-start | bytes 294920 | tf_op jit(solution)/shard_map/ppermute | solution.py:542
  19.8 0.6 collective-permute-start.8
  20.4 0.2 collective-permute-start.7
  20.6 0.3 collective-permute-start.6
  20.9 0.2 collective-permute-start.9
  21.1 2.8 %row_attention.1 = (bf16[2,256,768]{2,1,0:T(8,128)(2,1)S(1)}, bf16[2,128,128]{2,1,0:T(8,128)(2,1)S(1)}, f32[16,128]{1,0:T(8,128)S(1)}) custom-call(bf16[48,576]{1,0:T(8,128)(2,1)S(1)} %pack.1.refs_0_, bf16[48,576]{1,0:T(8,128)(2,1)S(1)} %collective-permute-done.2.refs_1_, bf16[48,576]{1,0:T(8,128)(2,1)S(1)} %collective-permute-done.3.refs_2_, ...), custom_call_target="tpu_custom_call" | custom-call | flops 3000000000 | bytes 1000000 | tf_op jit(solution)/shard_map/row_attention/pallas_call | solution.py:312
  23.9 0.0 collective-permute-done.10.refs_7_
  23.9 2.0 %collective-permute-done.8.refs_5_ = bf16[64,768]{1,0:T(8,128)(2,1)S(1)} collective-permute-done((bf16[64,768]{1,0:T(8,128)(2,1)S(1)}, bf16[64,768]{1,0:T(8,128)(2,1)S(1)}, u32[]{:S(2)}, u32[]{:S(2)}) %collective-permute-start.8) | collective-permute-done | bytes 98336 | tf_op jit(solution)/shard_map/ppermute | solution.py:542
  25.9 0.0 collective-permute-done.7.refs_3_
  25.9 0.0 collective-permute-done.6.refs_2_
  25.9 0.0 collective-permute-done.9.refs_6_
  25.9 0.0 copy-done
  25.9 2.1 %column_attention.3 = (bf16[384,128]{1,0:T(8,128)(2,1)S(1)}, f32[256,192]{1,0:T(8,128)S(1)}) custom-call(bf16[128,768]{1,0:T(8,128)(2,1)S(1)} %get-tuple-element.26.refs_0_, bf16[64,768]{1,0:T(8,128)(2,1)S(1)} %get-tuple-element.25.refs_1_, bf16[128,768]{1,0:T(8,128)(2,1)S(1)} %collective-permute-done.6.refs_2_, ...), custom_call_target="tpu_custom_call" | custom-call | flops 2000000000 | bytes 1000000 | tf_op jit(solution)/shard_map/column_attention/pallas_call | solution.py:438
  28.1 0.0 copy-start.2
  28.1 1.7 %collective-permute-start.15 = (bf16[384,128]{1,0:T(8,128)(2,1)S(1)}, bf16[384,128]{1,0:T(8,128)(2,1)S(1)}, u32[]{:S(2)}, u32[]{:S(2)}) collective-permute-start(bf16[384,128]{1,0:T(8,128)(2,1)S(1)} %get-tuple-element.37.refs_0_), channel_id=1, source_target_pairs={{0,2},{1,3},{2,0},{3,1},{4,6},{5,7},{6,4},{7,5},{8,10},{9,11},{10,... | collective-permute-start | bytes 294920 | tf_op jit(solution)/shard_map/ppermute | solution.py:542
  29.8 2.1 %column_attention.2 = (bf16[384,128]{1,0:T(8,128)(2,1)S(1)}, f32[256,192]{1,0:T(8,128)S(1)}) custom-call(bf16[128,768]{1,0:T(8,128)(2,1)S(1)} %get-tuple-element.26.refs_0_, bf16[64,768]{1,0:T(8,128)(2,1)S(1)} %get-tuple-element.25.refs_1_, bf16[128,768]{1,0:T(8,128)(2,1)S(1)} %collective-permute-done.6.refs_2_, ...), custom_call_target="tpu_custom_call" | custom-call | flops 2000000000 | bytes 1000000 | tf_op jit(solution)/shard_map/column_attention/pallas_call | solution.py:438
  31.9 0.5 collective-permute-start.12
  32.4 0.0 collective-permute-start.14
  32.4 0.5 collective-permute-done.15.refs_2_
  32.9 0.0 collective-permute-start.16
  32.9 0.5 collective-permute-start.11
  33.4 3.2 %collective-permute-done.12.refs_2_ = bf16[384,128]{1,0:T(8,128)(2,1)S(1)} collective-permute-done((bf16[384,128]{1,0:T(8,128)(2,1)S(1)}, bf16[384,128]{1,0:T(8,128)(2,1)S(1)}, u32[]{:S(2)}, u32[]{:S(2)}) %collective-permute-start.12) | collective-permute-done | bytes 98336 | tf_op jit(solution)/shard_map/ppermute | solution.py:542
  36.7 0.0 collective-permute-start.13
  36.7 0.0 collective-permute-done.14.refs_1_
  36.7 0.0 collective-permute-done.16.refs_3_
  36.7 1.4 %finish.3 = bf16[8,48,128]{2,1,0:T(8,128)(2,1)} custom-call(bf16[384,128]{1,0:T(8,128)(2,1)S(1)} %get-tuple-element.37.refs_0_, bf16[384,128]{1,0:T(8,128)(2,1)S(1)} %collective-permute-done.14.refs_1_, bf16[384,128]{1,0:T(8,128)(2,1)S(1)} %collective-permute-done.15.refs_2_, bf16[384,128]{1,0:T(8,128)(2,1)S(1)} %collective-permute-done.16.refs_3_, ...), custom_call_target="tpu_custom_call" | custom-call | flops 1000000000 | bytes 1000000 | tf_op jit(solution)/shard_map/finish/pallas_call | solution.py:489
  38.1 3.4 %all-to-all-start.1 = ((bf16[8,48,128]{2,1,0:T(8,128)(2,1)}), bf16[8,48,128]{2,1,0:T(8,128)(2,1)S(1)}, u32[]{:S(2)}, u32[]{:S(2)}) async-start(bf16[8,48,128]{2,1,0:T(8,128)(2,1)} %finish.3), calls=%async_computation.1 | async-start | bytes 196608 | tf_op jit(solution)/shard_map/all_to_all | solution.py:574
  41.5 0.0 collective-permute-done.11.refs_1_
  41.5 0.0 collective-permute-done.13.refs_3_
  41.5 0.8 %finish.2 = bf16[8,48,128]{2,1,0:T(8,128)(2,1)S(1)} custom-call(bf16[384,128]{1,0:T(8,128)(2,1)S(1)} %get-tuple-element.35.refs_0_, bf16[384,128]{1,0:T(8,128)(2,1)S(1)} %collective-permute-done.11.refs_1_, bf16[384,128]{1,0:T(8,128)(2,1)S(1)} %collective-permute-done.12.refs_2_, bf16[384,128]{1,0:T(8,128)(2,1)S(1)} %collective-permute-done.13.refs_3_, ...), custom_call_target="tpu_custom_call" | custom-call | flops 1000000000 | bytes 1000000 | tf_op jit(solution)/shard_map/finish/pallas_call | solution.py:489
  42.3 6.6 %all-to-all-done.1.refs_1_ = bf16[8,48,128]{2,1,0:T(8,128)(2,1)S(1)} async-done(((bf16[8,48,128]{2,1,0:T(8,128)(2,1)}), bf16[8,48,128]{2,1,0:T(8,128)(2,1)S(1)}, u32[]{:S(2)}, u32[]{:S(2)}) %all-to-all-start.1) | async-done | bytes 98336 | tf_op jit(solution)/shard_map/all_to_all | solution.py:574
  48.9 9.5 %all_to_all.10.refs_0_ = bf16[8,48,128]{2,1,0:T(8,128)(2,1)S(1)} all-to-all(bf16[8,48,128]{2,1,0:T(8,128)(2,1)S(1)} %finish.2), channel_id=1, replica_groups=mesh['seq'=8,'head'=4] {'seq'}, dimensions={0} | all-to-all | bytes 196608 | tf_op jit(solution)/shard_map/all_to_all | solution.py:574
  58.4 0.8 %order.1 = bf16[2,192,256]{2,1,0:T(8,128)(2,1)} custom-call(bf16[8,48,128]{2,1,0:T(8,128)(2,1)S(1)} %all_to_all.10.refs_0_, bf16[8,48,128]{2,1,0:T(8,128)(2,1)S(1)} %all-to-all-done.1.refs_1_), custom_call_target="tpu_custom_call" | custom-call | tf_op jit(solution)/shard_map/order/pallas_call | solution.py:523
  (4 shorter events, 0.0 us)
Async XLA Ops:
  1.0 17.6 %collective-permute-start.5 = (bf16[128,768]{1,0:T(8,128)(2,1)S(1)}, bf16[128,768]{1,0:T(8,128)(2,1)S(1)}, u32[]{:S(2)}, u32[]{:S(2)}) collective-permute-start(bf16[128,768]{1,0:T(8,128)(2,1)S(1)} %get-tuple-element.26.refs_0_), channel_id=1, source_target_pairs={{0,2},{1,3},{2,0},{3,1},{4,6},{5,7},{6,4},{7,5},{8,10},{9,11},{10,... | collective-permute-start | bytes 589832 | tf_op jit(solution)/shard_map/ppermute | solution.py:542
  4.0 4.0 %collective-permute-start.1 = (s32[2,256]{1,0:T(2,128)S(1)}, s32[2,256]{1,0:T(2,128)S(1)}, u32[]{:S(2)}, u32[]{:S(2)}) collective-permute-start(s32[2,256]{1,0:T(2,128)S(1)} %get-tuple-element.23), channel_id=1, source_target_pairs={{0,4},{1,13},{2,22},{3,31},{4,0},{5,9},{6,18},{7,27},{8,12},{9,5},... | collective-permute-start | bytes 6152 | tf_op jit(solution)/shard_map/ppermute | solution.py:542
  5.6 2.5 %collective-permute-start = (s32[2,256]{1,0:T(2,128)S(1)}, s32[2,256]{1,0:T(2,128)S(1)}, u32[]{:S(2)}, u32[]{:S(2)}) collective-permute-start(s32[2,256]{1,0:T(2,128)S(1)} %get-tuple-element.23), channel_id=1, source_target_pairs={{0,0},{1,9},{2,18},{3,27},{4,4},{5,13},{6,22},{7,31},{8,8},{9,1},{... | collective-permute-start | bytes 6152 | tf_op jit(solution)/shard_map/ppermute | solution.py:542
  8.1 8.5 %collective-permute-start.4 = (bf16[48,576]{1,0:T(8,128)(2,1)S(1)}, bf16[48,576]{1,0:T(8,128)(2,1)S(1)}, u32[]{:S(2)}, u32[]{:S(2)}) collective-permute-start(bf16[48,576]{1,0:T(8,128)(2,1)S(1)} %pack.1.refs_0_), channel_id=1, source_target_pairs={{0,3},{1,2},{2,1},{3,0},{4,7},{5,6},{6,5},{7,4},{8,11},{9,10},{10,... | collective-permute-start | bytes 165896 | tf_op jit(solution)/shard_map/ppermute | solution.py:542
  14.2 4.4 %collective-permute-start.3 = (bf16[48,576]{1,0:T(8,128)(2,1)S(1)}, bf16[48,576]{1,0:T(8,128)(2,1)S(1)}, u32[]{:S(2)}, u32[]{:S(2)}) collective-permute-start(bf16[48,576]{1,0:T(8,128)(2,1)S(1)} %pack.1.refs_0_), channel_id=1, source_target_pairs={{0,2},{1,3},{2,0},{3,1},{4,6},{5,7},{6,4},{7,5},{8,10},{9,11},{10,... | collective-permute-start | bytes 165896 | tf_op jit(solution)/shard_map/ppermute | solution.py:542
  14.7 3.9 %collective-permute-start.2 = (bf16[48,576]{1,0:T(8,128)(2,1)S(1)}, bf16[48,576]{1,0:T(8,128)(2,1)S(1)}, u32[]{:S(2)}, u32[]{:S(2)}) collective-permute-start(bf16[48,576]{1,0:T(8,128)(2,1)S(1)} %pack.1.refs_0_), channel_id=1, source_target_pairs={{0,1},{1,0},{2,3},{3,2},{4,5},{5,4},{6,7},{7,6},{8,9},{9,8},{10,11... | collective-permute-start | bytes 165896 | tf_op jit(solution)/shard_map/ppermute | solution.py:542
  18.6 7.3 %copy-start = (bf16[33,768]{1,0:T(8,128)(2,1)S(1)}, bf16[33,768]{1,0:T(8,128)(2,1)}, u32[]{:S(2)}) copy-start(bf16[33,768]{1,0:T(8,128)(2,1)} %refs_11_.3) | copy-start | bytes 152068
  18.6 7.3 %copy-start.1 = (bf16[3,192,768]{2,1,0:T(8,128)(2,1)S(1)}, bf16[3,192,768]{2,1,0:T(8,128)(2,1)}, u32[]{:S(2)}) copy-start(bf16[3,192,768]{2,1,0:T(8,128)(2,1)} %param.12) | copy-start | bytes 2654212
  18.6 5.3 %collective-permute-start.10 = (bf16[64,768]{1,0:T(8,128)(2,1)S(1)}, bf16[64,768]{1,0:T(8,128)(2,1)S(1)}, u32[]{:S(2)}, u32[]{:S(2)}) collective-permute-start(bf16[64,768]{1,0:T(8,128)(2,1)S(1)} %get-tuple-element.25.refs_1_), channel_id=1, source_target_pairs={{0,3},{1,2},{2,1},{3,0},{4,7},{5,6},{6,5},{7,4},{8,11},{9,10},{10,... | collective-permute-start | bytes 294920 | tf_op jit(solution)/shard_map/ppermute | solution.py:542
  19.8 6.1 %collective-permute-start.8 = (bf16[64,768]{1,0:T(8,128)(2,1)S(1)}, bf16[64,768]{1,0:T(8,128)(2,1)S(1)}, u32[]{:S(2)}, u32[]{:S(2)}) collective-permute-start(bf16[64,768]{1,0:T(8,128)(2,1)S(1)} %get-tuple-element.25.refs_1_), channel_id=1, source_target_pairs={{0,2},{1,3},{2,0},{3,1},{4,6},{5,7},{6,4},{7,5},{8,10},{9,11},{10,... | collective-permute-start | bytes 294920 | tf_op jit(solution)/shard_map/ppermute | solution.py:542
  20.4 5.5 %collective-permute-start.7 = (bf16[64,768]{1,0:T(8,128)(2,1)S(1)}, bf16[64,768]{1,0:T(8,128)(2,1)S(1)}, u32[]{:S(2)}, u32[]{:S(2)}) collective-permute-start(bf16[64,768]{1,0:T(8,128)(2,1)S(1)} %get-tuple-element.25.refs_1_), channel_id=1, source_target_pairs={{0,1},{1,0},{2,3},{3,2},{4,5},{5,4},{6,7},{7,6},{8,9},{9,8},{10,11... | collective-permute-start | bytes 294920 | tf_op jit(solution)/shard_map/ppermute | solution.py:542
  20.6 5.3 %collective-permute-start.6 = (bf16[128,768]{1,0:T(8,128)(2,1)S(1)}, bf16[128,768]{1,0:T(8,128)(2,1)S(1)}, u32[]{:S(2)}, u32[]{:S(2)}) collective-permute-start(bf16[128,768]{1,0:T(8,128)(2,1)S(1)} %get-tuple-element.26.refs_0_), channel_id=1, source_target_pairs={{0,1},{1,0},{2,3},{3,2},{4,5},{5,4},{6,7},{7,6},{8,9},{9,8},{10,11... | collective-permute-start | bytes 589832 | tf_op jit(solution)/shard_map/ppermute | solution.py:542
  20.9 5.0 %collective-permute-start.9 = (bf16[128,768]{1,0:T(8,128)(2,1)S(1)}, bf16[128,768]{1,0:T(8,128)(2,1)S(1)}, u32[]{:S(2)}, u32[]{:S(2)}) collective-permute-start(bf16[128,768]{1,0:T(8,128)(2,1)S(1)} %collective-permute-done.5.refs_4_), channel_id=1, source_target_pairs={{0,1},{1,0},{2,3},{3,2},{4,5},{5,4},{6,7},{7,6},{8,9},{9,8},{10,11... | collective-permute-start | bytes 589832 | tf_op jit(solution)/shard_map/ppermute | solution.py:542
  28.1 8.6 %copy-start.2 = (bf16[192,768]{1,0:T(8,128)(2,1)S(1)}, bf16[192,768]{1,0:T(8,128)(2,1)}, u32[]{:S(2)}) copy-start(bf16[192,768]{1,0:T(8,128)(2,1)} %refs_5_.3) | copy-start | bytes 884740
  28.1 4.9 %collective-permute-start.15 = (bf16[384,128]{1,0:T(8,128)(2,1)S(1)}, bf16[384,128]{1,0:T(8,128)(2,1)S(1)}, u32[]{:S(2)}, u32[]{:S(2)}) collective-permute-start(bf16[384,128]{1,0:T(8,128)(2,1)S(1)} %get-tuple-element.37.refs_0_), channel_id=1, source_target_pairs={{0,2},{1,3},{2,0},{3,1},{4,6},{5,7},{6,4},{7,5},{8,10},{9,11},{10,... | collective-permute-start | bytes 294920 | tf_op jit(solution)/shard_map/ppermute | solution.py:542
  31.9 4.8 %collective-permute-start.12 = (bf16[384,128]{1,0:T(8,128)(2,1)S(1)}, bf16[384,128]{1,0:T(8,128)(2,1)S(1)}, u32[]{:S(2)}, u32[]{:S(2)}) collective-permute-start(bf16[384,128]{1,0:T(8,128)(2,1)S(1)} %get-tuple-element.35.refs_0_), channel_id=1, source_target_pairs={{0,2},{1,3},{2,0},{3,1},{4,6},{5,7},{6,4},{7,5},{8,10},{9,11},{10,... | collective-permute-start | bytes 294920 | tf_op jit(solution)/shard_map/ppermute | solution.py:542
  32.4 4.3 %collective-permute-start.14 = (bf16[384,128]{1,0:T(8,128)(2,1)S(1)}, bf16[384,128]{1,0:T(8,128)(2,1)S(1)}, u32[]{:S(2)}, u32[]{:S(2)}) collective-permute-start(bf16[384,128]{1,0:T(8,128)(2,1)S(1)} %get-tuple-element.37.refs_0_), channel_id=1, source_target_pairs={{0,1},{1,0},{2,3},{3,2},{4,5},{5,4},{6,7},{7,6},{8,9},{9,8},{10,11... | collective-permute-start | bytes 294920 | tf_op jit(solution)/shard_map/ppermute | solution.py:542
  32.9 3.8 %collective-permute-start.16 = (bf16[384,128]{1,0:T(8,128)(2,1)S(1)}, bf16[384,128]{1,0:T(8,128)(2,1)S(1)}, u32[]{:S(2)}, u32[]{:S(2)}) collective-permute-start(bf16[384,128]{1,0:T(8,128)(2,1)S(1)} %collective-permute-done.15.refs_2_), channel_id=1, source_target_pairs={{0,1},{1,0},{2,3},{3,2},{4,5},{5,4},{6,7},{7,6},{8,9},{9,8},{10,11... | collective-permute-start | bytes 294920 | tf_op jit(solution)/shard_map/ppermute | solution.py:542
  32.9 8.6 %collective-permute-start.11 = (bf16[384,128]{1,0:T(8,128)(2,1)S(1)}, bf16[384,128]{1,0:T(8,128)(2,1)S(1)}, u32[]{:S(2)}, u32[]{:S(2)}) collective-permute-start(bf16[384,128]{1,0:T(8,128)(2,1)S(1)} %get-tuple-element.35.refs_0_), channel_id=1, source_target_pairs={{0,1},{1,0},{2,3},{3,2},{4,5},{5,4},{6,7},{7,6},{8,9},{9,8},{10,11... | collective-permute-start | bytes 294920 | tf_op jit(solution)/shard_map/ppermute | solution.py:542
  36.7 4.8 %collective-permute-start.13 = (bf16[384,128]{1,0:T(8,128)(2,1)S(1)}, bf16[384,128]{1,0:T(8,128)(2,1)S(1)}, u32[]{:S(2)}, u32[]{:S(2)}) collective-permute-start(bf16[384,128]{1,0:T(8,128)(2,1)S(1)} %collective-permute-done.12.refs_2_), channel_id=1, source_target_pairs={{0,1},{1,0},{2,3},{3,2},{4,5},{5,4},{6,7},{7,6},{8,9},{9,8},{10,11... | collective-permute-start | bytes 294920 | tf_op jit(solution)/shard_map/ppermute | solution.py:542
  38.1 10.8 %all-to-all-start.1 = ((bf16[8,48,128]{2,1,0:T(8,128)(2,1)}), bf16[8,48,128]{2,1,0:T(8,128)(2,1)S(1)}, u32[]{:S(2)}, u32[]{:S(2)}) async-start(bf16[8,48,128]{2,1,0:T(8,128)(2,1)} %finish.3), calls=%async_computation.1 | async-start | bytes 196608 | tf_op jit(solution)/shard_map/all_to_all | solution.py:574

commit v8 on v6

--- a/solution.py
+++ b/solution.py
@@ -203,8 +203,7 @@
     rows = depth // CODES
     pairs = rows // 2
     own = live_own_ref.shape[0] // pairs
-    half = own // 2
-    width = row_context_ref.shape[2]
+    width = row_context_ref.shape[1]
     heads = width // HEAD_DIM
     local = width // parts
     group = lax.axis_index("seq")
@@ -235,8 +234,7 @@
         value = jnp.where(first_half, mine[:, 2 * k : 2 * k + 1], mine[:, 2 * k + 1 : 2 * k + 2])
         hot = (value == lane_code).astype(f32)
         alive = jnp.where(first_half, live[2 * k : 2 * k + 1, :], live[2 * k + 1 : 2 * k + 2, :])
-        for c in range(2):
-            own_ref[c, k * half : (k + 1) * half, :] = hot[c * half : (c + 1) * half].astype(bf16)
+        own_ref[k * own : (k + 1) * own, :] = hot.astype(bf16)
         live_own_ref[k * own : (k + 1) * own, :] = (hot * alive).astype(bf16)
 
     spans = [slice(hp * LANES, (hp + 1) * LANES) for hp in range(heads // 2)]
@@ -286,12 +284,10 @@
     for hp in range(heads // 2):
         for k in range(pairs):
             for r2 in range(2):
-                at = (2 * k + r2) * half
-                for c in range(2):
-                    row_context_ref[c, at : at + half, spans[hp]] = contexts[hp][
-                        k * own + c * half : k * own + (c + 1) * half,
-                        r2 * LANES : (r2 + 1) * LANES,
-                    ]
+                at = (2 * k + r2) * own
+                row_context_ref[at : at + own, spans[hp]] = contexts[hp][
+                    k * own : (k + 1) * own, r2 * LANES : (r2 + 1) * LANES
+                ]
 
 
 def attend_rows(payloads, rows, cols, own, width):
@@ -300,8 +296,8 @@
     return pl.pallas_call(
         functools.partial(row_kernel, parts),
         out_shape=(
-            jax.ShapeDtypeStruct((2, rows * own // 2, width), bf16),
-            jax.ShapeDtypeStruct((2, rows * own // 4, LANES), bf16),
+            jax.ShapeDtypeStruct((rows * own, width), bf16),
+            jax.ShapeDtypeStruct((rows * own // 2, LANES), bf16),
             jax.ShapeDtypeStruct((rows, LANES), f32),
         ),
         scratch_shapes=[
@@ -318,7 +314,7 @@
     )(*payloads)
 
 
-def column_kernel(parts, c, *refs):
+def column_kernel(parts, *refs):
     row_out_refs, refs = refs[:parts], refs[parts:]
     (
         live_ref,
@@ -326,13 +322,13 @@
         own_ref,
         embed_ref,
         col_qkv_ref,
-        context_ref,
-        mixed_out_ref,
+        *out_refs,
         row_out_ref,
         embed2_ref,
     ) = refs
+    context_refs, mixed_refs = out_refs[:2], out_refs[2:]
     rows = live_ref.shape[0]
-    tokens, width = row_context_ref.shape[1:]
+    tokens, width = row_context_ref.shape
     pairs = rows // 2
     own = tokens // rows
     vocab = embed_ref.shape[0]
@@ -345,7 +341,7 @@
     embed2_ref[0:vocab, 0:width] = embed_ref[...]
     embed2_ref[CODES : CODES + vocab, width : 2 * width] = embed_ref[...]
 
-    embedded2 = dot_nn(own_ref[c], embed2_ref[...])
+    embedded2 = dot_nn(own_ref[...], embed2_ref[...])
     embedded = jnp.concatenate(
         [
             embedded2[k * own : (k + 1) * own, r2 * width : (r2 + 1) * width]
@@ -354,12 +350,15 @@
         ],
         0,
     )
-    mixed = embedded + dot_nt(row_context_ref[c], row_out_ref[...].reshape(width, width))
+    mixed = embedded + dot_nt(row_context_ref[...], row_out_ref[...].reshape(width, width))
     for p in range(parts):
 
         @pl.when(part == p)
         def _():
-            mixed_out_ref[...] = mixed[:, p * local : (p + 1) * local]
+            for c in range(2):
+                mixed_refs[c][...] = mixed[
+                    c * tokens // 2 : (c + 1) * tokens // 2, p * local : (p + 1) * local
+                ]
 
     normed = layer_norm(mixed).astype(bf16)
 
@@ -410,22 +409,24 @@
     ]
     whole = jnp.concatenate(blocks, 0).reshape(groups, rows, few, local)
     context = jnp.swapaxes(whole, 0, 1).reshape(tokens, local)
-    context_ref[0:tokens, :] = context[:, 0:LANES].astype(bf16)
-    some = tokens // 2
-    context_ref[tokens : tokens + some, :] = jnp.concatenate(
-        [context[0:some, LANES:local], context[some:tokens, LANES:local]], 1
-    ).astype(bf16)
-
-
-def attend_columns_here(c, row_outs, live, row_context, own_codes, embed, col_qkv):
+    half, some = tokens // 2, tokens // 4
+    for c in range(2):
+        part_of = context[c * half : (c + 1) * half]
+        context_refs[c][0:half, :] = part_of[:, 0:LANES].astype(bf16)
+        context_refs[c][half : half + some, :] = jnp.concatenate(
+            [part_of[0:some, LANES:local], part_of[some:half, LANES:local]], 1
+        ).astype(bf16)
+
+
+def attend_columns_here(row_outs, live, row_context, own_codes, embed, col_qkv):
     parts = len(row_outs)
-    tokens, width = row_context.shape[1:]
+    tokens, width = row_context.shape
     local = width // parts
     return pl.pallas_call(
-        functools.partial(column_kernel, parts, c),
+        functools.partial(column_kernel, parts),
         out_shape=(
-            jax.ShapeDtypeStruct((tokens * local // LANES, LANES), bf16),
-            jax.ShapeDtypeStruct((tokens, local), f32),
+            *[jax.ShapeDtypeStruct((tokens // 2 * local // LANES, LANES), bf16)] * 2,
+            *[jax.ShapeDtypeStruct((tokens // 2, local), f32)] * 2,
         ),
         scratch_shapes=[
             pltpu.VMEM((parts, local, width), bf16),
@@ -437,61 +438,55 @@
     )(*row_outs, live, row_context, own_codes, embed, col_qkv)
 
 
-def finish_kernel(parts, groups, *refs):
-    context_refs = [refs[:parts], refs[parts : 2 * parts]]
-    mixed_refs = refs[2 * parts : 2 * parts + 2]
-    col_out_ref, out_ref, weight_ref = refs[2 * parts + 2 :]
-    tokens, local = mixed_refs[0].shape
+def finish_kernel(parts, *refs):
+    context_refs = refs[:parts]
+    mixed_ref, col_out_ref, *out_refs, weight_ref = refs[parts:]
+    tokens, local = mixed_ref.shape
     some = tokens // 2
-    group = lax.axis_index("seq")
     part = lax.axis_index("head")
     for p in range(parts):
         weight_ref[p] = col_out_ref[:, p * local : (p + 1) * local]
-    totals = [ref[...] for ref in mixed_refs]
+    total = mixed_ref[...]
     for p in range(parts):
+        context = context_refs[p]
         weight = weight_ref[part ^ p]
         rest = weight[:, LANES:local]
         zero = jnp.zeros_like(rest)
         left = jnp.concatenate([rest, zero], 1)
         right = jnp.concatenate([zero, rest], 1)
-        for c in range(2):
-            context = context_refs[c][p]
-            last = context[tokens : tokens + some, :]
-            totals[c] = (
-                totals[c]
-                + dot_nt(context[0:tokens, :], weight[:, 0:LANES])
-                + jnp.concatenate([dot_nt(last, left), dot_nt(last, right)], 0)
-            )
-    own = tokens // groups // 2
-    for d in range(groups):
-        first, second = (
-            jnp.concatenate(
-                [total[(2 * d + r) * own : (2 * d + r + 1) * own, :] for total in totals], 0
-            )
-            for r in range(2)
+        last = context[tokens : tokens + some, :]
+        total = (
+            total
+            + dot_nt(context[0:tokens, :], weight[:, 0:LANES])
+            + jnp.concatenate([dot_nt(last, left), dot_nt(last, right)], 0)
         )
+    own = tokens // len(out_refs) // 2
+    for d, out_ref in enumerate(out_refs):
+        first, second = (total[(2 * d + r) * own : (2 * d + r + 1) * own, :] for r in range(2))
         rest = jnp.concatenate([first[:, LANES:local], second[:, LANES:local]], 1)
-        out_ref[group ^ d] = jnp.concatenate(
-            [first[:, 0:LANES], second[:, 0:LANES], rest], 0
-        ).astype(bf16)
-
-
-def finish(contexts, mixed, col_out, groups):
-    parts = len(contexts[0])
-    tokens, local = mixed[0].shape
+        out_ref[...] = jnp.concatenate([first[:, 0:LANES], second[:, 0:LANES], rest], 0).astype(bf16)
+
+
+def finish(contexts, mixed, col_out, slots):
+    parts = len(contexts)
+    tokens, local = mixed.shape
     return pl.pallas_call(
-        functools.partial(finish_kernel, parts, groups),
-        out_shape=jax.ShapeDtypeStruct(
-            (groups, 2 * tokens // groups * local // LANES, LANES), bf16
-        ),
+        functools.partial(finish_kernel, parts),
+        out_shape=[jax.ShapeDtypeStruct((tokens // slots * local // LANES, LANES), bf16)] * slots,
         scratch_shapes=[pltpu.VMEM((parts, local, local), bf16)],
+        cost_estimate=pl.CostEstimate(flops=10**9, bytes_accessed=10**6, transcendentals=0),
         compiler_params=pltpu.CompilerParams(vmem_limit_bytes=LARGE_VMEM),
         name="finish",
-    )(*contexts[0], *contexts[1], *mixed, col_out)
-
-
-def order_kernel(blocks_ref, out_ref):
-    groups = blocks_ref.shape[0]
+    )(*contexts, mixed, col_out)
+
+
+def order_kernel(*refs):
+    *slot_refs, out_ref, blocks_ref = refs
+    groups = len(slot_refs)
+    group = lax.axis_index("seq")
+    for place, slot_ref in enumerate(slot_refs):
+        d = groups - 1 - place
+        blocks_ref[group ^ d] = slot_ref[...]
     local, cols = out_ref.shape[1:]
     own = cols // groups
     rest = local - LANES
@@ -507,13 +502,14 @@
                 out_ref[r, LANES:local, :] = turned[r * rest : (r + 1) * rest, :]
 
 
-def order(blocks, cols, local):
+def order(slots, cols, local):
     return pl.pallas_call(
         order_kernel,
         out_shape=jax.ShapeDtypeStruct((2, local, cols), bf16),
+        scratch_shapes=[pltpu.VMEM((len(slots),) + slots[0].shape, bf16)],
         compiler_params=pltpu.CompilerParams(vmem_limit_bytes=SMALL_VMEM),
         name="order",
-    )(blocks)
+    )(*slots)
 
 
 def fast_body(ids, pad_mask, embed, row_qkv, row_out, col_qkv, col_out):
@@ -546,18 +542,19 @@
     *payloads, near, far = lax.optimization_barrier((*payloads, row_out, far))
     row_outs = [row_out, pairwise(near, sibling), far, pairwise(far, sibling)]
     row_context, own_codes, live = attend_rows(payloads, rows, cols, own, width)
-    contexts, mixed = [], []
-    for c in range(2):
-        context, residual = attend_columns_here(
-            c, row_outs, live, row_context, own_codes, embed, col_qkv.reshape(3 * local, width)
-        )
-        beyond = pairwise(context, across)
-        near = pairwise(context, sibling)
-        contexts.append((context, near, beyond, pairwise(beyond, sibling)))
-        mixed.append(residual)
-    blocks = finish(contexts, mixed, col_out, groups)
-    blocks = lax.all_to_all(blocks, "seq", split_axis=0, concat_axis=0, tiled=True)
-    return jnp.swapaxes(order(blocks, cols, local), 1, 2)
+    *contexts, mixed_low, mixed_high = attend_columns_here(
+        row_outs, live, row_context, own_codes, embed, col_qkv.reshape(3 * local, width)
+    )
+    slots = [None] * groups
+    for c, mixed in ((1, mixed_high), (0, mixed_low)):
+        beyond = pairwise(contexts[c], across)
+        near = pairwise(contexts[c], sibling)
+        whole = (contexts[c], near, beyond, pairwise(beyond, sibling))
+        some = groups // 2
+        for j, block in enumerate(finish(whole, mixed, col_out, some)):
+            d = c * some + j
+            slots[d] = pairwise(block, lambda g, p, d=d: (g ^ d, p)) if d else block
+    return jnp.swapaxes(order(slots[::-1], cols, local), 1, 2)
 
 
 def weight_fold(out_weight, piece):

time: 47 us -> 48.5 us (1.032)
  starting transfers between devices: 15 us -> 26.2 us
  blocking collectives: 11 us -> 0 us
  waiting for transfers between devices: 8.99 us -> 10.8 us
  Pallas kernels: 11.7 us -> 11.2 us
    ppermute x14 -> x21, starting transfers between devices: 15 us -> 26.2 us  [pairwise(): lax.ppermute(value, ('seq', 'head'), [(i, g * parts + p) for i, (g, p) in...]
    all_to_all x1 -> x0, blocking collectives: 11 us -> none  [fast_body(): lax.all_to_all(blocks, 'seq', split_axis=0, concat_axis=0, tiled=True)]
    ppermute x14 -> x21, waiting for transfers between devices: 8.99 us -> 10.8 us  [pairwise(): lax.ppermute(value, ('seq', 'head'), [(i, g * parts + p) for i, (g, p) in...]
  transfers between devices with their start and end apart: 14 -> 21, of which waited for: 5 -> 6; matrix products, arithmetic and copies ran while one was open for 0% -> 0% of each run, Pallas kernels for 16% -> 15%
where the time goes in v8:
time: 48.5 us; the launch traced here: 48.4 us
  starting transfers between devices  26.2 us (54%)
  Pallas kernels  11.2 us (23%)
  waiting for transfers between devices  10.8 us (22%)
    ppermute x21, starting transfers between devices, pairwise(): lax.ppermute(value, ('seq', 'head'), [(i, g * parts + p) for i, (g, p) in...  26.2 us
    ppermute x21, waiting for transfers between devices, pairwise(): lax.ppermute(value, ('seq', 'head'), [(i, g * parts + p) for i, (g, p) in...  10.8 us
    pallas_call x1, Pallas kernels, attend_columns_here(): pl.pallas_call(functools.partial(column_kernel, parts), out_shape=(*[jax....  3.33 us
    pallas_call x1, Pallas kernels, attend_rows(): pl.pallas_call(functools.partial(row_kernel, parts), out_shape=(jax.Shape...  2.84 us
    pallas_call x1, Pallas kernels, make_tables(): pl.pallas_call(table_kernel, out_shape=jax.ShapeDtypeStruct((TABLE_ROWS,...  1.85 us
    pallas_call x2, Pallas kernels, finish(): pl.pallas_call(functools.partial(finish_kernel, parts), out_shape=[jax.Sh...  1.54 us
  transfers between devices with their start and end apart: 21, of which 6 were waited for; matrix products, arithmetic and copies ran while one was open for 0% of the time, Pallas kernels for 15%

profile of v8, /device:TPU:0, one launch (start us, length us, event | category | flops | bytes accessed | tf_op | source)
XLA Modules:
  0.0 48.4 jit_solution(10532872637103590507)
XLA Ops:
  0.0 2.9 %collective-permute-start.5 = (bf16[192,768]{1,0:T(8,128)(2,1)}, bf16[192,768]{1,0:T(8,128)(2,1)S(1)}, u32[]{:S(2)}, u32[]{:S(2)}) collective-permute-start(bf16[192,768]{1,0:T(8,128)(2,1)} %refs_0_.1), channel_id=1, source_target_pairs={{0,2},{1,3},{2,0},{3,1},{4,6},{5,7},{6,4},{7,5},{8,10},{9,11},{10,... | collective-permute-start | bytes 884744 | tf_op jit(solution)/shard_map/ppermute | solution.py:526
  2.9 0.8 %codes.1 = s32[2,256]{1,0:T(2,128)S(1)} custom-call(s32[2,256]{1,0:T(2,128)} %ids_hbm.1, s32[2]{0:T(128)} %live_hbm.1), custom_call_target="tpu_custom_call" | custom-call | tf_op jit(solution)/shard_map/codes/pallas_call | solution.py:70
  3.8 0.0 copy-start.2
  3.8 1.6 %collective-permute-start.1 = (s32[2,256]{1,0:T(2,128)S(1)}, s32[2,256]{1,0:T(2,128)S(1)}, u32[]{:S(2)}, u32[]{:S(2)}) collective-permute-start(s32[2,256]{1,0:T(2,128)S(1)} %codes.1), channel_id=1, source_target_pairs={{0,4},{1,13},{2,22},{3,31},{4,0},{5,9},{6,18},{7,27},{8,12},{9,5},... | collective-permute-start | bytes 6152 | tf_op jit(solution)/shard_map/ppermute | solution.py:526
  5.4 0.6 %collective-permute-start = (s32[2,256]{1,0:T(2,128)S(1)}, s32[2,256]{1,0:T(2,128)S(1)}, u32[]{:S(2)}, u32[]{:S(2)}) collective-permute-start(s32[2,256]{1,0:T(2,128)S(1)} %codes.1), channel_id=1, source_target_pairs={{0,0},{1,9},{2,18},{3,27},{4,4},{5,13},{6,22},{7,31},{8,8},{9,1},{... | collective-permute-start | bytes 6152 | tf_op jit(solution)/shard_map/ppermute | solution.py:526
  6.0 1.8 %tables.1.table_ref = bf16[48,576]{1,0:T(8,128)(2,1)S(1)} custom-call(bf16[33,768]{1,0:T(8,128)(2,1)} %refs_7_.1, bf16[3,192,768]{2,1,0:T(8,128)(2,1)} %qkv_hbm.1), custom_call_target="tpu_custom_call" | custom-call | flops 42467328 | bytes 884736 | tf_op jit(solution)/shard_map/tables/pallas_call | solution.py:105
  7.9 0.0 collective-permute-done.1.refs_1_
  7.9 0.0 collective-permute-done.refs_0_
  7.9 0.0 copy-start
  7.9 0.0 copy-start.1
  7.9 6.1 %collective-permute-start.4 = (bf16[48,576]{1,0:T(8,128)(2,1)S(1)}, bf16[48,576]{1,0:T(8,128)(2,1)S(1)}, u32[]{:S(2)}, u32[]{:S(2)}) collective-permute-start(bf16[48,576]{1,0:T(8,128)(2,1)S(1)} %pack.1.refs_0_), channel_id=1, source_target_pairs={{0,3},{1,2},{2,1},{3,0},{4,7},{5,6},{6,5},{7,4},{8,11},{9,10},{10,... | collective-permute-start | bytes 165896 | tf_op jit(solution)/shard_map/ppermute | solution.py:526
  14.0 0.4 collective-permute-start.3
  14.5 0.0 collective-permute-start.2
  14.5 1.9 %collective-permute-done.4.refs_3_ = bf16[48,576]{1,0:T(8,128)(2,1)S(1)} collective-permute-done((bf16[48,576]{1,0:T(8,128)(2,1)S(1)}, bf16[48,576]{1,0:T(8,128)(2,1)S(1)}, u32[]{:S(2)}, u32[]{:S(2)}) %collective-permute-start.4) | collective-permute-done | bytes 55328 | tf_op jit(solution)/shard_map/ppermute | solution.py:526
  16.4 2.0 %collective-permute-done.3.refs_2_ = bf16[48,576]{1,0:T(8,128)(2,1)S(1)} collective-permute-done((bf16[48,576]{1,0:T(8,128)(2,1)S(1)}, bf16[48,576]{1,0:T(8,128)(2,1)S(1)}, u32[]{:S(2)}, u32[]{:S(2)}) %collective-permute-start.3) | collective-permute-done | bytes 55328 | tf_op jit(solution)/shard_map/ppermute | solution.py:526
  18.4 0.0 collective-permute-done.2.refs_1_
  18.4 0.0 collective-permute-done.5.refs_2_
  18.4 0.1 collective-permute-start.6
  18.5 0.5 %collective-permute-start.7 = (bf16[192,768]{1,0:T(8,128)(2,1)S(1)}, bf16[192,768]{1,0:T(8,128)(2,1)S(1)}, u32[]{:S(2)}, u32[]{:S(2)}) collective-permute-start(bf16[192,768]{1,0:T(8,128)(2,1)S(1)} %collective-permute-done.5.refs_2_), channel_id=1, source_target_pairs={{0,1},{1,0},{2,3},{3,2},{4,5},{5,4},{6,7},{7,6},{8,9},{9,8},{10,11... | collective-permute-start | bytes 884744 | tf_op jit(solution)/shard_map/ppermute | solution.py:526
  19.0 2.8 %row_attention.1 = (bf16[512,768]{1,0:T(8,128)(2,1)S(1)}, bf16[256,128]{1,0:T(8,128)(2,1)S(1)}, f32[16,128]{1,0:T(8,128)S(1)}) custom-call(bf16[48,576]{1,0:T(8,128)(2,1)S(1)} %pack.1.refs_0_, bf16[48,576]{1,0:T(8,128)(2,1)S(1)} %collective-permute-done.2.refs_1_, bf16[48,576]{1,0:T(8,128)(2,1)S(1)} %collective-permute-done.3.refs_2_, ...), custom_call_target="tpu_custom_call" | custom-call | flops 3000000000 | bytes 1000000 | tf_op jit(solution)/shard_map/row_attention/pallas_call | solution.py:296
  21.9 0.0 collective-permute-done.6.refs_1_
  21.9 0.0 collective-permute-done.7.refs_3_
  21.9 0.0 copy-start.3
  21.9 3.3 %column_attention.1 = (bf16[384,128]{1,0:T(8,128)(2,1)S(1)}, bf16[384,128]{1,0:T(8,128)(2,1)S(1)}, f32[256,192]{1,0:T(8,128)S(1)}, f32[256,192]{1,0:T(8,128)S(1)}) custom-call(bf16[192,768]{1,0:T(8,128)(2,1)S(1)} %copy-done.2, bf16[192,768]{1,0:T(8,128)(2,1)S(1)} %collective-permute-done.6.refs_1_, bf16[192,768]{1,0:T(8,128)(2,1)S(1)} %collective-permute-done.5.refs_2_, ...), custom_call_target="tpu_custom_call" | custom-call | flops 2000000000 | bytes 1000000 | tf_op jit(solution)/shard_map/column_attention/pallas_call | solution.py:425
  25.2 1.7 %collective-permute-start.9 = (bf16[384,128]{1,0:T(8,128)(2,1)S(1)}, bf16[384,128]{1,0:T(8,128)(2,1)S(1)}, u32[]{:S(2)}, u32[]{:S(2)}) collective-permute-start(bf16[384,128]{1,0:T(8,128)(2,1)S(1)} %get-tuple-element.35.refs_0_), channel_id=1, source_target_pairs={{0,2},{1,3},{2,0},{3,1},{4,6},{5,7},{6,4},{7,5},{8,10},{9,11},{10,... | collective-permute-start | bytes 294920 | tf_op jit(solution)/shard_map/ppermute | solution.py:526
  26.9 0.4 collective-permute-start.16
  27.3 0.0 collective-permute-start.8
  27.3 3.6 %collective-permute-done.9.refs_2_ = bf16[384,128]{1,0:T(8,128)(2,1)S(1)} collective-permute-done((bf16[384,128]{1,0:T(8,128)(2,1)S(1)}, bf16[384,128]{1,0:T(8,128)(2,1)S(1)}, u32[]{:S(2)}, u32[]{:S(2)}) %collective-permute-start.9) | collective-permute-done | bytes 98336 | tf_op jit(solution)/shard_map/ppermute | solution.py:526
  30.9 0.0 collective-permute-start.10
  30.9 0.5 %collective-permute-start.15 = (bf16[384,128]{1,0:T(8,128)(2,1)S(1)}, bf16[384,128]{1,0:T(8,128)(2,1)S(1)}, u32[]{:S(2)}, u32[]{:S(2)}) collective-permute-start(bf16[384,128]{1,0:T(8,128)(2,1)S(1)} %get-tuple-element.41.refs_0_), channel_id=1, source_target_pairs={{0,1},{1,0},{2,3},{3,2},{4,5},{5,4},{6,7},{7,6},{8,9},{9,8},{10,11... | collective-permute-start | bytes 294920 | tf_op jit(solution)/shard_map/ppermute | solution.py:526
  31.4 0.9 %collective-permute-done.16.refs_2_ = bf16[384,128]{1,0:T(8,128)(2,1)S(1)} collective-permute-done((bf16[384,128]{1,0:T(8,128)(2,1)S(1)}, bf16[384,128]{1,0:T(8,128)(2,1)S(1)}, u32[]{:S(2)}, u32[]{:S(2)}) %collective-permute-start.16) | collective-permute-done | bytes 98336 | tf_op jit(solution)/shard_map/ppermute | solution.py:526
  32.4 0.0 collective-permute-done.10.refs_3_
  32.4 0.8 %finish.2 = (bf16[96,128]{1,0:T(8,128)(2,1)S(1)}, bf16[96,128]{1,0:T(8,128)(2,1)S(1)}, bf16[96,128]{1,0:T(8,128)(2,1)S(1)}, bf16[96,128]{1,0:T(8,128)(2,1)S(1)}) custom-call(bf16[384,128]{1,0:T(8,128)(2,1)S(1)} %get-tuple-element.35.refs_0_, bf16[384,128]{1,0:T(8,128)(2,1)S(1)} %collective-permute-done.8.refs_1_, ...), custom_call_target="tpu_custom_call" | custom-call | flops 1000000000 | bytes 1000000 | tf_op jit(solution)/shard_map/finish/pallas_call | solution.py:473
  33.2 1.4 %collective-permute-start.11 = (bf16[96,128]{1,0:T(8,128)(2,1)S(1)}, bf16[96,128]{1,0:T(8,128)(2,1)S(1)}, u32[]{:S(2)}, u32[]{:S(2)}) collective-permute-start(bf16[96,128]{1,0:T(8,128)(2,1)S(1)} %get-tuple-element.37), channel_id=1, source_target_pairs={{0,28},{1,29},{2,30},{3,31},{4,24},{5,25},{6,26},{7,27},{8,20},{9,... | collective-permute-start | bytes 73736 | tf_op jit(solution)/shard_map/ppermute | solution.py:526
  34.5 2.5 %collective-permute-start.12 = (bf16[96,128]{1,0:T(8,128)(2,1)S(1)}, bf16[96,128]{1,0:T(8,128)(2,1)S(1)}, u32[]{:S(2)}, u32[]{:S(2)}) collective-permute-start(bf16[96,128]{1,0:T(8,128)(2,1)S(1)} %get-tuple-element.38), channel_id=1, source_target_pairs={{0,24},{1,25},{2,26},{3,27},{4,28},{5,29},{6,30},{7,31},{8,16},{9,... | collective-permute-start | bytes 73736 | tf_op jit(solution)/shard_map/ppermute | solution.py:526
  37.0 0.0 collective-permute-start.13
  37.0 0.0 collective-permute-done.15.refs_1_
  37.0 3.9 %collective-permute-start.14 = (bf16[96,128]{1,0:T(8,128)(2,1)S(1)}, bf16[96,128]{1,0:T(8,128)(2,1)S(1)}, u32[]{:S(2)}, u32[]{:S(2)}) collective-permute-start(bf16[96,128]{1,0:T(8,128)(2,1)S(1)} %get-tuple-element.40), channel_id=1, source_target_pairs={{0,16},{1,17},{2,18},{3,19},{4,20},{5,21},{6,22},{7,23},{8,24},{9,... | collective-permute-start | bytes 73736 | tf_op jit(solution)/shard_map/ppermute | solution.py:526
  40.9 0.8 %finish.3 = (bf16[96,128]{1,0:T(8,128)(2,1)S(1)}, bf16[96,128]{1,0:T(8,128)(2,1)S(1)}, bf16[96,128]{1,0:T(8,128)(2,1)S(1)}, bf16[96,128]{1,0:T(8,128)(2,1)S(1)}) custom-call(bf16[384,128]{1,0:T(8,128)(2,1)S(1)} %get-tuple-element.41.refs_0_, bf16[384,128]{1,0:T(8,128)(2,1)S(1)} %collective-permute-done.15.refs_1_, ...), custom_call_target="tpu_custom_call" | custom-call | flops 1000000000 | bytes 1000000 | tf_op jit(solution)/shard_map/finish/pallas_call | solution.py:473
  41.7 0.1 collective-permute-start.18
  41.7 0.0 collective-permute-done.11.refs_0_
  41.7 1.9 %collective-permute-start.19 = (bf16[96,128]{1,0:T(8,128)(2,1)S(1)}, bf16[96,128]{1,0:T(8,128)(2,1)S(1)}, u32[]{:S(2)}, u32[]{:S(2)}) collective-permute-start(bf16[96,128]{1,0:T(8,128)(2,1)S(1)} %get-tuple-element.44), channel_id=1, source_target_pairs={{0,8},{1,9},{2,10},{3,11},{4,12},{5,13},{6,14},{7,15},{8,0},{9,1},... | collective-permute-start | bytes 73736 | tf_op jit(solution)/shard_map/ppermute | solution.py:526
  43.7 1.5 %collective-permute-start.20 = (bf16[96,128]{1,0:T(8,128)(2,1)S(1)}, bf16[96,128]{1,0:T(8,128)(2,1)S(1)}, u32[]{:S(2)}, u32[]{:S(2)}) collective-permute-start(bf16[96,128]{1,0:T(8,128)(2,1)S(1)} %get-tuple-element.45), channel_id=1, source_target_pairs={{0,4},{1,5},{2,6},{3,7},{4,0},{5,1},{6,2},{7,3},{8,12},{9,13},{10,... | collective-permute-start | bytes 73736 | tf_op jit(solution)/shard_map/ppermute | solution.py:526
  45.2 0.0 collective-permute-done.13.refs_2_
  45.2 0.0 collective-permute-done.14.refs_3_
  45.2 1.2 %collective-permute-done.18.refs_4_ = bf16[96,128]{1,0:T(8,128)(2,1)S(1)} collective-permute-done((bf16[96,128]{1,0:T(8,128)(2,1)S(1)}, bf16[96,128]{1,0:T(8,128)(2,1)S(1)}, u32[]{:S(2)}, u32[]{:S(2)}) %collective-permute-start.18) | collective-permute-done | bytes 24608 | tf_op jit(solution)/shard_map/ppermute | solution.py:526
  46.4 1.1 %collective-permute-done.20.refs_6_ = bf16[96,128]{1,0:T(8,128)(2,1)S(1)} collective-permute-done((bf16[96,128]{1,0:T(8,128)(2,1)S(1)}, bf16[96,128]{1,0:T(8,128)(2,1)S(1)}, u32[]{:S(2)}, u32[]{:S(2)}) %collective-permute-start.20) | collective-permute-done | bytes 24608 | tf_op jit(solution)/shard_map/ppermute | solution.py:526
  47.5 0.8 %order.1 = bf16[2,192,256]{2,1,0:T(8,128)(2,1)} custom-call(bf16[96,128]{1,0:T(8,128)(2,1)S(1)} %collective-permute-done.11.refs_0_, bf16[96,128]{1,0:T(8,128)(2,1)S(1)} %collective-permute-done.12.refs_1_, bf16[96,128]{1,0:T(8,128)(2,1)S(1)} %collective-permute-done.13.refs_2_, bf16[96,128]{1,0:T(8,128)(2,1)S(1)} %collective-permute-done.14.refs_3_, ...), custom_call_target="tpu_custom_call" | custom-call | tf_op jit(solution)/shard_map/order/pallas_call | solution.py:506
  (10 shorter events, 0.0 us)
Async XLA Ops:
  0.0 18.4 %collective-permute-start.5 = (bf16[192,768]{1,0:T(8,128)(2,1)}, bf16[192,768]{1,0:T(8,128)(2,1)S(1)}, u32[]{:S(2)}, u32[]{:S(2)}) collective-permute-start(bf16[192,768]{1,0:T(8,128)(2,1)} %refs_0_.1), channel_id=1, source_target_pairs={{0,2},{1,3},{2,0},{3,1},{4,6},{5,7},{6,4},{7,5},{8,10},{9,11},{10,... | collective-permute-start | bytes 884744 | tf_op jit(solution)/shard_map/ppermute | solution.py:526
  3.8 14.7 %copy-start.2 = (bf16[192,768]{1,0:T(8,128)(2,1)S(1)}, bf16[192,768]{1,0:T(8,128)(2,1)}, u32[]{:S(2)}) copy-start(bf16[192,768]{1,0:T(8,128)(2,1)} %refs_0_.1) | copy-start | bytes 884740
  3.8 4.1 %collective-permute-start.1 = (s32[2,256]{1,0:T(2,128)S(1)}, s32[2,256]{1,0:T(2,128)S(1)}, u32[]{:S(2)}, u32[]{:S(2)}) collective-permute-start(s32[2,256]{1,0:T(2,128)S(1)} %codes.1), channel_id=1, source_target_pairs={{0,4},{1,13},{2,22},{3,31},{4,0},{5,9},{6,18},{7,27},{8,12},{9,5},... | collective-permute-start | bytes 6152 | tf_op jit(solution)/shard_map/ppermute | solution.py:526
  5.4 2.5 %collective-permute-start = (s32[2,256]{1,0:T(2,128)S(1)}, s32[2,256]{1,0:T(2,128)S(1)}, u32[]{:S(2)}, u32[]{:S(2)}) collective-permute-start(s32[2,256]{1,0:T(2,128)S(1)} %codes.1), channel_id=1, source_target_pairs={{0,0},{1,9},{2,18},{3,27},{4,4},{5,13},{6,22},{7,31},{8,8},{9,1},{... | collective-permute-start | bytes 6152 | tf_op jit(solution)/shard_map/ppermute | solution.py:526
  7.9 14.0 %copy-start = (bf16[33,768]{1,0:T(8,128)(2,1)S(1)}, bf16[33,768]{1,0:T(8,128)(2,1)}, u32[]{:S(2)}) copy-start(bf16[33,768]{1,0:T(8,128)(2,1)} %refs_7_.1) | copy-start | bytes 152068
  7.9 14.0 %copy-start.1 = (bf16[3,192,768]{2,1,0:T(8,128)(2,1)S(1)}, bf16[3,192,768]{2,1,0:T(8,128)(2,1)}, u32[]{:S(2)}) copy-start(bf16[3,192,768]{2,1,0:T(8,128)(2,1)} %param.12) | copy-start | bytes 2654212
  7.9 8.5 %collective-permute-start.4 = (bf16[48,576]{1,0:T(8,128)(2,1)S(1)}, bf16[48,576]{1,0:T(8,128)(2,1)S(1)}, u32[]{:S(2)}, u32[]{:S(2)}) collective-permute-start(bf16[48,576]{1,0:T(8,128)(2,1)S(1)} %pack.1.refs_0_), channel_id=1, source_target_pairs={{0,3},{1,2},{2,1},{3,0},{4,7},{5,6},{6,5},{7,4},{8,11},{9,10},{10,... | collective-permute-start | bytes 165896 | tf_op jit(solution)/shard_map/ppermute | solution.py:526
  14.0 4.4 %collective-permute-start.3 = (bf16[48,576]{1,0:T(8,128)(2,1)S(1)}, bf16[48,576]{1,0:T(8,128)(2,1)S(1)}, u32[]{:S(2)}, u32[]{:S(2)}) collective-permute-start(bf16[48,576]{1,0:T(8,128)(2,1)S(1)} %pack.1.refs_0_), channel_id=1, source_target_pairs={{0,2},{1,3},{2,0},{3,1},{4,6},{5,7},{6,4},{7,5},{8,10},{9,11},{10,... | collective-permute-start | bytes 165896 | tf_op jit(solution)/shard_map/ppermute | solution.py:526
  14.5 3.9 %collective-permute-start.2 = (bf16[48,576]{1,0:T(8,128)(2,1)S(1)}, bf16[48,576]{1,0:T(8,128)(2,1)S(1)}, u32[]{:S(2)}, u32[]{:S(2)}) collective-permute-start(bf16[48,576]{1,0:T(8,128)(2,1)S(1)} %pack.1.refs_0_), channel_id=1, source_target_pairs={{0,1},{1,0},{2,3},{3,2},{4,5},{5,4},{6,7},{7,6},{8,9},{9,8},{10,11... | collective-permute-start | bytes 165896 | tf_op jit(solution)/shard_map/ppermute | solution.py:526
  18.4 3.4 %collective-permute-start.6 = (bf16[192,768]{1,0:T(8,128)(2,1)S(1)}, bf16[192,768]{1,0:T(8,128)(2,1)S(1)}, u32[]{:S(2)}, u32[]{:S(2)}) collective-permute-start(bf16[192,768]{1,0:T(8,128)(2,1)S(1)} %copy-done.2), channel_id=1, source_target_pairs={{0,1},{1,0},{2,3},{3,2},{4,5},{5,4},{6,7},{7,6},{8,9},{9,8},{10,11... | collective-permute-start | bytes 884744 | tf_op jit(solution)/shard_map/ppermute | solution.py:526
  18.5 3.4 %collective-permute-start.7 = (bf16[192,768]{1,0:T(8,128)(2,1)S(1)}, bf16[192,768]{1,0:T(8,128)(2,1)S(1)}, u32[]{:S(2)}, u32[]{:S(2)}) collective-permute-start(bf16[192,768]{1,0:T(8,128)(2,1)S(1)} %collective-permute-done.5.refs_2_), channel_id=1, source_target_pairs={{0,1},{1,0},{2,3},{3,2},{4,5},{5,4},{6,7},{7,6},{8,9},{9,8},{10,11... | collective-permute-start | bytes 884744 | tf_op jit(solution)/shard_map/ppermute | solution.py:526
  21.9 10.5 %copy-start.3 = (bf16[192,768]{1,0:T(8,128)(2,1)S(1)}, bf16[192,768]{1,0:T(8,128)(2,1)}, u32[]{:S(2)}) copy-start(bf16[192,768]{1,0:T(8,128)(2,1)} %refs_5_.3) | copy-start | bytes 884740
  25.2 5.7 %collective-permute-start.9 = (bf16[384,128]{1,0:T(8,128)(2,1)S(1)}, bf16[384,128]{1,0:T(8,128)(2,1)S(1)}, u32[]{:S(2)}, u32[]{:S(2)}) collective-permute-start(bf16[384,128]{1,0:T(8,128)(2,1)S(1)} %get-tuple-element.35.refs_0_), channel_id=1, source_target_pairs={{0,2},{1,3},{2,0},{3,1},{4,6},{5,7},{6,4},{7,5},{8,10},{9,11},{10,... | collective-permute-start | bytes 294920 | tf_op jit(solution)/shard_map/ppermute | solution.py:526
  26.9 5.5 %collective-permute-start.16 = (bf16[384,128]{1,0:T(8,128)(2,1)S(1)}, bf16[384,128]{1,0:T(8,128)(2,1)S(1)}, u32[]{:S(2)}, u32[]{:S(2)}) collective-permute-start(bf16[384,128]{1,0:T(8,128)(2,1)S(1)} %get-tuple-element.41.refs_0_), channel_id=1, source_target_pairs={{0,2},{1,3},{2,0},{3,1},{4,6},{5,7},{6,4},{7,5},{8,10},{9,11},{10,... | collective-permute-start | bytes 294920 | tf_op jit(solution)/shard_map/ppermute | solution.py:526
  27.3 5.0 %collective-permute-start.8 = (bf16[384,128]{1,0:T(8,128)(2,1)S(1)}, bf16[384,128]{1,0:T(8,128)(2,1)S(1)}, u32[]{:S(2)}, u32[]{:S(2)}) collective-permute-start(bf16[384,128]{1,0:T(8,128)(2,1)S(1)} %get-tuple-element.35.refs_0_), channel_id=1, source_target_pairs={{0,1},{1,0},{2,3},{3,2},{4,5},{5,4},{6,7},{7,6},{8,9},{9,8},{10,11... | collective-permute-start | bytes 294920 | tf_op jit(solution)/shard_map/ppermute | solution.py:526
  30.9 1.5 %collective-permute-start.10 = (bf16[384,128]{1,0:T(8,128)(2,1)S(1)}, bf16[384,128]{1,0:T(8,128)(2,1)S(1)}, u32[]{:S(2)}, u32[]{:S(2)}) collective-permute-start(bf16[384,128]{1,0:T(8,128)(2,1)S(1)} %collective-permute-done.9.refs_2_), channel_id=1, source_target_pairs={{0,1},{1,0},{2,3},{3,2},{4,5},{5,4},{6,7},{7,6},{8,9},{9,8},{10,11... | collective-permute-start | bytes 294920 | tf_op jit(solution)/shard_map/ppermute | solution.py:526
  30.9 6.1 %collective-permute-start.15 = (bf16[384,128]{1,0:T(8,128)(2,1)S(1)}, bf16[384,128]{1,0:T(8,128)(2,1)S(1)}, u32[]{:S(2)}, u32[]{:S(2)}) collective-permute-start(bf16[384,128]{1,0:T(8,128)(2,1)S(1)} %get-tuple-element.41.refs_0_), channel_id=1, source_target_pairs={{0,1},{1,0},{2,3},{3,2},{4,5},{5,4},{6,7},{7,6},{8,9},{9,8},{10,11... | collective-permute-start | bytes 294920 | tf_op jit(solution)/shard_map/ppermute | solution.py:526
  32.4 8.5 %collective-permute-start.17 = (bf16[384,128]{1,0:T(8,128)(2,1)S(1)}, bf16[384,128]{1,0:T(8,128)(2,1)S(1)}, u32[]{:S(2)}, u32[]{:S(2)}) collective-permute-start(bf16[384,128]{1,0:T(8,128)(2,1)S(1)} %collective-permute-done.16.refs_2_), channel_id=1, source_target_pairs={{0,1},{1,0},{2,3},{3,2},{4,5},{5,4},{6,7},{7,6},{8,9},{9,8},{10,11... | collective-permute-start | bytes 294920 | tf_op jit(solution)/shard_map/ppermute | solution.py:526
  33.2 8.6 %collective-permute-start.11 = (bf16[96,128]{1,0:T(8,128)(2,1)S(1)}, bf16[96,128]{1,0:T(8,128)(2,1)S(1)}, u32[]{:S(2)}, u32[]{:S(2)}) collective-permute-start(bf16[96,128]{1,0:T(8,128)(2,1)S(1)} %get-tuple-element.37), channel_id=1, source_target_pairs={{0,28},{1,29},{2,30},{3,31},{4,24},{5,25},{6,26},{7,27},{8,20},{9,... | collective-permute-start | bytes 73736 | tf_op jit(solution)/shard_map/ppermute | solution.py:526
  34.5 9.2 %collective-permute-start.12 = (bf16[96,128]{1,0:T(8,128)(2,1)S(1)}, bf16[96,128]{1,0:T(8,128)(2,1)S(1)}, u32[]{:S(2)}, u32[]{:S(2)}) collective-permute-start(bf16[96,128]{1,0:T(8,128)(2,1)S(1)} %get-tuple-element.38), channel_id=1, source_target_pairs={{0,24},{1,25},{2,26},{3,27},{4,28},{5,29},{6,30},{7,31},{8,16},{9,... | collective-permute-start | bytes 73736 | tf_op jit(solution)/shard_map/ppermute | solution.py:526
  37.0 8.2 %collective-permute-start.13 = (bf16[96,128]{1,0:T(8,128)(2,1)S(1)}, bf16[96,128]{1,0:T(8,128)(2,1)S(1)}, u32[]{:S(2)}, u32[]{:S(2)}) collective-permute-start(bf16[96,128]{1,0:T(8,128)(2,1)S(1)} %get-tuple-element.39), channel_id=1, source_target_pairs={{0,20},{1,21},{2,22},{3,23},{4,16},{5,17},{6,18},{7,19},{8,28},{9,... | collective-permute-start | bytes 73736 | tf_op jit(solution)/shard_map/ppermute | solution.py:526
  37.0 8.2 %collective-permute-start.14 = (bf16[96,128]{1,0:T(8,128)(2,1)S(1)}, bf16[96,128]{1,0:T(8,128)(2,1)S(1)}, u32[]{:S(2)}, u32[]{:S(2)}) collective-permute-start(bf16[96,128]{1,0:T(8,128)(2,1)S(1)} %get-tuple-element.40), channel_id=1, source_target_pairs={{0,16},{1,17},{2,18},{3,19},{4,20},{5,21},{6,22},{7,23},{8,24},{9,... | collective-permute-start | bytes 73736 | tf_op jit(solution)/shard_map/ppermute | solution.py:526
  41.7 4.8 %collective-permute-start.18 = (bf16[96,128]{1,0:T(8,128)(2,1)S(1)}, bf16[96,128]{1,0:T(8,128)(2,1)S(1)}, u32[]{:S(2)}, u32[]{:S(2)}) collective-permute-start(bf16[96,128]{1,0:T(8,128)(2,1)S(1)} %get-tuple-element.43), channel_id=1, source_target_pairs={{0,12},{1,13},{2,14},{3,15},{4,8},{5,9},{6,10},{7,11},{8,4},{9,5},... | collective-permute-start | bytes 73736 | tf_op jit(solution)/shard_map/ppermute | solution.py:526
  41.7 4.7 %collective-permute-start.19 = (bf16[96,128]{1,0:T(8,128)(2,1)S(1)}, bf16[96,128]{1,0:T(8,128)(2,1)S(1)}, u32[]{:S(2)}, u32[]{:S(2)}) collective-permute-start(bf16[96,128]{1,0:T(8,128)(2,1)S(1)} %get-tuple-element.44), channel_id=1, source_target_pairs={{0,8},{1,9},{2,10},{3,11},{4,12},{5,13},{6,14},{7,15},{8,0},{9,1},... | collective-permute-start | bytes 73736 | tf_op jit(solution)/shard_map/ppermute | solution.py:526
  43.7 3.8 %collective-permute-start.20 = (bf16[96,128]{1,0:T(8,128)(2,1)S(1)}, bf16[96,128]{1,0:T(8,128)(2,1)S(1)}, u32[]{:S(2)}, u32[]{:S(2)}) collective-permute-start(bf16[96,128]{1,0:T(8,128)(2,1)S(1)} %get-tuple-element.45), channel_id=1, source_target_pairs={{0,4},{1,5},{2,6},{3,7},{4,0},{5,1},{6,2},{7,3},{8,12},{9,13},{10,... | collective-permute-start | bytes 73736 | tf_op jit(solution)/shard_map/ppermute | solution.py:526

commit v9 on v6

--- a/solution.py
+++ b/solution.py
@@ -11,8 +11,7 @@
 EPS = 1e-05
 LANES = 128
 CODES = 64
-VOCAB_ROWS = 40
-TABLE_ROWS = 48
+TABLE_ROWS = 40
 
 SMALL_VMEM = 8 * 1024 * 1024
 LARGE_VMEM = 32 * 1024 * 1024
@@ -50,67 +49,66 @@
     return lax.broadcasted_iota(jnp.int32, shape, axis)
 
 
-def code_kernel(ids_hbm, live_hbm, out_ref, ids_ref, live_ref, sems):
+def table_kernel(
+    ids_hbm,
+    live_hbm,
+    embed_hbm,
+    qkv_hbm,
+    out_ref,
+    coded_ref,
+    ids_ref,
+    live_ref,
+    embed_ref,
+    qkv_ref,
+    padded_ref,
+    sems,
+):
+    kinds = qkv_ref.shape[0]
     loads = [
-        pltpu.make_async_copy(ids_hbm, ids_ref, sems.at[0]),
-        pltpu.make_async_copy(live_hbm, live_ref, sems.at[1]),
+        pltpu.make_async_copy(embed_hbm, embed_ref, sems.at[kinds]),
+        pltpu.make_async_copy(ids_hbm, ids_ref, sems.at[kinds + 1]),
+        pltpu.make_async_copy(live_hbm, live_ref, sems.at[kinds + 2]),
     ]
-    for load in loads:
-        load.start()
-    for load in loads:
-        load.wait()
-    row = iota(ids_ref.shape, 0)
-    live = jnp.zeros(ids_ref.shape, jnp.int32)
-    for r in range(ids_ref.shape[0]):
-        live = jnp.where(row == r, live_ref[r], live)
-    out_ref[...] = ids_ref[...] + 65536 * live
-
-
-def make_codes(ids, pad_mask):
-    return pl.pallas_call(
-        code_kernel,
-        out_shape=jax.ShapeDtypeStruct(ids.shape, jnp.int32),
-        in_specs=[pl.BlockSpec(memory_space=pltpu.HBM)] * 2,
-        scratch_shapes=[
-            pltpu.VMEM(ids.shape, jnp.int32),
-            pltpu.SMEM(pad_mask.shape, jnp.int32),
-            pltpu.SemaphoreType.DMA((2,)),
-        ],
-        compiler_params=pltpu.CompilerParams(vmem_limit_bytes=SMALL_VMEM),
-        name="codes",
-    )(in_hbm(ids), in_hbm(pad_mask))
-
-
-def table_kernel(embed_hbm, qkv_hbm, out_ref, embed_ref, qkv_ref, padded_ref, sems):
-    kinds, local = qkv_ref.shape[0:2]
-    loads = [pltpu.make_async_copy(embed_hbm, embed_ref, sems.at[kinds])]
     loads += [
         pltpu.make_async_copy(qkv_hbm.at[t], qkv_ref.at[t], sems.at[t]) for t in range(kinds)
     ]
     for load in loads:
         load.start()
     padded_ref[...] = jnp.zeros(padded_ref.shape, f32)
-    loads[0].wait()
+    for load in loads[0:3]:
+        load.wait()
     padded_ref[0 : embed_ref.shape[0], :] = embed_ref[...].astype(f32)
     normed = layer_norm(padded_ref[...]).astype(bf16)
+    row = iota(ids_ref.shape, 0)
+    live = jnp.zeros(ids_ref.shape, jnp.int32)
+    for r in range(ids_ref.shape[0]):
+        live = jnp.where(row == r, live_ref[r], live)
+    coded = ids_ref[...] + 65536 * live
+    for g in range(coded_ref.shape[0]):
+        coded_ref[g] = coded
     tables = []
     for t in range(kinds):
-        loads[1 + t].wait()
+        loads[3 + t].wait()
         tables.append(dot_nt(normed, qkv_ref[t]))
     out_ref[...] = jnp.concatenate(tables, 1).astype(bf16)
 
 
-def make_tables(embed, row_qkv):
+def make_tables(ids, pad_mask, embed, row_qkv, groups):
     kinds, local, width = row_qkv.shape
     return pl.pallas_call(
         table_kernel,
-        out_shape=jax.ShapeDtypeStruct((TABLE_ROWS, kinds * local), bf16),
-        in_specs=[pl.BlockSpec(memory_space=pltpu.HBM)] * 2,
+        out_shape=(
+            jax.ShapeDtypeStruct((TABLE_ROWS, kinds * local), bf16),
+            jax.ShapeDtypeStruct((groups,) + ids.shape, jnp.int32),
+        ),
+        in_specs=[pl.BlockSpec(memory_space=pltpu.HBM)] * 4,
         scratch_shapes=[
+            pltpu.VMEM(ids.shape, jnp.int32),
+            pltpu.SMEM(pad_mask.shape, jnp.int32),
             pltpu.VMEM(embed.shape, bf16),
             pltpu.VMEM(row_qkv.shape, bf16),
             pltpu.VMEM((TABLE_ROWS, width), f32),
-            pltpu.SemaphoreType.DMA((kinds + 1,)),
+            pltpu.SemaphoreType.DMA((kinds + 3,)),
         ],
         cost_estimate=pl.CostEstimate(
             flops=2 * TABLE_ROWS * row_qkv.size,
@@ -119,32 +117,7 @@
         ),
         compiler_params=pltpu.CompilerParams(vmem_limit_bytes=SMALL_VMEM),
         name="tables",
-    )(in_hbm(embed), in_hbm(row_qkv))
-
-
-def pack_kernel(table_ref, *refs):
-    codes_refs, out_ref = refs[:-1], refs[-1]
-    coded = jnp.concatenate([ref[...] for ref in codes_refs], 0)
-    some, cols = coded.shape
-    ids = (coded & 0xFFFF).astype(f32)
-    live = (coded >> 16).astype(f32)
-    spare = jnp.concatenate(
-        [ids, live[:, 0:LANES], jnp.zeros((some, out_ref.shape[1] - cols - LANES), f32)], 1
-    )
-    if some < TABLE_ROWS - VOCAB_ROWS:
-        empty = jnp.zeros((TABLE_ROWS - VOCAB_ROWS - some, spare.shape[1]), f32)
-        spare = jnp.concatenate([spare, empty], 0)
-    table = table_ref[...].astype(f32)[0:VOCAB_ROWS]
-    out_ref[...] = jnp.concatenate([table, spare], 0).astype(bf16)
-
-
-def pack(table, codes):
-    return pl.pallas_call(
-        pack_kernel,
-        out_shape=jax.ShapeDtypeStruct(table.shape, bf16),
-        compiler_params=pltpu.CompilerParams(vmem_limit_bytes=SMALL_VMEM),
-        name="pack",
-    )(table, *codes)
+    )(in_hbm(ids), in_hbm(pad_mask), in_hbm(embed), in_hbm(row_qkv))
 
 
 def halves(pair):
@@ -174,25 +147,14 @@
     )
 
 
-def read_sequences(payload_ref, rows, first, last):
-    parts = payload_ref.shape[0]
-    each = rows // parts
-    return jnp.concatenate(
-        [
-            payload_ref[p, VOCAB_ROWS:TABLE_ROWS, first:last].astype(f32)[0:each]
-            for p in range(parts)
-        ],
-        0,
-    )
-
-
 def row_kernel(parts, *refs):
-    payload_refs, refs = refs[:parts], refs[parts:]
+    tables_refs, refs = refs[:parts], refs[parts:]
     (
+        codes_ref,
         row_context_ref,
         own_ref,
         live_ref,
-        payload_ref,
+        tables_ref,
         table_ref,
         hot_ref,
         live_own_ref,
@@ -203,23 +165,23 @@
     rows = depth // CODES
     pairs = rows // 2
     own = live_own_ref.shape[0] // pairs
-    half = own // 2
-    width = row_context_ref.shape[2]
+    width = row_context_ref.shape[1]
     heads = width // HEAD_DIM
     local = width // parts
     group = lax.axis_index("seq")
     part = lax.axis_index("head")
     for p in range(parts):
-        payload_ref[part ^ p] = payload_refs[p][...]
+        tables_ref[part ^ p] = tables_refs[p][...]
 
     for t in range(3):
-        table_ref[t, 0:VOCAB_ROWS, :] = jnp.concatenate(
-            [payload_ref[p, 0:VOCAB_ROWS, t * local : (t + 1) * local] for p in range(parts)], 1
+        table_ref[t, 0:TABLE_ROWS, :] = jnp.concatenate(
+            [tables_ref[p, :, t * local : (t + 1) * local] for p in range(parts)], 1
         )
-        table_ref[t, VOCAB_ROWS:CODES, :] = jnp.zeros((CODES - VOCAB_ROWS, width), bf16)
-
-    ids = read_sequences(payload_ref, rows, 0, cols)
-    live = read_sequences(payload_ref, rows, cols, cols + LANES)
+        table_ref[t, TABLE_ROWS:CODES, :] = jnp.zeros((CODES - TABLE_ROWS, width), bf16)
+
+    coded = jnp.concatenate([codes_ref[g] for g in range(codes_ref.shape[0])], 0)
+    ids = (coded & 0xFFFF).astype(f32)
+    live = (coded[:, 0:LANES] >> 16).astype(f32)
     live_ref[...] = live
     code = iota((CODES, cols), 0).astype(f32)
     for r in range(rows):
@@ -235,8 +197,7 @@
         value = jnp.where(first_half, mine[:, 2 * k : 2 * k + 1], mine[:, 2 * k + 1 : 2 * k + 2])
         hot = (value == lane_code).astype(f32)
         alive = jnp.where(first_half, live[2 * k : 2 * k + 1, :], live[2 * k + 1 : 2 * k + 2, :])
-        for c in range(2):
-            own_ref[c, k * half : (k + 1) * half, :] = hot[c * half : (c + 1) * half].astype(bf16)
+        own_ref[k * own : (k + 1) * own, :] = hot.astype(bf16)
         live_own_ref[k * own : (k + 1) * own, :] = (hot * alive).astype(bf16)
 
     spans = [slice(hp * LANES, (hp + 1) * LANES) for hp in range(heads // 2)]
@@ -286,26 +247,24 @@
     for hp in range(heads // 2):
         for k in range(pairs):
             for r2 in range(2):
-                at = (2 * k + r2) * half
-                for c in range(2):
-                    row_context_ref[c, at : at + half, spans[hp]] = contexts[hp][
-                        k * own + c * half : k * own + (c + 1) * half,
-                        r2 * LANES : (r2 + 1) * LANES,
-                    ]
-
-
-def attend_rows(payloads, rows, cols, own, width):
+                at = (2 * k + r2) * own
+                row_context_ref[at : at + own, spans[hp]] = contexts[hp][
+                    k * own : (k + 1) * own, r2 * LANES : (r2 + 1) * LANES
+                ]
+
+
+def attend_rows(tables, codes, rows, cols, own, width):
     heads = width // HEAD_DIM
-    parts = len(payloads)
+    parts = len(tables)
     return pl.pallas_call(
         functools.partial(row_kernel, parts),
         out_shape=(
-            jax.ShapeDtypeStruct((2, rows * own // 2, width), bf16),
-            jax.ShapeDtypeStruct((2, rows * own // 4, LANES), bf16),
+            jax.ShapeDtypeStruct((rows * own, width), bf16),
+            jax.ShapeDtypeStruct((rows * own // 2, LANES), bf16),
             jax.ShapeDtypeStruct((rows, LANES), f32),
         ),
         scratch_shapes=[
-            pltpu.VMEM((parts,) + payloads[0].shape, bf16),
+            pltpu.VMEM((parts,) + tables[0].shape, bf16),
             pltpu.VMEM((3, CODES, width), bf16),
             pltpu.VMEM((rows * CODES, cols), bf16),
             pltpu.VMEM((rows // 2 * own, LANES), bf16),
@@ -315,10 +274,10 @@
         cost_estimate=pl.CostEstimate(flops=3 * 10**9, bytes_accessed=10**6, transcendentals=0),
         compiler_params=pltpu.CompilerParams(vmem_limit_bytes=LARGE_VMEM),
         name="row_attention",
-    )(*payloads)
-
-
-def column_kernel(parts, c, *refs):
+    )(*tables, codes)
+
+
+def column_kernel(parts, *refs):
     row_out_refs, refs = refs[:parts], refs[parts:]
     (
         live_ref,
@@ -326,13 +285,13 @@
         own_ref,
         embed_ref,
         col_qkv_ref,
-        context_ref,
-        mixed_out_ref,
+        *out_refs,
         row_out_ref,
         embed2_ref,
     ) = refs
+    context_refs, mixed_refs = out_refs[:2], out_refs[2:]
     rows = live_ref.shape[0]
-    tokens, width = row_context_ref.shape[1:]
+    tokens, width = row_context_ref.shape
     pairs = rows // 2
     own = tokens // rows
     vocab = embed_ref.shape[0]
@@ -345,7 +304,7 @@
     embed2_ref[0:vocab, 0:width] = embed_ref[...]
     embed2_ref[CODES : CODES + vocab, width : 2 * width] = embed_ref[...]
 
-    embedded2 = dot_nn(own_ref[c], embed2_ref[...])
+    embedded2 = dot_nn(own_ref[...], embed2_ref[...])
     embedded = jnp.concatenate(
         [
             embedded2[k * own : (k + 1) * own, r2 * width : (r2 + 1) * width]
@@ -354,12 +313,15 @@
         ],
         0,
     )
-    mixed = embedded + dot_nt(row_context_ref[c], row_out_ref[...].reshape(width, width))
+    mixed = embedded + dot_nt(row_context_ref[...], row_out_ref[...].reshape(width, width))
     for p in range(parts):
 
         @pl.when(part == p)
         def _():
-            mixed_out_ref[...] = mixed[:, p * local : (p + 1) * local]
+            for c in range(2):
+                mixed_refs[c][...] = mixed[
+                    c * tokens // 2 : (c + 1) * tokens // 2, p * local : (p + 1) * local
+                ]
 
     normed = layer_norm(mixed).astype(bf16)
 
@@ -410,22 +372,24 @@
     ]
     whole = jnp.concatenate(blocks, 0).reshape(groups, rows, few, local)
     context = jnp.swapaxes(whole, 0, 1).reshape(tokens, local)
-    context_ref[0:tokens, :] = context[:, 0:LANES].astype(bf16)
-    some = tokens // 2
-    context_ref[tokens : tokens + some, :] = jnp.concatenate(
-        [context[0:some, LANES:local], context[some:tokens, LANES:local]], 1
-    ).astype(bf16)
-
-
-def attend_columns_here(c, row_outs, live, row_context, own_codes, embed, col_qkv):
+    half, some = tokens // 2, tokens // 4
+    for c in range(2):
+        part_of = context[c * half : (c + 1) * half]
+        context_refs[c][0:half, :] = part_of[:, 0:LANES].astype(bf16)
+        context_refs[c][half : half + some, :] = jnp.concatenate(
+            [part_of[0:some, LANES:local], part_of[some:half, LANES:local]], 1
+        ).astype(bf16)
+
+
+def attend_columns_here(row_outs, live, row_context, own_codes, embed, col_qkv):
     parts = len(row_outs)
-    tokens, width = row_context.shape[1:]
+    tokens, width = row_context.shape
     local = width // parts
     return pl.pallas_call(
-        functools.partial(column_kernel, parts, c),
+        functools.partial(column_kernel, parts),
         out_shape=(
-            jax.ShapeDtypeStruct((tokens * local // LANES, LANES), bf16),
-            jax.ShapeDtypeStruct((tokens, local), f32),
+            *[jax.ShapeDtypeStruct((tokens // 2 * local // LANES, LANES), bf16)] * 2,
+            *[jax.ShapeDtypeStruct((tokens // 2, local), f32)] * 2,
         ),
         scratch_shapes=[
             pltpu.VMEM((parts, local, width), bf16),
@@ -443,7 +407,6 @@
     col_out_ref, out_ref, weight_ref = refs[2 * parts + 2 :]
     tokens, local = mixed_refs[0].shape
     some = tokens // 2
-    group = lax.axis_index("seq")
     part = lax.axis_index("head")
     for p in range(parts):
         weight_ref[p] = col_out_ref[:, p * local : (p + 1) * local]
@@ -462,16 +425,15 @@
                 + dot_nt(context[0:tokens, :], weight[:, 0:LANES])
                 + jnp.concatenate([dot_nt(last, left), dot_nt(last, right)], 0)
             )
-    own = tokens // groups // 2
+    slots = groups // 2
+    own = tokens // slots // 2
     for d in range(groups):
         first, second = (
-            jnp.concatenate(
-                [total[(2 * d + r) * own : (2 * d + r + 1) * own, :] for total in totals], 0
-            )
+            totals[d // slots][(2 * (d % slots) + r) * own : (2 * (d % slots) + r + 1) * own, :]
             for r in range(2)
         )
         rest = jnp.concatenate([first[:, LANES:local], second[:, LANES:local]], 1)
-        out_ref[group ^ d] = jnp.concatenate(
+        out_ref[d] = jnp.concatenate(
             [first[:, 0:LANES], second[:, 0:LANES], rest], 0
         ).astype(bf16)
 
@@ -522,7 +484,6 @@
     local = row_out.shape[0]
     groups, parts = lax.axis_size("seq"), lax.axis_size("head")
     own, rows = cols // groups, rows_here * groups
-    each = groups // parts
 
     def pairwise(value, partner):
         order = [(g, p) for g in range(groups) for p in range(parts)]
@@ -539,23 +500,22 @@
         return g, p ^ 3
 
     far = pairwise(row_out, across)
-    coded = make_codes(ids, pad_mask)
-    codes = [pairwise(coded, lambda g, p, b=b: (g ^ (p * each + b), p)) for b in range(each)]
-    payload = pack(make_tables(embed, row_qkv), codes)
-    payloads = [payload] + [pairwise(payload, to) for to in (sibling, across, opposite)]
-    *payloads, near, far = lax.optimization_barrier((*payloads, row_out, far))
+    table, codes = make_tables(ids, pad_mask, embed, row_qkv, groups)
+    tables = [table] + [pairwise(table, to) for to in (sibling, across, opposite)]
+    codes = lax.all_to_all(codes, "seq", split_axis=0, concat_axis=0, tiled=True)
+    codes, near, far = lax.optimization_barrier((codes, row_out, far))
     row_outs = [row_out, pairwise(near, sibling), far, pairwise(far, sibling)]
-    row_context, own_codes, live = attend_rows(payloads, rows, cols, own, width)
-    contexts, mixed = [], []
-    for c in range(2):
-        context, residual = attend_columns_here(
-            c, row_outs, live, row_context, own_codes, embed, col_qkv.reshape(3 * local, width)
+    row_context, own_codes, live = attend_rows(tables, codes, rows, cols, own, width)
+    *halves_here, mixed_low, mixed_high = attend_columns_here(
+        row_outs, live, row_context, own_codes, embed, col_qkv.reshape(3 * local, width)
+    )
+    contexts = []
+    for context in halves_here:
+        beyond = pairwise(context, across)
+        contexts.append(
+            (context, pairwise(context, sibling), beyond, pairwise(beyond, sibling))
         )
-        beyond = pairwise(context, across)
-        near = pairwise(context, sibling)
-        contexts.append((context, near, beyond, pairwise(beyond, sibling)))
-        mixed.append(residual)
-    blocks = finish(contexts, mixed, col_out, groups)
+    blocks = finish(contexts, (mixed_low, mixed_high), col_out, groups)
     blocks = lax.all_to_all(blocks, "seq", split_axis=0, concat_axis=0, tiled=True)
     return jnp.swapaxes(order(blocks, cols, local), 1, 2)
 
@@ -645,16 +605,14 @@
     parts = lax.axis_size("head")
     local = row_out.shape[0]
     fits = (
-        groups & (groups - 1) == 0
-        and parts == 4
-        and groups % parts == 0
+        parts == 4
+        and groups % 2 == 0
         and rows * 8 == LANES
         and rows_here == 2
-        and rows <= 8 * parts
         and own % 32 == 0
-        and cols + LANES <= 3 * local
+        and cols >= LANES
         and local == LANES + HEAD_DIM
-        and embed.shape[0] <= VOCAB_ROWS
+        and embed.shape[0] <= TABLE_ROWS
     )
     chosen = fast_body if fits else general_body
     return chosen(ids, pad_mask, embed, row_qkv, row_out, col_qkv, col_out)

time: 47 us -> 47.3 us (level)
  blocking collectives: 11 us -> 23.1 us
  starting transfers between devices: 15 us -> 8.03 us
  waiting for transfers between devices: 8.99 us -> 5.83 us
  Pallas kernels: 11.7 us -> 9.95 us
    all_to_all x0 -> x1, blocking collectives: none -> 12.2 us  [fast_body(): lax.all_to_all(codes, 'seq', split_axis=0, concat_axis=0, tiled=True)]
    ppermute x14 -> x12, starting transfers between devices: 15 us -> 8.03 us  [pairwise(): lax.ppermute(value, ('seq', 'head'), [(i, g * parts + p) for i, (g, p) in...]
    ppermute x14 -> x12, waiting for transfers between devices: 8.99 us -> 5.83 us  [pairwise(): lax.ppermute(value, ('seq', 'head'), [(i, g * parts + p) for i, (g, p) in...]
    pallas_call x5 -> x2, Pallas kernels: 6.94 us -> 5.19 us  [the longest x1 3.33 us: attend_columns_here(): pl.pallas_call(functools.partial(column_kernel, parts), out_shape=(*[jax....]
  transfers between devices with their start and end apart: 14 -> 12, of which waited for: 5 -> 3; matrix products, arithmetic and copies ran while one was open for 0% -> 0% of each run, Pallas kernels for 16% -> 10%
where the time goes in v9:
time: 47.3 us; the launch traced here: 47.1 us
  blocking collectives  23.1 us (49%)
  Pallas kernels  9.95 us (21%)
  starting transfers between devices  8.03 us (17%)
  waiting for transfers between devices  5.83 us (12%)
    all_to_all x1, blocking collectives, fast_body(): lax.all_to_all(codes, 'seq', split_axis=0, concat_axis=0, tiled=True)  12.2 us
    all_to_all x1, blocking collectives, fast_body(): lax.all_to_all(blocks, 'seq', split_axis=0, concat_axis=0, tiled=True)  11 us
    ppermute x12, starting transfers between devices, pairwise(): lax.ppermute(value, ('seq', 'head'), [(i, g * parts + p) for i, (g, p) in...  8.03 us
    ppermute x12, waiting for transfers between devices, pairwise(): lax.ppermute(value, ('seq', 'head'), [(i, g * parts + p) for i, (g, p) in...  5.83 us
    pallas_call x1, Pallas kernels, attend_columns_here(): pl.pallas_call(functools.partial(column_kernel, parts), out_shape=(*[jax....  3.33 us
    pallas_call x1, Pallas kernels, attend_rows(): pl.pallas_call(functools.partial(row_kernel, parts), out_shape=(jax.Shape...  2.85 us
    pallas_call x1, Pallas kernels, make_tables(): pl.pallas_call(table_kernel, out_shape=(jax.ShapeDtypeStruct((TABLE_ROWS,...  1.87 us
    pallas_call x1, Pallas kernels, finish(): pl.pallas_call(functools.partial(finish_kernel, parts, groups), out_shape...  1.09 us
  transfers between devices with their start and end apart: 12, of which 3 were waited for; matrix products, arithmetic and copies ran while one was open for 0% of the time, Pallas kernels for 10%

profile of v9, /device:TPU:0, one launch (start us, length us, event | category | flops | bytes accessed | tf_op | source)
XLA Modules:
  0.0 47.1 jit_solution(11722916831669034025)
XLA Ops:
  0.0 0.0 copy-start.3
  0.0 2.9 %collective-permute-start = (bf16[192,768]{1,0:T(8,128)(2,1)}, bf16[192,768]{1,0:T(8,128)(2,1)S(1)}, u32[]{:S(2)}, u32[]{:S(2)}) collective-permute-start(bf16[192,768]{1,0:T(8,128)(2,1)} %refs_0_.1), channel_id=1, source_target_pairs={{0,2},{1,3},{2,0},{3,1},{4,6},{5,7},{6,4},{7,5},{8,10},{9,11},{10,... | collective-permute-start | bytes 884744 | tf_op jit(solution)/shard_map/ppermute | solution.py:491
  2.9 1.9 %tables.1 = (bf16[40,576]{1,0:T(8,128)(2,1)S(1)}, s32[8,2,256]{2,1,0:T(2,128)S(1)}) custom-call(s32[2,256]{1,0:T(2,128)} %ids_hbm.1, s32[2]{0:T(128)} %live_hbm.1, bf16[33,768]{1,0:T(8,128)(2,1)} %refs_7_.1, bf16[3,192,768]{2,1,0:T(8,128)(2,1)} %qkv_hbm.1), custom_call_target="tpu_custom_call" | custom-call | flops 35389440 | bytes 884736 | tf_op jit(solution)/shard_map/tables/pallas_call | solution.py:98
  4.8 0.1 collective-permute-start.5
  4.9 1.2 %collective-permute-start.4 = (bf16[40,576]{1,0:T(8,128)(2,1)S(1)}, bf16[40,576]{1,0:T(8,128)(2,1)S(1)}, u32[]{:S(2)}, u32[]{:S(2)}) collective-permute-start(bf16[40,576]{1,0:T(8,128)(2,1)S(1)} %get-tuple-element.20.refs_0_), channel_id=1, source_target_pairs={{0,2},{1,3},{2,0},{3,1},{4,6},{5,7},{6,4},{7,5},{8,10},{9,11},{10,... | collective-permute-start | bytes 138248 | tf_op jit(solution)/shard_map/ppermute | solution.py:491
  6.1 0.7 %collective-permute-start.3 = (bf16[40,576]{1,0:T(8,128)(2,1)S(1)}, bf16[40,576]{1,0:T(8,128)(2,1)S(1)}, u32[]{:S(2)}, u32[]{:S(2)}) collective-permute-start(bf16[40,576]{1,0:T(8,128)(2,1)S(1)} %get-tuple-element.20.refs_0_), channel_id=1, source_target_pairs={{0,1},{1,0},{2,3},{3,2},{4,5},{5,4},{6,7},{7,6},{8,9},{9,8},{10,11... | collective-permute-start | bytes 138248 | tf_op jit(solution)/shard_map/ppermute | solution.py:491
  6.7 12.2 %all_to_all.10.refs_4_ = s32[8,2,256]{2,1,0:T(2,128)S(1)} all-to-all(s32[8,2,256]{2,1,0:T(2,128)S(1)} %get-tuple-element.17), channel_id=1, replica_groups=mesh['seq'=8,'head'=4] {'seq'}, dimensions={0} | all-to-all | bytes 32768 | tf_op jit(solution)/shard_map/all_to_all | solution.py:505
  18.9 0.0 copy-start.1
  18.9 0.0 copy-start.2
  18.9 0.0 collective-permute-done.refs_2_
  18.9 0.0 copy-done.3
  19.0 0.1 collective-permute-start.1
  19.0 0.5 %collective-permute-start.2 = (bf16[192,768]{1,0:T(8,128)(2,1)S(1)}, bf16[192,768]{1,0:T(8,128)(2,1)S(1)}, u32[]{:S(2)}, u32[]{:S(2)}) collective-permute-start(bf16[192,768]{1,0:T(8,128)(2,1)S(1)} %collective-permute-done.refs_2_), channel_id=1, source_target_pairs={{0,1},{1,0},{2,3},{3,2},{4,5},{5,4},{6,7},{7,6},{8,9},{9,8},{10,11... | collective-permute-start | bytes 884744 | tf_op jit(solution)/shard_map/ppermute | solution.py:491
  19.5 0.0 collective-permute-done.5.refs_3_
  19.5 0.0 collective-permute-done.4.refs_2_
  19.5 0.0 collective-permute-done.3.refs_1_
  19.5 2.9 %row_attention.1 = (bf16[512,768]{1,0:T(8,128)(2,1)S(1)}, bf16[256,128]{1,0:T(8,128)(2,1)S(1)}, f32[16,128]{1,0:T(8,128)S(1)}) custom-call(bf16[40,576]{1,0:T(8,128)(2,1)S(1)} %get-tuple-element.20.refs_0_, bf16[40,576]{1,0:T(8,128)(2,1)S(1)} %collective-permute-done.3.refs_1_, bf16[40,576]{1,0:T(8,128)(2,1)S(1)} %collective-permute-done.4.refs_2_, ...), custom_call_target="tpu_custom_call" | custom-call | flops 3000000000 | bytes 1000000 | tf_op jit(solution)/shard_map/row_attention/pallas_call | solution.py:259
  22.4 0.0 collective-permute-done.1.refs_1_
  22.4 0.0 collective-permute-done.2.refs_3_
  22.4 0.0 copy-done.1
  22.4 0.0 copy-done.2
  22.4 0.0 copy-start
  22.5 3.3 %column_attention.1 = (bf16[384,128]{1,0:T(8,128)(2,1)S(1)}, bf16[384,128]{1,0:T(8,128)(2,1)S(1)}, f32[256,192]{1,0:T(8,128)S(1)}, f32[256,192]{1,0:T(8,128)S(1)}) custom-call(bf16[192,768]{1,0:T(8,128)(2,1)S(1)} %copy-done.3, bf16[192,768]{1,0:T(8,128)(2,1)S(1)} %collective-permute-done.1.refs_1_, bf16[192,768]{1,0:T(8,128)(2,1)S(1)} %collective-permute-done.refs_2_, ...), custom_call_target="tpu_custom_call" | custom-call | flops 2000000000 | bytes 1000000 | tf_op jit(solution)/shard_map/column_attention/pallas_call | solution.py:388
  25.8 0.6 %collective-permute-start.7 = (bf16[384,128]{1,0:T(8,128)(2,1)S(1)}, bf16[384,128]{1,0:T(8,128)(2,1)S(1)}, u32[]{:S(2)}, u32[]{:S(2)}) collective-permute-start(bf16[384,128]{1,0:T(8,128)(2,1)S(1)} %get-tuple-element.25.refs_0_), channel_id=1, source_target_pairs={{0,2},{1,3},{2,0},{3,1},{4,6},{5,7},{6,4},{7,5},{8,10},{9,11},{10,... | collective-permute-start | bytes 294920 | tf_op jit(solution)/shard_map/ppermute | solution.py:491
  26.4 1.5 %collective-permute-start.10 = (bf16[384,128]{1,0:T(8,128)(2,1)S(1)}, bf16[384,128]{1,0:T(8,128)(2,1)S(1)}, u32[]{:S(2)}, u32[]{:S(2)}) collective-permute-start(bf16[384,128]{1,0:T(8,128)(2,1)S(1)} %get-tuple-element.26.refs_4_), channel_id=1, source_target_pairs={{0,2},{1,3},{2,0},{3,1},{4,6},{5,7},{6,4},{7,5},{8,10},{9,11},{10,... | collective-permute-start | bytes 294920 | tf_op jit(solution)/shard_map/ppermute | solution.py:491
  27.9 0.0 collective-permute-start.6
  27.9 0.5 %collective-permute-start.9 = (bf16[384,128]{1,0:T(8,128)(2,1)S(1)}, bf16[384,128]{1,0:T(8,128)(2,1)S(1)}, u32[]{:S(2)}, u32[]{:S(2)}) collective-permute-start(bf16[384,128]{1,0:T(8,128)(2,1)S(1)} %get-tuple-element.26.refs_4_), channel_id=1, source_target_pairs={{0,1},{1,0},{2,3},{3,2},{4,5},{5,4},{6,7},{7,6},{8,9},{9,8},{10,11... | collective-permute-start | bytes 294920 | tf_op jit(solution)/shard_map/ppermute | solution.py:491
  28.4 3.1 %collective-permute-done.7.refs_2_ = bf16[384,128]{1,0:T(8,128)(2,1)S(1)} collective-permute-done((bf16[384,128]{1,0:T(8,128)(2,1)S(1)}, bf16[384,128]{1,0:T(8,128)(2,1)S(1)}, u32[]{:S(2)}, u32[]{:S(2)}) %collective-permute-start.7) | collective-permute-done | bytes 98336 | tf_op jit(solution)/shard_map/ppermute | solution.py:491
  31.5 0.0 collective-permute-start.8
  31.5 1.4 %collective-permute-done.10.refs_6_ = bf16[384,128]{1,0:T(8,128)(2,1)S(1)} collective-permute-done((bf16[384,128]{1,0:T(8,128)(2,1)S(1)}, bf16[384,128]{1,0:T(8,128)(2,1)S(1)}, u32[]{:S(2)}, u32[]{:S(2)}) %collective-permute-start.10) | collective-permute-done | bytes 98336 | tf_op jit(solution)/shard_map/ppermute | solution.py:491
  32.9 0.0 collective-permute-start.11
  32.9 0.0 collective-permute-done.6.refs_1_
  32.9 0.0 collective-permute-done.9.refs_5_
  32.9 0.0 collective-permute-done.8.refs_3_
  32.9 1.3 %collective-permute-done.11.refs_7_ = bf16[384,128]{1,0:T(8,128)(2,1)S(1)} collective-permute-done((bf16[384,128]{1,0:T(8,128)(2,1)S(1)}, bf16[384,128]{1,0:T(8,128)(2,1)S(1)}, u32[]{:S(2)}, u32[]{:S(2)}) %collective-permute-start.11) | collective-permute-done | bytes 98336 | tf_op jit(solution)/shard_map/ppermute | solution.py:491
  34.2 0.0 copy-done
  34.2 1.1 %finish.1 = bf16[8,96,128]{2,1,0:T(8,128)(2,1)S(1)} custom-call(bf16[384,128]{1,0:T(8,128)(2,1)S(1)} %get-tuple-element.25.refs_0_, bf16[384,128]{1,0:T(8,128)(2,1)S(1)} %collective-permute-done.6.refs_1_, bf16[384,128]{1,0:T(8,128)(2,1)S(1)} %collective-permute-done.7.refs_2_, bf16[384,128]{1,0:T(8,128)(2,1)S(1)} %collective-permute-done.8.refs_3_, ...), custom_call_target="tpu_custom_call" | custom-call | tf_op jit(solution)/shard_map/finish/pallas_call | solution.py:444
  35.3 11.0 %all_to_all.11.blocks_ref = bf16[8,96,128]{2,1,0:T(8,128)(2,1)S(1)} all-to-all(bf16[8,96,128]{2,1,0:T(8,128)(2,1)S(1)} %finish.1), channel_id=1, replica_groups=mesh['seq'=8,'head'=4] {'seq'}, dimensions={0} | all-to-all | bytes 393216 | tf_op jit(solution)/shard_map/all_to_all | solution.py:519
  46.3 0.8 %order.1 = bf16[2,192,256]{2,1,0:T(8,128)(2,1)} custom-call(bf16[8,96,128]{2,1,0:T(8,128)(2,1)S(1)} %all_to_all.11.blocks_ref), custom_call_target="tpu_custom_call" | custom-call | tf_op jit(solution)/shard_map/order/pallas_call | solution.py:473
Async XLA Ops:
  0.0 18.9 %copy-start.3 = (bf16[192,768]{1,0:T(8,128)(2,1)S(1)}, bf16[192,768]{1,0:T(8,128)(2,1)}, u32[]{:S(2)}) copy-start(bf16[192,768]{1,0:T(8,128)(2,1)} %refs_0_.1) | copy-start | bytes 884740
  0.0 18.9 %collective-permute-start = (bf16[192,768]{1,0:T(8,128)(2,1)}, bf16[192,768]{1,0:T(8,128)(2,1)S(1)}, u32[]{:S(2)}, u32[]{:S(2)}) collective-permute-start(bf16[192,768]{1,0:T(8,128)(2,1)} %refs_0_.1), channel_id=1, source_target_pairs={{0,2},{1,3},{2,0},{3,1},{4,6},{5,7},{6,4},{7,5},{8,10},{9,11},{10,... | collective-permute-start | bytes 884744 | tf_op jit(solution)/shard_map/ppermute | solution.py:491
  4.8 14.7 %collective-permute-start.5 = (bf16[40,576]{1,0:T(8,128)(2,1)S(1)}, bf16[40,576]{1,0:T(8,128)(2,1)S(1)}, u32[]{:S(2)}, u32[]{:S(2)}) collective-permute-start(bf16[40,576]{1,0:T(8,128)(2,1)S(1)} %get-tuple-element.20.refs_0_), channel_id=1, source_target_pairs={{0,3},{1,2},{2,1},{3,0},{4,7},{5,6},{6,5},{7,4},{8,11},{9,10},{10,... | collective-permute-start | bytes 138248 | tf_op jit(solution)/shard_map/ppermute | solution.py:491
  4.9 14.6 %collective-permute-start.4 = (bf16[40,576]{1,0:T(8,128)(2,1)S(1)}, bf16[40,576]{1,0:T(8,128)(2,1)S(1)}, u32[]{:S(2)}, u32[]{:S(2)}) collective-permute-start(bf16[40,576]{1,0:T(8,128)(2,1)S(1)} %get-tuple-element.20.refs_0_), channel_id=1, source_target_pairs={{0,2},{1,3},{2,0},{3,1},{4,6},{5,7},{6,4},{7,5},{8,10},{9,11},{10,... | collective-permute-start | bytes 138248 | tf_op jit(solution)/shard_map/ppermute | solution.py:491
  6.1 13.5 %collective-permute-start.3 = (bf16[40,576]{1,0:T(8,128)(2,1)S(1)}, bf16[40,576]{1,0:T(8,128)(2,1)S(1)}, u32[]{:S(2)}, u32[]{:S(2)}) collective-permute-start(bf16[40,576]{1,0:T(8,128)(2,1)S(1)} %get-tuple-element.20.refs_0_), channel_id=1, source_target_pairs={{0,1},{1,0},{2,3},{3,2},{4,5},{5,4},{6,7},{7,6},{8,9},{9,8},{10,11... | collective-permute-start | bytes 138248 | tf_op jit(solution)/shard_map/ppermute | solution.py:491
  18.9 3.5 %copy-start.1 = (bf16[33,768]{1,0:T(8,128)(2,1)S(1)}, bf16[33,768]{1,0:T(8,128)(2,1)}, u32[]{:S(2)}) copy-start(bf16[33,768]{1,0:T(8,128)(2,1)} %refs_7_.1) | copy-start | bytes 152068
  18.9 3.5 %copy-start.2 = (bf16[3,192,768]{2,1,0:T(8,128)(2,1)S(1)}, bf16[3,192,768]{2,1,0:T(8,128)(2,1)}, u32[]{:S(2)}) copy-start(bf16[3,192,768]{2,1,0:T(8,128)(2,1)} %param.12) | copy-start | bytes 2654212
  19.0 3.5 %collective-permute-start.1 = (bf16[192,768]{1,0:T(8,128)(2,1)S(1)}, bf16[192,768]{1,0:T(8,128)(2,1)S(1)}, u32[]{:S(2)}, u32[]{:S(2)}) collective-permute-start(bf16[192,768]{1,0:T(8,128)(2,1)S(1)} %copy-done.3), channel_id=1, source_target_pairs={{0,1},{1,0},{2,3},{3,2},{4,5},{5,4},{6,7},{7,6},{8,9},{9,8},{10,11... | collective-permute-start | bytes 884744 | tf_op jit(solution)/shard_map/ppermute | solution.py:491
  19.0 3.4 %collective-permute-start.2 = (bf16[192,768]{1,0:T(8,128)(2,1)S(1)}, bf16[192,768]{1,0:T(8,128)(2,1)S(1)}, u32[]{:S(2)}, u32[]{:S(2)}) collective-permute-start(bf16[192,768]{1,0:T(8,128)(2,1)S(1)} %collective-permute-done.refs_2_), channel_id=1, source_target_pairs={{0,1},{1,0},{2,3},{3,2},{4,5},{5,4},{6,7},{7,6},{8,9},{9,8},{10,11... | collective-permute-start | bytes 884744 | tf_op jit(solution)/shard_map/ppermute | solution.py:491
  22.4 11.8 %copy-start = (bf16[192,768]{1,0:T(8,128)(2,1)S(1)}, bf16[192,768]{1,0:T(8,128)(2,1)}, u32[]{:S(2)}) copy-start(bf16[192,768]{1,0:T(8,128)(2,1)} %refs_10_.1) | copy-start | bytes 884740
  25.8 5.7 %collective-permute-start.7 = (bf16[384,128]{1,0:T(8,128)(2,1)S(1)}, bf16[384,128]{1,0:T(8,128)(2,1)S(1)}, u32[]{:S(2)}, u32[]{:S(2)}) collective-permute-start(bf16[384,128]{1,0:T(8,128)(2,1)S(1)} %get-tuple-element.25.refs_0_), channel_id=1, source_target_pairs={{0,2},{1,3},{2,0},{3,1},{4,6},{5,7},{6,4},{7,5},{8,10},{9,11},{10,... | collective-permute-start | bytes 294920 | tf_op jit(solution)/shard_map/ppermute | solution.py:491
  26.4 6.5 %collective-permute-start.10 = (bf16[384,128]{1,0:T(8,128)(2,1)S(1)}, bf16[384,128]{1,0:T(8,128)(2,1)S(1)}, u32[]{:S(2)}, u32[]{:S(2)}) collective-permute-start(bf16[384,128]{1,0:T(8,128)(2,1)S(1)} %get-tuple-element.26.refs_4_), channel_id=1, source_target_pairs={{0,2},{1,3},{2,0},{3,1},{4,6},{5,7},{6,4},{7,5},{8,10},{9,11},{10,... | collective-permute-start | bytes 294920 | tf_op jit(solution)/shard_map/ppermute | solution.py:491
  27.9 5.0 %collective-permute-start.6 = (bf16[384,128]{1,0:T(8,128)(2,1)S(1)}, bf16[384,128]{1,0:T(8,128)(2,1)S(1)}, u32[]{:S(2)}, u32[]{:S(2)}) collective-permute-start(bf16[384,128]{1,0:T(8,128)(2,1)S(1)} %get-tuple-element.25.refs_0_), channel_id=1, source_target_pairs={{0,1},{1,0},{2,3},{3,2},{4,5},{5,4},{6,7},{7,6},{8,9},{9,8},{10,11... | collective-permute-start | bytes 294920 | tf_op jit(solution)/shard_map/ppermute | solution.py:491
  27.9 5.0 %collective-permute-start.9 = (bf16[384,128]{1,0:T(8,128)(2,1)S(1)}, bf16[384,128]{1,0:T(8,128)(2,1)S(1)}, u32[]{:S(2)}, u32[]{:S(2)}) collective-permute-start(bf16[384,128]{1,0:T(8,128)(2,1)S(1)} %get-tuple-element.26.refs_4_), channel_id=1, source_target_pairs={{0,1},{1,0},{2,3},{3,2},{4,5},{5,4},{6,7},{7,6},{8,9},{9,8},{10,11... | collective-permute-start | bytes 294920 | tf_op jit(solution)/shard_map/ppermute | solution.py:491
  31.5 1.5 %collective-permute-start.8 = (bf16[384,128]{1,0:T(8,128)(2,1)S(1)}, bf16[384,128]{1,0:T(8,128)(2,1)S(1)}, u32[]{:S(2)}, u32[]{:S(2)}) collective-permute-start(bf16[384,128]{1,0:T(8,128)(2,1)S(1)} %collective-permute-done.7.refs_2_), channel_id=1, source_target_pairs={{0,1},{1,0},{2,3},{3,2},{4,5},{5,4},{6,7},{7,6},{8,9},{9,8},{10,11... | collective-permute-start | bytes 294920 | tf_op jit(solution)/shard_map/ppermute | solution.py:491
  32.9 1.3 %collective-permute-start.11 = (bf16[384,128]{1,0:T(8,128)(2,1)S(1)}, bf16[384,128]{1,0:T(8,128)(2,1)S(1)}, u32[]{:S(2)}, u32[]{:S(2)}) collective-permute-start(bf16[384,128]{1,0:T(8,128)(2,1)S(1)} %collective-permute-done.10.refs_6_), channel_id=1, source_target_pairs={{0,1},{1,0},{2,3},{3,2},{4,5},{5,4},{6,7},{7,6},{8,9},{9,8},{10,11... | collective-permute-start | bytes 294920 | tf_op jit(solution)/shard_map/ppermute | solution.py:491

commit v10 on v8

--- a/solution.py
+++ b/solution.py
@@ -11,8 +11,7 @@
 EPS = 1e-05
 LANES = 128
 CODES = 64
-VOCAB_ROWS = 40
-TABLE_ROWS = 48
+TABLE_ROWS = 40
 
 SMALL_VMEM = 8 * 1024 * 1024
 LARGE_VMEM = 32 * 1024 * 1024
@@ -63,13 +62,15 @@
     live = jnp.zeros(ids_ref.shape, jnp.int32)
     for r in range(ids_ref.shape[0]):
         live = jnp.where(row == r, live_ref[r], live)
-    out_ref[...] = ids_ref[...] + 65536 * live
-
-
-def make_codes(ids, pad_mask):
+    coded = ids_ref[...] + 65536 * live
+    for g in range(out_ref.shape[0]):
+        out_ref[g] = coded
+
+
+def make_codes(ids, pad_mask, groups):
     return pl.pallas_call(
         code_kernel,
-        out_shape=jax.ShapeDtypeStruct(ids.shape, jnp.int32),
+        out_shape=jax.ShapeDtypeStruct((groups,) + ids.shape, jnp.int32),
         in_specs=[pl.BlockSpec(memory_space=pltpu.HBM)] * 2,
         scratch_shapes=[
             pltpu.VMEM(ids.shape, jnp.int32),
@@ -82,7 +83,7 @@
 
 
 def table_kernel(embed_hbm, qkv_hbm, out_ref, embed_ref, qkv_ref, padded_ref, sems):
-    kinds, local = qkv_ref.shape[0:2]
+    kinds = qkv_ref.shape[0]
     loads = [pltpu.make_async_copy(embed_hbm, embed_ref, sems.at[kinds])]
     loads += [
         pltpu.make_async_copy(qkv_hbm.at[t], qkv_ref.at[t], sems.at[t]) for t in range(kinds)
@@ -113,38 +114,11 @@
             pltpu.SemaphoreType.DMA((kinds + 1,)),
         ],
         cost_estimate=pl.CostEstimate(
-            flops=2 * TABLE_ROWS * row_qkv.size,
-            bytes_accessed=2 * row_qkv.size,
-            transcendentals=0,
+            flops=2 * 10**9, bytes_accessed=2 * row_qkv.size, transcendentals=0
         ),
         compiler_params=pltpu.CompilerParams(vmem_limit_bytes=SMALL_VMEM),
         name="tables",
     )(in_hbm(embed), in_hbm(row_qkv))
-
-
-def pack_kernel(table_ref, *refs):
-    codes_refs, out_ref = refs[:-1], refs[-1]
-    coded = jnp.concatenate([ref[...] for ref in codes_refs], 0)
-    some, cols = coded.shape
-    ids = (coded & 0xFFFF).astype(f32)
-    live = (coded >> 16).astype(f32)
-    spare = jnp.concatenate(
-        [ids, live[:, 0:LANES], jnp.zeros((some, out_ref.shape[1] - cols - LANES), f32)], 1
-    )
-    if some < TABLE_ROWS - VOCAB_ROWS:
-        empty = jnp.zeros((TABLE_ROWS - VOCAB_ROWS - some, spare.shape[1]), f32)
-        spare = jnp.concatenate([spare, empty], 0)
-    table = table_ref[...].astype(f32)[0:VOCAB_ROWS]
-    out_ref[...] = jnp.concatenate([table, spare], 0).astype(bf16)
-
-
-def pack(table, codes):
-    return pl.pallas_call(
-        pack_kernel,
-        out_shape=jax.ShapeDtypeStruct(table.shape, bf16),
-        compiler_params=pltpu.CompilerParams(vmem_limit_bytes=SMALL_VMEM),
-        name="pack",
-    )(table, *codes)
 
 
 def halves(pair):
@@ -174,25 +148,18 @@
     )
 
 
-def read_sequences(payload_ref, rows, first, last):
-    parts = payload_ref.shape[0]
-    each = rows // parts
-    return jnp.concatenate(
-        [
-            payload_ref[p, VOCAB_ROWS:TABLE_ROWS, first:last].astype(f32)[0:each]
-            for p in range(parts)
-        ],
-        0,
-    )
+def slot_order(groups):
+    return list(range(0, groups, 2)) + list(range(1, groups, 2))
 
 
 def row_kernel(parts, *refs):
-    payload_refs, refs = refs[:parts], refs[parts:]
+    tables_refs, refs = refs[:parts], refs[parts:]
     (
+        codes_ref,
         row_context_ref,
         own_ref,
         live_ref,
-        payload_ref,
+        tables_ref,
         table_ref,
         hot_ref,
         live_own_ref,
@@ -209,16 +176,17 @@
     group = lax.axis_index("seq")
     part = lax.axis_index("head")
     for p in range(parts):
-        payload_ref[part ^ p] = payload_refs[p][...]
+        tables_ref[part ^ p] = tables_refs[p][...]
 
     for t in range(3):
-        table_ref[t, 0:VOCAB_ROWS, :] = jnp.concatenate(
-            [payload_ref[p, 0:VOCAB_ROWS, t * local : (t + 1) * local] for p in range(parts)], 1
+        table_ref[t, 0:TABLE_ROWS, :] = jnp.concatenate(
+            [tables_ref[p, :, t * local : (t + 1) * local] for p in range(parts)], 1
         )
-        table_ref[t, VOCAB_ROWS:CODES, :] = jnp.zeros((CODES - VOCAB_ROWS, width), bf16)
-
-    ids = read_sequences(payload_ref, rows, 0, cols)
-    live = read_sequences(payload_ref, rows, cols, cols + LANES)
+        table_ref[t, TABLE_ROWS:CODES, :] = jnp.zeros((CODES - TABLE_ROWS, width), bf16)
+
+    coded = jnp.concatenate([codes_ref[group ^ d] for d in slot_order(codes_ref.shape[0])], 0)
+    ids = (coded & 0xFFFF).astype(f32)
+    live = (coded[:, 0:LANES] >> 16).astype(f32)
     live_ref[...] = live
     code = iota((CODES, cols), 0).astype(f32)
     for r in range(rows):
@@ -290,9 +258,9 @@
                 ]
 
 
-def attend_rows(payloads, rows, cols, own, width):
+def attend_rows(tables, codes, rows, cols, own, width):
     heads = width // HEAD_DIM
-    parts = len(payloads)
+    parts = len(tables)
     return pl.pallas_call(
         functools.partial(row_kernel, parts),
         out_shape=(
@@ -301,7 +269,7 @@
             jax.ShapeDtypeStruct((rows, LANES), f32),
         ),
         scratch_shapes=[
-            pltpu.VMEM((parts,) + payloads[0].shape, bf16),
+            pltpu.VMEM((parts,) + tables[0].shape, bf16),
             pltpu.VMEM((3, CODES, width), bf16),
             pltpu.VMEM((rows * CODES, cols), bf16),
             pltpu.VMEM((rows // 2 * own, LANES), bf16),
@@ -311,7 +279,7 @@
         cost_estimate=pl.CostEstimate(flops=3 * 10**9, bytes_accessed=10**6, transcendentals=0),
         compiler_params=pltpu.CompilerParams(vmem_limit_bytes=LARGE_VMEM),
         name="row_attention",
-    )(*payloads)
+    )(*tables, codes)
 
 
 def column_kernel(parts, *refs):
@@ -440,9 +408,10 @@
 
 def finish_kernel(parts, *refs):
     context_refs = refs[:parts]
-    mixed_ref, col_out_ref, *out_refs, weight_ref = refs[parts:]
+    mixed_ref, col_out_ref, out_ref, weight_ref = refs[parts:]
     tokens, local = mixed_ref.shape
     some = tokens // 2
+    pair = lax.axis_index("seq") // 2
     part = lax.axis_index("head")
     for p in range(parts):
         weight_ref[p] = col_out_ref[:, p * local : (p + 1) * local]
@@ -460,19 +429,21 @@
             + dot_nt(context[0:tokens, :], weight[:, 0:LANES])
             + jnp.concatenate([dot_nt(last, left), dot_nt(last, right)], 0)
         )
-    own = tokens // len(out_refs) // 2
-    for d, out_ref in enumerate(out_refs):
+    own = tokens // out_ref.shape[0] // 2
+    for d in range(out_ref.shape[0]):
         first, second = (total[(2 * d + r) * own : (2 * d + r + 1) * own, :] for r in range(2))
         rest = jnp.concatenate([first[:, LANES:local], second[:, LANES:local]], 1)
-        out_ref[...] = jnp.concatenate([first[:, 0:LANES], second[:, 0:LANES], rest], 0).astype(bf16)
-
-
-def finish(contexts, mixed, col_out, slots):
+        out_ref[pair ^ d] = jnp.concatenate(
+            [first[:, 0:LANES], second[:, 0:LANES], rest], 0
+        ).astype(bf16)
+
+
+def finish(contexts, mixed, col_out, count):
     parts = len(contexts)
     tokens, local = mixed.shape
     return pl.pallas_call(
         functools.partial(finish_kernel, parts),
-        out_shape=[jax.ShapeDtypeStruct((tokens // slots * local // LANES, LANES), bf16)] * slots,
+        out_shape=jax.ShapeDtypeStruct((count, tokens // count * local // LANES, LANES), bf16),
         scratch_shapes=[pltpu.VMEM((parts, local, local), bf16)],
         cost_estimate=pl.CostEstimate(flops=10**9, bytes_accessed=10**6, transcendentals=0),
         compiler_params=pltpu.CompilerParams(vmem_limit_bytes=LARGE_VMEM),
@@ -480,19 +451,32 @@
     )(*contexts, mixed, col_out)
 
 
-def order_kernel(*refs):
-    *slot_refs, out_ref, blocks_ref = refs
-    groups = len(slot_refs)
-    group = lax.axis_index("seq")
-    for place, slot_ref in enumerate(slot_refs):
-        d = groups - 1 - place
-        blocks_ref[group ^ d] = slot_ref[...]
+def join_kernel(other_ref, own_ref, out_ref):
+    out_ref[:, 0] = own_ref[...]
+    out_ref[:, 1] = other_ref[...]
+
+
+def join(other, own):
+    return pl.pallas_call(
+        join_kernel,
+        out_shape=jax.ShapeDtypeStruct((own.shape[0], 2) + own.shape[1:], own.dtype),
+        compiler_params=pltpu.CompilerParams(vmem_limit_bytes=SMALL_VMEM),
+        name="join",
+    )(other, own)
+
+
+def order_kernel(blocks_ref, out_ref, ordered_ref):
+    groups = ordered_ref.shape[0]
+    here = lax.axis_index("seq") % 2
+    for pair in range(blocks_ref.shape[0]):
+        for k in range(2):
+            ordered_ref[2 * pair + (here ^ k)] = blocks_ref[pair, k]
     local, cols = out_ref.shape[1:]
     own = cols // groups
     rest = local - LANES
     for part in range(3):
         piece = jnp.concatenate(
-            [blocks_ref[g, part * own : (part + 1) * own, :] for g in range(groups)], 0
+            [ordered_ref[g, part * own : (part + 1) * own, :] for g in range(groups)], 0
         )
         turned = piece.astype(f32).T.astype(bf16)
         if part < 2:
@@ -502,14 +486,15 @@
                 out_ref[r, LANES:local, :] = turned[r * rest : (r + 1) * rest, :]
 
 
-def order(slots, cols, local):
+def order(blocks, cols, local):
+    pairs, _, rows, lanes = blocks.shape
     return pl.pallas_call(
         order_kernel,
         out_shape=jax.ShapeDtypeStruct((2, local, cols), bf16),
-        scratch_shapes=[pltpu.VMEM((len(slots),) + slots[0].shape, bf16)],
+        scratch_shapes=[pltpu.VMEM((2 * pairs, rows, lanes), bf16)],
         compiler_params=pltpu.CompilerParams(vmem_limit_bytes=SMALL_VMEM),
         name="order",
-    )(*slots)
+    )(blocks)
 
 
 def fast_body(ids, pad_mask, embed, row_qkv, row_out, col_qkv, col_out):
@@ -518,7 +503,6 @@
     local = row_out.shape[0]
     groups, parts = lax.axis_size("seq"), lax.axis_size("head")
     own, rows = cols // groups, rows_here * groups
-    each = groups // parts
 
     def pairwise(value, partner):
         order = [(g, p) for g in range(groups) for p in range(parts)]
@@ -535,26 +519,33 @@
         return g, p ^ 3
 
     far = pairwise(row_out, across)
-    coded = make_codes(ids, pad_mask)
-    codes = [pairwise(coded, lambda g, p, b=b: (g ^ (p * each + b), p)) for b in range(each)]
-    payload = pack(make_tables(embed, row_qkv), codes)
-    payloads = [payload] + [pairwise(payload, to) for to in (sibling, across, opposite)]
-    *payloads, near, far = lax.optimization_barrier((*payloads, row_out, far))
+    codes = make_codes(ids, pad_mask, groups)
+    codes, row_qkv = lax.optimization_barrier((codes, row_qkv))
+    table = make_tables(embed, row_qkv)
+    tables = [table] + [pairwise(table, to) for to in (sibling, across, opposite)]
+    codes = lax.all_to_all(codes, "seq", split_axis=0, concat_axis=0, tiled=True)
+    codes, near, far = lax.optimization_barrier((codes, row_out, far))
     row_outs = [row_out, pairwise(near, sibling), far, pairwise(far, sibling)]
-    row_context, own_codes, live = attend_rows(payloads, rows, cols, own, width)
-    *contexts, mixed_low, mixed_high = attend_columns_here(
+    row_context, own_codes, live = attend_rows(tables, codes, rows, cols, own, width)
+    *halves_here, mixed_low, mixed_high = attend_columns_here(
         row_outs, live, row_context, own_codes, embed, col_qkv.reshape(3 * local, width)
     )
-    slots = [None] * groups
-    for c, mixed in ((1, mixed_high), (0, mixed_low)):
-        beyond = pairwise(contexts[c], across)
-        near = pairwise(contexts[c], sibling)
-        whole = (contexts[c], near, beyond, pairwise(beyond, sibling))
-        some = groups // 2
-        for j, block in enumerate(finish(whole, mixed, col_out, some)):
-            d = c * some + j
-            slots[d] = pairwise(block, lambda g, p, d=d: (g ^ d, p)) if d else block
-    return jnp.swapaxes(order(slots[::-1], cols, local), 1, 2)
+    results = []
+    for context, mixed in zip(halves_here, (mixed_low, mixed_high)):
+        beyond = pairwise(context, across)
+        whole = (context, pairwise(context, sibling), beyond, pairwise(beyond, sibling))
+        results.append(finish(whole, mixed, col_out, groups // 2))
+    own_result, other_result = results
+    other_result = pairwise(other_result, lambda g, p: (g ^ 1, p))
+    blocks = lax.all_to_all(
+        join(other_result, own_result),
+        "seq",
+        split_axis=0,
+        concat_axis=0,
+        tiled=True,
+        axis_index_groups=[list(range(k, groups, 2)) for k in range(2)],
+    )
+    return jnp.swapaxes(order(blocks, cols, local), 1, 2)
 
 
 def weight_fold(out_weight, piece):
@@ -642,16 +633,15 @@
     parts = lax.axis_size("head")
     local = row_out.shape[0]
     fits = (
-        groups & (groups - 1) == 0
-        and parts == 4
-        and groups % parts == 0
+        parts == 4
+        and groups >= 2
+        and groups & (groups - 1) == 0
         and rows * 8 == LANES
         and rows_here == 2
-        and rows <= 8 * parts
         and own % 32 == 0
-        and cols + LANES <= 3 * local
+        and cols >= LANES
         and local == LANES + HEAD_DIM
-        and embed.shape[0] <= VOCAB_ROWS
+        and embed.shape[0] <= TABLE_ROWS
     )
     chosen = fast_body if fits else general_body
     return chosen(ids, pad_mask, embed, row_qkv, row_out, col_qkv, col_out)

time: 48.5 us -> 50.9 us (1.049)
  blocking collectives: 0 us -> 22.2 us
  starting transfers between devices: 26.2 us -> 8.61 us
  waiting for transfers between devices: 10.8 us -> 8.43 us
    all_to_all x0 -> x2, blocking collectives: none -> 22.2 us  [the longest x1 12.2 us: fast_body(): lax.all_to_all(codes, 'seq', split_axis=0, concat_axis=0, tiled=True)]
    ppermute x21 -> x13, starting transfers between devices: 26.2 us -> 8.61 us  [pairwise(): lax.ppermute(value, ('seq', 'head'), [(i, g * parts + p) for i, (g, p) in...]
    ppermute x21 -> x13, waiting for transfers between devices: 10.8 us -> 8.43 us  [pairwise(): lax.ppermute(value, ('seq', 'head'), [(i, g * parts + p) for i, (g, p) in...]
  transfers between devices with their start and end apart: 21 -> 13, of which waited for: 6 -> 3; matrix products, arithmetic and copies ran while one was open for 0% -> 0% of each run, Pallas kernels for 15% -> 14%
where the time goes in v10:
time: 50.9 us; the launch traced here: 50.6 us
  blocking collectives  22.2 us (44%)
  Pallas kernels  11.3 us (22%)
  starting transfers between devices  8.61 us (17%)
  waiting for transfers between devices  8.43 us (17%)
    all_to_all x1, blocking collectives, fast_body(): lax.all_to_all(codes, 'seq', split_axis=0, concat_axis=0, tiled=True)  12.2 us
    all_to_all x1, blocking collectives, fast_body(): lax.all_to_all(join(other_result, own_result), 'seq', split_axis=0, conca...  9.99 us
    ppermute x13, starting transfers between devices, pairwise(): lax.ppermute(value, ('seq', 'head'), [(i, g * parts + p) for i, (g, p) in...  8.61 us
    ppermute x13, waiting for transfers between devices, pairwise(): lax.ppermute(value, ('seq', 'head'), [(i, g * parts + p) for i, (g, p) in...  8.43 us
    pallas_call x1, Pallas kernels, attend_columns_here(): pl.pallas_call(functools.partial(column_kernel, parts), out_shape=(*[jax....  3.33 us
    pallas_call x1, Pallas kernels, attend_rows(): pl.pallas_call(functools.partial(row_kernel, parts), out_shape=(jax.Shape...  2.83 us
    pallas_call x1, Pallas kernels, make_tables(): pl.pallas_call(table_kernel, out_shape=jax.ShapeDtypeStruct((TABLE_ROWS,...  1.88 us
    pallas_call x2, Pallas kernels, finish(): pl.pallas_call(functools.partial(finish_kernel, parts), out_shape=jax.Sha...  1.55 us
  transfers between devices with their start and end apart: 13, of which 3 were waited for; matrix products, arithmetic and copies ran while one was open for 0% of the time, Pallas kernels for 14%

profile of v10, /device:TPU:0, one launch (start us, length us, event | category | flops | bytes accessed | tf_op | source)
XLA Modules:
  0.0 50.6 jit_solution(3571392238329576652)
XLA Ops:
  0.0 2.9 %collective-permute-start = (bf16[192,768]{1,0:T(8,128)(2,1)}, bf16[192,768]{1,0:T(8,128)(2,1)S(1)}, u32[]{:S(2)}, u32[]{:S(2)}) collective-permute-start(bf16[192,768]{1,0:T(8,128)(2,1)} %refs_0_.1), channel_id=1, source_target_pairs={{0,2},{1,3},{2,0},{3,1},{4,6},{5,7},{6,4},{7,5},{8,10},{9,11},{10,... | collective-permute-start | bytes 884744 | tf_op jit(solution)/shard_map/ppermute | solution.py:510
  2.9 0.8 %codes.1 = s32[8,2,256]{2,1,0:T(2,128)S(1)} custom-call(s32[2,256]{1,0:T(2,128)} %ids_hbm.1, s32[2]{0:T(128)} %live_hbm.1), custom_call_target="tpu_custom_call" | custom-call | tf_op jit(solution)/shard_map/codes/pallas_call | solution.py:71
  3.8 0.0 copy-start.1
  3.8 1.9 %tables.1.refs_0_ = bf16[40,576]{1,0:T(8,128)(2,1)S(1)} custom-call(bf16[33,768]{1,0:T(8,128)(2,1)} %refs_7_.1, bf16[3,192,768]{2,1,0:T(8,128)(2,1)} %qkv_hbm), custom_call_target="tpu_custom_call" | custom-call | flops 2000000000 | bytes 884736 | tf_op jit(solution)/shard_map/tables/pallas_call | solution.py:106
  5.7 0.1 collective-permute-start.5
  5.8 1.2 %collective-permute-start.4 = (bf16[40,576]{1,0:T(8,128)(2,1)S(1)}, bf16[40,576]{1,0:T(8,128)(2,1)S(1)}, u32[]{:S(2)}, u32[]{:S(2)}) collective-permute-start(bf16[40,576]{1,0:T(8,128)(2,1)S(1)} %tables.1.refs_0_), channel_id=1, source_target_pairs={{0,2},{1,3},{2,0},{3,1},{4,6},{5,7},{6,4},{7,5},{8,10},{9,11},{10,... | collective-permute-start | bytes 138248 | tf_op jit(solution)/shard_map/ppermute | solution.py:510
  6.9 0.7 %collective-permute-start.3 = (bf16[40,576]{1,0:T(8,128)(2,1)S(1)}, bf16[40,576]{1,0:T(8,128)(2,1)S(1)}, u32[]{:S(2)}, u32[]{:S(2)}) collective-permute-start(bf16[40,576]{1,0:T(8,128)(2,1)S(1)} %tables.1.refs_0_), channel_id=1, source_target_pairs={{0,1},{1,0},{2,3},{3,2},{4,5},{5,4},{6,7},{7,6},{8,9},{9,8},{10,11... | collective-permute-start | bytes 138248 | tf_op jit(solution)/shard_map/ppermute | solution.py:510
  7.6 12.2 %all_to_all.10.refs_4_ = s32[8,2,256]{2,1,0:T(2,128)S(1)} all-to-all(s32[8,2,256]{2,1,0:T(2,128)S(1)} %codes.1), channel_id=1, replica_groups=mesh['seq'=8,'head'=4] {'seq'}, dimensions={0} | all-to-all | bytes 32768 | tf_op jit(solution)/shard_map/all_to_all | solution.py:526
  19.8 0.0 copy-start
  19.8 0.0 copy-start.3
  19.8 0.0 collective-permute-done.refs_2_
  19.8 0.0 copy-done.1
  19.8 0.1 collective-permute-start.1
  19.9 0.5 collective-permute-start.2
  20.4 0.0 collective-permute-done.5.refs_3_
  20.4 0.0 collective-permute-done.4.refs_2_
  20.4 0.0 collective-permute-done.3.refs_1_
  20.4 2.8 %row_attention.1 = (bf16[512,768]{1,0:T(8,128)(2,1)S(1)}, bf16[256,128]{1,0:T(8,128)(2,1)S(1)}, f32[16,128]{1,0:T(8,128)S(1)}) custom-call(bf16[40,576]{1,0:T(8,128)(2,1)S(1)} %tables.1.refs_0_, bf16[40,576]{1,0:T(8,128)(2,1)S(1)} %collective-permute-done.3.refs_1_, bf16[40,576]{1,0:T(8,128)(2,1)S(1)} %collective-permute-done.4.refs_2_, ...), custom_call_target="tpu_custom_call" | custom-call | flops 3000000000 | bytes 1000000 | tf_op jit(solution)/shard_map/row_attention/pallas_call | solution.py:264
  23.2 0.0 collective-permute-done.1.refs_1_
  23.2 0.0 collective-permute-done.2.refs_3_
  23.3 0.0 copy-done
  23.3 0.0 copy-done.3
  23.3 0.0 copy-start.2
  23.3 3.3 %column_attention.1 = (bf16[384,128]{1,0:T(8,128)(2,1)S(1)}, bf16[384,128]{1,0:T(8,128)(2,1)S(1)}, f32[256,192]{1,0:T(8,128)S(1)}, f32[256,192]{1,0:T(8,128)S(1)}) custom-call(bf16[192,768]{1,0:T(8,128)(2,1)S(1)} %copy-done.1, bf16[192,768]{1,0:T(8,128)(2,1)S(1)} %collective-permute-done.1.refs_1_, bf16[192,768]{1,0:T(8,128)(2,1)S(1)} %collective-permute-done.refs_2_, ...), custom_call_target="tpu_custom_call" | custom-call | flops 2000000000 | bytes 1000000 | tf_op jit(solution)/shard_map/column_attention/pallas_call | solution.py:393
  26.6 0.6 %collective-permute-start.7 = (bf16[384,128]{1,0:T(8,128)(2,1)S(1)}, bf16[384,128]{1,0:T(8,128)(2,1)S(1)}, u32[]{:S(2)}, u32[]{:S(2)}) collective-permute-start(bf16[384,128]{1,0:T(8,128)(2,1)S(1)} %get-tuple-element.25.refs_0_), channel_id=1, source_target_pairs={{0,2},{1,3},{2,0},{3,1},{4,6},{5,7},{6,4},{7,5},{8,10},{9,11},{10,... | collective-permute-start | bytes 294920 | tf_op jit(solution)/shard_map/ppermute | solution.py:510
  27.2 1.5 %collective-permute-start.11 = (bf16[384,128]{1,0:T(8,128)(2,1)S(1)}, bf16[384,128]{1,0:T(8,128)(2,1)S(1)}, u32[]{:S(2)}, u32[]{:S(2)}) collective-permute-start(bf16[384,128]{1,0:T(8,128)(2,1)S(1)} %get-tuple-element.27.refs_0_), channel_id=1, source_target_pairs={{0,2},{1,3},{2,0},{3,1},{4,6},{5,7},{6,4},{7,5},{8,10},{9,11},{10,... | collective-permute-start | bytes 294920 | tf_op jit(solution)/shard_map/ppermute | solution.py:510
  28.7 0.0 collective-permute-start.6
  28.7 3.6 %collective-permute-done.7.refs_2_ = bf16[384,128]{1,0:T(8,128)(2,1)S(1)} collective-permute-done((bf16[384,128]{1,0:T(8,128)(2,1)S(1)}, bf16[384,128]{1,0:T(8,128)(2,1)S(1)}, u32[]{:S(2)}, u32[]{:S(2)}) %collective-permute-start.7) | collective-permute-done | bytes 98336 | tf_op jit(solution)/shard_map/ppermute | solution.py:510
  32.3 0.0 collective-permute-start.8
  32.3 0.5 %collective-permute-start.10 = (bf16[384,128]{1,0:T(8,128)(2,1)S(1)}, bf16[384,128]{1,0:T(8,128)(2,1)S(1)}, u32[]{:S(2)}, u32[]{:S(2)}) collective-permute-start(bf16[384,128]{1,0:T(8,128)(2,1)S(1)} %get-tuple-element.27.refs_0_), channel_id=1, source_target_pairs={{0,1},{1,0},{2,3},{3,2},{4,5},{5,4},{6,7},{7,6},{8,9},{9,8},{10,11... | collective-permute-start | bytes 294920 | tf_op jit(solution)/shard_map/ppermute | solution.py:510
  32.8 0.9 %collective-permute-done.11.refs_2_ = bf16[384,128]{1,0:T(8,128)(2,1)S(1)} collective-permute-done((bf16[384,128]{1,0:T(8,128)(2,1)S(1)}, bf16[384,128]{1,0:T(8,128)(2,1)S(1)}, u32[]{:S(2)}, u32[]{:S(2)}) %collective-permute-start.11) | collective-permute-done | bytes 98336 | tf_op jit(solution)/shard_map/ppermute | solution.py:510
  33.7 0.0 collective-permute-start.12
  33.7 0.0 collective-permute-done.6.refs_1_
  33.7 0.0 collective-permute-done.8.refs_3_
  33.8 0.0 copy-done.2
  33.8 0.8 %finish.2 = bf16[4,96,128]{2,1,0:T(8,128)(2,1)S(1)} custom-call(bf16[384,128]{1,0:T(8,128)(2,1)S(1)} %get-tuple-element.25.refs_0_, bf16[384,128]{1,0:T(8,128)(2,1)S(1)} %collective-permute-done.6.refs_1_, bf16[384,128]{1,0:T(8,128)(2,1)S(1)} %collective-permute-done.7.refs_2_, bf16[384,128]{1,0:T(8,128)(2,1)S(1)} %collective-permute-done.8.refs_3_, ...), custom_call_target="tpu_custom_call" | custom-call | flops 1000000000 | bytes 1000000 | tf_op jit(solution)/shard_map/finish/pallas_call | solution.py:444
  34.5 0.6 %collective-permute-start.9 = (bf16[4,96,128]{2,1,0:T(8,128)(2,1)S(1)}, bf16[4,96,128]{2,1,0:T(8,128)(2,1)S(1)}, u32[]{:S(2)}, u32[]{:S(2)}) collective-permute-start(bf16[4,96,128]{2,1,0:T(8,128)(2,1)S(1)} %finish.2), channel_id=1, source_target_pairs={{0,4},{1,5},{2,6},{3,7},{4,0},{5,1},{6,2},{7,3},{8,12},{9,13},{10,... | collective-permute-start | bytes 294920 | tf_op jit(solution)/shard_map/ppermute | solution.py:510
  35.1 0.0 collective-permute-done.10.refs_1_
  35.1 0.0 collective-permute-done.12.refs_3_
  35.1 0.8 %finish.3.own_ref = bf16[4,96,128]{2,1,0:T(8,128)(2,1)S(1)} custom-call(bf16[384,128]{1,0:T(8,128)(2,1)S(1)} %get-tuple-element.27.refs_0_, bf16[384,128]{1,0:T(8,128)(2,1)S(1)} %collective-permute-done.10.refs_1_, bf16[384,128]{1,0:T(8,128)(2,1)S(1)} %collective-permute-done.11.refs_2_, bf16[384,128]{1,0:T(8,128)(2,1)S(1)} %collective-permute-done.12.refs_3_, ...), custom_call_target="tpu_custom_call" | custom-call | flops 1000000000 | bytes 1000000 | tf_op jit(solution)/shard_map/finish/pallas_call | solution.py:444
  35.9 3.9 %collective-permute-done.9.other_ref = bf16[4,96,128]{2,1,0:T(8,128)(2,1)S(1)} collective-permute-done((bf16[4,96,128]{2,1,0:T(8,128)(2,1)S(1)}, bf16[4,96,128]{2,1,0:T(8,128)(2,1)S(1)}, u32[]{:S(2)}, u32[]{:S(2)}) %collective-permute-start.9) | collective-permute-done | bytes 98336 | tf_op jit(solution)/shard_map/ppermute | solution.py:510
  39.8 10.0 %all_to_all.11.blocks_ref = bf16[4,2,96,128]{3,2,1,0:T(8,128)(2,1)S(1)} all-to-all(bf16[4,2,96,128]{3,2,1,0:T(8,128)(2,1)S(1)} %join.1), channel_id=1, replica_groups={{0,8,16,24},{4,12,20,28},{1,9,17,25},{5,13,21,29},{2,10,18,26},{6,14,22..., dimensions={0} | all-to-all | bytes 393216 | tf_op jit(solution)/shard_map/all_to_all | solution.py:540
  49.8 0.8 %order.1 = bf16[2,192,256]{2,1,0:T(8,128)(2,1)} custom-call(bf16[4,2,96,128]{3,2,1,0:T(8,128)(2,1)S(1)} %all_to_all.11.blocks_ref), custom_call_target="tpu_custom_call" | custom-call | tf_op jit(solution)/shard_map/order/pallas_call | solution.py:491
  (1 shorter events, 0.0 us)
Async XLA Ops:
  0.0 19.8 %collective-permute-start = (bf16[192,768]{1,0:T(8,128)(2,1)}, bf16[192,768]{1,0:T(8,128)(2,1)S(1)}, u32[]{:S(2)}, u32[]{:S(2)}) collective-permute-start(bf16[192,768]{1,0:T(8,128)(2,1)} %refs_0_.1), channel_id=1, source_target_pairs={{0,2},{1,3},{2,0},{3,1},{4,6},{5,7},{6,4},{7,5},{8,10},{9,11},{10,... | collective-permute-start | bytes 884744 | tf_op jit(solution)/shard_map/ppermute | solution.py:510
  3.8 16.0 %copy-start.1 = (bf16[192,768]{1,0:T(8,128)(2,1)S(1)}, bf16[192,768]{1,0:T(8,128)(2,1)}, u32[]{:S(2)}) copy-start(bf16[192,768]{1,0:T(8,128)(2,1)} %refs_0_.1) | copy-start | bytes 884740
  5.7 14.7 %collective-permute-start.5 = (bf16[40,576]{1,0:T(8,128)(2,1)S(1)}, bf16[40,576]{1,0:T(8,128)(2,1)S(1)}, u32[]{:S(2)}, u32[]{:S(2)}) collective-permute-start(bf16[40,576]{1,0:T(8,128)(2,1)S(1)} %tables.1.refs_0_), channel_id=1, source_target_pairs={{0,3},{1,2},{2,1},{3,0},{4,7},{5,6},{6,5},{7,4},{8,11},{9,10},{10,... | collective-permute-start | bytes 138248 | tf_op jit(solution)/shard_map/ppermute | solution.py:510
  5.8 14.6 %collective-permute-start.4 = (bf16[40,576]{1,0:T(8,128)(2,1)S(1)}, bf16[40,576]{1,0:T(8,128)(2,1)S(1)}, u32[]{:S(2)}, u32[]{:S(2)}) collective-permute-start(bf16[40,576]{1,0:T(8,128)(2,1)S(1)} %tables.1.refs_0_), channel_id=1, source_target_pairs={{0,2},{1,3},{2,0},{3,1},{4,6},{5,7},{6,4},{7,5},{8,10},{9,11},{10,... | collective-permute-start | bytes 138248 | tf_op jit(solution)/shard_map/ppermute | solution.py:510
  6.9 13.5 %collective-permute-start.3 = (bf16[40,576]{1,0:T(8,128)(2,1)S(1)}, bf16[40,576]{1,0:T(8,128)(2,1)S(1)}, u32[]{:S(2)}, u32[]{:S(2)}) collective-permute-start(bf16[40,576]{1,0:T(8,128)(2,1)S(1)} %tables.1.refs_0_), channel_id=1, source_target_pairs={{0,1},{1,0},{2,3},{3,2},{4,5},{5,4},{6,7},{7,6},{8,9},{9,8},{10,11... | collective-permute-start | bytes 138248 | tf_op jit(solution)/shard_map/ppermute | solution.py:510
  19.8 3.5 %copy-start = (bf16[3,192,768]{2,1,0:T(8,128)(2,1)S(1)}, bf16[3,192,768]{2,1,0:T(8,128)(2,1)}, u32[]{:S(2)}) copy-start(bf16[3,192,768]{2,1,0:T(8,128)(2,1)} %param.12) | copy-start | bytes 2654212
  19.8 3.5 %copy-start.3 = (bf16[33,768]{1,0:T(8,128)(2,1)S(1)}, bf16[33,768]{1,0:T(8,128)(2,1)}, u32[]{:S(2)}) copy-start(bf16[33,768]{1,0:T(8,128)(2,1)} %refs_7_.1) | copy-start | bytes 152068
  19.8 3.4 %collective-permute-start.1 = (bf16[192,768]{1,0:T(8,128)(2,1)S(1)}, bf16[192,768]{1,0:T(8,128)(2,1)S(1)}, u32[]{:S(2)}, u32[]{:S(2)}) collective-permute-start(bf16[192,768]{1,0:T(8,128)(2,1)S(1)} %copy-done.1), channel_id=1, source_target_pairs={{0,1},{1,0},{2,3},{3,2},{4,5},{5,4},{6,7},{7,6},{8,9},{9,8},{10,11... | collective-permute-start | bytes 884744 | tf_op jit(solution)/shard_map/ppermute | solution.py:510
  19.9 3.4 %collective-permute-start.2 = (bf16[192,768]{1,0:T(8,128)(2,1)S(1)}, bf16[192,768]{1,0:T(8,128)(2,1)S(1)}, u32[]{:S(2)}, u32[]{:S(2)}) collective-permute-start(bf16[192,768]{1,0:T(8,128)(2,1)S(1)} %collective-permute-done.refs_2_), channel_id=1, source_target_pairs={{0,1},{1,0},{2,3},{3,2},{4,5},{5,4},{6,7},{7,6},{8,9},{9,8},{10,11... | collective-permute-start | bytes 884744 | tf_op jit(solution)/shard_map/ppermute | solution.py:510
  23.3 10.5 %copy-start.2 = (bf16[192,768]{1,0:T(8,128)(2,1)S(1)}, bf16[192,768]{1,0:T(8,128)(2,1)}, u32[]{:S(2)}) copy-start(bf16[192,768]{1,0:T(8,128)(2,1)} %refs_5_.3) | copy-start | bytes 884740
  26.6 5.7 %collective-permute-start.7 = (bf16[384,128]{1,0:T(8,128)(2,1)S(1)}, bf16[384,128]{1,0:T(8,128)(2,1)S(1)}, u32[]{:S(2)}, u32[]{:S(2)}) collective-permute-start(bf16[384,128]{1,0:T(8,128)(2,1)S(1)} %get-tuple-element.25.refs_0_), channel_id=1, source_target_pairs={{0,2},{1,3},{2,0},{3,1},{4,6},{5,7},{6,4},{7,5},{8,10},{9,11},{10,... | collective-permute-start | bytes 294920 | tf_op jit(solution)/shard_map/ppermute | solution.py:510
  27.2 6.5 %collective-permute-start.11 = (bf16[384,128]{1,0:T(8,128)(2,1)S(1)}, bf16[384,128]{1,0:T(8,128)(2,1)S(1)}, u32[]{:S(2)}, u32[]{:S(2)}) collective-permute-start(bf16[384,128]{1,0:T(8,128)(2,1)S(1)} %get-tuple-element.27.refs_0_), channel_id=1, source_target_pairs={{0,2},{1,3},{2,0},{3,1},{4,6},{5,7},{6,4},{7,5},{8,10},{9,11},{10,... | collective-permute-start | bytes 294920 | tf_op jit(solution)/shard_map/ppermute | solution.py:510
  28.7 5.0 %collective-permute-start.6 = (bf16[384,128]{1,0:T(8,128)(2,1)S(1)}, bf16[384,128]{1,0:T(8,128)(2,1)S(1)}, u32[]{:S(2)}, u32[]{:S(2)}) collective-permute-start(bf16[384,128]{1,0:T(8,128)(2,1)S(1)} %get-tuple-element.25.refs_0_), channel_id=1, source_target_pairs={{0,1},{1,0},{2,3},{3,2},{4,5},{5,4},{6,7},{7,6},{8,9},{9,8},{10,11... | collective-permute-start | bytes 294920 | tf_op jit(solution)/shard_map/ppermute | solution.py:510
  32.3 1.4 %collective-permute-start.8 = (bf16[384,128]{1,0:T(8,128)(2,1)S(1)}, bf16[384,128]{1,0:T(8,128)(2,1)S(1)}, u32[]{:S(2)}, u32[]{:S(2)}) collective-permute-start(bf16[384,128]{1,0:T(8,128)(2,1)S(1)} %collective-permute-done.7.refs_2_), channel_id=1, source_target_pairs={{0,1},{1,0},{2,3},{3,2},{4,5},{5,4},{6,7},{7,6},{8,9},{9,8},{10,11... | collective-permute-start | bytes 294920 | tf_op jit(solution)/shard_map/ppermute | solution.py:510
  32.3 2.8 %collective-permute-start.10 = (bf16[384,128]{1,0:T(8,128)(2,1)S(1)}, bf16[384,128]{1,0:T(8,128)(2,1)S(1)}, u32[]{:S(2)}, u32[]{:S(2)}) collective-permute-start(bf16[384,128]{1,0:T(8,128)(2,1)S(1)} %get-tuple-element.27.refs_0_), channel_id=1, source_target_pairs={{0,1},{1,0},{2,3},{3,2},{4,5},{5,4},{6,7},{7,6},{8,9},{9,8},{10,11... | collective-permute-start | bytes 294920 | tf_op jit(solution)/shard_map/ppermute | solution.py:510
  33.7 1.4 %collective-permute-start.12 = (bf16[384,128]{1,0:T(8,128)(2,1)S(1)}, bf16[384,128]{1,0:T(8,128)(2,1)S(1)}, u32[]{:S(2)}, u32[]{:S(2)}) collective-permute-start(bf16[384,128]{1,0:T(8,128)(2,1)S(1)} %collective-permute-done.11.refs_2_), channel_id=1, source_target_pairs={{0,1},{1,0},{2,3},{3,2},{4,5},{5,4},{6,7},{7,6},{8,9},{9,8},{10,11... | collective-permute-start | bytes 294920 | tf_op jit(solution)/shard_map/ppermute | solution.py:510
  34.5 5.3 %collective-permute-start.9 = (bf16[4,96,128]{2,1,0:T(8,128)(2,1)S(1)}, bf16[4,96,128]{2,1,0:T(8,128)(2,1)S(1)}, u32[]{:S(2)}, u32[]{:S(2)}) collective-permute-start(bf16[4,96,128]{2,1,0:T(8,128)(2,1)S(1)} %finish.2), channel_id=1, source_target_pairs={{0,4},{1,5},{2,6},{3,7},{4,0},{5,1},{6,2},{7,3},{8,12},{9,13},{10,... | collective-permute-start | bytes 294920 | tf_op jit(solution)/shard_map/ppermute | solution.py:510

commit v11 on v9

--- a/solution.py
+++ b/solution.py
@@ -49,75 +49,90 @@
     return lax.broadcasted_iota(jnp.int32, shape, axis)
 
 
-def table_kernel(
-    ids_hbm,
-    live_hbm,
-    embed_hbm,
-    qkv_hbm,
-    out_ref,
-    coded_ref,
-    ids_ref,
-    live_ref,
-    embed_ref,
-    qkv_ref,
-    padded_ref,
-    sems,
-):
+def code_kernel(ids_hbm, live_hbm, out_ref, ids_ref, live_ref, sems):
+    loads = [
+        pltpu.make_async_copy(ids_hbm, ids_ref, sems.at[0]),
+        pltpu.make_async_copy(live_hbm, live_ref, sems.at[1]),
+    ]
+    for load in loads:
+        load.start()
+    for load in loads:
+        load.wait()
+    row = iota(ids_ref.shape, 0)
+    live = jnp.zeros(ids_ref.shape, jnp.int32)
+    for r in range(ids_ref.shape[0]):
+        live = jnp.where(row == r, live_ref[r], live)
+    coded = ids_ref[...] + 65536 * live
+    out_ref[...] = jnp.concatenate([coded] * (out_ref.shape[0] // coded.shape[0]), 0)
+
+
+def make_codes(ids, pad_mask, height):
+    return pl.pallas_call(
+        code_kernel,
+        out_shape=jax.ShapeDtypeStruct((height, ids.shape[1]), jnp.int32),
+        in_specs=[pl.BlockSpec(memory_space=pltpu.HBM)] * 2,
+        scratch_shapes=[
+            pltpu.VMEM(ids.shape, jnp.int32),
+            pltpu.SMEM(pad_mask.shape, jnp.int32),
+            pltpu.SemaphoreType.DMA((2,)),
+        ],
+        compiler_params=pltpu.CompilerParams(vmem_limit_bytes=SMALL_VMEM),
+        name="codes",
+    )(in_hbm(ids), in_hbm(pad_mask))
+
+
+def join_kernel(rows, own_ref, other_ref, out_ref):
+    own, other = own_ref[...], other_ref[...]
+    both = jnp.concatenate([own[0:rows], other[0:rows]], 0)
+    out_ref[...] = jnp.concatenate([both] * (own.shape[0] // (2 * rows)), 0)
+
+
+def join(own, other, rows):
+    return pl.pallas_call(
+        functools.partial(join_kernel, rows),
+        out_shape=jax.ShapeDtypeStruct(own.shape, own.dtype),
+        compiler_params=pltpu.CompilerParams(vmem_limit_bytes=SMALL_VMEM),
+        name="join",
+    )(own, other)
+
+
+def table_kernel(embed_hbm, qkv_hbm, out_ref, embed_ref, qkv_ref, padded_ref, sems):
     kinds = qkv_ref.shape[0]
-    loads = [
-        pltpu.make_async_copy(embed_hbm, embed_ref, sems.at[kinds]),
-        pltpu.make_async_copy(ids_hbm, ids_ref, sems.at[kinds + 1]),
-        pltpu.make_async_copy(live_hbm, live_ref, sems.at[kinds + 2]),
-    ]
+    loads = [pltpu.make_async_copy(embed_hbm, embed_ref, sems.at[kinds])]
     loads += [
         pltpu.make_async_copy(qkv_hbm.at[t], qkv_ref.at[t], sems.at[t]) for t in range(kinds)
     ]
     for load in loads:
         load.start()
     padded_ref[...] = jnp.zeros(padded_ref.shape, f32)
-    for load in loads[0:3]:
-        load.wait()
+    loads[0].wait()
     padded_ref[0 : embed_ref.shape[0], :] = embed_ref[...].astype(f32)
     normed = layer_norm(padded_ref[...]).astype(bf16)
-    row = iota(ids_ref.shape, 0)
-    live = jnp.zeros(ids_ref.shape, jnp.int32)
-    for r in range(ids_ref.shape[0]):
-        live = jnp.where(row == r, live_ref[r], live)
-    coded = ids_ref[...] + 65536 * live
-    for g in range(coded_ref.shape[0]):
-        coded_ref[g] = coded
     tables = []
     for t in range(kinds):
-        loads[3 + t].wait()
+        loads[1 + t].wait()
         tables.append(dot_nt(normed, qkv_ref[t]))
     out_ref[...] = jnp.concatenate(tables, 1).astype(bf16)
 
 
-def make_tables(ids, pad_mask, embed, row_qkv, groups):
+def make_tables(embed, row_qkv):
     kinds, local, width = row_qkv.shape
     return pl.pallas_call(
         table_kernel,
-        out_shape=(
-            jax.ShapeDtypeStruct((TABLE_ROWS, kinds * local), bf16),
-            jax.ShapeDtypeStruct((groups,) + ids.shape, jnp.int32),
-        ),
-        in_specs=[pl.BlockSpec(memory_space=pltpu.HBM)] * 4,
+        out_shape=jax.ShapeDtypeStruct((TABLE_ROWS, kinds * local), bf16),
+        in_specs=[pl.BlockSpec(memory_space=pltpu.HBM)] * 2,
         scratch_shapes=[
-            pltpu.VMEM(ids.shape, jnp.int32),
-            pltpu.SMEM(pad_mask.shape, jnp.int32),
             pltpu.VMEM(embed.shape, bf16),
             pltpu.VMEM(row_qkv.shape, bf16),
             pltpu.VMEM((TABLE_ROWS, width), f32),
-            pltpu.SemaphoreType.DMA((kinds + 3,)),
+            pltpu.SemaphoreType.DMA((kinds + 1,)),
         ],
         cost_estimate=pl.CostEstimate(
-            flops=2 * TABLE_ROWS * row_qkv.size,
-            bytes_accessed=2 * row_qkv.size,
-            transcendentals=0,
+            flops=2 * 10**9, bytes_accessed=2 * row_qkv.size, transcendentals=0
         ),
         compiler_params=pltpu.CompilerParams(vmem_limit_bytes=SMALL_VMEM),
         name="tables",
-    )(in_hbm(ids), in_hbm(pad_mask), in_hbm(embed), in_hbm(row_qkv))
+    )(in_hbm(embed), in_hbm(row_qkv))
 
 
 def halves(pair):
@@ -150,7 +165,8 @@
 def row_kernel(parts, *refs):
     tables_refs, refs = refs[:parts], refs[parts:]
     (
-        codes_ref,
+        near_codes_ref,
+        far_codes_ref,
         row_context_ref,
         own_ref,
         live_ref,
@@ -179,7 +195,7 @@
         )
         table_ref[t, TABLE_ROWS:CODES, :] = jnp.zeros((CODES - TABLE_ROWS, width), bf16)
 
-    coded = jnp.concatenate([codes_ref[g] for g in range(codes_ref.shape[0])], 0)
+    coded = jnp.concatenate([near_codes_ref[...], far_codes_ref[...]], 0)
     ids = (coded & 0xFFFF).astype(f32)
     live = (coded[:, 0:LANES] >> 16).astype(f32)
     live_ref[...] = live
@@ -274,7 +290,7 @@
         cost_estimate=pl.CostEstimate(flops=3 * 10**9, bytes_accessed=10**6, transcendentals=0),
         compiler_params=pltpu.CompilerParams(vmem_limit_bytes=LARGE_VMEM),
         name="row_attention",
-    )(*tables, codes)
+    )(*tables, *codes)
 
 
 def column_kernel(parts, *refs):
@@ -407,6 +423,7 @@
     col_out_ref, out_ref, weight_ref = refs[2 * parts + 2 :]
     tokens, local = mixed_refs[0].shape
     some = tokens // 2
+    group = lax.axis_index("seq")
     part = lax.axis_index("head")
     for p in range(parts):
         weight_ref[p] = col_out_ref[:, p * local : (p + 1) * local]
@@ -433,7 +450,7 @@
             for r in range(2)
         )
         rest = jnp.concatenate([first[:, LANES:local], second[:, LANES:local]], 1)
-        out_ref[d] = jnp.concatenate(
+        out_ref[group ^ d] = jnp.concatenate(
             [first[:, 0:LANES], second[:, 0:LANES], rest], 0
         ).astype(bf16)
 
@@ -500,10 +517,23 @@
         return g, p ^ 3
 
     far = pairwise(row_out, across)
-    table, codes = make_tables(ids, pad_mask, embed, row_qkv, groups)
-    tables = [table] + [pairwise(table, to) for to in (sibling, across, opposite)]
-    codes = lax.all_to_all(codes, "seq", split_axis=0, concat_axis=0, tiled=True)
-    codes, near, far = lax.optimization_barrier((codes, row_out, far))
+    coded = make_codes(ids, pad_mask, rows_here * groups // 2)
+    coded, row_qkv = lax.optimization_barrier((coded, row_qkv))
+    received = pairwise(coded, lambda g, p: (g ^ 1, p))
+    table = make_tables(embed, row_qkv)
+    step = 2
+    while step < groups:
+        coded = join(coded, received, rows_here * step // 2)
+        if step == 2:
+            coded, table = lax.optimization_barrier((coded, table))
+            far_tables = [pairwise(table, to) for to in (across, opposite)]
+        received = pairwise(coded, lambda g, p, step=step: (g ^ step, p))
+        step *= 2
+    codes = (coded, received)
+    coded, late_table = lax.optimization_barrier((coded, table))
+    codes = (coded, received)
+    tables = [table, pairwise(late_table, sibling)] + far_tables
+    *codes, near, far = lax.optimization_barrier((*codes, row_out, far))
     row_outs = [row_out, pairwise(near, sibling), far, pairwise(far, sibling)]
     row_context, own_codes, live = attend_rows(tables, codes, rows, cols, own, width)
     *halves_here, mixed_low, mixed_high = attend_columns_here(
@@ -606,7 +636,8 @@
     local = row_out.shape[0]
     fits = (
         parts == 4
-        and groups % 2 == 0
+        and groups >= 4
+        and groups & (groups - 1) == 0
         and rows * 8 == LANES
         and rows_here == 2
         and own % 32 == 0

time: 47.3 us -> 47.1 us (level)
  blocking collectives: 23.1 us -> 13.9 us
  starting transfers between devices: 8.03 us -> 12.5 us
  waiting for transfers between devices: 5.83 us -> 9.57 us
  Pallas kernels: 9.95 us -> 10.7 us
    all_to_all x1 -> x0, blocking collectives: 12.2 us -> none  [fast_body(): lax.all_to_all(codes, 'seq', split_axis=0, concat_axis=0, tiled=True)]
    ppermute x12 -> x15, starting transfers between devices: 8.03 us -> 12.5 us  [pairwise(): lax.ppermute(value, ('seq', 'head'), [(i, g * parts + p) for i, (g, p) in...]
    ppermute x12 -> x15, waiting for transfers between devices: 5.83 us -> 9.57 us  [pairwise(): lax.ppermute(value, ('seq', 'head'), [(i, g * parts + p) for i, (g, p) in...]
    all_to_all x1, blocking collectives: 11 us -> 13.9 us  [fast_body(): lax.all_to_all(blocks, 'seq', split_axis=0, concat_axis=0, tiled=True)]
    pallas_call x1 -> x4, Pallas kernels: 1.87 us -> 2.67 us  [the longest x1 1.84 us: make_tables(): pl.pallas_call(table_kernel, out_shape=jax.ShapeDtypeStruct((TABLE_ROWS,...]
  transfers between devices with their start and end apart: 12 -> 15, of which waited for: 3 -> 6; matrix products, arithmetic and copies ran while one was open for 0% -> 0% of each run, Pallas kernels for 10% -> 12%
where the time goes in v11:
time: 47.1 us; the launch traced here: 46.9 us
  blocking collectives  13.9 us (30%)
  starting transfers between devices  12.5 us (27%)
  Pallas kernels  10.7 us (23%)
  waiting for transfers between devices  9.57 us (20%)
    all_to_all x1, blocking collectives, fast_body(): lax.all_to_all(blocks, 'seq', split_axis=0, concat_axis=0, tiled=True)  13.9 us
    ppermute x15, starting transfers between devices, pairwise(): lax.ppermute(value, ('seq', 'head'), [(i, g * parts + p) for i, (g, p) in...  12.5 us
    ppermute x15, waiting for transfers between devices, pairwise(): lax.ppermute(value, ('seq', 'head'), [(i, g * parts + p) for i, (g, p) in...  9.57 us
    pallas_call x1, Pallas kernels, attend_columns_here(): pl.pallas_call(functools.partial(column_kernel, parts), out_shape=(*[jax....  3.33 us
    pallas_call x1, Pallas kernels, attend_rows(): pl.pallas_call(functools.partial(row_kernel, parts), out_shape=(jax.Shape...  2.82 us
    pallas_call x1, Pallas kernels, make_tables(): pl.pallas_call(table_kernel, out_shape=jax.ShapeDtypeStruct((TABLE_ROWS,...  1.84 us
    pallas_call x1, Pallas kernels, finish(): pl.pallas_call(functools.partial(finish_kernel, parts, groups), out_shape...  1.1 us
  transfers between devices with their start and end apart: 15, of which 6 were waited for; matrix products, arithmetic and copies ran while one was open for 0% of the time, Pallas kernels for 12%

profile of v11, /device:TPU:0, one launch (start us, length us, event | category | flops | bytes accessed | tf_op | source)
XLA Modules:
  0.0 46.9 jit_solution(11715653772027636814)
XLA Ops:
  0.0 2.9 %collective-permute-start.3 = (bf16[192,768]{1,0:T(8,128)(2,1)}, bf16[192,768]{1,0:T(8,128)(2,1)S(1)}, u32[]{:S(2)}, u32[]{:S(2)}) collective-permute-start(bf16[192,768]{1,0:T(8,128)(2,1)} %refs_0_.1), channel_id=1, source_target_pairs={{0,2},{1,3},{2,0},{3,1},{4,6},{5,7},{6,4},{7,5},{8,10},{9,11},{10,... | collective-permute-start | bytes 884744 | tf_op jit(solution)/shard_map/ppermute | solution.py:508
  2.9 0.8 %codes.1.own_ref = s32[8,256]{1,0:T(8,128)S(1)} custom-call(s32[2,256]{1,0:T(2,128)} %ids_hbm.1, s32[2]{0:T(128)} %live_hbm.1), custom_call_target="tpu_custom_call" | custom-call | tf_op jit(solution)/shard_map/codes/pallas_call | solution.py:70
  3.8 0.0 copy-start.2
  3.8 1.6 %collective-permute-start = (s32[8,256]{1,0:T(8,128)S(1)}, s32[8,256]{1,0:T(8,128)S(1)}, u32[]{:S(2)}, u32[]{:S(2)}) collective-permute-start(s32[8,256]{1,0:T(8,128)S(1)} %codes.1.own_ref), channel_id=1, source_target_pairs={{0,4},{1,5},{2,6},{3,7},{4,0},{5,1},{6,2},{7,3},{8,12},{9,13},{10,... | collective-permute-start | bytes 24584 | tf_op jit(solution)/shard_map/ppermute | solution.py:508
  5.4 1.8 %tables.1.refs_0_ = bf16[40,576]{1,0:T(8,128)(2,1)S(1)} custom-call(bf16[33,768]{1,0:T(8,128)(2,1)} %refs_7_.1, bf16[3,192,768]{2,1,0:T(8,128)(2,1)} %qkv_hbm), custom_call_target="tpu_custom_call" | custom-call | flops 2000000000 | bytes 884736 | tf_op jit(solution)/shard_map/tables/pallas_call | solution.py:120
  7.2 0.3 collective-permute-done.other_ref
  7.5 1.6 %collective-permute-start.1 = (s32[8,256]{1,0:T(8,128)S(1)}, s32[8,256]{1,0:T(8,128)S(1)}, u32[]{:S(2)}, u32[]{:S(2)}) collective-permute-start(s32[8,256]{1,0:T(8,128)S(1)} %join.2.own_ref), channel_id=1, source_target_pairs={{0,8},{1,9},{2,10},{3,11},{4,12},{5,13},{6,14},{7,15},{8,0},{9,1},... | collective-permute-start | bytes 24584 | tf_op jit(solution)/shard_map/ppermute | solution.py:508
  9.1 0.0 collective-permute-start.8
  9.1 0.6 %collective-permute-start.7 = (bf16[40,576]{1,0:T(8,128)(2,1)S(1)}, bf16[40,576]{1,0:T(8,128)(2,1)S(1)}, u32[]{:S(2)}, u32[]{:S(2)}) collective-permute-start(bf16[40,576]{1,0:T(8,128)(2,1)S(1)} %tables.1.refs_0_), channel_id=1, source_target_pairs={{0,2},{1,3},{2,0},{3,1},{4,6},{5,7},{6,4},{7,5},{8,10},{9,11},{10,... | collective-permute-start | bytes 138248 | tf_op jit(solution)/shard_map/ppermute | solution.py:508
  9.7 1.5 %collective-permute-done.1.other_ref = s32[8,256]{1,0:T(8,128)S(1)} collective-permute-done((s32[8,256]{1,0:T(8,128)S(1)}, s32[8,256]{1,0:T(8,128)S(1)}, u32[]{:S(2)}, u32[]{:S(2)}) %collective-permute-start.1) | collective-permute-done | bytes 8224 | tf_op jit(solution)/shard_map/ppermute | solution.py:508
  11.2 0.0 copy-start.1
  11.2 0.0 copy-start.3
  11.2 0.1 collective-permute-start.6
  11.2 2.7 %collective-permute-start.2 = (s32[8,256]{1,0:T(8,128)S(1)}, s32[8,256]{1,0:T(8,128)S(1)}, u32[]{:S(2)}, u32[]{:S(2)}) collective-permute-start(s32[8,256]{1,0:T(8,128)S(1)} %join.3.refs_4_), channel_id=1, source_target_pairs={{0,16},{1,17},{2,18},{3,19},{4,20},{5,21},{6,22},{7,23},{8,24},{9,... | collective-permute-start | bytes 24584 | tf_op jit(solution)/shard_map/ppermute | solution.py:508
  13.9 2.0 %collective-permute-done.2.refs_5_ = s32[8,256]{1,0:T(8,128)S(1)} collective-permute-done((s32[8,256]{1,0:T(8,128)S(1)}, s32[8,256]{1,0:T(8,128)S(1)}, u32[]{:S(2)}, u32[]{:S(2)}) %collective-permute-start.2) | collective-permute-done | bytes 8224 | tf_op jit(solution)/shard_map/ppermute | solution.py:508
  15.9 0.0 collective-permute-done.3.refs_2_
  15.9 0.0 copy-done.2
  15.9 0.0 collective-permute-start.4
  15.9 0.5 %collective-permute-start.5 = (bf16[192,768]{1,0:T(8,128)(2,1)S(1)}, bf16[192,768]{1,0:T(8,128)(2,1)S(1)}, u32[]{:S(2)}, u32[]{:S(2)}) collective-permute-start(bf16[192,768]{1,0:T(8,128)(2,1)S(1)} %collective-permute-done.3.refs_2_), channel_id=1, source_target_pairs={{0,1},{1,0},{2,3},{3,2},{4,5},{5,4},{6,7},{7,6},{8,9},{9,8},{10,11... | collective-permute-start | bytes 884744 | tf_op jit(solution)/shard_map/ppermute | solution.py:508
  16.4 0.0 collective-permute-done.8.refs_3_
  16.4 0.0 collective-permute-done.7.refs_2_
  16.4 0.0 collective-permute-done.6.refs_1_
  16.4 2.8 %row_attention.1 = (bf16[512,768]{1,0:T(8,128)(2,1)S(1)}, bf16[256,128]{1,0:T(8,128)(2,1)S(1)}, f32[16,128]{1,0:T(8,128)S(1)}) custom-call(bf16[40,576]{1,0:T(8,128)(2,1)S(1)} %tables.1.refs_0_, bf16[40,576]{1,0:T(8,128)(2,1)S(1)} %collective-permute-done.6.refs_1_, bf16[40,576]{1,0:T(8,128)(2,1)S(1)} %collective-permute-done.7.refs_2_, ...), custom_call_target="tpu_custom_call" | custom-call | flops 3000000000 | bytes 1000000 | tf_op jit(solution)/shard_map/row_attention/pallas_call | solution.py:275
  19.2 0.0 collective-permute-done.4.refs_1_
  19.2 0.0 collective-permute-done.5.refs_3_
  19.2 0.0 copy-done.1
  19.3 0.0 copy-done.3
  19.3 0.0 copy-start
  19.3 3.3 %column_attention.1 = (bf16[384,128]{1,0:T(8,128)(2,1)S(1)}, bf16[384,128]{1,0:T(8,128)(2,1)S(1)}, f32[256,192]{1,0:T(8,128)S(1)}, f32[256,192]{1,0:T(8,128)S(1)}) custom-call(bf16[192,768]{1,0:T(8,128)(2,1)S(1)} %copy-done.2, bf16[192,768]{1,0:T(8,128)(2,1)S(1)} %collective-permute-done.4.refs_1_, bf16[192,768]{1,0:T(8,128)(2,1)S(1)} %collective-permute-done.3.refs_2_, ...), custom_call_target="tpu_custom_call" | custom-call | flops 2000000000 | bytes 1000000 | tf_op jit(solution)/shard_map/column_attention/pallas_call | solution.py:404
  22.6 0.4 collective-permute-start.10
  23.0 1.7 %collective-permute-start.13 = (bf16[384,128]{1,0:T(8,128)(2,1)S(1)}, bf16[384,128]{1,0:T(8,128)(2,1)S(1)}, u32[]{:S(2)}, u32[]{:S(2)}) collective-permute-start(bf16[384,128]{1,0:T(8,128)(2,1)S(1)} %get-tuple-element.36.refs_4_), channel_id=1, source_target_pairs={{0,2},{1,3},{2,0},{3,1},{4,6},{5,7},{6,4},{7,5},{8,10},{9,11},{10,... | collective-permute-start | bytes 294920 | tf_op jit(solution)/shard_map/ppermute | solution.py:508
  24.7 0.0 collective-permute-start.9
  24.7 0.5 %collective-permute-start.12 = (bf16[384,128]{1,0:T(8,128)(2,1)S(1)}, bf16[384,128]{1,0:T(8,128)(2,1)S(1)}, u32[]{:S(2)}, u32[]{:S(2)}) collective-permute-start(bf16[384,128]{1,0:T(8,128)(2,1)S(1)} %get-tuple-element.36.refs_4_), channel_id=1, source_target_pairs={{0,1},{1,0},{2,3},{3,2},{4,5},{5,4},{6,7},{7,6},{8,9},{9,8},{10,11... | collective-permute-start | bytes 294920 | tf_op jit(solution)/shard_map/ppermute | solution.py:508
  25.2 3.1 %collective-permute-done.10.refs_2_ = bf16[384,128]{1,0:T(8,128)(2,1)S(1)} collective-permute-done((bf16[384,128]{1,0:T(8,128)(2,1)S(1)}, bf16[384,128]{1,0:T(8,128)(2,1)S(1)}, u32[]{:S(2)}, u32[]{:S(2)}) %collective-permute-start.10) | collective-permute-done | bytes 98336 | tf_op jit(solution)/shard_map/ppermute | solution.py:508
  28.3 0.0 collective-permute-start.11
  28.3 1.4 %collective-permute-done.13.refs_6_ = bf16[384,128]{1,0:T(8,128)(2,1)S(1)} collective-permute-done((bf16[384,128]{1,0:T(8,128)(2,1)S(1)}, bf16[384,128]{1,0:T(8,128)(2,1)S(1)}, u32[]{:S(2)}, u32[]{:S(2)}) %collective-permute-start.13) | collective-permute-done | bytes 98336 | tf_op jit(solution)/shard_map/ppermute | solution.py:508
  29.7 0.0 collective-permute-start.14
  29.7 0.0 collective-permute-done.9.refs_1_
  29.7 0.0 collective-permute-done.12.refs_5_
  29.7 0.0 collective-permute-done.11.refs_3_
  29.8 1.3 %collective-permute-done.14.refs_7_ = bf16[384,128]{1,0:T(8,128)(2,1)S(1)} collective-permute-done((bf16[384,128]{1,0:T(8,128)(2,1)S(1)}, bf16[384,128]{1,0:T(8,128)(2,1)S(1)}, u32[]{:S(2)}, u32[]{:S(2)}) %collective-permute-start.14) | collective-permute-done | bytes 98336 | tf_op jit(solution)/shard_map/ppermute | solution.py:508
  31.0 0.0 copy-done
  31.0 1.1 %finish.1 = bf16[8,96,128]{2,1,0:T(8,128)(2,1)S(1)} custom-call(bf16[384,128]{1,0:T(8,128)(2,1)S(1)} %get-tuple-element.35.refs_0_, bf16[384,128]{1,0:T(8,128)(2,1)S(1)} %collective-permute-done.9.refs_1_, bf16[384,128]{1,0:T(8,128)(2,1)S(1)} %collective-permute-done.10.refs_2_, bf16[384,128]{1,0:T(8,128)(2,1)S(1)} %collective-permute-done.11.refs_3_, ...), custom_call_target="tpu_custom_call" | custom-call | tf_op jit(solution)/shard_map/finish/pallas_call | solution.py:461
  32.1 13.9 %all_to_all.5.blocks_ref = bf16[8,96,128]{2,1,0:T(8,128)(2,1)S(1)} all-to-all(bf16[8,96,128]{2,1,0:T(8,128)(2,1)S(1)} %finish.1), channel_id=1, replica_groups=mesh['seq'=8,'head'=4] {'seq'}, dimensions={0} | all-to-all | bytes 393216 | tf_op jit(solution)/shard_map/all_to_all | solution.py:549
  46.1 0.8 %order.1 = bf16[2,192,256]{2,1,0:T(8,128)(2,1)} custom-call(bf16[8,96,128]{2,1,0:T(8,128)(2,1)S(1)} %all_to_all.5.blocks_ref), custom_call_target="tpu_custom_call" | custom-call | tf_op jit(solution)/shard_map/order/pallas_call | solution.py:490
  (2 shorter events, 0.0 us)
Async XLA Ops:
  0.0 15.9 %collective-permute-start.3 = (bf16[192,768]{1,0:T(8,128)(2,1)}, bf16[192,768]{1,0:T(8,128)(2,1)S(1)}, u32[]{:S(2)}, u32[]{:S(2)}) collective-permute-start(bf16[192,768]{1,0:T(8,128)(2,1)} %refs_0_.1), channel_id=1, source_target_pairs={{0,2},{1,3},{2,0},{3,1},{4,6},{5,7},{6,4},{7,5},{8,10},{9,11},{10,... | collective-permute-start | bytes 884744 | tf_op jit(solution)/shard_map/ppermute | solution.py:508
  3.8 12.1 %copy-start.2 = (bf16[192,768]{1,0:T(8,128)(2,1)S(1)}, bf16[192,768]{1,0:T(8,128)(2,1)}, u32[]{:S(2)}) copy-start(bf16[192,768]{1,0:T(8,128)(2,1)} %refs_0_.1) | copy-start | bytes 884740
  3.8 3.7 %collective-permute-start = (s32[8,256]{1,0:T(8,128)S(1)}, s32[8,256]{1,0:T(8,128)S(1)}, u32[]{:S(2)}, u32[]{:S(2)}) collective-permute-start(s32[8,256]{1,0:T(8,128)S(1)} %codes.1.own_ref), channel_id=1, source_target_pairs={{0,4},{1,5},{2,6},{3,7},{4,0},{5,1},{6,2},{7,3},{8,12},{9,13},{10,... | collective-permute-start | bytes 24584 | tf_op jit(solution)/shard_map/ppermute | solution.py:508
  7.5 3.7 %collective-permute-start.1 = (s32[8,256]{1,0:T(8,128)S(1)}, s32[8,256]{1,0:T(8,128)S(1)}, u32[]{:S(2)}, u32[]{:S(2)}) collective-permute-start(s32[8,256]{1,0:T(8,128)S(1)} %join.2.own_ref), channel_id=1, source_target_pairs={{0,8},{1,9},{2,10},{3,11},{4,12},{5,13},{6,14},{7,15},{8,0},{9,1},... | collective-permute-start | bytes 24584 | tf_op jit(solution)/shard_map/ppermute | solution.py:508
  9.1 7.3 %collective-permute-start.8 = (bf16[40,576]{1,0:T(8,128)(2,1)S(1)}, bf16[40,576]{1,0:T(8,128)(2,1)S(1)}, u32[]{:S(2)}, u32[]{:S(2)}) collective-permute-start(bf16[40,576]{1,0:T(8,128)(2,1)S(1)} %tables.1.refs_0_), channel_id=1, source_target_pairs={{0,3},{1,2},{2,1},{3,0},{4,7},{5,6},{6,5},{7,4},{8,11},{9,10},{10,... | collective-permute-start | bytes 138248 | tf_op jit(solution)/shard_map/ppermute | solution.py:508
  9.1 7.3 %collective-permute-start.7 = (bf16[40,576]{1,0:T(8,128)(2,1)S(1)}, bf16[40,576]{1,0:T(8,128)(2,1)S(1)}, u32[]{:S(2)}, u32[]{:S(2)}) collective-permute-start(bf16[40,576]{1,0:T(8,128)(2,1)S(1)} %tables.1.refs_0_), channel_id=1, source_target_pairs={{0,2},{1,3},{2,0},{3,1},{4,6},{5,7},{6,4},{7,5},{8,10},{9,11},{10,... | collective-permute-start | bytes 138248 | tf_op jit(solution)/shard_map/ppermute | solution.py:508
  11.2 8.1 %copy-start.1 = (bf16[3,192,768]{2,1,0:T(8,128)(2,1)S(1)}, bf16[3,192,768]{2,1,0:T(8,128)(2,1)}, u32[]{:S(2)}) copy-start(bf16[3,192,768]{2,1,0:T(8,128)(2,1)} %param.12) | copy-start | bytes 2654212
  11.2 8.1 %copy-start.3 = (bf16[33,768]{1,0:T(8,128)(2,1)S(1)}, bf16[33,768]{1,0:T(8,128)(2,1)}, u32[]{:S(2)}) copy-start(bf16[33,768]{1,0:T(8,128)(2,1)} %refs_7_.1) | copy-start | bytes 152068
  11.2 5.2 %collective-permute-start.6 = (bf16[40,576]{1,0:T(8,128)(2,1)S(1)}, bf16[40,576]{1,0:T(8,128)(2,1)S(1)}, u32[]{:S(2)}, u32[]{:S(2)}) collective-permute-start(bf16[40,576]{1,0:T(8,128)(2,1)S(1)} %tables.1.refs_0_), channel_id=1, source_target_pairs={{0,1},{1,0},{2,3},{3,2},{4,5},{5,4},{6,7},{7,6},{8,9},{9,8},{10,11... | collective-permute-start | bytes 138248 | tf_op jit(solution)/shard_map/ppermute | solution.py:508
  11.2 4.6 %collective-permute-start.2 = (s32[8,256]{1,0:T(8,128)S(1)}, s32[8,256]{1,0:T(8,128)S(1)}, u32[]{:S(2)}, u32[]{:S(2)}) collective-permute-start(s32[8,256]{1,0:T(8,128)S(1)} %join.3.refs_4_), channel_id=1, source_target_pairs={{0,16},{1,17},{2,18},{3,19},{4,20},{5,21},{6,22},{7,23},{8,24},{9,... | collective-permute-start | bytes 24584 | tf_op jit(solution)/shard_map/ppermute | solution.py:508
  15.9 3.4 %collective-permute-start.4 = (bf16[192,768]{1,0:T(8,128)(2,1)S(1)}, bf16[192,768]{1,0:T(8,128)(2,1)S(1)}, u32[]{:S(2)}, u32[]{:S(2)}) collective-permute-start(bf16[192,768]{1,0:T(8,128)(2,1)S(1)} %copy-done.2), channel_id=1, source_target_pairs={{0,1},{1,0},{2,3},{3,2},{4,5},{5,4},{6,7},{7,6},{8,9},{9,8},{10,11... | collective-permute-start | bytes 884744 | tf_op jit(solution)/shard_map/ppermute | solution.py:508
  15.9 3.4 %collective-permute-start.5 = (bf16[192,768]{1,0:T(8,128)(2,1)S(1)}, bf16[192,768]{1,0:T(8,128)(2,1)S(1)}, u32[]{:S(2)}, u32[]{:S(2)}) collective-permute-start(bf16[192,768]{1,0:T(8,128)(2,1)S(1)} %collective-permute-done.3.refs_2_), channel_id=1, source_target_pairs={{0,1},{1,0},{2,3},{3,2},{4,5},{5,4},{6,7},{7,6},{8,9},{9,8},{10,11... | collective-permute-start | bytes 884744 | tf_op jit(solution)/shard_map/ppermute | solution.py:508
  19.3 11.8 %copy-start = (bf16[192,768]{1,0:T(8,128)(2,1)S(1)}, bf16[192,768]{1,0:T(8,128)(2,1)}, u32[]{:S(2)}) copy-start(bf16[192,768]{1,0:T(8,128)(2,1)} %refs_10_.1) | copy-start | bytes 884740
  22.6 5.7 %collective-permute-start.10 = (bf16[384,128]{1,0:T(8,128)(2,1)S(1)}, bf16[384,128]{1,0:T(8,128)(2,1)S(1)}, u32[]{:S(2)}, u32[]{:S(2)}) collective-permute-start(bf16[384,128]{1,0:T(8,128)(2,1)S(1)} %get-tuple-element.35.refs_0_), channel_id=1, source_target_pairs={{0,2},{1,3},{2,0},{3,1},{4,6},{5,7},{6,4},{7,5},{8,10},{9,11},{10,... | collective-permute-start | bytes 294920 | tf_op jit(solution)/shard_map/ppermute | solution.py:508
  23.0 6.7 %collective-permute-start.13 = (bf16[384,128]{1,0:T(8,128)(2,1)S(1)}, bf16[384,128]{1,0:T(8,128)(2,1)S(1)}, u32[]{:S(2)}, u32[]{:S(2)}) collective-permute-start(bf16[384,128]{1,0:T(8,128)(2,1)S(1)} %get-tuple-element.36.refs_4_), channel_id=1, source_target_pairs={{0,2},{1,3},{2,0},{3,1},{4,6},{5,7},{6,4},{7,5},{8,10},{9,11},{10,... | collective-permute-start | bytes 294920 | tf_op jit(solution)/shard_map/ppermute | solution.py:508
  24.7 5.0 %collective-permute-start.9 = (bf16[384,128]{1,0:T(8,128)(2,1)S(1)}, bf16[384,128]{1,0:T(8,128)(2,1)S(1)}, u32[]{:S(2)}, u32[]{:S(2)}) collective-permute-start(bf16[384,128]{1,0:T(8,128)(2,1)S(1)} %get-tuple-element.35.refs_0_), channel_id=1, source_target_pairs={{0,1},{1,0},{2,3},{3,2},{4,5},{5,4},{6,7},{7,6},{8,9},{9,8},{10,11... | collective-permute-start | bytes 294920 | tf_op jit(solution)/shard_map/ppermute | solution.py:508
  24.7 5.0 %collective-permute-start.12 = (bf16[384,128]{1,0:T(8,128)(2,1)S(1)}, bf16[384,128]{1,0:T(8,128)(2,1)S(1)}, u32[]{:S(2)}, u32[]{:S(2)}) collective-permute-start(bf16[384,128]{1,0:T(8,128)(2,1)S(1)} %get-tuple-element.36.refs_4_), channel_id=1, source_target_pairs={{0,1},{1,0},{2,3},{3,2},{4,5},{5,4},{6,7},{7,6},{8,9},{9,8},{10,11... | collective-permute-start | bytes 294920 | tf_op jit(solution)/shard_map/ppermute | solution.py:508
  28.3 1.4 %collective-permute-start.11 = (bf16[384,128]{1,0:T(8,128)(2,1)S(1)}, bf16[384,128]{1,0:T(8,128)(2,1)S(1)}, u32[]{:S(2)}, u32[]{:S(2)}) collective-permute-start(bf16[384,128]{1,0:T(8,128)(2,1)S(1)} %collective-permute-done.10.refs_2_), channel_id=1, source_target_pairs={{0,1},{1,0},{2,3},{3,2},{4,5},{5,4},{6,7},{7,6},{8,9},{9,8},{10,11... | collective-permute-start | bytes 294920 | tf_op jit(solution)/shard_map/ppermute | solution.py:508
  29.7 1.3 %collective-permute-start.14 = (bf16[384,128]{1,0:T(8,128)(2,1)S(1)}, bf16[384,128]{1,0:T(8,128)(2,1)S(1)}, u32[]{:S(2)}, u32[]{:S(2)}) collective-permute-start(bf16[384,128]{1,0:T(8,128)(2,1)S(1)} %collective-permute-done.13.refs_6_), channel_id=1, source_target_pairs={{0,1},{1,0},{2,3},{3,2},{4,5},{5,4},{6,7},{7,6},{8,9},{9,8},{10,11... | collective-permute-start | bytes 294920 | tf_op jit(solution)/shard_map/ppermute | solution.py:508

commit v12 on v11

--- a/solution.py
+++ b/solution.py
@@ -97,10 +97,17 @@
 
 
 def table_kernel(embed_hbm, qkv_hbm, out_ref, embed_ref, qkv_ref, padded_ref, sems):
-    kinds = qkv_ref.shape[0]
-    loads = [pltpu.make_async_copy(embed_hbm, embed_ref, sems.at[kinds])]
+    kinds, local = qkv_ref.shape[0:2]
+    cut = local // 2
+    loads = [pltpu.make_async_copy(embed_hbm, embed_ref, sems.at[2 * kinds])]
     loads += [
-        pltpu.make_async_copy(qkv_hbm.at[t], qkv_ref.at[t], sems.at[t]) for t in range(kinds)
+        pltpu.make_async_copy(
+            qkv_hbm.at[t, half * cut : (half + 1) * cut],
+            qkv_ref.at[t, half * cut : (half + 1) * cut],
+            sems.at[2 * t + half],
+        )
+        for t in range(kinds)
+        for half in range(2)
     ]
     for load in loads:
         load.start()
@@ -110,7 +117,8 @@
     normed = layer_norm(padded_ref[...]).astype(bf16)
     tables = []
     for t in range(kinds):
-        loads[1 + t].wait()
+        loads[1 + 2 * t].wait()
+        loads[2 + 2 * t].wait()
         tables.append(dot_nt(normed, qkv_ref[t]))
     out_ref[...] = jnp.concatenate(tables, 1).astype(bf16)
 
@@ -125,7 +133,7 @@
             pltpu.VMEM(embed.shape, bf16),
             pltpu.VMEM(row_qkv.shape, bf16),
             pltpu.VMEM((TABLE_ROWS, width), f32),
-            pltpu.SemaphoreType.DMA((kinds + 1,)),
+            pltpu.SemaphoreType.DMA((2 * kinds + 1,)),
         ],
         cost_estimate=pl.CostEstimate(
             flops=2 * 10**9, bytes_accessed=2 * row_qkv.size, transcendentals=0
@@ -516,16 +524,17 @@
     def opposite(g, p):
         return g, p ^ 3
 
+    coded = make_codes(ids, pad_mask, rows_here * groups // 2)
+    coded, row_qkv, row_out = lax.optimization_barrier((coded, row_qkv, row_out))
+    received = pairwise(coded, lambda g, p: (g ^ 1, p))
     far = pairwise(row_out, across)
-    coded = make_codes(ids, pad_mask, rows_here * groups // 2)
-    coded, row_qkv = lax.optimization_barrier((coded, row_qkv))
-    received = pairwise(coded, lambda g, p: (g ^ 1, p))
+    near = pairwise(row_out, sibling)
     table = make_tables(embed, row_qkv)
     step = 2
     while step < groups:
         coded = join(coded, received, rows_here * step // 2)
         if step == 2:
-            coded, table = lax.optimization_barrier((coded, table))
+            coded, table, near = lax.optimization_barrier((coded, table, near))
             far_tables = [pairwise(table, to) for to in (across, opposite)]
         received = pairwise(coded, lambda g, p, step=step: (g ^ step, p))
         step *= 2
@@ -533,8 +542,8 @@
     coded, late_table = lax.optimization_barrier((coded, table))
     codes = (coded, received)
     tables = [table, pairwise(late_table, sibling)] + far_tables
-    *codes, near, far = lax.optimization_barrier((*codes, row_out, far))
-    row_outs = [row_out, pairwise(near, sibling), far, pairwise(far, sibling)]
+    *codes, far = lax.optimization_barrier((*codes, far))
+    row_outs = [row_out, near, far, pairwise(far, sibling)]
     row_context, own_codes, live = attend_rows(tables, codes, rows, cols, own, width)
     *halves_here, mixed_low, mixed_high = attend_columns_here(
         row_outs, live, row_context, own_codes, embed, col_qkv.reshape(3 * local, width)

time: 47.1 us -> 47.1 us (level)
  transfers between devices with their start and end apart: 15 -> 15, of which waited for: 6 -> 6; matrix products, arithmetic and copies ran while one was open for 0% -> 0% of each run, Pallas kernels for 12% -> 10%
where the time goes in v12:
time: 47.1 us; the launch traced here: 46.9 us
  blocking collectives  13.9 us (30%)
  starting transfers between devices  12.6 us (27%)
  Pallas kernels  10.8 us (23%)
  waiting for transfers between devices  9.52 us (20%)
    all_to_all x1, blocking collectives, fast_body(): lax.all_to_all(blocks, 'seq', split_axis=0, concat_axis=0, tiled=True)  13.9 us
    ppermute x15, starting transfers between devices, pairwise(): lax.ppermute(value, ('seq', 'head'), [(i, g * parts + p) for i, (g, p) in...  12.6 us
    ppermute x15, waiting for transfers between devices, pairwise(): lax.ppermute(value, ('seq', 'head'), [(i, g * parts + p) for i, (g, p) in...  9.52 us
    pallas_call x1, Pallas kernels, attend_columns_here(): pl.pallas_call(functools.partial(column_kernel, parts), out_shape=(*[jax....  3.33 us
    pallas_call x1, Pallas kernels, attend_rows(): pl.pallas_call(functools.partial(row_kernel, parts), out_shape=(jax.Shape...  2.83 us
    pallas_call x1, Pallas kernels, make_tables(): pl.pallas_call(table_kernel, out_shape=jax.ShapeDtypeStruct((TABLE_ROWS,...  1.87 us
    pallas_call x1, Pallas kernels, finish(): pl.pallas_call(functools.partial(finish_kernel, parts, groups), out_shape...  1.1 us
  transfers between devices with their start and end apart: 15, of which 6 were waited for; matrix products, arithmetic and copies ran while one was open for 0% of the time, Pallas kernels for 10%

profile of v12, /device:TPU:0, one launch (start us, length us, event | category | flops | bytes accessed | tf_op | source)
XLA Modules:
  0.0 46.9 jit_solution(15739270912722726086)
XLA Ops:
  0.0 0.8 %codes.1.own_ref = s32[8,256]{1,0:T(8,128)S(1)} custom-call(s32[2,256]{1,0:T(2,128)} %ids_hbm.1, s32[2]{0:T(128)} %live_hbm.1), custom_call_target="tpu_custom_call" | custom-call | tf_op jit(solution)/shard_map/codes/pallas_call | solution.py:70
  0.8 0.5 %collective-permute-start.1 = (bf16[192,768]{1,0:T(8,128)(2,1)}, bf16[192,768]{1,0:T(8,128)(2,1)S(1)}, u32[]{:S(2)}, u32[]{:S(2)}) collective-permute-start(bf16[192,768]{1,0:T(8,128)(2,1)} %refs_0_), channel_id=1, source_target_pairs={{0,1},{1,0},{2,3},{3,2},{4,5},{5,4},{6,7},{7,6},{8,9},{9,8},{10,11... | collective-permute-start | bytes 884744 | tf_op jit(solution)/shard_map/ppermute | solution.py:516
  1.4 2.6 %collective-permute-start.4 = (bf16[192,768]{1,0:T(8,128)(2,1)}, bf16[192,768]{1,0:T(8,128)(2,1)S(1)}, u32[]{:S(2)}, u32[]{:S(2)}) collective-permute-start(bf16[192,768]{1,0:T(8,128)(2,1)} %refs_0_), channel_id=1, source_target_pairs={{0,2},{1,3},{2,0},{3,1},{4,6},{5,7},{6,4},{7,5},{8,10},{9,11},{10,... | collective-permute-start | bytes 884744 | tf_op jit(solution)/shard_map/ppermute | solution.py:516
  3.9 1.5 %collective-permute-start = (s32[8,256]{1,0:T(8,128)S(1)}, s32[8,256]{1,0:T(8,128)S(1)}, u32[]{:S(2)}, u32[]{:S(2)}) collective-permute-start(s32[8,256]{1,0:T(8,128)S(1)} %codes.1.own_ref), channel_id=1, source_target_pairs={{0,4},{1,5},{2,6},{3,7},{4,0},{5,1},{6,2},{7,3},{8,12},{9,13},{10,... | collective-permute-start | bytes 24584 | tf_op jit(solution)/shard_map/ppermute | solution.py:516
  5.4 1.9 %tables.1.refs_0_ = bf16[40,576]{1,0:T(8,128)(2,1)S(1)} custom-call(bf16[33,768]{1,0:T(8,128)(2,1)} %refs_7_.1, bf16[3,192,768]{2,1,0:T(8,128)(2,1)} %qkv_hbm), custom_call_target="tpu_custom_call" | custom-call | flops 2000000000 | bytes 884736 | tf_op jit(solution)/shard_map/tables/pallas_call | solution.py:128
  7.3 0.3 collective-permute-done.other_ref
  7.6 0.0 collective-permute-done.1.refs_1_
  7.6 1.6 %collective-permute-start.2 = (s32[8,256]{1,0:T(8,128)S(1)}, s32[8,256]{1,0:T(8,128)S(1)}, u32[]{:S(2)}, u32[]{:S(2)}) collective-permute-start(s32[8,256]{1,0:T(8,128)S(1)} %join.2.own_ref), channel_id=1, source_target_pairs={{0,8},{1,9},{2,10},{3,11},{4,12},{5,13},{6,14},{7,15},{8,0},{9,1},... | collective-permute-start | bytes 24584 | tf_op jit(solution)/shard_map/ppermute | solution.py:516
  9.2 0.0 collective-permute-start.8
  9.2 1.0 %collective-permute-start.7 = (bf16[40,576]{1,0:T(8,128)(2,1)S(1)}, bf16[40,576]{1,0:T(8,128)(2,1)S(1)}, u32[]{:S(2)}, u32[]{:S(2)}) collective-permute-start(bf16[40,576]{1,0:T(8,128)(2,1)S(1)} %tables.1.refs_0_), channel_id=1, source_target_pairs={{0,2},{1,3},{2,0},{3,1},{4,6},{5,7},{6,4},{7,5},{8,10},{9,11},{10,... | collective-permute-start | bytes 138248 | tf_op jit(solution)/shard_map/ppermute | solution.py:516
  10.2 1.1 %collective-permute-done.2.other_ref = s32[8,256]{1,0:T(8,128)S(1)} collective-permute-done((s32[8,256]{1,0:T(8,128)S(1)}, s32[8,256]{1,0:T(8,128)S(1)}, u32[]{:S(2)}, u32[]{:S(2)}) %collective-permute-start.2) | collective-permute-done | bytes 8224 | tf_op jit(solution)/shard_map/ppermute | solution.py:516
  11.3 0.0 copy-start.1
  11.3 0.0 copy-start.2
  11.3 0.0 copy-start.3
  11.3 0.1 collective-permute-start.6
  11.4 2.7 %collective-permute-start.3 = (s32[8,256]{1,0:T(8,128)S(1)}, s32[8,256]{1,0:T(8,128)S(1)}, u32[]{:S(2)}, u32[]{:S(2)}) collective-permute-start(s32[8,256]{1,0:T(8,128)S(1)} %join.3.refs_4_), channel_id=1, source_target_pairs={{0,16},{1,17},{2,18},{3,19},{4,20},{5,21},{6,22},{7,23},{8,24},{9,... | collective-permute-start | bytes 24584 | tf_op jit(solution)/shard_map/ppermute | solution.py:516
  14.1 0.0 collective-permute-done.4.refs_2_
  14.1 2.0 %collective-permute-done.3.refs_5_ = s32[8,256]{1,0:T(8,128)S(1)} collective-permute-done((s32[8,256]{1,0:T(8,128)S(1)}, s32[8,256]{1,0:T(8,128)S(1)}, u32[]{:S(2)}, u32[]{:S(2)}) %collective-permute-start.3) | collective-permute-done | bytes 8224 | tf_op jit(solution)/shard_map/ppermute | solution.py:516
  16.0 0.0 collective-permute-start.5
  16.0 0.0 collective-permute-done.8.refs_3_
  16.0 0.0 collective-permute-done.7.refs_2_
  16.0 0.0 collective-permute-done.6.refs_1_
  16.0 2.8 %row_attention.1 = (bf16[512,768]{1,0:T(8,128)(2,1)S(1)}, bf16[256,128]{1,0:T(8,128)(2,1)S(1)}, f32[16,128]{1,0:T(8,128)S(1)}) custom-call(bf16[40,576]{1,0:T(8,128)(2,1)S(1)} %tables.1.refs_0_, bf16[40,576]{1,0:T(8,128)(2,1)S(1)} %collective-permute-done.6.refs_1_, bf16[40,576]{1,0:T(8,128)(2,1)S(1)} %collective-permute-done.7.refs_2_, ...), custom_call_target="tpu_custom_call" | custom-call | flops 3000000000 | bytes 1000000 | tf_op jit(solution)/shard_map/row_attention/pallas_call | solution.py:283
  18.9 0.0 collective-permute-done.5.refs_3_
  18.9 0.0 copy-done.1
  18.9 0.0 copy-done.2
  18.9 0.0 copy-done.3
  18.9 0.0 copy-start
  18.9 3.3 %column_attention.1 = (bf16[384,128]{1,0:T(8,128)(2,1)S(1)}, bf16[384,128]{1,0:T(8,128)(2,1)S(1)}, f32[256,192]{1,0:T(8,128)S(1)}, f32[256,192]{1,0:T(8,128)S(1)}) custom-call(bf16[192,768]{1,0:T(8,128)(2,1)S(1)} %copy-done.2, bf16[192,768]{1,0:T(8,128)(2,1)S(1)} %collective-permute-done.1.refs_1_, bf16[192,768]{1,0:T(8,128)(2,1)S(1)} %collective-permute-done.4.refs_2_, ...), custom_call_target="tpu_custom_call" | custom-call | flops 2000000000 | bytes 1000000 | tf_op jit(solution)/shard_map/column_attention/pallas_call | solution.py:412
  22.3 0.4 collective-permute-start.10
  22.6 1.7 %collective-permute-start.13 = (bf16[384,128]{1,0:T(8,128)(2,1)S(1)}, bf16[384,128]{1,0:T(8,128)(2,1)S(1)}, u32[]{:S(2)}, u32[]{:S(2)}) collective-permute-start(bf16[384,128]{1,0:T(8,128)(2,1)S(1)} %get-tuple-element.38.refs_4_), channel_id=1, source_target_pairs={{0,2},{1,3},{2,0},{3,1},{4,6},{5,7},{6,4},{7,5},{8,10},{9,11},{10,... | collective-permute-start | bytes 294920 | tf_op jit(solution)/shard_map/ppermute | solution.py:516
  24.4 0.1 collective-permute-start.9
  24.5 0.4 collective-permute-start.12
  24.9 3.1 %collective-permute-done.10.refs_2_ = bf16[384,128]{1,0:T(8,128)(2,1)S(1)} collective-permute-done((bf16[384,128]{1,0:T(8,128)(2,1)S(1)}, bf16[384,128]{1,0:T(8,128)(2,1)S(1)}, u32[]{:S(2)}, u32[]{:S(2)}) %collective-permute-start.10) | collective-permute-done | bytes 98336 | tf_op jit(solution)/shard_map/ppermute | solution.py:516
  28.0 0.0 collective-permute-start.11
  28.0 1.8 %collective-permute-done.13.refs_6_ = bf16[384,128]{1,0:T(8,128)(2,1)S(1)} collective-permute-done((bf16[384,128]{1,0:T(8,128)(2,1)S(1)}, bf16[384,128]{1,0:T(8,128)(2,1)S(1)}, u32[]{:S(2)}, u32[]{:S(2)}) %collective-permute-start.13) | collective-permute-done | bytes 98336 | tf_op jit(solution)/shard_map/ppermute | solution.py:516
  29.8 0.0 collective-permute-start.14
  29.8 0.0 collective-permute-done.9.refs_1_
  29.8 0.0 collective-permute-done.12.refs_5_
  29.8 0.0 collective-permute-done.11.refs_3_
  29.8 1.3 %collective-permute-done.14.refs_7_ = bf16[384,128]{1,0:T(8,128)(2,1)S(1)} collective-permute-done((bf16[384,128]{1,0:T(8,128)(2,1)S(1)}, bf16[384,128]{1,0:T(8,128)(2,1)S(1)}, u32[]{:S(2)}, u32[]{:S(2)}) %collective-permute-start.14) | collective-permute-done | bytes 98336 | tf_op jit(solution)/shard_map/ppermute | solution.py:516
  31.1 0.0 copy-done
  31.1 1.1 %finish.1 = bf16[8,96,128]{2,1,0:T(8,128)(2,1)S(1)} custom-call(bf16[384,128]{1,0:T(8,128)(2,1)S(1)} %get-tuple-element.37.refs_0_, bf16[384,128]{1,0:T(8,128)(2,1)S(1)} %collective-permute-done.9.refs_1_, bf16[384,128]{1,0:T(8,128)(2,1)S(1)} %collective-permute-done.10.refs_2_, bf16[384,128]{1,0:T(8,128)(2,1)S(1)} %collective-permute-done.11.refs_3_, ...), custom_call_target="tpu_custom_call" | custom-call | tf_op jit(solution)/shard_map/finish/pallas_call | solution.py:469
  32.2 13.9 %all_to_all.5.blocks_ref = bf16[8,96,128]{2,1,0:T(8,128)(2,1)S(1)} all-to-all(bf16[8,96,128]{2,1,0:T(8,128)(2,1)S(1)} %finish.1), channel_id=1, replica_groups=mesh['seq'=8,'head'=4] {'seq'}, dimensions={0} | all-to-all | bytes 393216 | tf_op jit(solution)/shard_map/all_to_all | solution.py:558
  46.1 0.8 %order.1 = bf16[2,192,256]{2,1,0:T(8,128)(2,1)} custom-call(bf16[8,96,128]{2,1,0:T(8,128)(2,1)S(1)} %all_to_all.5.blocks_ref), custom_call_target="tpu_custom_call" | custom-call | tf_op jit(solution)/shard_map/order/pallas_call | solution.py:498
  (2 shorter events, 0.0 us)
Async XLA Ops:
  0.8 6.7 %collective-permute-start.1 = (bf16[192,768]{1,0:T(8,128)(2,1)}, bf16[192,768]{1,0:T(8,128)(2,1)S(1)}, u32[]{:S(2)}, u32[]{:S(2)}) collective-permute-start(bf16[192,768]{1,0:T(8,128)(2,1)} %refs_0_), channel_id=1, source_target_pairs={{0,1},{1,0},{2,3},{3,2},{4,5},{5,4},{6,7},{7,6},{8,9},{9,8},{10,11... | collective-permute-start | bytes 884744 | tf_op jit(solution)/shard_map/ppermute | solution.py:516
  1.4 12.7 %collective-permute-start.4 = (bf16[192,768]{1,0:T(8,128)(2,1)}, bf16[192,768]{1,0:T(8,128)(2,1)S(1)}, u32[]{:S(2)}, u32[]{:S(2)}) collective-permute-start(bf16[192,768]{1,0:T(8,128)(2,1)} %refs_0_), channel_id=1, source_target_pairs={{0,2},{1,3},{2,0},{3,1},{4,6},{5,7},{6,4},{7,5},{8,10},{9,11},{10,... | collective-permute-start | bytes 884744 | tf_op jit(solution)/shard_map/ppermute | solution.py:516
  3.9 3.7 %collective-permute-start = (s32[8,256]{1,0:T(8,128)S(1)}, s32[8,256]{1,0:T(8,128)S(1)}, u32[]{:S(2)}, u32[]{:S(2)}) collective-permute-start(s32[8,256]{1,0:T(8,128)S(1)} %codes.1.own_ref), channel_id=1, source_target_pairs={{0,4},{1,5},{2,6},{3,7},{4,0},{5,1},{6,2},{7,3},{8,12},{9,13},{10,... | collective-permute-start | bytes 24584 | tf_op jit(solution)/shard_map/ppermute | solution.py:516
  7.6 3.7 %collective-permute-start.2 = (s32[8,256]{1,0:T(8,128)S(1)}, s32[8,256]{1,0:T(8,128)S(1)}, u32[]{:S(2)}, u32[]{:S(2)}) collective-permute-start(s32[8,256]{1,0:T(8,128)S(1)} %join.2.own_ref), channel_id=1, source_target_pairs={{0,8},{1,9},{2,10},{3,11},{4,12},{5,13},{6,14},{7,15},{8,0},{9,1},... | collective-permute-start | bytes 24584 | tf_op jit(solution)/shard_map/ppermute | solution.py:516
  9.2 6.8 %collective-permute-start.8 = (bf16[40,576]{1,0:T(8,128)(2,1)S(1)}, bf16[40,576]{1,0:T(8,128)(2,1)S(1)}, u32[]{:S(2)}, u32[]{:S(2)}) collective-permute-start(bf16[40,576]{1,0:T(8,128)(2,1)S(1)} %tables.1.refs_0_), channel_id=1, source_target_pairs={{0,3},{1,2},{2,1},{3,0},{4,7},{5,6},{6,5},{7,4},{8,11},{9,10},{10,... | collective-permute-start | bytes 138248 | tf_op jit(solution)/shard_map/ppermute | solution.py:516
  9.2 6.8 %collective-permute-start.7 = (bf16[40,576]{1,0:T(8,128)(2,1)S(1)}, bf16[40,576]{1,0:T(8,128)(2,1)S(1)}, u32[]{:S(2)}, u32[]{:S(2)}) collective-permute-start(bf16[40,576]{1,0:T(8,128)(2,1)S(1)} %tables.1.refs_0_), channel_id=1, source_target_pairs={{0,2},{1,3},{2,0},{3,1},{4,6},{5,7},{6,4},{7,5},{8,10},{9,11},{10,... | collective-permute-start | bytes 138248 | tf_op jit(solution)/shard_map/ppermute | solution.py:516
  11.3 7.6 %copy-start.1 = (bf16[3,192,768]{2,1,0:T(8,128)(2,1)S(1)}, bf16[3,192,768]{2,1,0:T(8,128)(2,1)}, u32[]{:S(2)}) copy-start(bf16[3,192,768]{2,1,0:T(8,128)(2,1)} %param.12) | copy-start | bytes 2654212
  11.3 7.6 %copy-start.2 = (bf16[192,768]{1,0:T(8,128)(2,1)S(1)}, bf16[192,768]{1,0:T(8,128)(2,1)}, u32[]{:S(2)}) copy-start(bf16[192,768]{1,0:T(8,128)(2,1)} %refs_0_) | copy-start | bytes 884740
  11.3 7.6 %copy-start.3 = (bf16[33,768]{1,0:T(8,128)(2,1)S(1)}, bf16[33,768]{1,0:T(8,128)(2,1)}, u32[]{:S(2)}) copy-start(bf16[33,768]{1,0:T(8,128)(2,1)} %refs_7_.1) | copy-start | bytes 152068
  11.3 4.7 %collective-permute-start.6 = (bf16[40,576]{1,0:T(8,128)(2,1)S(1)}, bf16[40,576]{1,0:T(8,128)(2,1)S(1)}, u32[]{:S(2)}, u32[]{:S(2)}) collective-permute-start(bf16[40,576]{1,0:T(8,128)(2,1)S(1)} %tables.1.refs_0_), channel_id=1, source_target_pairs={{0,1},{1,0},{2,3},{3,2},{4,5},{5,4},{6,7},{7,6},{8,9},{9,8},{10,11... | collective-permute-start | bytes 138248 | tf_op jit(solution)/shard_map/ppermute | solution.py:516
  11.4 4.6 %collective-permute-start.3 = (s32[8,256]{1,0:T(8,128)S(1)}, s32[8,256]{1,0:T(8,128)S(1)}, u32[]{:S(2)}, u32[]{:S(2)}) collective-permute-start(s32[8,256]{1,0:T(8,128)S(1)} %join.3.refs_4_), channel_id=1, source_target_pairs={{0,16},{1,17},{2,18},{3,19},{4,20},{5,21},{6,22},{7,23},{8,24},{9,... | collective-permute-start | bytes 24584 | tf_op jit(solution)/shard_map/ppermute | solution.py:516
  16.0 2.9 %collective-permute-start.5 = (bf16[192,768]{1,0:T(8,128)(2,1)S(1)}, bf16[192,768]{1,0:T(8,128)(2,1)S(1)}, u32[]{:S(2)}, u32[]{:S(2)}) collective-permute-start(bf16[192,768]{1,0:T(8,128)(2,1)S(1)} %collective-permute-done.4.refs_2_), channel_id=1, source_target_pairs={{0,1},{1,0},{2,3},{3,2},{4,5},{5,4},{6,7},{7,6},{8,9},{9,8},{10,11... | collective-permute-start | bytes 884744 | tf_op jit(solution)/shard_map/ppermute | solution.py:516
  18.9 12.2 %copy-start = (bf16[192,768]{1,0:T(8,128)(2,1)S(1)}, bf16[192,768]{1,0:T(8,128)(2,1)}, u32[]{:S(2)}) copy-start(bf16[192,768]{1,0:T(8,128)(2,1)} %refs_10_.1) | copy-start | bytes 884740
  22.3 5.7 %collective-permute-start.10 = (bf16[384,128]{1,0:T(8,128)(2,1)S(1)}, bf16[384,128]{1,0:T(8,128)(2,1)S(1)}, u32[]{:S(2)}, u32[]{:S(2)}) collective-permute-start(bf16[384,128]{1,0:T(8,128)(2,1)S(1)} %get-tuple-element.37.refs_0_), channel_id=1, source_target_pairs={{0,2},{1,3},{2,0},{3,1},{4,6},{5,7},{6,4},{7,5},{8,10},{9,11},{10,... | collective-permute-start | bytes 294920 | tf_op jit(solution)/shard_map/ppermute | solution.py:516
  22.6 7.2 %collective-permute-start.13 = (bf16[384,128]{1,0:T(8,128)(2,1)S(1)}, bf16[384,128]{1,0:T(8,128)(2,1)S(1)}, u32[]{:S(2)}, u32[]{:S(2)}) collective-permute-start(bf16[384,128]{1,0:T(8,128)(2,1)S(1)} %get-tuple-element.38.refs_4_), channel_id=1, source_target_pairs={{0,2},{1,3},{2,0},{3,1},{4,6},{5,7},{6,4},{7,5},{8,10},{9,11},{10,... | collective-permute-start | bytes 294920 | tf_op jit(solution)/shard_map/ppermute | solution.py:516
  24.4 5.5 %collective-permute-start.9 = (bf16[384,128]{1,0:T(8,128)(2,1)S(1)}, bf16[384,128]{1,0:T(8,128)(2,1)S(1)}, u32[]{:S(2)}, u32[]{:S(2)}) collective-permute-start(bf16[384,128]{1,0:T(8,128)(2,1)S(1)} %get-tuple-element.37.refs_0_), channel_id=1, source_target_pairs={{0,1},{1,0},{2,3},{3,2},{4,5},{5,4},{6,7},{7,6},{8,9},{9,8},{10,11... | collective-permute-start | bytes 294920 | tf_op jit(solution)/shard_map/ppermute | solution.py:516
  24.5 5.3 %collective-permute-start.12 = (bf16[384,128]{1,0:T(8,128)(2,1)S(1)}, bf16[384,128]{1,0:T(8,128)(2,1)S(1)}, u32[]{:S(2)}, u32[]{:S(2)}) collective-permute-start(bf16[384,128]{1,0:T(8,128)(2,1)S(1)} %get-tuple-element.38.refs_4_), channel_id=1, source_target_pairs={{0,1},{1,0},{2,3},{3,2},{4,5},{5,4},{6,7},{7,6},{8,9},{9,8},{10,11... | collective-permute-start | bytes 294920 | tf_op jit(solution)/shard_map/ppermute | solution.py:516
  28.0 1.8 %collective-permute-start.11 = (bf16[384,128]{1,0:T(8,128)(2,1)S(1)}, bf16[384,128]{1,0:T(8,128)(2,1)S(1)}, u32[]{:S(2)}, u32[]{:S(2)}) collective-permute-start(bf16[384,128]{1,0:T(8,128)(2,1)S(1)} %collective-permute-done.10.refs_2_), channel_id=1, source_target_pairs={{0,1},{1,0},{2,3},{3,2},{4,5},{5,4},{6,7},{7,6},{8,9},{9,8},{10,11... | collective-permute-start | bytes 294920 | tf_op jit(solution)/shard_map/ppermute | solution.py:516
  29.8 1.3 %collective-permute-start.14 = (bf16[384,128]{1,0:T(8,128)(2,1)S(1)}, bf16[384,128]{1,0:T(8,128)(2,1)S(1)}, u32[]{:S(2)}, u32[]{:S(2)}) collective-permute-start(bf16[384,128]{1,0:T(8,128)(2,1)S(1)} %collective-permute-done.13.refs_6_), channel_id=1, source_target_pairs={{0,1},{1,0},{2,3},{3,2},{4,5},{5,4},{6,7},{7,6},{8,9},{9,8},{10,11... | collective-permute-start | bytes 294920 | tf_op jit(solution)/shard_map/ppermute | solution.py:516

commit v13 on v11

--- a/solution.py
+++ b/solution.py
@@ -62,14 +62,13 @@
     live = jnp.zeros(ids_ref.shape, jnp.int32)
     for r in range(ids_ref.shape[0]):
         live = jnp.where(row == r, live_ref[r], live)
-    coded = ids_ref[...] + 65536 * live
-    out_ref[...] = jnp.concatenate([coded] * (out_ref.shape[0] // coded.shape[0]), 0)
-
-
-def make_codes(ids, pad_mask, height):
+    out_ref[...] = ids_ref[...] + 65536 * live
+
+
+def make_codes(ids, pad_mask):
     return pl.pallas_call(
         code_kernel,
-        out_shape=jax.ShapeDtypeStruct((height, ids.shape[1]), jnp.int32),
+        out_shape=jax.ShapeDtypeStruct(ids.shape, jnp.int32),
         in_specs=[pl.BlockSpec(memory_space=pltpu.HBM)] * 2,
         scratch_shapes=[
             pltpu.VMEM(ids.shape, jnp.int32),
@@ -81,16 +80,17 @@
     )(in_hbm(ids), in_hbm(pad_mask))
 
 
-def join_kernel(rows, own_ref, other_ref, out_ref):
-    own, other = own_ref[...], other_ref[...]
-    both = jnp.concatenate([own[0:rows], other[0:rows]], 0)
-    out_ref[...] = jnp.concatenate([both] * (own.shape[0] // (2 * rows)), 0)
-
-
-def join(own, other, rows):
+def join_kernel(own_ref, other_ref, out_ref):
+    both = jnp.concatenate([own_ref[...], other_ref[...]], 0)
+    for pair in range(out_ref.shape[0]):
+        out_ref[pair] = both
+
+
+def join(own, other, pairs):
+    rows, cols = own.shape
     return pl.pallas_call(
-        functools.partial(join_kernel, rows),
-        out_shape=jax.ShapeDtypeStruct(own.shape, own.dtype),
+        join_kernel,
+        out_shape=jax.ShapeDtypeStruct((pairs, 2 * rows, cols), own.dtype),
         compiler_params=pltpu.CompilerParams(vmem_limit_bytes=SMALL_VMEM),
         name="join",
     )(own, other)
@@ -165,8 +165,7 @@
 def row_kernel(parts, *refs):
     tables_refs, refs = refs[:parts], refs[parts:]
     (
-        near_codes_ref,
-        far_codes_ref,
+        codes_ref,
         row_context_ref,
         own_ref,
         live_ref,
@@ -195,7 +194,8 @@
         )
         table_ref[t, TABLE_ROWS:CODES, :] = jnp.zeros((CODES - TABLE_ROWS, width), bf16)
 
-    coded = jnp.concatenate([near_codes_ref[...], far_codes_ref[...]], 0)
+    pair = group // 2
+    coded = jnp.concatenate([codes_ref[pair ^ d] for d in range(codes_ref.shape[0])], 0)
     ids = (coded & 0xFFFF).astype(f32)
     live = (coded[:, 0:LANES] >> 16).astype(f32)
     live_ref[...] = live
@@ -290,7 +290,7 @@
         cost_estimate=pl.CostEstimate(flops=3 * 10**9, bytes_accessed=10**6, transcendentals=0),
         compiler_params=pltpu.CompilerParams(vmem_limit_bytes=LARGE_VMEM),
         name="row_attention",
-    )(*tables, *codes)
+    )(*tables, codes)
 
 
 def column_kernel(parts, *refs):
@@ -516,25 +516,25 @@
     def opposite(g, p):
         return g, p ^ 3
 
-    far = pairwise(row_out, across)
-    coded = make_codes(ids, pad_mask, rows_here * groups // 2)
+    coded = make_codes(ids, pad_mask)
     coded, row_qkv = lax.optimization_barrier((coded, row_qkv))
     received = pairwise(coded, lambda g, p: (g ^ 1, p))
     table = make_tables(embed, row_qkv)
-    step = 2
-    while step < groups:
-        coded = join(coded, received, rows_here * step // 2)
-        if step == 2:
-            coded, table = lax.optimization_barrier((coded, table))
-            far_tables = [pairwise(table, to) for to in (across, opposite)]
-        received = pairwise(coded, lambda g, p, step=step: (g ^ step, p))
-        step *= 2
-    codes = (coded, received)
-    coded, late_table = lax.optimization_barrier((coded, table))
-    codes = (coded, received)
-    tables = [table, pairwise(late_table, sibling)] + far_tables
-    *codes, near, far = lax.optimization_barrier((*codes, row_out, far))
-    row_outs = [row_out, pairwise(near, sibling), far, pairwise(far, sibling)]
+    codes = join(coded, received, groups // 2)
+    codes, table, row_out = lax.optimization_barrier((codes, table, row_out))
+    tables = [table] + [pairwise(table, to) for to in (sibling, across, opposite)]
+    far = pairwise(row_out, across)
+    near = pairwise(row_out, sibling)
+    codes = lax.all_to_all(
+        codes,
+        "seq",
+        split_axis=0,
+        concat_axis=0,
+        tiled=True,
+        axis_index_groups=[list(range(k, groups, 2)) for k in range(2)],
+    )
+    codes, far = lax.optimization_barrier((codes, far))
+    row_outs = [row_out, near, far, pairwise(far, sibling)]
     row_context, own_codes, live = attend_rows(tables, codes, rows, cols, own, width)
     *halves_here, mixed_low, mixed_high = attend_columns_here(
         row_outs, live, row_context, own_codes, embed, col_qkv.reshape(3 * local, width)

time: 47.1 us -> 48.7 us (1.034)
  blocking collectives: 13.9 us -> 11 us
  waiting for transfers between devices: 9.57 us -> 11.8 us
  starting transfers between devices: 12.5 us -> 14.1 us
  Pallas kernels: 10.7 us -> 11.3 us
    all_to_all x0 -> x1, waiting for transfers between devices: none -> 5.6 us  [fast_body(): lax.all_to_all(codes, 'seq', split_axis=0, concat_axis=0, tiled=True, axi...]
    all_to_all x0 -> x1, starting transfers between devices: none -> 4.87 us  [fast_body(): lax.all_to_all(codes, 'seq', split_axis=0, concat_axis=0, tiled=True, axi...]
    ppermute x15 -> x13, waiting for transfers between devices: 9.57 us -> 6.25 us  [pairwise(): lax.ppermute(value, ('seq', 'head'), [(i, g * parts + p) for i, (g, p) in...]
    ppermute x15 -> x13, starting transfers between devices: 12.5 us -> 9.2 us  [pairwise(): lax.ppermute(value, ('seq', 'head'), [(i, g * parts + p) for i, (g, p) in...]
    all_to_all x1, blocking collectives: 13.9 us -> 11 us  [fast_body(): lax.all_to_all(blocks, 'seq', split_axis=0, concat_axis=0, tiled=True)]
    pallas_call x3 -> x2, Pallas kernels: 0.83 us -> 1.43 us  [the longest x1 0.82 us: make_codes(): pl.pallas_call(code_kernel, out_shape=jax.ShapeDtypeStruct(ids.shape, jnp...]
  transfers between devices with their start and end apart: 15 -> 14, of which waited for: 6 -> 4; matrix products, arithmetic and copies ran while one was open for 0% -> 0% of each run, Pallas kernels for 12% -> 10%
where the time goes in v13:
time: 48.7 us; the launch traced here: 48.4 us
  starting transfers between devices  14.1 us (29%)
  waiting for transfers between devices  11.8 us (24%)
  Pallas kernels  11.3 us (23%)
  blocking collectives  11 us (23%)
    all_to_all x1, blocking collectives, fast_body(): lax.all_to_all(blocks, 'seq', split_axis=0, concat_axis=0, tiled=True)  11 us
    ppermute x13, starting transfers between devices, pairwise(): lax.ppermute(value, ('seq', 'head'), [(i, g * parts + p) for i, (g, p) in...  9.2 us
    ppermute x13, waiting for transfers between devices, pairwise(): lax.ppermute(value, ('seq', 'head'), [(i, g * parts + p) for i, (g, p) in...  6.25 us
    all_to_all x1, waiting for transfers between devices, fast_body(): lax.all_to_all(codes, 'seq', split_axis=0, concat_axis=0, tiled=True, axi...  5.6 us
    all_to_all x1, starting transfers between devices, fast_body(): lax.all_to_all(codes, 'seq', split_axis=0, concat_axis=0, tiled=True, axi...  4.87 us
    pallas_call x1, Pallas kernels, attend_columns_here(): pl.pallas_call(functools.partial(column_kernel, parts), out_shape=(*[jax....  3.31 us
    pallas_call x1, Pallas kernels, attend_rows(): pl.pallas_call(functools.partial(row_kernel, parts), out_shape=(jax.Shape...  2.84 us
    pallas_call x1, Pallas kernels, make_tables(): pl.pallas_call(table_kernel, out_shape=jax.ShapeDtypeStruct((TABLE_ROWS,...  1.84 us
  transfers between devices with their start and end apart: 14, of which 4 were waited for; matrix products, arithmetic and copies ran while one was open for 0% of the time, Pallas kernels for 10%

profile of v13, /device:TPU:0, one launch (start us, length us, event | category | flops | bytes accessed | tf_op | source)
XLA Modules:
  0.0 48.4 jit_solution(8555042992828139537)
XLA Ops:
  0.0 0.8 %codes.1.own_ref = s32[2,256]{1,0:T(2,128)S(1)} custom-call(s32[2,256]{1,0:T(2,128)} %ids_hbm.1, s32[2]{0:T(128)} %live_hbm.1), custom_call_target="tpu_custom_call" | custom-call | tf_op jit(solution)/shard_map/codes/pallas_call | solution.py:69
  0.8 0.0 copy-start.2
  0.8 3.0 %collective-permute-start = (s32[2,256]{1,0:T(2,128)S(1)}, s32[2,256]{1,0:T(2,128)S(1)}, u32[]{:S(2)}, u32[]{:S(2)}) collective-permute-start(s32[2,256]{1,0:T(2,128)S(1)} %codes.1.own_ref), channel_id=1, source_target_pairs={{0,4},{1,5},{2,6},{3,7},{4,0},{5,1},{6,2},{7,3},{8,12},{9,13},{10,... | collective-permute-start | bytes 6152 | tf_op jit(solution)/shard_map/ppermute | solution.py:508
  3.9 1.8 %tables.1.refs_0_ = bf16[40,576]{1,0:T(8,128)(2,1)S(1)} custom-call(bf16[33,768]{1,0:T(8,128)(2,1)} %refs_7_.1, bf16[3,192,768]{2,1,0:T(8,128)(2,1)} %qkv_hbm), custom_call_target="tpu_custom_call" | custom-call | flops 2000000000 | bytes 884736 | tf_op jit(solution)/shard_map/tables/pallas_call | solution.py:120
  5.7 0.0 collective-permute-done.other_ref
  5.7 0.6 %join.1 = s32[4,4,256]{2,1,0:T(4,128)} custom-call(s32[2,256]{1,0:T(2,128)S(1)} %codes.1.own_ref, s32[2,256]{1,0:T(2,128)S(1)} %collective-permute-done.other_ref), custom_call_target="tpu_custom_call" | custom-call | tf_op jit(solution)/shard_map/join/pallas_call | solution.py:91
  6.3 0.0 copy-done.2
  6.3 1.7 %collective-permute-start.2 = (bf16[192,768]{1,0:T(8,128)(2,1)S(1)}, bf16[192,768]{1,0:T(8,128)(2,1)S(1)}, u32[]{:S(2)}, u32[]{:S(2)}) collective-permute-start(bf16[192,768]{1,0:T(8,128)(2,1)S(1)} %copy-done.2), channel_id=1, source_target_pairs={{0,2},{1,3},{2,0},{3,1},{4,6},{5,7},{6,4},{7,5},{8,10},{9,11},{10,... | collective-permute-start | bytes 884744 | tf_op jit(solution)/shard_map/ppermute | solution.py:508
  8.0 0.0 collective-permute-start.6
  8.0 0.7 %collective-permute-start.5 = (bf16[40,576]{1,0:T(8,128)(2,1)S(1)}, bf16[40,576]{1,0:T(8,128)(2,1)S(1)}, u32[]{:S(2)}, u32[]{:S(2)}) collective-permute-start(bf16[40,576]{1,0:T(8,128)(2,1)S(1)} %tables.1.refs_0_), channel_id=1, source_target_pairs={{0,2},{1,3},{2,0},{3,1},{4,6},{5,7},{6,4},{7,5},{8,10},{9,11},{10,... | collective-permute-start | bytes 138248 | tf_op jit(solution)/shard_map/ppermute | solution.py:508
  8.7 1.2 %collective-permute-start.4 = (bf16[40,576]{1,0:T(8,128)(2,1)S(1)}, bf16[40,576]{1,0:T(8,128)(2,1)S(1)}, u32[]{:S(2)}, u32[]{:S(2)}) collective-permute-start(bf16[40,576]{1,0:T(8,128)(2,1)S(1)} %tables.1.refs_0_), channel_id=1, source_target_pairs={{0,1},{1,0},{2,3},{3,2},{4,5},{5,4},{6,7},{7,6},{8,9},{9,8},{10,11... | collective-permute-start | bytes 138248 | tf_op jit(solution)/shard_map/ppermute | solution.py:508
  9.9 4.9 %all-to-all-start = ((s32[4,4,256]{2,1,0:T(4,128)}), s32[4,4,256]{2,1,0:T(4,128)S(1)}, u32[]{:S(2)}, u32[]{:S(2)}) async-start(s32[4,4,256]{2,1,0:T(4,128)} %join.1), calls=%async_computation | async-start | bytes 32768 | tf_op jit(solution)/shard_map/all_to_all | solution.py:528
  14.8 0.0 copy-start.1
  14.8 0.0 copy-start.3
  14.8 0.0 collective-permute-start.1
  14.8 5.6 %all-to-all-done.refs_4_ = s32[4,4,256]{2,1,0:T(4,128)S(1)} async-done(((s32[4,4,256]{2,1,0:T(4,128)}), s32[4,4,256]{2,1,0:T(4,128)S(1)}, u32[]{:S(2)}, u32[]{:S(2)}) %all-to-all-start) | async-done | bytes 16416 | tf_op jit(solution)/shard_map/all_to_all | solution.py:528
  20.4 0.0 collective-permute-done.2.refs_2_
  20.4 0.0 collective-permute-start.3
  20.4 0.0 collective-permute-done.6.refs_3_
  20.4 0.0 collective-permute-done.5.refs_2_
  20.4 0.0 collective-permute-done.4.refs_1_
  20.4 2.8 %row_attention.1 = (bf16[512,768]{1,0:T(8,128)(2,1)S(1)}, bf16[256,128]{1,0:T(8,128)(2,1)S(1)}, f32[16,128]{1,0:T(8,128)S(1)}) custom-call(bf16[40,576]{1,0:T(8,128)(2,1)S(1)} %tables.1.refs_0_, bf16[40,576]{1,0:T(8,128)(2,1)S(1)} %collective-permute-done.4.refs_1_, bf16[40,576]{1,0:T(8,128)(2,1)S(1)} %collective-permute-done.5.refs_2_, ...), custom_call_target="tpu_custom_call" | custom-call | flops 3000000000 | bytes 1000000 | tf_op jit(solution)/shard_map/row_attention/pallas_call | solution.py:275
  23.3 0.0 collective-permute-done.1.refs_1_
  23.3 0.0 collective-permute-done.3.refs_3_
  23.3 0.0 copy-done.1
  23.3 0.0 copy-done.3
  23.3 0.0 copy-start
  23.3 3.3 %column_attention.1 = (bf16[384,128]{1,0:T(8,128)(2,1)S(1)}, bf16[384,128]{1,0:T(8,128)(2,1)S(1)}, f32[256,192]{1,0:T(8,128)S(1)}, f32[256,192]{1,0:T(8,128)S(1)}) custom-call(bf16[192,768]{1,0:T(8,128)(2,1)S(1)} %copy-done.2, bf16[192,768]{1,0:T(8,128)(2,1)S(1)} %collective-permute-done.1.refs_1_, bf16[192,768]{1,0:T(8,128)(2,1)S(1)} %collective-permute-done.2.refs_2_, ...), custom_call_target="tpu_custom_call" | custom-call | flops 2000000000 | bytes 1000000 | tf_op jit(solution)/shard_map/column_attention/pallas_call | solution.py:404
  26.6 0.6 %collective-permute-start.8 = (bf16[384,128]{1,0:T(8,128)(2,1)S(1)}, bf16[384,128]{1,0:T(8,128)(2,1)S(1)}, u32[]{:S(2)}, u32[]{:S(2)}) collective-permute-start(bf16[384,128]{1,0:T(8,128)(2,1)S(1)} %get-tuple-element.29.refs_0_), channel_id=1, source_target_pairs={{0,2},{1,3},{2,0},{3,1},{4,6},{5,7},{6,4},{7,5},{8,10},{9,11},{10,... | collective-permute-start | bytes 294920 | tf_op jit(solution)/shard_map/ppermute | solution.py:508
  27.3 1.5 %collective-permute-start.11 = (bf16[384,128]{1,0:T(8,128)(2,1)S(1)}, bf16[384,128]{1,0:T(8,128)(2,1)S(1)}, u32[]{:S(2)}, u32[]{:S(2)}) collective-permute-start(bf16[384,128]{1,0:T(8,128)(2,1)S(1)} %get-tuple-element.30.refs_4_), channel_id=1, source_target_pairs={{0,2},{1,3},{2,0},{3,1},{4,6},{5,7},{6,4},{7,5},{8,10},{9,11},{10,... | collective-permute-start | bytes 294920 | tf_op jit(solution)/shard_map/ppermute | solution.py:508
  28.7 0.1 collective-permute-start.7
  28.9 0.4 collective-permute-start.10
  29.2 3.1 %collective-permute-done.8.refs_2_ = bf16[384,128]{1,0:T(8,128)(2,1)S(1)} collective-permute-done((bf16[384,128]{1,0:T(8,128)(2,1)S(1)}, bf16[384,128]{1,0:T(8,128)(2,1)S(1)}, u32[]{:S(2)}, u32[]{:S(2)}) %collective-permute-start.8) | collective-permute-done | bytes 98336 | tf_op jit(solution)/shard_map/ppermute | solution.py:508
  32.4 0.0 collective-permute-start.9
  32.4 1.8 %collective-permute-done.11.refs_6_ = bf16[384,128]{1,0:T(8,128)(2,1)S(1)} collective-permute-done((bf16[384,128]{1,0:T(8,128)(2,1)S(1)}, bf16[384,128]{1,0:T(8,128)(2,1)S(1)}, u32[]{:S(2)}, u32[]{:S(2)}) %collective-permute-start.11) | collective-permute-done | bytes 98336 | tf_op jit(solution)/shard_map/ppermute | solution.py:508
  34.2 0.0 collective-permute-start.12
  34.2 0.0 collective-permute-done.7.refs_1_
  34.2 0.0 collective-permute-done.10.refs_5_
  34.2 0.0 collective-permute-done.9.refs_3_
  34.2 1.3 %collective-permute-done.12.refs_7_ = bf16[384,128]{1,0:T(8,128)(2,1)S(1)} collective-permute-done((bf16[384,128]{1,0:T(8,128)(2,1)S(1)}, bf16[384,128]{1,0:T(8,128)(2,1)S(1)}, u32[]{:S(2)}, u32[]{:S(2)}) %collective-permute-start.12) | collective-permute-done | bytes 98336 | tf_op jit(solution)/shard_map/ppermute | solution.py:508
  35.5 0.0 copy-done
  35.5 1.1 %finish.1 = bf16[8,96,128]{2,1,0:T(8,128)(2,1)S(1)} custom-call(bf16[384,128]{1,0:T(8,128)(2,1)S(1)} %get-tuple-element.29.refs_0_, bf16[384,128]{1,0:T(8,128)(2,1)S(1)} %collective-permute-done.7.refs_1_, bf16[384,128]{1,0:T(8,128)(2,1)S(1)} %collective-permute-done.8.refs_2_, bf16[384,128]{1,0:T(8,128)(2,1)S(1)} %collective-permute-done.9.refs_3_, ...), custom_call_target="tpu_custom_call" | custom-call | tf_op jit(solution)/shard_map/finish/pallas_call | solution.py:461
  36.6 11.0 %all_to_all.10.blocks_ref = bf16[8,96,128]{2,1,0:T(8,128)(2,1)S(1)} all-to-all(bf16[8,96,128]{2,1,0:T(8,128)(2,1)S(1)} %finish.1), channel_id=1, replica_groups=mesh['seq'=8,'head'=4] {'seq'}, dimensions={0} | all-to-all | bytes 393216 | tf_op jit(solution)/shard_map/all_to_all | solution.py:549
  47.6 0.8 %order.1 = bf16[2,192,256]{2,1,0:T(8,128)(2,1)} custom-call(bf16[8,96,128]{2,1,0:T(8,128)(2,1)S(1)} %all_to_all.10.blocks_ref), custom_call_target="tpu_custom_call" | custom-call | tf_op jit(solution)/shard_map/order/pallas_call | solution.py:490
Async XLA Ops:
  0.8 5.5 %copy-start.2 = (bf16[192,768]{1,0:T(8,128)(2,1)S(1)}, bf16[192,768]{1,0:T(8,128)(2,1)}, u32[]{:S(2)}) copy-start(bf16[192,768]{1,0:T(8,128)(2,1)} %refs_0_) | copy-start | bytes 884740
  0.8 4.9 %collective-permute-start = (s32[2,256]{1,0:T(2,128)S(1)}, s32[2,256]{1,0:T(2,128)S(1)}, u32[]{:S(2)}, u32[]{:S(2)}) collective-permute-start(s32[2,256]{1,0:T(2,128)S(1)} %codes.1.own_ref), channel_id=1, source_target_pairs={{0,4},{1,5},{2,6},{3,7},{4,0},{5,1},{6,2},{7,3},{8,12},{9,13},{10,... | collective-permute-start | bytes 6152 | tf_op jit(solution)/shard_map/ppermute | solution.py:508
  6.3 14.0 %collective-permute-start.2 = (bf16[192,768]{1,0:T(8,128)(2,1)S(1)}, bf16[192,768]{1,0:T(8,128)(2,1)S(1)}, u32[]{:S(2)}, u32[]{:S(2)}) collective-permute-start(bf16[192,768]{1,0:T(8,128)(2,1)S(1)} %copy-done.2), channel_id=1, source_target_pairs={{0,2},{1,3},{2,0},{3,1},{4,6},{5,7},{6,4},{7,5},{8,10},{9,11},{10,... | collective-permute-start | bytes 884744 | tf_op jit(solution)/shard_map/ppermute | solution.py:508
  8.0 12.4 %collective-permute-start.6 = (bf16[40,576]{1,0:T(8,128)(2,1)S(1)}, bf16[40,576]{1,0:T(8,128)(2,1)S(1)}, u32[]{:S(2)}, u32[]{:S(2)}) collective-permute-start(bf16[40,576]{1,0:T(8,128)(2,1)S(1)} %tables.1.refs_0_), channel_id=1, source_target_pairs={{0,3},{1,2},{2,1},{3,0},{4,7},{5,6},{6,5},{7,4},{8,11},{9,10},{10,... | collective-permute-start | bytes 138248 | tf_op jit(solution)/shard_map/ppermute | solution.py:508
  8.0 12.4 %collective-permute-start.5 = (bf16[40,576]{1,0:T(8,128)(2,1)S(1)}, bf16[40,576]{1,0:T(8,128)(2,1)S(1)}, u32[]{:S(2)}, u32[]{:S(2)}) collective-permute-start(bf16[40,576]{1,0:T(8,128)(2,1)S(1)} %tables.1.refs_0_), channel_id=1, source_target_pairs={{0,2},{1,3},{2,0},{3,1},{4,6},{5,7},{6,4},{7,5},{8,10},{9,11},{10,... | collective-permute-start | bytes 138248 | tf_op jit(solution)/shard_map/ppermute | solution.py:508
  8.7 11.7 %collective-permute-start.4 = (bf16[40,576]{1,0:T(8,128)(2,1)S(1)}, bf16[40,576]{1,0:T(8,128)(2,1)S(1)}, u32[]{:S(2)}, u32[]{:S(2)}) collective-permute-start(bf16[40,576]{1,0:T(8,128)(2,1)S(1)} %tables.1.refs_0_), channel_id=1, source_target_pairs={{0,1},{1,0},{2,3},{3,2},{4,5},{5,4},{6,7},{7,6},{8,9},{9,8},{10,11... | collective-permute-start | bytes 138248 | tf_op jit(solution)/shard_map/ppermute | solution.py:508
  9.9 10.5 %all-to-all-start = ((s32[4,4,256]{2,1,0:T(4,128)}), s32[4,4,256]{2,1,0:T(4,128)S(1)}, u32[]{:S(2)}, u32[]{:S(2)}) async-start(s32[4,4,256]{2,1,0:T(4,128)} %join.1), calls=%async_computation | async-start | bytes 32768 | tf_op jit(solution)/shard_map/all_to_all | solution.py:528
  14.8 8.5 %copy-start.1 = (bf16[3,192,768]{2,1,0:T(8,128)(2,1)S(1)}, bf16[3,192,768]{2,1,0:T(8,128)(2,1)}, u32[]{:S(2)}) copy-start(bf16[3,192,768]{2,1,0:T(8,128)(2,1)} %param.12) | copy-start | bytes 2654212
  14.8 8.5 %copy-start.3 = (bf16[33,768]{1,0:T(8,128)(2,1)S(1)}, bf16[33,768]{1,0:T(8,128)(2,1)}, u32[]{:S(2)}) copy-start(bf16[33,768]{1,0:T(8,128)(2,1)} %refs_7_.1) | copy-start | bytes 152068
  14.8 8.5 %collective-permute-start.1 = (bf16[192,768]{1,0:T(8,128)(2,1)S(1)}, bf16[192,768]{1,0:T(8,128)(2,1)S(1)}, u32[]{:S(2)}, u32[]{:S(2)}) collective-permute-start(bf16[192,768]{1,0:T(8,128)(2,1)S(1)} %copy-done.2), channel_id=1, source_target_pairs={{0,1},{1,0},{2,3},{3,2},{4,5},{5,4},{6,7},{7,6},{8,9},{9,8},{10,11... | collective-permute-start | bytes 884744 | tf_op jit(solution)/shard_map/ppermute | solution.py:508
  20.4 2.9 %collective-permute-start.3 = (bf16[192,768]{1,0:T(8,128)(2,1)S(1)}, bf16[192,768]{1,0:T(8,128)(2,1)S(1)}, u32[]{:S(2)}, u32[]{:S(2)}) collective-permute-start(bf16[192,768]{1,0:T(8,128)(2,1)S(1)} %collective-permute-done.2.refs_2_), channel_id=1, source_target_pairs={{0,1},{1,0},{2,3},{3,2},{4,5},{5,4},{6,7},{7,6},{8,9},{9,8},{10,11... | collective-permute-start | bytes 884744 | tf_op jit(solution)/shard_map/ppermute | solution.py:508
  23.3 12.2 %copy-start = (bf16[192,768]{1,0:T(8,128)(2,1)S(1)}, bf16[192,768]{1,0:T(8,128)(2,1)}, u32[]{:S(2)}) copy-start(bf16[192,768]{1,0:T(8,128)(2,1)} %refs_10_.1) | copy-start | bytes 884740
  26.6 5.7 %collective-permute-start.8 = (bf16[384,128]{1,0:T(8,128)(2,1)S(1)}, bf16[384,128]{1,0:T(8,128)(2,1)S(1)}, u32[]{:S(2)}, u32[]{:S(2)}) collective-permute-start(bf16[384,128]{1,0:T(8,128)(2,1)S(1)} %get-tuple-element.29.refs_0_), channel_id=1, source_target_pairs={{0,2},{1,3},{2,0},{3,1},{4,6},{5,7},{6,4},{7,5},{8,10},{9,11},{10,... | collective-permute-start | bytes 294920 | tf_op jit(solution)/shard_map/ppermute | solution.py:508
  27.3 6.9 %collective-permute-start.11 = (bf16[384,128]{1,0:T(8,128)(2,1)S(1)}, bf16[384,128]{1,0:T(8,128)(2,1)S(1)}, u32[]{:S(2)}, u32[]{:S(2)}) collective-permute-start(bf16[384,128]{1,0:T(8,128)(2,1)S(1)} %get-tuple-element.30.refs_4_), channel_id=1, source_target_pairs={{0,2},{1,3},{2,0},{3,1},{4,6},{5,7},{6,4},{7,5},{8,10},{9,11},{10,... | collective-permute-start | bytes 294920 | tf_op jit(solution)/shard_map/ppermute | solution.py:508
  28.7 5.5 %collective-permute-start.7 = (bf16[384,128]{1,0:T(8,128)(2,1)S(1)}, bf16[384,128]{1,0:T(8,128)(2,1)S(1)}, u32[]{:S(2)}, u32[]{:S(2)}) collective-permute-start(bf16[384,128]{1,0:T(8,128)(2,1)S(1)} %get-tuple-element.29.refs_0_), channel_id=1, source_target_pairs={{0,1},{1,0},{2,3},{3,2},{4,5},{5,4},{6,7},{7,6},{8,9},{9,8},{10,11... | collective-permute-start | bytes 294920 | tf_op jit(solution)/shard_map/ppermute | solution.py:508
  28.9 5.3 %collective-permute-start.10 = (bf16[384,128]{1,0:T(8,128)(2,1)S(1)}, bf16[384,128]{1,0:T(8,128)(2,1)S(1)}, u32[]{:S(2)}, u32[]{:S(2)}) collective-permute-start(bf16[384,128]{1,0:T(8,128)(2,1)S(1)} %get-tuple-element.30.refs_4_), channel_id=1, source_target_pairs={{0,1},{1,0},{2,3},{3,2},{4,5},{5,4},{6,7},{7,6},{8,9},{9,8},{10,11... | collective-permute-start | bytes 294920 | tf_op jit(solution)/shard_map/ppermute | solution.py:508
  32.4 1.8 %collective-permute-start.9 = (bf16[384,128]{1,0:T(8,128)(2,1)S(1)}, bf16[384,128]{1,0:T(8,128)(2,1)S(1)}, u32[]{:S(2)}, u32[]{:S(2)}) collective-permute-start(bf16[384,128]{1,0:T(8,128)(2,1)S(1)} %collective-permute-done.8.refs_2_), channel_id=1, source_target_pairs={{0,1},{1,0},{2,3},{3,2},{4,5},{5,4},{6,7},{7,6},{8,9},{9,8},{10,11... | collective-permute-start | bytes 294920 | tf_op jit(solution)/shard_map/ppermute | solution.py:508
  34.2 1.3 %collective-permute-start.12 = (bf16[384,128]{1,0:T(8,128)(2,1)S(1)}, bf16[384,128]{1,0:T(8,128)(2,1)S(1)}, u32[]{:S(2)}, u32[]{:S(2)}) collective-permute-start(bf16[384,128]{1,0:T(8,128)(2,1)S(1)} %collective-permute-done.11.refs_6_), channel_id=1, source_target_pairs={{0,1},{1,0},{2,3},{3,2},{4,5},{5,4},{6,7},{7,6},{8,9},{9,8},{10,11... | collective-permute-start | bytes 294920 | tf_op jit(solution)/shard_map/ppermute | solution.py:508

commit v14 on v11

--- a/solution.py
+++ b/solution.py
@@ -301,11 +301,12 @@
         own_ref,
         embed_ref,
         col_qkv_ref,
-        *out_refs,
+        *context_refs,
+        mixed_out_ref,
         row_out_ref,
         embed2_ref,
+        weight_ref,
     ) = refs
-    context_refs, mixed_refs = out_refs[:2], out_refs[2:]
     rows = live_ref.shape[0]
     tokens, width = row_context_ref.shape
     pairs = rows // 2
@@ -334,10 +335,7 @@
 
         @pl.when(part == p)
         def _():
-            for c in range(2):
-                mixed_refs[c][...] = mixed[
-                    c * tokens // 2 : (c + 1) * tokens // 2, p * local : (p + 1) * local
-                ]
+            mixed_out_ref[...] = mixed[:, p * local : (p + 1) * local]
 
     normed = layer_norm(mixed).astype(bf16)
 
@@ -349,10 +347,22 @@
         shape = (rows, groups, few, values.shape[1])
         return jnp.swapaxes(values.reshape(shape), 0, 1).reshape(tokens, values.shape[1])
 
+    odd = part % 2
+    for t in range(3):
+        first = pl.multiple_of(t * local + odd * HEAD_DIM, HEAD_DIM)
+        last = pl.multiple_of(t * local + (1 - odd) * LANES, HEAD_DIM)
+        third = (3 + t) * LANES
+        weight_ref[t * LANES : (t + 1) * LANES, :] = col_qkv_ref[pl.ds(first, LANES), :]
+        weight_ref[third : third + HEAD_DIM, :] = col_qkv_ref[pl.ds(last, HEAD_DIM), :]
+        weight_ref[third + HEAD_DIM : third + LANES, :] = jnp.zeros((HEAD_DIM, width), bf16)
     proj = [
-        dot_nt(normed, col_qkv_ref[t * local : (t + 1) * local, :]) for t in range(3)
+        dot_nt(normed, weight_ref[2 * j * LANES : 2 * (j + 1) * LANES, :]) for j in range(3)
     ]
-    proj[0] = proj[0] * HEAD_DIM ** (-0.5)
+    proj = [
+        proj[j][:, k * LANES : (k + 1) * LANES] * (HEAD_DIM ** (-0.5) if (2 * j + k) % 3 == 0 else 1.0)
+        for j in range(3)
+        for k in range(2)
+    ]
     proj = [regroup(values).astype(bf16) for values in proj]
     sub, lan = iota((unit, unit), 0), iota((unit, unit), 1)
     same_column = (sub % few) == (lan % few)
@@ -364,52 +374,56 @@
     chosen = []
     for g in range(groups):
         at = slice(g * unit, (g + 1) * unit)
-        for h in range(local // HEAD_DIM):
-            first = h * HEAD_DIM // LANES * LANES
-            span = slice(first, min(first + LANES, local))
-            query, keys, values = (proj[t][at, span] for t in range(3))
-            if query.shape[1] > HEAD_DIM:
-                inside = iota(query.shape, 1) // HEAD_DIM == h % 2
-                query = jnp.where(inside, query, jnp.zeros_like(query))
-            chosen.append((query, keys, values))
+        query, keys, values = (proj[t][at] for t in range(3))
+        chosen += [(half, keys, values) for half in halves(query)]
+        chosen.append(tuple(proj[3 + t][at] for t in range(3)))
     scores = [jnp.where(visible, dot_nt(query, keys), -jnp.inf) for query, keys, _ in chosen]
     tops = [jnp.max(score, axis=-1, keepdims=True) for score in scores]
     weights = [jnp.exp(score - top) for score, top in zip(scores, tops)]
     shares = [1.0 / jnp.sum(weight, axis=-1, keepdims=True) for weight in weights]
     probs = [(weight * share).astype(bf16) for weight, share in zip(weights, shares)]
     found = [dot_nn(prob, values) for prob, (_, _, values) in zip(probs, chosen)]
-    many = local // HEAD_DIM
     first_head = iota((unit, LANES), 1) < HEAD_DIM
-    blocks = [
-        jnp.concatenate(
-            [jnp.where(first_head, found[g * many], found[g * many + 1]), found[g * many + 2]], 1
-        )
-        for g in range(groups)
-    ]
-    whole = jnp.concatenate(blocks, 0).reshape(groups, rows, few, local)
-    context = jnp.swapaxes(whole, 0, 1).reshape(tokens, local)
-    half, some = tokens // 2, tokens // 4
-    for c in range(2):
-        part_of = context[c * half : (c + 1) * half]
-        context_refs[c][0:half, :] = part_of[:, 0:LANES].astype(bf16)
-        context_refs[c][half : half + some, :] = jnp.concatenate(
-            [part_of[0:some, LANES:local], part_of[some:half, LANES:local]], 1
+
+    def ungroup(blocks):
+        whole = jnp.concatenate(blocks, 0).reshape(groups, rows, few, LANES)
+        return jnp.swapaxes(whole, 0, 1).reshape(tokens, LANES)
+
+    main = ungroup(
+        [jnp.where(first_head, found[3 * g], found[3 * g + 1]) for g in range(groups)]
+    )
+    third = ungroup([found[3 * g + 2] for g in range(groups)])
+    start = 0
+    for context_ref in context_refs:
+        count = context_ref.shape[0] * 2 // 3
+        some = count // 2
+        context_ref[0:count, :] = main[start : start + count].astype(bf16)
+        early = third[start : start + some]
+        late = third[start + some : start + count]
+        left = jnp.where(odd == 1, late, early)
+        right = jnp.where(odd == 1, early, late)
+        context_ref[count : count + some, :] = jnp.concatenate(
+            [left[:, 0:HEAD_DIM], right[:, 0:HEAD_DIM]], 1
         ).astype(bf16)
+        start += count
 
 
 def attend_columns_here(row_outs, live, row_context, own_codes, embed, col_qkv):
     parts = len(row_outs)
     tokens, width = row_context.shape
     local = width // parts
+    half = tokens // 2 * local // LANES
     return pl.pallas_call(
         functools.partial(column_kernel, parts),
         out_shape=(
-            *[jax.ShapeDtypeStruct((tokens // 2 * local // LANES, LANES), bf16)] * 2,
-            *[jax.ShapeDtypeStruct((tokens // 2, local), f32)] * 2,
+            jax.ShapeDtypeStruct((half, LANES), bf16),
+            jax.ShapeDtypeStruct((half, LANES), bf16),
+            jax.ShapeDtypeStruct((tokens, local), f32),
         ),
         scratch_shapes=[
             pltpu.VMEM((parts, local, width), bf16),
             pltpu.VMEM((2 * CODES, 2 * width), bf16),
+            pltpu.VMEM((6 * LANES, width), bf16),
         ],
         cost_estimate=pl.CostEstimate(flops=2 * 10**9, bytes_accessed=10**6, transcendentals=0),
         compiler_params=pltpu.CompilerParams(vmem_limit_bytes=LARGE_VMEM),
@@ -419,36 +433,36 @@
 
 def finish_kernel(parts, groups, *refs):
     context_refs = [refs[:parts], refs[parts : 2 * parts]]
-    mixed_refs = refs[2 * parts : 2 * parts + 2]
-    col_out_ref, out_ref, weight_ref = refs[2 * parts + 2 :]
-    tokens, local = mixed_refs[0].shape
-    some = tokens // 2
+    mixed_ref, col_out_ref, out_ref, context_ref = refs[2 * parts :]
+    tokens, local = mixed_ref.shape
     group = lax.axis_index("seq")
     part = lax.axis_index("head")
-    for p in range(parts):
-        weight_ref[p] = col_out_ref[:, p * local : (p + 1) * local]
-    totals = [ref[...] for ref in mixed_refs]
-    for p in range(parts):
-        weight = weight_ref[part ^ p]
-        rest = weight[:, LANES:local]
-        zero = jnp.zeros_like(rest)
-        left = jnp.concatenate([rest, zero], 1)
-        right = jnp.concatenate([zero, rest], 1)
-        for c in range(2):
-            context = context_refs[c][p]
-            last = context[tokens : tokens + some, :]
-            totals[c] = (
-                totals[c]
-                + dot_nt(context[0:tokens, :], weight[:, 0:LANES])
-                + jnp.concatenate([dot_nt(last, left), dot_nt(last, right)], 0)
-            )
-    slots = groups // 2
-    own = tokens // slots // 2
+    starts = [0, context_refs[0][0].shape[0]]
+    for start, some_refs in zip(starts, context_refs):
+        for p in range(parts):
+            context_ref[part ^ p, start : start + some_refs[p].shape[0], :] = some_refs[p][...]
+    pieces = []
+    for start, some_refs in zip(starts, context_refs):
+        count = some_refs[0].shape[0] * 2 // 3
+        end = start + some_refs[0].shape[0]
+        low = iota((count // 2, LANES), 1) < HEAD_DIM
+        features = []
+        for p in range(0, parts, 2):
+            even = context_ref[p, start + count : end, :]
+            other = context_ref[p + 1, start + count : end, :]
+            early = jnp.where(low, even, other)
+            late = jnp.where(low, other, even)
+            late = jnp.concatenate([late[:, HEAD_DIM:], late[:, 0:HEAD_DIM]], 1)
+            features += [
+                context_ref[p, start : start + count, :],
+                jnp.concatenate([early, late], 0),
+                context_ref[p + 1, start : start + count, :],
+            ]
+        pieces.append(jnp.concatenate(features, 1))
+    total = mixed_ref[...] + dot_nt(jnp.concatenate(pieces, 0), col_out_ref[...])
+    own = tokens // groups // 2
     for d in range(groups):
-        first, second = (
-            totals[d // slots][(2 * (d % slots) + r) * own : (2 * (d % slots) + r + 1) * own, :]
-            for r in range(2)
-        )
+        first, second = (total[(2 * d + r) * own : (2 * d + r + 1) * own, :] for r in range(2))
         rest = jnp.concatenate([first[:, LANES:local], second[:, LANES:local]], 1)
         out_ref[group ^ d] = jnp.concatenate(
             [first[:, 0:LANES], second[:, 0:LANES], rest], 0
@@ -457,16 +471,14 @@
 
 def finish(contexts, mixed, col_out, groups):
     parts = len(contexts[0])
-    tokens, local = mixed[0].shape
+    tokens, local = mixed.shape
     return pl.pallas_call(
         functools.partial(finish_kernel, parts, groups),
-        out_shape=jax.ShapeDtypeStruct(
-            (groups, 2 * tokens // groups * local // LANES, LANES), bf16
-        ),
-        scratch_shapes=[pltpu.VMEM((parts, local, local), bf16)],
+        out_shape=jax.ShapeDtypeStruct((groups, tokens // groups * local // LANES, LANES), bf16),
+        scratch_shapes=[pltpu.VMEM((parts, tokens * local // LANES, LANES), bf16)],
         compiler_params=pltpu.CompilerParams(vmem_limit_bytes=LARGE_VMEM),
         name="finish",
-    )(*contexts[0], *contexts[1], *mixed, col_out)
+    )(*contexts[0], *contexts[1], mixed, col_out)
 
 
 def order_kernel(blocks_ref, out_ref):
@@ -536,7 +548,7 @@
     *codes, near, far = lax.optimization_barrier((*codes, row_out, far))
     row_outs = [row_out, pairwise(near, sibling), far, pairwise(far, sibling)]
     row_context, own_codes, live = attend_rows(tables, codes, rows, cols, own, width)
-    *halves_here, mixed_low, mixed_high = attend_columns_here(
+    *halves_here, mixed = attend_columns_here(
         row_outs, live, row_context, own_codes, embed, col_qkv.reshape(3 * local, width)
     )
     contexts = []
@@ -545,7 +557,7 @@
         contexts.append(
             (context, pairwise(context, sibling), beyond, pairwise(beyond, sibling))
         )
-    blocks = finish(contexts, (mixed_low, mixed_high), col_out, groups)
+    blocks = finish(contexts, mixed, col_out, groups)
     blocks = lax.all_to_all(blocks, "seq", split_axis=0, concat_axis=0, tiled=True)
     return jnp.swapaxes(order(blocks, cols, local), 1, 2)
 

time: 47.1 us -> 46.3 us (0.983)
  Pallas kernels: 10.7 us -> 9.96 us
    pallas_call x1, Pallas kernels: 1.1 us -> 0.51 us  [finish(): pl.pallas_call(functools.partial(finish_kernel, parts, groups), out_shape...]
where the time goes in v14:
time: 46.3 us; the launch traced here: 46.1 us
  blocking collectives  13.9 us (30%)
  starting transfers between devices  12.5 us (27%)
  Pallas kernels  9.96 us (22%)
  waiting for transfers between devices  9.58 us (21%)
    all_to_all x1, blocking collectives, fast_body(): lax.all_to_all(blocks, 'seq', split_axis=0, concat_axis=0, tiled=True)  13.9 us
    ppermute x15, starting transfers between devices, pairwise(): lax.ppermute(value, ('seq', 'head'), [(i, g * parts + p) for i, (g, p) in...  12.5 us
    ppermute x15, waiting for transfers between devices, pairwise(): lax.ppermute(value, ('seq', 'head'), [(i, g * parts + p) for i, (g, p) in...  9.58 us
    pallas_call x1, Pallas kernels, attend_columns_here(): pl.pallas_call(functools.partial(column_kernel, parts), out_shape=(jax.Sh...  3.14 us
    pallas_call x1, Pallas kernels, attend_rows(): pl.pallas_call(functools.partial(row_kernel, parts), out_shape=(jax.Shape...  2.82 us
    pallas_call x1, Pallas kernels, make_tables(): pl.pallas_call(table_kernel, out_shape=jax.ShapeDtypeStruct((TABLE_ROWS,...  1.84 us
  transfers between devices with their start and end apart: 15, of which 6 were waited for; matrix products, arithmetic and copies ran while one was open for 0% of the time, Pallas kernels for 12%

profile of v14, /device:TPU:0, one launch (start us, length us, event | category | flops | bytes accessed | tf_op | source)
XLA Modules:
  0.0 46.1 jit_solution(807332959794376435)
XLA Ops:
  0.0 2.9 %collective-permute-start.3 = (bf16[192,768]{1,0:T(8,128)(2,1)}, bf16[192,768]{1,0:T(8,128)(2,1)S(1)}, u32[]{:S(2)}, u32[]{:S(2)}) collective-permute-start(bf16[192,768]{1,0:T(8,128)(2,1)} %refs_0_.1), channel_id=1, source_target_pairs={{0,2},{1,3},{2,0},{3,1},{4,6},{5,7},{6,4},{7,5},{8,10},{9,11},{10,... | collective-permute-start | bytes 884744 | tf_op jit(solution)/shard_map/ppermute | solution.py:520
  2.9 0.8 %codes.1.own_ref = s32[8,256]{1,0:T(8,128)S(1)} custom-call(s32[2,256]{1,0:T(2,128)} %ids_hbm.1, s32[2]{0:T(128)} %live_hbm.1), custom_call_target="tpu_custom_call" | custom-call | tf_op jit(solution)/shard_map/codes/pallas_call | solution.py:70
  3.8 0.0 copy-start.2
  3.8 1.6 %collective-permute-start = (s32[8,256]{1,0:T(8,128)S(1)}, s32[8,256]{1,0:T(8,128)S(1)}, u32[]{:S(2)}, u32[]{:S(2)}) collective-permute-start(s32[8,256]{1,0:T(8,128)S(1)} %codes.1.own_ref), channel_id=1, source_target_pairs={{0,4},{1,5},{2,6},{3,7},{4,0},{5,1},{6,2},{7,3},{8,12},{9,13},{10,... | collective-permute-start | bytes 24584 | tf_op jit(solution)/shard_map/ppermute | solution.py:520
  5.4 1.8 %tables.1.refs_0_ = bf16[40,576]{1,0:T(8,128)(2,1)S(1)} custom-call(bf16[33,768]{1,0:T(8,128)(2,1)} %refs_7_.1, bf16[3,192,768]{2,1,0:T(8,128)(2,1)} %qkv_hbm), custom_call_target="tpu_custom_call" | custom-call | flops 2000000000 | bytes 884736 | tf_op jit(solution)/shard_map/tables/pallas_call | solution.py:120
  7.2 0.3 collective-permute-done.other_ref
  7.5 1.6 %collective-permute-start.1 = (s32[8,256]{1,0:T(8,128)S(1)}, s32[8,256]{1,0:T(8,128)S(1)}, u32[]{:S(2)}, u32[]{:S(2)}) collective-permute-start(s32[8,256]{1,0:T(8,128)S(1)} %join.2.own_ref), channel_id=1, source_target_pairs={{0,8},{1,9},{2,10},{3,11},{4,12},{5,13},{6,14},{7,15},{8,0},{9,1},... | collective-permute-start | bytes 24584 | tf_op jit(solution)/shard_map/ppermute | solution.py:520
  9.1 0.0 collective-permute-start.8
  9.1 0.6 %collective-permute-start.7 = (bf16[40,576]{1,0:T(8,128)(2,1)S(1)}, bf16[40,576]{1,0:T(8,128)(2,1)S(1)}, u32[]{:S(2)}, u32[]{:S(2)}) collective-permute-start(bf16[40,576]{1,0:T(8,128)(2,1)S(1)} %tables.1.refs_0_), channel_id=1, source_target_pairs={{0,2},{1,3},{2,0},{3,1},{4,6},{5,7},{6,4},{7,5},{8,10},{9,11},{10,... | collective-permute-start | bytes 138248 | tf_op jit(solution)/shard_map/ppermute | solution.py:520
  9.7 1.5 %collective-permute-done.1.other_ref = s32[8,256]{1,0:T(8,128)S(1)} collective-permute-done((s32[8,256]{1,0:T(8,128)S(1)}, s32[8,256]{1,0:T(8,128)S(1)}, u32[]{:S(2)}, u32[]{:S(2)}) %collective-permute-start.1) | collective-permute-done | bytes 8224 | tf_op jit(solution)/shard_map/ppermute | solution.py:520
  11.2 0.0 copy-start.1
  11.2 0.0 copy-start.3
  11.2 0.1 collective-permute-start.6
  11.2 2.7 %collective-permute-start.2 = (s32[8,256]{1,0:T(8,128)S(1)}, s32[8,256]{1,0:T(8,128)S(1)}, u32[]{:S(2)}, u32[]{:S(2)}) collective-permute-start(s32[8,256]{1,0:T(8,128)S(1)} %join.3.refs_4_), channel_id=1, source_target_pairs={{0,16},{1,17},{2,18},{3,19},{4,20},{5,21},{6,22},{7,23},{8,24},{9,... | collective-permute-start | bytes 24584 | tf_op jit(solution)/shard_map/ppermute | solution.py:520
  13.9 2.0 %collective-permute-done.2.refs_5_ = s32[8,256]{1,0:T(8,128)S(1)} collective-permute-done((s32[8,256]{1,0:T(8,128)S(1)}, s32[8,256]{1,0:T(8,128)S(1)}, u32[]{:S(2)}, u32[]{:S(2)}) %collective-permute-start.2) | collective-permute-done | bytes 8224 | tf_op jit(solution)/shard_map/ppermute | solution.py:520
  15.9 0.0 collective-permute-done.3.refs_2_
  15.9 0.0 copy-done.2
  15.9 0.0 collective-permute-start.4
  15.9 0.5 %collective-permute-start.5 = (bf16[192,768]{1,0:T(8,128)(2,1)S(1)}, bf16[192,768]{1,0:T(8,128)(2,1)S(1)}, u32[]{:S(2)}, u32[]{:S(2)}) collective-permute-start(bf16[192,768]{1,0:T(8,128)(2,1)S(1)} %collective-permute-done.3.refs_2_), channel_id=1, source_target_pairs={{0,1},{1,0},{2,3},{3,2},{4,5},{5,4},{6,7},{7,6},{8,9},{9,8},{10,11... | collective-permute-start | bytes 884744 | tf_op jit(solution)/shard_map/ppermute | solution.py:520
  16.4 0.0 collective-permute-done.8.refs_3_
  16.4 0.0 collective-permute-done.7.refs_2_
  16.4 0.0 collective-permute-done.6.refs_1_
  16.4 2.8 %row_attention.1 = (bf16[512,768]{1,0:T(8,128)(2,1)S(1)}, bf16[256,128]{1,0:T(8,128)(2,1)S(1)}, f32[16,128]{1,0:T(8,128)S(1)}) custom-call(bf16[40,576]{1,0:T(8,128)(2,1)S(1)} %tables.1.refs_0_, bf16[40,576]{1,0:T(8,128)(2,1)S(1)} %collective-permute-done.6.refs_1_, bf16[40,576]{1,0:T(8,128)(2,1)S(1)} %collective-permute-done.7.refs_2_, ...), custom_call_target="tpu_custom_call" | custom-call | flops 3000000000 | bytes 1000000 | tf_op jit(solution)/shard_map/row_attention/pallas_call | solution.py:275
  19.2 0.0 collective-permute-done.4.refs_1_
  19.2 0.0 collective-permute-done.5.refs_3_
  19.2 0.0 copy-done.1
  19.3 0.0 copy-done.3
  19.3 0.0 copy-start
  19.3 3.1 %column_attention.1 = (bf16[384,128]{1,0:T(8,128)(2,1)S(1)}, bf16[384,128]{1,0:T(8,128)(2,1)S(1)}, f32[512,192]{1,0:T(8,128)S(1)}) custom-call(bf16[192,768]{1,0:T(8,128)(2,1)S(1)} %copy-done.2, bf16[192,768]{1,0:T(8,128)(2,1)S(1)} %collective-permute-done.4.refs_1_, bf16[192,768]{1,0:T(8,128)(2,1)S(1)} %collective-permute-done.3.refs_2_, ...), custom_call_target="tpu_custom_call" | custom-call | flops 2000000000 | bytes 1000000 | tf_op jit(solution)/shard_map/column_attention/pallas_call | solution.py:416
  22.4 0.4 collective-permute-start.10
  22.8 1.7 %collective-permute-start.13 = (bf16[384,128]{1,0:T(8,128)(2,1)S(1)}, bf16[384,128]{1,0:T(8,128)(2,1)S(1)}, u32[]{:S(2)}, u32[]{:S(2)}) collective-permute-start(bf16[384,128]{1,0:T(8,128)(2,1)S(1)} %get-tuple-element.35.refs_4_), channel_id=1, source_target_pairs={{0,2},{1,3},{2,0},{3,1},{4,6},{5,7},{6,4},{7,5},{8,10},{9,11},{10,... | collective-permute-start | bytes 294920 | tf_op jit(solution)/shard_map/ppermute | solution.py:520
  24.5 0.0 collective-permute-start.9
  24.5 0.5 %collective-permute-start.12 = (bf16[384,128]{1,0:T(8,128)(2,1)S(1)}, bf16[384,128]{1,0:T(8,128)(2,1)S(1)}, u32[]{:S(2)}, u32[]{:S(2)}) collective-permute-start(bf16[384,128]{1,0:T(8,128)(2,1)S(1)} %get-tuple-element.35.refs_4_), channel_id=1, source_target_pairs={{0,1},{1,0},{2,3},{3,2},{4,5},{5,4},{6,7},{7,6},{8,9},{9,8},{10,11... | collective-permute-start | bytes 294920 | tf_op jit(solution)/shard_map/ppermute | solution.py:520
  25.0 3.1 %collective-permute-done.10.refs_2_ = bf16[384,128]{1,0:T(8,128)(2,1)S(1)} collective-permute-done((bf16[384,128]{1,0:T(8,128)(2,1)S(1)}, bf16[384,128]{1,0:T(8,128)(2,1)S(1)}, u32[]{:S(2)}, u32[]{:S(2)}) %collective-permute-start.10) | collective-permute-done | bytes 98336 | tf_op jit(solution)/shard_map/ppermute | solution.py:520
  28.1 0.0 collective-permute-start.11
  28.1 1.4 %collective-permute-done.13.refs_6_ = bf16[384,128]{1,0:T(8,128)(2,1)S(1)} collective-permute-done((bf16[384,128]{1,0:T(8,128)(2,1)S(1)}, bf16[384,128]{1,0:T(8,128)(2,1)S(1)}, u32[]{:S(2)}, u32[]{:S(2)}) %collective-permute-start.13) | collective-permute-done | bytes 98336 | tf_op jit(solution)/shard_map/ppermute | solution.py:520
  29.5 0.0 collective-permute-start.14
  29.5 0.0 collective-permute-done.9.refs_1_
  29.6 0.0 collective-permute-done.12.refs_5_
  29.6 0.0 collective-permute-done.11.refs_3_
  29.6 1.3 %collective-permute-done.14.refs_7_ = bf16[384,128]{1,0:T(8,128)(2,1)S(1)} collective-permute-done((bf16[384,128]{1,0:T(8,128)(2,1)S(1)}, bf16[384,128]{1,0:T(8,128)(2,1)S(1)}, u32[]{:S(2)}, u32[]{:S(2)}) %collective-permute-start.14) | collective-permute-done | bytes 98336 | tf_op jit(solution)/shard_map/ppermute | solution.py:520
  30.8 0.0 copy-done
  30.8 0.5 %finish.1 = bf16[8,96,128]{2,1,0:T(8,128)(2,1)S(1)} custom-call(bf16[384,128]{1,0:T(8,128)(2,1)S(1)} %get-tuple-element.34.refs_0_, bf16[384,128]{1,0:T(8,128)(2,1)S(1)} %collective-permute-done.9.refs_1_, bf16[384,128]{1,0:T(8,128)(2,1)S(1)} %collective-permute-done.10.refs_2_, bf16[384,128]{1,0:T(8,128)(2,1)S(1)} %collective-permute-done.11.refs_3_, ...), custom_call_target="tpu_custom_call" | custom-call | tf_op jit(solution)/shard_map/finish/pallas_call | solution.py:475
  31.4 13.9 %all_to_all.5.blocks_ref = bf16[8,96,128]{2,1,0:T(8,128)(2,1)S(1)} all-to-all(bf16[8,96,128]{2,1,0:T(8,128)(2,1)S(1)} %finish.1), channel_id=1, replica_groups=mesh['seq'=8,'head'=4] {'seq'}, dimensions={0} | all-to-all | bytes 393216 | tf_op jit(solution)/shard_map/all_to_all | solution.py:561
  45.3 0.8 %order.1 = bf16[2,192,256]{2,1,0:T(8,128)(2,1)} custom-call(bf16[8,96,128]{2,1,0:T(8,128)(2,1)S(1)} %all_to_all.5.blocks_ref), custom_call_target="tpu_custom_call" | custom-call | tf_op jit(solution)/shard_map/order/pallas_call | solution.py:502
  (2 shorter events, 0.0 us)
Async XLA Ops:
  0.0 15.9 %collective-permute-start.3 = (bf16[192,768]{1,0:T(8,128)(2,1)}, bf16[192,768]{1,0:T(8,128)(2,1)S(1)}, u32[]{:S(2)}, u32[]{:S(2)}) collective-permute-start(bf16[192,768]{1,0:T(8,128)(2,1)} %refs_0_.1), channel_id=1, source_target_pairs={{0,2},{1,3},{2,0},{3,1},{4,6},{5,7},{6,4},{7,5},{8,10},{9,11},{10,... | collective-permute-start | bytes 884744 | tf_op jit(solution)/shard_map/ppermute | solution.py:520
  3.8 12.1 %copy-start.2 = (bf16[192,768]{1,0:T(8,128)(2,1)S(1)}, bf16[192,768]{1,0:T(8,128)(2,1)}, u32[]{:S(2)}) copy-start(bf16[192,768]{1,0:T(8,128)(2,1)} %refs_0_.1) | copy-start | bytes 884740
  3.8 3.7 %collective-permute-start = (s32[8,256]{1,0:T(8,128)S(1)}, s32[8,256]{1,0:T(8,128)S(1)}, u32[]{:S(2)}, u32[]{:S(2)}) collective-permute-start(s32[8,256]{1,0:T(8,128)S(1)} %codes.1.own_ref), channel_id=1, source_target_pairs={{0,4},{1,5},{2,6},{3,7},{4,0},{5,1},{6,2},{7,3},{8,12},{9,13},{10,... | collective-permute-start | bytes 24584 | tf_op jit(solution)/shard_map/ppermute | solution.py:520
  7.5 3.7 %collective-permute-start.1 = (s32[8,256]{1,0:T(8,128)S(1)}, s32[8,256]{1,0:T(8,128)S(1)}, u32[]{:S(2)}, u32[]{:S(2)}) collective-permute-start(s32[8,256]{1,0:T(8,128)S(1)} %join.2.own_ref), channel_id=1, source_target_pairs={{0,8},{1,9},{2,10},{3,11},{4,12},{5,13},{6,14},{7,15},{8,0},{9,1},... | collective-permute-start | bytes 24584 | tf_op jit(solution)/shard_map/ppermute | solution.py:520
  9.1 7.3 %collective-permute-start.8 = (bf16[40,576]{1,0:T(8,128)(2,1)S(1)}, bf16[40,576]{1,0:T(8,128)(2,1)S(1)}, u32[]{:S(2)}, u32[]{:S(2)}) collective-permute-start(bf16[40,576]{1,0:T(8,128)(2,1)S(1)} %tables.1.refs_0_), channel_id=1, source_target_pairs={{0,3},{1,2},{2,1},{3,0},{4,7},{5,6},{6,5},{7,4},{8,11},{9,10},{10,... | collective-permute-start | bytes 138248 | tf_op jit(solution)/shard_map/ppermute | solution.py:520
  9.1 7.3 %collective-permute-start.7 = (bf16[40,576]{1,0:T(8,128)(2,1)S(1)}, bf16[40,576]{1,0:T(8,128)(2,1)S(1)}, u32[]{:S(2)}, u32[]{:S(2)}) collective-permute-start(bf16[40,576]{1,0:T(8,128)(2,1)S(1)} %tables.1.refs_0_), channel_id=1, source_target_pairs={{0,2},{1,3},{2,0},{3,1},{4,6},{5,7},{6,4},{7,5},{8,10},{9,11},{10,... | collective-permute-start | bytes 138248 | tf_op jit(solution)/shard_map/ppermute | solution.py:520
  11.2 8.1 %copy-start.1 = (bf16[3,192,768]{2,1,0:T(8,128)(2,1)S(1)}, bf16[3,192,768]{2,1,0:T(8,128)(2,1)}, u32[]{:S(2)}) copy-start(bf16[3,192,768]{2,1,0:T(8,128)(2,1)} %param.12) | copy-start | bytes 2654212
  11.2 8.1 %copy-start.3 = (bf16[33,768]{1,0:T(8,128)(2,1)S(1)}, bf16[33,768]{1,0:T(8,128)(2,1)}, u32[]{:S(2)}) copy-start(bf16[33,768]{1,0:T(8,128)(2,1)} %refs_7_.1) | copy-start | bytes 152068
  11.2 5.2 %collective-permute-start.6 = (bf16[40,576]{1,0:T(8,128)(2,1)S(1)}, bf16[40,576]{1,0:T(8,128)(2,1)S(1)}, u32[]{:S(2)}, u32[]{:S(2)}) collective-permute-start(bf16[40,576]{1,0:T(8,128)(2,1)S(1)} %tables.1.refs_0_), channel_id=1, source_target_pairs={{0,1},{1,0},{2,3},{3,2},{4,5},{5,4},{6,7},{7,6},{8,9},{9,8},{10,11... | collective-permute-start | bytes 138248 | tf_op jit(solution)/shard_map/ppermute | solution.py:520
  11.2 4.6 %collective-permute-start.2 = (s32[8,256]{1,0:T(8,128)S(1)}, s32[8,256]{1,0:T(8,128)S(1)}, u32[]{:S(2)}, u32[]{:S(2)}) collective-permute-start(s32[8,256]{1,0:T(8,128)S(1)} %join.3.refs_4_), channel_id=1, source_target_pairs={{0,16},{1,17},{2,18},{3,19},{4,20},{5,21},{6,22},{7,23},{8,24},{9,... | collective-permute-start | bytes 24584 | tf_op jit(solution)/shard_map/ppermute | solution.py:520
  15.9 3.4 %collective-permute-start.4 = (bf16[192,768]{1,0:T(8,128)(2,1)S(1)}, bf16[192,768]{1,0:T(8,128)(2,1)S(1)}, u32[]{:S(2)}, u32[]{:S(2)}) collective-permute-start(bf16[192,768]{1,0:T(8,128)(2,1)S(1)} %copy-done.2), channel_id=1, source_target_pairs={{0,1},{1,0},{2,3},{3,2},{4,5},{5,4},{6,7},{7,6},{8,9},{9,8},{10,11... | collective-permute-start | bytes 884744 | tf_op jit(solution)/shard_map/ppermute | solution.py:520
  15.9 3.4 %collective-permute-start.5 = (bf16[192,768]{1,0:T(8,128)(2,1)S(1)}, bf16[192,768]{1,0:T(8,128)(2,1)S(1)}, u32[]{:S(2)}, u32[]{:S(2)}) collective-permute-start(bf16[192,768]{1,0:T(8,128)(2,1)S(1)} %collective-permute-done.3.refs_2_), channel_id=1, source_target_pairs={{0,1},{1,0},{2,3},{3,2},{4,5},{5,4},{6,7},{7,6},{8,9},{9,8},{10,11... | collective-permute-start | bytes 884744 | tf_op jit(solution)/shard_map/ppermute | solution.py:520
  19.3 11.6 %copy-start = (bf16[192,768]{1,0:T(8,128)(2,1)S(1)}, bf16[192,768]{1,0:T(8,128)(2,1)}, u32[]{:S(2)}) copy-start(bf16[192,768]{1,0:T(8,128)(2,1)} %refs_9_.1) | copy-start | bytes 884740
  22.4 5.7 %collective-permute-start.10 = (bf16[384,128]{1,0:T(8,128)(2,1)S(1)}, bf16[384,128]{1,0:T(8,128)(2,1)S(1)}, u32[]{:S(2)}, u32[]{:S(2)}) collective-permute-start(bf16[384,128]{1,0:T(8,128)(2,1)S(1)} %get-tuple-element.34.refs_0_), channel_id=1, source_target_pairs={{0,2},{1,3},{2,0},{3,1},{4,6},{5,7},{6,4},{7,5},{8,10},{9,11},{10,... | collective-permute-start | bytes 294920 | tf_op jit(solution)/shard_map/ppermute | solution.py:520
  22.8 6.7 %collective-permute-start.13 = (bf16[384,128]{1,0:T(8,128)(2,1)S(1)}, bf16[384,128]{1,0:T(8,128)(2,1)S(1)}, u32[]{:S(2)}, u32[]{:S(2)}) collective-permute-start(bf16[384,128]{1,0:T(8,128)(2,1)S(1)} %get-tuple-element.35.refs_4_), channel_id=1, source_target_pairs={{0,2},{1,3},{2,0},{3,1},{4,6},{5,7},{6,4},{7,5},{8,10},{9,11},{10,... | collective-permute-start | bytes 294920 | tf_op jit(solution)/shard_map/ppermute | solution.py:520
  24.5 5.0 %collective-permute-start.9 = (bf16[384,128]{1,0:T(8,128)(2,1)S(1)}, bf16[384,128]{1,0:T(8,128)(2,1)S(1)}, u32[]{:S(2)}, u32[]{:S(2)}) collective-permute-start(bf16[384,128]{1,0:T(8,128)(2,1)S(1)} %get-tuple-element.34.refs_0_), channel_id=1, source_target_pairs={{0,1},{1,0},{2,3},{3,2},{4,5},{5,4},{6,7},{7,6},{8,9},{9,8},{10,11... | collective-permute-start | bytes 294920 | tf_op jit(solution)/shard_map/ppermute | solution.py:520
  24.5 5.0 %collective-permute-start.12 = (bf16[384,128]{1,0:T(8,128)(2,1)S(1)}, bf16[384,128]{1,0:T(8,128)(2,1)S(1)}, u32[]{:S(2)}, u32[]{:S(2)}) collective-permute-start(bf16[384,128]{1,0:T(8,128)(2,1)S(1)} %get-tuple-element.35.refs_4_), channel_id=1, source_target_pairs={{0,1},{1,0},{2,3},{3,2},{4,5},{5,4},{6,7},{7,6},{8,9},{9,8},{10,11... | collective-permute-start | bytes 294920 | tf_op jit(solution)/shard_map/ppermute | solution.py:520
  28.1 1.5 %collective-permute-start.11 = (bf16[384,128]{1,0:T(8,128)(2,1)S(1)}, bf16[384,128]{1,0:T(8,128)(2,1)S(1)}, u32[]{:S(2)}, u32[]{:S(2)}) collective-permute-start(bf16[384,128]{1,0:T(8,128)(2,1)S(1)} %collective-permute-done.10.refs_2_), channel_id=1, source_target_pairs={{0,1},{1,0},{2,3},{3,2},{4,5},{5,4},{6,7},{7,6},{8,9},{9,8},{10,11... | collective-permute-start | bytes 294920 | tf_op jit(solution)/shard_map/ppermute | solution.py:520
  29.5 1.3 %collective-permute-start.14 = (bf16[384,128]{1,0:T(8,128)(2,1)S(1)}, bf16[384,128]{1,0:T(8,128)(2,1)S(1)}, u32[]{:S(2)}, u32[]{:S(2)}) collective-permute-start(bf16[384,128]{1,0:T(8,128)(2,1)S(1)} %collective-permute-done.13.refs_6_), channel_id=1, source_target_pairs={{0,1},{1,0},{2,3},{3,2},{4,5},{5,4},{6,7},{7,6},{8,9},{9,8},{10,11... | collective-permute-start | bytes 294920 | tf_op jit(solution)/shard_map/ppermute | solution.py:520

commit v15 on v14

--- a/solution.py
+++ b/solution.py
@@ -533,20 +533,20 @@
     coded, row_qkv = lax.optimization_barrier((coded, row_qkv))
     received = pairwise(coded, lambda g, p: (g ^ 1, p))
     table = make_tables(embed, row_qkv)
+    tables = [table, None, pairwise(table, across), None]
     step = 2
     while step < groups:
         coded = join(coded, received, rows_here * step // 2)
         if step == 2:
             coded, table = lax.optimization_barrier((coded, table))
-            far_tables = [pairwise(table, to) for to in (across, opposite)]
+            tables[3] = pairwise(table, opposite)
+        elif step == 4:
+            coded, table, row_out, far = lax.optimization_barrier((coded, table, row_out, far))
+            tables[1] = pairwise(table, sibling)
+            row_outs = [row_out, pairwise(row_out, sibling), far, pairwise(far, sibling)]
         received = pairwise(coded, lambda g, p, step=step: (g ^ step, p))
         step *= 2
     codes = (coded, received)
-    coded, late_table = lax.optimization_barrier((coded, table))
-    codes = (coded, received)
-    tables = [table, pairwise(late_table, sibling)] + far_tables
-    *codes, near, far = lax.optimization_barrier((*codes, row_out, far))
-    row_outs = [row_out, pairwise(near, sibling), far, pairwise(far, sibling)]
     row_context, own_codes, live = attend_rows(tables, codes, rows, cols, own, width)
     *halves_here, mixed = attend_columns_here(
         row_outs, live, row_context, own_codes, embed, col_qkv.reshape(3 * local, width)
@@ -648,7 +648,7 @@
     local = row_out.shape[0]
     fits = (
         parts == 4
-        and groups >= 4
+        and groups >= 8
         and groups & (groups - 1) == 0
         and rows * 8 == LANES
         and rows_here == 2

time: 46.3 us -> 45.7 us (0.987)
  blocking collectives: 13.9 us -> 12.9 us
  waiting for transfers between devices: 9.58 us -> 10.1 us
    all_to_all x1, blocking collectives: 13.9 us -> 12.9 us  [fast_body(): lax.all_to_all(blocks, 'seq', split_axis=0, concat_axis=0, tiled=True)]
    ppermute x15, waiting for transfers between devices: 9.58 us -> 10.1 us  [pairwise(): lax.ppermute(value, ('seq', 'head'), [(i, g * parts + p) for i, (g, p) in...]
  transfers between devices with their start and end apart: 15 -> 15, of which waited for: 6 -> 8; matrix products, arithmetic and copies ran while one was open for 0% -> 0% of each run, Pallas kernels for 12% -> 12%
where the time goes in v15:
time: 45.7 us; the launch traced here: 45.5 us
  blocking collectives  12.9 us (28%)
  starting transfers between devices  12.5 us (27%)
  waiting for transfers between devices  10.1 us (22%)
  Pallas kernels  9.96 us (22%)
    all_to_all x1, blocking collectives, fast_body(): lax.all_to_all(blocks, 'seq', split_axis=0, concat_axis=0, tiled=True)  12.9 us
    ppermute x15, starting transfers between devices, pairwise(): lax.ppermute(value, ('seq', 'head'), [(i, g * parts + p) for i, (g, p) in...  12.5 us
    ppermute x15, waiting for transfers between devices, pairwise(): lax.ppermute(value, ('seq', 'head'), [(i, g * parts + p) for i, (g, p) in...  10.1 us
    pallas_call x1, Pallas kernels, attend_columns_here(): pl.pallas_call(functools.partial(column_kernel, parts), out_shape=(jax.Sh...  3.13 us
    pallas_call x1, Pallas kernels, attend_rows(): pl.pallas_call(functools.partial(row_kernel, parts), out_shape=(jax.Shape...  2.82 us
    pallas_call x1, Pallas kernels, make_tables(): pl.pallas_call(table_kernel, out_shape=jax.ShapeDtypeStruct((TABLE_ROWS,...  1.84 us
  transfers between devices with their start and end apart: 15, of which 8 were waited for; matrix products, arithmetic and copies ran while one was open for 0% of the time, Pallas kernels for 12%

profile of v15, /device:TPU:0, one launch (start us, length us, event | category | flops | bytes accessed | tf_op | source)
XLA Modules:
  0.0 45.5 jit_solution(18309536639251571309)
XLA Ops:
  0.0 2.9 %collective-permute-start.2 = (bf16[192,768]{1,0:T(8,128)(2,1)}, bf16[192,768]{1,0:T(8,128)(2,1)S(1)}, u32[]{:S(2)}, u32[]{:S(2)}) collective-permute-start(bf16[192,768]{1,0:T(8,128)(2,1)} %refs_0_), channel_id=1, source_target_pairs={{0,2},{1,3},{2,0},{3,1},{4,6},{5,7},{6,4},{7,5},{8,10},{9,11},{10,... | collective-permute-start | bytes 884744 | tf_op jit(solution)/shard_map/ppermute | solution.py:520
  2.9 0.8 %codes.1.own_ref = s32[8,256]{1,0:T(8,128)S(1)} custom-call(s32[2,256]{1,0:T(2,128)} %ids_hbm.1, s32[2]{0:T(128)} %live_hbm.1), custom_call_target="tpu_custom_call" | custom-call | tf_op jit(solution)/shard_map/codes/pallas_call | solution.py:70
  3.8 0.0 copy-start.2
  3.8 1.6 %collective-permute-start = (s32[8,256]{1,0:T(8,128)S(1)}, s32[8,256]{1,0:T(8,128)S(1)}, u32[]{:S(2)}, u32[]{:S(2)}) collective-permute-start(s32[8,256]{1,0:T(8,128)S(1)} %codes.1.own_ref), channel_id=1, source_target_pairs={{0,4},{1,5},{2,6},{3,7},{4,0},{5,1},{6,2},{7,3},{8,12},{9,13},{10,... | collective-permute-start | bytes 24584 | tf_op jit(solution)/shard_map/ppermute | solution.py:520
  5.4 1.8 %tables.1.refs_0_ = bf16[40,576]{1,0:T(8,128)(2,1)S(1)} custom-call(bf16[33,768]{1,0:T(8,128)(2,1)} %refs_7_.1, bf16[3,192,768]{2,1,0:T(8,128)(2,1)} %qkv_hbm), custom_call_target="tpu_custom_call" | custom-call | flops 2000000000 | bytes 884736 | tf_op jit(solution)/shard_map/tables/pallas_call | solution.py:120
  7.2 0.3 collective-permute-done.other_ref
  7.5 1.6 %collective-permute-start.1 = (s32[8,256]{1,0:T(8,128)S(1)}, s32[8,256]{1,0:T(8,128)S(1)}, u32[]{:S(2)}, u32[]{:S(2)}) collective-permute-start(s32[8,256]{1,0:T(8,128)S(1)} %join.2.own_ref), channel_id=1, source_target_pairs={{0,8},{1,9},{2,10},{3,11},{4,12},{5,13},{6,14},{7,15},{8,0},{9,1},... | collective-permute-start | bytes 24584 | tf_op jit(solution)/shard_map/ppermute | solution.py:520
  9.1 0.5 %collective-permute-start.6 = (bf16[40,576]{1,0:T(8,128)(2,1)S(1)}, bf16[40,576]{1,0:T(8,128)(2,1)S(1)}, u32[]{:S(2)}, u32[]{:S(2)}) collective-permute-start(bf16[40,576]{1,0:T(8,128)(2,1)S(1)} %tables.1.refs_0_), channel_id=1, source_target_pairs={{0,2},{1,3},{2,0},{3,1},{4,6},{5,7},{6,4},{7,5},{8,10},{9,11},{10,... | collective-permute-start | bytes 138248 | tf_op jit(solution)/shard_map/ppermute | solution.py:520
  9.6 0.0 collective-permute-start.7
  9.6 1.5 %collective-permute-done.1.other_ref = s32[8,256]{1,0:T(8,128)S(1)} collective-permute-done((s32[8,256]{1,0:T(8,128)S(1)}, s32[8,256]{1,0:T(8,128)S(1)}, u32[]{:S(2)}, u32[]{:S(2)}) %collective-permute-start.1) | collective-permute-done | bytes 8224 | tf_op jit(solution)/shard_map/ppermute | solution.py:520
  11.2 0.0 copy-start.1
  11.2 0.0 copy-start.3
  11.2 0.0 collective-permute-done.2.refs_2_
  11.2 0.1 collective-permute-start.5
  11.3 0.0 copy-done.2
  11.3 0.4 collective-permute-start.3
  11.8 0.1 collective-permute-start.4
  11.8 1.9 %collective-permute-done.6.refs_2_ = bf16[40,576]{1,0:T(8,128)(2,1)S(1)} collective-permute-done((bf16[40,576]{1,0:T(8,128)(2,1)S(1)}, bf16[40,576]{1,0:T(8,128)(2,1)S(1)}, u32[]{:S(2)}, u32[]{:S(2)}) %collective-permute-start.6) | collective-permute-done | bytes 46112 | tf_op jit(solution)/shard_map/ppermute | solution.py:520
  13.7 2.6 %collective-permute-start.8 = (s32[8,256]{1,0:T(8,128)S(1)}, s32[8,256]{1,0:T(8,128)S(1)}, u32[]{:S(2)}, u32[]{:S(2)}) collective-permute-start(s32[8,256]{1,0:T(8,128)S(1)} %join.3.refs_4_), channel_id=1, source_target_pairs={{0,16},{1,17},{2,18},{3,19},{4,20},{5,21},{6,22},{7,23},{8,24},{9,... | collective-permute-start | bytes 24584 | tf_op jit(solution)/shard_map/ppermute | solution.py:520
  16.3 0.0 collective-permute-done.7.refs_3_
  16.3 2.0 %collective-permute-done.8.refs_5_ = s32[8,256]{1,0:T(8,128)S(1)} collective-permute-done((s32[8,256]{1,0:T(8,128)S(1)}, s32[8,256]{1,0:T(8,128)S(1)}, u32[]{:S(2)}, u32[]{:S(2)}) %collective-permute-start.8) | collective-permute-done | bytes 8224 | tf_op jit(solution)/shard_map/ppermute | solution.py:520
  18.3 0.0 collective-permute-done.5.refs_1_
  18.3 2.8 %row_attention.1 = (bf16[512,768]{1,0:T(8,128)(2,1)S(1)}, bf16[256,128]{1,0:T(8,128)(2,1)S(1)}, f32[16,128]{1,0:T(8,128)S(1)}) custom-call(bf16[40,576]{1,0:T(8,128)(2,1)S(1)} %tables.1.refs_0_, bf16[40,576]{1,0:T(8,128)(2,1)S(1)} %collective-permute-done.5.refs_1_, bf16[40,576]{1,0:T(8,128)(2,1)S(1)} %collective-permute-done.6.refs_2_, ...), custom_call_target="tpu_custom_call" | custom-call | flops 3000000000 | bytes 1000000 | tf_op jit(solution)/shard_map/row_attention/pallas_call | solution.py:275
  21.1 0.0 collective-permute-done.3.refs_1_
  21.1 0.0 collective-permute-done.4.refs_3_
  21.1 0.0 copy-done.1
  21.1 0.0 copy-done.3
  21.1 0.0 copy-start
  21.1 3.1 %column_attention.1 = (bf16[384,128]{1,0:T(8,128)(2,1)S(1)}, bf16[384,128]{1,0:T(8,128)(2,1)S(1)}, f32[512,192]{1,0:T(8,128)S(1)}) custom-call(bf16[192,768]{1,0:T(8,128)(2,1)S(1)} %copy-done.2, bf16[192,768]{1,0:T(8,128)(2,1)S(1)} %collective-permute-done.3.refs_1_, bf16[192,768]{1,0:T(8,128)(2,1)S(1)} %collective-permute-done.2.refs_2_, ...), custom_call_target="tpu_custom_call" | custom-call | flops 2000000000 | bytes 1000000 | tf_op jit(solution)/shard_map/column_attention/pallas_call | solution.py:416
  24.3 0.1 collective-permute-start.10
  24.4 2.0 %collective-permute-start.13 = (bf16[384,128]{1,0:T(8,128)(2,1)S(1)}, bf16[384,128]{1,0:T(8,128)(2,1)S(1)}, u32[]{:S(2)}, u32[]{:S(2)}) collective-permute-start(bf16[384,128]{1,0:T(8,128)(2,1)S(1)} %get-tuple-element.31.refs_4_), channel_id=1, source_target_pairs={{0,2},{1,3},{2,0},{3,1},{4,6},{5,7},{6,4},{7,5},{8,10},{9,11},{10,... | collective-permute-start | bytes 294920 | tf_op jit(solution)/shard_map/ppermute | solution.py:520
  26.4 0.0 collective-permute-start.9
  26.4 0.5 %collective-permute-start.12 = (bf16[384,128]{1,0:T(8,128)(2,1)S(1)}, bf16[384,128]{1,0:T(8,128)(2,1)S(1)}, u32[]{:S(2)}, u32[]{:S(2)}) collective-permute-start(bf16[384,128]{1,0:T(8,128)(2,1)S(1)} %get-tuple-element.31.refs_4_), channel_id=1, source_target_pairs={{0,1},{1,0},{2,3},{3,2},{4,5},{5,4},{6,7},{7,6},{8,9},{9,8},{10,11... | collective-permute-start | bytes 294920 | tf_op jit(solution)/shard_map/ppermute | solution.py:520
  26.9 2.1 %collective-permute-done.10.refs_2_ = bf16[384,128]{1,0:T(8,128)(2,1)S(1)} collective-permute-done((bf16[384,128]{1,0:T(8,128)(2,1)S(1)}, bf16[384,128]{1,0:T(8,128)(2,1)S(1)}, u32[]{:S(2)}, u32[]{:S(2)}) %collective-permute-start.10) | collective-permute-done | bytes 98336 | tf_op jit(solution)/shard_map/ppermute | solution.py:520
  29.0 0.0 collective-permute-start.11
  29.0 1.0 %collective-permute-done.13.refs_6_ = bf16[384,128]{1,0:T(8,128)(2,1)S(1)} collective-permute-done((bf16[384,128]{1,0:T(8,128)(2,1)S(1)}, bf16[384,128]{1,0:T(8,128)(2,1)S(1)}, u32[]{:S(2)}, u32[]{:S(2)}) %collective-permute-start.13) | collective-permute-done | bytes 98336 | tf_op jit(solution)/shard_map/ppermute | solution.py:520
  30.0 0.0 collective-permute-start.14
  30.0 0.0 collective-permute-done.9.refs_1_
  30.0 0.0 collective-permute-done.12.refs_5_
  30.0 0.2 collective-permute-done.11.refs_3_
  30.3 1.1 %collective-permute-done.14.refs_7_ = bf16[384,128]{1,0:T(8,128)(2,1)S(1)} collective-permute-done((bf16[384,128]{1,0:T(8,128)(2,1)S(1)}, bf16[384,128]{1,0:T(8,128)(2,1)S(1)}, u32[]{:S(2)}, u32[]{:S(2)}) %collective-permute-start.14) | collective-permute-done | bytes 98336 | tf_op jit(solution)/shard_map/ppermute | solution.py:520
  31.3 0.0 copy-done
  31.3 0.5 %finish.1 = bf16[8,96,128]{2,1,0:T(8,128)(2,1)S(1)} custom-call(bf16[384,128]{1,0:T(8,128)(2,1)S(1)} %get-tuple-element.30.refs_0_, bf16[384,128]{1,0:T(8,128)(2,1)S(1)} %collective-permute-done.9.refs_1_, bf16[384,128]{1,0:T(8,128)(2,1)S(1)} %collective-permute-done.10.refs_2_, bf16[384,128]{1,0:T(8,128)(2,1)S(1)} %collective-permute-done.11.refs_3_, ...), custom_call_target="tpu_custom_call" | custom-call | tf_op jit(solution)/shard_map/finish/pallas_call | solution.py:475
  31.8 12.9 %all_to_all.5.blocks_ref = bf16[8,96,128]{2,1,0:T(8,128)(2,1)S(1)} all-to-all(bf16[8,96,128]{2,1,0:T(8,128)(2,1)S(1)} %finish.1), channel_id=1, replica_groups=mesh['seq'=8,'head'=4] {'seq'}, dimensions={0} | all-to-all | bytes 393216 | tf_op jit(solution)/shard_map/all_to_all | solution.py:561
  44.7 0.8 %order.1 = bf16[2,192,256]{2,1,0:T(8,128)(2,1)} custom-call(bf16[8,96,128]{2,1,0:T(8,128)(2,1)S(1)} %all_to_all.5.blocks_ref), custom_call_target="tpu_custom_call" | custom-call | tf_op jit(solution)/shard_map/order/pallas_call | solution.py:502
  (2 shorter events, 0.0 us)
Async XLA Ops:
  0.0 11.2 %collective-permute-start.2 = (bf16[192,768]{1,0:T(8,128)(2,1)}, bf16[192,768]{1,0:T(8,128)(2,1)S(1)}, u32[]{:S(2)}, u32[]{:S(2)}) collective-permute-start(bf16[192,768]{1,0:T(8,128)(2,1)} %refs_0_), channel_id=1, source_target_pairs={{0,2},{1,3},{2,0},{3,1},{4,6},{5,7},{6,4},{7,5},{8,10},{9,11},{10,... | collective-permute-start | bytes 884744 | tf_op jit(solution)/shard_map/ppermute | solution.py:520
  3.8 7.6 %copy-start.2 = (bf16[192,768]{1,0:T(8,128)(2,1)S(1)}, bf16[192,768]{1,0:T(8,128)(2,1)}, u32[]{:S(2)}) copy-start(bf16[192,768]{1,0:T(8,128)(2,1)} %refs_0_) | copy-start | bytes 884740
  3.8 3.7 %collective-permute-start = (s32[8,256]{1,0:T(8,128)S(1)}, s32[8,256]{1,0:T(8,128)S(1)}, u32[]{:S(2)}, u32[]{:S(2)}) collective-permute-start(s32[8,256]{1,0:T(8,128)S(1)} %codes.1.own_ref), channel_id=1, source_target_pairs={{0,4},{1,5},{2,6},{3,7},{4,0},{5,1},{6,2},{7,3},{8,12},{9,13},{10,... | collective-permute-start | bytes 24584 | tf_op jit(solution)/shard_map/ppermute | solution.py:520
  7.5 3.7 %collective-permute-start.1 = (s32[8,256]{1,0:T(8,128)S(1)}, s32[8,256]{1,0:T(8,128)S(1)}, u32[]{:S(2)}, u32[]{:S(2)}) collective-permute-start(s32[8,256]{1,0:T(8,128)S(1)} %join.2.own_ref), channel_id=1, source_target_pairs={{0,8},{1,9},{2,10},{3,11},{4,12},{5,13},{6,14},{7,15},{8,0},{9,1},... | collective-permute-start | bytes 24584 | tf_op jit(solution)/shard_map/ppermute | solution.py:520
  9.1 4.6 %collective-permute-start.6 = (bf16[40,576]{1,0:T(8,128)(2,1)S(1)}, bf16[40,576]{1,0:T(8,128)(2,1)S(1)}, u32[]{:S(2)}, u32[]{:S(2)}) collective-permute-start(bf16[40,576]{1,0:T(8,128)(2,1)S(1)} %tables.1.refs_0_), channel_id=1, source_target_pairs={{0,2},{1,3},{2,0},{3,1},{4,6},{5,7},{6,4},{7,5},{8,10},{9,11},{10,... | collective-permute-start | bytes 138248 | tf_op jit(solution)/shard_map/ppermute | solution.py:520
  9.6 6.7 %collective-permute-start.7 = (bf16[40,576]{1,0:T(8,128)(2,1)S(1)}, bf16[40,576]{1,0:T(8,128)(2,1)S(1)}, u32[]{:S(2)}, u32[]{:S(2)}) collective-permute-start(bf16[40,576]{1,0:T(8,128)(2,1)S(1)} %tables.1.refs_0_), channel_id=1, source_target_pairs={{0,3},{1,2},{2,1},{3,0},{4,7},{5,6},{6,5},{7,4},{8,11},{9,10},{10,... | collective-permute-start | bytes 138248 | tf_op jit(solution)/shard_map/ppermute | solution.py:520
  11.2 9.9 %copy-start.1 = (bf16[3,192,768]{2,1,0:T(8,128)(2,1)S(1)}, bf16[3,192,768]{2,1,0:T(8,128)(2,1)}, u32[]{:S(2)}) copy-start(bf16[3,192,768]{2,1,0:T(8,128)(2,1)} %param.12) | copy-start | bytes 2654212
  11.2 10.0 %copy-start.3 = (bf16[33,768]{1,0:T(8,128)(2,1)S(1)}, bf16[33,768]{1,0:T(8,128)(2,1)}, u32[]{:S(2)}) copy-start(bf16[33,768]{1,0:T(8,128)(2,1)} %refs_7_.1) | copy-start | bytes 152068
  11.2 7.1 %collective-permute-start.5 = (bf16[40,576]{1,0:T(8,128)(2,1)S(1)}, bf16[40,576]{1,0:T(8,128)(2,1)S(1)}, u32[]{:S(2)}, u32[]{:S(2)}) collective-permute-start(bf16[40,576]{1,0:T(8,128)(2,1)S(1)} %tables.1.refs_0_), channel_id=1, source_target_pairs={{0,1},{1,0},{2,3},{3,2},{4,5},{5,4},{6,7},{7,6},{8,9},{9,8},{10,11... | collective-permute-start | bytes 138248 | tf_op jit(solution)/shard_map/ppermute | solution.py:520
  11.3 9.8 %collective-permute-start.3 = (bf16[192,768]{1,0:T(8,128)(2,1)S(1)}, bf16[192,768]{1,0:T(8,128)(2,1)S(1)}, u32[]{:S(2)}, u32[]{:S(2)}) collective-permute-start(bf16[192,768]{1,0:T(8,128)(2,1)S(1)} %copy-done.2), channel_id=1, source_target_pairs={{0,1},{1,0},{2,3},{3,2},{4,5},{5,4},{6,7},{7,6},{8,9},{9,8},{10,11... | collective-permute-start | bytes 884744 | tf_op jit(solution)/shard_map/ppermute | solution.py:520
  11.8 9.3 %collective-permute-start.4 = (bf16[192,768]{1,0:T(8,128)(2,1)S(1)}, bf16[192,768]{1,0:T(8,128)(2,1)S(1)}, u32[]{:S(2)}, u32[]{:S(2)}) collective-permute-start(bf16[192,768]{1,0:T(8,128)(2,1)S(1)} %collective-permute-done.2.refs_2_), channel_id=1, source_target_pairs={{0,1},{1,0},{2,3},{3,2},{4,5},{5,4},{6,7},{7,6},{8,9},{9,8},{10,11... | collective-permute-start | bytes 884744 | tf_op jit(solution)/shard_map/ppermute | solution.py:520
  13.7 4.5 %collective-permute-start.8 = (s32[8,256]{1,0:T(8,128)S(1)}, s32[8,256]{1,0:T(8,128)S(1)}, u32[]{:S(2)}, u32[]{:S(2)}) collective-permute-start(s32[8,256]{1,0:T(8,128)S(1)} %join.3.refs_4_), channel_id=1, source_target_pairs={{0,16},{1,17},{2,18},{3,19},{4,20},{5,21},{6,22},{7,23},{8,24},{9,... | collective-permute-start | bytes 24584 | tf_op jit(solution)/shard_map/ppermute | solution.py:520
  21.1 10.2 %copy-start = (bf16[192,768]{1,0:T(8,128)(2,1)S(1)}, bf16[192,768]{1,0:T(8,128)(2,1)}, u32[]{:S(2)}) copy-start(bf16[192,768]{1,0:T(8,128)(2,1)} %refs_9_.1) | copy-start | bytes 884740
  24.3 4.7 %collective-permute-start.10 = (bf16[384,128]{1,0:T(8,128)(2,1)S(1)}, bf16[384,128]{1,0:T(8,128)(2,1)S(1)}, u32[]{:S(2)}, u32[]{:S(2)}) collective-permute-start(bf16[384,128]{1,0:T(8,128)(2,1)S(1)} %get-tuple-element.30.refs_0_), channel_id=1, source_target_pairs={{0,2},{1,3},{2,0},{3,1},{4,6},{5,7},{6,4},{7,5},{8,10},{9,11},{10,... | collective-permute-start | bytes 294920 | tf_op jit(solution)/shard_map/ppermute | solution.py:520
  24.4 5.6 %collective-permute-start.13 = (bf16[384,128]{1,0:T(8,128)(2,1)S(1)}, bf16[384,128]{1,0:T(8,128)(2,1)S(1)}, u32[]{:S(2)}, u32[]{:S(2)}) collective-permute-start(bf16[384,128]{1,0:T(8,128)(2,1)S(1)} %get-tuple-element.31.refs_4_), channel_id=1, source_target_pairs={{0,2},{1,3},{2,0},{3,1},{4,6},{5,7},{6,4},{7,5},{8,10},{9,11},{10,... | collective-permute-start | bytes 294920 | tf_op jit(solution)/shard_map/ppermute | solution.py:520
  26.4 3.6 %collective-permute-start.9 = (bf16[384,128]{1,0:T(8,128)(2,1)S(1)}, bf16[384,128]{1,0:T(8,128)(2,1)S(1)}, u32[]{:S(2)}, u32[]{:S(2)}) collective-permute-start(bf16[384,128]{1,0:T(8,128)(2,1)S(1)} %get-tuple-element.30.refs_0_), channel_id=1, source_target_pairs={{0,1},{1,0},{2,3},{3,2},{4,5},{5,4},{6,7},{7,6},{8,9},{9,8},{10,11... | collective-permute-start | bytes 294920 | tf_op jit(solution)/shard_map/ppermute | solution.py:520
  26.4 3.6 %collective-permute-start.12 = (bf16[384,128]{1,0:T(8,128)(2,1)S(1)}, bf16[384,128]{1,0:T(8,128)(2,1)S(1)}, u32[]{:S(2)}, u32[]{:S(2)}) collective-permute-start(bf16[384,128]{1,0:T(8,128)(2,1)S(1)} %get-tuple-element.31.refs_4_), channel_id=1, source_target_pairs={{0,1},{1,0},{2,3},{3,2},{4,5},{5,4},{6,7},{7,6},{8,9},{9,8},{10,11... | collective-permute-start | bytes 294920 | tf_op jit(solution)/shard_map/ppermute | solution.py:520
  29.0 1.3 %collective-permute-start.11 = (bf16[384,128]{1,0:T(8,128)(2,1)S(1)}, bf16[384,128]{1,0:T(8,128)(2,1)S(1)}, u32[]{:S(2)}, u32[]{:S(2)}) collective-permute-start(bf16[384,128]{1,0:T(8,128)(2,1)S(1)} %collective-permute-done.10.refs_2_), channel_id=1, source_target_pairs={{0,1},{1,0},{2,3},{3,2},{4,5},{5,4},{6,7},{7,6},{8,9},{9,8},{10,11... | collective-permute-start | bytes 294920 | tf_op jit(solution)/shard_map/ppermute | solution.py:520
  30.0 1.3 %collective-permute-start.14 = (bf16[384,128]{1,0:T(8,128)(2,1)S(1)}, bf16[384,128]{1,0:T(8,128)(2,1)S(1)}, u32[]{:S(2)}, u32[]{:S(2)}) collective-permute-start(bf16[384,128]{1,0:T(8,128)(2,1)S(1)} %collective-permute-done.13.refs_6_), channel_id=1, source_target_pairs={{0,1},{1,0},{2,3},{3,2},{4,5},{5,4},{6,7},{7,6},{8,9},{9,8},{10,11... | collective-permute-start | bytes 294920 | tf_op jit(solution)/shard_map/ppermute | solution.py:520

commit v16 on v15

--- a/solution.py
+++ b/solution.py
@@ -538,12 +538,13 @@
     while step < groups:
         coded = join(coded, received, rows_here * step // 2)
         if step == 2:
-            coded, table = lax.optimization_barrier((coded, table))
+            coded, table, row_out = lax.optimization_barrier((coded, table, row_out))
             tables[3] = pairwise(table, opposite)
+            near = pairwise(row_out, sibling)
         elif step == 4:
-            coded, table, row_out, far = lax.optimization_barrier((coded, table, row_out, far))
+            coded, table, near, far = lax.optimization_barrier((coded, table, near, far))
             tables[1] = pairwise(table, sibling)
-            row_outs = [row_out, pairwise(row_out, sibling), far, pairwise(far, sibling)]
+            row_outs = [row_out, near, far, pairwise(far, sibling)]
         received = pairwise(coded, lambda g, p, step=step: (g ^ step, p))
         step *= 2
     codes = (coded, received)

time: 45.7 us -> 46.7 us (1.022)
  starting transfers between devices: 12.5 us -> 13.5 us
    ppermute x15, starting transfers between devices: 12.5 us -> 13.5 us  [pairwise(): lax.ppermute(value, ('seq', 'head'), [(i, g * parts + p) for i, (g, p) in...]
  transfers between devices with their start and end apart: 15 -> 15, of which waited for: 8 -> 7; matrix products, arithmetic and copies ran while one was open for 0% -> 0% of each run, Pallas kernels for 12% -> 10%
where the time goes in v16:
time: 46.7 us; the launch traced here: 46.5 us
  starting transfers between devices  13.5 us (29%)
  blocking collectives  12.9 us (28%)
  waiting for transfers between devices  10 us (21%)
  Pallas kernels  9.96 us (21%)
    ppermute x15, starting transfers between devices, pairwise(): lax.ppermute(value, ('seq', 'head'), [(i, g * parts + p) for i, (g, p) in...  13.5 us
    all_to_all x1, blocking collectives, fast_body(): lax.all_to_all(blocks, 'seq', split_axis=0, concat_axis=0, tiled=True)  12.9 us
    ppermute x15, waiting for transfers between devices, pairwise(): lax.ppermute(value, ('seq', 'head'), [(i, g * parts + p) for i, (g, p) in...  10 us
    pallas_call x1, Pallas kernels, attend_columns_here(): pl.pallas_call(functools.partial(column_kernel, parts), out_shape=(jax.Sh...  3.14 us
    pallas_call x1, Pallas kernels, attend_rows(): pl.pallas_call(functools.partial(row_kernel, parts), out_shape=(jax.Shape...  2.82 us
    pallas_call x1, Pallas kernels, make_tables(): pl.pallas_call(table_kernel, out_shape=jax.ShapeDtypeStruct((TABLE_ROWS,...  1.84 us
  transfers between devices with their start and end apart: 15, of which 7 were waited for; matrix products, arithmetic and copies ran while one was open for 0% of the time, Pallas kernels for 10%

profile of v16, /device:TPU:0, one launch (start us, length us, event | category | flops | bytes accessed | tf_op | source)
XLA Modules:
  0.0 46.5 jit_solution(13827779604924873490)
XLA Ops:
  0.0 0.8 %codes.1.own_ref = s32[8,256]{1,0:T(8,128)S(1)} custom-call(s32[2,256]{1,0:T(2,128)} %ids_hbm.1, s32[2]{0:T(128)} %live_hbm.1), custom_call_target="tpu_custom_call" | custom-call | tf_op jit(solution)/shard_map/codes/pallas_call | solution.py:70
  0.8 0.0 copy-start.2
  0.8 3.0 %collective-permute-start = (s32[8,256]{1,0:T(8,128)S(1)}, s32[8,256]{1,0:T(8,128)S(1)}, u32[]{:S(2)}, u32[]{:S(2)}) collective-permute-start(s32[8,256]{1,0:T(8,128)S(1)} %codes.1.own_ref), channel_id=1, source_target_pairs={{0,4},{1,5},{2,6},{3,7},{4,0},{5,1},{6,2},{7,3},{8,12},{9,13},{10,... | collective-permute-start | bytes 24584 | tf_op jit(solution)/shard_map/ppermute | solution.py:520
  3.9 1.5 %collective-permute-start.3 = (bf16[192,768]{1,0:T(8,128)(2,1)}, bf16[192,768]{1,0:T(8,128)(2,1)S(1)}, u32[]{:S(2)}, u32[]{:S(2)}) collective-permute-start(bf16[192,768]{1,0:T(8,128)(2,1)} %refs_0_), channel_id=1, source_target_pairs={{0,2},{1,3},{2,0},{3,1},{4,6},{5,7},{6,4},{7,5},{8,10},{9,11},{10,... | collective-permute-start | bytes 884744 | tf_op jit(solution)/shard_map/ppermute | solution.py:520
  5.4 1.8 %tables.1.refs_0_ = bf16[40,576]{1,0:T(8,128)(2,1)S(1)} custom-call(bf16[33,768]{1,0:T(8,128)(2,1)} %refs_7_.1, bf16[3,192,768]{2,1,0:T(8,128)(2,1)} %qkv_hbm), custom_call_target="tpu_custom_call" | custom-call | flops 2000000000 | bytes 884736 | tf_op jit(solution)/shard_map/tables/pallas_call | solution.py:120
  7.2 0.0 collective-permute-done.other_ref
  7.2 0.0 copy-done.2
  7.2 0.1 collective-permute-start.2
  7.3 1.6 %collective-permute-start.1 = (s32[8,256]{1,0:T(8,128)S(1)}, s32[8,256]{1,0:T(8,128)S(1)}, u32[]{:S(2)}, u32[]{:S(2)}) collective-permute-start(s32[8,256]{1,0:T(8,128)S(1)} %join.2.own_ref), channel_id=1, source_target_pairs={{0,8},{1,9},{2,10},{3,11},{4,12},{5,13},{6,14},{7,15},{8,0},{9,1},... | collective-permute-start | bytes 24584 | tf_op jit(solution)/shard_map/ppermute | solution.py:520
  9.0 0.5 %collective-permute-start.6 = (bf16[40,576]{1,0:T(8,128)(2,1)S(1)}, bf16[40,576]{1,0:T(8,128)(2,1)S(1)}, u32[]{:S(2)}, u32[]{:S(2)}) collective-permute-start(bf16[40,576]{1,0:T(8,128)(2,1)S(1)} %tables.1.refs_0_), channel_id=1, source_target_pairs={{0,2},{1,3},{2,0},{3,1},{4,6},{5,7},{6,4},{7,5},{8,10},{9,11},{10,... | collective-permute-start | bytes 138248 | tf_op jit(solution)/shard_map/ppermute | solution.py:520
  9.5 1.0 %collective-permute-start.7 = (bf16[40,576]{1,0:T(8,128)(2,1)S(1)}, bf16[40,576]{1,0:T(8,128)(2,1)S(1)}, u32[]{:S(2)}, u32[]{:S(2)}) collective-permute-start(bf16[40,576]{1,0:T(8,128)(2,1)S(1)} %tables.1.refs_0_), channel_id=1, source_target_pairs={{0,3},{1,2},{2,1},{3,0},{4,7},{5,6},{6,5},{7,4},{8,11},{9,10},{10,... | collective-permute-start | bytes 138248 | tf_op jit(solution)/shard_map/ppermute | solution.py:520
  10.5 0.6 %collective-permute-done.1.other_ref = s32[8,256]{1,0:T(8,128)S(1)} collective-permute-done((s32[8,256]{1,0:T(8,128)S(1)}, s32[8,256]{1,0:T(8,128)S(1)}, u32[]{:S(2)}, u32[]{:S(2)}) %collective-permute-start.1) | collective-permute-done | bytes 8224 | tf_op jit(solution)/shard_map/ppermute | solution.py:520
  11.0 0.0 copy-start.1
  11.1 0.0 copy-start.3
  11.1 2.3 %collective-permute-done.3.refs_2_ = bf16[192,768]{1,0:T(8,128)(2,1)S(1)} collective-permute-done((bf16[192,768]{1,0:T(8,128)(2,1)}, bf16[192,768]{1,0:T(8,128)(2,1)S(1)}, u32[]{:S(2)}, u32[]{:S(2)}) %collective-permute-start.3) | collective-permute-done | bytes 294944 | tf_op jit(solution)/shard_map/ppermute | solution.py:520
  13.3 0.0 collective-permute-done.2.refs_1_
  13.3 0.0 collective-permute-start.5
  13.3 0.5 %collective-permute-start.4 = (bf16[192,768]{1,0:T(8,128)(2,1)S(1)}, bf16[192,768]{1,0:T(8,128)(2,1)S(1)}, u32[]{:S(2)}, u32[]{:S(2)}) collective-permute-start(bf16[192,768]{1,0:T(8,128)(2,1)S(1)} %collective-permute-done.3.refs_2_), channel_id=1, source_target_pairs={{0,1},{1,0},{2,3},{3,2},{4,5},{5,4},{6,7},{7,6},{8,9},{9,8},{10,11... | collective-permute-start | bytes 884744 | tf_op jit(solution)/shard_map/ppermute | solution.py:520
  13.8 2.6 %collective-permute-start.8 = (s32[8,256]{1,0:T(8,128)S(1)}, s32[8,256]{1,0:T(8,128)S(1)}, u32[]{:S(2)}, u32[]{:S(2)}) collective-permute-start(s32[8,256]{1,0:T(8,128)S(1)} %join.3.refs_4_), channel_id=1, source_target_pairs={{0,16},{1,17},{2,18},{3,19},{4,20},{5,21},{6,22},{7,23},{8,24},{9,... | collective-permute-start | bytes 24584 | tf_op jit(solution)/shard_map/ppermute | solution.py:520
  16.4 0.0 collective-permute-done.6.refs_2_
  16.4 0.0 collective-permute-done.7.refs_3_
  16.4 2.0 %collective-permute-done.8.refs_5_ = s32[8,256]{1,0:T(8,128)S(1)} collective-permute-done((s32[8,256]{1,0:T(8,128)S(1)}, s32[8,256]{1,0:T(8,128)S(1)}, u32[]{:S(2)}, u32[]{:S(2)}) %collective-permute-start.8) | collective-permute-done | bytes 8224 | tf_op jit(solution)/shard_map/ppermute | solution.py:520
  18.4 0.0 collective-permute-done.5.refs_1_
  18.4 2.8 %row_attention.1 = (bf16[512,768]{1,0:T(8,128)(2,1)S(1)}, bf16[256,128]{1,0:T(8,128)(2,1)S(1)}, f32[16,128]{1,0:T(8,128)S(1)}) custom-call(bf16[40,576]{1,0:T(8,128)(2,1)S(1)} %tables.1.refs_0_, bf16[40,576]{1,0:T(8,128)(2,1)S(1)} %collective-permute-done.5.refs_1_, bf16[40,576]{1,0:T(8,128)(2,1)S(1)} %collective-permute-done.6.refs_2_, ...), custom_call_target="tpu_custom_call" | custom-call | flops 3000000000 | bytes 1000000 | tf_op jit(solution)/shard_map/row_attention/pallas_call | solution.py:275
  21.2 0.0 collective-permute-done.4.refs_3_
  21.2 0.0 copy-done.1
  21.2 0.0 copy-done.3
  21.2 0.0 copy-start
  21.3 3.1 %column_attention.1 = (bf16[384,128]{1,0:T(8,128)(2,1)S(1)}, bf16[384,128]{1,0:T(8,128)(2,1)S(1)}, f32[512,192]{1,0:T(8,128)S(1)}) custom-call(bf16[192,768]{1,0:T(8,128)(2,1)S(1)} %copy-done.2, bf16[192,768]{1,0:T(8,128)(2,1)S(1)} %collective-permute-done.2.refs_1_, bf16[192,768]{1,0:T(8,128)(2,1)S(1)} %collective-permute-done.3.refs_2_, ...), custom_call_target="tpu_custom_call" | custom-call | flops 2000000000 | bytes 1000000 | tf_op jit(solution)/shard_map/column_attention/pallas_call | solution.py:416
  24.4 1.9 %collective-permute-start.10 = (bf16[384,128]{1,0:T(8,128)(2,1)S(1)}, bf16[384,128]{1,0:T(8,128)(2,1)S(1)}, u32[]{:S(2)}, u32[]{:S(2)}) collective-permute-start(bf16[384,128]{1,0:T(8,128)(2,1)S(1)} %get-tuple-element.32.refs_0_), channel_id=1, source_target_pairs={{0,2},{1,3},{2,0},{3,1},{4,6},{5,7},{6,4},{7,5},{8,10},{9,11},{10,... | collective-permute-start | bytes 294920 | tf_op jit(solution)/shard_map/ppermute | solution.py:520
  26.3 0.2 collective-permute-start.13
  26.5 0.0 collective-permute-start.9
  26.5 0.5 %collective-permute-start.12 = (bf16[384,128]{1,0:T(8,128)(2,1)S(1)}, bf16[384,128]{1,0:T(8,128)(2,1)S(1)}, u32[]{:S(2)}, u32[]{:S(2)}) collective-permute-start(bf16[384,128]{1,0:T(8,128)(2,1)S(1)} %get-tuple-element.33.refs_4_), channel_id=1, source_target_pairs={{0,1},{1,0},{2,3},{3,2},{4,5},{5,4},{6,7},{7,6},{8,9},{9,8},{10,11... | collective-permute-start | bytes 294920 | tf_op jit(solution)/shard_map/ppermute | solution.py:520
  27.0 2.7 %collective-permute-done.10.refs_2_ = bf16[384,128]{1,0:T(8,128)(2,1)S(1)} collective-permute-done((bf16[384,128]{1,0:T(8,128)(2,1)S(1)}, bf16[384,128]{1,0:T(8,128)(2,1)S(1)}, u32[]{:S(2)}, u32[]{:S(2)}) %collective-permute-start.10) | collective-permute-done | bytes 98336 | tf_op jit(solution)/shard_map/ppermute | solution.py:520
  29.7 0.0 collective-permute-start.11
  29.7 1.2 %collective-permute-done.13.refs_6_ = bf16[384,128]{1,0:T(8,128)(2,1)S(1)} collective-permute-done((bf16[384,128]{1,0:T(8,128)(2,1)S(1)}, bf16[384,128]{1,0:T(8,128)(2,1)S(1)}, u32[]{:S(2)}, u32[]{:S(2)}) %collective-permute-start.13) | collective-permute-done | bytes 98336 | tf_op jit(solution)/shard_map/ppermute | solution.py:520
  30.9 0.0 collective-permute-start.14
  30.9 0.0 collective-permute-done.9.refs_1_
  30.9 0.0 collective-permute-done.12.refs_5_
  30.9 0.1 collective-permute-done.11.refs_3_
  31.0 1.2 %collective-permute-done.14.refs_7_ = bf16[384,128]{1,0:T(8,128)(2,1)S(1)} collective-permute-done((bf16[384,128]{1,0:T(8,128)(2,1)S(1)}, bf16[384,128]{1,0:T(8,128)(2,1)S(1)}, u32[]{:S(2)}, u32[]{:S(2)}) %collective-permute-start.14) | collective-permute-done | bytes 98336 | tf_op jit(solution)/shard_map/ppermute | solution.py:520
  32.2 0.0 copy-done
  32.2 0.5 %finish.1 = bf16[8,96,128]{2,1,0:T(8,128)(2,1)S(1)} custom-call(bf16[384,128]{1,0:T(8,128)(2,1)S(1)} %get-tuple-element.32.refs_0_, bf16[384,128]{1,0:T(8,128)(2,1)S(1)} %collective-permute-done.9.refs_1_, bf16[384,128]{1,0:T(8,128)(2,1)S(1)} %collective-permute-done.10.refs_2_, bf16[384,128]{1,0:T(8,128)(2,1)S(1)} %collective-permute-done.11.refs_3_, ...), custom_call_target="tpu_custom_call" | custom-call | tf_op jit(solution)/shard_map/finish/pallas_call | solution.py:475
  32.7 12.9 %all_to_all.5.blocks_ref = bf16[8,96,128]{2,1,0:T(8,128)(2,1)S(1)} all-to-all(bf16[8,96,128]{2,1,0:T(8,128)(2,1)S(1)} %finish.1), channel_id=1, replica_groups=mesh['seq'=8,'head'=4] {'seq'}, dimensions={0} | all-to-all | bytes 393216 | tf_op jit(solution)/shard_map/all_to_all | solution.py:562
  45.7 0.8 %order.1 = bf16[2,192,256]{2,1,0:T(8,128)(2,1)} custom-call(bf16[8,96,128]{2,1,0:T(8,128)(2,1)S(1)} %all_to_all.5.blocks_ref), custom_call_target="tpu_custom_call" | custom-call | tf_op jit(solution)/shard_map/order/pallas_call | solution.py:502
  (2 shorter events, 0.0 us)
Async XLA Ops:
  0.8 6.4 %copy-start.2 = (bf16[192,768]{1,0:T(8,128)(2,1)S(1)}, bf16[192,768]{1,0:T(8,128)(2,1)}, u32[]{:S(2)}) copy-start(bf16[192,768]{1,0:T(8,128)(2,1)} %refs_0_) | copy-start | bytes 884740
  0.8 6.4 %collective-permute-start = (s32[8,256]{1,0:T(8,128)S(1)}, s32[8,256]{1,0:T(8,128)S(1)}, u32[]{:S(2)}, u32[]{:S(2)}) collective-permute-start(s32[8,256]{1,0:T(8,128)S(1)} %codes.1.own_ref), channel_id=1, source_target_pairs={{0,4},{1,5},{2,6},{3,7},{4,0},{5,1},{6,2},{7,3},{8,12},{9,13},{10,... | collective-permute-start | bytes 24584 | tf_op jit(solution)/shard_map/ppermute | solution.py:520
  3.9 9.4 %collective-permute-start.3 = (bf16[192,768]{1,0:T(8,128)(2,1)}, bf16[192,768]{1,0:T(8,128)(2,1)S(1)}, u32[]{:S(2)}, u32[]{:S(2)}) collective-permute-start(bf16[192,768]{1,0:T(8,128)(2,1)} %refs_0_), channel_id=1, source_target_pairs={{0,2},{1,3},{2,0},{3,1},{4,6},{5,7},{6,4},{7,5},{8,10},{9,11},{10,... | collective-permute-start | bytes 884744 | tf_op jit(solution)/shard_map/ppermute | solution.py:520
  7.2 6.1 %collective-permute-start.2 = (bf16[192,768]{1,0:T(8,128)(2,1)S(1)}, bf16[192,768]{1,0:T(8,128)(2,1)S(1)}, u32[]{:S(2)}, u32[]{:S(2)}) collective-permute-start(bf16[192,768]{1,0:T(8,128)(2,1)S(1)} %copy-done.2), channel_id=1, source_target_pairs={{0,1},{1,0},{2,3},{3,2},{4,5},{5,4},{6,7},{7,6},{8,9},{9,8},{10,11... | collective-permute-start | bytes 884744 | tf_op jit(solution)/shard_map/ppermute | solution.py:520
  7.3 3.7 %collective-permute-start.1 = (s32[8,256]{1,0:T(8,128)S(1)}, s32[8,256]{1,0:T(8,128)S(1)}, u32[]{:S(2)}, u32[]{:S(2)}) collective-permute-start(s32[8,256]{1,0:T(8,128)S(1)} %join.2.own_ref), channel_id=1, source_target_pairs={{0,8},{1,9},{2,10},{3,11},{4,12},{5,13},{6,14},{7,15},{8,0},{9,1},... | collective-permute-start | bytes 24584 | tf_op jit(solution)/shard_map/ppermute | solution.py:520
  9.0 7.5 %collective-permute-start.6 = (bf16[40,576]{1,0:T(8,128)(2,1)S(1)}, bf16[40,576]{1,0:T(8,128)(2,1)S(1)}, u32[]{:S(2)}, u32[]{:S(2)}) collective-permute-start(bf16[40,576]{1,0:T(8,128)(2,1)S(1)} %tables.1.refs_0_), channel_id=1, source_target_pairs={{0,2},{1,3},{2,0},{3,1},{4,6},{5,7},{6,4},{7,5},{8,10},{9,11},{10,... | collective-permute-start | bytes 138248 | tf_op jit(solution)/shard_map/ppermute | solution.py:520
  9.5 6.9 %collective-permute-start.7 = (bf16[40,576]{1,0:T(8,128)(2,1)S(1)}, bf16[40,576]{1,0:T(8,128)(2,1)S(1)}, u32[]{:S(2)}, u32[]{:S(2)}) collective-permute-start(bf16[40,576]{1,0:T(8,128)(2,1)S(1)} %tables.1.refs_0_), channel_id=1, source_target_pairs={{0,3},{1,2},{2,1},{3,0},{4,7},{5,6},{6,5},{7,4},{8,11},{9,10},{10,... | collective-permute-start | bytes 138248 | tf_op jit(solution)/shard_map/ppermute | solution.py:520
  11.0 10.2 %copy-start.1 = (bf16[3,192,768]{2,1,0:T(8,128)(2,1)S(1)}, bf16[3,192,768]{2,1,0:T(8,128)(2,1)}, u32[]{:S(2)}) copy-start(bf16[3,192,768]{2,1,0:T(8,128)(2,1)} %param.12) | copy-start | bytes 2654212
  11.1 10.2 %copy-start.3 = (bf16[33,768]{1,0:T(8,128)(2,1)S(1)}, bf16[33,768]{1,0:T(8,128)(2,1)}, u32[]{:S(2)}) copy-start(bf16[33,768]{1,0:T(8,128)(2,1)} %refs_7_.1) | copy-start | bytes 152068
  13.3 5.1 %collective-permute-start.5 = (bf16[40,576]{1,0:T(8,128)(2,1)S(1)}, bf16[40,576]{1,0:T(8,128)(2,1)S(1)}, u32[]{:S(2)}, u32[]{:S(2)}) collective-permute-start(bf16[40,576]{1,0:T(8,128)(2,1)S(1)} %tables.1.refs_0_), channel_id=1, source_target_pairs={{0,1},{1,0},{2,3},{3,2},{4,5},{5,4},{6,7},{7,6},{8,9},{9,8},{10,11... | collective-permute-start | bytes 138248 | tf_op jit(solution)/shard_map/ppermute | solution.py:520
  13.3 7.9 %collective-permute-start.4 = (bf16[192,768]{1,0:T(8,128)(2,1)S(1)}, bf16[192,768]{1,0:T(8,128)(2,1)S(1)}, u32[]{:S(2)}, u32[]{:S(2)}) collective-permute-start(bf16[192,768]{1,0:T(8,128)(2,1)S(1)} %collective-permute-done.3.refs_2_), channel_id=1, source_target_pairs={{0,1},{1,0},{2,3},{3,2},{4,5},{5,4},{6,7},{7,6},{8,9},{9,8},{10,11... | collective-permute-start | bytes 884744 | tf_op jit(solution)/shard_map/ppermute | solution.py:520
  13.8 4.5 %collective-permute-start.8 = (s32[8,256]{1,0:T(8,128)S(1)}, s32[8,256]{1,0:T(8,128)S(1)}, u32[]{:S(2)}, u32[]{:S(2)}) collective-permute-start(s32[8,256]{1,0:T(8,128)S(1)} %join.3.refs_4_), channel_id=1, source_target_pairs={{0,16},{1,17},{2,18},{3,19},{4,20},{5,21},{6,22},{7,23},{8,24},{9,... | collective-permute-start | bytes 24584 | tf_op jit(solution)/shard_map/ppermute | solution.py:520
  21.2 11.0 %copy-start = (bf16[192,768]{1,0:T(8,128)(2,1)S(1)}, bf16[192,768]{1,0:T(8,128)(2,1)}, u32[]{:S(2)}) copy-start(bf16[192,768]{1,0:T(8,128)(2,1)} %refs_9_.1) | copy-start | bytes 884740
  24.4 5.3 %collective-permute-start.10 = (bf16[384,128]{1,0:T(8,128)(2,1)S(1)}, bf16[384,128]{1,0:T(8,128)(2,1)S(1)}, u32[]{:S(2)}, u32[]{:S(2)}) collective-permute-start(bf16[384,128]{1,0:T(8,128)(2,1)S(1)} %get-tuple-element.32.refs_0_), channel_id=1, source_target_pairs={{0,2},{1,3},{2,0},{3,1},{4,6},{5,7},{6,4},{7,5},{8,10},{9,11},{10,... | collective-permute-start | bytes 294920 | tf_op jit(solution)/shard_map/ppermute | solution.py:520
  26.3 4.6 %collective-permute-start.13 = (bf16[384,128]{1,0:T(8,128)(2,1)S(1)}, bf16[384,128]{1,0:T(8,128)(2,1)S(1)}, u32[]{:S(2)}, u32[]{:S(2)}) collective-permute-start(bf16[384,128]{1,0:T(8,128)(2,1)S(1)} %get-tuple-element.33.refs_4_), channel_id=1, source_target_pairs={{0,2},{1,3},{2,0},{3,1},{4,6},{5,7},{6,4},{7,5},{8,10},{9,11},{10,... | collective-permute-start | bytes 294920 | tf_op jit(solution)/shard_map/ppermute | solution.py:520
  26.5 4.4 %collective-permute-start.9 = (bf16[384,128]{1,0:T(8,128)(2,1)S(1)}, bf16[384,128]{1,0:T(8,128)(2,1)S(1)}, u32[]{:S(2)}, u32[]{:S(2)}) collective-permute-start(bf16[384,128]{1,0:T(8,128)(2,1)S(1)} %get-tuple-element.32.refs_0_), channel_id=1, source_target_pairs={{0,1},{1,0},{2,3},{3,2},{4,5},{5,4},{6,7},{7,6},{8,9},{9,8},{10,11... | collective-permute-start | bytes 294920 | tf_op jit(solution)/shard_map/ppermute | solution.py:520
  26.5 4.4 %collective-permute-start.12 = (bf16[384,128]{1,0:T(8,128)(2,1)S(1)}, bf16[384,128]{1,0:T(8,128)(2,1)S(1)}, u32[]{:S(2)}, u32[]{:S(2)}) collective-permute-start(bf16[384,128]{1,0:T(8,128)(2,1)S(1)} %get-tuple-element.33.refs_4_), channel_id=1, source_target_pairs={{0,1},{1,0},{2,3},{3,2},{4,5},{5,4},{6,7},{7,6},{8,9},{9,8},{10,11... | collective-permute-start | bytes 294920 | tf_op jit(solution)/shard_map/ppermute | solution.py:520
  29.7 1.3 %collective-permute-start.11 = (bf16[384,128]{1,0:T(8,128)(2,1)S(1)}, bf16[384,128]{1,0:T(8,128)(2,1)S(1)}, u32[]{:S(2)}, u32[]{:S(2)}) collective-permute-start(bf16[384,128]{1,0:T(8,128)(2,1)S(1)} %collective-permute-done.10.refs_2_), channel_id=1, source_target_pairs={{0,1},{1,0},{2,3},{3,2},{4,5},{5,4},{6,7},{7,6},{8,9},{9,8},{10,11... | collective-permute-start | bytes 294920 | tf_op jit(solution)/shard_map/ppermute | solution.py:520
  30.9 1.3 %collective-permute-start.14 = (bf16[384,128]{1,0:T(8,128)(2,1)S(1)}, bf16[384,128]{1,0:T(8,128)(2,1)S(1)}, u32[]{:S(2)}, u32[]{:S(2)}) collective-permute-start(bf16[384,128]{1,0:T(8,128)(2,1)S(1)} %collective-permute-done.13.refs_6_), channel_id=1, source_target_pairs={{0,1},{1,0},{2,3},{3,2},{4,5},{5,4},{6,7},{7,6},{8,9},{9,8},{10,11... | collective-permute-start | bytes 294920 | tf_op jit(solution)/shard_map/ppermute | solution.py:520

commit v17 on v15

--- a/solution.py
+++ b/solution.py
@@ -162,38 +162,74 @@
     )
 
 
-def row_kernel(parts, *refs):
-    tables_refs, refs = refs[:parts], refs[parts:]
-    (
-        near_codes_ref,
-        far_codes_ref,
-        row_context_ref,
-        own_ref,
-        live_ref,
-        tables_ref,
-        table_ref,
-        hot_ref,
-        live_own_ref,
-        sum_ref,
-        spread_ref,
-    ) = refs
+def score_kernel(*refs):
+    *tables_refs, scores_ref, values_ref, tables_ref, table_ref = refs
+    parts = len(tables_refs)
+    width = values_ref.shape[1]
+    heads = width // HEAD_DIM
+    local = width // parts
+    part = lax.axis_index("head")
+    for p in range(parts):
+        tables_ref[part ^ p] = tables_refs[p][...]
+
+    for t in range(3):
+        to_ref = values_ref if t == 2 else table_ref.at[t]
+        to_ref[0:TABLE_ROWS, :] = jnp.concatenate(
+            [tables_ref[p, :, t * local : (t + 1) * local] for p in range(parts)], 1
+        )
+        to_ref[TABLE_ROWS:CODES, :] = jnp.zeros((CODES - TABLE_ROWS, width), bf16)
+
+    spans = [slice(hp * LANES, (hp + 1) * LANES) for hp in range(heads // 2)]
+    queries = [spread_pair(table_ref[0, :, span]) for span in spans]
+    keys = [double(table_ref[1, :, span]) for span in spans]
+    scores = [dot_nt(query, key) for query, key in zip(queries, keys)]
+    high = [score.astype(bf16) for score in scores]
+    low = [(score - part_of.astype(f32)).astype(bf16) for score, part_of in zip(scores, high)]
+    for h in range(heads):
+        these = slice(h % 2 * LANES, (h % 2 + 1) * LANES)
+        scores_ref[h, :, 0:LANES] = high[h // 2][these]
+        scores_ref[h, :, LANES : 2 * LANES] = low[h // 2][these]
+
+
+def score_tables(tables):
+    parts = len(tables)
+    width = tables[0].shape[1] // 3 * parts
+    return pl.pallas_call(
+        score_kernel,
+        out_shape=(
+            jax.ShapeDtypeStruct((width // HEAD_DIM, LANES, 2 * LANES), bf16),
+            jax.ShapeDtypeStruct((CODES, width), bf16),
+        ),
+        scratch_shapes=[
+            pltpu.VMEM((parts,) + tables[0].shape, bf16),
+            pltpu.VMEM((2, CODES, width), bf16),
+        ],
+        cost_estimate=pl.CostEstimate(flops=10**9, bytes_accessed=10**6, transcendentals=0),
+        compiler_params=pltpu.CompilerParams(vmem_limit_bytes=LARGE_VMEM),
+        name="scores",
+    )(*tables)
+
+
+def row_kernel(
+    scores_ref,
+    values_ref,
+    near_codes_ref,
+    far_codes_ref,
+    row_context_ref,
+    own_ref,
+    live_ref,
+    hot_ref,
+    live_own_ref,
+    sum_ref,
+    spread_ref,
+):
     depth, cols = hot_ref.shape
     rows = depth // CODES
     pairs = rows // 2
     own = live_own_ref.shape[0] // pairs
     width = row_context_ref.shape[1]
     heads = width // HEAD_DIM
-    local = width // parts
     group = lax.axis_index("seq")
-    part = lax.axis_index("head")
-    for p in range(parts):
-        tables_ref[part ^ p] = tables_refs[p][...]
-
-    for t in range(3):
-        table_ref[t, 0:TABLE_ROWS, :] = jnp.concatenate(
-            [tables_ref[p, :, t * local : (t + 1) * local] for p in range(parts)], 1
-        )
-        table_ref[t, TABLE_ROWS:CODES, :] = jnp.zeros((CODES - TABLE_ROWS, width), bf16)
 
     coded = jnp.concatenate([near_codes_ref[...], far_codes_ref[...]], 0)
     ids = (coded & 0xFFFF).astype(f32)
@@ -216,25 +252,14 @@
         own_ref[k * own : (k + 1) * own, :] = hot.astype(bf16)
         live_own_ref[k * own : (k + 1) * own, :] = (hot * alive).astype(bf16)
 
-    spans = [slice(hp * LANES, (hp + 1) * LANES) for hp in range(heads // 2)]
-    queries = [spread_pair(table_ref[0, :, span]) for span in spans]
-    keys = [double(table_ref[1, :, span]) for span in spans]
-    scores = [dot_nt(query, key) for query, key in zip(queries, keys)]
-    high = [score.astype(bf16) for score in scores]
-    low = [(score - part.astype(f32)).astype(bf16) for score, part in zip(scores, high)]
-    for hp in range(heads // 2):
-        for h2 in range(2):
-            these = slice(h2 * LANES, (h2 + 1) * LANES)
-            looked = dot_nn(
-                live_own_ref[...], jnp.concatenate([high[hp][these], low[hp][these]], 1)
-            ).astype(bf16)
-            base = (hp * 2 + h2) * own
-            for piece in range(2):
-                for k in range(pairs):
-                    to = piece * depth + k * LANES
-                    sum_ref[base : base + own, to : to + LANES] = looked[
-                        k * own : (k + 1) * own, piece * LANES : (piece + 1) * LANES
-                    ]
+    for h in range(heads):
+        looked = dot_nn(live_own_ref[...], scores_ref[h]).astype(bf16)
+        for piece in range(2):
+            for k in range(pairs):
+                to = piece * depth + k * LANES
+                sum_ref[h * own : (h + 1) * own, to : to + LANES] = looked[
+                    k * own : (k + 1) * own, piece * LANES : (piece + 1) * LANES
+                ]
     tied = dot_nn(sum_ref[:, 0:depth], hot_ref[...]) + dot_nn(
         sum_ref[:, depth : 2 * depth], hot_ref[...]
     )
@@ -242,7 +267,8 @@
     probs = softmax_last(tied * (HEAD_DIM ** (-0.5) / jnp.sqrt(count))).astype(bf16)
 
     spread_ref[...] = dot_nt(probs, hot_ref[...]).astype(bf16)
-    values = [spread_pair(table_ref[2, :, span]) for span in spans]
+    spans = [slice(hp * LANES, (hp + 1) * LANES) for hp in range(heads // 2)]
+    values = [spread_pair(values_ref[:, span]) for span in spans]
     contexts = []
     for hp in range(heads // 2):
         first = (hp * 2) * own
@@ -269,19 +295,16 @@
                 ]
 
 
-def attend_rows(tables, codes, rows, cols, own, width):
+def attend_rows(scores, values, codes, rows, cols, own, width):
     heads = width // HEAD_DIM
-    parts = len(tables)
     return pl.pallas_call(
-        functools.partial(row_kernel, parts),
+        row_kernel,
         out_shape=(
             jax.ShapeDtypeStruct((rows * own, width), bf16),
             jax.ShapeDtypeStruct((rows * own // 2, LANES), bf16),
             jax.ShapeDtypeStruct((rows, LANES), f32),
         ),
         scratch_shapes=[
-            pltpu.VMEM((parts,) + tables[0].shape, bf16),
-            pltpu.VMEM((3, CODES, width), bf16),
             pltpu.VMEM((rows * CODES, cols), bf16),
             pltpu.VMEM((rows // 2 * own, LANES), bf16),
             pltpu.VMEM((heads * own, 2 * rows * CODES), bf16),
@@ -290,7 +313,7 @@
         cost_estimate=pl.CostEstimate(flops=3 * 10**9, bytes_accessed=10**6, transcendentals=0),
         compiler_params=pltpu.CompilerParams(vmem_limit_bytes=LARGE_VMEM),
         name="row_attention",
-    )(*tables, *codes)
+    )(scores, values, *codes)
 
 
 def column_kernel(parts, *refs):
@@ -547,7 +570,9 @@
         received = pairwise(coded, lambda g, p, step=step: (g ^ step, p))
         step *= 2
     codes = (coded, received)
-    row_context, own_codes, live = attend_rows(tables, codes, rows, cols, own, width)
+    row_context, own_codes, live = attend_rows(
+        *score_tables(tables), codes, rows, cols, own, width
+    )
     *halves_here, mixed = attend_columns_here(
         row_outs, live, row_context, own_codes, embed, col_qkv.reshape(3 * local, width)
     )

time: 45.7 us -> 44.8 us (0.980)
  waiting for transfers between devices: 10.1 us -> 7.82 us
  blocking collectives: 12.9 us -> 13.9 us
    ppermute x15, waiting for transfers between devices: 10.1 us -> 7.82 us  [pairwise(): lax.ppermute(value, ('seq', 'head'), [(i, g * parts + p) for i, (g, p) in...]
    all_to_all x1, blocking collectives: 12.9 us -> 13.9 us  [fast_body(): lax.all_to_all(blocks, 'seq', split_axis=0, concat_axis=0, tiled=True)]
    pallas_call x1 -> x2, Pallas kernels: 2.82 us -> 3.16 us  [the longest x1 2.68 us: attend_rows(): pl.pallas_call(row_kernel, out_shape=(jax.ShapeDtypeStruct((rows * own, w...]
  transfers between devices with their start and end apart: 15 -> 15, of which waited for: 8 -> 7; matrix products, arithmetic and copies ran while one was open for 0% -> 0% of each run, Pallas kernels for 12% -> 13%
where the time goes in v17:
time: 44.8 us; the launch traced here: 44.6 us
  blocking collectives  13.9 us (31%)
  starting transfers between devices  12.5 us (28%)
  Pallas kernels  10.3 us (23%)
  waiting for transfers between devices  7.82 us (17%)
    all_to_all x1, blocking collectives, fast_body(): lax.all_to_all(blocks, 'seq', split_axis=0, concat_axis=0, tiled=True)  13.9 us
    ppermute x15, starting transfers between devices, pairwise(): lax.ppermute(value, ('seq', 'head'), [(i, g * parts + p) for i, (g, p) in...  12.5 us
    ppermute x15, waiting for transfers between devices, pairwise(): lax.ppermute(value, ('seq', 'head'), [(i, g * parts + p) for i, (g, p) in...  7.82 us
    pallas_call x1, Pallas kernels, attend_columns_here(): pl.pallas_call(functools.partial(column_kernel, parts), out_shape=(jax.Sh...  3.13 us
    pallas_call x1, Pallas kernels, attend_rows(): pl.pallas_call(row_kernel, out_shape=(jax.ShapeDtypeStruct((rows * own, w...  2.68 us
    pallas_call x1, Pallas kernels, make_tables(): pl.pallas_call(table_kernel, out_shape=jax.ShapeDtypeStruct((TABLE_ROWS,...  1.84 us
  transfers between devices with their start and end apart: 15, of which 7 were waited for; matrix products, arithmetic and copies ran while one was open for 0% of the time, Pallas kernels for 13%

profile of v17, /device:TPU:0, one launch (start us, length us, event | category | flops | bytes accessed | tf_op | source)
XLA Modules:
  0.0 44.6 jit_solution(9677475766619290514)
XLA Ops:
  0.0 2.9 %collective-permute-start.2 = (bf16[192,768]{1,0:T(8,128)(2,1)}, bf16[192,768]{1,0:T(8,128)(2,1)S(1)}, u32[]{:S(2)}, u32[]{:S(2)}) collective-permute-start(bf16[192,768]{1,0:T(8,128)(2,1)} %refs_0_), channel_id=1, source_target_pairs={{0,2},{1,3},{2,0},{3,1},{4,6},{5,7},{6,4},{7,5},{8,10},{9,11},{10,... | collective-permute-start | bytes 884744 | tf_op jit(solution)/shard_map/ppermute | solution.py:543
  2.9 0.8 %codes.1.own_ref = s32[8,256]{1,0:T(8,128)S(1)} custom-call(s32[2,256]{1,0:T(2,128)} %ids_hbm.1, s32[2]{0:T(128)} %live_hbm.1), custom_call_target="tpu_custom_call" | custom-call | tf_op jit(solution)/shard_map/codes/pallas_call | solution.py:70
  3.8 0.0 copy-start.2
  3.8 1.6 %collective-permute-start = (s32[8,256]{1,0:T(8,128)S(1)}, s32[8,256]{1,0:T(8,128)S(1)}, u32[]{:S(2)}, u32[]{:S(2)}) collective-permute-start(s32[8,256]{1,0:T(8,128)S(1)} %codes.1.own_ref), channel_id=1, source_target_pairs={{0,4},{1,5},{2,6},{3,7},{4,0},{5,1},{6,2},{7,3},{8,12},{9,13},{10,... | collective-permute-start | bytes 24584 | tf_op jit(solution)/shard_map/ppermute | solution.py:543
  5.4 1.8 %tables.1.refs_0_ = bf16[40,576]{1,0:T(8,128)(2,1)S(1)} custom-call(bf16[33,768]{1,0:T(8,128)(2,1)} %refs_7_.1, bf16[3,192,768]{2,1,0:T(8,128)(2,1)} %qkv_hbm), custom_call_target="tpu_custom_call" | custom-call | flops 2000000000 | bytes 884736 | tf_op jit(solution)/shard_map/tables/pallas_call | solution.py:120
  7.2 0.3 collective-permute-done.other_ref
  7.5 1.6 %collective-permute-start.1 = (s32[8,256]{1,0:T(8,128)S(1)}, s32[8,256]{1,0:T(8,128)S(1)}, u32[]{:S(2)}, u32[]{:S(2)}) collective-permute-start(s32[8,256]{1,0:T(8,128)S(1)} %join.2.own_ref), channel_id=1, source_target_pairs={{0,8},{1,9},{2,10},{3,11},{4,12},{5,13},{6,14},{7,15},{8,0},{9,1},... | collective-permute-start | bytes 24584 | tf_op jit(solution)/shard_map/ppermute | solution.py:543
  9.1 0.5 %collective-permute-start.6 = (bf16[40,576]{1,0:T(8,128)(2,1)S(1)}, bf16[40,576]{1,0:T(8,128)(2,1)S(1)}, u32[]{:S(2)}, u32[]{:S(2)}) collective-permute-start(bf16[40,576]{1,0:T(8,128)(2,1)S(1)} %tables.1.refs_0_), channel_id=1, source_target_pairs={{0,2},{1,3},{2,0},{3,1},{4,6},{5,7},{6,4},{7,5},{8,10},{9,11},{10,... | collective-permute-start | bytes 138248 | tf_op jit(solution)/shard_map/ppermute | solution.py:543
  9.6 0.0 collective-permute-start.7
  9.6 1.5 %collective-permute-done.1.other_ref = s32[8,256]{1,0:T(8,128)S(1)} collective-permute-done((s32[8,256]{1,0:T(8,128)S(1)}, s32[8,256]{1,0:T(8,128)S(1)}, u32[]{:S(2)}, u32[]{:S(2)}) %collective-permute-start.1) | collective-permute-done | bytes 8224 | tf_op jit(solution)/shard_map/ppermute | solution.py:543
  11.2 0.0 collective-permute-done.2.refs_2_
  11.2 0.1 collective-permute-start.5
  11.3 2.6 %collective-permute-start.8 = (s32[8,256]{1,0:T(8,128)S(1)}, s32[8,256]{1,0:T(8,128)S(1)}, u32[]{:S(2)}, u32[]{:S(2)}) collective-permute-start(s32[8,256]{1,0:T(8,128)S(1)} %join.3.near_codes_ref), channel_id=1, source_target_pairs={{0,16},{1,17},{2,18},{3,19},{4,20},{5,21},{6,22},{7,23},{8,24},{9,... | collective-permute-start | bytes 24584 | tf_op jit(solution)/shard_map/ppermute | solution.py:543
  13.9 0.0 copy-done.2
  13.9 0.2 collective-permute-start.3
  14.1 0.0 collective-permute-done.6.refs_2_
  14.1 0.3 collective-permute-start.4
  14.4 0.0 collective-permute-done.7.refs_3_
  14.4 0.0 collective-permute-done.5.refs_1_
  14.4 0.5 %scores.1 = (bf16[12,128,256]{2,1,0:T(8,128)(2,1)S(1)}, bf16[64,768]{1,0:T(8,128)(2,1)S(1)}) custom-call(bf16[40,576]{1,0:T(8,128)(2,1)S(1)} %tables.1.refs_0_, bf16[40,576]{1,0:T(8,128)(2,1)S(1)} %collective-permute-done.5.refs_1_, bf16[40,576]{1,0:T(8,128)(2,1)S(1)} %collective-permute-done.6.refs_2_, bf16[40,576]{1,0:T(8,128)(2,1)S(1)} %collective-permute-done.7.refs_3_), custom_call_target="tpu_custom_call" | custom-call | flops 1000000000 | bytes 1000000 | tf_op jit(solution)/shard_map/scores/pallas_call | solution.py:197
  14.9 0.9 %collective-permute-done.8.far_codes_ref = s32[8,256]{1,0:T(8,128)S(1)} collective-permute-done((s32[8,256]{1,0:T(8,128)S(1)}, s32[8,256]{1,0:T(8,128)S(1)}, u32[]{:S(2)}, u32[]{:S(2)}) %collective-permute-start.8) | collective-permute-done | bytes 8224 | tf_op jit(solution)/shard_map/ppermute | solution.py:543
  15.9 0.0 copy-start.1
  15.9 0.0 copy-start.3
  15.9 2.7 %row_attention.1 = (bf16[512,768]{1,0:T(8,128)(2,1)S(1)}, bf16[256,128]{1,0:T(8,128)(2,1)S(1)}, f32[16,128]{1,0:T(8,128)S(1)}) custom-call(bf16[12,128,256]{2,1,0:T(8,128)(2,1)S(1)} %get-tuple-element.28.scores_ref, bf16[64,768]{1,0:T(8,128)(2,1)S(1)} %get-tuple-element.29.values_ref, s32[8,256]{1,0:T(8,128)S(1)} %join.3.near_codes_ref, ...), custom_call_target="tpu_custom_call" | custom-call | flops 3000000000 | bytes 1000000 | tf_op jit(solution)/shard_map/row_attention/pallas_call | solution.py:300
  18.5 0.0 collective-permute-done.3.refs_1_
  18.6 0.0 collective-permute-done.4.refs_3_
  18.6 0.0 copy-done.1
  18.6 0.0 copy-done.3
  18.6 0.0 copy-start
  18.6 3.1 %column_attention.1 = (bf16[384,128]{1,0:T(8,128)(2,1)S(1)}, bf16[384,128]{1,0:T(8,128)(2,1)S(1)}, f32[512,192]{1,0:T(8,128)S(1)}) custom-call(bf16[192,768]{1,0:T(8,128)(2,1)S(1)} %copy-done.2, bf16[192,768]{1,0:T(8,128)(2,1)S(1)} %collective-permute-done.3.refs_1_, bf16[192,768]{1,0:T(8,128)(2,1)S(1)} %collective-permute-done.2.refs_2_, ...), custom_call_target="tpu_custom_call" | custom-call | flops 2000000000 | bytes 1000000 | tf_op jit(solution)/shard_map/column_attention/pallas_call | solution.py:439
  21.7 1.2 %collective-permute-start.10 = (bf16[384,128]{1,0:T(8,128)(2,1)S(1)}, bf16[384,128]{1,0:T(8,128)(2,1)S(1)}, u32[]{:S(2)}, u32[]{:S(2)}) collective-permute-start(bf16[384,128]{1,0:T(8,128)(2,1)S(1)} %get-tuple-element.34.refs_0_), channel_id=1, source_target_pairs={{0,2},{1,3},{2,0},{3,1},{4,6},{5,7},{6,4},{7,5},{8,10},{9,11},{10,... | collective-permute-start | bytes 294920 | tf_op jit(solution)/shard_map/ppermute | solution.py:543
  23.0 0.9 %collective-permute-start.13 = (bf16[384,128]{1,0:T(8,128)(2,1)S(1)}, bf16[384,128]{1,0:T(8,128)(2,1)S(1)}, u32[]{:S(2)}, u32[]{:S(2)}) collective-permute-start(bf16[384,128]{1,0:T(8,128)(2,1)S(1)} %get-tuple-element.35.refs_4_), channel_id=1, source_target_pairs={{0,2},{1,3},{2,0},{3,1},{4,6},{5,7},{6,4},{7,5},{8,10},{9,11},{10,... | collective-permute-start | bytes 294920 | tf_op jit(solution)/shard_map/ppermute | solution.py:543
  23.8 0.0 collective-permute-start.12
  23.8 0.5 %collective-permute-start.9 = (bf16[384,128]{1,0:T(8,128)(2,1)S(1)}, bf16[384,128]{1,0:T(8,128)(2,1)S(1)}, u32[]{:S(2)}, u32[]{:S(2)}) collective-permute-start(bf16[384,128]{1,0:T(8,128)(2,1)S(1)} %get-tuple-element.34.refs_0_), channel_id=1, source_target_pairs={{0,1},{1,0},{2,3},{3,2},{4,5},{5,4},{6,7},{7,6},{8,9},{9,8},{10,11... | collective-permute-start | bytes 294920 | tf_op jit(solution)/shard_map/ppermute | solution.py:543
  24.3 2.7 %collective-permute-done.10.refs_2_ = bf16[384,128]{1,0:T(8,128)(2,1)S(1)} collective-permute-done((bf16[384,128]{1,0:T(8,128)(2,1)S(1)}, bf16[384,128]{1,0:T(8,128)(2,1)S(1)}, u32[]{:S(2)}, u32[]{:S(2)}) %collective-permute-start.10) | collective-permute-done | bytes 98336 | tf_op jit(solution)/shard_map/ppermute | solution.py:543
  27.0 0.0 collective-permute-start.11
  27.0 1.1 %collective-permute-done.13.refs_6_ = bf16[384,128]{1,0:T(8,128)(2,1)S(1)} collective-permute-done((bf16[384,128]{1,0:T(8,128)(2,1)S(1)}, bf16[384,128]{1,0:T(8,128)(2,1)S(1)}, u32[]{:S(2)}, u32[]{:S(2)}) %collective-permute-start.13) | collective-permute-done | bytes 98336 | tf_op jit(solution)/shard_map/ppermute | solution.py:543
  28.1 0.0 collective-permute-start.14
  28.1 0.0 collective-permute-done.12.refs_5_
  28.1 0.0 collective-permute-done.9.refs_1_
  28.1 0.2 collective-permute-done.11.refs_3_
  28.3 1.1 %collective-permute-done.14.refs_7_ = bf16[384,128]{1,0:T(8,128)(2,1)S(1)} collective-permute-done((bf16[384,128]{1,0:T(8,128)(2,1)S(1)}, bf16[384,128]{1,0:T(8,128)(2,1)S(1)}, u32[]{:S(2)}, u32[]{:S(2)}) %collective-permute-start.14) | collective-permute-done | bytes 98336 | tf_op jit(solution)/shard_map/ppermute | solution.py:543
  29.4 0.0 copy-done
  29.4 0.5 %finish.1 = bf16[8,96,128]{2,1,0:T(8,128)(2,1)S(1)} custom-call(bf16[384,128]{1,0:T(8,128)(2,1)S(1)} %get-tuple-element.34.refs_0_, bf16[384,128]{1,0:T(8,128)(2,1)S(1)} %collective-permute-done.9.refs_1_, bf16[384,128]{1,0:T(8,128)(2,1)S(1)} %collective-permute-done.10.refs_2_, bf16[384,128]{1,0:T(8,128)(2,1)S(1)} %collective-permute-done.11.refs_3_, ...), custom_call_target="tpu_custom_call" | custom-call | tf_op jit(solution)/shard_map/finish/pallas_call | solution.py:498
  29.9 13.9 %all_to_all.5.blocks_ref = bf16[8,96,128]{2,1,0:T(8,128)(2,1)S(1)} all-to-all(bf16[8,96,128]{2,1,0:T(8,128)(2,1)S(1)} %finish.1), channel_id=1, replica_groups=mesh['seq'=8,'head'=4] {'seq'}, dimensions={0} | all-to-all | bytes 393216 | tf_op jit(solution)/shard_map/all_to_all | solution.py:586
  43.8 0.8 %order.1 = bf16[2,192,256]{2,1,0:T(8,128)(2,1)} custom-call(bf16[8,96,128]{2,1,0:T(8,128)(2,1)S(1)} %all_to_all.5.blocks_ref), custom_call_target="tpu_custom_call" | custom-call | tf_op jit(solution)/shard_map/order/pallas_call | solution.py:525
  (2 shorter events, 0.0 us)
Async XLA Ops:
  0.0 11.2 %collective-permute-start.2 = (bf16[192,768]{1,0:T(8,128)(2,1)}, bf16[192,768]{1,0:T(8,128)(2,1)S(1)}, u32[]{:S(2)}, u32[]{:S(2)}) collective-permute-start(bf16[192,768]{1,0:T(8,128)(2,1)} %refs_0_), channel_id=1, source_target_pairs={{0,2},{1,3},{2,0},{3,1},{4,6},{5,7},{6,4},{7,5},{8,10},{9,11},{10,... | collective-permute-start | bytes 884744 | tf_op jit(solution)/shard_map/ppermute | solution.py:543
  3.8 10.1 %copy-start.2 = (bf16[192,768]{1,0:T(8,128)(2,1)S(1)}, bf16[192,768]{1,0:T(8,128)(2,1)}, u32[]{:S(2)}) copy-start(bf16[192,768]{1,0:T(8,128)(2,1)} %refs_0_) | copy-start | bytes 884740
  3.8 3.7 %collective-permute-start = (s32[8,256]{1,0:T(8,128)S(1)}, s32[8,256]{1,0:T(8,128)S(1)}, u32[]{:S(2)}, u32[]{:S(2)}) collective-permute-start(s32[8,256]{1,0:T(8,128)S(1)} %codes.1.own_ref), channel_id=1, source_target_pairs={{0,4},{1,5},{2,6},{3,7},{4,0},{5,1},{6,2},{7,3},{8,12},{9,13},{10,... | collective-permute-start | bytes 24584 | tf_op jit(solution)/shard_map/ppermute | solution.py:543
  7.5 3.7 %collective-permute-start.1 = (s32[8,256]{1,0:T(8,128)S(1)}, s32[8,256]{1,0:T(8,128)S(1)}, u32[]{:S(2)}, u32[]{:S(2)}) collective-permute-start(s32[8,256]{1,0:T(8,128)S(1)} %join.2.own_ref), channel_id=1, source_target_pairs={{0,8},{1,9},{2,10},{3,11},{4,12},{5,13},{6,14},{7,15},{8,0},{9,1},... | collective-permute-start | bytes 24584 | tf_op jit(solution)/shard_map/ppermute | solution.py:543
  9.1 5.0 %collective-permute-start.6 = (bf16[40,576]{1,0:T(8,128)(2,1)S(1)}, bf16[40,576]{1,0:T(8,128)(2,1)S(1)}, u32[]{:S(2)}, u32[]{:S(2)}) collective-permute-start(bf16[40,576]{1,0:T(8,128)(2,1)S(1)} %tables.1.refs_0_), channel_id=1, source_target_pairs={{0,2},{1,3},{2,0},{3,1},{4,6},{5,7},{6,4},{7,5},{8,10},{9,11},{10,... | collective-permute-start | bytes 138248 | tf_op jit(solution)/shard_map/ppermute | solution.py:543
  9.6 4.8 %collective-permute-start.7 = (bf16[40,576]{1,0:T(8,128)(2,1)S(1)}, bf16[40,576]{1,0:T(8,128)(2,1)S(1)}, u32[]{:S(2)}, u32[]{:S(2)}) collective-permute-start(bf16[40,576]{1,0:T(8,128)(2,1)S(1)} %tables.1.refs_0_), channel_id=1, source_target_pairs={{0,3},{1,2},{2,1},{3,0},{4,7},{5,6},{6,5},{7,4},{8,11},{9,10},{10,... | collective-permute-start | bytes 138248 | tf_op jit(solution)/shard_map/ppermute | solution.py:543
  11.2 3.3 %collective-permute-start.5 = (bf16[40,576]{1,0:T(8,128)(2,1)S(1)}, bf16[40,576]{1,0:T(8,128)(2,1)S(1)}, u32[]{:S(2)}, u32[]{:S(2)}) collective-permute-start(bf16[40,576]{1,0:T(8,128)(2,1)S(1)} %tables.1.refs_0_), channel_id=1, source_target_pairs={{0,1},{1,0},{2,3},{3,2},{4,5},{5,4},{6,7},{7,6},{8,9},{9,8},{10,11... | collective-permute-start | bytes 138248 | tf_op jit(solution)/shard_map/ppermute | solution.py:543
  11.3 4.6 %collective-permute-start.8 = (s32[8,256]{1,0:T(8,128)S(1)}, s32[8,256]{1,0:T(8,128)S(1)}, u32[]{:S(2)}, u32[]{:S(2)}) collective-permute-start(s32[8,256]{1,0:T(8,128)S(1)} %join.3.near_codes_ref), channel_id=1, source_target_pairs={{0,16},{1,17},{2,18},{3,19},{4,20},{5,21},{6,22},{7,23},{8,24},{9,... | collective-permute-start | bytes 24584 | tf_op jit(solution)/shard_map/ppermute | solution.py:543
  13.9 4.7 %collective-permute-start.3 = (bf16[192,768]{1,0:T(8,128)(2,1)S(1)}, bf16[192,768]{1,0:T(8,128)(2,1)S(1)}, u32[]{:S(2)}, u32[]{:S(2)}) collective-permute-start(bf16[192,768]{1,0:T(8,128)(2,1)S(1)} %copy-done.2), channel_id=1, source_target_pairs={{0,1},{1,0},{2,3},{3,2},{4,5},{5,4},{6,7},{7,6},{8,9},{9,8},{10,11... | collective-permute-start | bytes 884744 | tf_op jit(solution)/shard_map/ppermute | solution.py:543
  14.1 4.5 %collective-permute-start.4 = (bf16[192,768]{1,0:T(8,128)(2,1)S(1)}, bf16[192,768]{1,0:T(8,128)(2,1)S(1)}, u32[]{:S(2)}, u32[]{:S(2)}) collective-permute-start(bf16[192,768]{1,0:T(8,128)(2,1)S(1)} %collective-permute-done.2.refs_2_), channel_id=1, source_target_pairs={{0,1},{1,0},{2,3},{3,2},{4,5},{5,4},{6,7},{7,6},{8,9},{9,8},{10,11... | collective-permute-start | bytes 884744 | tf_op jit(solution)/shard_map/ppermute | solution.py:543
  15.9 2.7 %copy-start.1 = (bf16[3,192,768]{2,1,0:T(8,128)(2,1)S(1)}, bf16[3,192,768]{2,1,0:T(8,128)(2,1)}, u32[]{:S(2)}) copy-start(bf16[3,192,768]{2,1,0:T(8,128)(2,1)} %param.12) | copy-start | bytes 2654212
  15.9 2.7 %copy-start.3 = (bf16[33,768]{1,0:T(8,128)(2,1)S(1)}, bf16[33,768]{1,0:T(8,128)(2,1)}, u32[]{:S(2)}) copy-start(bf16[33,768]{1,0:T(8,128)(2,1)} %refs_7_.1) | copy-start | bytes 152068
  18.6 10.8 %copy-start = (bf16[192,768]{1,0:T(8,128)(2,1)S(1)}, bf16[192,768]{1,0:T(8,128)(2,1)}, u32[]{:S(2)}) copy-start(bf16[192,768]{1,0:T(8,128)(2,1)} %refs_9_.1) | copy-start | bytes 884740
  21.7 5.3 %collective-permute-start.10 = (bf16[384,128]{1,0:T(8,128)(2,1)S(1)}, bf16[384,128]{1,0:T(8,128)(2,1)S(1)}, u32[]{:S(2)}, u32[]{:S(2)}) collective-permute-start(bf16[384,128]{1,0:T(8,128)(2,1)S(1)} %get-tuple-element.34.refs_0_), channel_id=1, source_target_pairs={{0,2},{1,3},{2,0},{3,1},{4,6},{5,7},{6,4},{7,5},{8,10},{9,11},{10,... | collective-permute-start | bytes 294920 | tf_op jit(solution)/shard_map/ppermute | solution.py:543
  23.0 5.1 %collective-permute-start.13 = (bf16[384,128]{1,0:T(8,128)(2,1)S(1)}, bf16[384,128]{1,0:T(8,128)(2,1)S(1)}, u32[]{:S(2)}, u32[]{:S(2)}) collective-permute-start(bf16[384,128]{1,0:T(8,128)(2,1)S(1)} %get-tuple-element.35.refs_4_), channel_id=1, source_target_pairs={{0,2},{1,3},{2,0},{3,1},{4,6},{5,7},{6,4},{7,5},{8,10},{9,11},{10,... | collective-permute-start | bytes 294920 | tf_op jit(solution)/shard_map/ppermute | solution.py:543
  23.8 4.3 %collective-permute-start.12 = (bf16[384,128]{1,0:T(8,128)(2,1)S(1)}, bf16[384,128]{1,0:T(8,128)(2,1)S(1)}, u32[]{:S(2)}, u32[]{:S(2)}) collective-permute-start(bf16[384,128]{1,0:T(8,128)(2,1)S(1)} %get-tuple-element.35.refs_4_), channel_id=1, source_target_pairs={{0,1},{1,0},{2,3},{3,2},{4,5},{5,4},{6,7},{7,6},{8,9},{9,8},{10,11... | collective-permute-start | bytes 294920 | tf_op jit(solution)/shard_map/ppermute | solution.py:543
  23.8 4.3 %collective-permute-start.9 = (bf16[384,128]{1,0:T(8,128)(2,1)S(1)}, bf16[384,128]{1,0:T(8,128)(2,1)S(1)}, u32[]{:S(2)}, u32[]{:S(2)}) collective-permute-start(bf16[384,128]{1,0:T(8,128)(2,1)S(1)} %get-tuple-element.34.refs_0_), channel_id=1, source_target_pairs={{0,1},{1,0},{2,3},{3,2},{4,5},{5,4},{6,7},{7,6},{8,9},{9,8},{10,11... | collective-permute-start | bytes 294920 | tf_op jit(solution)/shard_map/ppermute | solution.py:543
  27.0 1.3 %collective-permute-start.11 = (bf16[384,128]{1,0:T(8,128)(2,1)S(1)}, bf16[384,128]{1,0:T(8,128)(2,1)S(1)}, u32[]{:S(2)}, u32[]{:S(2)}) collective-permute-start(bf16[384,128]{1,0:T(8,128)(2,1)S(1)} %collective-permute-done.10.refs_2_), channel_id=1, source_target_pairs={{0,1},{1,0},{2,3},{3,2},{4,5},{5,4},{6,7},{7,6},{8,9},{9,8},{10,11... | collective-permute-start | bytes 294920 | tf_op jit(solution)/shard_map/ppermute | solution.py:543
  28.1 1.3 %collective-permute-start.14 = (bf16[384,128]{1,0:T(8,128)(2,1)S(1)}, bf16[384,128]{1,0:T(8,128)(2,1)S(1)}, u32[]{:S(2)}, u32[]{:S(2)}) collective-permute-start(bf16[384,128]{1,0:T(8,128)(2,1)S(1)} %collective-permute-done.13.refs_6_), channel_id=1, source_target_pairs={{0,1},{1,0},{2,3},{3,2},{4,5},{5,4},{6,7},{7,6},{8,9},{9,8},{10,11... | collective-permute-start | bytes 294920 | tf_op jit(solution)/shard_map/ppermute | solution.py:543

commit v18 on v17

--- a/solution.py
+++ b/solution.py
@@ -162,79 +162,14 @@
     )
 
 
-def score_kernel(*refs):
-    *tables_refs, scores_ref, values_ref, tables_ref, table_ref = refs
-    parts = len(tables_refs)
-    width = values_ref.shape[1]
-    heads = width // HEAD_DIM
-    local = width // parts
-    part = lax.axis_index("head")
-    for p in range(parts):
-        tables_ref[part ^ p] = tables_refs[p][...]
-
-    for t in range(3):
-        to_ref = values_ref if t == 2 else table_ref.at[t]
-        to_ref[0:TABLE_ROWS, :] = jnp.concatenate(
-            [tables_ref[p, :, t * local : (t + 1) * local] for p in range(parts)], 1
-        )
-        to_ref[TABLE_ROWS:CODES, :] = jnp.zeros((CODES - TABLE_ROWS, width), bf16)
-
-    spans = [slice(hp * LANES, (hp + 1) * LANES) for hp in range(heads // 2)]
-    queries = [spread_pair(table_ref[0, :, span]) for span in spans]
-    keys = [double(table_ref[1, :, span]) for span in spans]
-    scores = [dot_nt(query, key) for query, key in zip(queries, keys)]
-    high = [score.astype(bf16) for score in scores]
-    low = [(score - part_of.astype(f32)).astype(bf16) for score, part_of in zip(scores, high)]
-    for h in range(heads):
-        these = slice(h % 2 * LANES, (h % 2 + 1) * LANES)
-        scores_ref[h, :, 0:LANES] = high[h // 2][these]
-        scores_ref[h, :, LANES : 2 * LANES] = low[h // 2][these]
-
-
-def score_tables(tables):
-    parts = len(tables)
-    width = tables[0].shape[1] // 3 * parts
-    return pl.pallas_call(
-        score_kernel,
-        out_shape=(
-            jax.ShapeDtypeStruct((width // HEAD_DIM, LANES, 2 * LANES), bf16),
-            jax.ShapeDtypeStruct((CODES, width), bf16),
-        ),
-        scratch_shapes=[
-            pltpu.VMEM((parts,) + tables[0].shape, bf16),
-            pltpu.VMEM((2, CODES, width), bf16),
-        ],
-        cost_estimate=pl.CostEstimate(flops=10**9, bytes_accessed=10**6, transcendentals=0),
-        compiler_params=pltpu.CompilerParams(vmem_limit_bytes=LARGE_VMEM),
-        name="scores",
-    )(*tables)
-
-
-def row_kernel(
-    scores_ref,
-    values_ref,
-    near_codes_ref,
-    far_codes_ref,
-    row_context_ref,
-    own_ref,
-    live_ref,
-    hot_ref,
-    live_own_ref,
-    sum_ref,
-    spread_ref,
-):
+def one_hots(coded, group, hot_ref, own_ref, live_own_ref):
     depth, cols = hot_ref.shape
     rows = depth // CODES
     pairs = rows // 2
-    own = live_own_ref.shape[0] // pairs
-    width = row_context_ref.shape[1]
-    heads = width // HEAD_DIM
-    group = lax.axis_index("seq")
-
-    coded = jnp.concatenate([near_codes_ref[...], far_codes_ref[...]], 0)
+    own = own_ref.shape[0] // pairs
     ids = (coded & 0xFFFF).astype(f32)
     live = (coded[:, 0:LANES] >> 16).astype(f32)
-    live_ref[...] = live
+
     code = iota((CODES, cols), 0).astype(f32)
     for r in range(rows):
         hot = jnp.broadcast_to(ids[r : r + 1, :], (CODES, cols)) == code
@@ -251,7 +186,14 @@
         alive = jnp.where(first_half, live[2 * k : 2 * k + 1, :], live[2 * k + 1 : 2 * k + 2, :])
         own_ref[k * own : (k + 1) * own, :] = hot.astype(bf16)
         live_own_ref[k * own : (k + 1) * own, :] = (hot * alive).astype(bf16)
-
+    return live
+
+
+def tied_sum(scores_ref, live_own_ref, hot_ref, sum_ref):
+    heads = scores_ref.shape[0]
+    own = sum_ref.shape[0] // heads
+    depth = hot_ref.shape[0]
+    pairs = depth // CODES // 2
     for h in range(heads):
         looked = dot_nn(live_own_ref[...], scores_ref[h]).astype(bf16)
         for piece in range(2):
@@ -260,13 +202,113 @@
                 sum_ref[h * own : (h + 1) * own, to : to + LANES] = looked[
                     k * own : (k + 1) * own, piece * LANES : (piece + 1) * LANES
                 ]
-    tied = dot_nn(sum_ref[:, 0:depth], hot_ref[...]) + dot_nn(
+    return dot_nn(sum_ref[:, 0:depth], hot_ref[...]) + dot_nn(
         sum_ref[:, depth : 2 * depth], hot_ref[...]
     )
+
+
+def near_kernel(parts, *refs):
+    tables_refs, refs = refs[:parts], refs[parts:]
+    (
+        codes_ref,
+        scores_ref,
+        values_ref,
+        tied_ref,
+        hot_ref,
+        own_ref,
+        tables_ref,
+        table_ref,
+        live_own_ref,
+        sum_ref,
+    ) = refs
+    width = values_ref.shape[1]
+    heads = width // HEAD_DIM
+    local = width // parts
+    group = lax.axis_index("seq")
+    part = lax.axis_index("head")
+    for p in range(parts):
+        tables_ref[part ^ p] = tables_refs[p][...]
+
+    for t in range(3):
+        to_ref = values_ref if t == 2 else table_ref.at[t]
+        to_ref[0:TABLE_ROWS, :] = jnp.concatenate(
+            [tables_ref[p, :, t * local : (t + 1) * local] for p in range(parts)], 1
+        )
+        to_ref[TABLE_ROWS:CODES, :] = jnp.zeros((CODES - TABLE_ROWS, width), bf16)
+
+    spans = [slice(hp * LANES, (hp + 1) * LANES) for hp in range(heads // 2)]
+    queries = [spread_pair(table_ref[0, :, span]) for span in spans]
+    keys = [double(table_ref[1, :, span]) for span in spans]
+    scores = [dot_nt(query, key) for query, key in zip(queries, keys)]
+    high = [score.astype(bf16) for score in scores]
+    low = [(score - part_of.astype(f32)).astype(bf16) for score, part_of in zip(scores, high)]
+    for h in range(heads):
+        these = slice(h % 2 * LANES, (h % 2 + 1) * LANES)
+        scores_ref[h, :, 0:LANES] = high[h // 2][these]
+        scores_ref[h, :, LANES : 2 * LANES] = low[h // 2][these]
+
+    one_hots(codes_ref[...], group, hot_ref, own_ref, live_own_ref)
+    tied_ref[...] = tied_sum(scores_ref, live_own_ref, hot_ref, sum_ref)
+
+
+def attend_near(tables, codes, own):
+    parts = len(tables)
+    width = tables[0].shape[1] // 3 * parts
+    heads = width // HEAD_DIM
+    rows, cols = codes.shape
+    return pl.pallas_call(
+        functools.partial(near_kernel, parts),
+        out_shape=(
+            jax.ShapeDtypeStruct((heads, LANES, 2 * LANES), bf16),
+            jax.ShapeDtypeStruct((CODES, width), bf16),
+            jax.ShapeDtypeStruct((heads * own, cols), f32),
+            jax.ShapeDtypeStruct((rows * CODES, cols), bf16),
+            jax.ShapeDtypeStruct((rows // 2 * own, LANES), bf16),
+        ),
+        scratch_shapes=[
+            pltpu.VMEM((parts,) + tables[0].shape, bf16),
+            pltpu.VMEM((2, CODES, width), bf16),
+            pltpu.VMEM((rows // 2 * own, LANES), bf16),
+            pltpu.VMEM((heads * own, 2 * rows * CODES), bf16),
+        ],
+        cost_estimate=pl.CostEstimate(flops=10**9, bytes_accessed=10**6, transcendentals=0),
+        compiler_params=pltpu.CompilerParams(vmem_limit_bytes=LARGE_VMEM),
+        name="near_scores",
+    )(*tables, codes)
+
+
+def row_kernel(
+    scores_ref,
+    values_ref,
+    near_tied_ref,
+    near_hot_ref,
+    near_codes_ref,
+    far_codes_ref,
+    row_context_ref,
+    own_ref,
+    live_ref,
+    hot_ref,
+    live_own_ref,
+    sum_ref,
+    spread_ref,
+):
+    depth = hot_ref.shape[0]
+    rows = 2 * depth // CODES
+    pairs = rows // 2
+    width = row_context_ref.shape[1]
+    heads = width // HEAD_DIM
+    own = spread_ref.shape[0] // heads
+    group = lax.axis_index("seq")
+
+    live = one_hots(far_codes_ref[...], group, hot_ref, own_ref, live_own_ref)
+    live = jnp.concatenate([(near_codes_ref[:, 0:LANES] >> 16).astype(f32), live], 0)
+    live_ref[...] = live
+    tied = near_tied_ref[...] + tied_sum(scores_ref, live_own_ref, hot_ref, sum_ref)
     count = jnp.sum(live, axis=0, keepdims=True)[:, 0:1]
     probs = softmax_last(tied * (HEAD_DIM ** (-0.5) / jnp.sqrt(count))).astype(bf16)
 
-    spread_ref[...] = dot_nt(probs, hot_ref[...]).astype(bf16)
+    spread_ref[:, 0:depth] = dot_nt(probs, near_hot_ref[...]).astype(bf16)
+    spread_ref[:, depth : 2 * depth] = dot_nt(probs, hot_ref[...]).astype(bf16)
     spans = [slice(hp * LANES, (hp + 1) * LANES) for hp in range(heads // 2)]
     values = [spread_pair(values_ref[:, span]) for span in spans]
     contexts = []
@@ -295,25 +337,27 @@
                 ]
 
 
-def attend_rows(scores, values, codes, rows, cols, own, width):
-    heads = width // HEAD_DIM
+def attend_rows(near, near_codes, far_codes, own):
+    scores, values, near_tied, near_hot = near
+    heads, width = scores.shape[0], values.shape[1]
+    half, cols = near_codes.shape
     return pl.pallas_call(
         row_kernel,
         out_shape=(
-            jax.ShapeDtypeStruct((rows * own, width), bf16),
-            jax.ShapeDtypeStruct((rows * own // 2, LANES), bf16),
-            jax.ShapeDtypeStruct((rows, LANES), f32),
+            jax.ShapeDtypeStruct((2 * half * own, width), bf16),
+            jax.ShapeDtypeStruct((half // 2 * own, LANES), bf16),
+            jax.ShapeDtypeStruct((2 * half, LANES), f32),
         ),
         scratch_shapes=[
-            pltpu.VMEM((rows * CODES, cols), bf16),
-            pltpu.VMEM((rows // 2 * own, LANES), bf16),
-            pltpu.VMEM((heads * own, 2 * rows * CODES), bf16),
-            pltpu.VMEM((heads * own, rows * CODES), bf16),
+            pltpu.VMEM((half * CODES, cols), bf16),
+            pltpu.VMEM((half // 2 * own, LANES), bf16),
+            pltpu.VMEM((heads * own, 2 * half * CODES), bf16),
+            pltpu.VMEM((heads * own, 2 * half * CODES), bf16),
         ],
         cost_estimate=pl.CostEstimate(flops=3 * 10**9, bytes_accessed=10**6, transcendentals=0),
         compiler_params=pltpu.CompilerParams(vmem_limit_bytes=LARGE_VMEM),
         name="row_attention",
-    )(scores, values, *codes)
+    )(scores, values, near_tied, near_hot, near_codes, far_codes)
 
 
 def column_kernel(parts, *refs):
@@ -321,7 +365,8 @@
     (
         live_ref,
         row_context_ref,
-        own_ref,
+        near_own_ref,
+        far_own_ref,
         embed_ref,
         col_qkv_ref,
         *context_refs,
@@ -344,7 +389,8 @@
     embed2_ref[0:vocab, 0:width] = embed_ref[...]
     embed2_ref[CODES : CODES + vocab, width : 2 * width] = embed_ref[...]
 
-    embedded2 = dot_nn(own_ref[...], embed2_ref[...])
+    own_codes = jnp.concatenate([near_own_ref[...], far_own_ref[...]], 0)
+    embedded2 = dot_nn(own_codes, embed2_ref[...])
     embedded = jnp.concatenate(
         [
             embedded2[k * own : (k + 1) * own, r2 * width : (r2 + 1) * width]
@@ -431,7 +477,7 @@
         start += count
 
 
-def attend_columns_here(row_outs, live, row_context, own_codes, embed, col_qkv):
+def attend_columns_here(row_outs, live, row_context, near_own, far_own, embed, col_qkv):
     parts = len(row_outs)
     tokens, width = row_context.shape
     local = width // parts
@@ -451,7 +497,7 @@
         cost_estimate=pl.CostEstimate(flops=2 * 10**9, bytes_accessed=10**6, transcendentals=0),
         compiler_params=pltpu.CompilerParams(vmem_limit_bytes=LARGE_VMEM),
         name="column_attention",
-    )(*row_outs, live, row_context, own_codes, embed, col_qkv)
+    )(*row_outs, live, row_context, near_own, far_own, embed, col_qkv)
 
 
 def finish_kernel(parts, groups, *refs):
@@ -570,11 +616,16 @@
         received = pairwise(coded, lambda g, p, step=step: (g ^ step, p))
         step *= 2
     codes = (coded, received)
-    row_context, own_codes, live = attend_rows(
-        *score_tables(tables), codes, rows, cols, own, width
-    )
+    *near_scores, near_own = attend_near(tables, codes[0], own)
+    row_context, far_own, live = attend_rows(near_scores, *codes, own)
     *halves_here, mixed = attend_columns_here(
-        row_outs, live, row_context, own_codes, embed, col_qkv.reshape(3 * local, width)
+        row_outs,
+        live,
+        row_context,
+        near_own,
+        far_own,
+        embed,
+        col_qkv.reshape(3 * local, width),
     )
     contexts = []
     for context in halves_here:

time: 44.8 us -> 44 us (0.982)
  blocking collectives: 13.9 us -> 13.3 us
    all_to_all x1, blocking collectives: 13.9 us -> 13.3 us  [fast_body(): lax.all_to_all(blocks, 'seq', split_axis=0, concat_axis=0, tiled=True)]
  transfers between devices with their start and end apart: 15 -> 15, of which waited for: 7 -> 6; matrix products, arithmetic and copies ran while one was open for 0% -> 0% of each run, Pallas kernels for 13% -> 13%
where the time goes in v18:
time: 44 us; the launch traced here: 43.8 us
  blocking collectives  13.3 us (30%)
  starting transfers between devices  12.5 us (28%)
  Pallas kernels  10.2 us (23%)
  waiting for transfers between devices  7.76 us (18%)
    all_to_all x1, blocking collectives, fast_body(): lax.all_to_all(blocks, 'seq', split_axis=0, concat_axis=0, tiled=True)  13.3 us
    ppermute x15, starting transfers between devices, pairwise(): lax.ppermute(value, ('seq', 'head'), [(i, g * parts + p) for i, (g, p) in...  12.5 us
    ppermute x15, waiting for transfers between devices, pairwise(): lax.ppermute(value, ('seq', 'head'), [(i, g * parts + p) for i, (g, p) in...  7.76 us
    pallas_call x1, Pallas kernels, attend_columns_here(): pl.pallas_call(functools.partial(column_kernel, parts), out_shape=(jax.Sh...  3.14 us
    pallas_call x1, Pallas kernels, attend_rows(): pl.pallas_call(row_kernel, out_shape=(jax.ShapeDtypeStruct((2 * half * ow...  1.86 us
    pallas_call x1, Pallas kernels, make_tables(): pl.pallas_call(table_kernel, out_shape=jax.ShapeDtypeStruct((TABLE_ROWS,...  1.84 us
    pallas_call x1, Pallas kernels, attend_near(): pl.pallas_call(functools.partial(near_kernel, parts), out_shape=(jax.Shap...  1.19 us
  transfers between devices with their start and end apart: 15, of which 6 were waited for; matrix products, arithmetic and copies ran while one was open for 0% of the time, Pallas kernels for 13%

profile of v18, /device:TPU:0, one launch (start us, length us, event | category | flops | bytes accessed | tf_op | source)
XLA Modules:
  0.0 43.8 jit_solution(2841714224496204302)
XLA Ops:
  0.0 2.9 %collective-permute-start.2 = (bf16[192,768]{1,0:T(8,128)(2,1)}, bf16[192,768]{1,0:T(8,128)(2,1)S(1)}, u32[]{:S(2)}, u32[]{:S(2)}) collective-permute-start(bf16[192,768]{1,0:T(8,128)(2,1)} %refs_0_), channel_id=1, source_target_pairs={{0,2},{1,3},{2,0},{3,1},{4,6},{5,7},{6,4},{7,5},{8,10},{9,11},{10,... | collective-permute-start | bytes 884744 | tf_op jit(solution)/shard_map/ppermute | solution.py:589
  2.9 0.8 %codes.1.own_ref = s32[8,256]{1,0:T(8,128)S(1)} custom-call(s32[2,256]{1,0:T(2,128)} %ids_hbm.1, s32[2]{0:T(128)} %live_hbm.1), custom_call_target="tpu_custom_call" | custom-call | tf_op jit(solution)/shard_map/codes/pallas_call | solution.py:70
  3.8 0.0 copy-start.2
  3.8 1.6 %collective-permute-start = (s32[8,256]{1,0:T(8,128)S(1)}, s32[8,256]{1,0:T(8,128)S(1)}, u32[]{:S(2)}, u32[]{:S(2)}) collective-permute-start(s32[8,256]{1,0:T(8,128)S(1)} %codes.1.own_ref), channel_id=1, source_target_pairs={{0,4},{1,5},{2,6},{3,7},{4,0},{5,1},{6,2},{7,3},{8,12},{9,13},{10,... | collective-permute-start | bytes 24584 | tf_op jit(solution)/shard_map/ppermute | solution.py:589
  5.4 1.8 %tables.1.refs_0_ = bf16[40,576]{1,0:T(8,128)(2,1)S(1)} custom-call(bf16[33,768]{1,0:T(8,128)(2,1)} %refs_8_.1, bf16[3,192,768]{2,1,0:T(8,128)(2,1)} %qkv_hbm), custom_call_target="tpu_custom_call" | custom-call | flops 2000000000 | bytes 884736 | tf_op jit(solution)/shard_map/tables/pallas_call | solution.py:120
  7.2 0.3 collective-permute-done.other_ref
  7.5 1.6 %collective-permute-start.1 = (s32[8,256]{1,0:T(8,128)S(1)}, s32[8,256]{1,0:T(8,128)S(1)}, u32[]{:S(2)}, u32[]{:S(2)}) collective-permute-start(s32[8,256]{1,0:T(8,128)S(1)} %join.2.own_ref), channel_id=1, source_target_pairs={{0,8},{1,9},{2,10},{3,11},{4,12},{5,13},{6,14},{7,15},{8,0},{9,1},... | collective-permute-start | bytes 24584 | tf_op jit(solution)/shard_map/ppermute | solution.py:589
  9.1 0.5 %collective-permute-start.6 = (bf16[40,576]{1,0:T(8,128)(2,1)S(1)}, bf16[40,576]{1,0:T(8,128)(2,1)S(1)}, u32[]{:S(2)}, u32[]{:S(2)}) collective-permute-start(bf16[40,576]{1,0:T(8,128)(2,1)S(1)} %tables.1.refs_0_), channel_id=1, source_target_pairs={{0,2},{1,3},{2,0},{3,1},{4,6},{5,7},{6,4},{7,5},{8,10},{9,11},{10,... | collective-permute-start | bytes 138248 | tf_op jit(solution)/shard_map/ppermute | solution.py:589
  9.6 0.0 collective-permute-start.7
  9.6 1.5 %collective-permute-done.1.other_ref = s32[8,256]{1,0:T(8,128)S(1)} collective-permute-done((s32[8,256]{1,0:T(8,128)S(1)}, s32[8,256]{1,0:T(8,128)S(1)}, u32[]{:S(2)}, u32[]{:S(2)}) %collective-permute-start.1) | collective-permute-done | bytes 8224 | tf_op jit(solution)/shard_map/ppermute | solution.py:589
  11.2 0.0 collective-permute-done.2.refs_2_
  11.2 0.1 collective-permute-start.5
  11.3 2.6 %collective-permute-start.8 = (s32[8,256]{1,0:T(8,128)S(1)}, s32[8,256]{1,0:T(8,128)S(1)}, u32[]{:S(2)}, u32[]{:S(2)}) collective-permute-start(s32[8,256]{1,0:T(8,128)S(1)} %join.3.refs_4_.near_codes_ref), channel_id=1, source_target_pairs={{0,16},{1,17},{2,18},{3,19},{4,20},{5,21},{6,22},{7,23},{8,24},{9,... | collective-permute-start | bytes 24584 | tf_op jit(solution)/shard_map/ppermute | solution.py:589
  13.9 0.0 copy-done.2
  13.9 0.2 collective-permute-start.3
  14.1 0.0 collective-permute-done.6.refs_2_
  14.1 0.3 collective-permute-start.4
  14.4 0.0 collective-permute-done.7.refs_3_
  14.4 0.0 collective-permute-done.5.refs_1_
  14.4 1.2 %near_scores.1 = (bf16[12,128,256]{2,1,0:T(8,128)(2,1)S(1)}, bf16[64,768]{1,0:T(8,128)(2,1)S(1)}, f32[384,256]{1,0:T(8,128)S(1)}, bf16[512,256]{1,0:T(8,128)(2,1)S(1)}, bf16[128,128]{1,0:T(8,128)(2,1)S(1)}) custom-call(bf16[40,576]{1,0:T(8,128)(2,1)S(1)} %tables.1.refs_0_, bf16[40,576]{1,0:T(8,128)(2,1)S(1)} %collective-permute-done.5.refs_1_, ...), custom_call_target="tpu_custom_call" | custom-call | flops 1000000000 | bytes 1000000 | tf_op jit(solution)/shard_map/near_scores/pallas_call | solution.py:259
  15.6 0.2 collective-permute-done.8.far_codes_ref
  15.9 0.0 copy-start.1
  15.9 0.0 copy-start.3
  15.9 1.9 %row_attention.1 = (bf16[512,768]{1,0:T(8,128)(2,1)S(1)}, bf16[128,128]{1,0:T(8,128)(2,1)S(1)}, f32[16,128]{1,0:T(8,128)S(1)}) custom-call(bf16[12,128,256]{2,1,0:T(8,128)(2,1)S(1)} %get-tuple-element.32.scores_ref, bf16[64,768]{1,0:T(8,128)(2,1)S(1)} %get-tuple-element.33.values_ref, f32[384,256]{1,0:T(8,128)S(1)} %get-tuple-element.34.near_tied_ref, ...), custom_call_target="tpu_custom_call" | custom-call | flops 3000000000 | bytes 1000000 | tf_op jit(solution)/shard_map/row_attention/pallas_call | solution.py:344
  17.7 0.0 collective-permute-done.3.refs_1_
  17.7 0.0 collective-permute-done.4.refs_3_
  17.8 0.0 copy-done.1
  17.8 0.0 copy-done.3
  17.8 0.0 copy-start
  17.8 3.1 %column_attention.1 = (bf16[384,128]{1,0:T(8,128)(2,1)S(1)}, bf16[384,128]{1,0:T(8,128)(2,1)S(1)}, f32[512,192]{1,0:T(8,128)S(1)}) custom-call(bf16[192,768]{1,0:T(8,128)(2,1)S(1)} %copy-done.2, bf16[192,768]{1,0:T(8,128)(2,1)S(1)} %collective-permute-done.3.refs_1_, bf16[192,768]{1,0:T(8,128)(2,1)S(1)} %collective-permute-done.2.refs_2_, ...), custom_call_target="tpu_custom_call" | custom-call | flops 2000000000 | bytes 1000000 | tf_op jit(solution)/shard_map/column_attention/pallas_call | solution.py:485
  20.9 1.2 %collective-permute-start.10 = (bf16[384,128]{1,0:T(8,128)(2,1)S(1)}, bf16[384,128]{1,0:T(8,128)(2,1)S(1)}, u32[]{:S(2)}, u32[]{:S(2)}) collective-permute-start(bf16[384,128]{1,0:T(8,128)(2,1)S(1)} %get-tuple-element.40.refs_0_), channel_id=1, source_target_pairs={{0,2},{1,3},{2,0},{3,1},{4,6},{5,7},{6,4},{7,5},{8,10},{9,11},{10,... | collective-permute-start | bytes 294920 | tf_op jit(solution)/shard_map/ppermute | solution.py:589
  22.1 0.9 %collective-permute-start.13 = (bf16[384,128]{1,0:T(8,128)(2,1)S(1)}, bf16[384,128]{1,0:T(8,128)(2,1)S(1)}, u32[]{:S(2)}, u32[]{:S(2)}) collective-permute-start(bf16[384,128]{1,0:T(8,128)(2,1)S(1)} %get-tuple-element.41.refs_4_), channel_id=1, source_target_pairs={{0,2},{1,3},{2,0},{3,1},{4,6},{5,7},{6,4},{7,5},{8,10},{9,11},{10,... | collective-permute-start | bytes 294920 | tf_op jit(solution)/shard_map/ppermute | solution.py:589
  23.0 0.0 collective-permute-start.12
  23.0 0.5 %collective-permute-start.9 = (bf16[384,128]{1,0:T(8,128)(2,1)S(1)}, bf16[384,128]{1,0:T(8,128)(2,1)S(1)}, u32[]{:S(2)}, u32[]{:S(2)}) collective-permute-start(bf16[384,128]{1,0:T(8,128)(2,1)S(1)} %get-tuple-element.40.refs_0_), channel_id=1, source_target_pairs={{0,1},{1,0},{2,3},{3,2},{4,5},{5,4},{6,7},{7,6},{8,9},{9,8},{10,11... | collective-permute-start | bytes 294920 | tf_op jit(solution)/shard_map/ppermute | solution.py:589
  23.5 3.1 %collective-permute-done.10.refs_2_ = bf16[384,128]{1,0:T(8,128)(2,1)S(1)} collective-permute-done((bf16[384,128]{1,0:T(8,128)(2,1)S(1)}, bf16[384,128]{1,0:T(8,128)(2,1)S(1)}, u32[]{:S(2)}, u32[]{:S(2)}) %collective-permute-start.10) | collective-permute-done | bytes 98336 | tf_op jit(solution)/shard_map/ppermute | solution.py:589
  26.6 0.0 collective-permute-start.11
  26.6 1.3 %collective-permute-done.13.refs_6_ = bf16[384,128]{1,0:T(8,128)(2,1)S(1)} collective-permute-done((bf16[384,128]{1,0:T(8,128)(2,1)S(1)}, bf16[384,128]{1,0:T(8,128)(2,1)S(1)}, u32[]{:S(2)}, u32[]{:S(2)}) %collective-permute-start.13) | collective-permute-done | bytes 98336 | tf_op jit(solution)/shard_map/ppermute | solution.py:589
  27.9 0.0 collective-permute-start.14
  27.9 0.0 collective-permute-done.12.refs_5_
  27.9 0.0 collective-permute-done.9.refs_1_
  27.9 0.0 collective-permute-done.11.refs_3_
  27.9 1.3 %collective-permute-done.14.refs_7_ = bf16[384,128]{1,0:T(8,128)(2,1)S(1)} collective-permute-done((bf16[384,128]{1,0:T(8,128)(2,1)S(1)}, bf16[384,128]{1,0:T(8,128)(2,1)S(1)}, u32[]{:S(2)}, u32[]{:S(2)}) %collective-permute-start.14) | collective-permute-done | bytes 98336 | tf_op jit(solution)/shard_map/ppermute | solution.py:589
  29.2 0.0 copy-done
  29.2 0.5 %finish.1 = bf16[8,96,128]{2,1,0:T(8,128)(2,1)S(1)} custom-call(bf16[384,128]{1,0:T(8,128)(2,1)S(1)} %get-tuple-element.40.refs_0_, bf16[384,128]{1,0:T(8,128)(2,1)S(1)} %collective-permute-done.9.refs_1_, bf16[384,128]{1,0:T(8,128)(2,1)S(1)} %collective-permute-done.10.refs_2_, bf16[384,128]{1,0:T(8,128)(2,1)S(1)} %collective-permute-done.11.refs_3_, ...), custom_call_target="tpu_custom_call" | custom-call | tf_op jit(solution)/shard_map/finish/pallas_call | solution.py:544
  29.7 13.3 %all_to_all.5.blocks_ref = bf16[8,96,128]{2,1,0:T(8,128)(2,1)S(1)} all-to-all(bf16[8,96,128]{2,1,0:T(8,128)(2,1)S(1)} %finish.1), channel_id=1, replica_groups=mesh['seq'=8,'head'=4] {'seq'}, dimensions={0} | all-to-all | bytes 393216 | tf_op jit(solution)/shard_map/all_to_all | solution.py:637
  43.0 0.8 %order.1 = bf16[2,192,256]{2,1,0:T(8,128)(2,1)} custom-call(bf16[8,96,128]{2,1,0:T(8,128)(2,1)S(1)} %all_to_all.5.blocks_ref), custom_call_target="tpu_custom_call" | custom-call | tf_op jit(solution)/shard_map/order/pallas_call | solution.py:571
  (2 shorter events, 0.0 us)
Async XLA Ops:
  0.0 11.2 %collective-permute-start.2 = (bf16[192,768]{1,0:T(8,128)(2,1)}, bf16[192,768]{1,0:T(8,128)(2,1)S(1)}, u32[]{:S(2)}, u32[]{:S(2)}) collective-permute-start(bf16[192,768]{1,0:T(8,128)(2,1)} %refs_0_), channel_id=1, source_target_pairs={{0,2},{1,3},{2,0},{3,1},{4,6},{5,7},{6,4},{7,5},{8,10},{9,11},{10,... | collective-permute-start | bytes 884744 | tf_op jit(solution)/shard_map/ppermute | solution.py:589
  3.8 10.1 %copy-start.2 = (bf16[192,768]{1,0:T(8,128)(2,1)S(1)}, bf16[192,768]{1,0:T(8,128)(2,1)}, u32[]{:S(2)}) copy-start(bf16[192,768]{1,0:T(8,128)(2,1)} %refs_0_) | copy-start | bytes 884740
  3.8 3.7 %collective-permute-start = (s32[8,256]{1,0:T(8,128)S(1)}, s32[8,256]{1,0:T(8,128)S(1)}, u32[]{:S(2)}, u32[]{:S(2)}) collective-permute-start(s32[8,256]{1,0:T(8,128)S(1)} %codes.1.own_ref), channel_id=1, source_target_pairs={{0,4},{1,5},{2,6},{3,7},{4,0},{5,1},{6,2},{7,3},{8,12},{9,13},{10,... | collective-permute-start | bytes 24584 | tf_op jit(solution)/shard_map/ppermute | solution.py:589
  7.5 3.7 %collective-permute-start.1 = (s32[8,256]{1,0:T(8,128)S(1)}, s32[8,256]{1,0:T(8,128)S(1)}, u32[]{:S(2)}, u32[]{:S(2)}) collective-permute-start(s32[8,256]{1,0:T(8,128)S(1)} %join.2.own_ref), channel_id=1, source_target_pairs={{0,8},{1,9},{2,10},{3,11},{4,12},{5,13},{6,14},{7,15},{8,0},{9,1},... | collective-permute-start | bytes 24584 | tf_op jit(solution)/shard_map/ppermute | solution.py:589
  9.1 5.0 %collective-permute-start.6 = (bf16[40,576]{1,0:T(8,128)(2,1)S(1)}, bf16[40,576]{1,0:T(8,128)(2,1)S(1)}, u32[]{:S(2)}, u32[]{:S(2)}) collective-permute-start(bf16[40,576]{1,0:T(8,128)(2,1)S(1)} %tables.1.refs_0_), channel_id=1, source_target_pairs={{0,2},{1,3},{2,0},{3,1},{4,6},{5,7},{6,4},{7,5},{8,10},{9,11},{10,... | collective-permute-start | bytes 138248 | tf_op jit(solution)/shard_map/ppermute | solution.py:589
  9.6 4.8 %collective-permute-start.7 = (bf16[40,576]{1,0:T(8,128)(2,1)S(1)}, bf16[40,576]{1,0:T(8,128)(2,1)S(1)}, u32[]{:S(2)}, u32[]{:S(2)}) collective-permute-start(bf16[40,576]{1,0:T(8,128)(2,1)S(1)} %tables.1.refs_0_), channel_id=1, source_target_pairs={{0,3},{1,2},{2,1},{3,0},{4,7},{5,6},{6,5},{7,4},{8,11},{9,10},{10,... | collective-permute-start | bytes 138248 | tf_op jit(solution)/shard_map/ppermute | solution.py:589
  11.2 3.3 %collective-permute-start.5 = (bf16[40,576]{1,0:T(8,128)(2,1)S(1)}, bf16[40,576]{1,0:T(8,128)(2,1)S(1)}, u32[]{:S(2)}, u32[]{:S(2)}) collective-permute-start(bf16[40,576]{1,0:T(8,128)(2,1)S(1)} %tables.1.refs_0_), channel_id=1, source_target_pairs={{0,1},{1,0},{2,3},{3,2},{4,5},{5,4},{6,7},{7,6},{8,9},{9,8},{10,11... | collective-permute-start | bytes 138248 | tf_op jit(solution)/shard_map/ppermute | solution.py:589
  11.3 4.6 %collective-permute-start.8 = (s32[8,256]{1,0:T(8,128)S(1)}, s32[8,256]{1,0:T(8,128)S(1)}, u32[]{:S(2)}, u32[]{:S(2)}) collective-permute-start(s32[8,256]{1,0:T(8,128)S(1)} %join.3.refs_4_.near_codes_ref), channel_id=1, source_target_pairs={{0,16},{1,17},{2,18},{3,19},{4,20},{5,21},{6,22},{7,23},{8,24},{9,... | collective-permute-start | bytes 24584 | tf_op jit(solution)/shard_map/ppermute | solution.py:589
  13.9 3.8 %collective-permute-start.3 = (bf16[192,768]{1,0:T(8,128)(2,1)S(1)}, bf16[192,768]{1,0:T(8,128)(2,1)S(1)}, u32[]{:S(2)}, u32[]{:S(2)}) collective-permute-start(bf16[192,768]{1,0:T(8,128)(2,1)S(1)} %copy-done.2), channel_id=1, source_target_pairs={{0,1},{1,0},{2,3},{3,2},{4,5},{5,4},{6,7},{7,6},{8,9},{9,8},{10,11... | collective-permute-start | bytes 884744 | tf_op jit(solution)/shard_map/ppermute | solution.py:589
  14.1 3.7 %collective-permute-start.4 = (bf16[192,768]{1,0:T(8,128)(2,1)S(1)}, bf16[192,768]{1,0:T(8,128)(2,1)S(1)}, u32[]{:S(2)}, u32[]{:S(2)}) collective-permute-start(bf16[192,768]{1,0:T(8,128)(2,1)S(1)} %collective-permute-done.2.refs_2_), channel_id=1, source_target_pairs={{0,1},{1,0},{2,3},{3,2},{4,5},{5,4},{6,7},{7,6},{8,9},{9,8},{10,11... | collective-permute-start | bytes 884744 | tf_op jit(solution)/shard_map/ppermute | solution.py:589
  15.9 1.9 %copy-start.1 = (bf16[3,192,768]{2,1,0:T(8,128)(2,1)S(1)}, bf16[3,192,768]{2,1,0:T(8,128)(2,1)}, u32[]{:S(2)}) copy-start(bf16[3,192,768]{2,1,0:T(8,128)(2,1)} %param.12) | copy-start | bytes 2654212
  15.9 1.9 %copy-start.3 = (bf16[33,768]{1,0:T(8,128)(2,1)S(1)}, bf16[33,768]{1,0:T(8,128)(2,1)}, u32[]{:S(2)}) copy-start(bf16[33,768]{1,0:T(8,128)(2,1)} %refs_8_.1) | copy-start | bytes 152068
  17.8 11.5 %copy-start = (bf16[192,768]{1,0:T(8,128)(2,1)S(1)}, bf16[192,768]{1,0:T(8,128)(2,1)}, u32[]{:S(2)}) copy-start(bf16[192,768]{1,0:T(8,128)(2,1)} %refs_9_.1) | copy-start | bytes 884740
  20.9 5.7 %collective-permute-start.10 = (bf16[384,128]{1,0:T(8,128)(2,1)S(1)}, bf16[384,128]{1,0:T(8,128)(2,1)S(1)}, u32[]{:S(2)}, u32[]{:S(2)}) collective-permute-start(bf16[384,128]{1,0:T(8,128)(2,1)S(1)} %get-tuple-element.40.refs_0_), channel_id=1, source_target_pairs={{0,2},{1,3},{2,0},{3,1},{4,6},{5,7},{6,4},{7,5},{8,10},{9,11},{10,... | collective-permute-start | bytes 294920 | tf_op jit(solution)/shard_map/ppermute | solution.py:589
  22.1 5.8 %collective-permute-start.13 = (bf16[384,128]{1,0:T(8,128)(2,1)S(1)}, bf16[384,128]{1,0:T(8,128)(2,1)S(1)}, u32[]{:S(2)}, u32[]{:S(2)}) collective-permute-start(bf16[384,128]{1,0:T(8,128)(2,1)S(1)} %get-tuple-element.41.refs_4_), channel_id=1, source_target_pairs={{0,2},{1,3},{2,0},{3,1},{4,6},{5,7},{6,4},{7,5},{8,10},{9,11},{10,... | collective-permute-start | bytes 294920 | tf_op jit(solution)/shard_map/ppermute | solution.py:589
  23.0 4.9 %collective-permute-start.12 = (bf16[384,128]{1,0:T(8,128)(2,1)S(1)}, bf16[384,128]{1,0:T(8,128)(2,1)S(1)}, u32[]{:S(2)}, u32[]{:S(2)}) collective-permute-start(bf16[384,128]{1,0:T(8,128)(2,1)S(1)} %get-tuple-element.41.refs_4_), channel_id=1, source_target_pairs={{0,1},{1,0},{2,3},{3,2},{4,5},{5,4},{6,7},{7,6},{8,9},{9,8},{10,11... | collective-permute-start | bytes 294920 | tf_op jit(solution)/shard_map/ppermute | solution.py:589
  23.0 4.9 %collective-permute-start.9 = (bf16[384,128]{1,0:T(8,128)(2,1)S(1)}, bf16[384,128]{1,0:T(8,128)(2,1)S(1)}, u32[]{:S(2)}, u32[]{:S(2)}) collective-permute-start(bf16[384,128]{1,0:T(8,128)(2,1)S(1)} %get-tuple-element.40.refs_0_), channel_id=1, source_target_pairs={{0,1},{1,0},{2,3},{3,2},{4,5},{5,4},{6,7},{7,6},{8,9},{9,8},{10,11... | collective-permute-start | bytes 294920 | tf_op jit(solution)/shard_map/ppermute | solution.py:589
  26.6 1.3 %collective-permute-start.11 = (bf16[384,128]{1,0:T(8,128)(2,1)S(1)}, bf16[384,128]{1,0:T(8,128)(2,1)S(1)}, u32[]{:S(2)}, u32[]{:S(2)}) collective-permute-start(bf16[384,128]{1,0:T(8,128)(2,1)S(1)} %collective-permute-done.10.refs_2_), channel_id=1, source_target_pairs={{0,1},{1,0},{2,3},{3,2},{4,5},{5,4},{6,7},{7,6},{8,9},{9,8},{10,11... | collective-permute-start | bytes 294920 | tf_op jit(solution)/shard_map/ppermute | solution.py:589
  27.9 1.3 %collective-permute-start.14 = (bf16[384,128]{1,0:T(8,128)(2,1)S(1)}, bf16[384,128]{1,0:T(8,128)(2,1)S(1)}, u32[]{:S(2)}, u32[]{:S(2)}) collective-permute-start(bf16[384,128]{1,0:T(8,128)(2,1)S(1)} %collective-permute-done.13.refs_6_), channel_id=1, source_target_pairs={{0,1},{1,0},{2,3},{3,2},{4,5},{5,4},{6,7},{7,6},{8,9},{9,8},{10,11... | collective-permute-start | bytes 294920 | tf_op jit(solution)/shard_map/ppermute | solution.py:589

commit v19 on v18

--- a/solution.py
+++ b/solution.py
@@ -207,25 +207,70 @@
     )
 
 
+def embed_own(own_ref, embed2_ref, own):
+    width = embed2_ref.shape[1] // 2
+    both = dot_nn(own_ref[...], embed2_ref[...])
+    return jnp.concatenate(
+        [
+            both[k * own : (k + 1) * own, r2 * width : (r2 + 1) * width]
+            for k in range(both.shape[0] // own)
+            for r2 in range(2)
+        ],
+        0,
+    )
+
+
 def near_kernel(parts, *refs):
     tables_refs, refs = refs[:parts], refs[parts:]
     (
         codes_ref,
+        embed_ref,
+        col_qkv_hbm,
         scores_ref,
         values_ref,
         tied_ref,
         hot_ref,
-        own_ref,
+        embed2_ref,
+        embedded_ref,
+        weight_ref,
         tables_ref,
         table_ref,
+        own_ref,
         live_own_ref,
         sum_ref,
+        sems,
     ) = refs
     width = values_ref.shape[1]
     heads = width // HEAD_DIM
     local = width // parts
+    vocab = embed_ref.shape[0]
     group = lax.axis_index("seq")
     part = lax.axis_index("head")
+
+    odd = part % 2
+    loads = []
+    for t in range(3):
+        first = pl.multiple_of(t * local + odd * HEAD_DIM, HEAD_DIM)
+        last = pl.multiple_of(t * local + (1 - odd) * LANES, HEAD_DIM)
+        third = (3 + t) * LANES
+        loads += [
+            pltpu.make_async_copy(
+                col_qkv_hbm.at[pl.ds(first, LANES)],
+                weight_ref.at[pl.ds(t * LANES, LANES)],
+                sems.at[2 * t],
+            ),
+            pltpu.make_async_copy(
+                col_qkv_hbm.at[pl.ds(last, HEAD_DIM)],
+                weight_ref.at[pl.ds(third, HEAD_DIM)],
+                sems.at[2 * t + 1],
+            ),
+        ]
+        weight_ref[third + HEAD_DIM : third + LANES, :] = jnp.zeros((HEAD_DIM, width), bf16)
+    for load in loads:
+        load.start()
+    embed2_ref[...] = jnp.zeros(embed2_ref.shape, bf16)
+    embed2_ref[0:vocab, 0:width] = embed_ref[...]
+    embed2_ref[CODES : CODES + vocab, width : 2 * width] = embed_ref[...]
     for p in range(parts):
         tables_ref[part ^ p] = tables_refs[p][...]
 
@@ -249,9 +294,12 @@
 
     one_hots(codes_ref[...], group, hot_ref, own_ref, live_own_ref)
     tied_ref[...] = tied_sum(scores_ref, live_own_ref, hot_ref, sum_ref)
-
-
-def attend_near(tables, codes, own):
+    embedded_ref[...] = embed_own(own_ref, embed2_ref, own_ref.shape[0] // (hot_ref.shape[0] // LANES))
+    for load in loads:
+        load.wait()
+
+
+def attend_near(tables, codes, embed, col_qkv, own):
     parts = len(tables)
     width = tables[0].shape[1] // 3 * parts
     heads = width // HEAD_DIM
@@ -263,18 +311,24 @@
             jax.ShapeDtypeStruct((CODES, width), bf16),
             jax.ShapeDtypeStruct((heads * own, cols), f32),
             jax.ShapeDtypeStruct((rows * CODES, cols), bf16),
-            jax.ShapeDtypeStruct((rows // 2 * own, LANES), bf16),
+            jax.ShapeDtypeStruct((2 * CODES, 2 * width), bf16),
+            jax.ShapeDtypeStruct((rows * own, width), f32),
+            jax.ShapeDtypeStruct((6 * LANES, width), bf16),
         ),
+        in_specs=[pl.BlockSpec(memory_space=pltpu.VMEM)] * (parts + 2)
+        + [pl.BlockSpec(memory_space=pltpu.HBM)],
         scratch_shapes=[
             pltpu.VMEM((parts,) + tables[0].shape, bf16),
             pltpu.VMEM((2, CODES, width), bf16),
             pltpu.VMEM((rows // 2 * own, LANES), bf16),
+            pltpu.VMEM((rows // 2 * own, LANES), bf16),
             pltpu.VMEM((heads * own, 2 * rows * CODES), bf16),
+            pltpu.SemaphoreType.DMA((6,)),
         ],
         cost_estimate=pl.CostEstimate(flops=10**9, bytes_accessed=10**6, transcendentals=0),
         compiler_params=pltpu.CompilerParams(vmem_limit_bytes=LARGE_VMEM),
         name="near_scores",
-    )(*tables, codes)
+    )(*tables, codes, embed, in_hbm(col_qkv))
 
 
 def row_kernel(
@@ -365,40 +419,25 @@
     (
         live_ref,
         row_context_ref,
-        near_own_ref,
+        embedded_ref,
         far_own_ref,
-        embed_ref,
-        col_qkv_ref,
+        embed2_ref,
+        weight_ref,
         *context_refs,
         mixed_out_ref,
         row_out_ref,
-        embed2_ref,
-        weight_ref,
     ) = refs
     rows = live_ref.shape[0]
     tokens, width = row_context_ref.shape
     pairs = rows // 2
     own = tokens // rows
-    vocab = embed_ref.shape[0]
     local = width // parts
     part = lax.axis_index("head")
 
     for p in range(parts):
         row_out_ref[part ^ p] = row_out_refs[p][...]
-    embed2_ref[...] = jnp.zeros(embed2_ref.shape, bf16)
-    embed2_ref[0:vocab, 0:width] = embed_ref[...]
-    embed2_ref[CODES : CODES + vocab, width : 2 * width] = embed_ref[...]
-
-    own_codes = jnp.concatenate([near_own_ref[...], far_own_ref[...]], 0)
-    embedded2 = dot_nn(own_codes, embed2_ref[...])
-    embedded = jnp.concatenate(
-        [
-            embedded2[k * own : (k + 1) * own, r2 * width : (r2 + 1) * width]
-            for k in range(pairs)
-            for r2 in range(2)
-        ],
-        0,
-    )
+
+    embedded = jnp.concatenate([embedded_ref[...], embed_own(far_own_ref, embed2_ref, own)], 0)
     mixed = embedded + dot_nt(row_context_ref[...], row_out_ref[...].reshape(width, width))
     for p in range(parts):
 
@@ -417,13 +456,6 @@
         return jnp.swapaxes(values.reshape(shape), 0, 1).reshape(tokens, values.shape[1])
 
     odd = part % 2
-    for t in range(3):
-        first = pl.multiple_of(t * local + odd * HEAD_DIM, HEAD_DIM)
-        last = pl.multiple_of(t * local + (1 - odd) * LANES, HEAD_DIM)
-        third = (3 + t) * LANES
-        weight_ref[t * LANES : (t + 1) * LANES, :] = col_qkv_ref[pl.ds(first, LANES), :]
-        weight_ref[third : third + HEAD_DIM, :] = col_qkv_ref[pl.ds(last, HEAD_DIM), :]
-        weight_ref[third + HEAD_DIM : third + LANES, :] = jnp.zeros((HEAD_DIM, width), bf16)
     proj = [
         dot_nt(normed, weight_ref[2 * j * LANES : 2 * (j + 1) * LANES, :]) for j in range(3)
     ]
@@ -477,7 +509,7 @@
         start += count
 
 
-def attend_columns_here(row_outs, live, row_context, near_own, far_own, embed, col_qkv):
+def attend_columns_here(row_outs, live, row_context, embedded, far_own, embed2, weights):
     parts = len(row_outs)
     tokens, width = row_context.shape
     local = width // parts
@@ -491,13 +523,11 @@
         ),
         scratch_shapes=[
             pltpu.VMEM((parts, local, width), bf16),
-            pltpu.VMEM((2 * CODES, 2 * width), bf16),
-            pltpu.VMEM((6 * LANES, width), bf16),
         ],
         cost_estimate=pl.CostEstimate(flops=2 * 10**9, bytes_accessed=10**6, transcendentals=0),
         compiler_params=pltpu.CompilerParams(vmem_limit_bytes=LARGE_VMEM),
         name="column_attention",
-    )(*row_outs, live, row_context, near_own, far_own, embed, col_qkv)
+    )(*row_outs, live, row_context, embedded, far_own, embed2, weights)
 
 
 def finish_kernel(parts, groups, *refs):
@@ -616,16 +646,12 @@
         received = pairwise(coded, lambda g, p, step=step: (g ^ step, p))
         step *= 2
     codes = (coded, received)
-    *near_scores, near_own = attend_near(tables, codes[0], own)
+    *near_scores, embed2, embedded, weights = attend_near(
+        tables, coded, embed, col_qkv.reshape(3 * local, width), own
+    )
     row_context, far_own, live = attend_rows(near_scores, *codes, own)
     *halves_here, mixed = attend_columns_here(
-        row_outs,
-        live,
-        row_context,
-        near_own,
-        far_own,
-        embed,
-        col_qkv.reshape(3 * local, width),
+        row_outs, live, row_context, embedded, far_own, embed2, weights
     )
     contexts = []
     for context in halves_here:

time: 44 us -> 44.6 us (1.014)
  Pallas kernels: 10.2 us -> 11.5 us
  blocking collectives: 13.3 us -> 12.5 us
    pallas_call x1, Pallas kernels: 1.19 us -> 2.52 us  [attend_near(): pl.pallas_call(functools.partial(near_kernel, parts), out_shape=(jax.Shap...]
    all_to_all x1, blocking collectives: 13.3 us -> 12.5 us  [fast_body(): lax.all_to_all(blocks, 'seq', split_axis=0, concat_axis=0, tiled=True)]
  transfers between devices with their start and end apart: 15 -> 15, of which waited for: 6 -> 5; matrix products, arithmetic and copies ran while one was open for 0% -> 0% of each run, Pallas kernels for 13% -> 16%
where the time goes in v19:
time: 44.6 us; the launch traced here: 44.4 us
  starting transfers between devices  12.5 us (28%)
  blocking collectives  12.5 us (28%)
  Pallas kernels  11.5 us (26%)
  waiting for transfers between devices  7.72 us (17%)
    all_to_all x1, blocking collectives, fast_body(): lax.all_to_all(blocks, 'seq', split_axis=0, concat_axis=0, tiled=True)  12.5 us
    ppermute x15, starting transfers between devices, pairwise(): lax.ppermute(value, ('seq', 'head'), [(i, g * parts + p) for i, (g, p) in...  12.5 us
    ppermute x15, waiting for transfers between devices, pairwise(): lax.ppermute(value, ('seq', 'head'), [(i, g * parts + p) for i, (g, p) in...  7.72 us
    pallas_call x1, Pallas kernels, attend_columns_here(): pl.pallas_call(functools.partial(column_kernel, parts), out_shape=(jax.Sh...  3.14 us
    pallas_call x1, Pallas kernels, attend_near(): pl.pallas_call(functools.partial(near_kernel, parts), out_shape=(jax.Shap...  2.52 us
    pallas_call x1, Pallas kernels, attend_rows(): pl.pallas_call(row_kernel, out_shape=(jax.ShapeDtypeStruct((2 * half * ow...  1.87 us
    pallas_call x1, Pallas kernels, make_tables(): pl.pallas_call(table_kernel, out_shape=jax.ShapeDtypeStruct((TABLE_ROWS,...  1.84 us
  transfers between devices with their start and end apart: 15, of which 5 were waited for; matrix products, arithmetic and copies ran while one was open for 0% of the time, Pallas kernels for 16%

profile of v19, /device:TPU:0, one launch (start us, length us, event | category | flops | bytes accessed | tf_op | source)
XLA Modules:
  0.0 44.4 jit_solution(12060348005127902830)
XLA Ops:
  0.0 2.9 %collective-permute-start.2 = (bf16[192,768]{1,0:T(8,128)(2,1)}, bf16[192,768]{1,0:T(8,128)(2,1)S(1)}, u32[]{:S(2)}, u32[]{:S(2)}) collective-permute-start(bf16[192,768]{1,0:T(8,128)(2,1)} %refs_0_), channel_id=1, source_target_pairs={{0,2},{1,3},{2,0},{3,1},{4,6},{5,7},{6,4},{7,5},{8,10},{9,11},{10,... | collective-permute-start | bytes 884744 | tf_op jit(solution)/shard_map/ppermute | solution.py:619
  2.9 0.8 %codes.1.own_ref = s32[8,256]{1,0:T(8,128)S(1)} custom-call(s32[2,256]{1,0:T(2,128)} %ids_hbm.1, s32[2]{0:T(128)} %live_hbm.1), custom_call_target="tpu_custom_call" | custom-call | tf_op jit(solution)/shard_map/codes/pallas_call | solution.py:70
  3.8 0.0 copy-start.1
  3.8 0.0 copy-start.2
  3.8 1.6 %collective-permute-start = (s32[8,256]{1,0:T(8,128)S(1)}, s32[8,256]{1,0:T(8,128)S(1)}, u32[]{:S(2)}, u32[]{:S(2)}) collective-permute-start(s32[8,256]{1,0:T(8,128)S(1)} %codes.1.own_ref), channel_id=1, source_target_pairs={{0,4},{1,5},{2,6},{3,7},{4,0},{5,1},{6,2},{7,3},{8,12},{9,13},{10,... | collective-permute-start | bytes 24584 | tf_op jit(solution)/shard_map/ppermute | solution.py:619
  5.4 1.8 %tables.1.refs_0_ = bf16[40,576]{1,0:T(8,128)(2,1)S(1)} custom-call(bf16[33,768]{1,0:T(8,128)(2,1)} %refs_5_.1, bf16[3,192,768]{2,1,0:T(8,128)(2,1)} %qkv_hbm), custom_call_target="tpu_custom_call" | custom-call | flops 2000000000 | bytes 884736 | tf_op jit(solution)/shard_map/tables/pallas_call | solution.py:120
  7.2 0.3 collective-permute-done.other_ref
  7.5 1.6 %collective-permute-start.1 = (s32[8,256]{1,0:T(8,128)S(1)}, s32[8,256]{1,0:T(8,128)S(1)}, u32[]{:S(2)}, u32[]{:S(2)}) collective-permute-start(s32[8,256]{1,0:T(8,128)S(1)} %join.2.own_ref), channel_id=1, source_target_pairs={{0,8},{1,9},{2,10},{3,11},{4,12},{5,13},{6,14},{7,15},{8,0},{9,1},... | collective-permute-start | bytes 24584 | tf_op jit(solution)/shard_map/ppermute | solution.py:619
  9.1 0.5 %collective-permute-start.6 = (bf16[40,576]{1,0:T(8,128)(2,1)S(1)}, bf16[40,576]{1,0:T(8,128)(2,1)S(1)}, u32[]{:S(2)}, u32[]{:S(2)}) collective-permute-start(bf16[40,576]{1,0:T(8,128)(2,1)S(1)} %tables.1.refs_0_), channel_id=1, source_target_pairs={{0,2},{1,3},{2,0},{3,1},{4,6},{5,7},{6,4},{7,5},{8,10},{9,11},{10,... | collective-permute-start | bytes 138248 | tf_op jit(solution)/shard_map/ppermute | solution.py:619
  9.6 0.0 collective-permute-start.7
  9.6 1.5 %collective-permute-done.1.other_ref = s32[8,256]{1,0:T(8,128)S(1)} collective-permute-done((s32[8,256]{1,0:T(8,128)S(1)}, s32[8,256]{1,0:T(8,128)S(1)}, u32[]{:S(2)}, u32[]{:S(2)}) %collective-permute-start.1) | collective-permute-done | bytes 8224 | tf_op jit(solution)/shard_map/ppermute | solution.py:619
  11.2 0.0 collective-permute-done.2.refs_2_
  11.2 0.1 collective-permute-start.5
  11.3 2.6 %collective-permute-start.8 = (s32[8,256]{1,0:T(8,128)S(1)}, s32[8,256]{1,0:T(8,128)S(1)}, u32[]{:S(2)}, u32[]{:S(2)}) collective-permute-start(s32[8,256]{1,0:T(8,128)S(1)} %join.3.refs_4_.near_codes_ref), channel_id=1, source_target_pairs={{0,16},{1,17},{2,18},{3,19},{4,20},{5,21},{6,22},{7,23},{8,24},{9,... | collective-permute-start | bytes 24584 | tf_op jit(solution)/shard_map/ppermute | solution.py:619
  13.9 0.0 copy-done.1
  13.9 0.2 collective-permute-start.3
  14.1 0.0 collective-permute-done.6.refs_2_
  14.1 0.3 collective-permute-start.4
  14.4 0.0 collective-permute-done.7.refs_3_
  14.4 0.0 collective-permute-done.5.refs_1_
  14.4 0.0 copy-done.2
  14.4 2.5 %near_scores.1 = (bf16[12,128,256]{2,1,0:T(8,128)(2,1)S(1)}, bf16[64,768]{1,0:T(8,128)(2,1)S(1)}, f32[384,256]{1,0:T(8,128)S(1)}, bf16[512,256]{1,0:T(8,128)(2,1...) custom-call(bf16[40,576]{1,0:T(8,128)(2,1)S(1)} %tables.1.refs_0_, ...), custom_call_target="tpu_custom_call" | custom-call | flops 1000000000 | bytes 1000000 | tf_op jit(solution)/shard_map/near_scores/pallas_call | solution.py:307
  17.0 0.0 collective-permute-done.8.far_codes_ref
  17.0 1.9 %row_attention.1 = (bf16[512,768]{1,0:T(8,128)(2,1)S(1)}, bf16[128,128]{1,0:T(8,128)(2,1)S(1)}, f32[16,128]{1,0:T(8,128)S(1)}) custom-call(bf16[12,128,256]{2,1,0:T(8,128)(2,1)S(1)} %get-tuple-element.34.scores_ref, bf16[64,768]{1,0:T(8,128)(2,1)S(1)} %get-tuple-element.35.values_ref, f32[384,256]{1,0:T(8,128)S(1)} %get-tuple-element.36.near_tied_ref, ...), custom_call_target="tpu_custom_call" | custom-call | flops 3000000000 | bytes 1000000 | tf_op jit(solution)/shard_map/row_attention/pallas_call | solution.py:398
  18.8 0.0 collective-permute-done.3.refs_1_
  18.9 0.0 collective-permute-done.4.refs_3_
  18.9 0.0 copy-start
  18.9 3.1 %column_attention.1 = (bf16[384,128]{1,0:T(8,128)(2,1)S(1)}, bf16[384,128]{1,0:T(8,128)(2,1)S(1)}, f32[512,192]{1,0:T(8,128)S(1)}) custom-call(bf16[192,768]{1,0:T(8,128)(2,1)S(1)} %copy-done.1, bf16[192,768]{1,0:T(8,128)(2,1)S(1)} %collective-permute-done.3.refs_1_, bf16[192,768]{1,0:T(8,128)(2,1)S(1)} %collective-permute-done.2.refs_2_, ...), custom_call_target="tpu_custom_call" | custom-call | flops 2000000000 | bytes 1000000 | tf_op jit(solution)/shard_map/column_attention/pallas_call | solution.py:517
  22.0 1.2 %collective-permute-start.10 = (bf16[384,128]{1,0:T(8,128)(2,1)S(1)}, bf16[384,128]{1,0:T(8,128)(2,1)S(1)}, u32[]{:S(2)}, u32[]{:S(2)}) collective-permute-start(bf16[384,128]{1,0:T(8,128)(2,1)S(1)} %get-tuple-element.44.refs_0_), channel_id=1, source_target_pairs={{0,2},{1,3},{2,0},{3,1},{4,6},{5,7},{6,4},{7,5},{8,10},{9,11},{10,... | collective-permute-start | bytes 294920 | tf_op jit(solution)/shard_map/ppermute | solution.py:619
  23.2 0.9 %collective-permute-start.13 = (bf16[384,128]{1,0:T(8,128)(2,1)S(1)}, bf16[384,128]{1,0:T(8,128)(2,1)S(1)}, u32[]{:S(2)}, u32[]{:S(2)}) collective-permute-start(bf16[384,128]{1,0:T(8,128)(2,1)S(1)} %get-tuple-element.45.refs_4_), channel_id=1, source_target_pairs={{0,2},{1,3},{2,0},{3,1},{4,6},{5,7},{6,4},{7,5},{8,10},{9,11},{10,... | collective-permute-start | bytes 294920 | tf_op jit(solution)/shard_map/ppermute | solution.py:619
  24.1 0.0 collective-permute-start.12
  24.1 0.5 %collective-permute-start.9 = (bf16[384,128]{1,0:T(8,128)(2,1)S(1)}, bf16[384,128]{1,0:T(8,128)(2,1)S(1)}, u32[]{:S(2)}, u32[]{:S(2)}) collective-permute-start(bf16[384,128]{1,0:T(8,128)(2,1)S(1)} %get-tuple-element.44.refs_0_), channel_id=1, source_target_pairs={{0,1},{1,0},{2,3},{3,2},{4,5},{5,4},{6,7},{7,6},{8,9},{9,8},{10,11... | collective-permute-start | bytes 294920 | tf_op jit(solution)/shard_map/ppermute | solution.py:619
  24.6 3.1 %collective-permute-done.10.refs_2_ = bf16[384,128]{1,0:T(8,128)(2,1)S(1)} collective-permute-done((bf16[384,128]{1,0:T(8,128)(2,1)S(1)}, bf16[384,128]{1,0:T(8,128)(2,1)S(1)}, u32[]{:S(2)}, u32[]{:S(2)}) %collective-permute-start.10) | collective-permute-done | bytes 98336 | tf_op jit(solution)/shard_map/ppermute | solution.py:619
  27.7 0.0 collective-permute-start.11
  27.7 1.5 %collective-permute-done.13.refs_6_ = bf16[384,128]{1,0:T(8,128)(2,1)S(1)} collective-permute-done((bf16[384,128]{1,0:T(8,128)(2,1)S(1)}, bf16[384,128]{1,0:T(8,128)(2,1)S(1)}, u32[]{:S(2)}, u32[]{:S(2)}) %collective-permute-start.13) | collective-permute-done | bytes 98336 | tf_op jit(solution)/shard_map/ppermute | solution.py:619
  29.2 0.0 collective-permute-start.14
  29.2 0.0 collective-permute-done.12.refs_5_
  29.2 0.0 collective-permute-done.9.refs_1_
  29.2 0.0 collective-permute-done.11.refs_3_
  29.2 1.3 %collective-permute-done.14.refs_7_ = bf16[384,128]{1,0:T(8,128)(2,1)S(1)} collective-permute-done((bf16[384,128]{1,0:T(8,128)(2,1)S(1)}, bf16[384,128]{1,0:T(8,128)(2,1)S(1)}, u32[]{:S(2)}, u32[]{:S(2)}) %collective-permute-start.14) | collective-permute-done | bytes 98336 | tf_op jit(solution)/shard_map/ppermute | solution.py:619
  30.5 0.0 copy-done
  30.5 0.5 %finish.1 = bf16[8,96,128]{2,1,0:T(8,128)(2,1)S(1)} custom-call(bf16[384,128]{1,0:T(8,128)(2,1)S(1)} %get-tuple-element.44.refs_0_, bf16[384,128]{1,0:T(8,128)(2,1)S(1)} %collective-permute-done.9.refs_1_, bf16[384,128]{1,0:T(8,128)(2,1)S(1)} %collective-permute-done.10.refs_2_, bf16[384,128]{1,0:T(8,128)(2,1)S(1)} %collective-permute-done.11.refs_3_, ...), custom_call_target="tpu_custom_call" | custom-call | tf_op jit(solution)/shard_map/finish/pallas_call | solution.py:574
  31.0 12.5 %all_to_all.5.blocks_ref = bf16[8,96,128]{2,1,0:T(8,128)(2,1)S(1)} all-to-all(bf16[8,96,128]{2,1,0:T(8,128)(2,1)S(1)} %finish.1), channel_id=1, replica_groups=mesh['seq'=8,'head'=4] {'seq'}, dimensions={0} | all-to-all | bytes 393216 | tf_op jit(solution)/shard_map/all_to_all | solution.py:663
  43.6 0.8 %order.1 = bf16[2,192,256]{2,1,0:T(8,128)(2,1)} custom-call(bf16[8,96,128]{2,1,0:T(8,128)(2,1)S(1)} %all_to_all.5.blocks_ref), custom_call_target="tpu_custom_call" | custom-call | tf_op jit(solution)/shard_map/order/pallas_call | solution.py:601
  (2 shorter events, 0.0 us)
Async XLA Ops:
  0.0 11.2 %collective-permute-start.2 = (bf16[192,768]{1,0:T(8,128)(2,1)}, bf16[192,768]{1,0:T(8,128)(2,1)S(1)}, u32[]{:S(2)}, u32[]{:S(2)}) collective-permute-start(bf16[192,768]{1,0:T(8,128)(2,1)} %refs_0_), channel_id=1, source_target_pairs={{0,2},{1,3},{2,0},{3,1},{4,6},{5,7},{6,4},{7,5},{8,10},{9,11},{10,... | collective-permute-start | bytes 884744 | tf_op jit(solution)/shard_map/ppermute | solution.py:619
  3.8 10.1 %copy-start.1 = (bf16[192,768]{1,0:T(8,128)(2,1)S(1)}, bf16[192,768]{1,0:T(8,128)(2,1)}, u32[]{:S(2)}) copy-start(bf16[192,768]{1,0:T(8,128)(2,1)} %refs_0_) | copy-start | bytes 884740
  3.8 10.6 %copy-start.2 = (bf16[33,768]{1,0:T(8,128)(2,1)S(1)}, bf16[33,768]{1,0:T(8,128)(2,1)}, u32[]{:S(2)}) copy-start(bf16[33,768]{1,0:T(8,128)(2,1)} %refs_5_.1) | copy-start | bytes 152068
  3.8 3.7 %collective-permute-start = (s32[8,256]{1,0:T(8,128)S(1)}, s32[8,256]{1,0:T(8,128)S(1)}, u32[]{:S(2)}, u32[]{:S(2)}) collective-permute-start(s32[8,256]{1,0:T(8,128)S(1)} %codes.1.own_ref), channel_id=1, source_target_pairs={{0,4},{1,5},{2,6},{3,7},{4,0},{5,1},{6,2},{7,3},{8,12},{9,13},{10,... | collective-permute-start | bytes 24584 | tf_op jit(solution)/shard_map/ppermute | solution.py:619
  7.5 3.7 %collective-permute-start.1 = (s32[8,256]{1,0:T(8,128)S(1)}, s32[8,256]{1,0:T(8,128)S(1)}, u32[]{:S(2)}, u32[]{:S(2)}) collective-permute-start(s32[8,256]{1,0:T(8,128)S(1)} %join.2.own_ref), channel_id=1, source_target_pairs={{0,8},{1,9},{2,10},{3,11},{4,12},{5,13},{6,14},{7,15},{8,0},{9,1},... | collective-permute-start | bytes 24584 | tf_op jit(solution)/shard_map/ppermute | solution.py:619
  9.1 5.0 %collective-permute-start.6 = (bf16[40,576]{1,0:T(8,128)(2,1)S(1)}, bf16[40,576]{1,0:T(8,128)(2,1)S(1)}, u32[]{:S(2)}, u32[]{:S(2)}) collective-permute-start(bf16[40,576]{1,0:T(8,128)(2,1)S(1)} %tables.1.refs_0_), channel_id=1, source_target_pairs={{0,2},{1,3},{2,0},{3,1},{4,6},{5,7},{6,4},{7,5},{8,10},{9,11},{10,... | collective-permute-start | bytes 138248 | tf_op jit(solution)/shard_map/ppermute | solution.py:619
  9.6 4.8 %collective-permute-start.7 = (bf16[40,576]{1,0:T(8,128)(2,1)S(1)}, bf16[40,576]{1,0:T(8,128)(2,1)S(1)}, u32[]{:S(2)}, u32[]{:S(2)}) collective-permute-start(bf16[40,576]{1,0:T(8,128)(2,1)S(1)} %tables.1.refs_0_), channel_id=1, source_target_pairs={{0,3},{1,2},{2,1},{3,0},{4,7},{5,6},{6,5},{7,4},{8,11},{9,10},{10,... | collective-permute-start | bytes 138248 | tf_op jit(solution)/shard_map/ppermute | solution.py:619
  11.2 3.3 %collective-permute-start.5 = (bf16[40,576]{1,0:T(8,128)(2,1)S(1)}, bf16[40,576]{1,0:T(8,128)(2,1)S(1)}, u32[]{:S(2)}, u32[]{:S(2)}) collective-permute-start(bf16[40,576]{1,0:T(8,128)(2,1)S(1)} %tables.1.refs_0_), channel_id=1, source_target_pairs={{0,1},{1,0},{2,3},{3,2},{4,5},{5,4},{6,7},{7,6},{8,9},{9,8},{10,11... | collective-permute-start | bytes 138248 | tf_op jit(solution)/shard_map/ppermute | solution.py:619
  11.3 5.7 %collective-permute-start.8 = (s32[8,256]{1,0:T(8,128)S(1)}, s32[8,256]{1,0:T(8,128)S(1)}, u32[]{:S(2)}, u32[]{:S(2)}) collective-permute-start(s32[8,256]{1,0:T(8,128)S(1)} %join.3.refs_4_.near_codes_ref), channel_id=1, source_target_pairs={{0,16},{1,17},{2,18},{3,19},{4,20},{5,21},{6,22},{7,23},{8,24},{9,... | collective-permute-start | bytes 24584 | tf_op jit(solution)/shard_map/ppermute | solution.py:619
  13.9 4.9 %collective-permute-start.3 = (bf16[192,768]{1,0:T(8,128)(2,1)S(1)}, bf16[192,768]{1,0:T(8,128)(2,1)S(1)}, u32[]{:S(2)}, u32[]{:S(2)}) collective-permute-start(bf16[192,768]{1,0:T(8,128)(2,1)S(1)} %copy-done.1), channel_id=1, source_target_pairs={{0,1},{1,0},{2,3},{3,2},{4,5},{5,4},{6,7},{7,6},{8,9},{9,8},{10,11... | collective-permute-start | bytes 884744 | tf_op jit(solution)/shard_map/ppermute | solution.py:619
  14.1 4.8 %collective-permute-start.4 = (bf16[192,768]{1,0:T(8,128)(2,1)S(1)}, bf16[192,768]{1,0:T(8,128)(2,1)S(1)}, u32[]{:S(2)}, u32[]{:S(2)}) collective-permute-start(bf16[192,768]{1,0:T(8,128)(2,1)S(1)} %collective-permute-done.2.refs_2_), channel_id=1, source_target_pairs={{0,1},{1,0},{2,3},{3,2},{4,5},{5,4},{6,7},{7,6},{8,9},{9,8},{10,11... | collective-permute-start | bytes 884744 | tf_op jit(solution)/shard_map/ppermute | solution.py:619
  18.9 11.7 %copy-start = (bf16[192,768]{1,0:T(8,128)(2,1)S(1)}, bf16[192,768]{1,0:T(8,128)(2,1)}, u32[]{:S(2)}) copy-start(bf16[192,768]{1,0:T(8,128)(2,1)} %refs_9_.1) | copy-start | bytes 884740
  22.0 5.7 %collective-permute-start.10 = (bf16[384,128]{1,0:T(8,128)(2,1)S(1)}, bf16[384,128]{1,0:T(8,128)(2,1)S(1)}, u32[]{:S(2)}, u32[]{:S(2)}) collective-permute-start(bf16[384,128]{1,0:T(8,128)(2,1)S(1)} %get-tuple-element.44.refs_0_), channel_id=1, source_target_pairs={{0,2},{1,3},{2,0},{3,1},{4,6},{5,7},{6,4},{7,5},{8,10},{9,11},{10,... | collective-permute-start | bytes 294920 | tf_op jit(solution)/shard_map/ppermute | solution.py:619
  23.2 6.0 %collective-permute-start.13 = (bf16[384,128]{1,0:T(8,128)(2,1)S(1)}, bf16[384,128]{1,0:T(8,128)(2,1)S(1)}, u32[]{:S(2)}, u32[]{:S(2)}) collective-permute-start(bf16[384,128]{1,0:T(8,128)(2,1)S(1)} %get-tuple-element.45.refs_4_), channel_id=1, source_target_pairs={{0,2},{1,3},{2,0},{3,1},{4,6},{5,7},{6,4},{7,5},{8,10},{9,11},{10,... | collective-permute-start | bytes 294920 | tf_op jit(solution)/shard_map/ppermute | solution.py:619
  24.1 5.1 %collective-permute-start.12 = (bf16[384,128]{1,0:T(8,128)(2,1)S(1)}, bf16[384,128]{1,0:T(8,128)(2,1)S(1)}, u32[]{:S(2)}, u32[]{:S(2)}) collective-permute-start(bf16[384,128]{1,0:T(8,128)(2,1)S(1)} %get-tuple-element.45.refs_4_), channel_id=1, source_target_pairs={{0,1},{1,0},{2,3},{3,2},{4,5},{5,4},{6,7},{7,6},{8,9},{9,8},{10,11... | collective-permute-start | bytes 294920 | tf_op jit(solution)/shard_map/ppermute | solution.py:619
  24.1 5.1 %collective-permute-start.9 = (bf16[384,128]{1,0:T(8,128)(2,1)S(1)}, bf16[384,128]{1,0:T(8,128)(2,1)S(1)}, u32[]{:S(2)}, u32[]{:S(2)}) collective-permute-start(bf16[384,128]{1,0:T(8,128)(2,1)S(1)} %get-tuple-element.44.refs_0_), channel_id=1, source_target_pairs={{0,1},{1,0},{2,3},{3,2},{4,5},{5,4},{6,7},{7,6},{8,9},{9,8},{10,11... | collective-permute-start | bytes 294920 | tf_op jit(solution)/shard_map/ppermute | solution.py:619
  27.7 1.5 %collective-permute-start.11 = (bf16[384,128]{1,0:T(8,128)(2,1)S(1)}, bf16[384,128]{1,0:T(8,128)(2,1)S(1)}, u32[]{:S(2)}, u32[]{:S(2)}) collective-permute-start(bf16[384,128]{1,0:T(8,128)(2,1)S(1)} %collective-permute-done.10.refs_2_), channel_id=1, source_target_pairs={{0,1},{1,0},{2,3},{3,2},{4,5},{5,4},{6,7},{7,6},{8,9},{9,8},{10,11... | collective-permute-start | bytes 294920 | tf_op jit(solution)/shard_map/ppermute | solution.py:619
  29.2 1.3 %collective-permute-start.14 = (bf16[384,128]{1,0:T(8,128)(2,1)S(1)}, bf16[384,128]{1,0:T(8,128)(2,1)S(1)}, u32[]{:S(2)}, u32[]{:S(2)}) collective-permute-start(bf16[384,128]{1,0:T(8,128)(2,1)S(1)} %collective-permute-done.13.refs_6_), channel_id=1, source_target_pairs={{0,1},{1,0},{2,3},{3,2},{4,5},{5,4},{6,7},{7,6},{8,9},{9,8},{10,11... | collective-permute-start | bytes 294920 | tf_op jit(solution)/shard_map/ppermute | solution.py:619

commit v20 on v18

--- a/solution.py
+++ b/solution.py
@@ -47,38 +47,6 @@
 
 def iota(shape, axis):
     return lax.broadcasted_iota(jnp.int32, shape, axis)
-
-
-def code_kernel(ids_hbm, live_hbm, out_ref, ids_ref, live_ref, sems):
-    loads = [
-        pltpu.make_async_copy(ids_hbm, ids_ref, sems.at[0]),
-        pltpu.make_async_copy(live_hbm, live_ref, sems.at[1]),
-    ]
-    for load in loads:
-        load.start()
-    for load in loads:
-        load.wait()
-    row = iota(ids_ref.shape, 0)
-    live = jnp.zeros(ids_ref.shape, jnp.int32)
-    for r in range(ids_ref.shape[0]):
-        live = jnp.where(row == r, live_ref[r], live)
-    coded = ids_ref[...] + 65536 * live
-    out_ref[...] = jnp.concatenate([coded] * (out_ref.shape[0] // coded.shape[0]), 0)
-
-
-def make_codes(ids, pad_mask, height):
-    return pl.pallas_call(
-        code_kernel,
-        out_shape=jax.ShapeDtypeStruct((height, ids.shape[1]), jnp.int32),
-        in_specs=[pl.BlockSpec(memory_space=pltpu.HBM)] * 2,
-        scratch_shapes=[
-            pltpu.VMEM(ids.shape, jnp.int32),
-            pltpu.SMEM(pad_mask.shape, jnp.int32),
-            pltpu.SemaphoreType.DMA((2,)),
-        ],
-        compiler_params=pltpu.CompilerParams(vmem_limit_bytes=SMALL_VMEM),
-        name="codes",
-    )(in_hbm(ids), in_hbm(pad_mask))
 
 
 def join_kernel(rows, own_ref, other_ref, out_ref):
@@ -96,43 +64,91 @@
     )(own, other)
 
 
-def table_kernel(embed_hbm, qkv_hbm, out_ref, embed_ref, qkv_ref, padded_ref, sems):
+def join_raw_kernel(own_ref, ids_ref, live_ref, out_ref):
+    rows = ids_ref.shape[0]
+    live = live_ref[...]
+    other = ids_ref[...] + 65536 * jnp.concatenate(
+        [jnp.broadcast_to(live[:, r : r + 1], (1, ids_ref.shape[1])) for r in range(rows)], 0
+    )
+    both = jnp.concatenate([own_ref[0:rows], other], 0)
+    out_ref[...] = jnp.concatenate([both] * (out_ref.shape[0] // (2 * rows)), 0)
+
+
+def join_raw(own, ids, pad_mask):
+    return pl.pallas_call(
+        join_raw_kernel,
+        out_shape=jax.ShapeDtypeStruct(own.shape, own.dtype),
+        compiler_params=pltpu.CompilerParams(vmem_limit_bytes=SMALL_VMEM),
+        name="join_raw",
+    )(own, ids, pad_mask)
+
+
+def table_kernel(
+    ids_hbm,
+    live_hbm,
+    embed_hbm,
+    qkv_hbm,
+    out_ref,
+    coded_ref,
+    ids_ref,
+    live_ref,
+    embed_ref,
+    qkv_ref,
+    padded_ref,
+    sems,
+):
     kinds = qkv_ref.shape[0]
-    loads = [pltpu.make_async_copy(embed_hbm, embed_ref, sems.at[kinds])]
+    loads = [
+        pltpu.make_async_copy(embed_hbm, embed_ref, sems.at[kinds]),
+        pltpu.make_async_copy(ids_hbm, ids_ref, sems.at[kinds + 1]),
+        pltpu.make_async_copy(live_hbm, live_ref, sems.at[kinds + 2]),
+    ]
     loads += [
         pltpu.make_async_copy(qkv_hbm.at[t], qkv_ref.at[t], sems.at[t]) for t in range(kinds)
     ]
     for load in loads:
         load.start()
     padded_ref[...] = jnp.zeros(padded_ref.shape, f32)
-    loads[0].wait()
+    for load in loads[0:3]:
+        load.wait()
     padded_ref[0 : embed_ref.shape[0], :] = embed_ref[...].astype(f32)
     normed = layer_norm(padded_ref[...]).astype(bf16)
+    row = iota(ids_ref.shape, 0)
+    live = jnp.zeros(ids_ref.shape, jnp.int32)
+    for r in range(ids_ref.shape[0]):
+        live = jnp.where(row == r, live_ref[r], live)
+    coded = ids_ref[...] + 65536 * live
+    coded_ref[...] = jnp.concatenate([coded] * (coded_ref.shape[0] // coded.shape[0]), 0)
     tables = []
     for t in range(kinds):
-        loads[1 + t].wait()
+        loads[3 + t].wait()
         tables.append(dot_nt(normed, qkv_ref[t]))
     out_ref[...] = jnp.concatenate(tables, 1).astype(bf16)
 
 
-def make_tables(embed, row_qkv):
+def make_tables(ids, pad_mask, embed, row_qkv, height):
     kinds, local, width = row_qkv.shape
     return pl.pallas_call(
         table_kernel,
-        out_shape=jax.ShapeDtypeStruct((TABLE_ROWS, kinds * local), bf16),
-        in_specs=[pl.BlockSpec(memory_space=pltpu.HBM)] * 2,
+        out_shape=(
+            jax.ShapeDtypeStruct((TABLE_ROWS, kinds * local), bf16),
+            jax.ShapeDtypeStruct((height, ids.shape[1]), jnp.int32),
+        ),
+        in_specs=[pl.BlockSpec(memory_space=pltpu.HBM)] * 4,
         scratch_shapes=[
+            pltpu.VMEM(ids.shape, jnp.int32),
+            pltpu.SMEM(pad_mask.shape, jnp.int32),
             pltpu.VMEM(embed.shape, bf16),
             pltpu.VMEM(row_qkv.shape, bf16),
             pltpu.VMEM((TABLE_ROWS, width), f32),
-            pltpu.SemaphoreType.DMA((kinds + 1,)),
+            pltpu.SemaphoreType.DMA((kinds + 3,)),
         ],
         cost_estimate=pl.CostEstimate(
             flops=2 * 10**9, bytes_accessed=2 * row_qkv.size, transcendentals=0
         ),
         compiler_params=pltpu.CompilerParams(vmem_limit_bytes=SMALL_VMEM),
         name="tables",
-    )(in_hbm(embed), in_hbm(row_qkv))
+    )(in_hbm(ids), in_hbm(pad_mask), in_hbm(embed), in_hbm(row_qkv))
 
 
 def halves(pair):
@@ -598,14 +614,16 @@
         return g, p ^ 3
 
     far = pairwise(row_out, across)
-    coded = make_codes(ids, pad_mask, rows_here * groups // 2)
-    coded, row_qkv = lax.optimization_barrier((coded, row_qkv))
-    received = pairwise(coded, lambda g, p: (g ^ 1, p))
-    table = make_tables(embed, row_qkv)
+    other_ids = pairwise(ids, lambda g, p: (g ^ 1, p))
+    other_mask = pairwise(pad_mask.reshape(1, rows_here), lambda g, p: (g ^ 1, p))
+    table, coded = make_tables(ids, pad_mask, embed, row_qkv, rows_here * groups // 2)
     tables = [table, None, pairwise(table, across), None]
     step = 2
     while step < groups:
-        coded = join(coded, received, rows_here * step // 2)
+        if step == 2:
+            coded = join_raw(coded, other_ids, other_mask)
+        else:
+            coded = join(coded, received, rows_here * step // 2)
         if step == 2:
             coded, table = lax.optimization_barrier((coded, table))
             tables[3] = pairwise(table, opposite)

time: 44 us -> 43.9 us (level)
  waiting for transfers between devices: 7.76 us -> 8.65 us
  blocking collectives: 13.3 us -> 12.5 us
  Pallas kernels: 10.2 us -> 9.46 us
  starting transfers between devices: 12.5 us -> 13 us
    ppermute x15 -> x16, waiting for transfers between devices: 7.76 us -> 8.65 us  [pairwise(): lax.ppermute(value, ('seq', 'head'), [(i, g * parts + p) for i, (g, p) in...]
    all_to_all x1, blocking collectives: 13.3 us -> 12.5 us  [fast_body(): lax.all_to_all(blocks, 'seq', split_axis=0, concat_axis=0, tiled=True)]
    pallas_call x2, Pallas kernels: 2.66 us -> 1.95 us  [the longest x1 1.87 us: make_tables(): pl.pallas_call(table_kernel, out_shape=(jax.ShapeDtypeStruct((TABLE_ROWS,...]
    ppermute x15 -> x16, starting transfers between devices: 12.5 us -> 13 us  [pairwise(): lax.ppermute(value, ('seq', 'head'), [(i, g * parts + p) for i, (g, p) in...]
  transfers between devices with their start and end apart: 15 -> 16, of which waited for: 6 -> 6; matrix products, arithmetic and copies ran while one was open for 0% -> 0% of each run, Pallas kernels for 13% -> 11%
where the time goes in v20:
time: 43.9 us; the launch traced here: 43.7 us
  starting transfers between devices  13 us (30%)
  blocking collectives  12.5 us (28%)
  Pallas kernels  9.46 us (22%)
  waiting for transfers between devices  8.65 us (20%)
    ppermute x16, starting transfers between devices, pairwise(): lax.ppermute(value, ('seq', 'head'), [(i, g * parts + p) for i, (g, p) in...  13 us
    all_to_all x1, blocking collectives, fast_body(): lax.all_to_all(blocks, 'seq', split_axis=0, concat_axis=0, tiled=True)  12.5 us
    ppermute x16, waiting for transfers between devices, pairwise(): lax.ppermute(value, ('seq', 'head'), [(i, g * parts + p) for i, (g, p) in...  8.65 us
    pallas_call x1, Pallas kernels, attend_columns_here(): pl.pallas_call(functools.partial(column_kernel, parts), out_shape=(jax.Sh...  3.14 us
    pallas_call x1, Pallas kernels, make_tables(): pl.pallas_call(table_kernel, out_shape=(jax.ShapeDtypeStruct((TABLE_ROWS,...  1.87 us
    pallas_call x1, Pallas kernels, attend_rows(): pl.pallas_call(row_kernel, out_shape=(jax.ShapeDtypeStruct((2 * half * ow...  1.86 us
    pallas_call x1, Pallas kernels, attend_near(): pl.pallas_call(functools.partial(near_kernel, parts), out_shape=(jax.Shap...  1.18 us
  transfers between devices with their start and end apart: 16, of which 6 were waited for; matrix products, arithmetic and copies ran while one was open for 0% of the time, Pallas kernels for 11%

profile of v20, /device:TPU:0, one launch (start us, length us, event | category | flops | bytes accessed | tf_op | source)
XLA Modules:
  0.0 43.7 jit_solution(5090509925508806026)
XLA Ops:
  0.0 0.0 copy-start.4
  0.0 2.9 %collective-permute-start.3 = (bf16[192,768]{1,0:T(8,128)(2,1)}, bf16[192,768]{1,0:T(8,128)(2,1)S(1)}, u32[]{:S(2)}, u32[]{:S(2)}) collective-permute-start(bf16[192,768]{1,0:T(8,128)(2,1)} %refs_0_), channel_id=1, source_target_pairs={{0,2},{1,3},{2,0},{3,1},{4,6},{5,7},{6,4},{7,5},{8,10},{9,11},{10,... | collective-permute-start | bytes 884744 | tf_op jit(solution)/shard_map/ppermute | solution.py:605
  2.9 1.5 %collective-permute-start = (s32[2,256]{1,0:T(2,128)}, s32[2,256]{1,0:T(2,128)S(1)}, u32[]{:S(2)}, u32[]{:S(2)}) collective-permute-start(s32[2,256]{1,0:T(2,128)} %ids_hbm.1), channel_id=1, source_target_pairs={{0,4},{1,5},{2,6},{3,7},{4,0},{5,1},{6,2},{7,3},{8,12},{9,13},{10,... | collective-permute-start | bytes 6152 | tf_op jit(solution)/shard_map/ppermute | solution.py:605
  4.5 0.0 copy-done.4
  4.5 0.0 copy-start.2
  4.5 0.5 %collective-permute-start.1 = (s32[1,2]{1,0:T(1,128)S(1)}, s32[1,2]{1,0:T(1,128)S(1)}, u32[]{:S(2)}, u32[]{:S(2)}) collective-permute-start(s32[1,2]{1,0:T(1,128)S(1)} %bitcast.4), channel_id=1, source_target_pairs={{0,4},{1,5},{2,6},{3,7},{4,0},{5,1},{6,2},{7,3},{8,12},{9,13},{10,... | collective-permute-start | bytes 32 | tf_op jit(solution)/shard_map/ppermute | solution.py:605
  5.0 1.9 %tables.1 = (bf16[40,576]{1,0:T(8,128)(2,1)S(1)}, s32[8,256]{1,0:T(8,128)S(1)}) custom-call(s32[2,256]{1,0:T(2,128)} %ids_hbm.1, s32[2]{0:T(128)} %live_hbm.1, bf16[33,768]{1,0:T(8,128)(2,1)} %refs_8_.1, bf16[3,192,768]{2,1,0:T(8,128)(2,1)} %qkv_hbm.1), custom_call_target="tpu_custom_call" | custom-call | flops 2000000000 | bytes 884736 | tf_op jit(solution)/shard_map/tables/pallas_call | solution.py:131
  6.8 1.2 %collective-permute-done.1.live_ref = s32[1,2]{1,0:T(1,128)S(1)} collective-permute-done((s32[1,2]{1,0:T(1,128)S(1)}, s32[1,2]{1,0:T(1,128)S(1)}, u32[]{:S(2)}, u32[]{:S(2)}) %collective-permute-start.1) | collective-permute-done | bytes 40 | tf_op jit(solution)/shard_map/ppermute | solution.py:605
  8.0 0.0 collective-permute-done.ids_ref
  8.0 0.1 join_raw.1.own_ref
  8.1 1.6 %collective-permute-start.2 = (s32[8,256]{1,0:T(8,128)S(1)}, s32[8,256]{1,0:T(8,128)S(1)}, u32[]{:S(2)}, u32[]{:S(2)}) collective-permute-start(s32[8,256]{1,0:T(8,128)S(1)} %join_raw.1.own_ref), channel_id=1, source_target_pairs={{0,8},{1,9},{2,10},{3,11},{4,12},{5,13},{6,14},{7,15},{8,0},{9,1},... | collective-permute-start | bytes 24584 | tf_op jit(solution)/shard_map/ppermute | solution.py:605
  9.7 0.5 %collective-permute-start.7 = (bf16[40,576]{1,0:T(8,128)(2,1)S(1)}, bf16[40,576]{1,0:T(8,128)(2,1)S(1)}, u32[]{:S(2)}, u32[]{:S(2)}) collective-permute-start(bf16[40,576]{1,0:T(8,128)(2,1)S(1)} %get-tuple-element.30.refs_0_), channel_id=1, source_target_pairs={{0,2},{1,3},{2,0},{3,1},{4,6},{5,7},{6,4},{7,5},{8,10},{9,11},{10,... | collective-permute-start | bytes 138248 | tf_op jit(solution)/shard_map/ppermute | solution.py:605
  10.3 0.0 collective-permute-start.8
  10.3 1.5 %collective-permute-done.2.other_ref = s32[8,256]{1,0:T(8,128)S(1)} collective-permute-done((s32[8,256]{1,0:T(8,128)S(1)}, s32[8,256]{1,0:T(8,128)S(1)}, u32[]{:S(2)}, u32[]{:S(2)}) %collective-permute-start.2) | collective-permute-done | bytes 8224 | tf_op jit(solution)/shard_map/ppermute | solution.py:605
  11.8 0.0 collective-permute-done.3.refs_2_
  11.8 0.1 collective-permute-start.6
  11.9 2.6 %collective-permute-start.9 = (s32[8,256]{1,0:T(8,128)S(1)}, s32[8,256]{1,0:T(8,128)S(1)}, u32[]{:S(2)}, u32[]{:S(2)}) collective-permute-start(s32[8,256]{1,0:T(8,128)S(1)} %join.1.refs_4_.near_codes_ref), channel_id=1, source_target_pairs={{0,16},{1,17},{2,18},{3,19},{4,20},{5,21},{6,22},{7,23},{8,24},{9,... | collective-permute-start | bytes 24584 | tf_op jit(solution)/shard_map/ppermute | solution.py:605
  14.5 0.0 copy-done.2
  14.5 0.2 collective-permute-start.4
  14.7 0.0 collective-permute-done.7.refs_2_
  14.7 0.3 collective-permute-start.5
  15.1 0.0 collective-permute-done.8.refs_3_
  15.1 0.0 collective-permute-done.6.refs_1_
  15.1 1.2 %near_scores.1 = (bf16[12,128,256]{2,1,0:T(8,128)(2,1)S(1)}, bf16[64,768]{1,0:T(8,128)(2,1)S(1)}, f32[384,256]{1,0:T(8,128)S(1)}, bf16[512,256]{1,0:T(8,128)(2,1)S(1)}, bf16[128,128]{1,0:T(8,128)(2,1)S(1)}) custom-call(bf16[40,576]{1,0:T(8,128)(2,1)S(1)} %get-tuple-element.30.refs_0_, bf16[40,576]{1,0:T(8,128)(2,1)S(1)} %collective-permute-done.6.refs_1_, ...), custom_call_target="tpu_custom_call" | custom-call | flops 1000000000 | bytes 1000000 | tf_op jit(solution)/shard_map/near_scores/pallas_call | solution.py:275
  16.2 0.3 collective-permute-done.9.far_codes_ref
  16.5 1.9 %row_attention.1 = (bf16[512,768]{1,0:T(8,128)(2,1)S(1)}, bf16[128,128]{1,0:T(8,128)(2,1)S(1)}, f32[16,128]{1,0:T(8,128)S(1)}) custom-call(bf16[12,128,256]{2,1,0:T(8,128)(2,1)S(1)} %get-tuple-element.32.scores_ref, bf16[64,768]{1,0:T(8,128)(2,1)S(1)} %get-tuple-element.33.values_ref, f32[384,256]{1,0:T(8,128)S(1)} %get-tuple-element.34.near_tied_ref, ...), custom_call_target="tpu_custom_call" | custom-call | flops 3000000000 | bytes 1000000 | tf_op jit(solution)/shard_map/row_attention/pallas_call | solution.py:360
  18.4 0.0 collective-permute-done.4.refs_1_
  18.4 0.0 collective-permute-done.5.refs_3_
  18.4 0.0 copy-done.1
  18.4 0.0 copy-done.3
  18.4 0.0 copy-start
  18.4 3.1 %column_attention.1 = (bf16[384,128]{1,0:T(8,128)(2,1)S(1)}, bf16[384,128]{1,0:T(8,128)(2,1)S(1)}, f32[512,192]{1,0:T(8,128)S(1)}) custom-call(bf16[192,768]{1,0:T(8,128)(2,1)S(1)} %copy-done.2, bf16[192,768]{1,0:T(8,128)(2,1)S(1)} %collective-permute-done.4.refs_1_, bf16[192,768]{1,0:T(8,128)(2,1)S(1)} %collective-permute-done.3.refs_2_, ...), custom_call_target="tpu_custom_call" | custom-call | flops 2000000000 | bytes 1000000 | tf_op jit(solution)/shard_map/column_attention/pallas_call | solution.py:501
  21.6 0.6 %collective-permute-start.11 = (bf16[384,128]{1,0:T(8,128)(2,1)S(1)}, bf16[384,128]{1,0:T(8,128)(2,1)S(1)}, u32[]{:S(2)}, u32[]{:S(2)}) collective-permute-start(bf16[384,128]{1,0:T(8,128)(2,1)S(1)} %get-tuple-element.40.refs_0_), channel_id=1, source_target_pairs={{0,2},{1,3},{2,0},{3,1},{4,6},{5,7},{6,4},{7,5},{8,10},{9,11},{10,... | collective-permute-start | bytes 294920 | tf_op jit(solution)/shard_map/ppermute | solution.py:605
  22.2 1.5 %collective-permute-start.14 = (bf16[384,128]{1,0:T(8,128)(2,1)S(1)}, bf16[384,128]{1,0:T(8,128)(2,1)S(1)}, u32[]{:S(2)}, u32[]{:S(2)}) collective-permute-start(bf16[384,128]{1,0:T(8,128)(2,1)S(1)} %get-tuple-element.41.refs_4_), channel_id=1, source_target_pairs={{0,2},{1,3},{2,0},{3,1},{4,6},{5,7},{6,4},{7,5},{8,10},{9,11},{10,... | collective-permute-start | bytes 294920 | tf_op jit(solution)/shard_map/ppermute | solution.py:605
  23.7 0.0 collective-permute-start.10
  23.7 0.5 %collective-permute-start.13 = (bf16[384,128]{1,0:T(8,128)(2,1)S(1)}, bf16[384,128]{1,0:T(8,128)(2,1)S(1)}, u32[]{:S(2)}, u32[]{:S(2)}) collective-permute-start(bf16[384,128]{1,0:T(8,128)(2,1)S(1)} %get-tuple-element.41.refs_4_), channel_id=1, source_target_pairs={{0,1},{1,0},{2,3},{3,2},{4,5},{5,4},{6,7},{7,6},{8,9},{9,8},{10,11... | collective-permute-start | bytes 294920 | tf_op jit(solution)/shard_map/ppermute | solution.py:605
  24.2 3.1 %collective-permute-done.11.refs_2_ = bf16[384,128]{1,0:T(8,128)(2,1)S(1)} collective-permute-done((bf16[384,128]{1,0:T(8,128)(2,1)S(1)}, bf16[384,128]{1,0:T(8,128)(2,1)S(1)}, u32[]{:S(2)}, u32[]{:S(2)}) %collective-permute-start.11) | collective-permute-done | bytes 98336 | tf_op jit(solution)/shard_map/ppermute | solution.py:605
  27.3 0.0 collective-permute-start.12
  27.3 1.3 %collective-permute-done.14.refs_6_ = bf16[384,128]{1,0:T(8,128)(2,1)S(1)} collective-permute-done((bf16[384,128]{1,0:T(8,128)(2,1)S(1)}, bf16[384,128]{1,0:T(8,128)(2,1)S(1)}, u32[]{:S(2)}, u32[]{:S(2)}) %collective-permute-start.14) | collective-permute-done | bytes 98336 | tf_op jit(solution)/shard_map/ppermute | solution.py:605
  28.6 0.0 collective-permute-start.15
  28.6 0.0 collective-permute-done.10.refs_1_
  28.6 0.0 collective-permute-done.13.refs_5_
  28.6 0.0 collective-permute-done.12.refs_3_
  28.6 1.3 %collective-permute-done.15.refs_7_ = bf16[384,128]{1,0:T(8,128)(2,1)S(1)} collective-permute-done((bf16[384,128]{1,0:T(8,128)(2,1)S(1)}, bf16[384,128]{1,0:T(8,128)(2,1)S(1)}, u32[]{:S(2)}, u32[]{:S(2)}) %collective-permute-start.15) | collective-permute-done | bytes 98336 | tf_op jit(solution)/shard_map/ppermute | solution.py:605
  29.9 0.0 copy-done
  29.9 0.5 %finish.1 = bf16[8,96,128]{2,1,0:T(8,128)(2,1)S(1)} custom-call(bf16[384,128]{1,0:T(8,128)(2,1)S(1)} %get-tuple-element.40.refs_0_, bf16[384,128]{1,0:T(8,128)(2,1)S(1)} %collective-permute-done.10.refs_1_, bf16[384,128]{1,0:T(8,128)(2,1)S(1)} %collective-permute-done.11.refs_2_, bf16[384,128]{1,0:T(8,128)(2,1)S(1)} %collective-permute-done.12.refs_3_, ...), custom_call_target="tpu_custom_call" | custom-call | tf_op jit(solution)/shard_map/finish/pallas_call | solution.py:560
  30.4 12.5 %all_to_all.5.blocks_ref = bf16[8,96,128]{2,1,0:T(8,128)(2,1)S(1)} all-to-all(bf16[8,96,128]{2,1,0:T(8,128)(2,1)S(1)} %finish.1), channel_id=1, replica_groups=mesh['seq'=8,'head'=4] {'seq'}, dimensions={0} | all-to-all | bytes 393216 | tf_op jit(solution)/shard_map/all_to_all | solution.py:655
  42.9 0.8 %order.1 = bf16[2,192,256]{2,1,0:T(8,128)(2,1)} custom-call(bf16[8,96,128]{2,1,0:T(8,128)(2,1)S(1)} %all_to_all.5.blocks_ref), custom_call_target="tpu_custom_call" | custom-call | tf_op jit(solution)/shard_map/order/pallas_call | solution.py:587
  (3 shorter events, 0.0 us)
Async XLA Ops:
  0.0 4.5 %copy-start.4 = (s32[2]{0:T(128)S(1)}, s32[2]{0:T(128)}, u32[]{:S(2)}) copy-start(s32[2]{0:T(128)} %live_hbm.1) | copy-start | bytes 28
  0.0 11.8 %collective-permute-start.3 = (bf16[192,768]{1,0:T(8,128)(2,1)}, bf16[192,768]{1,0:T(8,128)(2,1)S(1)}, u32[]{:S(2)}, u32[]{:S(2)}) collective-permute-start(bf16[192,768]{1,0:T(8,128)(2,1)} %refs_0_), channel_id=1, source_target_pairs={{0,2},{1,3},{2,0},{3,1},{4,6},{5,7},{6,4},{7,5},{8,10},{9,11},{10,... | collective-permute-start | bytes 884744 | tf_op jit(solution)/shard_map/ppermute | solution.py:605
  2.9 5.1 %collective-permute-start = (s32[2,256]{1,0:T(2,128)}, s32[2,256]{1,0:T(2,128)S(1)}, u32[]{:S(2)}, u32[]{:S(2)}) collective-permute-start(s32[2,256]{1,0:T(2,128)} %ids_hbm.1), channel_id=1, source_target_pairs={{0,4},{1,5},{2,6},{3,7},{4,0},{5,1},{6,2},{7,3},{8,12},{9,13},{10,... | collective-permute-start | bytes 6152 | tf_op jit(solution)/shard_map/ppermute | solution.py:605
  4.5 10.1 %copy-start.2 = (bf16[192,768]{1,0:T(8,128)(2,1)S(1)}, bf16[192,768]{1,0:T(8,128)(2,1)}, u32[]{:S(2)}) copy-start(bf16[192,768]{1,0:T(8,128)(2,1)} %refs_0_) | copy-start | bytes 884740
  4.5 3.5 %collective-permute-start.1 = (s32[1,2]{1,0:T(1,128)S(1)}, s32[1,2]{1,0:T(1,128)S(1)}, u32[]{:S(2)}, u32[]{:S(2)}) collective-permute-start(s32[1,2]{1,0:T(1,128)S(1)} %bitcast.4), channel_id=1, source_target_pairs={{0,4},{1,5},{2,6},{3,7},{4,0},{5,1},{6,2},{7,3},{8,12},{9,13},{10,... | collective-permute-start | bytes 32 | tf_op jit(solution)/shard_map/ppermute | solution.py:605
  8.1 3.7 %collective-permute-start.2 = (s32[8,256]{1,0:T(8,128)S(1)}, s32[8,256]{1,0:T(8,128)S(1)}, u32[]{:S(2)}, u32[]{:S(2)}) collective-permute-start(s32[8,256]{1,0:T(8,128)S(1)} %join_raw.1.own_ref), channel_id=1, source_target_pairs={{0,8},{1,9},{2,10},{3,11},{4,12},{5,13},{6,14},{7,15},{8,0},{9,1},... | collective-permute-start | bytes 24584 | tf_op jit(solution)/shard_map/ppermute | solution.py:605
  9.7 5.0 %collective-permute-start.7 = (bf16[40,576]{1,0:T(8,128)(2,1)S(1)}, bf16[40,576]{1,0:T(8,128)(2,1)S(1)}, u32[]{:S(2)}, u32[]{:S(2)}) collective-permute-start(bf16[40,576]{1,0:T(8,128)(2,1)S(1)} %get-tuple-element.30.refs_0_), channel_id=1, source_target_pairs={{0,2},{1,3},{2,0},{3,1},{4,6},{5,7},{6,4},{7,5},{8,10},{9,11},{10,... | collective-permute-start | bytes 138248 | tf_op jit(solution)/shard_map/ppermute | solution.py:605
  10.3 4.8 %collective-permute-start.8 = (bf16[40,576]{1,0:T(8,128)(2,1)S(1)}, bf16[40,576]{1,0:T(8,128)(2,1)S(1)}, u32[]{:S(2)}, u32[]{:S(2)}) collective-permute-start(bf16[40,576]{1,0:T(8,128)(2,1)S(1)} %get-tuple-element.30.refs_0_), channel_id=1, source_target_pairs={{0,3},{1,2},{2,1},{3,0},{4,7},{5,6},{6,5},{7,4},{8,11},{9,10},{10,... | collective-permute-start | bytes 138248 | tf_op jit(solution)/shard_map/ppermute | solution.py:605
  11.8 3.3 %collective-permute-start.6 = (bf16[40,576]{1,0:T(8,128)(2,1)S(1)}, bf16[40,576]{1,0:T(8,128)(2,1)S(1)}, u32[]{:S(2)}, u32[]{:S(2)}) collective-permute-start(bf16[40,576]{1,0:T(8,128)(2,1)S(1)} %get-tuple-element.30.refs_0_), channel_id=1, source_target_pairs={{0,1},{1,0},{2,3},{3,2},{4,5},{5,4},{6,7},{7,6},{8,9},{9,8},{10,11... | collective-permute-start | bytes 138248 | tf_op jit(solution)/shard_map/ppermute | solution.py:605
  11.9 4.6 %collective-permute-start.9 = (s32[8,256]{1,0:T(8,128)S(1)}, s32[8,256]{1,0:T(8,128)S(1)}, u32[]{:S(2)}, u32[]{:S(2)}) collective-permute-start(s32[8,256]{1,0:T(8,128)S(1)} %join.1.refs_4_.near_codes_ref), channel_id=1, source_target_pairs={{0,16},{1,17},{2,18},{3,19},{4,20},{5,21},{6,22},{7,23},{8,24},{9,... | collective-permute-start | bytes 24584 | tf_op jit(solution)/shard_map/ppermute | solution.py:605
  14.5 3.8 %collective-permute-start.4 = (bf16[192,768]{1,0:T(8,128)(2,1)S(1)}, bf16[192,768]{1,0:T(8,128)(2,1)S(1)}, u32[]{:S(2)}, u32[]{:S(2)}) collective-permute-start(bf16[192,768]{1,0:T(8,128)(2,1)S(1)} %copy-done.2), channel_id=1, source_target_pairs={{0,1},{1,0},{2,3},{3,2},{4,5},{5,4},{6,7},{7,6},{8,9},{9,8},{10,11... | collective-permute-start | bytes 884744 | tf_op jit(solution)/shard_map/ppermute | solution.py:605
  14.7 3.7 %collective-permute-start.5 = (bf16[192,768]{1,0:T(8,128)(2,1)S(1)}, bf16[192,768]{1,0:T(8,128)(2,1)S(1)}, u32[]{:S(2)}, u32[]{:S(2)}) collective-permute-start(bf16[192,768]{1,0:T(8,128)(2,1)S(1)} %collective-permute-done.3.refs_2_), channel_id=1, source_target_pairs={{0,1},{1,0},{2,3},{3,2},{4,5},{5,4},{6,7},{7,6},{8,9},{9,8},{10,11... | collective-permute-start | bytes 884744 | tf_op jit(solution)/shard_map/ppermute | solution.py:605
  16.5 1.9 %copy-start.1 = (bf16[3,192,768]{2,1,0:T(8,128)(2,1)S(1)}, bf16[3,192,768]{2,1,0:T(8,128)(2,1)}, u32[]{:S(2)}) copy-start(bf16[3,192,768]{2,1,0:T(8,128)(2,1)} %param.12) | copy-start | bytes 2654212
  16.5 1.9 %copy-start.3 = (bf16[33,768]{1,0:T(8,128)(2,1)S(1)}, bf16[33,768]{1,0:T(8,128)(2,1)}, u32[]{:S(2)}) copy-start(bf16[33,768]{1,0:T(8,128)(2,1)} %refs_8_.1) | copy-start | bytes 152068
  18.4 11.5 %copy-start = (bf16[192,768]{1,0:T(8,128)(2,1)S(1)}, bf16[192,768]{1,0:T(8,128)(2,1)}, u32[]{:S(2)}) copy-start(bf16[192,768]{1,0:T(8,128)(2,1)} %refs_9_.1) | copy-start | bytes 884740
  21.6 5.7 %collective-permute-start.11 = (bf16[384,128]{1,0:T(8,128)(2,1)S(1)}, bf16[384,128]{1,0:T(8,128)(2,1)S(1)}, u32[]{:S(2)}, u32[]{:S(2)}) collective-permute-start(bf16[384,128]{1,0:T(8,128)(2,1)S(1)} %get-tuple-element.40.refs_0_), channel_id=1, source_target_pairs={{0,2},{1,3},{2,0},{3,1},{4,6},{5,7},{6,4},{7,5},{8,10},{9,11},{10,... | collective-permute-start | bytes 294920 | tf_op jit(solution)/shard_map/ppermute | solution.py:605
  22.2 6.4 %collective-permute-start.14 = (bf16[384,128]{1,0:T(8,128)(2,1)S(1)}, bf16[384,128]{1,0:T(8,128)(2,1)S(1)}, u32[]{:S(2)}, u32[]{:S(2)}) collective-permute-start(bf16[384,128]{1,0:T(8,128)(2,1)S(1)} %get-tuple-element.41.refs_4_), channel_id=1, source_target_pairs={{0,2},{1,3},{2,0},{3,1},{4,6},{5,7},{6,4},{7,5},{8,10},{9,11},{10,... | collective-permute-start | bytes 294920 | tf_op jit(solution)/shard_map/ppermute | solution.py:605
  23.7 4.9 %collective-permute-start.10 = (bf16[384,128]{1,0:T(8,128)(2,1)S(1)}, bf16[384,128]{1,0:T(8,128)(2,1)S(1)}, u32[]{:S(2)}, u32[]{:S(2)}) collective-permute-start(bf16[384,128]{1,0:T(8,128)(2,1)S(1)} %get-tuple-element.40.refs_0_), channel_id=1, source_target_pairs={{0,1},{1,0},{2,3},{3,2},{4,5},{5,4},{6,7},{7,6},{8,9},{9,8},{10,11... | collective-permute-start | bytes 294920 | tf_op jit(solution)/shard_map/ppermute | solution.py:605
  23.7 4.9 %collective-permute-start.13 = (bf16[384,128]{1,0:T(8,128)(2,1)S(1)}, bf16[384,128]{1,0:T(8,128)(2,1)S(1)}, u32[]{:S(2)}, u32[]{:S(2)}) collective-permute-start(bf16[384,128]{1,0:T(8,128)(2,1)S(1)} %get-tuple-element.41.refs_4_), channel_id=1, source_target_pairs={{0,1},{1,0},{2,3},{3,2},{4,5},{5,4},{6,7},{7,6},{8,9},{9,8},{10,11... | collective-permute-start | bytes 294920 | tf_op jit(solution)/shard_map/ppermute | solution.py:605
  27.3 1.3 %collective-permute-start.12 = (bf16[384,128]{1,0:T(8,128)(2,1)S(1)}, bf16[384,128]{1,0:T(8,128)(2,1)S(1)}, u32[]{:S(2)}, u32[]{:S(2)}) collective-permute-start(bf16[384,128]{1,0:T(8,128)(2,1)S(1)} %collective-permute-done.11.refs_2_), channel_id=1, source_target_pairs={{0,1},{1,0},{2,3},{3,2},{4,5},{5,4},{6,7},{7,6},{8,9},{9,8},{10,11... | collective-permute-start | bytes 294920 | tf_op jit(solution)/shard_map/ppermute | solution.py:605
  28.6 1.3 %collective-permute-start.15 = (bf16[384,128]{1,0:T(8,128)(2,1)S(1)}, bf16[384,128]{1,0:T(8,128)(2,1)S(1)}, u32[]{:S(2)}, u32[]{:S(2)}) collective-permute-start(bf16[384,128]{1,0:T(8,128)(2,1)S(1)} %collective-permute-done.14.refs_6_), channel_id=1, source_target_pairs={{0,1},{1,0},{2,3},{3,2},{4,5},{5,4},{6,7},{7,6},{8,9},{9,8},{10,11... | collective-permute-start | bytes 294920 | tf_op jit(solution)/shard_map/ppermute | solution.py:605

commit v21 on v20

--- a/solution.py
+++ b/solution.py
@@ -390,6 +390,7 @@
         row_out_ref,
         embed2_ref,
         weight_ref,
+        mixed_ref,
     ) = refs
     rows = live_ref.shape[0]
     tokens, width = row_context_ref.shape
@@ -415,14 +416,13 @@
         ],
         0,
     )
-    mixed = embedded + dot_nt(row_context_ref[...], row_out_ref[...].reshape(width, width))
-    for p in range(parts):
-
-        @pl.when(part == p)
-        def _():
-            mixed_out_ref[...] = mixed[:, p * local : (p + 1) * local]
-
-    normed = layer_norm(mixed).astype(bf16)
+    row_out = row_out_ref[...].reshape(width, width)
+    halves_at = [slice(c * tokens // 2, (c + 1) * tokens // 2) for c in range(2)]
+    normed = []
+    for at in halves_at:
+        mixed = embedded[at] + dot_nt(row_context_ref[at, :], row_out)
+        mixed_ref[at, :] = mixed
+        normed.append(layer_norm(mixed).astype(bf16))
 
     few = 8
     groups = own // few
@@ -441,7 +441,11 @@
         weight_ref[third : third + HEAD_DIM, :] = col_qkv_ref[pl.ds(last, HEAD_DIM), :]
         weight_ref[third + HEAD_DIM : third + LANES, :] = jnp.zeros((HEAD_DIM, width), bf16)
     proj = [
-        dot_nt(normed, weight_ref[2 * j * LANES : 2 * (j + 1) * LANES, :]) for j in range(3)
+        jnp.concatenate(
+            [dot_nt(part_of, weight_ref[2 * j * LANES : 2 * (j + 1) * LANES, :]) for part_of in normed],
+            0,
+        )
+        for j in range(3)
     ]
     proj = [
         proj[j][:, k * LANES : (k + 1) * LANES] * (HEAD_DIM ** (-0.5) if (2 * j + k) % 3 == 0 else 1.0)
@@ -491,6 +495,11 @@
             [left[:, 0:HEAD_DIM], right[:, 0:HEAD_DIM]], 1
         ).astype(bf16)
         start += count
+    for p in range(parts):
+
+        @pl.when(part == p)
+        def _():
+            mixed_out_ref[...] = mixed_ref[:, p * local : (p + 1) * local]
 
 
 def attend_columns_here(row_outs, live, row_context, near_own, far_own, embed, col_qkv):
@@ -509,6 +518,7 @@
             pltpu.VMEM((parts, local, width), bf16),
             pltpu.VMEM((2 * CODES, 2 * width), bf16),
             pltpu.VMEM((6 * LANES, width), bf16),
+            pltpu.VMEM((tokens, width), f32),
         ],
         cost_estimate=pl.CostEstimate(flops=2 * 10**9, bytes_accessed=10**6, transcendentals=0),
         compiler_params=pltpu.CompilerParams(vmem_limit_bytes=LARGE_VMEM),

time: 43.9 us -> 43.6 us (level)
  no operation moved by 1% of the time
where the time goes in v21:
time: 43.6 us; the launch traced here: 43.5 us
  starting transfers between devices  13 us (30%)
  blocking collectives  12.5 us (29%)
  Pallas kernels  9.27 us (21%)
  waiting for transfers between devices  8.66 us (20%)
    ppermute x16, starting transfers between devices, pairwise(): lax.ppermute(value, ('seq', 'head'), [(i, g * parts + p) for i, (g, p) in...  13 us
    all_to_all x1, blocking collectives, fast_body(): lax.all_to_all(blocks, 'seq', split_axis=0, concat_axis=0, tiled=True)  12.5 us
    ppermute x16, waiting for transfers between devices, pairwise(): lax.ppermute(value, ('seq', 'head'), [(i, g * parts + p) for i, (g, p) in...  8.66 us
    pallas_call x1, Pallas kernels, attend_columns_here(): pl.pallas_call(functools.partial(column_kernel, parts), out_shape=(jax.Sh...  2.94 us
    pallas_call x1, Pallas kernels, make_tables(): pl.pallas_call(table_kernel, out_shape=(jax.ShapeDtypeStruct((TABLE_ROWS,...  1.87 us
    pallas_call x1, Pallas kernels, attend_rows(): pl.pallas_call(row_kernel, out_shape=(jax.ShapeDtypeStruct((2 * half * ow...  1.86 us
    pallas_call x1, Pallas kernels, attend_near(): pl.pallas_call(functools.partial(near_kernel, parts), out_shape=(jax.Shap...  1.18 us
  transfers between devices with their start and end apart: 16, of which 6 were waited for; matrix products, arithmetic and copies ran while one was open for 0% of the time, Pallas kernels for 11%

profile of v21, /device:TPU:0, one launch (start us, length us, event | category | flops | bytes accessed | tf_op | source)
XLA Modules:
  0.0 43.5 jit_solution(2365378319299843827)
XLA Ops:
  0.0 0.0 copy-start.4
  0.0 2.9 %collective-permute-start.3 = (bf16[192,768]{1,0:T(8,128)(2,1)}, bf16[192,768]{1,0:T(8,128)(2,1)S(1)}, u32[]{:S(2)}, u32[]{:S(2)}) collective-permute-start(bf16[192,768]{1,0:T(8,128)(2,1)} %refs_0_), channel_id=1, source_target_pairs={{0,2},{1,3},{2,0},{3,1},{4,6},{5,7},{6,4},{7,5},{8,10},{9,11},{10,... | collective-permute-start | bytes 884744 | tf_op jit(solution)/shard_map/ppermute | solution.py:615
  2.9 1.5 %collective-permute-start = (s32[2,256]{1,0:T(2,128)}, s32[2,256]{1,0:T(2,128)S(1)}, u32[]{:S(2)}, u32[]{:S(2)}) collective-permute-start(s32[2,256]{1,0:T(2,128)} %ids_hbm.1), channel_id=1, source_target_pairs={{0,4},{1,5},{2,6},{3,7},{4,0},{5,1},{6,2},{7,3},{8,12},{9,13},{10,... | collective-permute-start | bytes 6152 | tf_op jit(solution)/shard_map/ppermute | solution.py:615
  4.5 0.0 copy-done.4
  4.5 0.0 copy-start.2
  4.5 0.5 %collective-permute-start.1 = (s32[1,2]{1,0:T(1,128)S(1)}, s32[1,2]{1,0:T(1,128)S(1)}, u32[]{:S(2)}, u32[]{:S(2)}) collective-permute-start(s32[1,2]{1,0:T(1,128)S(1)} %bitcast.4), channel_id=1, source_target_pairs={{0,4},{1,5},{2,6},{3,7},{4,0},{5,1},{6,2},{7,3},{8,12},{9,13},{10,... | collective-permute-start | bytes 32 | tf_op jit(solution)/shard_map/ppermute | solution.py:615
  5.0 1.9 %tables.1 = (bf16[40,576]{1,0:T(8,128)(2,1)S(1)}, s32[8,256]{1,0:T(8,128)S(1)}) custom-call(s32[2,256]{1,0:T(2,128)} %ids_hbm.1, s32[2]{0:T(128)} %live_hbm.1, bf16[33,768]{1,0:T(8,128)(2,1)} %refs_8_.1, bf16[3,192,768]{2,1,0:T(8,128)(2,1)} %qkv_hbm.1), custom_call_target="tpu_custom_call" | custom-call | flops 2000000000 | bytes 884736 | tf_op jit(solution)/shard_map/tables/pallas_call | solution.py:131
  6.8 1.2 %collective-permute-done.1.live_ref = s32[1,2]{1,0:T(1,128)S(1)} collective-permute-done((s32[1,2]{1,0:T(1,128)S(1)}, s32[1,2]{1,0:T(1,128)S(1)}, u32[]{:S(2)}, u32[]{:S(2)}) %collective-permute-start.1) | collective-permute-done | bytes 40 | tf_op jit(solution)/shard_map/ppermute | solution.py:615
  8.0 0.0 collective-permute-done.ids_ref
  8.0 0.1 join_raw.1.own_ref
  8.1 1.6 %collective-permute-start.2 = (s32[8,256]{1,0:T(8,128)S(1)}, s32[8,256]{1,0:T(8,128)S(1)}, u32[]{:S(2)}, u32[]{:S(2)}) collective-permute-start(s32[8,256]{1,0:T(8,128)S(1)} %join_raw.1.own_ref), channel_id=1, source_target_pairs={{0,8},{1,9},{2,10},{3,11},{4,12},{5,13},{6,14},{7,15},{8,0},{9,1},... | collective-permute-start | bytes 24584 | tf_op jit(solution)/shard_map/ppermute | solution.py:615
  9.7 0.5 %collective-permute-start.7 = (bf16[40,576]{1,0:T(8,128)(2,1)S(1)}, bf16[40,576]{1,0:T(8,128)(2,1)S(1)}, u32[]{:S(2)}, u32[]{:S(2)}) collective-permute-start(bf16[40,576]{1,0:T(8,128)(2,1)S(1)} %get-tuple-element.30.refs_0_), channel_id=1, source_target_pairs={{0,2},{1,3},{2,0},{3,1},{4,6},{5,7},{6,4},{7,5},{8,10},{9,11},{10,... | collective-permute-start | bytes 138248 | tf_op jit(solution)/shard_map/ppermute | solution.py:615
  10.3 0.0 collective-permute-start.8
  10.3 1.5 %collective-permute-done.2.other_ref = s32[8,256]{1,0:T(8,128)S(1)} collective-permute-done((s32[8,256]{1,0:T(8,128)S(1)}, s32[8,256]{1,0:T(8,128)S(1)}, u32[]{:S(2)}, u32[]{:S(2)}) %collective-permute-start.2) | collective-permute-done | bytes 8224 | tf_op jit(solution)/shard_map/ppermute | solution.py:615
  11.8 0.0 collective-permute-done.3.refs_2_
  11.8 0.1 collective-permute-start.6
  11.9 2.6 %collective-permute-start.9 = (s32[8,256]{1,0:T(8,128)S(1)}, s32[8,256]{1,0:T(8,128)S(1)}, u32[]{:S(2)}, u32[]{:S(2)}) collective-permute-start(s32[8,256]{1,0:T(8,128)S(1)} %join.1.refs_4_.near_codes_ref), channel_id=1, source_target_pairs={{0,16},{1,17},{2,18},{3,19},{4,20},{5,21},{6,22},{7,23},{8,24},{9,... | collective-permute-start | bytes 24584 | tf_op jit(solution)/shard_map/ppermute | solution.py:615
  14.5 0.0 copy-done.2
  14.5 0.2 collective-permute-start.4
  14.7 0.0 collective-permute-done.7.refs_2_
  14.7 0.3 collective-permute-start.5
  15.1 0.0 collective-permute-done.8.refs_3_
  15.1 0.0 collective-permute-done.6.refs_1_
  15.1 1.2 %near_scores.1 = (bf16[12,128,256]{2,1,0:T(8,128)(2,1)S(1)}, bf16[64,768]{1,0:T(8,128)(2,1)S(1)}, f32[384,256]{1,0:T(8,128)S(1)}, bf16[512,256]{1,0:T(8,128)(2,1)S(1)}, bf16[128,128]{1,0:T(8,128)(2,1)S(1)}) custom-call(bf16[40,576]{1,0:T(8,128)(2,1)S(1)} %get-tuple-element.30.refs_0_, bf16[40,576]{1,0:T(8,128)(2,1)S(1)} %collective-permute-done.6.refs_1_, ...), custom_call_target="tpu_custom_call" | custom-call | flops 1000000000 | bytes 1000000 | tf_op jit(solution)/shard_map/near_scores/pallas_call | solution.py:275
  16.2 0.3 collective-permute-done.9.far_codes_ref
  16.5 1.9 %row_attention.1 = (bf16[512,768]{1,0:T(8,128)(2,1)S(1)}, bf16[128,128]{1,0:T(8,128)(2,1)S(1)}, f32[16,128]{1,0:T(8,128)S(1)}) custom-call(bf16[12,128,256]{2,1,0:T(8,128)(2,1)S(1)} %get-tuple-element.32.scores_ref, bf16[64,768]{1,0:T(8,128)(2,1)S(1)} %get-tuple-element.33.values_ref, f32[384,256]{1,0:T(8,128)S(1)} %get-tuple-element.34.near_tied_ref, ...), custom_call_target="tpu_custom_call" | custom-call | flops 3000000000 | bytes 1000000 | tf_op jit(solution)/shard_map/row_attention/pallas_call | solution.py:360
  18.4 0.0 collective-permute-done.4.refs_1_
  18.4 0.0 collective-permute-done.5.refs_3_
  18.4 0.0 copy-done.1
  18.4 0.0 copy-done.3
  18.4 0.0 copy-start
  18.4 2.9 %column_attention.1 = (bf16[384,128]{1,0:T(8,128)(2,1)S(1)}, bf16[384,128]{1,0:T(8,128)(2,1)S(1)}, f32[512,192]{1,0:T(8,128)S(1)}) custom-call(bf16[192,768]{1,0:T(8,128)(2,1)S(1)} %copy-done.2, bf16[192,768]{1,0:T(8,128)(2,1)S(1)} %collective-permute-done.4.refs_1_, bf16[192,768]{1,0:T(8,128)(2,1)S(1)} %collective-permute-done.3.refs_2_, ...), custom_call_target="tpu_custom_call" | custom-call | flops 2000000000 | bytes 1000000 | tf_op jit(solution)/shard_map/column_attention/pallas_call | solution.py:510
  21.4 0.6 %collective-permute-start.11 = (bf16[384,128]{1,0:T(8,128)(2,1)S(1)}, bf16[384,128]{1,0:T(8,128)(2,1)S(1)}, u32[]{:S(2)}, u32[]{:S(2)}) collective-permute-start(bf16[384,128]{1,0:T(8,128)(2,1)S(1)} %get-tuple-element.40.refs_0_), channel_id=1, source_target_pairs={{0,2},{1,3},{2,0},{3,1},{4,6},{5,7},{6,4},{7,5},{8,10},{9,11},{10,... | collective-permute-start | bytes 294920 | tf_op jit(solution)/shard_map/ppermute | solution.py:615
  22.0 1.5 %collective-permute-start.14 = (bf16[384,128]{1,0:T(8,128)(2,1)S(1)}, bf16[384,128]{1,0:T(8,128)(2,1)S(1)}, u32[]{:S(2)}, u32[]{:S(2)}) collective-permute-start(bf16[384,128]{1,0:T(8,128)(2,1)S(1)} %get-tuple-element.41.refs_4_), channel_id=1, source_target_pairs={{0,2},{1,3},{2,0},{3,1},{4,6},{5,7},{6,4},{7,5},{8,10},{9,11},{10,... | collective-permute-start | bytes 294920 | tf_op jit(solution)/shard_map/ppermute | solution.py:615
  23.5 0.0 collective-permute-start.10
  23.5 0.5 %collective-permute-start.13 = (bf16[384,128]{1,0:T(8,128)(2,1)S(1)}, bf16[384,128]{1,0:T(8,128)(2,1)S(1)}, u32[]{:S(2)}, u32[]{:S(2)}) collective-permute-start(bf16[384,128]{1,0:T(8,128)(2,1)S(1)} %get-tuple-element.41.refs_4_), channel_id=1, source_target_pairs={{0,1},{1,0},{2,3},{3,2},{4,5},{5,4},{6,7},{7,6},{8,9},{9,8},{10,11... | collective-permute-start | bytes 294920 | tf_op jit(solution)/shard_map/ppermute | solution.py:615
  24.0 3.1 %collective-permute-done.11.refs_2_ = bf16[384,128]{1,0:T(8,128)(2,1)S(1)} collective-permute-done((bf16[384,128]{1,0:T(8,128)(2,1)S(1)}, bf16[384,128]{1,0:T(8,128)(2,1)S(1)}, u32[]{:S(2)}, u32[]{:S(2)}) %collective-permute-start.11) | collective-permute-done | bytes 98336 | tf_op jit(solution)/shard_map/ppermute | solution.py:615
  27.1 0.0 collective-permute-start.12
  27.1 1.3 %collective-permute-done.14.refs_6_ = bf16[384,128]{1,0:T(8,128)(2,1)S(1)} collective-permute-done((bf16[384,128]{1,0:T(8,128)(2,1)S(1)}, bf16[384,128]{1,0:T(8,128)(2,1)S(1)}, u32[]{:S(2)}, u32[]{:S(2)}) %collective-permute-start.14) | collective-permute-done | bytes 98336 | tf_op jit(solution)/shard_map/ppermute | solution.py:615
  28.4 0.0 collective-permute-start.15
  28.4 0.0 collective-permute-done.10.refs_1_
  28.4 0.0 collective-permute-done.13.refs_5_
  28.4 0.0 collective-permute-done.12.refs_3_
  28.4 1.3 %collective-permute-done.15.refs_7_ = bf16[384,128]{1,0:T(8,128)(2,1)S(1)} collective-permute-done((bf16[384,128]{1,0:T(8,128)(2,1)S(1)}, bf16[384,128]{1,0:T(8,128)(2,1)S(1)}, u32[]{:S(2)}, u32[]{:S(2)}) %collective-permute-start.15) | collective-permute-done | bytes 98336 | tf_op jit(solution)/shard_map/ppermute | solution.py:615
  29.7 0.0 copy-done
  29.7 0.5 %finish.1 = bf16[8,96,128]{2,1,0:T(8,128)(2,1)S(1)} custom-call(bf16[384,128]{1,0:T(8,128)(2,1)S(1)} %get-tuple-element.40.refs_0_, bf16[384,128]{1,0:T(8,128)(2,1)S(1)} %collective-permute-done.10.refs_1_, bf16[384,128]{1,0:T(8,128)(2,1)S(1)} %collective-permute-done.11.refs_2_, bf16[384,128]{1,0:T(8,128)(2,1)S(1)} %collective-permute-done.12.refs_3_, ...), custom_call_target="tpu_custom_call" | custom-call | tf_op jit(solution)/shard_map/finish/pallas_call | solution.py:570
  30.2 12.5 %all_to_all.5.blocks_ref = bf16[8,96,128]{2,1,0:T(8,128)(2,1)S(1)} all-to-all(bf16[8,96,128]{2,1,0:T(8,128)(2,1)S(1)} %finish.1), channel_id=1, replica_groups=mesh['seq'=8,'head'=4] {'seq'}, dimensions={0} | all-to-all | bytes 393216 | tf_op jit(solution)/shard_map/all_to_all | solution.py:665
  42.7 0.8 %order.1 = bf16[2,192,256]{2,1,0:T(8,128)(2,1)} custom-call(bf16[8,96,128]{2,1,0:T(8,128)(2,1)S(1)} %all_to_all.5.blocks_ref), custom_call_target="tpu_custom_call" | custom-call | tf_op jit(solution)/shard_map/order/pallas_call | solution.py:597
  (3 shorter events, 0.0 us)
Async XLA Ops:
  0.0 4.5 %copy-start.4 = (s32[2]{0:T(128)S(1)}, s32[2]{0:T(128)}, u32[]{:S(2)}) copy-start(s32[2]{0:T(128)} %live_hbm.1) | copy-start | bytes 28
  0.0 11.8 %collective-permute-start.3 = (bf16[192,768]{1,0:T(8,128)(2,1)}, bf16[192,768]{1,0:T(8,128)(2,1)S(1)}, u32[]{:S(2)}, u32[]{:S(2)}) collective-permute-start(bf16[192,768]{1,0:T(8,128)(2,1)} %refs_0_), channel_id=1, source_target_pairs={{0,2},{1,3},{2,0},{3,1},{4,6},{5,7},{6,4},{7,5},{8,10},{9,11},{10,... | collective-permute-start | bytes 884744 | tf_op jit(solution)/shard_map/ppermute | solution.py:615
  2.9 5.1 %collective-permute-start = (s32[2,256]{1,0:T(2,128)}, s32[2,256]{1,0:T(2,128)S(1)}, u32[]{:S(2)}, u32[]{:S(2)}) collective-permute-start(s32[2,256]{1,0:T(2,128)} %ids_hbm.1), channel_id=1, source_target_pairs={{0,4},{1,5},{2,6},{3,7},{4,0},{5,1},{6,2},{7,3},{8,12},{9,13},{10,... | collective-permute-start | bytes 6152 | tf_op jit(solution)/shard_map/ppermute | solution.py:615
  4.5 10.1 %copy-start.2 = (bf16[192,768]{1,0:T(8,128)(2,1)S(1)}, bf16[192,768]{1,0:T(8,128)(2,1)}, u32[]{:S(2)}) copy-start(bf16[192,768]{1,0:T(8,128)(2,1)} %refs_0_) | copy-start | bytes 884740
  4.5 3.5 %collective-permute-start.1 = (s32[1,2]{1,0:T(1,128)S(1)}, s32[1,2]{1,0:T(1,128)S(1)}, u32[]{:S(2)}, u32[]{:S(2)}) collective-permute-start(s32[1,2]{1,0:T(1,128)S(1)} %bitcast.4), channel_id=1, source_target_pairs={{0,4},{1,5},{2,6},{3,7},{4,0},{5,1},{6,2},{7,3},{8,12},{9,13},{10,... | collective-permute-start | bytes 32 | tf_op jit(solution)/shard_map/ppermute | solution.py:615
  8.1 3.7 %collective-permute-start.2 = (s32[8,256]{1,0:T(8,128)S(1)}, s32[8,256]{1,0:T(8,128)S(1)}, u32[]{:S(2)}, u32[]{:S(2)}) collective-permute-start(s32[8,256]{1,0:T(8,128)S(1)} %join_raw.1.own_ref), channel_id=1, source_target_pairs={{0,8},{1,9},{2,10},{3,11},{4,12},{5,13},{6,14},{7,15},{8,0},{9,1},... | collective-permute-start | bytes 24584 | tf_op jit(solution)/shard_map/ppermute | solution.py:615
  9.7 5.0 %collective-permute-start.7 = (bf16[40,576]{1,0:T(8,128)(2,1)S(1)}, bf16[40,576]{1,0:T(8,128)(2,1)S(1)}, u32[]{:S(2)}, u32[]{:S(2)}) collective-permute-start(bf16[40,576]{1,0:T(8,128)(2,1)S(1)} %get-tuple-element.30.refs_0_), channel_id=1, source_target_pairs={{0,2},{1,3},{2,0},{3,1},{4,6},{5,7},{6,4},{7,5},{8,10},{9,11},{10,... | collective-permute-start | bytes 138248 | tf_op jit(solution)/shard_map/ppermute | solution.py:615
  10.3 4.8 %collective-permute-start.8 = (bf16[40,576]{1,0:T(8,128)(2,1)S(1)}, bf16[40,576]{1,0:T(8,128)(2,1)S(1)}, u32[]{:S(2)}, u32[]{:S(2)}) collective-permute-start(bf16[40,576]{1,0:T(8,128)(2,1)S(1)} %get-tuple-element.30.refs_0_), channel_id=1, source_target_pairs={{0,3},{1,2},{2,1},{3,0},{4,7},{5,6},{6,5},{7,4},{8,11},{9,10},{10,... | collective-permute-start | bytes 138248 | tf_op jit(solution)/shard_map/ppermute | solution.py:615
  11.8 3.3 %collective-permute-start.6 = (bf16[40,576]{1,0:T(8,128)(2,1)S(1)}, bf16[40,576]{1,0:T(8,128)(2,1)S(1)}, u32[]{:S(2)}, u32[]{:S(2)}) collective-permute-start(bf16[40,576]{1,0:T(8,128)(2,1)S(1)} %get-tuple-element.30.refs_0_), channel_id=1, source_target_pairs={{0,1},{1,0},{2,3},{3,2},{4,5},{5,4},{6,7},{7,6},{8,9},{9,8},{10,11... | collective-permute-start | bytes 138248 | tf_op jit(solution)/shard_map/ppermute | solution.py:615
  11.9 4.6 %collective-permute-start.9 = (s32[8,256]{1,0:T(8,128)S(1)}, s32[8,256]{1,0:T(8,128)S(1)}, u32[]{:S(2)}, u32[]{:S(2)}) collective-permute-start(s32[8,256]{1,0:T(8,128)S(1)} %join.1.refs_4_.near_codes_ref), channel_id=1, source_target_pairs={{0,16},{1,17},{2,18},{3,19},{4,20},{5,21},{6,22},{7,23},{8,24},{9,... | collective-permute-start | bytes 24584 | tf_op jit(solution)/shard_map/ppermute | solution.py:615
  14.5 3.8 %collective-permute-start.4 = (bf16[192,768]{1,0:T(8,128)(2,1)S(1)}, bf16[192,768]{1,0:T(8,128)(2,1)S(1)}, u32[]{:S(2)}, u32[]{:S(2)}) collective-permute-start(bf16[192,768]{1,0:T(8,128)(2,1)S(1)} %copy-done.2), channel_id=1, source_target_pairs={{0,1},{1,0},{2,3},{3,2},{4,5},{5,4},{6,7},{7,6},{8,9},{9,8},{10,11... | collective-permute-start | bytes 884744 | tf_op jit(solution)/shard_map/ppermute | solution.py:615
  14.7 3.7 %collective-permute-start.5 = (bf16[192,768]{1,0:T(8,128)(2,1)S(1)}, bf16[192,768]{1,0:T(8,128)(2,1)S(1)}, u32[]{:S(2)}, u32[]{:S(2)}) collective-permute-start(bf16[192,768]{1,0:T(8,128)(2,1)S(1)} %collective-permute-done.3.refs_2_), channel_id=1, source_target_pairs={{0,1},{1,0},{2,3},{3,2},{4,5},{5,4},{6,7},{7,6},{8,9},{9,8},{10,11... | collective-permute-start | bytes 884744 | tf_op jit(solution)/shard_map/ppermute | solution.py:615
  16.5 1.9 %copy-start.1 = (bf16[3,192,768]{2,1,0:T(8,128)(2,1)S(1)}, bf16[3,192,768]{2,1,0:T(8,128)(2,1)}, u32[]{:S(2)}) copy-start(bf16[3,192,768]{2,1,0:T(8,128)(2,1)} %param.12) | copy-start | bytes 2654212
  16.5 1.9 %copy-start.3 = (bf16[33,768]{1,0:T(8,128)(2,1)S(1)}, bf16[33,768]{1,0:T(8,128)(2,1)}, u32[]{:S(2)}) copy-start(bf16[33,768]{1,0:T(8,128)(2,1)} %refs_8_.1) | copy-start | bytes 152068
  18.4 11.3 %copy-start = (bf16[192,768]{1,0:T(8,128)(2,1)S(1)}, bf16[192,768]{1,0:T(8,128)(2,1)}, u32[]{:S(2)}) copy-start(bf16[192,768]{1,0:T(8,128)(2,1)} %refs_9_.1) | copy-start | bytes 884740
  21.4 5.7 %collective-permute-start.11 = (bf16[384,128]{1,0:T(8,128)(2,1)S(1)}, bf16[384,128]{1,0:T(8,128)(2,1)S(1)}, u32[]{:S(2)}, u32[]{:S(2)}) collective-permute-start(bf16[384,128]{1,0:T(8,128)(2,1)S(1)} %get-tuple-element.40.refs_0_), channel_id=1, source_target_pairs={{0,2},{1,3},{2,0},{3,1},{4,6},{5,7},{6,4},{7,5},{8,10},{9,11},{10,... | collective-permute-start | bytes 294920 | tf_op jit(solution)/shard_map/ppermute | solution.py:615
  22.0 6.4 %collective-permute-start.14 = (bf16[384,128]{1,0:T(8,128)(2,1)S(1)}, bf16[384,128]{1,0:T(8,128)(2,1)S(1)}, u32[]{:S(2)}, u32[]{:S(2)}) collective-permute-start(bf16[384,128]{1,0:T(8,128)(2,1)S(1)} %get-tuple-element.41.refs_4_), channel_id=1, source_target_pairs={{0,2},{1,3},{2,0},{3,1},{4,6},{5,7},{6,4},{7,5},{8,10},{9,11},{10,... | collective-permute-start | bytes 294920 | tf_op jit(solution)/shard_map/ppermute | solution.py:615
  23.5 4.9 %collective-permute-start.10 = (bf16[384,128]{1,0:T(8,128)(2,1)S(1)}, bf16[384,128]{1,0:T(8,128)(2,1)S(1)}, u32[]{:S(2)}, u32[]{:S(2)}) collective-permute-start(bf16[384,128]{1,0:T(8,128)(2,1)S(1)} %get-tuple-element.40.refs_0_), channel_id=1, source_target_pairs={{0,1},{1,0},{2,3},{3,2},{4,5},{5,4},{6,7},{7,6},{8,9},{9,8},{10,11... | collective-permute-start | bytes 294920 | tf_op jit(solution)/shard_map/ppermute | solution.py:615
  23.5 4.9 %collective-permute-start.13 = (bf16[384,128]{1,0:T(8,128)(2,1)S(1)}, bf16[384,128]{1,0:T(8,128)(2,1)S(1)}, u32[]{:S(2)}, u32[]{:S(2)}) collective-permute-start(bf16[384,128]{1,0:T(8,128)(2,1)S(1)} %get-tuple-element.41.refs_4_), channel_id=1, source_target_pairs={{0,1},{1,0},{2,3},{3,2},{4,5},{5,4},{6,7},{7,6},{8,9},{9,8},{10,11... | collective-permute-start | bytes 294920 | tf_op jit(solution)/shard_map/ppermute | solution.py:615
  27.1 1.3 %collective-permute-start.12 = (bf16[384,128]{1,0:T(8,128)(2,1)S(1)}, bf16[384,128]{1,0:T(8,128)(2,1)S(1)}, u32[]{:S(2)}, u32[]{:S(2)}) collective-permute-start(bf16[384,128]{1,0:T(8,128)(2,1)S(1)} %collective-permute-done.11.refs_2_), channel_id=1, source_target_pairs={{0,1},{1,0},{2,3},{3,2},{4,5},{5,4},{6,7},{7,6},{8,9},{9,8},{10,11... | collective-permute-start | bytes 294920 | tf_op jit(solution)/shard_map/ppermute | solution.py:615
  28.4 1.3 %collective-permute-start.15 = (bf16[384,128]{1,0:T(8,128)(2,1)S(1)}, bf16[384,128]{1,0:T(8,128)(2,1)S(1)}, u32[]{:S(2)}, u32[]{:S(2)}) collective-permute-start(bf16[384,128]{1,0:T(8,128)(2,1)S(1)} %collective-permute-done.14.refs_6_), channel_id=1, source_target_pairs={{0,1},{1,0},{2,3},{3,2},{4,5},{5,4},{6,7},{7,6},{8,9},{9,8},{10,11... | collective-permute-start | bytes 294920 | tf_op jit(solution)/shard_map/ppermute | solution.py:615

commit v22 on v21

--- a/solution.py
+++ b/solution.py
@@ -205,12 +205,16 @@
     return live
 
 
-def tied_sum(scores_ref, live_own_ref, hot_ref, sum_ref):
-    heads = scores_ref.shape[0]
-    own = sum_ref.shape[0] // heads
+def head_groups(heads, own):
+    some = heads // 2
+    return [(slice(g * some * own, (g + 1) * some * own), g * some, (g + 1) * some) for g in range(2)]
+
+
+def tied_sum(scores_ref, live_own_ref, hot_ref, sum_ref, first, last):
+    own = sum_ref.shape[0] // scores_ref.shape[0]
     depth = hot_ref.shape[0]
     pairs = depth // CODES // 2
-    for h in range(heads):
+    for h in range(first, last):
         looked = dot_nn(live_own_ref[...], scores_ref[h]).astype(bf16)
         for piece in range(2):
             for k in range(pairs):
@@ -218,8 +222,9 @@
                 sum_ref[h * own : (h + 1) * own, to : to + LANES] = looked[
                     k * own : (k + 1) * own, piece * LANES : (piece + 1) * LANES
                 ]
-    return dot_nn(sum_ref[:, 0:depth], hot_ref[...]) + dot_nn(
-        sum_ref[:, depth : 2 * depth], hot_ref[...]
+    at = slice(first * own, last * own)
+    return dot_nn(sum_ref[at, 0:depth], hot_ref[...]) + dot_nn(
+        sum_ref[at, depth : 2 * depth], hot_ref[...]
     )
 
 
@@ -264,7 +269,8 @@
         scores_ref[h, :, LANES : 2 * LANES] = low[h // 2][these]
 
     one_hots(codes_ref[...], group, hot_ref, own_ref, live_own_ref)
-    tied_ref[...] = tied_sum(scores_ref, live_own_ref, hot_ref, sum_ref)
+    for at, first, last in head_groups(heads, sum_ref.shape[0] // heads):
+        tied_ref[at, :] = tied_sum(scores_ref, live_own_ref, hot_ref, sum_ref, first, last)
 
 
 def attend_near(tables, codes, own):
@@ -319,12 +325,18 @@
     live = one_hots(far_codes_ref[...], group, hot_ref, own_ref, live_own_ref)
     live = jnp.concatenate([(near_codes_ref[:, 0:LANES] >> 16).astype(f32), live], 0)
     live_ref[...] = live
-    tied = near_tied_ref[...] + tied_sum(scores_ref, live_own_ref, hot_ref, sum_ref)
     count = jnp.sum(live, axis=0, keepdims=True)[:, 0:1]
-    probs = softmax_last(tied * (HEAD_DIM ** (-0.5) / jnp.sqrt(count))).astype(bf16)
-
-    spread_ref[:, 0:depth] = dot_nt(probs, near_hot_ref[...]).astype(bf16)
-    spread_ref[:, depth : 2 * depth] = dot_nt(probs, hot_ref[...]).astype(bf16)
+    scale = HEAD_DIM ** (-0.5) / jnp.sqrt(count)
+    groups = head_groups(heads, own)
+    tied = [
+        near_tied_ref[at, :] + tied_sum(scores_ref, live_own_ref, hot_ref, sum_ref, first, last)
+        for at, first, last in groups
+    ]
+    probs = [softmax_last(some * scale).astype(bf16) for some in tied]
+
+    for (at, _, _), some in zip(groups, probs):
+        spread_ref[at, 0:depth] = dot_nt(some, near_hot_ref[...]).astype(bf16)
+        spread_ref[at, depth : 2 * depth] = dot_nt(some, hot_ref[...]).astype(bf16)
     spans = [slice(hp * LANES, (hp + 1) * LANES) for hp in range(heads // 2)]
     values = [spread_pair(values_ref[:, span]) for span in spans]
     contexts = []
@@ -576,27 +588,42 @@
     )(*contexts[0], *contexts[1], mixed, col_out)
 
 
-def order_kernel(blocks_ref, out_ref):
+def order_kernel(blocks_ref, out_hbm, out_ref, sems):
     groups = blocks_ref.shape[0]
     local, cols = out_ref.shape[1:]
     own = cols // groups
     rest = local - LANES
+    stores = []
+
+    def store(row, first, last, values):
+        out_ref[row, first:last, :] = values
+        stores.append(
+            pltpu.make_async_copy(
+                out_ref.at[row, first:last], out_hbm.at[row, first:last], sems.at[len(stores)]
+            )
+        )
+        stores[-1].start()
+
     for part in range(3):
         piece = jnp.concatenate(
             [blocks_ref[g, part * own : (part + 1) * own, :] for g in range(groups)], 0
         )
         turned = piece.astype(f32).T.astype(bf16)
         if part < 2:
-            out_ref[part, 0:LANES, :] = turned
+            store(part, 0, LANES, turned)
         else:
             for r in range(2):
-                out_ref[r, LANES:local, :] = turned[r * rest : (r + 1) * rest, :]
+                store(r, LANES, local, turned[r * rest : (r + 1) * rest, :])
+    for started in stores:
+        started.wait()
 
 
 def order(blocks, cols, local):
     return pl.pallas_call(
         order_kernel,
         out_shape=jax.ShapeDtypeStruct((2, local, cols), bf16),
+        out_specs=pl.BlockSpec(memory_space=pl.ANY),
+        scratch_shapes=[pltpu.VMEM((2, local, cols), bf16), pltpu.SemaphoreType.DMA((4,))],
         compiler_params=pltpu.CompilerParams(vmem_limit_bytes=SMALL_VMEM),
         name="order",
     )(blocks)

time: 43.6 us -> 43.4 us (level)
  transfers between devices with their start and end apart: 16 -> 16, of which waited for: 6 -> 5; matrix products, arithmetic and copies ran while one was open for 0% -> 0% of each run, Pallas kernels for 11% -> 12%
where the time goes in v22:
time: 43.4 us; the launch traced here: 43.2 us
  starting transfers between devices  13 us (30%)
  blocking collectives  12.2 us (28%)
  Pallas kernels  9.25 us (21%)
  waiting for transfers between devices  8.63 us (20%)
    ppermute x16, starting transfers between devices, pairwise(): lax.ppermute(value, ('seq', 'head'), [(i, g * parts + p) for i, (g, p) in...  13 us
    all_to_all x1, blocking collectives, fast_body(): lax.all_to_all(blocks, 'seq', split_axis=0, concat_axis=0, tiled=True)  12.2 us
    ppermute x16, waiting for transfers between devices, pairwise(): lax.ppermute(value, ('seq', 'head'), [(i, g * parts + p) for i, (g, p) in...  8.63 us
    pallas_call x1, Pallas kernels, attend_columns_here(): pl.pallas_call(functools.partial(column_kernel, parts), out_shape=(jax.Sh...  2.94 us
    pallas_call x1, Pallas kernels, make_tables(): pl.pallas_call(table_kernel, out_shape=(jax.ShapeDtypeStruct((TABLE_ROWS,...  1.87 us
    pallas_call x1, Pallas kernels, attend_rows(): pl.pallas_call(row_kernel, out_shape=(jax.ShapeDtypeStruct((2 * half * ow...  1.63 us
    pallas_call x1, Pallas kernels, attend_near(): pl.pallas_call(functools.partial(near_kernel, parts), out_shape=(jax.Shap...  1.41 us
  transfers between devices with their start and end apart: 16, of which 5 were waited for; matrix products, arithmetic and copies ran while one was open for 0% of the time, Pallas kernels for 12%

profile of v22, /device:TPU:0, one launch (start us, length us, event | category | flops | bytes accessed | tf_op | source)
XLA Modules:
  0.0 43.2 jit_solution(8292395484059304035)
XLA Ops:
  0.0 0.0 copy-start.4
  0.0 2.9 %collective-permute-start.3 = (bf16[192,768]{1,0:T(8,128)(2,1)}, bf16[192,768]{1,0:T(8,128)(2,1)S(1)}, u32[]{:S(2)}, u32[]{:S(2)}) collective-permute-start(bf16[192,768]{1,0:T(8,128)(2,1)} %refs_0_), channel_id=1, source_target_pairs={{0,2},{1,3},{2,0},{3,1},{4,6},{5,7},{6,4},{7,5},{8,10},{9,11},{10,... | collective-permute-start | bytes 884744 | tf_op jit(solution)/shard_map/ppermute | solution.py:642
  2.9 1.5 %collective-permute-start = (s32[2,256]{1,0:T(2,128)}, s32[2,256]{1,0:T(2,128)S(1)}, u32[]{:S(2)}, u32[]{:S(2)}) collective-permute-start(s32[2,256]{1,0:T(2,128)} %ids_hbm.1), channel_id=1, source_target_pairs={{0,4},{1,5},{2,6},{3,7},{4,0},{5,1},{6,2},{7,3},{8,12},{9,13},{10,... | collective-permute-start | bytes 6152 | tf_op jit(solution)/shard_map/ppermute | solution.py:642
  4.5 0.0 copy-done.4
  4.5 0.0 copy-start.2
  4.5 0.5 %collective-permute-start.1 = (s32[1,2]{1,0:T(1,128)S(1)}, s32[1,2]{1,0:T(1,128)S(1)}, u32[]{:S(2)}, u32[]{:S(2)}) collective-permute-start(s32[1,2]{1,0:T(1,128)S(1)} %bitcast.4), channel_id=1, source_target_pairs={{0,4},{1,5},{2,6},{3,7},{4,0},{5,1},{6,2},{7,3},{8,12},{9,13},{10,... | collective-permute-start | bytes 32 | tf_op jit(solution)/shard_map/ppermute | solution.py:642
  5.0 1.9 %tables.1 = (bf16[40,576]{1,0:T(8,128)(2,1)S(1)}, s32[8,256]{1,0:T(8,128)S(1)}) custom-call(s32[2,256]{1,0:T(2,128)} %ids_hbm.1, s32[2]{0:T(128)} %live_hbm.1, bf16[33,768]{1,0:T(8,128)(2,1)} %refs_8_.1, bf16[3,192,768]{2,1,0:T(8,128)(2,1)} %qkv_hbm.1), custom_call_target="tpu_custom_call" | custom-call | flops 2000000000 | bytes 884736 | tf_op jit(solution)/shard_map/tables/pallas_call | solution.py:131
  6.8 1.2 %collective-permute-done.1.live_ref = s32[1,2]{1,0:T(1,128)S(1)} collective-permute-done((s32[1,2]{1,0:T(1,128)S(1)}, s32[1,2]{1,0:T(1,128)S(1)}, u32[]{:S(2)}, u32[]{:S(2)}) %collective-permute-start.1) | collective-permute-done | bytes 40 | tf_op jit(solution)/shard_map/ppermute | solution.py:642
  8.0 0.0 collective-permute-done.ids_ref
  8.0 0.1 join_raw.1.own_ref
  8.1 1.6 %collective-permute-start.2 = (s32[8,256]{1,0:T(8,128)S(1)}, s32[8,256]{1,0:T(8,128)S(1)}, u32[]{:S(2)}, u32[]{:S(2)}) collective-permute-start(s32[8,256]{1,0:T(8,128)S(1)} %join_raw.1.own_ref), channel_id=1, source_target_pairs={{0,8},{1,9},{2,10},{3,11},{4,12},{5,13},{6,14},{7,15},{8,0},{9,1},... | collective-permute-start | bytes 24584 | tf_op jit(solution)/shard_map/ppermute | solution.py:642
  9.7 0.5 %collective-permute-start.7 = (bf16[40,576]{1,0:T(8,128)(2,1)S(1)}, bf16[40,576]{1,0:T(8,128)(2,1)S(1)}, u32[]{:S(2)}, u32[]{:S(2)}) collective-permute-start(bf16[40,576]{1,0:T(8,128)(2,1)S(1)} %get-tuple-element.30.refs_0_), channel_id=1, source_target_pairs={{0,2},{1,3},{2,0},{3,1},{4,6},{5,7},{6,4},{7,5},{8,10},{9,11},{10,... | collective-permute-start | bytes 138248 | tf_op jit(solution)/shard_map/ppermute | solution.py:642
  10.3 0.0 collective-permute-start.8
  10.3 1.5 %collective-permute-done.2.other_ref = s32[8,256]{1,0:T(8,128)S(1)} collective-permute-done((s32[8,256]{1,0:T(8,128)S(1)}, s32[8,256]{1,0:T(8,128)S(1)}, u32[]{:S(2)}, u32[]{:S(2)}) %collective-permute-start.2) | collective-permute-done | bytes 8224 | tf_op jit(solution)/shard_map/ppermute | solution.py:642
  11.8 0.0 collective-permute-done.3.refs_2_
  11.8 0.1 collective-permute-start.6
  11.9 2.6 %collective-permute-start.9 = (s32[8,256]{1,0:T(8,128)S(1)}, s32[8,256]{1,0:T(8,128)S(1)}, u32[]{:S(2)}, u32[]{:S(2)}) collective-permute-start(s32[8,256]{1,0:T(8,128)S(1)} %join.1.refs_4_.near_codes_ref), channel_id=1, source_target_pairs={{0,16},{1,17},{2,18},{3,19},{4,20},{5,21},{6,22},{7,23},{8,24},{9,... | collective-permute-start | bytes 24584 | tf_op jit(solution)/shard_map/ppermute | solution.py:642
  14.5 0.0 copy-done.2
  14.5 0.2 collective-permute-start.4
  14.7 0.0 collective-permute-done.7.refs_2_
  14.7 0.3 collective-permute-start.5
  15.1 0.0 collective-permute-done.8.refs_3_
  15.1 0.0 collective-permute-done.6.refs_1_
  15.1 1.4 %near_scores.1 = (bf16[12,128,256]{2,1,0:T(8,128)(2,1)S(1)}, bf16[64,768]{1,0:T(8,128)(2,1)S(1)}, f32[384,256]{1,0:T(8,128)S(1)}, bf16[512,256]{1,0:T(8,128)(2,1)S(1)}, bf16[128,128]{1,0:T(8,128)(2,1)S(1)}) custom-call(bf16[40,576]{1,0:T(8,128)(2,1)S(1)} %get-tuple-element.30.refs_0_, bf16[40,576]{1,0:T(8,128)(2,1)S(1)} %collective-permute-done.6.refs_1_, ...), custom_call_target="tpu_custom_call" | custom-call | flops 1000000000 | bytes 1000000 | tf_op jit(solution)/shard_map/near_scores/pallas_call | solution.py:281
  16.5 0.0 collective-permute-done.9.far_codes_ref
  16.5 1.6 %row_attention.1 = (bf16[512,768]{1,0:T(8,128)(2,1)S(1)}, bf16[128,128]{1,0:T(8,128)(2,1)S(1)}, f32[16,128]{1,0:T(8,128)S(1)}) custom-call(bf16[12,128,256]{2,1,0:T(8,128)(2,1)S(1)} %get-tuple-element.32.scores_ref, bf16[64,768]{1,0:T(8,128)(2,1)S(1)} %get-tuple-element.33.values_ref, f32[384,256]{1,0:T(8,128)S(1)} %get-tuple-element.34.near_tied_ref, ...), custom_call_target="tpu_custom_call" | custom-call | flops 3000000000 | bytes 1000000 | tf_op jit(solution)/shard_map/row_attention/pallas_call | solution.py:372
  18.1 0.0 collective-permute-done.4.refs_1_
  18.2 0.0 collective-permute-done.5.refs_3_
  18.2 0.0 copy-done.1
  18.2 0.0 copy-done.3
  18.2 0.0 copy-start
  18.2 2.9 %column_attention.1 = (bf16[384,128]{1,0:T(8,128)(2,1)S(1)}, bf16[384,128]{1,0:T(8,128)(2,1)S(1)}, f32[512,192]{1,0:T(8,128)S(1)}) custom-call(bf16[192,768]{1,0:T(8,128)(2,1)S(1)} %copy-done.2, bf16[192,768]{1,0:T(8,128)(2,1)S(1)} %collective-permute-done.4.refs_1_, bf16[192,768]{1,0:T(8,128)(2,1)S(1)} %collective-permute-done.3.refs_2_, ...), custom_call_target="tpu_custom_call" | custom-call | flops 2000000000 | bytes 1000000 | tf_op jit(solution)/shard_map/column_attention/pallas_call | solution.py:522
  21.1 0.6 %collective-permute-start.11 = (bf16[384,128]{1,0:T(8,128)(2,1)S(1)}, bf16[384,128]{1,0:T(8,128)(2,1)S(1)}, u32[]{:S(2)}, u32[]{:S(2)}) collective-permute-start(bf16[384,128]{1,0:T(8,128)(2,1)S(1)} %get-tuple-element.40.refs_0_), channel_id=1, source_target_pairs={{0,2},{1,3},{2,0},{3,1},{4,6},{5,7},{6,4},{7,5},{8,10},{9,11},{10,... | collective-permute-start | bytes 294920 | tf_op jit(solution)/shard_map/ppermute | solution.py:642
  21.8 1.5 %collective-permute-start.14 = (bf16[384,128]{1,0:T(8,128)(2,1)S(1)}, bf16[384,128]{1,0:T(8,128)(2,1)S(1)}, u32[]{:S(2)}, u32[]{:S(2)}) collective-permute-start(bf16[384,128]{1,0:T(8,128)(2,1)S(1)} %get-tuple-element.41.refs_4_), channel_id=1, source_target_pairs={{0,2},{1,3},{2,0},{3,1},{4,6},{5,7},{6,4},{7,5},{8,10},{9,11},{10,... | collective-permute-start | bytes 294920 | tf_op jit(solution)/shard_map/ppermute | solution.py:642
  23.3 0.0 collective-permute-start.10
  23.3 0.5 %collective-permute-start.13 = (bf16[384,128]{1,0:T(8,128)(2,1)S(1)}, bf16[384,128]{1,0:T(8,128)(2,1)S(1)}, u32[]{:S(2)}, u32[]{:S(2)}) collective-permute-start(bf16[384,128]{1,0:T(8,128)(2,1)S(1)} %get-tuple-element.41.refs_4_), channel_id=1, source_target_pairs={{0,1},{1,0},{2,3},{3,2},{4,5},{5,4},{6,7},{7,6},{8,9},{9,8},{10,11... | collective-permute-start | bytes 294920 | tf_op jit(solution)/shard_map/ppermute | solution.py:642
  23.8 3.1 %collective-permute-done.11.refs_2_ = bf16[384,128]{1,0:T(8,128)(2,1)S(1)} collective-permute-done((bf16[384,128]{1,0:T(8,128)(2,1)S(1)}, bf16[384,128]{1,0:T(8,128)(2,1)S(1)}, u32[]{:S(2)}, u32[]{:S(2)}) %collective-permute-start.11) | collective-permute-done | bytes 98336 | tf_op jit(solution)/shard_map/ppermute | solution.py:642
  26.8 0.0 collective-permute-start.12
  26.8 1.5 %collective-permute-done.14.refs_6_ = bf16[384,128]{1,0:T(8,128)(2,1)S(1)} collective-permute-done((bf16[384,128]{1,0:T(8,128)(2,1)S(1)}, bf16[384,128]{1,0:T(8,128)(2,1)S(1)}, u32[]{:S(2)}, u32[]{:S(2)}) %collective-permute-start.14) | collective-permute-done | bytes 98336 | tf_op jit(solution)/shard_map/ppermute | solution.py:642
  28.4 0.0 collective-permute-start.15
  28.4 0.0 collective-permute-done.10.refs_1_
  28.4 0.0 collective-permute-done.13.refs_5_
  28.4 0.0 collective-permute-done.12.refs_3_
  28.4 1.3 %collective-permute-done.15.refs_7_ = bf16[384,128]{1,0:T(8,128)(2,1)S(1)} collective-permute-done((bf16[384,128]{1,0:T(8,128)(2,1)S(1)}, bf16[384,128]{1,0:T(8,128)(2,1)S(1)}, u32[]{:S(2)}, u32[]{:S(2)}) %collective-permute-start.15) | collective-permute-done | bytes 98336 | tf_op jit(solution)/shard_map/ppermute | solution.py:642
  29.7 0.0 copy-done
  29.7 0.5 %finish.1 = bf16[8,96,128]{2,1,0:T(8,128)(2,1)S(1)} custom-call(bf16[384,128]{1,0:T(8,128)(2,1)S(1)} %get-tuple-element.40.refs_0_, bf16[384,128]{1,0:T(8,128)(2,1)S(1)} %collective-permute-done.10.refs_1_, bf16[384,128]{1,0:T(8,128)(2,1)S(1)} %collective-permute-done.11.refs_2_, bf16[384,128]{1,0:T(8,128)(2,1)S(1)} %collective-permute-done.12.refs_3_, ...), custom_call_target="tpu_custom_call" | custom-call | tf_op jit(solution)/shard_map/finish/pallas_call | solution.py:582
  30.2 12.2 %all_to_all.5.blocks_ref = bf16[8,96,128]{2,1,0:T(8,128)(2,1)S(1)} all-to-all(bf16[8,96,128]{2,1,0:T(8,128)(2,1)S(1)} %finish.1), channel_id=1, replica_groups=mesh['seq'=8,'head'=4] {'seq'}, dimensions={0} | all-to-all | bytes 393216 | tf_op jit(solution)/shard_map/all_to_all | solution.py:692
  42.4 0.8 %order.1 = bf16[2,192,256]{2,1,0:T(8,128)(2,1)} custom-call(bf16[8,96,128]{2,1,0:T(8,128)(2,1)S(1)} %all_to_all.5.blocks_ref), custom_call_target="tpu_custom_call" | custom-call | tf_op jit(solution)/shard_map/order/pallas_call | solution.py:622
  (3 shorter events, 0.0 us)
Async XLA Ops:
  0.0 4.5 %copy-start.4 = (s32[2]{0:T(128)S(1)}, s32[2]{0:T(128)}, u32[]{:S(2)}) copy-start(s32[2]{0:T(128)} %live_hbm.1) | copy-start | bytes 28
  0.0 11.8 %collective-permute-start.3 = (bf16[192,768]{1,0:T(8,128)(2,1)}, bf16[192,768]{1,0:T(8,128)(2,1)S(1)}, u32[]{:S(2)}, u32[]{:S(2)}) collective-permute-start(bf16[192,768]{1,0:T(8,128)(2,1)} %refs_0_), channel_id=1, source_target_pairs={{0,2},{1,3},{2,0},{3,1},{4,6},{5,7},{6,4},{7,5},{8,10},{9,11},{10,... | collective-permute-start | bytes 884744 | tf_op jit(solution)/shard_map/ppermute | solution.py:642
  2.9 5.1 %collective-permute-start = (s32[2,256]{1,0:T(2,128)}, s32[2,256]{1,0:T(2,128)S(1)}, u32[]{:S(2)}, u32[]{:S(2)}) collective-permute-start(s32[2,256]{1,0:T(2,128)} %ids_hbm.1), channel_id=1, source_target_pairs={{0,4},{1,5},{2,6},{3,7},{4,0},{5,1},{6,2},{7,3},{8,12},{9,13},{10,... | collective-permute-start | bytes 6152 | tf_op jit(solution)/shard_map/ppermute | solution.py:642
  4.5 10.1 %copy-start.2 = (bf16[192,768]{1,0:T(8,128)(2,1)S(1)}, bf16[192,768]{1,0:T(8,128)(2,1)}, u32[]{:S(2)}) copy-start(bf16[192,768]{1,0:T(8,128)(2,1)} %refs_0_) | copy-start | bytes 884740
  4.5 3.5 %collective-permute-start.1 = (s32[1,2]{1,0:T(1,128)S(1)}, s32[1,2]{1,0:T(1,128)S(1)}, u32[]{:S(2)}, u32[]{:S(2)}) collective-permute-start(s32[1,2]{1,0:T(1,128)S(1)} %bitcast.4), channel_id=1, source_target_pairs={{0,4},{1,5},{2,6},{3,7},{4,0},{5,1},{6,2},{7,3},{8,12},{9,13},{10,... | collective-permute-start | bytes 32 | tf_op jit(solution)/shard_map/ppermute | solution.py:642
  8.1 3.7 %collective-permute-start.2 = (s32[8,256]{1,0:T(8,128)S(1)}, s32[8,256]{1,0:T(8,128)S(1)}, u32[]{:S(2)}, u32[]{:S(2)}) collective-permute-start(s32[8,256]{1,0:T(8,128)S(1)} %join_raw.1.own_ref), channel_id=1, source_target_pairs={{0,8},{1,9},{2,10},{3,11},{4,12},{5,13},{6,14},{7,15},{8,0},{9,1},... | collective-permute-start | bytes 24584 | tf_op jit(solution)/shard_map/ppermute | solution.py:642
  9.7 5.0 %collective-permute-start.7 = (bf16[40,576]{1,0:T(8,128)(2,1)S(1)}, bf16[40,576]{1,0:T(8,128)(2,1)S(1)}, u32[]{:S(2)}, u32[]{:S(2)}) collective-permute-start(bf16[40,576]{1,0:T(8,128)(2,1)S(1)} %get-tuple-element.30.refs_0_), channel_id=1, source_target_pairs={{0,2},{1,3},{2,0},{3,1},{4,6},{5,7},{6,4},{7,5},{8,10},{9,11},{10,... | collective-permute-start | bytes 138248 | tf_op jit(solution)/shard_map/ppermute | solution.py:642
  10.3 4.8 %collective-permute-start.8 = (bf16[40,576]{1,0:T(8,128)(2,1)S(1)}, bf16[40,576]{1,0:T(8,128)(2,1)S(1)}, u32[]{:S(2)}, u32[]{:S(2)}) collective-permute-start(bf16[40,576]{1,0:T(8,128)(2,1)S(1)} %get-tuple-element.30.refs_0_), channel_id=1, source_target_pairs={{0,3},{1,2},{2,1},{3,0},{4,7},{5,6},{6,5},{7,4},{8,11},{9,10},{10,... | collective-permute-start | bytes 138248 | tf_op jit(solution)/shard_map/ppermute | solution.py:642
  11.8 3.3 %collective-permute-start.6 = (bf16[40,576]{1,0:T(8,128)(2,1)S(1)}, bf16[40,576]{1,0:T(8,128)(2,1)S(1)}, u32[]{:S(2)}, u32[]{:S(2)}) collective-permute-start(bf16[40,576]{1,0:T(8,128)(2,1)S(1)} %get-tuple-element.30.refs_0_), channel_id=1, source_target_pairs={{0,1},{1,0},{2,3},{3,2},{4,5},{5,4},{6,7},{7,6},{8,9},{9,8},{10,11... | collective-permute-start | bytes 138248 | tf_op jit(solution)/shard_map/ppermute | solution.py:642
  11.9 4.6 %collective-permute-start.9 = (s32[8,256]{1,0:T(8,128)S(1)}, s32[8,256]{1,0:T(8,128)S(1)}, u32[]{:S(2)}, u32[]{:S(2)}) collective-permute-start(s32[8,256]{1,0:T(8,128)S(1)} %join.1.refs_4_.near_codes_ref), channel_id=1, source_target_pairs={{0,16},{1,17},{2,18},{3,19},{4,20},{5,21},{6,22},{7,23},{8,24},{9,... | collective-permute-start | bytes 24584 | tf_op jit(solution)/shard_map/ppermute | solution.py:642
  14.5 3.6 %collective-permute-start.4 = (bf16[192,768]{1,0:T(8,128)(2,1)S(1)}, bf16[192,768]{1,0:T(8,128)(2,1)S(1)}, u32[]{:S(2)}, u32[]{:S(2)}) collective-permute-start(bf16[192,768]{1,0:T(8,128)(2,1)S(1)} %copy-done.2), channel_id=1, source_target_pairs={{0,1},{1,0},{2,3},{3,2},{4,5},{5,4},{6,7},{7,6},{8,9},{9,8},{10,11... | collective-permute-start | bytes 884744 | tf_op jit(solution)/shard_map/ppermute | solution.py:642
  14.7 3.4 %collective-permute-start.5 = (bf16[192,768]{1,0:T(8,128)(2,1)S(1)}, bf16[192,768]{1,0:T(8,128)(2,1)S(1)}, u32[]{:S(2)}, u32[]{:S(2)}) collective-permute-start(bf16[192,768]{1,0:T(8,128)(2,1)S(1)} %collective-permute-done.3.refs_2_), channel_id=1, source_target_pairs={{0,1},{1,0},{2,3},{3,2},{4,5},{5,4},{6,7},{7,6},{8,9},{9,8},{10,11... | collective-permute-start | bytes 884744 | tf_op jit(solution)/shard_map/ppermute | solution.py:642
  16.5 1.7 %copy-start.1 = (bf16[3,192,768]{2,1,0:T(8,128)(2,1)S(1)}, bf16[3,192,768]{2,1,0:T(8,128)(2,1)}, u32[]{:S(2)}) copy-start(bf16[3,192,768]{2,1,0:T(8,128)(2,1)} %param.12) | copy-start | bytes 2654212
  16.5 1.7 %copy-start.3 = (bf16[33,768]{1,0:T(8,128)(2,1)S(1)}, bf16[33,768]{1,0:T(8,128)(2,1)}, u32[]{:S(2)}) copy-start(bf16[33,768]{1,0:T(8,128)(2,1)} %refs_8_.1) | copy-start | bytes 152068
  18.2 11.5 %copy-start = (bf16[192,768]{1,0:T(8,128)(2,1)S(1)}, bf16[192,768]{1,0:T(8,128)(2,1)}, u32[]{:S(2)}) copy-start(bf16[192,768]{1,0:T(8,128)(2,1)} %refs_9_.1) | copy-start | bytes 884740
  21.1 5.7 %collective-permute-start.11 = (bf16[384,128]{1,0:T(8,128)(2,1)S(1)}, bf16[384,128]{1,0:T(8,128)(2,1)S(1)}, u32[]{:S(2)}, u32[]{:S(2)}) collective-permute-start(bf16[384,128]{1,0:T(8,128)(2,1)S(1)} %get-tuple-element.40.refs_0_), channel_id=1, source_target_pairs={{0,2},{1,3},{2,0},{3,1},{4,6},{5,7},{6,4},{7,5},{8,10},{9,11},{10,... | collective-permute-start | bytes 294920 | tf_op jit(solution)/shard_map/ppermute | solution.py:642
  21.8 6.6 %collective-permute-start.14 = (bf16[384,128]{1,0:T(8,128)(2,1)S(1)}, bf16[384,128]{1,0:T(8,128)(2,1)S(1)}, u32[]{:S(2)}, u32[]{:S(2)}) collective-permute-start(bf16[384,128]{1,0:T(8,128)(2,1)S(1)} %get-tuple-element.41.refs_4_), channel_id=1, source_target_pairs={{0,2},{1,3},{2,0},{3,1},{4,6},{5,7},{6,4},{7,5},{8,10},{9,11},{10,... | collective-permute-start | bytes 294920 | tf_op jit(solution)/shard_map/ppermute | solution.py:642
  23.3 5.1 %collective-permute-start.10 = (bf16[384,128]{1,0:T(8,128)(2,1)S(1)}, bf16[384,128]{1,0:T(8,128)(2,1)S(1)}, u32[]{:S(2)}, u32[]{:S(2)}) collective-permute-start(bf16[384,128]{1,0:T(8,128)(2,1)S(1)} %get-tuple-element.40.refs_0_), channel_id=1, source_target_pairs={{0,1},{1,0},{2,3},{3,2},{4,5},{5,4},{6,7},{7,6},{8,9},{9,8},{10,11... | collective-permute-start | bytes 294920 | tf_op jit(solution)/shard_map/ppermute | solution.py:642
  23.3 5.1 %collective-permute-start.13 = (bf16[384,128]{1,0:T(8,128)(2,1)S(1)}, bf16[384,128]{1,0:T(8,128)(2,1)S(1)}, u32[]{:S(2)}, u32[]{:S(2)}) collective-permute-start(bf16[384,128]{1,0:T(8,128)(2,1)S(1)} %get-tuple-element.41.refs_4_), channel_id=1, source_target_pairs={{0,1},{1,0},{2,3},{3,2},{4,5},{5,4},{6,7},{7,6},{8,9},{9,8},{10,11... | collective-permute-start | bytes 294920 | tf_op jit(solution)/shard_map/ppermute | solution.py:642
  26.8 1.6 %collective-permute-start.12 = (bf16[384,128]{1,0:T(8,128)(2,1)S(1)}, bf16[384,128]{1,0:T(8,128)(2,1)S(1)}, u32[]{:S(2)}, u32[]{:S(2)}) collective-permute-start(bf16[384,128]{1,0:T(8,128)(2,1)S(1)} %collective-permute-done.11.refs_2_), channel_id=1, source_target_pairs={{0,1},{1,0},{2,3},{3,2},{4,5},{5,4},{6,7},{7,6},{8,9},{9,8},{10,11... | collective-permute-start | bytes 294920 | tf_op jit(solution)/shard_map/ppermute | solution.py:642
  28.4 1.3 %collective-permute-start.15 = (bf16[384,128]{1,0:T(8,128)(2,1)S(1)}, bf16[384,128]{1,0:T(8,128)(2,1)S(1)}, u32[]{:S(2)}, u32[]{:S(2)}) collective-permute-start(bf16[384,128]{1,0:T(8,128)(2,1)S(1)} %collective-permute-done.14.refs_6_), channel_id=1, source_target_pairs={{0,1},{1,0},{2,3},{3,2},{4,5},{5,4},{6,7},{7,6},{8,9},{9,8},{10,11... | collective-permute-start | bytes 294920 | tf_op jit(solution)/shard_map/ppermute | solution.py:642

commit v23 on v22

--- a/solution.py
+++ b/solution.py
@@ -269,8 +269,7 @@
         scores_ref[h, :, LANES : 2 * LANES] = low[h // 2][these]
 
     one_hots(codes_ref[...], group, hot_ref, own_ref, live_own_ref)
-    for at, first, last in head_groups(heads, sum_ref.shape[0] // heads):
-        tied_ref[at, :] = tied_sum(scores_ref, live_own_ref, hot_ref, sum_ref, first, last)
+    tied_ref[...] = tied_sum(scores_ref, live_own_ref, hot_ref, sum_ref, 0, heads)
 
 
 def attend_near(tables, codes, own):
@@ -429,9 +428,9 @@
         0,
     )
     row_out = row_out_ref[...].reshape(width, width)
-    halves_at = [slice(c * tokens // 2, (c + 1) * tokens // 2) for c in range(2)]
+    quarters = [slice(c * tokens // 4, (c + 1) * tokens // 4) for c in range(4)]
     normed = []
-    for at in halves_at:
+    for at in quarters:
         mixed = embedded[at] + dot_nt(row_context_ref[at, :], row_out)
         mixed_ref[at, :] = mixed
         normed.append(layer_norm(mixed).astype(bf16))
@@ -588,42 +587,28 @@
     )(*contexts[0], *contexts[1], mixed, col_out)
 
 
-def order_kernel(blocks_ref, out_hbm, out_ref, sems):
+def order_kernel(blocks_ref, out_ref):
     groups = blocks_ref.shape[0]
     local, cols = out_ref.shape[1:]
     own = cols // groups
     rest = local - LANES
-    stores = []
-
-    def store(row, first, last, values):
-        out_ref[row, first:last, :] = values
-        stores.append(
-            pltpu.make_async_copy(
-                out_ref.at[row, first:last], out_hbm.at[row, first:last], sems.at[len(stores)]
-            )
-        )
-        stores[-1].start()
-
+    one = (iota((LANES, LANES), 0) == iota((LANES, LANES), 1)).astype(f32).astype(bf16)
     for part in range(3):
         piece = jnp.concatenate(
             [blocks_ref[g, part * own : (part + 1) * own, :] for g in range(groups)], 0
         )
-        turned = piece.astype(f32).T.astype(bf16)
+        turned = dot_nt(one, piece).astype(bf16)
         if part < 2:
-            store(part, 0, LANES, turned)
+            out_ref[part, 0:LANES, :] = turned
         else:
             for r in range(2):
-                store(r, LANES, local, turned[r * rest : (r + 1) * rest, :])
-    for started in stores:
-        started.wait()
+                out_ref[r, LANES:local, :] = turned[r * rest : (r + 1) * rest, :]
 
 
 def order(blocks, cols, local):
     return pl.pallas_call(
         order_kernel,
         out_shape=jax.ShapeDtypeStruct((2, local, cols), bf16),
-        out_specs=pl.BlockSpec(memory_space=pl.ANY),
-        scratch_shapes=[pltpu.VMEM((2, local, cols), bf16), pltpu.SemaphoreType.DMA((4,))],
         compiler_params=pltpu.CompilerParams(vmem_limit_bytes=SMALL_VMEM),
         name="order",
     )(blocks)

time: 43.4 us -> 45.1 us (1.039)
  Pallas kernels: 9.25 us -> 10.7 us
    pallas_call x1, Pallas kernels: 2.94 us -> 4.54 us  [attend_columns_here(): pl.pallas_call(functools.partial(column_kernel, parts), out_shape=(jax.Sh...]
  transfers between devices with their start and end apart: 16 -> 16, of which waited for: 5 -> 6; matrix products, arithmetic and copies ran while one was open for 0% -> 0% of each run, Pallas kernels for 12% -> 11%
where the time goes in v23:
time: 45.1 us; the launch traced here: 44.9 us
  starting transfers between devices  13 us (29%)
  blocking collectives  12.5 us (28%)
  Pallas kernels  10.7 us (24%)
  waiting for transfers between devices  8.66 us (19%)
    ppermute x16, starting transfers between devices, pairwise(): lax.ppermute(value, ('seq', 'head'), [(i, g * parts + p) for i, (g, p) in...  13 us
    all_to_all x1, blocking collectives, fast_body(): lax.all_to_all(blocks, 'seq', split_axis=0, concat_axis=0, tiled=True)  12.5 us
    ppermute x16, waiting for transfers between devices, pairwise(): lax.ppermute(value, ('seq', 'head'), [(i, g * parts + p) for i, (g, p) in...  8.66 us
    pallas_call x1, Pallas kernels, attend_columns_here(): pl.pallas_call(functools.partial(column_kernel, parts), out_shape=(jax.Sh...  4.54 us
    pallas_call x1, Pallas kernels, make_tables(): pl.pallas_call(table_kernel, out_shape=(jax.ShapeDtypeStruct((TABLE_ROWS,...  1.87 us
    pallas_call x1, Pallas kernels, attend_rows(): pl.pallas_call(row_kernel, out_shape=(jax.ShapeDtypeStruct((2 * half * ow...  1.62 us
    pallas_call x1, Pallas kernels, attend_near(): pl.pallas_call(functools.partial(near_kernel, parts), out_shape=(jax.Shap...  1.18 us
  transfers between devices with their start and end apart: 16, of which 6 were waited for; matrix products, arithmetic and copies ran while one was open for 0% of the time, Pallas kernels for 11%

profile of v23, /device:TPU:0, one launch (start us, length us, event | category | flops | bytes accessed | tf_op | source)
XLA Modules:
  0.0 44.9 jit_solution(3656079109314722362)
XLA Ops:
  0.0 0.0 copy-start.4
  0.0 2.9 %collective-permute-start.3 = (bf16[192,768]{1,0:T(8,128)(2,1)}, bf16[192,768]{1,0:T(8,128)(2,1)S(1)}, u32[]{:S(2)}, u32[]{:S(2)}) collective-permute-start(bf16[192,768]{1,0:T(8,128)(2,1)} %refs_0_), channel_id=1, source_target_pairs={{0,2},{1,3},{2,0},{3,1},{4,6},{5,7},{6,4},{7,5},{8,10},{9,11},{10,... | collective-permute-start | bytes 884744 | tf_op jit(solution)/shard_map/ppermute | solution.py:627
  2.9 1.5 %collective-permute-start = (s32[2,256]{1,0:T(2,128)}, s32[2,256]{1,0:T(2,128)S(1)}, u32[]{:S(2)}, u32[]{:S(2)}) collective-permute-start(s32[2,256]{1,0:T(2,128)} %ids_hbm.1), channel_id=1, source_target_pairs={{0,4},{1,5},{2,6},{3,7},{4,0},{5,1},{6,2},{7,3},{8,12},{9,13},{10,... | collective-permute-start | bytes 6152 | tf_op jit(solution)/shard_map/ppermute | solution.py:627
  4.5 0.0 copy-done.4
  4.5 0.0 copy-start.2
  4.5 0.5 %collective-permute-start.1 = (s32[1,2]{1,0:T(1,128)S(1)}, s32[1,2]{1,0:T(1,128)S(1)}, u32[]{:S(2)}, u32[]{:S(2)}) collective-permute-start(s32[1,2]{1,0:T(1,128)S(1)} %bitcast.4), channel_id=1, source_target_pairs={{0,4},{1,5},{2,6},{3,7},{4,0},{5,1},{6,2},{7,3},{8,12},{9,13},{10,... | collective-permute-start | bytes 32 | tf_op jit(solution)/shard_map/ppermute | solution.py:627
  5.0 1.9 %tables.1 = (bf16[40,576]{1,0:T(8,128)(2,1)S(1)}, s32[8,256]{1,0:T(8,128)S(1)}) custom-call(s32[2,256]{1,0:T(2,128)} %ids_hbm.1, s32[2]{0:T(128)} %live_hbm.1, bf16[33,768]{1,0:T(8,128)(2,1)} %refs_8_.1, bf16[3,192,768]{2,1,0:T(8,128)(2,1)} %qkv_hbm.1), custom_call_target="tpu_custom_call" | custom-call | flops 2000000000 | bytes 884736 | tf_op jit(solution)/shard_map/tables/pallas_call | solution.py:131
  6.8 1.2 %collective-permute-done.1.live_ref = s32[1,2]{1,0:T(1,128)S(1)} collective-permute-done((s32[1,2]{1,0:T(1,128)S(1)}, s32[1,2]{1,0:T(1,128)S(1)}, u32[]{:S(2)}, u32[]{:S(2)}) %collective-permute-start.1) | collective-permute-done | bytes 40 | tf_op jit(solution)/shard_map/ppermute | solution.py:627
  8.0 0.0 collective-permute-done.ids_ref
  8.0 0.1 join_raw.1.own_ref
  8.1 1.6 %collective-permute-start.2 = (s32[8,256]{1,0:T(8,128)S(1)}, s32[8,256]{1,0:T(8,128)S(1)}, u32[]{:S(2)}, u32[]{:S(2)}) collective-permute-start(s32[8,256]{1,0:T(8,128)S(1)} %join_raw.1.own_ref), channel_id=1, source_target_pairs={{0,8},{1,9},{2,10},{3,11},{4,12},{5,13},{6,14},{7,15},{8,0},{9,1},... | collective-permute-start | bytes 24584 | tf_op jit(solution)/shard_map/ppermute | solution.py:627
  9.7 0.5 %collective-permute-start.7 = (bf16[40,576]{1,0:T(8,128)(2,1)S(1)}, bf16[40,576]{1,0:T(8,128)(2,1)S(1)}, u32[]{:S(2)}, u32[]{:S(2)}) collective-permute-start(bf16[40,576]{1,0:T(8,128)(2,1)S(1)} %get-tuple-element.30.refs_0_), channel_id=1, source_target_pairs={{0,2},{1,3},{2,0},{3,1},{4,6},{5,7},{6,4},{7,5},{8,10},{9,11},{10,... | collective-permute-start | bytes 138248 | tf_op jit(solution)/shard_map/ppermute | solution.py:627
  10.3 0.0 collective-permute-start.8
  10.3 1.5 %collective-permute-done.2.other_ref = s32[8,256]{1,0:T(8,128)S(1)} collective-permute-done((s32[8,256]{1,0:T(8,128)S(1)}, s32[8,256]{1,0:T(8,128)S(1)}, u32[]{:S(2)}, u32[]{:S(2)}) %collective-permute-start.2) | collective-permute-done | bytes 8224 | tf_op jit(solution)/shard_map/ppermute | solution.py:627
  11.8 0.0 collective-permute-done.3.refs_2_
  11.8 0.1 collective-permute-start.6
  11.9 2.6 %collective-permute-start.9 = (s32[8,256]{1,0:T(8,128)S(1)}, s32[8,256]{1,0:T(8,128)S(1)}, u32[]{:S(2)}, u32[]{:S(2)}) collective-permute-start(s32[8,256]{1,0:T(8,128)S(1)} %join.1.refs_4_.near_codes_ref), channel_id=1, source_target_pairs={{0,16},{1,17},{2,18},{3,19},{4,20},{5,21},{6,22},{7,23},{8,24},{9,... | collective-permute-start | bytes 24584 | tf_op jit(solution)/shard_map/ppermute | solution.py:627
  14.5 0.0 copy-done.2
  14.5 0.2 collective-permute-start.4
  14.7 0.0 collective-permute-done.7.refs_2_
  14.7 0.3 collective-permute-start.5
  15.1 0.0 collective-permute-done.8.refs_3_
  15.1 0.0 collective-permute-done.6.refs_1_
  15.1 1.2 %near_scores.1 = (bf16[12,128,256]{2,1,0:T(8,128)(2,1)S(1)}, bf16[64,768]{1,0:T(8,128)(2,1)S(1)}, f32[384,256]{1,0:T(8,128)S(1)}, bf16[512,256]{1,0:T(8,128)(2,1)S(1)}, bf16[128,128]{1,0:T(8,128)(2,1)S(1)}) custom-call(bf16[40,576]{1,0:T(8,128)(2,1)S(1)} %get-tuple-element.30.refs_0_, bf16[40,576]{1,0:T(8,128)(2,1)S(1)} %collective-permute-done.6.refs_1_, ...), custom_call_target="tpu_custom_call" | custom-call | flops 1000000000 | bytes 1000000 | tf_op jit(solution)/shard_map/near_scores/pallas_call | solution.py:280
  16.2 0.3 collective-permute-done.9.far_codes_ref
  16.5 1.6 %row_attention.1 = (bf16[512,768]{1,0:T(8,128)(2,1)S(1)}, bf16[128,128]{1,0:T(8,128)(2,1)S(1)}, f32[16,128]{1,0:T(8,128)S(1)}) custom-call(bf16[12,128,256]{2,1,0:T(8,128)(2,1)S(1)} %get-tuple-element.32.scores_ref, bf16[64,768]{1,0:T(8,128)(2,1)S(1)} %get-tuple-element.33.values_ref, f32[384,256]{1,0:T(8,128)S(1)} %get-tuple-element.34.near_tied_ref, ...), custom_call_target="tpu_custom_call" | custom-call | flops 3000000000 | bytes 1000000 | tf_op jit(solution)/shard_map/row_attention/pallas_call | solution.py:371
  18.1 0.0 collective-permute-done.4.refs_1_
  18.1 0.0 collective-permute-done.5.refs_3_
  18.2 0.0 copy-done.1
  18.2 0.0 copy-done.3
  18.2 0.0 copy-start
  18.2 4.5 %column_attention.1 = (bf16[384,128]{1,0:T(8,128)(2,1)S(1)}, bf16[384,128]{1,0:T(8,128)(2,1)S(1)}, f32[512,192]{1,0:T(8,128)S(1)}) custom-call(bf16[192,768]{1,0:T(8,128)(2,1)S(1)} %copy-done.2, bf16[192,768]{1,0:T(8,128)(2,1)S(1)} %collective-permute-done.4.refs_1_, bf16[192,768]{1,0:T(8,128)(2,1)S(1)} %collective-permute-done.3.refs_2_, ...), custom_call_target="tpu_custom_call" | custom-call | flops 2000000000 | bytes 1000000 | tf_op jit(solution)/shard_map/column_attention/pallas_call | solution.py:521
  22.7 0.6 %collective-permute-start.11 = (bf16[384,128]{1,0:T(8,128)(2,1)S(1)}, bf16[384,128]{1,0:T(8,128)(2,1)S(1)}, u32[]{:S(2)}, u32[]{:S(2)}) collective-permute-start(bf16[384,128]{1,0:T(8,128)(2,1)S(1)} %get-tuple-element.40.refs_0_), channel_id=1, source_target_pairs={{0,2},{1,3},{2,0},{3,1},{4,6},{5,7},{6,4},{7,5},{8,10},{9,11},{10,... | collective-permute-start | bytes 294920 | tf_op jit(solution)/shard_map/ppermute | solution.py:627
  23.4 1.5 %collective-permute-start.14 = (bf16[384,128]{1,0:T(8,128)(2,1)S(1)}, bf16[384,128]{1,0:T(8,128)(2,1)S(1)}, u32[]{:S(2)}, u32[]{:S(2)}) collective-permute-start(bf16[384,128]{1,0:T(8,128)(2,1)S(1)} %get-tuple-element.41.refs_4_), channel_id=1, source_target_pairs={{0,2},{1,3},{2,0},{3,1},{4,6},{5,7},{6,4},{7,5},{8,10},{9,11},{10,... | collective-permute-start | bytes 294920 | tf_op jit(solution)/shard_map/ppermute | solution.py:627
  24.8 0.0 collective-permute-start.10
  24.8 0.5 %collective-permute-start.13 = (bf16[384,128]{1,0:T(8,128)(2,1)S(1)}, bf16[384,128]{1,0:T(8,128)(2,1)S(1)}, u32[]{:S(2)}, u32[]{:S(2)}) collective-permute-start(bf16[384,128]{1,0:T(8,128)(2,1)S(1)} %get-tuple-element.41.refs_4_), channel_id=1, source_target_pairs={{0,1},{1,0},{2,3},{3,2},{4,5},{5,4},{6,7},{7,6},{8,9},{9,8},{10,11... | collective-permute-start | bytes 294920 | tf_op jit(solution)/shard_map/ppermute | solution.py:627
  25.3 3.1 %collective-permute-done.11.refs_2_ = bf16[384,128]{1,0:T(8,128)(2,1)S(1)} collective-permute-done((bf16[384,128]{1,0:T(8,128)(2,1)S(1)}, bf16[384,128]{1,0:T(8,128)(2,1)S(1)}, u32[]{:S(2)}, u32[]{:S(2)}) %collective-permute-start.11) | collective-permute-done | bytes 98336 | tf_op jit(solution)/shard_map/ppermute | solution.py:627
  28.4 0.0 collective-permute-start.12
  28.4 1.3 %collective-permute-done.14.refs_6_ = bf16[384,128]{1,0:T(8,128)(2,1)S(1)} collective-permute-done((bf16[384,128]{1,0:T(8,128)(2,1)S(1)}, bf16[384,128]{1,0:T(8,128)(2,1)S(1)}, u32[]{:S(2)}, u32[]{:S(2)}) %collective-permute-start.14) | collective-permute-done | bytes 98336 | tf_op jit(solution)/shard_map/ppermute | solution.py:627
  29.7 0.0 collective-permute-start.15
  29.7 0.0 collective-permute-done.10.refs_1_
  29.7 0.0 collective-permute-done.13.refs_5_
  29.8 0.0 collective-permute-done.12.refs_3_
  29.8 1.3 %collective-permute-done.15.refs_7_ = bf16[384,128]{1,0:T(8,128)(2,1)S(1)} collective-permute-done((bf16[384,128]{1,0:T(8,128)(2,1)S(1)}, bf16[384,128]{1,0:T(8,128)(2,1)S(1)}, u32[]{:S(2)}, u32[]{:S(2)}) %collective-permute-start.15) | collective-permute-done | bytes 98336 | tf_op jit(solution)/shard_map/ppermute | solution.py:627
  31.0 0.0 copy-done
  31.0 0.5 %finish.1 = bf16[8,96,128]{2,1,0:T(8,128)(2,1)S(1)} custom-call(bf16[384,128]{1,0:T(8,128)(2,1)S(1)} %get-tuple-element.40.refs_0_, bf16[384,128]{1,0:T(8,128)(2,1)S(1)} %collective-permute-done.10.refs_1_, bf16[384,128]{1,0:T(8,128)(2,1)S(1)} %collective-permute-done.11.refs_2_, bf16[384,128]{1,0:T(8,128)(2,1)S(1)} %collective-permute-done.12.refs_3_, ...), custom_call_target="tpu_custom_call" | custom-call | tf_op jit(solution)/shard_map/finish/pallas_call | solution.py:581
  31.6 12.5 %all_to_all.5.blocks_ref = bf16[8,96,128]{2,1,0:T(8,128)(2,1)S(1)} all-to-all(bf16[8,96,128]{2,1,0:T(8,128)(2,1)S(1)} %finish.1), channel_id=1, replica_groups=mesh['seq'=8,'head'=4] {'seq'}, dimensions={0} | all-to-all | bytes 393216 | tf_op jit(solution)/shard_map/all_to_all | solution.py:677
  44.0 0.9 %order.1 = bf16[2,192,256]{2,1,0:T(8,128)(2,1)} custom-call(bf16[8,96,128]{2,1,0:T(8,128)(2,1)S(1)} %all_to_all.5.blocks_ref), custom_call_target="tpu_custom_call" | custom-call | tf_op jit(solution)/shard_map/order/pallas_call | solution.py:609
  (3 shorter events, 0.0 us)
Async XLA Ops:
  0.0 4.5 %copy-start.4 = (s32[2]{0:T(128)S(1)}, s32[2]{0:T(128)}, u32[]{:S(2)}) copy-start(s32[2]{0:T(128)} %live_hbm.1) | copy-start | bytes 28
  0.0 11.8 %collective-permute-start.3 = (bf16[192,768]{1,0:T(8,128)(2,1)}, bf16[192,768]{1,0:T(8,128)(2,1)S(1)}, u32[]{:S(2)}, u32[]{:S(2)}) collective-permute-start(bf16[192,768]{1,0:T(8,128)(2,1)} %refs_0_), channel_id=1, source_target_pairs={{0,2},{1,3},{2,0},{3,1},{4,6},{5,7},{6,4},{7,5},{8,10},{9,11},{10,... | collective-permute-start | bytes 884744 | tf_op jit(solution)/shard_map/ppermute | solution.py:627
  2.9 5.1 %collective-permute-start = (s32[2,256]{1,0:T(2,128)}, s32[2,256]{1,0:T(2,128)S(1)}, u32[]{:S(2)}, u32[]{:S(2)}) collective-permute-start(s32[2,256]{1,0:T(2,128)} %ids_hbm.1), channel_id=1, source_target_pairs={{0,4},{1,5},{2,6},{3,7},{4,0},{5,1},{6,2},{7,3},{8,12},{9,13},{10,... | collective-permute-start | bytes 6152 | tf_op jit(solution)/shard_map/ppermute | solution.py:627
  4.5 10.1 %copy-start.2 = (bf16[192,768]{1,0:T(8,128)(2,1)S(1)}, bf16[192,768]{1,0:T(8,128)(2,1)}, u32[]{:S(2)}) copy-start(bf16[192,768]{1,0:T(8,128)(2,1)} %refs_0_) | copy-start | bytes 884740
  4.5 3.5 %collective-permute-start.1 = (s32[1,2]{1,0:T(1,128)S(1)}, s32[1,2]{1,0:T(1,128)S(1)}, u32[]{:S(2)}, u32[]{:S(2)}) collective-permute-start(s32[1,2]{1,0:T(1,128)S(1)} %bitcast.4), channel_id=1, source_target_pairs={{0,4},{1,5},{2,6},{3,7},{4,0},{5,1},{6,2},{7,3},{8,12},{9,13},{10,... | collective-permute-start | bytes 32 | tf_op jit(solution)/shard_map/ppermute | solution.py:627
  8.1 3.7 %collective-permute-start.2 = (s32[8,256]{1,0:T(8,128)S(1)}, s32[8,256]{1,0:T(8,128)S(1)}, u32[]{:S(2)}, u32[]{:S(2)}) collective-permute-start(s32[8,256]{1,0:T(8,128)S(1)} %join_raw.1.own_ref), channel_id=1, source_target_pairs={{0,8},{1,9},{2,10},{3,11},{4,12},{5,13},{6,14},{7,15},{8,0},{9,1},... | collective-permute-start | bytes 24584 | tf_op jit(solution)/shard_map/ppermute | solution.py:627
  9.7 5.0 %collective-permute-start.7 = (bf16[40,576]{1,0:T(8,128)(2,1)S(1)}, bf16[40,576]{1,0:T(8,128)(2,1)S(1)}, u32[]{:S(2)}, u32[]{:S(2)}) collective-permute-start(bf16[40,576]{1,0:T(8,128)(2,1)S(1)} %get-tuple-element.30.refs_0_), channel_id=1, source_target_pairs={{0,2},{1,3},{2,0},{3,1},{4,6},{5,7},{6,4},{7,5},{8,10},{9,11},{10,... | collective-permute-start | bytes 138248 | tf_op jit(solution)/shard_map/ppermute | solution.py:627
  10.3 4.8 %collective-permute-start.8 = (bf16[40,576]{1,0:T(8,128)(2,1)S(1)}, bf16[40,576]{1,0:T(8,128)(2,1)S(1)}, u32[]{:S(2)}, u32[]{:S(2)}) collective-permute-start(bf16[40,576]{1,0:T(8,128)(2,1)S(1)} %get-tuple-element.30.refs_0_), channel_id=1, source_target_pairs={{0,3},{1,2},{2,1},{3,0},{4,7},{5,6},{6,5},{7,4},{8,11},{9,10},{10,... | collective-permute-start | bytes 138248 | tf_op jit(solution)/shard_map/ppermute | solution.py:627
  11.8 3.3 %collective-permute-start.6 = (bf16[40,576]{1,0:T(8,128)(2,1)S(1)}, bf16[40,576]{1,0:T(8,128)(2,1)S(1)}, u32[]{:S(2)}, u32[]{:S(2)}) collective-permute-start(bf16[40,576]{1,0:T(8,128)(2,1)S(1)} %get-tuple-element.30.refs_0_), channel_id=1, source_target_pairs={{0,1},{1,0},{2,3},{3,2},{4,5},{5,4},{6,7},{7,6},{8,9},{9,8},{10,11... | collective-permute-start | bytes 138248 | tf_op jit(solution)/shard_map/ppermute | solution.py:627
  11.9 4.6 %collective-permute-start.9 = (s32[8,256]{1,0:T(8,128)S(1)}, s32[8,256]{1,0:T(8,128)S(1)}, u32[]{:S(2)}, u32[]{:S(2)}) collective-permute-start(s32[8,256]{1,0:T(8,128)S(1)} %join.1.refs_4_.near_codes_ref), channel_id=1, source_target_pairs={{0,16},{1,17},{2,18},{3,19},{4,20},{5,21},{6,22},{7,23},{8,24},{9,... | collective-permute-start | bytes 24584 | tf_op jit(solution)/shard_map/ppermute | solution.py:627
  14.5 3.6 %collective-permute-start.4 = (bf16[192,768]{1,0:T(8,128)(2,1)S(1)}, bf16[192,768]{1,0:T(8,128)(2,1)S(1)}, u32[]{:S(2)}, u32[]{:S(2)}) collective-permute-start(bf16[192,768]{1,0:T(8,128)(2,1)S(1)} %copy-done.2), channel_id=1, source_target_pairs={{0,1},{1,0},{2,3},{3,2},{4,5},{5,4},{6,7},{7,6},{8,9},{9,8},{10,11... | collective-permute-start | bytes 884744 | tf_op jit(solution)/shard_map/ppermute | solution.py:627
  14.7 3.4 %collective-permute-start.5 = (bf16[192,768]{1,0:T(8,128)(2,1)S(1)}, bf16[192,768]{1,0:T(8,128)(2,1)S(1)}, u32[]{:S(2)}, u32[]{:S(2)}) collective-permute-start(bf16[192,768]{1,0:T(8,128)(2,1)S(1)} %collective-permute-done.3.refs_2_), channel_id=1, source_target_pairs={{0,1},{1,0},{2,3},{3,2},{4,5},{5,4},{6,7},{7,6},{8,9},{9,8},{10,11... | collective-permute-start | bytes 884744 | tf_op jit(solution)/shard_map/ppermute | solution.py:627
  16.5 1.7 %copy-start.1 = (bf16[3,192,768]{2,1,0:T(8,128)(2,1)S(1)}, bf16[3,192,768]{2,1,0:T(8,128)(2,1)}, u32[]{:S(2)}) copy-start(bf16[3,192,768]{2,1,0:T(8,128)(2,1)} %param.12) | copy-start | bytes 2654212
  16.5 1.7 %copy-start.3 = (bf16[33,768]{1,0:T(8,128)(2,1)S(1)}, bf16[33,768]{1,0:T(8,128)(2,1)}, u32[]{:S(2)}) copy-start(bf16[33,768]{1,0:T(8,128)(2,1)} %refs_8_.1) | copy-start | bytes 152068
  18.2 12.9 %copy-start = (bf16[192,768]{1,0:T(8,128)(2,1)S(1)}, bf16[192,768]{1,0:T(8,128)(2,1)}, u32[]{:S(2)}) copy-start(bf16[192,768]{1,0:T(8,128)(2,1)} %refs_9_.1) | copy-start | bytes 884740
  22.7 5.7 %collective-permute-start.11 = (bf16[384,128]{1,0:T(8,128)(2,1)S(1)}, bf16[384,128]{1,0:T(8,128)(2,1)S(1)}, u32[]{:S(2)}, u32[]{:S(2)}) collective-permute-start(bf16[384,128]{1,0:T(8,128)(2,1)S(1)} %get-tuple-element.40.refs_0_), channel_id=1, source_target_pairs={{0,2},{1,3},{2,0},{3,1},{4,6},{5,7},{6,4},{7,5},{8,10},{9,11},{10,... | collective-permute-start | bytes 294920 | tf_op jit(solution)/shard_map/ppermute | solution.py:627
  23.4 6.4 %collective-permute-start.14 = (bf16[384,128]{1,0:T(8,128)(2,1)S(1)}, bf16[384,128]{1,0:T(8,128)(2,1)S(1)}, u32[]{:S(2)}, u32[]{:S(2)}) collective-permute-start(bf16[384,128]{1,0:T(8,128)(2,1)S(1)} %get-tuple-element.41.refs_4_), channel_id=1, source_target_pairs={{0,2},{1,3},{2,0},{3,1},{4,6},{5,7},{6,4},{7,5},{8,10},{9,11},{10,... | collective-permute-start | bytes 294920 | tf_op jit(solution)/shard_map/ppermute | solution.py:627
  24.8 4.9 %collective-permute-start.10 = (bf16[384,128]{1,0:T(8,128)(2,1)S(1)}, bf16[384,128]{1,0:T(8,128)(2,1)S(1)}, u32[]{:S(2)}, u32[]{:S(2)}) collective-permute-start(bf16[384,128]{1,0:T(8,128)(2,1)S(1)} %get-tuple-element.40.refs_0_), channel_id=1, source_target_pairs={{0,1},{1,0},{2,3},{3,2},{4,5},{5,4},{6,7},{7,6},{8,9},{9,8},{10,11... | collective-permute-start | bytes 294920 | tf_op jit(solution)/shard_map/ppermute | solution.py:627
  24.8 4.9 %collective-permute-start.13 = (bf16[384,128]{1,0:T(8,128)(2,1)S(1)}, bf16[384,128]{1,0:T(8,128)(2,1)S(1)}, u32[]{:S(2)}, u32[]{:S(2)}) collective-permute-start(bf16[384,128]{1,0:T(8,128)(2,1)S(1)} %get-tuple-element.41.refs_4_), channel_id=1, source_target_pairs={{0,1},{1,0},{2,3},{3,2},{4,5},{5,4},{6,7},{7,6},{8,9},{9,8},{10,11... | collective-permute-start | bytes 294920 | tf_op jit(solution)/shard_map/ppermute | solution.py:627
  28.4 1.3 %collective-permute-start.12 = (bf16[384,128]{1,0:T(8,128)(2,1)S(1)}, bf16[384,128]{1,0:T(8,128)(2,1)S(1)}, u32[]{:S(2)}, u32[]{:S(2)}) collective-permute-start(bf16[384,128]{1,0:T(8,128)(2,1)S(1)} %collective-permute-done.11.refs_2_), channel_id=1, source_target_pairs={{0,1},{1,0},{2,3},{3,2},{4,5},{5,4},{6,7},{7,6},{8,9},{9,8},{10,11... | collective-permute-start | bytes 294920 | tf_op jit(solution)/shard_map/ppermute | solution.py:627
  29.7 1.3 %collective-permute-start.15 = (bf16[384,128]{1,0:T(8,128)(2,1)S(1)}, bf16[384,128]{1,0:T(8,128)(2,1)S(1)}, u32[]{:S(2)}, u32[]{:S(2)}) collective-permute-start(bf16[384,128]{1,0:T(8,128)(2,1)S(1)} %collective-permute-done.14.refs_6_), channel_id=1, source_target_pairs={{0,1},{1,0},{2,3},{3,2},{4,5},{5,4},{6,7},{7,6},{8,9},{9,8},{10,11... | collective-permute-start | bytes 294920 | tf_op jit(solution)/shard_map/ppermute | solution.py:627

commit v24 on v23

--- a/solution.py
+++ b/solution.py
@@ -427,13 +427,9 @@
         ],
         0,
     )
-    row_out = row_out_ref[...].reshape(width, width)
-    quarters = [slice(c * tokens // 4, (c + 1) * tokens // 4) for c in range(4)]
-    normed = []
-    for at in quarters:
-        mixed = embedded[at] + dot_nt(row_context_ref[at, :], row_out)
-        mixed_ref[at, :] = mixed
-        normed.append(layer_norm(mixed).astype(bf16))
+    mixed = embedded + dot_nt(row_context_ref[...], row_out_ref[...].reshape(width, width))
+    mixed_ref[...] = mixed
+    normed = layer_norm(mixed).astype(bf16)
 
     few = 8
     groups = own // few
@@ -452,11 +448,7 @@
         weight_ref[third : third + HEAD_DIM, :] = col_qkv_ref[pl.ds(last, HEAD_DIM), :]
         weight_ref[third + HEAD_DIM : third + LANES, :] = jnp.zeros((HEAD_DIM, width), bf16)
     proj = [
-        jnp.concatenate(
-            [dot_nt(part_of, weight_ref[2 * j * LANES : 2 * (j + 1) * LANES, :]) for part_of in normed],
-            0,
-        )
-        for j in range(3)
+        dot_nt(normed, weight_ref[2 * j * LANES : 2 * (j + 1) * LANES, :]) for j in range(3)
     ]
     proj = [
         proj[j][:, k * LANES : (k + 1) * LANES] * (HEAD_DIM ** (-0.5) if (2 * j + k) % 3 == 0 else 1.0)
@@ -592,12 +584,11 @@
     local, cols = out_ref.shape[1:]
     own = cols // groups
     rest = local - LANES
-    one = (iota((LANES, LANES), 0) == iota((LANES, LANES), 1)).astype(f32).astype(bf16)
     for part in range(3):
         piece = jnp.concatenate(
             [blocks_ref[g, part * own : (part + 1) * own, :] for g in range(groups)], 0
         )
-        turned = dot_nt(one, piece).astype(bf16)
+        turned = piece.astype(f32).T.astype(bf16)
         if part < 2:
             out_ref[part, 0:LANES, :] = turned
         else:

time: 45.1 us -> 43.5 us (0.965)
  Pallas kernels: 10.7 us -> 9.1 us
    pallas_call x1, Pallas kernels: 4.54 us -> 3.02 us  [attend_columns_here(): pl.pallas_call(functools.partial(column_kernel, parts), out_shape=(jax.Sh...]
where the time goes in v24:
time: 43.5 us; the launch traced here: 43.3 us
  starting transfers between devices  13 us (30%)
  blocking collectives  12.5 us (29%)
  Pallas kernels  9.1 us (21%)
  waiting for transfers between devices  8.66 us (20%)
    ppermute x16, starting transfers between devices, pairwise(): lax.ppermute(value, ('seq', 'head'), [(i, g * parts + p) for i, (g, p) in...  13 us
    all_to_all x1, blocking collectives, fast_body(): lax.all_to_all(blocks, 'seq', split_axis=0, concat_axis=0, tiled=True)  12.5 us
    ppermute x16, waiting for transfers between devices, pairwise(): lax.ppermute(value, ('seq', 'head'), [(i, g * parts + p) for i, (g, p) in...  8.66 us
    pallas_call x1, Pallas kernels, attend_columns_here(): pl.pallas_call(functools.partial(column_kernel, parts), out_shape=(jax.Sh...  3.02 us
    pallas_call x1, Pallas kernels, make_tables(): pl.pallas_call(table_kernel, out_shape=(jax.ShapeDtypeStruct((TABLE_ROWS,...  1.87 us
    pallas_call x1, Pallas kernels, attend_rows(): pl.pallas_call(row_kernel, out_shape=(jax.ShapeDtypeStruct((2 * half * ow...  1.62 us
    pallas_call x1, Pallas kernels, attend_near(): pl.pallas_call(functools.partial(near_kernel, parts), out_shape=(jax.Shap...  1.18 us
  transfers between devices with their start and end apart: 16, of which 6 were waited for; matrix products, arithmetic and copies ran while one was open for 0% of the time, Pallas kernels for 11%

profile of v24, /device:TPU:0, one launch (start us, length us, event | category | flops | bytes accessed | tf_op | source)
XLA Modules:
  0.0 43.3 jit_solution(11302428909941714405)
XLA Ops:
  0.0 0.0 copy-start.4
  0.0 2.9 %collective-permute-start.3 = (bf16[192,768]{1,0:T(8,128)(2,1)}, bf16[192,768]{1,0:T(8,128)(2,1)S(1)}, u32[]{:S(2)}, u32[]{:S(2)}) collective-permute-start(bf16[192,768]{1,0:T(8,128)(2,1)} %refs_0_), channel_id=1, source_target_pairs={{0,2},{1,3},{2,0},{3,1},{4,6},{5,7},{6,4},{7,5},{8,10},{9,11},{10,... | collective-permute-start | bytes 884744 | tf_op jit(solution)/shard_map/ppermute | solution.py:618
  2.9 1.5 %collective-permute-start = (s32[2,256]{1,0:T(2,128)}, s32[2,256]{1,0:T(2,128)S(1)}, u32[]{:S(2)}, u32[]{:S(2)}) collective-permute-start(s32[2,256]{1,0:T(2,128)} %ids_hbm.1), channel_id=1, source_target_pairs={{0,4},{1,5},{2,6},{3,7},{4,0},{5,1},{6,2},{7,3},{8,12},{9,13},{10,... | collective-permute-start | bytes 6152 | tf_op jit(solution)/shard_map/ppermute | solution.py:618
  4.5 0.0 copy-done.4
  4.5 0.0 copy-start.2
  4.5 0.5 %collective-permute-start.1 = (s32[1,2]{1,0:T(1,128)S(1)}, s32[1,2]{1,0:T(1,128)S(1)}, u32[]{:S(2)}, u32[]{:S(2)}) collective-permute-start(s32[1,2]{1,0:T(1,128)S(1)} %bitcast.4), channel_id=1, source_target_pairs={{0,4},{1,5},{2,6},{3,7},{4,0},{5,1},{6,2},{7,3},{8,12},{9,13},{10,... | collective-permute-start | bytes 32 | tf_op jit(solution)/shard_map/ppermute | solution.py:618
  5.0 1.9 %tables.1 = (bf16[40,576]{1,0:T(8,128)(2,1)S(1)}, s32[8,256]{1,0:T(8,128)S(1)}) custom-call(s32[2,256]{1,0:T(2,128)} %ids_hbm.1, s32[2]{0:T(128)} %live_hbm.1, bf16[33,768]{1,0:T(8,128)(2,1)} %refs_8_.1, bf16[3,192,768]{2,1,0:T(8,128)(2,1)} %qkv_hbm.1), custom_call_target="tpu_custom_call" | custom-call | flops 2000000000 | bytes 884736 | tf_op jit(solution)/shard_map/tables/pallas_call | solution.py:131
  6.8 1.2 %collective-permute-done.1.live_ref = s32[1,2]{1,0:T(1,128)S(1)} collective-permute-done((s32[1,2]{1,0:T(1,128)S(1)}, s32[1,2]{1,0:T(1,128)S(1)}, u32[]{:S(2)}, u32[]{:S(2)}) %collective-permute-start.1) | collective-permute-done | bytes 40 | tf_op jit(solution)/shard_map/ppermute | solution.py:618
  8.0 0.0 collective-permute-done.ids_ref
  8.0 0.1 join_raw.1.own_ref
  8.1 1.6 %collective-permute-start.2 = (s32[8,256]{1,0:T(8,128)S(1)}, s32[8,256]{1,0:T(8,128)S(1)}, u32[]{:S(2)}, u32[]{:S(2)}) collective-permute-start(s32[8,256]{1,0:T(8,128)S(1)} %join_raw.1.own_ref), channel_id=1, source_target_pairs={{0,8},{1,9},{2,10},{3,11},{4,12},{5,13},{6,14},{7,15},{8,0},{9,1},... | collective-permute-start | bytes 24584 | tf_op jit(solution)/shard_map/ppermute | solution.py:618
  9.7 0.5 %collective-permute-start.7 = (bf16[40,576]{1,0:T(8,128)(2,1)S(1)}, bf16[40,576]{1,0:T(8,128)(2,1)S(1)}, u32[]{:S(2)}, u32[]{:S(2)}) collective-permute-start(bf16[40,576]{1,0:T(8,128)(2,1)S(1)} %get-tuple-element.30.refs_0_), channel_id=1, source_target_pairs={{0,2},{1,3},{2,0},{3,1},{4,6},{5,7},{6,4},{7,5},{8,10},{9,11},{10,... | collective-permute-start | bytes 138248 | tf_op jit(solution)/shard_map/ppermute | solution.py:618
  10.3 0.0 collective-permute-start.8
  10.3 1.5 %collective-permute-done.2.other_ref = s32[8,256]{1,0:T(8,128)S(1)} collective-permute-done((s32[8,256]{1,0:T(8,128)S(1)}, s32[8,256]{1,0:T(8,128)S(1)}, u32[]{:S(2)}, u32[]{:S(2)}) %collective-permute-start.2) | collective-permute-done | bytes 8224 | tf_op jit(solution)/shard_map/ppermute | solution.py:618
  11.8 0.0 collective-permute-done.3.refs_2_
  11.8 0.1 collective-permute-start.6
  11.9 2.6 %collective-permute-start.9 = (s32[8,256]{1,0:T(8,128)S(1)}, s32[8,256]{1,0:T(8,128)S(1)}, u32[]{:S(2)}, u32[]{:S(2)}) collective-permute-start(s32[8,256]{1,0:T(8,128)S(1)} %join.1.refs_4_.near_codes_ref), channel_id=1, source_target_pairs={{0,16},{1,17},{2,18},{3,19},{4,20},{5,21},{6,22},{7,23},{8,24},{9,... | collective-permute-start | bytes 24584 | tf_op jit(solution)/shard_map/ppermute | solution.py:618
  14.5 0.0 copy-done.2
  14.5 0.2 collective-permute-start.4
  14.7 0.0 collective-permute-done.7.refs_2_
  14.7 0.3 collective-permute-start.5
  15.1 0.0 collective-permute-done.8.refs_3_
  15.1 0.0 collective-permute-done.6.refs_1_
  15.1 1.2 %near_scores.1 = (bf16[12,128,256]{2,1,0:T(8,128)(2,1)S(1)}, bf16[64,768]{1,0:T(8,128)(2,1)S(1)}, f32[384,256]{1,0:T(8,128)S(1)}, bf16[512,256]{1,0:T(8,128)(2,1)S(1)}, bf16[128,128]{1,0:T(8,128)(2,1)S(1)}) custom-call(bf16[40,576]{1,0:T(8,128)(2,1)S(1)} %get-tuple-element.30.refs_0_, bf16[40,576]{1,0:T(8,128)(2,1)S(1)} %collective-permute-done.6.refs_1_, ...), custom_call_target="tpu_custom_call" | custom-call | flops 1000000000 | bytes 1000000 | tf_op jit(solution)/shard_map/near_scores/pallas_call | solution.py:280
  16.2 0.3 collective-permute-done.9.far_codes_ref
  16.5 1.6 %row_attention.1 = (bf16[512,768]{1,0:T(8,128)(2,1)S(1)}, bf16[128,128]{1,0:T(8,128)(2,1)S(1)}, f32[16,128]{1,0:T(8,128)S(1)}) custom-call(bf16[12,128,256]{2,1,0:T(8,128)(2,1)S(1)} %get-tuple-element.32.scores_ref, bf16[64,768]{1,0:T(8,128)(2,1)S(1)} %get-tuple-element.33.values_ref, f32[384,256]{1,0:T(8,128)S(1)} %get-tuple-element.34.near_tied_ref, ...), custom_call_target="tpu_custom_call" | custom-call | flops 3000000000 | bytes 1000000 | tf_op jit(solution)/shard_map/row_attention/pallas_call | solution.py:371
  18.1 0.0 collective-permute-done.4.refs_1_
  18.1 0.0 collective-permute-done.5.refs_3_
  18.2 0.0 copy-done.1
  18.2 0.0 copy-done.3
  18.2 0.0 copy-start
  18.2 3.0 %column_attention.1 = (bf16[384,128]{1,0:T(8,128)(2,1)S(1)}, bf16[384,128]{1,0:T(8,128)(2,1)S(1)}, f32[512,192]{1,0:T(8,128)S(1)}) custom-call(bf16[192,768]{1,0:T(8,128)(2,1)S(1)} %copy-done.2, bf16[192,768]{1,0:T(8,128)(2,1)S(1)} %collective-permute-done.4.refs_1_, bf16[192,768]{1,0:T(8,128)(2,1)S(1)} %collective-permute-done.3.refs_2_, ...), custom_call_target="tpu_custom_call" | custom-call | flops 2000000000 | bytes 1000000 | tf_op jit(solution)/shard_map/column_attention/pallas_call | solution.py:513
  21.2 0.6 %collective-permute-start.11 = (bf16[384,128]{1,0:T(8,128)(2,1)S(1)}, bf16[384,128]{1,0:T(8,128)(2,1)S(1)}, u32[]{:S(2)}, u32[]{:S(2)}) collective-permute-start(bf16[384,128]{1,0:T(8,128)(2,1)S(1)} %get-tuple-element.40.refs_0_), channel_id=1, source_target_pairs={{0,2},{1,3},{2,0},{3,1},{4,6},{5,7},{6,4},{7,5},{8,10},{9,11},{10,... | collective-permute-start | bytes 294920 | tf_op jit(solution)/shard_map/ppermute | solution.py:618
  21.8 1.5 %collective-permute-start.14 = (bf16[384,128]{1,0:T(8,128)(2,1)S(1)}, bf16[384,128]{1,0:T(8,128)(2,1)S(1)}, u32[]{:S(2)}, u32[]{:S(2)}) collective-permute-start(bf16[384,128]{1,0:T(8,128)(2,1)S(1)} %get-tuple-element.41.refs_4_), channel_id=1, source_target_pairs={{0,2},{1,3},{2,0},{3,1},{4,6},{5,7},{6,4},{7,5},{8,10},{9,11},{10,... | collective-permute-start | bytes 294920 | tf_op jit(solution)/shard_map/ppermute | solution.py:618
  23.3 0.0 collective-permute-start.10
  23.3 0.5 %collective-permute-start.13 = (bf16[384,128]{1,0:T(8,128)(2,1)S(1)}, bf16[384,128]{1,0:T(8,128)(2,1)S(1)}, u32[]{:S(2)}, u32[]{:S(2)}) collective-permute-start(bf16[384,128]{1,0:T(8,128)(2,1)S(1)} %get-tuple-element.41.refs_4_), channel_id=1, source_target_pairs={{0,1},{1,0},{2,3},{3,2},{4,5},{5,4},{6,7},{7,6},{8,9},{9,8},{10,11... | collective-permute-start | bytes 294920 | tf_op jit(solution)/shard_map/ppermute | solution.py:618
  23.8 3.1 %collective-permute-done.11.refs_2_ = bf16[384,128]{1,0:T(8,128)(2,1)S(1)} collective-permute-done((bf16[384,128]{1,0:T(8,128)(2,1)S(1)}, bf16[384,128]{1,0:T(8,128)(2,1)S(1)}, u32[]{:S(2)}, u32[]{:S(2)}) %collective-permute-start.11) | collective-permute-done | bytes 98336 | tf_op jit(solution)/shard_map/ppermute | solution.py:618
  26.9 0.0 collective-permute-start.12
  26.9 1.3 %collective-permute-done.14.refs_6_ = bf16[384,128]{1,0:T(8,128)(2,1)S(1)} collective-permute-done((bf16[384,128]{1,0:T(8,128)(2,1)S(1)}, bf16[384,128]{1,0:T(8,128)(2,1)S(1)}, u32[]{:S(2)}, u32[]{:S(2)}) %collective-permute-start.14) | collective-permute-done | bytes 98336 | tf_op jit(solution)/shard_map/ppermute | solution.py:618
  28.2 0.0 collective-permute-start.15
  28.2 0.0 collective-permute-done.10.refs_1_
  28.2 0.0 collective-permute-done.13.refs_5_
  28.2 0.0 collective-permute-done.12.refs_3_
  28.2 1.3 %collective-permute-done.15.refs_7_ = bf16[384,128]{1,0:T(8,128)(2,1)S(1)} collective-permute-done((bf16[384,128]{1,0:T(8,128)(2,1)S(1)}, bf16[384,128]{1,0:T(8,128)(2,1)S(1)}, u32[]{:S(2)}, u32[]{:S(2)}) %collective-permute-start.15) | collective-permute-done | bytes 98336 | tf_op jit(solution)/shard_map/ppermute | solution.py:618
  29.5 0.0 copy-done
  29.5 0.5 %finish.1 = bf16[8,96,128]{2,1,0:T(8,128)(2,1)S(1)} custom-call(bf16[384,128]{1,0:T(8,128)(2,1)S(1)} %get-tuple-element.40.refs_0_, bf16[384,128]{1,0:T(8,128)(2,1)S(1)} %collective-permute-done.10.refs_1_, bf16[384,128]{1,0:T(8,128)(2,1)S(1)} %collective-permute-done.11.refs_2_, bf16[384,128]{1,0:T(8,128)(2,1)S(1)} %collective-permute-done.12.refs_3_, ...), custom_call_target="tpu_custom_call" | custom-call | tf_op jit(solution)/shard_map/finish/pallas_call | solution.py:573
  30.0 12.5 %all_to_all.5.blocks_ref = bf16[8,96,128]{2,1,0:T(8,128)(2,1)S(1)} all-to-all(bf16[8,96,128]{2,1,0:T(8,128)(2,1)S(1)} %finish.1), channel_id=1, replica_groups=mesh['seq'=8,'head'=4] {'seq'}, dimensions={0} | all-to-all | bytes 393216 | tf_op jit(solution)/shard_map/all_to_all | solution.py:668
  42.5 0.8 %order.1 = bf16[2,192,256]{2,1,0:T(8,128)(2,1)} custom-call(bf16[8,96,128]{2,1,0:T(8,128)(2,1)S(1)} %all_to_all.5.blocks_ref), custom_call_target="tpu_custom_call" | custom-call | tf_op jit(solution)/shard_map/order/pallas_call | solution.py:600
  (3 shorter events, 0.0 us)
Async XLA Ops:
  0.0 4.5 %copy-start.4 = (s32[2]{0:T(128)S(1)}, s32[2]{0:T(128)}, u32[]{:S(2)}) copy-start(s32[2]{0:T(128)} %live_hbm.1) | copy-start | bytes 28
  0.0 11.8 %collective-permute-start.3 = (bf16[192,768]{1,0:T(8,128)(2,1)}, bf16[192,768]{1,0:T(8,128)(2,1)S(1)}, u32[]{:S(2)}, u32[]{:S(2)}) collective-permute-start(bf16[192,768]{1,0:T(8,128)(2,1)} %refs_0_), channel_id=1, source_target_pairs={{0,2},{1,3},{2,0},{3,1},{4,6},{5,7},{6,4},{7,5},{8,10},{9,11},{10,... | collective-permute-start | bytes 884744 | tf_op jit(solution)/shard_map/ppermute | solution.py:618
  2.9 5.1 %collective-permute-start = (s32[2,256]{1,0:T(2,128)}, s32[2,256]{1,0:T(2,128)S(1)}, u32[]{:S(2)}, u32[]{:S(2)}) collective-permute-start(s32[2,256]{1,0:T(2,128)} %ids_hbm.1), channel_id=1, source_target_pairs={{0,4},{1,5},{2,6},{3,7},{4,0},{5,1},{6,2},{7,3},{8,12},{9,13},{10,... | collective-permute-start | bytes 6152 | tf_op jit(solution)/shard_map/ppermute | solution.py:618
  4.5 10.1 %copy-start.2 = (bf16[192,768]{1,0:T(8,128)(2,1)S(1)}, bf16[192,768]{1,0:T(8,128)(2,1)}, u32[]{:S(2)}) copy-start(bf16[192,768]{1,0:T(8,128)(2,1)} %refs_0_) | copy-start | bytes 884740
  4.5 3.5 %collective-permute-start.1 = (s32[1,2]{1,0:T(1,128)S(1)}, s32[1,2]{1,0:T(1,128)S(1)}, u32[]{:S(2)}, u32[]{:S(2)}) collective-permute-start(s32[1,2]{1,0:T(1,128)S(1)} %bitcast.4), channel_id=1, source_target_pairs={{0,4},{1,5},{2,6},{3,7},{4,0},{5,1},{6,2},{7,3},{8,12},{9,13},{10,... | collective-permute-start | bytes 32 | tf_op jit(solution)/shard_map/ppermute | solution.py:618
  8.1 3.7 %collective-permute-start.2 = (s32[8,256]{1,0:T(8,128)S(1)}, s32[8,256]{1,0:T(8,128)S(1)}, u32[]{:S(2)}, u32[]{:S(2)}) collective-permute-start(s32[8,256]{1,0:T(8,128)S(1)} %join_raw.1.own_ref), channel_id=1, source_target_pairs={{0,8},{1,9},{2,10},{3,11},{4,12},{5,13},{6,14},{7,15},{8,0},{9,1},... | collective-permute-start | bytes 24584 | tf_op jit(solution)/shard_map/ppermute | solution.py:618
  9.7 5.0 %collective-permute-start.7 = (bf16[40,576]{1,0:T(8,128)(2,1)S(1)}, bf16[40,576]{1,0:T(8,128)(2,1)S(1)}, u32[]{:S(2)}, u32[]{:S(2)}) collective-permute-start(bf16[40,576]{1,0:T(8,128)(2,1)S(1)} %get-tuple-element.30.refs_0_), channel_id=1, source_target_pairs={{0,2},{1,3},{2,0},{3,1},{4,6},{5,7},{6,4},{7,5},{8,10},{9,11},{10,... | collective-permute-start | bytes 138248 | tf_op jit(solution)/shard_map/ppermute | solution.py:618
  10.3 4.8 %collective-permute-start.8 = (bf16[40,576]{1,0:T(8,128)(2,1)S(1)}, bf16[40,576]{1,0:T(8,128)(2,1)S(1)}, u32[]{:S(2)}, u32[]{:S(2)}) collective-permute-start(bf16[40,576]{1,0:T(8,128)(2,1)S(1)} %get-tuple-element.30.refs_0_), channel_id=1, source_target_pairs={{0,3},{1,2},{2,1},{3,0},{4,7},{5,6},{6,5},{7,4},{8,11},{9,10},{10,... | collective-permute-start | bytes 138248 | tf_op jit(solution)/shard_map/ppermute | solution.py:618
  11.8 3.3 %collective-permute-start.6 = (bf16[40,576]{1,0:T(8,128)(2,1)S(1)}, bf16[40,576]{1,0:T(8,128)(2,1)S(1)}, u32[]{:S(2)}, u32[]{:S(2)}) collective-permute-start(bf16[40,576]{1,0:T(8,128)(2,1)S(1)} %get-tuple-element.30.refs_0_), channel_id=1, source_target_pairs={{0,1},{1,0},{2,3},{3,2},{4,5},{5,4},{6,7},{7,6},{8,9},{9,8},{10,11... | collective-permute-start | bytes 138248 | tf_op jit(solution)/shard_map/ppermute | solution.py:618
  11.9 4.6 %collective-permute-start.9 = (s32[8,256]{1,0:T(8,128)S(1)}, s32[8,256]{1,0:T(8,128)S(1)}, u32[]{:S(2)}, u32[]{:S(2)}) collective-permute-start(s32[8,256]{1,0:T(8,128)S(1)} %join.1.refs_4_.near_codes_ref), channel_id=1, source_target_pairs={{0,16},{1,17},{2,18},{3,19},{4,20},{5,21},{6,22},{7,23},{8,24},{9,... | collective-permute-start | bytes 24584 | tf_op jit(solution)/shard_map/ppermute | solution.py:618
  14.5 3.6 %collective-permute-start.4 = (bf16[192,768]{1,0:T(8,128)(2,1)S(1)}, bf16[192,768]{1,0:T(8,128)(2,1)S(1)}, u32[]{:S(2)}, u32[]{:S(2)}) collective-permute-start(bf16[192,768]{1,0:T(8,128)(2,1)S(1)} %copy-done.2), channel_id=1, source_target_pairs={{0,1},{1,0},{2,3},{3,2},{4,5},{5,4},{6,7},{7,6},{8,9},{9,8},{10,11... | collective-permute-start | bytes 884744 | tf_op jit(solution)/shard_map/ppermute | solution.py:618
  14.7 3.4 %collective-permute-start.5 = (bf16[192,768]{1,0:T(8,128)(2,1)S(1)}, bf16[192,768]{1,0:T(8,128)(2,1)S(1)}, u32[]{:S(2)}, u32[]{:S(2)}) collective-permute-start(bf16[192,768]{1,0:T(8,128)(2,1)S(1)} %collective-permute-done.3.refs_2_), channel_id=1, source_target_pairs={{0,1},{1,0},{2,3},{3,2},{4,5},{5,4},{6,7},{7,6},{8,9},{9,8},{10,11... | collective-permute-start | bytes 884744 | tf_op jit(solution)/shard_map/ppermute | solution.py:618
  16.5 1.7 %copy-start.1 = (bf16[3,192,768]{2,1,0:T(8,128)(2,1)S(1)}, bf16[3,192,768]{2,1,0:T(8,128)(2,1)}, u32[]{:S(2)}) copy-start(bf16[3,192,768]{2,1,0:T(8,128)(2,1)} %param.12) | copy-start | bytes 2654212
  16.5 1.7 %copy-start.3 = (bf16[33,768]{1,0:T(8,128)(2,1)S(1)}, bf16[33,768]{1,0:T(8,128)(2,1)}, u32[]{:S(2)}) copy-start(bf16[33,768]{1,0:T(8,128)(2,1)} %refs_8_.1) | copy-start | bytes 152068
  18.2 11.4 %copy-start = (bf16[192,768]{1,0:T(8,128)(2,1)S(1)}, bf16[192,768]{1,0:T(8,128)(2,1)}, u32[]{:S(2)}) copy-start(bf16[192,768]{1,0:T(8,128)(2,1)} %refs_9_.1) | copy-start | bytes 884740
  21.2 5.7 %collective-permute-start.11 = (bf16[384,128]{1,0:T(8,128)(2,1)S(1)}, bf16[384,128]{1,0:T(8,128)(2,1)S(1)}, u32[]{:S(2)}, u32[]{:S(2)}) collective-permute-start(bf16[384,128]{1,0:T(8,128)(2,1)S(1)} %get-tuple-element.40.refs_0_), channel_id=1, source_target_pairs={{0,2},{1,3},{2,0},{3,1},{4,6},{5,7},{6,4},{7,5},{8,10},{9,11},{10,... | collective-permute-start | bytes 294920 | tf_op jit(solution)/shard_map/ppermute | solution.py:618
  21.8 6.4 %collective-permute-start.14 = (bf16[384,128]{1,0:T(8,128)(2,1)S(1)}, bf16[384,128]{1,0:T(8,128)(2,1)S(1)}, u32[]{:S(2)}, u32[]{:S(2)}) collective-permute-start(bf16[384,128]{1,0:T(8,128)(2,1)S(1)} %get-tuple-element.41.refs_4_), channel_id=1, source_target_pairs={{0,2},{1,3},{2,0},{3,1},{4,6},{5,7},{6,4},{7,5},{8,10},{9,11},{10,... | collective-permute-start | bytes 294920 | tf_op jit(solution)/shard_map/ppermute | solution.py:618
  23.3 4.9 %collective-permute-start.10 = (bf16[384,128]{1,0:T(8,128)(2,1)S(1)}, bf16[384,128]{1,0:T(8,128)(2,1)S(1)}, u32[]{:S(2)}, u32[]{:S(2)}) collective-permute-start(bf16[384,128]{1,0:T(8,128)(2,1)S(1)} %get-tuple-element.40.refs_0_), channel_id=1, source_target_pairs={{0,1},{1,0},{2,3},{3,2},{4,5},{5,4},{6,7},{7,6},{8,9},{9,8},{10,11... | collective-permute-start | bytes 294920 | tf_op jit(solution)/shard_map/ppermute | solution.py:618
  23.3 4.9 %collective-permute-start.13 = (bf16[384,128]{1,0:T(8,128)(2,1)S(1)}, bf16[384,128]{1,0:T(8,128)(2,1)S(1)}, u32[]{:S(2)}, u32[]{:S(2)}) collective-permute-start(bf16[384,128]{1,0:T(8,128)(2,1)S(1)} %get-tuple-element.41.refs_4_), channel_id=1, source_target_pairs={{0,1},{1,0},{2,3},{3,2},{4,5},{5,4},{6,7},{7,6},{8,9},{9,8},{10,11... | collective-permute-start | bytes 294920 | tf_op jit(solution)/shard_map/ppermute | solution.py:618
  26.9 1.3 %collective-permute-start.12 = (bf16[384,128]{1,0:T(8,128)(2,1)S(1)}, bf16[384,128]{1,0:T(8,128)(2,1)S(1)}, u32[]{:S(2)}, u32[]{:S(2)}) collective-permute-start(bf16[384,128]{1,0:T(8,128)(2,1)S(1)} %collective-permute-done.11.refs_2_), channel_id=1, source_target_pairs={{0,1},{1,0},{2,3},{3,2},{4,5},{5,4},{6,7},{7,6},{8,9},{9,8},{10,11... | collective-permute-start | bytes 294920 | tf_op jit(solution)/shard_map/ppermute | solution.py:618
  28.2 1.3 %collective-permute-start.15 = (bf16[384,128]{1,0:T(8,128)(2,1)S(1)}, bf16[384,128]{1,0:T(8,128)(2,1)S(1)}, u32[]{:S(2)}, u32[]{:S(2)}) collective-permute-start(bf16[384,128]{1,0:T(8,128)(2,1)S(1)} %collective-permute-done.14.refs_6_), channel_id=1, source_target_pairs={{0,1},{1,0},{2,3},{3,2},{4,5},{5,4},{6,7},{7,6},{8,9},{9,8},{10,11... | collective-permute-start | bytes 294920 | tf_op jit(solution)/shard_map/ppermute | solution.py:618

commit v25 on v24

--- a/solution.py
+++ b/solution.py
@@ -509,12 +509,10 @@
     parts = len(row_outs)
     tokens, width = row_context.shape
     local = width // parts
-    half = tokens // 2 * local // LANES
     return pl.pallas_call(
         functools.partial(column_kernel, parts),
         out_shape=(
-            jax.ShapeDtypeStruct((half, LANES), bf16),
-            jax.ShapeDtypeStruct((half, LANES), bf16),
+            jax.ShapeDtypeStruct((tokens * local // LANES, LANES), bf16),
             jax.ShapeDtypeStruct((tokens, local), f32),
         ),
         scratch_shapes=[
@@ -530,12 +528,12 @@
 
 
 def finish_kernel(parts, groups, *refs):
-    context_refs = [refs[:parts], refs[parts : 2 * parts]]
-    mixed_ref, col_out_ref, out_ref, context_ref = refs[2 * parts :]
+    context_refs = [refs[:parts]]
+    mixed_ref, col_out_ref, out_ref, context_ref = refs[parts:]
     tokens, local = mixed_ref.shape
     group = lax.axis_index("seq")
     part = lax.axis_index("head")
-    starts = [0, context_refs[0][0].shape[0]]
+    starts = [0]
     for start, some_refs in zip(starts, context_refs):
         for p in range(parts):
             context_ref[part ^ p, start : start + some_refs[p].shape[0], :] = some_refs[p][...]
@@ -576,7 +574,7 @@
         scratch_shapes=[pltpu.VMEM((parts, tokens * local // LANES, LANES), bf16)],
         compiler_params=pltpu.CompilerParams(vmem_limit_bytes=LARGE_VMEM),
         name="finish",
-    )(*contexts[0], *contexts[1], mixed, col_out)
+    )(*contexts[0], mixed, col_out)
 
 
 def order_kernel(blocks_ref, out_ref):

time: 43.5 us -> 43.4 us (level)
  waiting for transfers between devices: 8.66 us -> 10.8 us
  starting transfers between devices: 13 us -> 11 us
    ppermute x16 -> x13, waiting for transfers between devices: 8.66 us -> 10.8 us  [pairwise(): lax.ppermute(value, ('seq', 'head'), [(i, g * parts + p) for i, (g, p) in...]
    ppermute x16 -> x13, starting transfers between devices: 13 us -> 11 us  [pairwise(): lax.ppermute(value, ('seq', 'head'), [(i, g * parts + p) for i, (g, p) in...]
  transfers between devices with their start and end apart: 16 -> 13, of which waited for: 6 -> 5; matrix products, arithmetic and copies ran while one was open for 0% -> 0% of each run, Pallas kernels for 11% -> 11%
where the time goes in v25:
time: 43.4 us; the launch traced here: 43.3 us
  blocking collectives  12.3 us (28%)
  starting transfers between devices  11 us (25%)
  waiting for transfers between devices  10.8 us (25%)
  Pallas kernels  9.09 us (21%)
    all_to_all x1, blocking collectives, fast_body(): lax.all_to_all(blocks, 'seq', split_axis=0, concat_axis=0, tiled=True)  12.3 us
    ppermute x13, starting transfers between devices, pairwise(): lax.ppermute(value, ('seq', 'head'), [(i, g * parts + p) for i, (g, p) in...  11 us
    ppermute x13, waiting for transfers between devices, pairwise(): lax.ppermute(value, ('seq', 'head'), [(i, g * parts + p) for i, (g, p) in...  10.8 us
    pallas_call x1, Pallas kernels, attend_columns_here(): pl.pallas_call(functools.partial(column_kernel, parts), out_shape=(jax.Sh...  3.03 us
    pallas_call x1, Pallas kernels, make_tables(): pl.pallas_call(table_kernel, out_shape=(jax.ShapeDtypeStruct((TABLE_ROWS,...  1.87 us
    pallas_call x1, Pallas kernels, attend_rows(): pl.pallas_call(row_kernel, out_shape=(jax.ShapeDtypeStruct((2 * half * ow...  1.62 us
    pallas_call x1, Pallas kernels, attend_near(): pl.pallas_call(functools.partial(near_kernel, parts), out_shape=(jax.Shap...  1.18 us
  transfers between devices with their start and end apart: 13, of which 5 were waited for; matrix products, arithmetic and copies ran while one was open for 0% of the time, Pallas kernels for 11%

profile of v25, /device:TPU:0, one launch (start us, length us, event | category | flops | bytes accessed | tf_op | source)
XLA Modules:
  0.0 43.3 jit_solution(5741919560978577944)
XLA Ops:
  0.0 0.0 copy-start.4
  0.0 2.9 %collective-permute-start.3 = (bf16[192,768]{1,0:T(8,128)(2,1)}, bf16[192,768]{1,0:T(8,128)(2,1)S(1)}, u32[]{:S(2)}, u32[]{:S(2)}) collective-permute-start(bf16[192,768]{1,0:T(8,128)(2,1)} %refs_0_), channel_id=1, source_target_pairs={{0,2},{1,3},{2,0},{3,1},{4,6},{5,7},{6,4},{7,5},{8,10},{9,11},{10,... | collective-permute-start | bytes 884744 | tf_op jit(solution)/shard_map/ppermute | solution.py:616
  2.9 1.5 %collective-permute-start = (s32[2,256]{1,0:T(2,128)}, s32[2,256]{1,0:T(2,128)S(1)}, u32[]{:S(2)}, u32[]{:S(2)}) collective-permute-start(s32[2,256]{1,0:T(2,128)} %ids_hbm.1), channel_id=1, source_target_pairs={{0,4},{1,5},{2,6},{3,7},{4,0},{5,1},{6,2},{7,3},{8,12},{9,13},{10,... | collective-permute-start | bytes 6152 | tf_op jit(solution)/shard_map/ppermute | solution.py:616
  4.5 0.0 copy-done.4
  4.5 0.0 copy-start.2
  4.5 0.5 %collective-permute-start.1 = (s32[1,2]{1,0:T(1,128)S(1)}, s32[1,2]{1,0:T(1,128)S(1)}, u32[]{:S(2)}, u32[]{:S(2)}) collective-permute-start(s32[1,2]{1,0:T(1,128)S(1)} %bitcast.4), channel_id=1, source_target_pairs={{0,4},{1,5},{2,6},{3,7},{4,0},{5,1},{6,2},{7,3},{8,12},{9,13},{10,... | collective-permute-start | bytes 32 | tf_op jit(solution)/shard_map/ppermute | solution.py:616
  5.0 1.9 %tables.1 = (bf16[40,576]{1,0:T(8,128)(2,1)S(1)}, s32[8,256]{1,0:T(8,128)S(1)}) custom-call(s32[2,256]{1,0:T(2,128)} %ids_hbm.1, s32[2]{0:T(128)} %live_hbm.1, bf16[33,768]{1,0:T(8,128)(2,1)} %refs_8_.1, bf16[3,192,768]{2,1,0:T(8,128)(2,1)} %qkv_hbm.1), custom_call_target="tpu_custom_call" | custom-call | flops 2000000000 | bytes 884736 | tf_op jit(solution)/shard_map/tables/pallas_call | solution.py:131
  6.8 1.2 %collective-permute-done.1.live_ref = s32[1,2]{1,0:T(1,128)S(1)} collective-permute-done((s32[1,2]{1,0:T(1,128)S(1)}, s32[1,2]{1,0:T(1,128)S(1)}, u32[]{:S(2)}, u32[]{:S(2)}) %collective-permute-start.1) | collective-permute-done | bytes 40 | tf_op jit(solution)/shard_map/ppermute | solution.py:616
  8.0 0.0 collective-permute-done.ids_ref
  8.0 0.1 join_raw.1.own_ref
  8.1 1.6 %collective-permute-start.2 = (s32[8,256]{1,0:T(8,128)S(1)}, s32[8,256]{1,0:T(8,128)S(1)}, u32[]{:S(2)}, u32[]{:S(2)}) collective-permute-start(s32[8,256]{1,0:T(8,128)S(1)} %join_raw.1.own_ref), channel_id=1, source_target_pairs={{0,8},{1,9},{2,10},{3,11},{4,12},{5,13},{6,14},{7,15},{8,0},{9,1},... | collective-permute-start | bytes 24584 | tf_op jit(solution)/shard_map/ppermute | solution.py:616
  9.7 0.5 %collective-permute-start.7 = (bf16[40,576]{1,0:T(8,128)(2,1)S(1)}, bf16[40,576]{1,0:T(8,128)(2,1)S(1)}, u32[]{:S(2)}, u32[]{:S(2)}) collective-permute-start(bf16[40,576]{1,0:T(8,128)(2,1)S(1)} %get-tuple-element.29.refs_0_), channel_id=1, source_target_pairs={{0,2},{1,3},{2,0},{3,1},{4,6},{5,7},{6,4},{7,5},{8,10},{9,11},{10,... | collective-permute-start | bytes 138248 | tf_op jit(solution)/shard_map/ppermute | solution.py:616
  10.3 0.0 collective-permute-start.8
  10.3 1.5 %collective-permute-done.2.other_ref = s32[8,256]{1,0:T(8,128)S(1)} collective-permute-done((s32[8,256]{1,0:T(8,128)S(1)}, s32[8,256]{1,0:T(8,128)S(1)}, u32[]{:S(2)}, u32[]{:S(2)}) %collective-permute-start.2) | collective-permute-done | bytes 8224 | tf_op jit(solution)/shard_map/ppermute | solution.py:616
  11.8 0.0 collective-permute-done.3.refs_2_
  11.8 0.1 collective-permute-start.6
  11.9 2.6 %collective-permute-start.9 = (s32[8,256]{1,0:T(8,128)S(1)}, s32[8,256]{1,0:T(8,128)S(1)}, u32[]{:S(2)}, u32[]{:S(2)}) collective-permute-start(s32[8,256]{1,0:T(8,128)S(1)} %join.1.refs_4_.near_codes_ref), channel_id=1, source_target_pairs={{0,16},{1,17},{2,18},{3,19},{4,20},{5,21},{6,22},{7,23},{8,24},{9,... | collective-permute-start | bytes 24584 | tf_op jit(solution)/shard_map/ppermute | solution.py:616
  14.5 0.0 copy-done.2
  14.5 0.2 collective-permute-start.4
  14.7 0.0 collective-permute-done.7.refs_2_
  14.7 0.3 collective-permute-start.5
  15.1 0.0 collective-permute-done.8.refs_3_
  15.1 0.0 collective-permute-done.6.refs_1_
  15.1 1.2 %near_scores.1 = (bf16[12,128,256]{2,1,0:T(8,128)(2,1)S(1)}, bf16[64,768]{1,0:T(8,128)(2,1)S(1)}, f32[384,256]{1,0:T(8,128)S(1)}, bf16[512,256]{1,0:T(8,128)(2,1)S(1)}, bf16[128,128]{1,0:T(8,128)(2,1)S(1)}) custom-call(bf16[40,576]{1,0:T(8,128)(2,1)S(1)} %get-tuple-element.29.refs_0_, bf16[40,576]{1,0:T(8,128)(2,1)S(1)} %collective-permute-done.6.refs_1_, ...), custom_call_target="tpu_custom_call" | custom-call | flops 1000000000 | bytes 1000000 | tf_op jit(solution)/shard_map/near_scores/pallas_call | solution.py:280
  16.2 0.3 collective-permute-done.9.far_codes_ref
  16.5 0.0 copy-start.1
  16.5 0.0 copy-start.3
  16.5 1.6 %row_attention.1 = (bf16[512,768]{1,0:T(8,128)(2,1)S(1)}, bf16[128,128]{1,0:T(8,128)(2,1)S(1)}, f32[16,128]{1,0:T(8,128)S(1)}) custom-call(bf16[12,128,256]{2,1,0:T(8,128)(2,1)S(1)} %get-tuple-element.31.scores_ref, bf16[64,768]{1,0:T(8,128)(2,1)S(1)} %get-tuple-element.32.values_ref, f32[384,256]{1,0:T(8,128)S(1)} %get-tuple-element.33.near_tied_ref, ...), custom_call_target="tpu_custom_call" | custom-call | flops 3000000000 | bytes 1000000 | tf_op jit(solution)/shard_map/row_attention/pallas_call | solution.py:371
  18.1 0.0 collective-permute-done.4.refs_1_
  18.1 0.0 collective-permute-done.5.refs_3_
  18.2 0.0 copy-done.1
  18.2 0.0 copy-done.3
  18.2 0.0 copy-start
  18.2 3.0 %column_attention.1 = (bf16[768,128]{1,0:T(8,128)(2,1)S(1)}, f32[512,192]{1,0:T(8,128)S(1)}) custom-call(bf16[192,768]{1,0:T(8,128)(2,1)S(1)} %copy-done.2, bf16[192,768]{1,0:T(8,128)(2,1)S(1)} %collective-permute-done.4.refs_1_, bf16[192,768]{1,0:T(8,128)(2,1)S(1)} %collective-permute-done.3.refs_2_, bf16[192,768]{1,0:T(8,128)(2,1)S(1)} %collective-permute-done.5.refs_3_, ...), custom_call_target="tpu_custom_call" | custom-call | flops 2000000000 | bytes 1000000 | tf_op jit(solution)/shard_map/column_attention/pallas_call | solution.py:512
  21.2 0.6 %collective-permute-start.11 = (bf16[768,128]{1,0:T(8,128)(2,1)S(1)}, bf16[768,128]{1,0:T(8,128)(2,1)S(1)}, u32[]{:S(2)}, u32[]{:S(2)}) collective-permute-start(bf16[768,128]{1,0:T(8,128)(2,1)S(1)} %get-tuple-element.39.refs_0_), channel_id=1, source_target_pairs={{0,2},{1,3},{2,0},{3,1},{4,6},{5,7},{6,4},{7,5},{8,10},{9,11},{10,... | collective-permute-start | bytes 589832 | tf_op jit(solution)/shard_map/ppermute | solution.py:616
  21.8 0.0 collective-permute-start.10
  21.8 6.4 %collective-permute-done.11.refs_2_ = bf16[768,128]{1,0:T(8,128)(2,1)S(1)} collective-permute-done((bf16[768,128]{1,0:T(8,128)(2,1)S(1)}, bf16[768,128]{1,0:T(8,128)(2,1)S(1)}, u32[]{:S(2)}, u32[]{:S(2)}) %collective-permute-start.11) | collective-permute-done | bytes 196640 | tf_op jit(solution)/shard_map/ppermute | solution.py:616
  28.2 0.0 collective-permute-start.12
  28.2 0.0 collective-permute-done.10.refs_1_
  28.2 1.4 %collective-permute-done.12.refs_3_ = bf16[768,128]{1,0:T(8,128)(2,1)S(1)} collective-permute-done((bf16[768,128]{1,0:T(8,128)(2,1)S(1)}, bf16[768,128]{1,0:T(8,128)(2,1)S(1)}, u32[]{:S(2)}, u32[]{:S(2)}) %collective-permute-start.12) | collective-permute-done | bytes 196640 | tf_op jit(solution)/shard_map/ppermute | solution.py:616
  29.7 0.0 copy-done
  29.7 0.5 %finish.1 = bf16[8,96,128]{2,1,0:T(8,128)(2,1)S(1)} custom-call(bf16[768,128]{1,0:T(8,128)(2,1)S(1)} %get-tuple-element.39.refs_0_, bf16[768,128]{1,0:T(8,128)(2,1)S(1)} %collective-permute-done.10.refs_1_, bf16[768,128]{1,0:T(8,128)(2,1)S(1)} %collective-permute-done.11.refs_2_, bf16[768,128]{1,0:T(8,128)(2,1)S(1)} %collective-permute-done.12.refs_3_, ...), custom_call_target="tpu_custom_call" | custom-call | tf_op jit(solution)/shard_map/finish/pallas_call | solution.py:571
  30.2 12.3 %all_to_all.5.blocks_ref = bf16[8,96,128]{2,1,0:T(8,128)(2,1)S(1)} all-to-all(bf16[8,96,128]{2,1,0:T(8,128)(2,1)S(1)} %finish.1), channel_id=1, replica_groups=mesh['seq'=8,'head'=4] {'seq'}, dimensions={0} | all-to-all | bytes 393216 | tf_op jit(solution)/shard_map/all_to_all | solution.py:666
  42.5 0.8 %order.1 = bf16[2,192,256]{2,1,0:T(8,128)(2,1)} custom-call(bf16[8,96,128]{2,1,0:T(8,128)(2,1)S(1)} %all_to_all.5.blocks_ref), custom_call_target="tpu_custom_call" | custom-call | tf_op jit(solution)/shard_map/order/pallas_call | solution.py:598
  (1 shorter events, 0.0 us)
Async XLA Ops:
  0.0 4.5 %copy-start.4 = (s32[2]{0:T(128)S(1)}, s32[2]{0:T(128)}, u32[]{:S(2)}) copy-start(s32[2]{0:T(128)} %live_hbm.1) | copy-start | bytes 28
  0.0 11.8 %collective-permute-start.3 = (bf16[192,768]{1,0:T(8,128)(2,1)}, bf16[192,768]{1,0:T(8,128)(2,1)S(1)}, u32[]{:S(2)}, u32[]{:S(2)}) collective-permute-start(bf16[192,768]{1,0:T(8,128)(2,1)} %refs_0_), channel_id=1, source_target_pairs={{0,2},{1,3},{2,0},{3,1},{4,6},{5,7},{6,4},{7,5},{8,10},{9,11},{10,... | collective-permute-start | bytes 884744 | tf_op jit(solution)/shard_map/ppermute | solution.py:616
  2.9 5.1 %collective-permute-start = (s32[2,256]{1,0:T(2,128)}, s32[2,256]{1,0:T(2,128)S(1)}, u32[]{:S(2)}, u32[]{:S(2)}) collective-permute-start(s32[2,256]{1,0:T(2,128)} %ids_hbm.1), channel_id=1, source_target_pairs={{0,4},{1,5},{2,6},{3,7},{4,0},{5,1},{6,2},{7,3},{8,12},{9,13},{10,... | collective-permute-start | bytes 6152 | tf_op jit(solution)/shard_map/ppermute | solution.py:616
  4.5 10.1 %copy-start.2 = (bf16[192,768]{1,0:T(8,128)(2,1)S(1)}, bf16[192,768]{1,0:T(8,128)(2,1)}, u32[]{:S(2)}) copy-start(bf16[192,768]{1,0:T(8,128)(2,1)} %refs_0_) | copy-start | bytes 884740
  4.5 3.5 %collective-permute-start.1 = (s32[1,2]{1,0:T(1,128)S(1)}, s32[1,2]{1,0:T(1,128)S(1)}, u32[]{:S(2)}, u32[]{:S(2)}) collective-permute-start(s32[1,2]{1,0:T(1,128)S(1)} %bitcast.4), channel_id=1, source_target_pairs={{0,4},{1,5},{2,6},{3,7},{4,0},{5,1},{6,2},{7,3},{8,12},{9,13},{10,... | collective-permute-start | bytes 32 | tf_op jit(solution)/shard_map/ppermute | solution.py:616
  8.1 3.7 %collective-permute-start.2 = (s32[8,256]{1,0:T(8,128)S(1)}, s32[8,256]{1,0:T(8,128)S(1)}, u32[]{:S(2)}, u32[]{:S(2)}) collective-permute-start(s32[8,256]{1,0:T(8,128)S(1)} %join_raw.1.own_ref), channel_id=1, source_target_pairs={{0,8},{1,9},{2,10},{3,11},{4,12},{5,13},{6,14},{7,15},{8,0},{9,1},... | collective-permute-start | bytes 24584 | tf_op jit(solution)/shard_map/ppermute | solution.py:616
  9.7 5.0 %collective-permute-start.7 = (bf16[40,576]{1,0:T(8,128)(2,1)S(1)}, bf16[40,576]{1,0:T(8,128)(2,1)S(1)}, u32[]{:S(2)}, u32[]{:S(2)}) collective-permute-start(bf16[40,576]{1,0:T(8,128)(2,1)S(1)} %get-tuple-element.29.refs_0_), channel_id=1, source_target_pairs={{0,2},{1,3},{2,0},{3,1},{4,6},{5,7},{6,4},{7,5},{8,10},{9,11},{10,... | collective-permute-start | bytes 138248 | tf_op jit(solution)/shard_map/ppermute | solution.py:616
  10.3 4.8 %collective-permute-start.8 = (bf16[40,576]{1,0:T(8,128)(2,1)S(1)}, bf16[40,576]{1,0:T(8,128)(2,1)S(1)}, u32[]{:S(2)}, u32[]{:S(2)}) collective-permute-start(bf16[40,576]{1,0:T(8,128)(2,1)S(1)} %get-tuple-element.29.refs_0_), channel_id=1, source_target_pairs={{0,3},{1,2},{2,1},{3,0},{4,7},{5,6},{6,5},{7,4},{8,11},{9,10},{10,... | collective-permute-start | bytes 138248 | tf_op jit(solution)/shard_map/ppermute | solution.py:616
  11.8 3.3 %collective-permute-start.6 = (bf16[40,576]{1,0:T(8,128)(2,1)S(1)}, bf16[40,576]{1,0:T(8,128)(2,1)S(1)}, u32[]{:S(2)}, u32[]{:S(2)}) collective-permute-start(bf16[40,576]{1,0:T(8,128)(2,1)S(1)} %get-tuple-element.29.refs_0_), channel_id=1, source_target_pairs={{0,1},{1,0},{2,3},{3,2},{4,5},{5,4},{6,7},{7,6},{8,9},{9,8},{10,11... | collective-permute-start | bytes 138248 | tf_op jit(solution)/shard_map/ppermute | solution.py:616
  11.9 4.6 %collective-permute-start.9 = (s32[8,256]{1,0:T(8,128)S(1)}, s32[8,256]{1,0:T(8,128)S(1)}, u32[]{:S(2)}, u32[]{:S(2)}) collective-permute-start(s32[8,256]{1,0:T(8,128)S(1)} %join.1.refs_4_.near_codes_ref), channel_id=1, source_target_pairs={{0,16},{1,17},{2,18},{3,19},{4,20},{5,21},{6,22},{7,23},{8,24},{9,... | collective-permute-start | bytes 24584 | tf_op jit(solution)/shard_map/ppermute | solution.py:616
  14.5 3.6 %collective-permute-start.4 = (bf16[192,768]{1,0:T(8,128)(2,1)S(1)}, bf16[192,768]{1,0:T(8,128)(2,1)S(1)}, u32[]{:S(2)}, u32[]{:S(2)}) collective-permute-start(bf16[192,768]{1,0:T(8,128)(2,1)S(1)} %copy-done.2), channel_id=1, source_target_pairs={{0,1},{1,0},{2,3},{3,2},{4,5},{5,4},{6,7},{7,6},{8,9},{9,8},{10,11... | collective-permute-start | bytes 884744 | tf_op jit(solution)/shard_map/ppermute | solution.py:616
  14.7 3.4 %collective-permute-start.5 = (bf16[192,768]{1,0:T(8,128)(2,1)S(1)}, bf16[192,768]{1,0:T(8,128)(2,1)S(1)}, u32[]{:S(2)}, u32[]{:S(2)}) collective-permute-start(bf16[192,768]{1,0:T(8,128)(2,1)S(1)} %collective-permute-done.3.refs_2_), channel_id=1, source_target_pairs={{0,1},{1,0},{2,3},{3,2},{4,5},{5,4},{6,7},{7,6},{8,9},{9,8},{10,11... | collective-permute-start | bytes 884744 | tf_op jit(solution)/shard_map/ppermute | solution.py:616
  16.5 1.7 %copy-start.1 = (bf16[3,192,768]{2,1,0:T(8,128)(2,1)S(1)}, bf16[3,192,768]{2,1,0:T(8,128)(2,1)}, u32[]{:S(2)}) copy-start(bf16[3,192,768]{2,1,0:T(8,128)(2,1)} %param.12) | copy-start | bytes 2654212
  16.5 1.7 %copy-start.3 = (bf16[33,768]{1,0:T(8,128)(2,1)S(1)}, bf16[33,768]{1,0:T(8,128)(2,1)}, u32[]{:S(2)}) copy-start(bf16[33,768]{1,0:T(8,128)(2,1)} %refs_8_.1) | copy-start | bytes 152068
  18.2 11.5 %copy-start = (bf16[192,768]{1,0:T(8,128)(2,1)S(1)}, bf16[192,768]{1,0:T(8,128)(2,1)}, u32[]{:S(2)}) copy-start(bf16[192,768]{1,0:T(8,128)(2,1)} %refs_5_.1) | copy-start | bytes 884740
  21.2 7.0 %collective-permute-start.11 = (bf16[768,128]{1,0:T(8,128)(2,1)S(1)}, bf16[768,128]{1,0:T(8,128)(2,1)S(1)}, u32[]{:S(2)}, u32[]{:S(2)}) collective-permute-start(bf16[768,128]{1,0:T(8,128)(2,1)S(1)} %get-tuple-element.39.refs_0_), channel_id=1, source_target_pairs={{0,2},{1,3},{2,0},{3,1},{4,6},{5,7},{6,4},{7,5},{8,10},{9,11},{10,... | collective-permute-start | bytes 589832 | tf_op jit(solution)/shard_map/ppermute | solution.py:616
  21.8 6.4 %collective-permute-start.10 = (bf16[768,128]{1,0:T(8,128)(2,1)S(1)}, bf16[768,128]{1,0:T(8,128)(2,1)S(1)}, u32[]{:S(2)}, u32[]{:S(2)}) collective-permute-start(bf16[768,128]{1,0:T(8,128)(2,1)S(1)} %get-tuple-element.39.refs_0_), channel_id=1, source_target_pairs={{0,1},{1,0},{2,3},{3,2},{4,5},{5,4},{6,7},{7,6},{8,9},{9,8},{10,11... | collective-permute-start | bytes 589832 | tf_op jit(solution)/shard_map/ppermute | solution.py:616
  28.2 1.4 %collective-permute-start.12 = (bf16[768,128]{1,0:T(8,128)(2,1)S(1)}, bf16[768,128]{1,0:T(8,128)(2,1)S(1)}, u32[]{:S(2)}, u32[]{:S(2)}) collective-permute-start(bf16[768,128]{1,0:T(8,128)(2,1)S(1)} %collective-permute-done.11.refs_2_), channel_id=1, source_target_pairs={{0,1},{1,0},{2,3},{3,2},{4,5},{5,4},{6,7},{7,6},{8,9},{9,8},{10,11... | collective-permute-start | bytes 589832 | tf_op jit(solution)/shard_map/ppermute | solution.py:616

commit v26 on v24

--- a/solution.py
+++ b/solution.py
@@ -529,6 +529,17 @@
     )(*row_outs, live, row_context, near_own, far_own, embed, col_qkv)
 
 
+def steps_of(groups):
+    return [1] + [1 << k for k in range(groups.bit_length() - 2, 0, -1)]
+
+
+def slot_order(groups):
+    order = [0]
+    for step in steps_of(groups):
+        order += [slot ^ step for slot in order]
+    return order
+
+
 def finish_kernel(parts, groups, *refs):
     context_refs = [refs[:parts], refs[parts : 2 * parts]]
     mixed_ref, col_out_ref, out_ref, context_ref = refs[2 * parts :]
@@ -559,10 +570,10 @@
         pieces.append(jnp.concatenate(features, 1))
     total = mixed_ref[...] + dot_nt(jnp.concatenate(pieces, 0), col_out_ref[...])
     own = tokens // groups // 2
-    for d in range(groups):
+    for d, slot in enumerate(slot_order(groups)):
         first, second = (total[(2 * d + r) * own : (2 * d + r + 1) * own, :] for r in range(2))
         rest = jnp.concatenate([first[:, LANES:local], second[:, LANES:local]], 1)
-        out_ref[group ^ d] = jnp.concatenate(
+        out_ref[group ^ slot] = jnp.concatenate(
             [first[:, 0:LANES], second[:, 0:LANES], rest], 0
         ).astype(bf16)
 
@@ -631,21 +642,18 @@
     other_mask = pairwise(pad_mask.reshape(1, rows_here), lambda g, p: (g ^ 1, p))
     table, coded = make_tables(ids, pad_mask, embed, row_qkv, rows_here * groups // 2)
     tables = [table, None, pairwise(table, across), None]
-    step = 2
-    while step < groups:
-        if step == 2:
+    for count, step in enumerate(steps_of(groups)[1:], 1):
+        if count == 1:
             coded = join_raw(coded, other_ids, other_mask)
-        else:
-            coded = join(coded, received, rows_here * step // 2)
-        if step == 2:
             coded, table = lax.optimization_barrier((coded, table))
             tables[3] = pairwise(table, opposite)
-        elif step == 4:
+        else:
+            coded = join(coded, received, rows_here << (count - 1))
+        if count == 2:
             coded, table, row_out, far = lax.optimization_barrier((coded, table, row_out, far))
             tables[1] = pairwise(table, sibling)
             row_outs = [row_out, pairwise(row_out, sibling), far, pairwise(far, sibling)]
         received = pairwise(coded, lambda g, p, step=step: (g ^ step, p))
-        step *= 2
     codes = (coded, received)
     *near_scores, near_own = attend_near(tables, codes[0], own)
     row_context, far_own, live = attend_rows(near_scores, *codes, own)

time: 43.5 us -> 43.3 us (level)
  waiting for transfers between devices: 8.66 us -> 9.62 us
  blocking collectives: 12.5 us -> 11.6 us
    ppermute x16, waiting for transfers between devices: 8.66 us -> 9.62 us  [pairwise(): lax.ppermute(value, ('seq', 'head'), [(i, g * parts + p) for i, (g, p) in...]
    all_to_all x1, blocking collectives: 12.5 us -> 11.6 us  [fast_body(): lax.all_to_all(blocks, 'seq', split_axis=0, concat_axis=0, tiled=True)]
where the time goes in v26:
time: 43.3 us; the launch traced here: 43.1 us
  starting transfers between devices  12.7 us (29%)
  blocking collectives  11.6 us (27%)
  waiting for transfers between devices  9.62 us (22%)
  Pallas kernels  9.12 us (21%)
    ppermute x16, starting transfers between devices, pairwise(): lax.ppermute(value, ('seq', 'head'), [(i, g * parts + p) for i, (g, p) in...  12.7 us
    all_to_all x1, blocking collectives, fast_body(): lax.all_to_all(blocks, 'seq', split_axis=0, concat_axis=0, tiled=True)  11.6 us
    ppermute x16, waiting for transfers between devices, pairwise(): lax.ppermute(value, ('seq', 'head'), [(i, g * parts + p) for i, (g, p) in...  9.62 us
    pallas_call x1, Pallas kernels, attend_columns_here(): pl.pallas_call(functools.partial(column_kernel, parts), out_shape=(jax.Sh...  3.02 us
    pallas_call x1, Pallas kernels, make_tables(): pl.pallas_call(table_kernel, out_shape=(jax.ShapeDtypeStruct((TABLE_ROWS,...  1.87 us
    pallas_call x1, Pallas kernels, attend_rows(): pl.pallas_call(row_kernel, out_shape=(jax.ShapeDtypeStruct((2 * half * ow...  1.62 us
    pallas_call x1, Pallas kernels, attend_near(): pl.pallas_call(functools.partial(near_kernel, parts), out_shape=(jax.Shap...  1.19 us
  transfers between devices with their start and end apart: 16, of which 6 were waited for; matrix products, arithmetic and copies ran while one was open for 0% of the time, Pallas kernels for 11%

profile of v26, /device:TPU:0, one launch (start us, length us, event | category | flops | bytes accessed | tf_op | source)
XLA Modules:
  0.0 43.1 jit_solution(1220614063234594384)
XLA Ops:
  0.0 2.9 %collective-permute-start.3 = (bf16[192,768]{1,0:T(8,128)(2,1)}, bf16[192,768]{1,0:T(8,128)(2,1)S(1)}, u32[]{:S(2)}, u32[]{:S(2)}) collective-permute-start(bf16[192,768]{1,0:T(8,128)(2,1)} %refs_0_), channel_id=1, source_target_pairs={{0,2},{1,3},{2,0},{3,1},{4,6},{5,7},{6,4},{7,5},{8,10},{9,11},{10,... | collective-permute-start | bytes 884744 | tf_op jit(solution)/shard_map/ppermute | solution.py:629
  2.9 1.5 %collective-permute-start = (s32[2,256]{1,0:T(2,128)}, s32[2,256]{1,0:T(2,128)S(1)}, u32[]{:S(2)}, u32[]{:S(2)}) collective-permute-start(s32[2,256]{1,0:T(2,128)} %ids_hbm.1), channel_id=1, source_target_pairs={{0,4},{1,5},{2,6},{3,7},{4,0},{5,1},{6,2},{7,3},{8,12},{9,13},{10,... | collective-permute-start | bytes 6152 | tf_op jit(solution)/shard_map/ppermute | solution.py:629
  4.5 0.0 copy-done.4
  4.5 0.0 copy-start.2
  4.5 0.5 %collective-permute-start.1 = (s32[1,2]{1,0:T(1,128)S(1)}, s32[1,2]{1,0:T(1,128)S(1)}, u32[]{:S(2)}, u32[]{:S(2)}) collective-permute-start(s32[1,2]{1,0:T(1,128)S(1)} %bitcast.4), channel_id=1, source_target_pairs={{0,4},{1,5},{2,6},{3,7},{4,0},{5,1},{6,2},{7,3},{8,12},{9,13},{10,... | collective-permute-start | bytes 32 | tf_op jit(solution)/shard_map/ppermute | solution.py:629
  5.0 1.9 %tables.1 = (bf16[40,576]{1,0:T(8,128)(2,1)S(1)}, s32[8,256]{1,0:T(8,128)S(1)}) custom-call(s32[2,256]{1,0:T(2,128)} %ids_hbm.1, s32[2]{0:T(128)} %live_hbm.1, bf16[33,768]{1,0:T(8,128)(2,1)} %refs_8_.1, bf16[3,192,768]{2,1,0:T(8,128)(2,1)} %qkv_hbm.1), custom_call_target="tpu_custom_call" | custom-call | flops 2000000000 | bytes 884736 | tf_op jit(solution)/shard_map/tables/pallas_call | solution.py:131
  6.8 1.2 %collective-permute-done.1.live_ref = s32[1,2]{1,0:T(1,128)S(1)} collective-permute-done((s32[1,2]{1,0:T(1,128)S(1)}, s32[1,2]{1,0:T(1,128)S(1)}, u32[]{:S(2)}, u32[]{:S(2)}) %collective-permute-start.1) | collective-permute-done | bytes 40 | tf_op jit(solution)/shard_map/ppermute | solution.py:629
  8.0 0.0 collective-permute-done.ids_ref
  8.0 0.1 join_raw.1.own_ref
  8.1 2.6 %collective-permute-start.2 = (s32[8,256]{1,0:T(8,128)S(1)}, s32[8,256]{1,0:T(8,128)S(1)}, u32[]{:S(2)}, u32[]{:S(2)}) collective-permute-start(s32[8,256]{1,0:T(8,128)S(1)} %join_raw.1.own_ref), channel_id=1, source_target_pairs={{0,16},{1,17},{2,18},{3,19},{4,20},{5,21},{6,22},{7,23},{8,24},{9,... | collective-permute-start | bytes 24584 | tf_op jit(solution)/shard_map/ppermute | solution.py:629
  10.7 0.5 %collective-permute-start.7 = (bf16[40,576]{1,0:T(8,128)(2,1)S(1)}, bf16[40,576]{1,0:T(8,128)(2,1)S(1)}, u32[]{:S(2)}, u32[]{:S(2)}) collective-permute-start(bf16[40,576]{1,0:T(8,128)(2,1)S(1)} %get-tuple-element.30.refs_0_), channel_id=1, source_target_pairs={{0,2},{1,3},{2,0},{3,1},{4,6},{5,7},{6,4},{7,5},{8,10},{9,11},{10,... | collective-permute-start | bytes 138248 | tf_op jit(solution)/shard_map/ppermute | solution.py:629
  11.3 0.0 collective-permute-start.8
  11.3 1.4 %collective-permute-done.2.other_ref = s32[8,256]{1,0:T(8,128)S(1)} collective-permute-done((s32[8,256]{1,0:T(8,128)S(1)}, s32[8,256]{1,0:T(8,128)S(1)}, u32[]{:S(2)}, u32[]{:S(2)}) %collective-permute-start.2) | collective-permute-done | bytes 8224 | tf_op jit(solution)/shard_map/ppermute | solution.py:629
  12.7 0.0 collective-permute-done.3.refs_2_
  12.7 0.3 collective-permute-start.6
  13.0 1.6 %collective-permute-start.9 = (s32[8,256]{1,0:T(8,128)S(1)}, s32[8,256]{1,0:T(8,128)S(1)}, u32[]{:S(2)}, u32[]{:S(2)}) collective-permute-start(s32[8,256]{1,0:T(8,128)S(1)} %join.1.refs_4_.near_codes_ref), channel_id=1, source_target_pairs={{0,8},{1,9},{2,10},{3,11},{4,12},{5,13},{6,14},{7,15},{8,0},{9,1},... | collective-permute-start | bytes 24584 | tf_op jit(solution)/shard_map/ppermute | solution.py:629
  14.5 0.0 copy-done.2
  14.5 0.0 collective-permute-start.4
  14.6 0.8 %collective-permute-done.7.refs_2_ = bf16[40,576]{1,0:T(8,128)(2,1)S(1)} collective-permute-done((bf16[40,576]{1,0:T(8,128)(2,1)S(1)}, bf16[40,576]{1,0:T(8,128)(2,1)S(1)}, u32[]{:S(2)}, u32[]{:S(2)}) %collective-permute-start.7) | collective-permute-done | bytes 46112 | tf_op jit(solution)/shard_map/ppermute | solution.py:629
  15.4 0.0 collective-permute-start.5
  15.4 0.0 collective-permute-done.8.refs_3_
  15.4 0.0 collective-permute-done.6.refs_1_
  15.4 1.2 %near_scores.1 = (bf16[12,128,256]{2,1,0:T(8,128)(2,1)S(1)}, bf16[64,768]{1,0:T(8,128)(2,1)S(1)}, f32[384,256]{1,0:T(8,128)S(1)}, bf16[512,256]{1,0:T(8,128)(2,1)S(1)}, bf16[128,128]{1,0:T(8,128)(2,1)S(1)}) custom-call(bf16[40,576]{1,0:T(8,128)(2,1)S(1)} %get-tuple-element.30.refs_0_, bf16[40,576]{1,0:T(8,128)(2,1)S(1)} %collective-permute-done.6.refs_1_, ...), custom_call_target="tpu_custom_call" | custom-call | flops 1000000000 | bytes 1000000 | tf_op jit(solution)/shard_map/near_scores/pallas_call | solution.py:280
  16.6 0.0 collective-permute-done.9.far_codes_ref
  16.6 0.0 copy-start.1
  16.6 1.6 %row_attention.1 = (bf16[512,768]{1,0:T(8,128)(2,1)S(1)}, bf16[128,128]{1,0:T(8,128)(2,1)S(1)}, f32[16,128]{1,0:T(8,128)S(1)}) custom-call(bf16[12,128,256]{2,1,0:T(8,128)(2,1)S(1)} %get-tuple-element.32.scores_ref, bf16[64,768]{1,0:T(8,128)(2,1)S(1)} %get-tuple-element.33.values_ref, f32[384,256]{1,0:T(8,128)S(1)} %get-tuple-element.34.near_tied_ref, ...), custom_call_target="tpu_custom_call" | custom-call | flops 3000000000 | bytes 1000000 | tf_op jit(solution)/shard_map/row_attention/pallas_call | solution.py:371
  18.2 0.0 collective-permute-done.4.refs_1_
  18.3 0.0 collective-permute-done.5.refs_3_
  18.3 0.0 copy-done.1
  18.3 0.0 copy-done.3
  18.3 0.0 copy-start
  18.3 3.0 %column_attention.1 = (bf16[384,128]{1,0:T(8,128)(2,1)S(1)}, bf16[384,128]{1,0:T(8,128)(2,1)S(1)}, f32[512,192]{1,0:T(8,128)S(1)}) custom-call(bf16[192,768]{1,0:T(8,128)(2,1)S(1)} %copy-done.2, bf16[192,768]{1,0:T(8,128)(2,1)S(1)} %collective-permute-done.4.refs_1_, bf16[192,768]{1,0:T(8,128)(2,1)S(1)} %collective-permute-done.3.refs_2_, ...), custom_call_target="tpu_custom_call" | custom-call | flops 2000000000 | bytes 1000000 | tf_op jit(solution)/shard_map/column_attention/pallas_call | solution.py:513
  21.3 1.2 %collective-permute-start.11 = (bf16[384,128]{1,0:T(8,128)(2,1)S(1)}, bf16[384,128]{1,0:T(8,128)(2,1)S(1)}, u32[]{:S(2)}, u32[]{:S(2)}) collective-permute-start(bf16[384,128]{1,0:T(8,128)(2,1)S(1)} %get-tuple-element.40.refs_0_), channel_id=1, source_target_pairs={{0,2},{1,3},{2,0},{3,1},{4,6},{5,7},{6,4},{7,5},{8,10},{9,11},{10,... | collective-permute-start | bytes 294920 | tf_op jit(solution)/shard_map/ppermute | solution.py:629
  22.5 0.9 %collective-permute-start.14 = (bf16[384,128]{1,0:T(8,128)(2,1)S(1)}, bf16[384,128]{1,0:T(8,128)(2,1)S(1)}, u32[]{:S(2)}, u32[]{:S(2)}) collective-permute-start(bf16[384,128]{1,0:T(8,128)(2,1)S(1)} %get-tuple-element.41.refs_4_), channel_id=1, source_target_pairs={{0,2},{1,3},{2,0},{3,1},{4,6},{5,7},{6,4},{7,5},{8,10},{9,11},{10,... | collective-permute-start | bytes 294920 | tf_op jit(solution)/shard_map/ppermute | solution.py:629
  23.4 0.1 collective-permute-start.10
  23.5 0.4 collective-permute-start.13
  24.0 3.1 %collective-permute-done.11.refs_2_ = bf16[384,128]{1,0:T(8,128)(2,1)S(1)} collective-permute-done((bf16[384,128]{1,0:T(8,128)(2,1)S(1)}, bf16[384,128]{1,0:T(8,128)(2,1)S(1)}, u32[]{:S(2)}, u32[]{:S(2)}) %collective-permute-start.11) | collective-permute-done | bytes 98336 | tf_op jit(solution)/shard_map/ppermute | solution.py:629
  27.1 0.0 collective-permute-start.12
  27.1 1.8 %collective-permute-done.14.refs_6_ = bf16[384,128]{1,0:T(8,128)(2,1)S(1)} collective-permute-done((bf16[384,128]{1,0:T(8,128)(2,1)S(1)}, bf16[384,128]{1,0:T(8,128)(2,1)S(1)}, u32[]{:S(2)}, u32[]{:S(2)}) %collective-permute-start.14) | collective-permute-done | bytes 98336 | tf_op jit(solution)/shard_map/ppermute | solution.py:629
  28.9 0.0 collective-permute-start.15
  28.9 0.0 collective-permute-done.10.refs_1_
  28.9 0.0 collective-permute-done.13.refs_5_
  28.9 0.0 collective-permute-done.12.refs_3_
  28.9 1.3 %collective-permute-done.15.refs_7_ = bf16[384,128]{1,0:T(8,128)(2,1)S(1)} collective-permute-done((bf16[384,128]{1,0:T(8,128)(2,1)S(1)}, bf16[384,128]{1,0:T(8,128)(2,1)S(1)}, u32[]{:S(2)}, u32[]{:S(2)}) %collective-permute-start.15) | collective-permute-done | bytes 98336 | tf_op jit(solution)/shard_map/ppermute | solution.py:629
  30.2 0.0 copy-done
  30.2 0.5 %finish.1 = bf16[8,96,128]{2,1,0:T(8,128)(2,1)S(1)} custom-call(bf16[384,128]{1,0:T(8,128)(2,1)S(1)} %get-tuple-element.40.refs_0_, bf16[384,128]{1,0:T(8,128)(2,1)S(1)} %collective-permute-done.10.refs_1_, bf16[384,128]{1,0:T(8,128)(2,1)S(1)} %collective-permute-done.11.refs_2_, bf16[384,128]{1,0:T(8,128)(2,1)S(1)} %collective-permute-done.12.refs_3_, ...), custom_call_target="tpu_custom_call" | custom-call | tf_op jit(solution)/shard_map/finish/pallas_call | solution.py:584
  30.7 11.6 %all_to_all.5.blocks_ref = bf16[8,96,128]{2,1,0:T(8,128)(2,1)S(1)} all-to-all(bf16[8,96,128]{2,1,0:T(8,128)(2,1)S(1)} %finish.1), channel_id=1, replica_groups=mesh['seq'=8,'head'=4] {'seq'}, dimensions={0} | all-to-all | bytes 393216 | tf_op jit(solution)/shard_map/all_to_all | solution.py:676
  42.3 0.8 %order.1 = bf16[2,192,256]{2,1,0:T(8,128)(2,1)} custom-call(bf16[8,96,128]{2,1,0:T(8,128)(2,1)S(1)} %all_to_all.5.blocks_ref), custom_call_target="tpu_custom_call" | custom-call | tf_op jit(solution)/shard_map/order/pallas_call | solution.py:611
  (3 shorter events, 0.0 us)
Async XLA Ops:
  0.0 4.5 %copy-start.4 = (s32[2]{0:T(128)S(1)}, s32[2]{0:T(128)}, u32[]{:S(2)}) copy-start(s32[2]{0:T(128)} %live_hbm.1) | copy-start | bytes 28
  0.0 12.7 %collective-permute-start.3 = (bf16[192,768]{1,0:T(8,128)(2,1)}, bf16[192,768]{1,0:T(8,128)(2,1)S(1)}, u32[]{:S(2)}, u32[]{:S(2)}) collective-permute-start(bf16[192,768]{1,0:T(8,128)(2,1)} %refs_0_), channel_id=1, source_target_pairs={{0,2},{1,3},{2,0},{3,1},{4,6},{5,7},{6,4},{7,5},{8,10},{9,11},{10,... | collective-permute-start | bytes 884744 | tf_op jit(solution)/shard_map/ppermute | solution.py:629
  2.9 5.1 %collective-permute-start = (s32[2,256]{1,0:T(2,128)}, s32[2,256]{1,0:T(2,128)S(1)}, u32[]{:S(2)}, u32[]{:S(2)}) collective-permute-start(s32[2,256]{1,0:T(2,128)} %ids_hbm.1), channel_id=1, source_target_pairs={{0,4},{1,5},{2,6},{3,7},{4,0},{5,1},{6,2},{7,3},{8,12},{9,13},{10,... | collective-permute-start | bytes 6152 | tf_op jit(solution)/shard_map/ppermute | solution.py:629
  4.5 10.1 %copy-start.2 = (bf16[192,768]{1,0:T(8,128)(2,1)S(1)}, bf16[192,768]{1,0:T(8,128)(2,1)}, u32[]{:S(2)}) copy-start(bf16[192,768]{1,0:T(8,128)(2,1)} %refs_0_) | copy-start | bytes 884740
  4.5 3.5 %collective-permute-start.1 = (s32[1,2]{1,0:T(1,128)S(1)}, s32[1,2]{1,0:T(1,128)S(1)}, u32[]{:S(2)}, u32[]{:S(2)}) collective-permute-start(s32[1,2]{1,0:T(1,128)S(1)} %bitcast.4), channel_id=1, source_target_pairs={{0,4},{1,5},{2,6},{3,7},{4,0},{5,1},{6,2},{7,3},{8,12},{9,13},{10,... | collective-permute-start | bytes 32 | tf_op jit(solution)/shard_map/ppermute | solution.py:629
  8.1 4.6 %collective-permute-start.2 = (s32[8,256]{1,0:T(8,128)S(1)}, s32[8,256]{1,0:T(8,128)S(1)}, u32[]{:S(2)}, u32[]{:S(2)}) collective-permute-start(s32[8,256]{1,0:T(8,128)S(1)} %join_raw.1.own_ref), channel_id=1, source_target_pairs={{0,16},{1,17},{2,18},{3,19},{4,20},{5,21},{6,22},{7,23},{8,24},{9,... | collective-permute-start | bytes 24584 | tf_op jit(solution)/shard_map/ppermute | solution.py:629
  10.7 4.6 %collective-permute-start.7 = (bf16[40,576]{1,0:T(8,128)(2,1)S(1)}, bf16[40,576]{1,0:T(8,128)(2,1)S(1)}, u32[]{:S(2)}, u32[]{:S(2)}) collective-permute-start(bf16[40,576]{1,0:T(8,128)(2,1)S(1)} %get-tuple-element.30.refs_0_), channel_id=1, source_target_pairs={{0,2},{1,3},{2,0},{3,1},{4,6},{5,7},{6,4},{7,5},{8,10},{9,11},{10,... | collective-permute-start | bytes 138248 | tf_op jit(solution)/shard_map/ppermute | solution.py:629
  11.3 4.1 %collective-permute-start.8 = (bf16[40,576]{1,0:T(8,128)(2,1)S(1)}, bf16[40,576]{1,0:T(8,128)(2,1)S(1)}, u32[]{:S(2)}, u32[]{:S(2)}) collective-permute-start(bf16[40,576]{1,0:T(8,128)(2,1)S(1)} %get-tuple-element.30.refs_0_), channel_id=1, source_target_pairs={{0,3},{1,2},{2,1},{3,0},{4,7},{5,6},{6,5},{7,4},{8,11},{9,10},{10,... | collective-permute-start | bytes 138248 | tf_op jit(solution)/shard_map/ppermute | solution.py:629
  12.7 2.7 %collective-permute-start.6 = (bf16[40,576]{1,0:T(8,128)(2,1)S(1)}, bf16[40,576]{1,0:T(8,128)(2,1)S(1)}, u32[]{:S(2)}, u32[]{:S(2)}) collective-permute-start(bf16[40,576]{1,0:T(8,128)(2,1)S(1)} %get-tuple-element.30.refs_0_), channel_id=1, source_target_pairs={{0,1},{1,0},{2,3},{3,2},{4,5},{5,4},{6,7},{7,6},{8,9},{9,8},{10,11... | collective-permute-start | bytes 138248 | tf_op jit(solution)/shard_map/ppermute | solution.py:629
  13.0 3.7 %collective-permute-start.9 = (s32[8,256]{1,0:T(8,128)S(1)}, s32[8,256]{1,0:T(8,128)S(1)}, u32[]{:S(2)}, u32[]{:S(2)}) collective-permute-start(s32[8,256]{1,0:T(8,128)S(1)} %join.1.refs_4_.near_codes_ref), channel_id=1, source_target_pairs={{0,8},{1,9},{2,10},{3,11},{4,12},{5,13},{6,14},{7,15},{8,0},{9,1},... | collective-permute-start | bytes 24584 | tf_op jit(solution)/shard_map/ppermute | solution.py:629
  14.5 3.7 %collective-permute-start.4 = (bf16[192,768]{1,0:T(8,128)(2,1)S(1)}, bf16[192,768]{1,0:T(8,128)(2,1)S(1)}, u32[]{:S(2)}, u32[]{:S(2)}) collective-permute-start(bf16[192,768]{1,0:T(8,128)(2,1)S(1)} %copy-done.2), channel_id=1, source_target_pairs={{0,1},{1,0},{2,3},{3,2},{4,5},{5,4},{6,7},{7,6},{8,9},{9,8},{10,11... | collective-permute-start | bytes 884744 | tf_op jit(solution)/shard_map/ppermute | solution.py:629
  15.4 2.9 %collective-permute-start.5 = (bf16[192,768]{1,0:T(8,128)(2,1)S(1)}, bf16[192,768]{1,0:T(8,128)(2,1)S(1)}, u32[]{:S(2)}, u32[]{:S(2)}) collective-permute-start(bf16[192,768]{1,0:T(8,128)(2,1)S(1)} %collective-permute-done.3.refs_2_), channel_id=1, source_target_pairs={{0,1},{1,0},{2,3},{3,2},{4,5},{5,4},{6,7},{7,6},{8,9},{9,8},{10,11... | collective-permute-start | bytes 884744 | tf_op jit(solution)/shard_map/ppermute | solution.py:629
  16.6 1.7 %copy-start.1 = (bf16[3,192,768]{2,1,0:T(8,128)(2,1)S(1)}, bf16[3,192,768]{2,1,0:T(8,128)(2,1)}, u32[]{:S(2)}) copy-start(bf16[3,192,768]{2,1,0:T(8,128)(2,1)} %param.12) | copy-start | bytes 2654212
  16.6 1.7 %copy-start.3 = (bf16[33,768]{1,0:T(8,128)(2,1)S(1)}, bf16[33,768]{1,0:T(8,128)(2,1)}, u32[]{:S(2)}) copy-start(bf16[33,768]{1,0:T(8,128)(2,1)} %refs_8_.1) | copy-start | bytes 152068
  18.3 11.9 %copy-start = (bf16[192,768]{1,0:T(8,128)(2,1)S(1)}, bf16[192,768]{1,0:T(8,128)(2,1)}, u32[]{:S(2)}) copy-start(bf16[192,768]{1,0:T(8,128)(2,1)} %refs_9_.1) | copy-start | bytes 884740
  21.3 5.7 %collective-permute-start.11 = (bf16[384,128]{1,0:T(8,128)(2,1)S(1)}, bf16[384,128]{1,0:T(8,128)(2,1)S(1)}, u32[]{:S(2)}, u32[]{:S(2)}) collective-permute-start(bf16[384,128]{1,0:T(8,128)(2,1)S(1)} %get-tuple-element.40.refs_0_), channel_id=1, source_target_pairs={{0,2},{1,3},{2,0},{3,1},{4,6},{5,7},{6,4},{7,5},{8,10},{9,11},{10,... | collective-permute-start | bytes 294920 | tf_op jit(solution)/shard_map/ppermute | solution.py:629
  22.5 6.4 %collective-permute-start.14 = (bf16[384,128]{1,0:T(8,128)(2,1)S(1)}, bf16[384,128]{1,0:T(8,128)(2,1)S(1)}, u32[]{:S(2)}, u32[]{:S(2)}) collective-permute-start(bf16[384,128]{1,0:T(8,128)(2,1)S(1)} %get-tuple-element.41.refs_4_), channel_id=1, source_target_pairs={{0,2},{1,3},{2,0},{3,1},{4,6},{5,7},{6,4},{7,5},{8,10},{9,11},{10,... | collective-permute-start | bytes 294920 | tf_op jit(solution)/shard_map/ppermute | solution.py:629
  23.4 5.4 %collective-permute-start.10 = (bf16[384,128]{1,0:T(8,128)(2,1)S(1)}, bf16[384,128]{1,0:T(8,128)(2,1)S(1)}, u32[]{:S(2)}, u32[]{:S(2)}) collective-permute-start(bf16[384,128]{1,0:T(8,128)(2,1)S(1)} %get-tuple-element.40.refs_0_), channel_id=1, source_target_pairs={{0,1},{1,0},{2,3},{3,2},{4,5},{5,4},{6,7},{7,6},{8,9},{9,8},{10,11... | collective-permute-start | bytes 294920 | tf_op jit(solution)/shard_map/ppermute | solution.py:629
  23.5 5.3 %collective-permute-start.13 = (bf16[384,128]{1,0:T(8,128)(2,1)S(1)}, bf16[384,128]{1,0:T(8,128)(2,1)S(1)}, u32[]{:S(2)}, u32[]{:S(2)}) collective-permute-start(bf16[384,128]{1,0:T(8,128)(2,1)S(1)} %get-tuple-element.41.refs_4_), channel_id=1, source_target_pairs={{0,1},{1,0},{2,3},{3,2},{4,5},{5,4},{6,7},{7,6},{8,9},{9,8},{10,11... | collective-permute-start | bytes 294920 | tf_op jit(solution)/shard_map/ppermute | solution.py:629
  27.1 1.8 %collective-permute-start.12 = (bf16[384,128]{1,0:T(8,128)(2,1)S(1)}, bf16[384,128]{1,0:T(8,128)(2,1)S(1)}, u32[]{:S(2)}, u32[]{:S(2)}) collective-permute-start(bf16[384,128]{1,0:T(8,128)(2,1)S(1)} %collective-permute-done.11.refs_2_), channel_id=1, source_target_pairs={{0,1},{1,0},{2,3},{3,2},{4,5},{5,4},{6,7},{7,6},{8,9},{9,8},{10,11... | collective-permute-start | bytes 294920 | tf_op jit(solution)/shard_map/ppermute | solution.py:629
  28.9 1.3 %collective-permute-start.15 = (bf16[384,128]{1,0:T(8,128)(2,1)S(1)}, bf16[384,128]{1,0:T(8,128)(2,1)S(1)}, u32[]{:S(2)}, u32[]{:S(2)}) collective-permute-start(bf16[384,128]{1,0:T(8,128)(2,1)S(1)} %collective-permute-done.14.refs_6_), channel_id=1, source_target_pairs={{0,1},{1,0},{2,3},{3,2},{4,5},{5,4},{6,7},{7,6},{8,9},{9,8},{10,11... | collective-permute-start | bytes 294920 | tf_op jit(solution)/shard_map/ppermute | solution.py:629

commit v27 on v26

--- a/solution.py
+++ b/solution.py
@@ -634,24 +634,21 @@
     def across(g, p):
         return g, p ^ 2
 
-    def opposite(g, p):
-        return g, p ^ 3
-
     far = pairwise(row_out, across)
     other_ids = pairwise(ids, lambda g, p: (g ^ 1, p))
     other_mask = pairwise(pad_mask.reshape(1, rows_here), lambda g, p: (g ^ 1, p))
     table, coded = make_tables(ids, pad_mask, embed, row_qkv, rows_here * groups // 2)
-    tables = [table, None, pairwise(table, across), None]
+    tables = [table, None, None, None]
     for count, step in enumerate(steps_of(groups)[1:], 1):
         if count == 1:
             coded = join_raw(coded, other_ids, other_mask)
             coded, table = lax.optimization_barrier((coded, table))
-            tables[3] = pairwise(table, opposite)
+            tables[2] = pairwise(table, across)
         else:
             coded = join(coded, received, rows_here << (count - 1))
         if count == 2:
             coded, table, row_out, far = lax.optimization_barrier((coded, table, row_out, far))
-            tables[1] = pairwise(table, sibling)
+            tables[1], tables[3] = pairwise(table, sibling), pairwise(tables[2], sibling)
             row_outs = [row_out, pairwise(row_out, sibling), far, pairwise(far, sibling)]
         received = pairwise(coded, lambda g, p, step=step: (g ^ step, p))
     codes = (coded, received)

time: 43.3 us -> 44.1 us (1.018)
  blocking collectives: 11.6 us -> 12.3 us
  starting transfers between devices: 12.7 us -> 13.4 us
  waiting for transfers between devices: 9.62 us -> 8.98 us
    ppermute x16, starting transfers between devices: 12.7 us -> 13.4 us  [pairwise(): lax.ppermute(value, ('seq', 'head'), [(i, g * parts + p) for i, (g, p) in...]
    all_to_all x1, blocking collectives: 11.6 us -> 12.3 us  [fast_body(): lax.all_to_all(blocks, 'seq', split_axis=0, concat_axis=0, tiled=True)]
    ppermute x16, waiting for transfers between devices: 9.62 us -> 8.98 us  [pairwise(): lax.ppermute(value, ('seq', 'head'), [(i, g * parts + p) for i, (g, p) in...]
  transfers between devices with their start and end apart: 16 -> 16, of which waited for: 6 -> 7; matrix products, arithmetic and copies ran while one was open for 0% -> 0% of each run, Pallas kernels for 11% -> 11%
where the time goes in v27:
time: 44.1 us; the launch traced here: 43.9 us
  starting transfers between devices  13.4 us (30%)
  blocking collectives  12.3 us (28%)
  Pallas kernels  9.12 us (21%)
  waiting for transfers between devices  8.98 us (20%)
    ppermute x16, starting transfers between devices, pairwise(): lax.ppermute(value, ('seq', 'head'), [(i, g * parts + p) for i, (g, p) in...  13.4 us
    all_to_all x1, blocking collectives, fast_body(): lax.all_to_all(blocks, 'seq', split_axis=0, concat_axis=0, tiled=True)  12.3 us
    ppermute x16, waiting for transfers between devices, pairwise(): lax.ppermute(value, ('seq', 'head'), [(i, g * parts + p) for i, (g, p) in...  8.98 us
    pallas_call x1, Pallas kernels, attend_columns_here(): pl.pallas_call(functools.partial(column_kernel, parts), out_shape=(jax.Sh...  3.02 us
    pallas_call x1, Pallas kernels, make_tables(): pl.pallas_call(table_kernel, out_shape=(jax.ShapeDtypeStruct((TABLE_ROWS,...  1.87 us
    pallas_call x1, Pallas kernels, attend_rows(): pl.pallas_call(row_kernel, out_shape=(jax.ShapeDtypeStruct((2 * half * ow...  1.63 us
    pallas_call x1, Pallas kernels, attend_near(): pl.pallas_call(functools.partial(near_kernel, parts), out_shape=(jax.Shap...  1.19 us
  transfers between devices with their start and end apart: 16, of which 7 were waited for; matrix products, arithmetic and copies ran while one was open for 0% of the time, Pallas kernels for 11%

profile of v27, /device:TPU:0, one launch (start us, length us, event | category | flops | bytes accessed | tf_op | source)
XLA Modules:
  0.0 43.9 jit_solution(13296935717834598944)
XLA Ops:
  0.0 0.0 copy-start.4
  0.0 2.9 %collective-permute-start.3 = (bf16[192,768]{1,0:T(8,128)(2,1)}, bf16[192,768]{1,0:T(8,128)(2,1)S(1)}, u32[]{:S(2)}, u32[]{:S(2)}) collective-permute-start(bf16[192,768]{1,0:T(8,128)(2,1)} %refs_0_), channel_id=1, source_target_pairs={{0,2},{1,3},{2,0},{3,1},{4,6},{5,7},{6,4},{7,5},{8,10},{9,11},{10,... | collective-permute-start | bytes 884744 | tf_op jit(solution)/shard_map/ppermute | solution.py:629
  2.9 1.5 %collective-permute-start = (s32[2,256]{1,0:T(2,128)}, s32[2,256]{1,0:T(2,128)S(1)}, u32[]{:S(2)}, u32[]{:S(2)}) collective-permute-start(s32[2,256]{1,0:T(2,128)} %ids_hbm.1), channel_id=1, source_target_pairs={{0,4},{1,5},{2,6},{3,7},{4,0},{5,1},{6,2},{7,3},{8,12},{9,13},{10,... | collective-permute-start | bytes 6152 | tf_op jit(solution)/shard_map/ppermute | solution.py:629
  4.5 0.0 copy-done.4
  4.5 0.0 copy-start.2
  4.5 0.5 %collective-permute-start.1 = (s32[1,2]{1,0:T(1,128)S(1)}, s32[1,2]{1,0:T(1,128)S(1)}, u32[]{:S(2)}, u32[]{:S(2)}) collective-permute-start(s32[1,2]{1,0:T(1,128)S(1)} %bitcast.4), channel_id=1, source_target_pairs={{0,4},{1,5},{2,6},{3,7},{4,0},{5,1},{6,2},{7,3},{8,12},{9,13},{10,... | collective-permute-start | bytes 32 | tf_op jit(solution)/shard_map/ppermute | solution.py:629
  5.0 1.9 %tables.1 = (bf16[40,576]{1,0:T(8,128)(2,1)S(1)}, s32[8,256]{1,0:T(8,128)S(1)}) custom-call(s32[2,256]{1,0:T(2,128)} %ids_hbm.1, s32[2]{0:T(128)} %live_hbm.1, bf16[33,768]{1,0:T(8,128)(2,1)} %refs_8_.1, bf16[3,192,768]{2,1,0:T(8,128)(2,1)} %qkv_hbm.1), custom_call_target="tpu_custom_call" | custom-call | flops 2000000000 | bytes 884736 | tf_op jit(solution)/shard_map/tables/pallas_call | solution.py:131
  6.8 1.2 %collective-permute-done.1.live_ref = s32[1,2]{1,0:T(1,128)S(1)} collective-permute-done((s32[1,2]{1,0:T(1,128)S(1)}, s32[1,2]{1,0:T(1,128)S(1)}, u32[]{:S(2)}, u32[]{:S(2)}) %collective-permute-start.1) | collective-permute-done | bytes 40 | tf_op jit(solution)/shard_map/ppermute | solution.py:629
  8.0 0.0 collective-permute-done.ids_ref
  8.0 0.1 join_raw.1.own_ref
  8.1 0.6 %collective-permute-start.7 = (bf16[40,576]{1,0:T(8,128)(2,1)S(1)}, bf16[40,576]{1,0:T(8,128)(2,1)S(1)}, u32[]{:S(2)}, u32[]{:S(2)}) collective-permute-start(bf16[40,576]{1,0:T(8,128)(2,1)S(1)} %get-tuple-element.30.refs_0_), channel_id=1, source_target_pairs={{0,2},{1,3},{2,0},{3,1},{4,6},{5,7},{6,4},{7,5},{8,10},{9,11},{10,... | collective-permute-start | bytes 138248 | tf_op jit(solution)/shard_map/ppermute | solution.py:629
  8.7 2.6 %collective-permute-start.2 = (s32[8,256]{1,0:T(8,128)S(1)}, s32[8,256]{1,0:T(8,128)S(1)}, u32[]{:S(2)}, u32[]{:S(2)}) collective-permute-start(s32[8,256]{1,0:T(8,128)S(1)} %join_raw.1.own_ref), channel_id=1, source_target_pairs={{0,16},{1,17},{2,18},{3,19},{4,20},{5,21},{6,22},{7,23},{8,24},{9,... | collective-permute-start | bytes 24584 | tf_op jit(solution)/shard_map/ppermute | solution.py:629
  11.3 2.0 %collective-permute-done.2.other_ref = s32[8,256]{1,0:T(8,128)S(1)} collective-permute-done((s32[8,256]{1,0:T(8,128)S(1)}, s32[8,256]{1,0:T(8,128)S(1)}, u32[]{:S(2)}, u32[]{:S(2)}) %collective-permute-start.2) | collective-permute-done | bytes 8224 | tf_op jit(solution)/shard_map/ppermute | solution.py:629
  13.2 0.0 collective-permute-done.7.refs_2_
  13.2 0.1 collective-permute-start.8
  13.3 0.0 collective-permute-done.3.refs_2_
  13.3 0.5 %collective-permute-start.6 = (bf16[40,576]{1,0:T(8,128)(2,1)S(1)}, bf16[40,576]{1,0:T(8,128)(2,1)S(1)}, u32[]{:S(2)}, u32[]{:S(2)}) collective-permute-start(bf16[40,576]{1,0:T(8,128)(2,1)S(1)} %get-tuple-element.30.refs_0_), channel_id=1, source_target_pairs={{0,1},{1,0},{2,3},{3,2},{4,5},{5,4},{6,7},{7,6},{8,9},{9,8},{10,11... | collective-permute-start | bytes 138248 | tf_op jit(solution)/shard_map/ppermute | solution.py:629
  13.8 1.6 %collective-permute-start.9 = (s32[8,256]{1,0:T(8,128)S(1)}, s32[8,256]{1,0:T(8,128)S(1)}, u32[]{:S(2)}, u32[]{:S(2)}) collective-permute-start(s32[8,256]{1,0:T(8,128)S(1)} %join.1.refs_4_.near_codes_ref), channel_id=1, source_target_pairs={{0,8},{1,9},{2,10},{3,11},{4,12},{5,13},{6,14},{7,15},{8,0},{9,1},... | collective-permute-start | bytes 24584 | tf_op jit(solution)/shard_map/ppermute | solution.py:629
  15.4 0.0 copy-done.2
  15.4 0.0 collective-permute-start.4
  15.4 0.5 %collective-permute-start.5 = (bf16[192,768]{1,0:T(8,128)(2,1)S(1)}, bf16[192,768]{1,0:T(8,128)(2,1)S(1)}, u32[]{:S(2)}, u32[]{:S(2)}) collective-permute-start(bf16[192,768]{1,0:T(8,128)(2,1)S(1)} %collective-permute-done.3.refs_2_), channel_id=1, source_target_pairs={{0,1},{1,0},{2,3},{3,2},{4,5},{5,4},{6,7},{7,6},{8,9},{9,8},{10,11... | collective-permute-start | bytes 884744 | tf_op jit(solution)/shard_map/ppermute | solution.py:629
  15.9 0.0 collective-permute-done.8.refs_3_
  15.9 0.0 collective-permute-done.6.refs_1_
  15.9 1.2 %near_scores.1 = (bf16[12,128,256]{2,1,0:T(8,128)(2,1)S(1)}, bf16[64,768]{1,0:T(8,128)(2,1)S(1)}, f32[384,256]{1,0:T(8,128)S(1)}, bf16[512,256]{1,0:T(8,128)(2,1)S(1)}, bf16[128,128]{1,0:T(8,128)(2,1)S(1)}) custom-call(bf16[40,576]{1,0:T(8,128)(2,1)S(1)} %get-tuple-element.30.refs_0_, bf16[40,576]{1,0:T(8,128)(2,1)S(1)} %collective-permute-done.6.refs_1_, ...), custom_call_target="tpu_custom_call" | custom-call | flops 1000000000 | bytes 1000000 | tf_op jit(solution)/shard_map/near_scores/pallas_call | solution.py:280
  17.1 0.4 collective-permute-done.9.far_codes_ref
  17.5 1.6 %row_attention.1 = (bf16[512,768]{1,0:T(8,128)(2,1)S(1)}, bf16[128,128]{1,0:T(8,128)(2,1)S(1)}, f32[16,128]{1,0:T(8,128)S(1)}) custom-call(bf16[12,128,256]{2,1,0:T(8,128)(2,1)S(1)} %get-tuple-element.32.scores_ref, bf16[64,768]{1,0:T(8,128)(2,1)S(1)} %get-tuple-element.33.values_ref, f32[384,256]{1,0:T(8,128)S(1)} %get-tuple-element.34.near_tied_ref, ...), custom_call_target="tpu_custom_call" | custom-call | flops 3000000000 | bytes 1000000 | tf_op jit(solution)/shard_map/row_attention/pallas_call | solution.py:371
  19.1 0.0 collective-permute-done.4.refs_1_
  19.1 0.0 collective-permute-done.5.refs_3_
  19.1 0.0 copy-done.1
  19.1 0.0 copy-done.3
  19.2 0.0 copy-start
  19.2 3.0 %column_attention.1 = (bf16[384,128]{1,0:T(8,128)(2,1)S(1)}, bf16[384,128]{1,0:T(8,128)(2,1)S(1)}, f32[512,192]{1,0:T(8,128)S(1)}) custom-call(bf16[192,768]{1,0:T(8,128)(2,1)S(1)} %copy-done.2, bf16[192,768]{1,0:T(8,128)(2,1)S(1)} %collective-permute-done.4.refs_1_, bf16[192,768]{1,0:T(8,128)(2,1)S(1)} %collective-permute-done.3.refs_2_, ...), custom_call_target="tpu_custom_call" | custom-call | flops 2000000000 | bytes 1000000 | tf_op jit(solution)/shard_map/column_attention/pallas_call | solution.py:513
  22.2 1.6 %collective-permute-start.11 = (bf16[384,128]{1,0:T(8,128)(2,1)S(1)}, bf16[384,128]{1,0:T(8,128)(2,1)S(1)}, u32[]{:S(2)}, u32[]{:S(2)}) collective-permute-start(bf16[384,128]{1,0:T(8,128)(2,1)S(1)} %get-tuple-element.40.refs_0_), channel_id=1, source_target_pairs={{0,2},{1,3},{2,0},{3,1},{4,6},{5,7},{6,4},{7,5},{8,10},{9,11},{10,... | collective-permute-start | bytes 294920 | tf_op jit(solution)/shard_map/ppermute | solution.py:629
  23.8 0.5 %collective-permute-start.14 = (bf16[384,128]{1,0:T(8,128)(2,1)S(1)}, bf16[384,128]{1,0:T(8,128)(2,1)S(1)}, u32[]{:S(2)}, u32[]{:S(2)}) collective-permute-start(bf16[384,128]{1,0:T(8,128)(2,1)S(1)} %get-tuple-element.41.refs_4_), channel_id=1, source_target_pairs={{0,2},{1,3},{2,0},{3,1},{4,6},{5,7},{6,4},{7,5},{8,10},{9,11},{10,... | collective-permute-start | bytes 294920 | tf_op jit(solution)/shard_map/ppermute | solution.py:629
  24.3 0.0 collective-permute-start.10
  24.3 0.5 %collective-permute-start.13 = (bf16[384,128]{1,0:T(8,128)(2,1)S(1)}, bf16[384,128]{1,0:T(8,128)(2,1)S(1)}, u32[]{:S(2)}, u32[]{:S(2)}) collective-permute-start(bf16[384,128]{1,0:T(8,128)(2,1)S(1)} %get-tuple-element.41.refs_4_), channel_id=1, source_target_pairs={{0,1},{1,0},{2,3},{3,2},{4,5},{5,4},{6,7},{7,6},{8,9},{9,8},{10,11... | collective-permute-start | bytes 294920 | tf_op jit(solution)/shard_map/ppermute | solution.py:629
  24.8 3.1 %collective-permute-done.11.refs_2_ = bf16[384,128]{1,0:T(8,128)(2,1)S(1)} collective-permute-done((bf16[384,128]{1,0:T(8,128)(2,1)S(1)}, bf16[384,128]{1,0:T(8,128)(2,1)S(1)}, u32[]{:S(2)}, u32[]{:S(2)}) %collective-permute-start.11) | collective-permute-done | bytes 98336 | tf_op jit(solution)/shard_map/ppermute | solution.py:629
  27.8 0.0 collective-permute-start.12
  27.9 1.1 %collective-permute-done.14.refs_6_ = bf16[384,128]{1,0:T(8,128)(2,1)S(1)} collective-permute-done((bf16[384,128]{1,0:T(8,128)(2,1)S(1)}, bf16[384,128]{1,0:T(8,128)(2,1)S(1)}, u32[]{:S(2)}, u32[]{:S(2)}) %collective-permute-start.14) | collective-permute-done | bytes 98336 | tf_op jit(solution)/shard_map/ppermute | solution.py:629
  29.0 0.0 collective-permute-start.15
  29.0 0.0 collective-permute-done.10.refs_1_
  29.0 0.0 collective-permute-done.13.refs_5_
  29.0 0.2 collective-permute-done.12.refs_3_
  29.1 1.1 %collective-permute-done.15.refs_7_ = bf16[384,128]{1,0:T(8,128)(2,1)S(1)} collective-permute-done((bf16[384,128]{1,0:T(8,128)(2,1)S(1)}, bf16[384,128]{1,0:T(8,128)(2,1)S(1)}, u32[]{:S(2)}, u32[]{:S(2)}) %collective-permute-start.15) | collective-permute-done | bytes 98336 | tf_op jit(solution)/shard_map/ppermute | solution.py:629
  30.3 0.0 copy-done
  30.3 0.5 %finish.1 = bf16[8,96,128]{2,1,0:T(8,128)(2,1)S(1)} custom-call(bf16[384,128]{1,0:T(8,128)(2,1)S(1)} %get-tuple-element.40.refs_0_, bf16[384,128]{1,0:T(8,128)(2,1)S(1)} %collective-permute-done.10.refs_1_, bf16[384,128]{1,0:T(8,128)(2,1)S(1)} %collective-permute-done.11.refs_2_, bf16[384,128]{1,0:T(8,128)(2,1)S(1)} %collective-permute-done.12.refs_3_, ...), custom_call_target="tpu_custom_call" | custom-call | tf_op jit(solution)/shard_map/finish/pallas_call | solution.py:584
  30.8 12.3 %all_to_all.5.blocks_ref = bf16[8,96,128]{2,1,0:T(8,128)(2,1)S(1)} all-to-all(bf16[8,96,128]{2,1,0:T(8,128)(2,1)S(1)} %finish.1), channel_id=1, replica_groups=mesh['seq'=8,'head'=4] {'seq'}, dimensions={0} | all-to-all | bytes 393216 | tf_op jit(solution)/shard_map/all_to_all | solution.py:673
  43.1 0.8 %order.1 = bf16[2,192,256]{2,1,0:T(8,128)(2,1)} custom-call(bf16[8,96,128]{2,1,0:T(8,128)(2,1)S(1)} %all_to_all.5.blocks_ref), custom_call_target="tpu_custom_call" | custom-call | tf_op jit(solution)/shard_map/order/pallas_call | solution.py:611
  (3 shorter events, 0.0 us)
Async XLA Ops:
  0.0 4.5 %copy-start.4 = (s32[2]{0:T(128)S(1)}, s32[2]{0:T(128)}, u32[]{:S(2)}) copy-start(s32[2]{0:T(128)} %live_hbm.1) | copy-start | bytes 28
  0.0 13.3 %collective-permute-start.3 = (bf16[192,768]{1,0:T(8,128)(2,1)}, bf16[192,768]{1,0:T(8,128)(2,1)S(1)}, u32[]{:S(2)}, u32[]{:S(2)}) collective-permute-start(bf16[192,768]{1,0:T(8,128)(2,1)} %refs_0_), channel_id=1, source_target_pairs={{0,2},{1,3},{2,0},{3,1},{4,6},{5,7},{6,4},{7,5},{8,10},{9,11},{10,... | collective-permute-start | bytes 884744 | tf_op jit(solution)/shard_map/ppermute | solution.py:629
  2.9 5.1 %collective-permute-start = (s32[2,256]{1,0:T(2,128)}, s32[2,256]{1,0:T(2,128)S(1)}, u32[]{:S(2)}, u32[]{:S(2)}) collective-permute-start(s32[2,256]{1,0:T(2,128)} %ids_hbm.1), channel_id=1, source_target_pairs={{0,4},{1,5},{2,6},{3,7},{4,0},{5,1},{6,2},{7,3},{8,12},{9,13},{10,... | collective-permute-start | bytes 6152 | tf_op jit(solution)/shard_map/ppermute | solution.py:629
  4.5 10.9 %copy-start.2 = (bf16[192,768]{1,0:T(8,128)(2,1)S(1)}, bf16[192,768]{1,0:T(8,128)(2,1)}, u32[]{:S(2)}) copy-start(bf16[192,768]{1,0:T(8,128)(2,1)} %refs_0_) | copy-start | bytes 884740
  4.5 3.5 %collective-permute-start.1 = (s32[1,2]{1,0:T(1,128)S(1)}, s32[1,2]{1,0:T(1,128)S(1)}, u32[]{:S(2)}, u32[]{:S(2)}) collective-permute-start(s32[1,2]{1,0:T(1,128)S(1)} %bitcast.4), channel_id=1, source_target_pairs={{0,4},{1,5},{2,6},{3,7},{4,0},{5,1},{6,2},{7,3},{8,12},{9,13},{10,... | collective-permute-start | bytes 32 | tf_op jit(solution)/shard_map/ppermute | solution.py:629
  8.1 5.2 %collective-permute-start.7 = (bf16[40,576]{1,0:T(8,128)(2,1)S(1)}, bf16[40,576]{1,0:T(8,128)(2,1)S(1)}, u32[]{:S(2)}, u32[]{:S(2)}) collective-permute-start(bf16[40,576]{1,0:T(8,128)(2,1)S(1)} %get-tuple-element.30.refs_0_), channel_id=1, source_target_pairs={{0,2},{1,3},{2,0},{3,1},{4,6},{5,7},{6,4},{7,5},{8,10},{9,11},{10,... | collective-permute-start | bytes 138248 | tf_op jit(solution)/shard_map/ppermute | solution.py:629
  8.7 4.5 %collective-permute-start.2 = (s32[8,256]{1,0:T(8,128)S(1)}, s32[8,256]{1,0:T(8,128)S(1)}, u32[]{:S(2)}, u32[]{:S(2)}) collective-permute-start(s32[8,256]{1,0:T(8,128)S(1)} %join_raw.1.own_ref), channel_id=1, source_target_pairs={{0,16},{1,17},{2,18},{3,19},{4,20},{5,21},{6,22},{7,23},{8,24},{9,... | collective-permute-start | bytes 24584 | tf_op jit(solution)/shard_map/ppermute | solution.py:629
  13.2 2.7 %collective-permute-start.8 = (bf16[40,576]{1,0:T(8,128)(2,1)S(1)}, bf16[40,576]{1,0:T(8,128)(2,1)S(1)}, u32[]{:S(2)}, u32[]{:S(2)}) collective-permute-start(bf16[40,576]{1,0:T(8,128)(2,1)S(1)} %collective-permute-done.7.refs_2_), channel_id=1, source_target_pairs={{0,1},{1,0},{2,3},{3,2},{4,5},{5,4},{6,7},{7,6},{8,9},{9,8},{10,11... | collective-permute-start | bytes 138248 | tf_op jit(solution)/shard_map/ppermute | solution.py:629
  13.3 2.6 %collective-permute-start.6 = (bf16[40,576]{1,0:T(8,128)(2,1)S(1)}, bf16[40,576]{1,0:T(8,128)(2,1)S(1)}, u32[]{:S(2)}, u32[]{:S(2)}) collective-permute-start(bf16[40,576]{1,0:T(8,128)(2,1)S(1)} %get-tuple-element.30.refs_0_), channel_id=1, source_target_pairs={{0,1},{1,0},{2,3},{3,2},{4,5},{5,4},{6,7},{7,6},{8,9},{9,8},{10,11... | collective-permute-start | bytes 138248 | tf_op jit(solution)/shard_map/ppermute | solution.py:629
  13.8 3.7 %collective-permute-start.9 = (s32[8,256]{1,0:T(8,128)S(1)}, s32[8,256]{1,0:T(8,128)S(1)}, u32[]{:S(2)}, u32[]{:S(2)}) collective-permute-start(s32[8,256]{1,0:T(8,128)S(1)} %join.1.refs_4_.near_codes_ref), channel_id=1, source_target_pairs={{0,8},{1,9},{2,10},{3,11},{4,12},{5,13},{6,14},{7,15},{8,0},{9,1},... | collective-permute-start | bytes 24584 | tf_op jit(solution)/shard_map/ppermute | solution.py:629
  15.4 3.7 %collective-permute-start.4 = (bf16[192,768]{1,0:T(8,128)(2,1)S(1)}, bf16[192,768]{1,0:T(8,128)(2,1)S(1)}, u32[]{:S(2)}, u32[]{:S(2)}) collective-permute-start(bf16[192,768]{1,0:T(8,128)(2,1)S(1)} %copy-done.2), channel_id=1, source_target_pairs={{0,1},{1,0},{2,3},{3,2},{4,5},{5,4},{6,7},{7,6},{8,9},{9,8},{10,11... | collective-permute-start | bytes 884744 | tf_op jit(solution)/shard_map/ppermute | solution.py:629
  15.4 3.7 %collective-permute-start.5 = (bf16[192,768]{1,0:T(8,128)(2,1)S(1)}, bf16[192,768]{1,0:T(8,128)(2,1)S(1)}, u32[]{:S(2)}, u32[]{:S(2)}) collective-permute-start(bf16[192,768]{1,0:T(8,128)(2,1)S(1)} %collective-permute-done.3.refs_2_), channel_id=1, source_target_pairs={{0,1},{1,0},{2,3},{3,2},{4,5},{5,4},{6,7},{7,6},{8,9},{9,8},{10,11... | collective-permute-start | bytes 884744 | tf_op jit(solution)/shard_map/ppermute | solution.py:629
  17.5 1.7 %copy-start.1 = (bf16[3,192,768]{2,1,0:T(8,128)(2,1)S(1)}, bf16[3,192,768]{2,1,0:T(8,128)(2,1)}, u32[]{:S(2)}) copy-start(bf16[3,192,768]{2,1,0:T(8,128)(2,1)} %param.12) | copy-start | bytes 2654212
  17.5 1.7 %copy-start.3 = (bf16[33,768]{1,0:T(8,128)(2,1)S(1)}, bf16[33,768]{1,0:T(8,128)(2,1)}, u32[]{:S(2)}) copy-start(bf16[33,768]{1,0:T(8,128)(2,1)} %refs_8_.1) | copy-start | bytes 152068
  19.2 11.1 %copy-start = (bf16[192,768]{1,0:T(8,128)(2,1)S(1)}, bf16[192,768]{1,0:T(8,128)(2,1)}, u32[]{:S(2)}) copy-start(bf16[192,768]{1,0:T(8,128)(2,1)} %refs_9_.1) | copy-start | bytes 884740
  22.2 5.7 %collective-permute-start.11 = (bf16[384,128]{1,0:T(8,128)(2,1)S(1)}, bf16[384,128]{1,0:T(8,128)(2,1)S(1)}, u32[]{:S(2)}, u32[]{:S(2)}) collective-permute-start(bf16[384,128]{1,0:T(8,128)(2,1)S(1)} %get-tuple-element.40.refs_0_), channel_id=1, source_target_pairs={{0,2},{1,3},{2,0},{3,1},{4,6},{5,7},{6,4},{7,5},{8,10},{9,11},{10,... | collective-permute-start | bytes 294920 | tf_op jit(solution)/shard_map/ppermute | solution.py:629
  23.8 5.2 %collective-permute-start.14 = (bf16[384,128]{1,0:T(8,128)(2,1)S(1)}, bf16[384,128]{1,0:T(8,128)(2,1)S(1)}, u32[]{:S(2)}, u32[]{:S(2)}) collective-permute-start(bf16[384,128]{1,0:T(8,128)(2,1)S(1)} %get-tuple-element.41.refs_4_), channel_id=1, source_target_pairs={{0,2},{1,3},{2,0},{3,1},{4,6},{5,7},{6,4},{7,5},{8,10},{9,11},{10,... | collective-permute-start | bytes 294920 | tf_op jit(solution)/shard_map/ppermute | solution.py:629
  24.3 4.7 %collective-permute-start.10 = (bf16[384,128]{1,0:T(8,128)(2,1)S(1)}, bf16[384,128]{1,0:T(8,128)(2,1)S(1)}, u32[]{:S(2)}, u32[]{:S(2)}) collective-permute-start(bf16[384,128]{1,0:T(8,128)(2,1)S(1)} %get-tuple-element.40.refs_0_), channel_id=1, source_target_pairs={{0,1},{1,0},{2,3},{3,2},{4,5},{5,4},{6,7},{7,6},{8,9},{9,8},{10,11... | collective-permute-start | bytes 294920 | tf_op jit(solution)/shard_map/ppermute | solution.py:629
  24.3 4.7 %collective-permute-start.13 = (bf16[384,128]{1,0:T(8,128)(2,1)S(1)}, bf16[384,128]{1,0:T(8,128)(2,1)S(1)}, u32[]{:S(2)}, u32[]{:S(2)}) collective-permute-start(bf16[384,128]{1,0:T(8,128)(2,1)S(1)} %get-tuple-element.41.refs_4_), channel_id=1, source_target_pairs={{0,1},{1,0},{2,3},{3,2},{4,5},{5,4},{6,7},{7,6},{8,9},{9,8},{10,11... | collective-permute-start | bytes 294920 | tf_op jit(solution)/shard_map/ppermute | solution.py:629
  27.8 1.3 %collective-permute-start.12 = (bf16[384,128]{1,0:T(8,128)(2,1)S(1)}, bf16[384,128]{1,0:T(8,128)(2,1)S(1)}, u32[]{:S(2)}, u32[]{:S(2)}) collective-permute-start(bf16[384,128]{1,0:T(8,128)(2,1)S(1)} %collective-permute-done.11.refs_2_), channel_id=1, source_target_pairs={{0,1},{1,0},{2,3},{3,2},{4,5},{5,4},{6,7},{7,6},{8,9},{9,8},{10,11... | collective-permute-start | bytes 294920 | tf_op jit(solution)/shard_map/ppermute | solution.py:629
  29.0 1.3 %collective-permute-start.15 = (bf16[384,128]{1,0:T(8,128)(2,1)S(1)}, bf16[384,128]{1,0:T(8,128)(2,1)S(1)}, u32[]{:S(2)}, u32[]{:S(2)}) collective-permute-start(bf16[384,128]{1,0:T(8,128)(2,1)S(1)} %collective-permute-done.14.refs_6_), channel_id=1, source_target_pairs={{0,1},{1,0},{2,3},{3,2},{4,5},{5,4},{6,7},{7,6},{8,9},{9,8},{10,11... | collective-permute-start | bytes 294920 | tf_op jit(solution)/shard_map/ppermute | solution.py:629

commit v28 on v26

--- a/solution.py
+++ b/solution.py
@@ -509,12 +509,10 @@
     parts = len(row_outs)
     tokens, width = row_context.shape
     local = width // parts
-    half = tokens // 2 * local // LANES
     return pl.pallas_call(
         functools.partial(column_kernel, parts),
         out_shape=(
-            jax.ShapeDtypeStruct((half, LANES), bf16),
-            jax.ShapeDtypeStruct((half, LANES), bf16),
+            jax.ShapeDtypeStruct((tokens * local // LANES, LANES), bf16),
             jax.ShapeDtypeStruct((tokens, local), f32),
         ),
         scratch_shapes=[
@@ -541,12 +539,12 @@
 
 
 def finish_kernel(parts, groups, *refs):
-    context_refs = [refs[:parts], refs[parts : 2 * parts]]
-    mixed_ref, col_out_ref, out_ref, context_ref = refs[2 * parts :]
+    context_refs = [refs[:parts]]
+    mixed_ref, col_out_ref, out_ref, context_ref = refs[parts:]
     tokens, local = mixed_ref.shape
     group = lax.axis_index("seq")
     part = lax.axis_index("head")
-    starts = [0, context_refs[0][0].shape[0]]
+    starts = [0]
     for start, some_refs in zip(starts, context_refs):
         for p in range(parts):
             context_ref[part ^ p, start : start + some_refs[p].shape[0], :] = some_refs[p][...]
@@ -587,7 +585,7 @@
         scratch_shapes=[pltpu.VMEM((parts, tokens * local // LANES, LANES), bf16)],
         compiler_params=pltpu.CompilerParams(vmem_limit_bytes=LARGE_VMEM),
         name="finish",
-    )(*contexts[0], *contexts[1], mixed, col_out)
+    )(*contexts[0], mixed, col_out)
 
 
 def order_kernel(blocks_ref, out_ref):

time: 43.3 us -> 43.4 us (level)
  waiting for transfers between devices: 9.62 us -> 11.2 us
  starting transfers between devices: 12.7 us -> 11.2 us
    ppermute x16 -> x13, waiting for transfers between devices: 9.62 us -> 11.2 us  [pairwise(): lax.ppermute(value, ('seq', 'head'), [(i, g * parts + p) for i, (g, p) in...]
    ppermute x16 -> x13, starting transfers between devices: 12.7 us -> 11.2 us  [pairwise(): lax.ppermute(value, ('seq', 'head'), [(i, g * parts + p) for i, (g, p) in...]
  transfers between devices with their start and end apart: 16 -> 13, of which waited for: 6 -> 5; matrix products, arithmetic and copies ran while one was open for 0% -> 0% of each run, Pallas kernels for 11% -> 11%
where the time goes in v28:
time: 43.4 us; the launch traced here: 43.2 us
  blocking collectives  11.6 us (27%)
  starting transfers between devices  11.2 us (26%)
  waiting for transfers between devices  11.2 us (26%)
  Pallas kernels  9.1 us (21%)
    all_to_all x1, blocking collectives, fast_body(): lax.all_to_all(blocks, 'seq', split_axis=0, concat_axis=0, tiled=True)  11.6 us
    ppermute x13, waiting for transfers between devices, pairwise(): lax.ppermute(value, ('seq', 'head'), [(i, g * parts + p) for i, (g, p) in...  11.2 us
    ppermute x13, starting transfers between devices, pairwise(): lax.ppermute(value, ('seq', 'head'), [(i, g * parts + p) for i, (g, p) in...  11.2 us
    pallas_call x1, Pallas kernels, attend_columns_here(): pl.pallas_call(functools.partial(column_kernel, parts), out_shape=(jax.Sh...  3.02 us
    pallas_call x1, Pallas kernels, make_tables(): pl.pallas_call(table_kernel, out_shape=(jax.ShapeDtypeStruct((TABLE_ROWS,...  1.87 us
    pallas_call x1, Pallas kernels, attend_rows(): pl.pallas_call(row_kernel, out_shape=(jax.ShapeDtypeStruct((2 * half * ow...  1.62 us
    pallas_call x1, Pallas kernels, attend_near(): pl.pallas_call(functools.partial(near_kernel, parts), out_shape=(jax.Shap...  1.19 us
  transfers between devices with their start and end apart: 13, of which 5 were waited for; matrix products, arithmetic and copies ran while one was open for 0% of the time, Pallas kernels for 11%

profile of v28, /device:TPU:0, one launch (start us, length us, event | category | flops | bytes accessed | tf_op | source)
XLA Modules:
  0.0 43.2 jit_solution(11312627545668618254)
XLA Ops:
  0.0 0.0 copy-start.4
  0.0 2.9 %collective-permute-start.3 = (bf16[192,768]{1,0:T(8,128)(2,1)}, bf16[192,768]{1,0:T(8,128)(2,1)S(1)}, u32[]{:S(2)}, u32[]{:S(2)}) collective-permute-start(bf16[192,768]{1,0:T(8,128)(2,1)} %refs_0_), channel_id=1, source_target_pairs={{0,2},{1,3},{2,0},{3,1},{4,6},{5,7},{6,4},{7,5},{8,10},{9,11},{10,... | collective-permute-start | bytes 884744 | tf_op jit(solution)/shard_map/ppermute | solution.py:627
  2.9 1.5 %collective-permute-start = (s32[2,256]{1,0:T(2,128)}, s32[2,256]{1,0:T(2,128)S(1)}, u32[]{:S(2)}, u32[]{:S(2)}) collective-permute-start(s32[2,256]{1,0:T(2,128)} %ids_hbm.1), channel_id=1, source_target_pairs={{0,4},{1,5},{2,6},{3,7},{4,0},{5,1},{6,2},{7,3},{8,12},{9,13},{10,... | collective-permute-start | bytes 6152 | tf_op jit(solution)/shard_map/ppermute | solution.py:627
  4.5 0.0 copy-done.4
  4.5 0.0 copy-start.2
  4.5 0.5 %collective-permute-start.1 = (s32[1,2]{1,0:T(1,128)S(1)}, s32[1,2]{1,0:T(1,128)S(1)}, u32[]{:S(2)}, u32[]{:S(2)}) collective-permute-start(s32[1,2]{1,0:T(1,128)S(1)} %bitcast.4), channel_id=1, source_target_pairs={{0,4},{1,5},{2,6},{3,7},{4,0},{5,1},{6,2},{7,3},{8,12},{9,13},{10,... | collective-permute-start | bytes 32 | tf_op jit(solution)/shard_map/ppermute | solution.py:627
  5.0 1.9 %tables.1 = (bf16[40,576]{1,0:T(8,128)(2,1)S(1)}, s32[8,256]{1,0:T(8,128)S(1)}) custom-call(s32[2,256]{1,0:T(2,128)} %ids_hbm.1, s32[2]{0:T(128)} %live_hbm.1, bf16[33,768]{1,0:T(8,128)(2,1)} %refs_8_.1, bf16[3,192,768]{2,1,0:T(8,128)(2,1)} %qkv_hbm.1), custom_call_target="tpu_custom_call" | custom-call | flops 2000000000 | bytes 884736 | tf_op jit(solution)/shard_map/tables/pallas_call | solution.py:131
  6.8 1.2 %collective-permute-done.1.live_ref = s32[1,2]{1,0:T(1,128)S(1)} collective-permute-done((s32[1,2]{1,0:T(1,128)S(1)}, s32[1,2]{1,0:T(1,128)S(1)}, u32[]{:S(2)}, u32[]{:S(2)}) %collective-permute-start.1) | collective-permute-done | bytes 40 | tf_op jit(solution)/shard_map/ppermute | solution.py:627
  8.0 0.0 collective-permute-done.ids_ref
  8.0 0.1 join_raw.1.own_ref
  8.1 2.6 %collective-permute-start.2 = (s32[8,256]{1,0:T(8,128)S(1)}, s32[8,256]{1,0:T(8,128)S(1)}, u32[]{:S(2)}, u32[]{:S(2)}) collective-permute-start(s32[8,256]{1,0:T(8,128)S(1)} %join_raw.1.own_ref), channel_id=1, source_target_pairs={{0,16},{1,17},{2,18},{3,19},{4,20},{5,21},{6,22},{7,23},{8,24},{9,... | collective-permute-start | bytes 24584 | tf_op jit(solution)/shard_map/ppermute | solution.py:627
  10.7 0.5 %collective-permute-start.7 = (bf16[40,576]{1,0:T(8,128)(2,1)S(1)}, bf16[40,576]{1,0:T(8,128)(2,1)S(1)}, u32[]{:S(2)}, u32[]{:S(2)}) collective-permute-start(bf16[40,576]{1,0:T(8,128)(2,1)S(1)} %get-tuple-element.29.refs_0_), channel_id=1, source_target_pairs={{0,2},{1,3},{2,0},{3,1},{4,6},{5,7},{6,4},{7,5},{8,10},{9,11},{10,... | collective-permute-start | bytes 138248 | tf_op jit(solution)/shard_map/ppermute | solution.py:627
  11.3 0.0 collective-permute-start.8
  11.3 1.4 %collective-permute-done.2.other_ref = s32[8,256]{1,0:T(8,128)S(1)} collective-permute-done((s32[8,256]{1,0:T(8,128)S(1)}, s32[8,256]{1,0:T(8,128)S(1)}, u32[]{:S(2)}, u32[]{:S(2)}) %collective-permute-start.2) | collective-permute-done | bytes 8224 | tf_op jit(solution)/shard_map/ppermute | solution.py:627
  12.7 0.0 collective-permute-done.3.refs_2_
  12.7 0.3 collective-permute-start.6
  13.0 1.6 %collective-permute-start.9 = (s32[8,256]{1,0:T(8,128)S(1)}, s32[8,256]{1,0:T(8,128)S(1)}, u32[]{:S(2)}, u32[]{:S(2)}) collective-permute-start(s32[8,256]{1,0:T(8,128)S(1)} %join.1.refs_4_.near_codes_ref), channel_id=1, source_target_pairs={{0,8},{1,9},{2,10},{3,11},{4,12},{5,13},{6,14},{7,15},{8,0},{9,1},... | collective-permute-start | bytes 24584 | tf_op jit(solution)/shard_map/ppermute | solution.py:627
  14.5 0.0 copy-done.2
  14.5 0.0 collective-permute-start.4
  14.6 0.8 %collective-permute-done.7.refs_2_ = bf16[40,576]{1,0:T(8,128)(2,1)S(1)} collective-permute-done((bf16[40,576]{1,0:T(8,128)(2,1)S(1)}, bf16[40,576]{1,0:T(8,128)(2,1)S(1)}, u32[]{:S(2)}, u32[]{:S(2)}) %collective-permute-start.7) | collective-permute-done | bytes 46112 | tf_op jit(solution)/shard_map/ppermute | solution.py:627
  15.4 0.0 collective-permute-start.5
  15.4 0.0 collective-permute-done.8.refs_3_
  15.4 0.0 collective-permute-done.6.refs_1_
  15.4 1.2 %near_scores.1 = (bf16[12,128,256]{2,1,0:T(8,128)(2,1)S(1)}, bf16[64,768]{1,0:T(8,128)(2,1)S(1)}, f32[384,256]{1,0:T(8,128)S(1)}, bf16[512,256]{1,0:T(8,128)(2,1)S(1)}, bf16[128,128]{1,0:T(8,128)(2,1)S(1)}) custom-call(bf16[40,576]{1,0:T(8,128)(2,1)S(1)} %get-tuple-element.29.refs_0_, bf16[40,576]{1,0:T(8,128)(2,1)S(1)} %collective-permute-done.6.refs_1_, ...), custom_call_target="tpu_custom_call" | custom-call | flops 1000000000 | bytes 1000000 | tf_op jit(solution)/shard_map/near_scores/pallas_call | solution.py:280
  16.6 0.0 collective-permute-done.9.far_codes_ref
  16.6 0.0 copy-start.1
  16.6 0.0 copy-start.3
  16.6 1.6 %row_attention.1 = (bf16[512,768]{1,0:T(8,128)(2,1)S(1)}, bf16[128,128]{1,0:T(8,128)(2,1)S(1)}, f32[16,128]{1,0:T(8,128)S(1)}) custom-call(bf16[12,128,256]{2,1,0:T(8,128)(2,1)S(1)} %get-tuple-element.31.scores_ref, bf16[64,768]{1,0:T(8,128)(2,1)S(1)} %get-tuple-element.32.values_ref, f32[384,256]{1,0:T(8,128)S(1)} %get-tuple-element.33.near_tied_ref, ...), custom_call_target="tpu_custom_call" | custom-call | flops 3000000000 | bytes 1000000 | tf_op jit(solution)/shard_map/row_attention/pallas_call | solution.py:371
  18.2 0.0 collective-permute-done.4.refs_1_
  18.3 0.0 collective-permute-done.5.refs_3_
  18.3 0.0 copy-done.1
  18.3 0.0 copy-done.3
  18.3 0.0 copy-start
  18.3 3.0 %column_attention.1 = (bf16[768,128]{1,0:T(8,128)(2,1)S(1)}, f32[512,192]{1,0:T(8,128)S(1)}) custom-call(bf16[192,768]{1,0:T(8,128)(2,1)S(1)} %copy-done.2, bf16[192,768]{1,0:T(8,128)(2,1)S(1)} %collective-permute-done.4.refs_1_, bf16[192,768]{1,0:T(8,128)(2,1)S(1)} %collective-permute-done.3.refs_2_, bf16[192,768]{1,0:T(8,128)(2,1)S(1)} %collective-permute-done.5.refs_3_, ...), custom_call_target="tpu_custom_call" | custom-call | flops 2000000000 | bytes 1000000 | tf_op jit(solution)/shard_map/column_attention/pallas_call | solution.py:512
  21.3 1.2 %collective-permute-start.11 = (bf16[768,128]{1,0:T(8,128)(2,1)S(1)}, bf16[768,128]{1,0:T(8,128)(2,1)S(1)}, u32[]{:S(2)}, u32[]{:S(2)}) collective-permute-start(bf16[768,128]{1,0:T(8,128)(2,1)S(1)} %get-tuple-element.39.refs_0_), channel_id=1, source_target_pairs={{0,2},{1,3},{2,0},{3,1},{4,6},{5,7},{6,4},{7,5},{8,10},{9,11},{10,... | collective-permute-start | bytes 589832 | tf_op jit(solution)/shard_map/ppermute | solution.py:627
  22.5 0.0 collective-permute-start.10
  22.5 6.4 %collective-permute-done.11.refs_2_ = bf16[768,128]{1,0:T(8,128)(2,1)S(1)} collective-permute-done((bf16[768,128]{1,0:T(8,128)(2,1)S(1)}, bf16[768,128]{1,0:T(8,128)(2,1)S(1)}, u32[]{:S(2)}, u32[]{:S(2)}) %collective-permute-start.11) | collective-permute-done | bytes 196640 | tf_op jit(solution)/shard_map/ppermute | solution.py:627
  28.9 0.0 collective-permute-start.12
  28.9 0.0 collective-permute-done.10.refs_1_
  28.9 1.4 %collective-permute-done.12.refs_3_ = bf16[768,128]{1,0:T(8,128)(2,1)S(1)} collective-permute-done((bf16[768,128]{1,0:T(8,128)(2,1)S(1)}, bf16[768,128]{1,0:T(8,128)(2,1)S(1)}, u32[]{:S(2)}, u32[]{:S(2)}) %collective-permute-start.12) | collective-permute-done | bytes 196640 | tf_op jit(solution)/shard_map/ppermute | solution.py:627
  30.3 0.0 copy-done
  30.3 0.5 %finish.1 = bf16[8,96,128]{2,1,0:T(8,128)(2,1)S(1)} custom-call(bf16[768,128]{1,0:T(8,128)(2,1)S(1)} %get-tuple-element.39.refs_0_, bf16[768,128]{1,0:T(8,128)(2,1)S(1)} %collective-permute-done.10.refs_1_, bf16[768,128]{1,0:T(8,128)(2,1)S(1)} %collective-permute-done.11.refs_2_, bf16[768,128]{1,0:T(8,128)(2,1)S(1)} %collective-permute-done.12.refs_3_, ...), custom_call_target="tpu_custom_call" | custom-call | tf_op jit(solution)/shard_map/finish/pallas_call | solution.py:582
  30.8 11.6 %all_to_all.5.blocks_ref = bf16[8,96,128]{2,1,0:T(8,128)(2,1)S(1)} all-to-all(bf16[8,96,128]{2,1,0:T(8,128)(2,1)S(1)} %finish.1), channel_id=1, replica_groups=mesh['seq'=8,'head'=4] {'seq'}, dimensions={0} | all-to-all | bytes 393216 | tf_op jit(solution)/shard_map/all_to_all | solution.py:674
  42.4 0.8 %order.1 = bf16[2,192,256]{2,1,0:T(8,128)(2,1)} custom-call(bf16[8,96,128]{2,1,0:T(8,128)(2,1)S(1)} %all_to_all.5.blocks_ref), custom_call_target="tpu_custom_call" | custom-call | tf_op jit(solution)/shard_map/order/pallas_call | solution.py:609
  (1 shorter events, 0.0 us)
Async XLA Ops:
  0.0 4.5 %copy-start.4 = (s32[2]{0:T(128)S(1)}, s32[2]{0:T(128)}, u32[]{:S(2)}) copy-start(s32[2]{0:T(128)} %live_hbm.1) | copy-start | bytes 28
  0.0 12.7 %collective-permute-start.3 = (bf16[192,768]{1,0:T(8,128)(2,1)}, bf16[192,768]{1,0:T(8,128)(2,1)S(1)}, u32[]{:S(2)}, u32[]{:S(2)}) collective-permute-start(bf16[192,768]{1,0:T(8,128)(2,1)} %refs_0_), channel_id=1, source_target_pairs={{0,2},{1,3},{2,0},{3,1},{4,6},{5,7},{6,4},{7,5},{8,10},{9,11},{10,... | collective-permute-start | bytes 884744 | tf_op jit(solution)/shard_map/ppermute | solution.py:627
  2.9 5.1 %collective-permute-start = (s32[2,256]{1,0:T(2,128)}, s32[2,256]{1,0:T(2,128)S(1)}, u32[]{:S(2)}, u32[]{:S(2)}) collective-permute-start(s32[2,256]{1,0:T(2,128)} %ids_hbm.1), channel_id=1, source_target_pairs={{0,4},{1,5},{2,6},{3,7},{4,0},{5,1},{6,2},{7,3},{8,12},{9,13},{10,... | collective-permute-start | bytes 6152 | tf_op jit(solution)/shard_map/ppermute | solution.py:627
  4.5 10.1 %copy-start.2 = (bf16[192,768]{1,0:T(8,128)(2,1)S(1)}, bf16[192,768]{1,0:T(8,128)(2,1)}, u32[]{:S(2)}) copy-start(bf16[192,768]{1,0:T(8,128)(2,1)} %refs_0_) | copy-start | bytes 884740
  4.5 3.5 %collective-permute-start.1 = (s32[1,2]{1,0:T(1,128)S(1)}, s32[1,2]{1,0:T(1,128)S(1)}, u32[]{:S(2)}, u32[]{:S(2)}) collective-permute-start(s32[1,2]{1,0:T(1,128)S(1)} %bitcast.4), channel_id=1, source_target_pairs={{0,4},{1,5},{2,6},{3,7},{4,0},{5,1},{6,2},{7,3},{8,12},{9,13},{10,... | collective-permute-start | bytes 32 | tf_op jit(solution)/shard_map/ppermute | solution.py:627
  8.1 4.6 %collective-permute-start.2 = (s32[8,256]{1,0:T(8,128)S(1)}, s32[8,256]{1,0:T(8,128)S(1)}, u32[]{:S(2)}, u32[]{:S(2)}) collective-permute-start(s32[8,256]{1,0:T(8,128)S(1)} %join_raw.1.own_ref), channel_id=1, source_target_pairs={{0,16},{1,17},{2,18},{3,19},{4,20},{5,21},{6,22},{7,23},{8,24},{9,... | collective-permute-start | bytes 24584 | tf_op jit(solution)/shard_map/ppermute | solution.py:627
  10.7 4.6 %collective-permute-start.7 = (bf16[40,576]{1,0:T(8,128)(2,1)S(1)}, bf16[40,576]{1,0:T(8,128)(2,1)S(1)}, u32[]{:S(2)}, u32[]{:S(2)}) collective-permute-start(bf16[40,576]{1,0:T(8,128)(2,1)S(1)} %get-tuple-element.29.refs_0_), channel_id=1, source_target_pairs={{0,2},{1,3},{2,0},{3,1},{4,6},{5,7},{6,4},{7,5},{8,10},{9,11},{10,... | collective-permute-start | bytes 138248 | tf_op jit(solution)/shard_map/ppermute | solution.py:627
  11.3 4.1 %collective-permute-start.8 = (bf16[40,576]{1,0:T(8,128)(2,1)S(1)}, bf16[40,576]{1,0:T(8,128)(2,1)S(1)}, u32[]{:S(2)}, u32[]{:S(2)}) collective-permute-start(bf16[40,576]{1,0:T(8,128)(2,1)S(1)} %get-tuple-element.29.refs_0_), channel_id=1, source_target_pairs={{0,3},{1,2},{2,1},{3,0},{4,7},{5,6},{6,5},{7,4},{8,11},{9,10},{10,... | collective-permute-start | bytes 138248 | tf_op jit(solution)/shard_map/ppermute | solution.py:627
  12.7 2.7 %collective-permute-start.6 = (bf16[40,576]{1,0:T(8,128)(2,1)S(1)}, bf16[40,576]{1,0:T(8,128)(2,1)S(1)}, u32[]{:S(2)}, u32[]{:S(2)}) collective-permute-start(bf16[40,576]{1,0:T(8,128)(2,1)S(1)} %get-tuple-element.29.refs_0_), channel_id=1, source_target_pairs={{0,1},{1,0},{2,3},{3,2},{4,5},{5,4},{6,7},{7,6},{8,9},{9,8},{10,11... | collective-permute-start | bytes 138248 | tf_op jit(solution)/shard_map/ppermute | solution.py:627
  13.0 3.7 %collective-permute-start.9 = (s32[8,256]{1,0:T(8,128)S(1)}, s32[8,256]{1,0:T(8,128)S(1)}, u32[]{:S(2)}, u32[]{:S(2)}) collective-permute-start(s32[8,256]{1,0:T(8,128)S(1)} %join.1.refs_4_.near_codes_ref), channel_id=1, source_target_pairs={{0,8},{1,9},{2,10},{3,11},{4,12},{5,13},{6,14},{7,15},{8,0},{9,1},... | collective-permute-start | bytes 24584 | tf_op jit(solution)/shard_map/ppermute | solution.py:627
  14.5 3.7 %collective-permute-start.4 = (bf16[192,768]{1,0:T(8,128)(2,1)S(1)}, bf16[192,768]{1,0:T(8,128)(2,1)S(1)}, u32[]{:S(2)}, u32[]{:S(2)}) collective-permute-start(bf16[192,768]{1,0:T(8,128)(2,1)S(1)} %copy-done.2), channel_id=1, source_target_pairs={{0,1},{1,0},{2,3},{3,2},{4,5},{5,4},{6,7},{7,6},{8,9},{9,8},{10,11... | collective-permute-start | bytes 884744 | tf_op jit(solution)/shard_map/ppermute | solution.py:627
  15.4 2.9 %collective-permute-start.5 = (bf16[192,768]{1,0:T(8,128)(2,1)S(1)}, bf16[192,768]{1,0:T(8,128)(2,1)S(1)}, u32[]{:S(2)}, u32[]{:S(2)}) collective-permute-start(bf16[192,768]{1,0:T(8,128)(2,1)S(1)} %collective-permute-done.3.refs_2_), channel_id=1, source_target_pairs={{0,1},{1,0},{2,3},{3,2},{4,5},{5,4},{6,7},{7,6},{8,9},{9,8},{10,11... | collective-permute-start | bytes 884744 | tf_op jit(solution)/shard_map/ppermute | solution.py:627
  16.6 1.7 %copy-start.1 = (bf16[3,192,768]{2,1,0:T(8,128)(2,1)S(1)}, bf16[3,192,768]{2,1,0:T(8,128)(2,1)}, u32[]{:S(2)}) copy-start(bf16[3,192,768]{2,1,0:T(8,128)(2,1)} %param.12) | copy-start | bytes 2654212
  16.6 1.7 %copy-start.3 = (bf16[33,768]{1,0:T(8,128)(2,1)S(1)}, bf16[33,768]{1,0:T(8,128)(2,1)}, u32[]{:S(2)}) copy-start(bf16[33,768]{1,0:T(8,128)(2,1)} %refs_8_.1) | copy-start | bytes 152068
  18.3 12.0 %copy-start = (bf16[192,768]{1,0:T(8,128)(2,1)S(1)}, bf16[192,768]{1,0:T(8,128)(2,1)}, u32[]{:S(2)}) copy-start(bf16[192,768]{1,0:T(8,128)(2,1)} %refs_5_.1) | copy-start | bytes 884740
  21.3 7.5 %collective-permute-start.11 = (bf16[768,128]{1,0:T(8,128)(2,1)S(1)}, bf16[768,128]{1,0:T(8,128)(2,1)S(1)}, u32[]{:S(2)}, u32[]{:S(2)}) collective-permute-start(bf16[768,128]{1,0:T(8,128)(2,1)S(1)} %get-tuple-element.39.refs_0_), channel_id=1, source_target_pairs={{0,2},{1,3},{2,0},{3,1},{4,6},{5,7},{6,4},{7,5},{8,10},{9,11},{10,... | collective-permute-start | bytes 589832 | tf_op jit(solution)/shard_map/ppermute | solution.py:627
  22.5 6.4 %collective-permute-start.10 = (bf16[768,128]{1,0:T(8,128)(2,1)S(1)}, bf16[768,128]{1,0:T(8,128)(2,1)S(1)}, u32[]{:S(2)}, u32[]{:S(2)}) collective-permute-start(bf16[768,128]{1,0:T(8,128)(2,1)S(1)} %get-tuple-element.39.refs_0_), channel_id=1, source_target_pairs={{0,1},{1,0},{2,3},{3,2},{4,5},{5,4},{6,7},{7,6},{8,9},{9,8},{10,11... | collective-permute-start | bytes 589832 | tf_op jit(solution)/shard_map/ppermute | solution.py:627
  28.9 1.4 %collective-permute-start.12 = (bf16[768,128]{1,0:T(8,128)(2,1)S(1)}, bf16[768,128]{1,0:T(8,128)(2,1)S(1)}, u32[]{:S(2)}, u32[]{:S(2)}) collective-permute-start(bf16[768,128]{1,0:T(8,128)(2,1)S(1)} %collective-permute-done.11.refs_2_), channel_id=1, source_target_pairs={{0,1},{1,0},{2,3},{3,2},{4,5},{5,4},{6,7},{7,6},{8,9},{9,8},{10,11... | collective-permute-start | bytes 589832 | tf_op jit(solution)/shard_map/ppermute | solution.py:627
